TPU v7x, 32 devices: a whole 2x2x4 slice. The times are simulated.
32 devices in a mesh: groups: 2 (over y), seq: 4 (over x, core), tensor: 4 (over z).
Axes of the slice: x: 2, y: 2, z: 4, core: 2. Of those that a mesh axis runs over, the one named last changes fastest.
Arguments:
- tokens: bfloat16 [6144, 4608], P(('groups', 'seq'), 'tensor'), parts along dimension 0, may hold values from -40 to 40
- seg_ids: int32 [6144], P(('groups', 'seq')), parts along dimension 0, may hold values from 0 to 7, never falling along the last dimension, each value on 1 to 1536 neighbouring positions
- in_gain: float32 [4608], replicated, may hold values from 0.25 to 1.75
- q_weight: bfloat16 [4608, 1024], P(None, 'tensor'), may hold values from -4 to 4
- k_weight: bfloat16 [4608, 512], P(None, 'tensor'), may hold values from -1 to 1
- value_weight: bfloat16 [4608, 512], P(None, 'tensor'), may hold values from -0.09375 to 0.09375
- o_weight: bfloat16 [1024, 4608], P('tensor'), may hold values from -1 to 1
- out_gain: float32 [4608], P('tensor'), may hold values from 0.1 to 1.9
Outputs:
- layer_out: bfloat16 [6144, 4608], P(('groups', 'seq'), 'tensor'), parts along dimension 0
There are 2 independent parts, one for each index of `groups`. A program takes and returns all parts, laid end to end along the dimension named above; an argument that names none is the same for every part. Nothing has to cross between parts.
Inputs may be any that keep to these rules, and one draw needn't show every extreme that they name: `seg_ids`: document numbers never fall along the prompt; each document has at most 1536 tokens, and one has exactly that many.
All inputs are finite; a program needn't handle non-finite values.
Results may differ from a plain program's by a relative error of at most 0.008.
Values may be sent and summed in bfloat16 or wider, within the bound.
No kernel may reach another device: no remote copies, remote signals or barrier semaphores. Data moves between devices by JAX's collectives and lax.ppermute only.
A program may use at most 128 MiB of HBM per device.

v0:
```python
from functools import partial

import jax
import jax.numpy as jnp
from jax import lax
from jax.sharding import PartitionSpec as P

HEAD_SIZE = 128


epsilon = 1e-06
query_scale = 144.0 ** (-0.5)
rope_base = 10000.0


def apply_rotation(vectors, token_places):
    half_dim = vectors.shape[-1] // 2
    inverse = rope_base ** (-jnp.arange(half_dim, dtype=jnp.float32) / half_dim)
    angles = token_places.astype(jnp.float32)[:, None] * inverse[None, :]
    cosine = jnp.cos(angles)[:, None, :]
    sine_val = jnp.sin(angles)[:, None, :]
    front_half = vectors[..., :half_dim]
    back_half = vectors[..., half_dim:]
    return jnp.concatenate(
        [front_half * cosine - back_half * sine_val, back_half * cosine + front_half * sine_val],
        axis=-1,
    )


def attend_piece(attn_state, block_in, offset, queries, seg_query, query_pos):
    run_max, run_sum, context_sum = attn_state
    key_rows, value_rows, seg_keys = block_in
    row_count = key_rows.shape[0]
    kv_heads = context_sum.shape[0]
    head_dim = context_sum.shape[-1]
    key_block = key_rows.reshape(row_count, kv_heads, head_dim)
    value_block = value_rows.reshape(row_count, kv_heads, head_dim)
    scores = (
        jnp.einsum("rkgd,skd->kgrs", queries, key_block, preferred_element_type=jnp.float32)
        * query_scale
    )
    key_pos = jnp.arange(row_count, dtype=jnp.int32)
    allowed = (seg_query[:, None] == seg_keys[None, :]) & (query_pos[:, None] >= key_pos[None, :])
    masked = jnp.where(allowed, scores, -1e30)
    new_max = jnp.maximum(run_max, jnp.max(masked, axis=-1))
    expo = jnp.where(allowed, jnp.exp(scores - new_max[..., None]), 0.0)
    factor = jnp.exp(run_max - new_max)
    run_sum = jnp.sum(expo, axis=-1)
    added = jnp.einsum(
        "kgrs,skd->kgrd", expo.astype(jnp.bfloat16), value_block, preferred_element_type=jnp.float32
    )
    context_sum = added
    return (new_max, run_sum, context_sum)


def per_device(tokens, seg_ids, in_gain, q_weight, k_weight, value_weight, o_weight, out_gain):
    tok_rows, col_count = tokens.shape
    model_width = in_gain.shape[0]
    wide_local = tokens.astype(jnp.float32)
    gathered = lax.all_gather(tokens, "tensor", axis=1, tiled=True).astype(jnp.float32)
    mean_sq = jnp.mean(gathered * gathered, axis=1, keepdims=True)
    normed = (gathered * lax.rsqrt(mean_sq + epsilon) * in_gain[None, :]).astype(jnp.bfloat16)
    query_proj = jnp.dot(normed, q_weight, preferred_element_type=jnp.float32)
    projected_keys = jnp.dot(normed, k_weight, preferred_element_type=jnp.float32)
    projected_values = jnp.dot(normed, value_weight, preferred_element_type=jnp.float32)
    q_heads = q_weight.shape[1] // HEAD_SIZE
    kv_heads = k_weight.shape[1] // HEAD_SIZE
    query_pos = lax.axis_index("seq") * tok_rows + jnp.arange(tok_rows, dtype=jnp.int32)
    queries = apply_rotation(query_proj.reshape(tok_rows, q_heads, HEAD_SIZE), query_pos).astype(
        jnp.bfloat16
    )
    queries = queries.reshape(tok_rows, kv_heads, q_heads // kv_heads, HEAD_SIZE)
    key_bf = (
        apply_rotation(projected_keys.reshape(tok_rows, kv_heads, HEAD_SIZE), query_pos)
        .astype(jnp.bfloat16)
        .reshape(tok_rows, kv_heads * HEAD_SIZE)
    )
    value_bf = projected_values.astype(jnp.bfloat16)
    seg_bf = seg_ids.astype(jnp.bfloat16)
    group_size = q_heads // kv_heads
    initial_state = (
        jnp.full((kv_heads, group_size, tok_rows), -1e30, jnp.float32),
        jnp.zeros((kv_heads, group_size, tok_rows), jnp.float32),
        jnp.zeros((kv_heads, group_size, tok_rows, HEAD_SIZE), jnp.float32),
    )
    folder = partial(attend_piece, queries=queries, seg_query=seg_bf, query_pos=query_pos)
    attn_state = folder(
        initial_state,
        (
            lax.all_gather(key_bf, "seq", axis=0, tiled=True),
            lax.all_gather(value_bf, "seq", axis=0, tiled=True),
            lax.all_gather(seg_bf, "seq", axis=0, tiled=True),
        ),
        jnp.int32(0),
    )
    run_max, run_sum, context_sum = attn_state
    context = (context_sum / run_sum[..., None]).astype(jnp.bfloat16)
    context = jnp.transpose(context, (2, 0, 1, 3)).reshape(tok_rows, q_heads * HEAD_SIZE)
    term = jnp.dot(context, o_weight, preferred_element_type=jnp.float32)
    branch_part = lax.psum_scatter(
        term.astype(jnp.bfloat16), "tensor", scatter_dimension=1, tiled=True
    ).astype(jnp.float32)
    out_sq = lax.psum(jnp.sum(branch_part * branch_part, axis=1), "tensor")
    layer_out = (
        wide_local
        + branch_part * lax.rsqrt(out_sq / model_width + epsilon)[:, None] * out_gain[None, :]
    )
    return layer_out.astype(jnp.bfloat16)


def solution(mesh):
    return jax.shard_map(
        per_device,
        mesh=mesh,
        in_specs=(
            P(("groups", "seq"), "tensor"),
            P(("groups", "seq")),
            P(),
            P(None, "tensor"),
            P(None, "tensor"),
            P(None, "tensor"),
            P("tensor", None),
            P("tensor"),
        ),
        out_specs=P(("groups", "seq"), "tensor"),
        check_vma=False,
    )
```

profile of v0, /device:TPU:2, one launch (start us, length us, event | category | flops | bytes accessed | tf_op | source)
XLA Modules:
  0.0 365.7 jit_solution(1520882804032134016)
XLA Ops:
  6.5 0.7 all-gather.3.cloned.1.call-update
  7.3 0.0 reduce-scatter.4.cloned.1.call-start
  7.3 0.7 convert_element_type.49
  8.0 5.1 %all-gather = bf16[4,1,768]{2,1,0:T(2,128)(2,1)S(1)} all-gather(bf16[1,1,768]{2,1,0:T(2,128)(2,1)S(1)} %reshape.183), channel_id=1, replica_groups=mesh['groups'=2,'seq'=4,'tensor'=4] {'seq'}, dimensions={0}, use_global_device_ids=true | all-gather | bytes 7680 | tf_op jit(solution)/shard_map/all_gather | solution.py:92
  13.3 2.4 multiply_cosine_fusion
  15.7 3.4 fusion.11
  19.1 119.3 %all-gather.3.cloned.1.call-done = bf16[768,4608]{1,0:T(8,128)(2,1)} async-done(((bf16[768,1152]{1,0:T(8,128)(2,1)}), bf16[768,4608]{1,0:T(8,128)(2,1)}) %all-gather.3.cloned.1.call-update) | async-done | bytes 7077904 | tf_op jit(solution)/shard_map/all_gather | solution.py:60
  138.4 4.5 %fusion.5 = f32[768]{0:T(1024)S(1)} fusion(bf16[768,4608]{1,0:T(8,128)(2,1)} %all-gather.3.cloned.1.call-done), kind=kLoop, calls=%fused_computation.9 | loop fusion | flops 10616064 | bytes 7080960 | tf_op jit(solution)/shard_map/reduce_sum | solution.py:61
  142.9 0.0 copy-start.6
  142.9 5.7 %fusion.7 = bf16[768,4608]{1,0:T(8,128)(2,1)S(1)} fusion(bf16[768,4608]{1,0:T(8,128)(2,1)} %all-gather.3.cloned.1.call-done, f32[4608]{0:T(1024)S(1)} %copy-done.3, f32[768]{0:T(1024)S(1)} %add_rsqrt_fusion.1), kind=kLoop, calls=%fused_computation.11 | loop fusion | flops 14155776 | bytes 14177280 | tf_op jit(solution)/shard_map/convert_element_type | solution.py:62
  148.7 2.7 convolution_convert_fusion.1
  151.3 2.4 convolution_bitcast_fusion
  153.8 2.0 fusion.44
  155.8 1.5 fusion.38
  157.3 0.9 fusion.43
  158.2 1.3 copy.30
  159.5 1.0 pad_maximum_fusion
  160.5 9.1 %all_gather.14 = bf16[3072,128]{0,1:T(8,128)(2,1)} all-gather(bf16[768,128]{0,1:T(8,128)(2,1)S(1)} %pad_maximum_fusion), channel_id=1, replica_groups=mesh['groups'=2,'seq'=4,'tensor'=4] {'seq'}, dimensions={0}, use_global_device_ids=true | all-gather | bytes 983040 | tf_op jit(solution)/shard_map/all_gather | solution.py:90
  169.5 9.9 %all_gather.15 = bf16[3072,128]{1,0:T(8,128)(2,1)} all-gather(bf16[768,128]{1,0:T(8,128)(2,1)} %convolution_convert_fusion.1), channel_id=1, replica_groups=mesh['groups'=2,'seq'=4,'tensor'=4] {'seq'}, dimensions={0}, use_global_device_ids=true | all-gather | bytes 983040 | tf_op jit(solution)/shard_map/all_gather | solution.py:91
  179.4 2.1 copy.29
  181.6 1.4 subtract_convert_fusion
  183.0 6.2 %fusion = (f32[2,768]{1,0:T(2,128)S(1)}, f32[3072,768,2]{1,0,2:T(8,128)S(1)}) fusion(pred[768,3072]{0,1:T(8,128)(4,1)} %fusion.11, bf16[768,2,64]{2,0,1:T(8,128)(2,1)S(1)} %get-tuple-element.6, bf16[768,2,64]{2,0,1:T(8,128)(2,1)S(1)} %get-tuple-element.5, bf16[3072,128]{0,1:T(8,128)(2,1)} %all_gather.14), kind=kOutput, calls=%fused_computation.2 | convolution fusion | flops 1222900224 | bytes 22419456 | tf_op jit(solution)/shard_map/rkgd,skd->kgrs/dot_general | solution.py:39
  189.3 5.8 %fusion.3 = f32[2,768]{1,0:T(2,128)S(1)} fusion(f32[3072,768,2]{1,0,2:T(8,128)S(1)} %get-tuple-element.14, f32[2,768]{1,0:T(2,128)S(1)} %broadcast_maximum_fusion, pred[768,3072]{0,1:T(8,128)(4,1)} %fusion.11), kind=kLoop, calls=%fused_computation.7 | loop fusion | flops 18872832 | bytes 21245952 | tf_op jit(solution)/shard_map/reduce_sum | solution.py:48
  195.1 5.7 %fusion.20 = bf16[2,768,128]{1,2,0:T(8,128)(2,1)S(1)} fusion(f32[3072,768,2]{1,0,2:T(8,128)S(1)} %get-tuple-element.14, f32[2,768]{1,0:T(2,128)S(1)} %broadcast_maximum_fusion, pred[768,3072]{0,1:T(8,128)(4,1)} %fusion.11, bf16[3072,128]{1,0:T(8,128)(2,1)S(1)} %copy-done.2, f32[2,768]{1,0:T(2,128)S(1)} %fusion.3), kind=kOutput, calls=%fused_computation.27 | convolution fusion | flops 1227227136 | bytes 22425600 | tf_op jit(solution)/shard_map/kgrs,skd->kgrd/dot_general | solution.py:49
  200.9 5.0 %convolution_convert_fusion = bf16[768,4608]{1,0:T(8,128)(2,1)} fusion(bf16[768,256]{0,1:T(8,128)(2,1)S(1)} %bitcast.62, bf16[256,4608]{1,0:T(8,128)(2,1)S(1)} %copy-done), kind=kOutput, calls=%fused_computation.17 | convolution fusion | flops 1815478272 | bytes 9830400 | tf_op jit(solution)/shard_map/dot_general | solution.py:99
  205.8 10.3 %copy.27 = bf16[768,4608]{0,1:T(8,128)(2,1)} copy(bf16[768,4608]{1,0:T(8,128)(2,1)} %convolution_convert_fusion) | data formatting | bytes 14155776
  216.1 0.0 reduce-scatter.4.cloned.1.call-update
  216.1 121.9 %reduce-scatter.4.cloned.1.call-done = bf16[1152,768]{1,0:T(8,128)(2,1)} async-done(((bf16[4608,768]{1,0:T(8,128)(2,1)}), bf16[1152,768]{1,0:T(8,128)(2,1)}) %reduce-scatter.4.cloned.1.call-update) | async-done | bytes 1769488
  338.0 3.9 %copy.28 = bf16[768,1152]{1,0:T(8,128)(2,1)} copy(bf16[768,1152]{0,1:T(8,128)(2,1)} %bitcast.60) | data formatting | bytes 3538944
  341.8 1.9 fusion.13
  343.7 11.2 %psum.7 = f32[768]{0:T(1024)S(1)} all-reduce(f32[768]{0:T(1024)S(1)} %fusion.13), channel_id=1, replica_groups=mesh['groups'=2,'seq'=4,'tensor'=4] {'tensor'}, use_global_device_ids=true, to_apply=%region_5.6 | all-reduce | flops 768 | bytes 6144 | tf_op jit(solution)/shard_map/psum | solution.py:103
  355.0 3.9 %fusion.16 = bf16[768,1152]{1,0:T(8,128)(2,1)} fusion(bf16[768,1152]{1,0:T(8,128)(2,1)} %copy.28, bf16[768,1152]{1,0:T(8,128)(2,1)} %param.8, f32[1152]{0:T(1024)S(1)} %copy-done.4, f32[768]{0:T(1024)S(1)} %add_rsqrt_fusion), kind=kLoop, calls=%fused_computation.23 | loop fusion | flops 5308416 | bytes 5316096 | tf_op jit(solution)/shard_map/convert_element_type | solution.py:108
  (23 shorter events, 0.1 us)
Async XLA Ops:
  6.5 194.3 %copy-start = (bf16[256,4608]{1,0:T(8,128)(2,1)S(1)}, bf16[256,4608]{1,0:T(8,128)(2,1)}, u32[]{:S(2)}) copy-start(bf16[256,4608]{1,0:T(8,128)(2,1)} %param.14) | copy-start | bytes 7077892
  6.5 136.3 %copy-start.3 = (f32[4608]{0:T(1024)S(1)}, f32[4608]{0:T(1024)}, u32[]{:S(2)}) copy-start(f32[4608]{0:T(1024)} %param.10) | copy-start | bytes 55300
  6.5 131.9 %all-gather.3.cloned.1.call-start = ((), (), s32[]{:S(2)}) async-start(), calls=%async_computation.1 | async-start | bytes 8847360 | tf_op jit(solution)/shard_map/all_gather | solution.py:60
  7.3 330.7 %reduce-scatter.4.cloned.1.call-start = ((), (), s32[]{:S(2)}) async-start(), calls=%async_computation.2 | async-start | bytes 8847360
  142.9 5.8 %copy-start.6 = (bf16[4608,128]{1,0:T(8,128)(2,1)S(1)}, bf16[4608,128]{1,0:T(8,128)(2,1)}, u32[]{:S(2)}) copy-start(bf16[4608,128]{1,0:T(8,128)(2,1)} %param.13) | copy-start | bytes 3538948
  148.6 2.7 copy-start.1
  151.3 2.5 copy-start.5
  189.3 5.8 %copy-start.2 = (bf16[3072,128]{1,0:T(8,128)(2,1)S(1)}, bf16[3072,128]{1,0:T(8,128)(2,1)}, u32[]{:S(2)}) copy-start(bf16[3072,128]{1,0:T(8,128)(2,1)} %all_gather.15) | copy-start | bytes 2359300
  216.1 138.8 %copy-start.4 = (f32[1152]{0:T(1024)S(1)}, f32[1152]{0:T(1024)}, u32[]{:S(2)}) copy-start(f32[1152]{0:T(1024)} %param.15) | copy-start | bytes 13828
Sparse Core Ops, SparseCore 0:
  8.9 129.4 all-gather.2
  216.3 121.6 reduce-scatter.3
where the time goes:
time: 368 us; the launch traced here: 366 us
  waiting for transfers between devices  242 us (66%)
  blocking collectives  35.3 us (10%)
  other arithmetic  32.3 us (9%)
  matrix products  24.1 us (7%)
  local copies, waits for them, and re-layouts  18.5 us (5%)
  between operations  13.6 us (4%)
    unnamed x3, waiting for transfers between devices  123 us
    all_gather x1, waiting for transfers between devices, per_device(): lax.all_gather(tokens, 'tensor', axis=1, tiled=True).astype(jnp.float32)  119 us
    unnamed x20, local copies, waits for them, and re-layouts  17.6 us
    psum x1, blocking collectives, per_device(): out_sq = lax.psum(jnp.sum(branch_part * branch_part, axis=1), 'tensor')  11.2 us
    all_gather x1, blocking collectives, per_device(): lax.all_gather(value_bf, 'seq', axis=0, tiled=True)  9.92 us
    all_gather x1, blocking collectives, per_device(): lax.all_gather(key_bf, 'seq', axis=0, tiled=True)  9.06 us
  transfers between devices with their start and end apart: 2, of which 2 were waited for; matrix products, arithmetic and copies ran while one was open for 2% of the time, Pallas kernels for 0%

commit v1 on v0

v1 whole, which is shorter than its diff:
```python
import math
from functools import partial

import jax
import jax.numpy as jnp
from jax import lax
from jax.experimental import pallas as pl
from jax.experimental.pallas import tpu as pltpu
from jax.sharding import PartitionSpec as P

HEAD_SIZE = 128
PLANE = ("groups", "seq")

epsilon = 1e-06
query_scale = 144.0 ** (-0.5)
rope_base = 10000.0
NEG = -1e30
Q_TILE = 128
K_TILE = 256


def rotation_table(token_places):
    half_dim = HEAD_SIZE // 2
    inverse = rope_base ** (-jnp.arange(half_dim, dtype=jnp.float32) / half_dim)
    angles = token_places.astype(jnp.float32)[:, None] * inverse[None, :]
    return jnp.cos(angles), jnp.sin(angles)


def rotate(vectors, cosine, sine):
    rows, width = vectors.shape
    half_dim = HEAD_SIZE // 2
    parts = []
    for c in range(0, width, HEAD_SIZE):
        front = vectors[:, c : c + half_dim]
        back = vectors[:, c + half_dim : c + HEAD_SIZE]
        parts += [front * cosine - back * sine, back * cosine + front * sine]
    return jnp.concatenate(parts, axis=1)


def attention_kernel(lo_ref, q_ref, start_ref, *rest, back, group):
    kv_refs = rest[: back + 1]
    out_ref, k_scr, vt_scr = rest[back + 1 :]
    rows = kv_refs[0].shape[0]
    tile = pl.program_id(0)

    @pl.when(tile == 0)
    def _():
        for b in range(back + 1):
            k_scr[b * rows : (b + 1) * rows, :] = kv_refs[b][:, :HEAD_SIZE]
            values = kv_refs[b][:, HEAD_SIZE:].astype(jnp.float32)
            vt_scr[:, b * rows : (b + 1) * rows] = values.T.astype(jnp.bfloat16)

    q = q_ref[...]
    q2 = jnp.concatenate(
        [q[:, g * HEAD_SIZE : (g + 1) * HEAD_SIZE] for g in range(group)], axis=0
    )
    width = group * Q_TILE
    start = jnp.concatenate([start_ref[...]] * group, axis=1)
    first = back * rows + tile * Q_TILE
    place = first + lax.broadcasted_iota(jnp.int32, (1, Q_TILE), 1)
    place = jnp.concatenate([place] * group, axis=1)

    def step(j, state):
        run_max, run_sum, acc = state
        base = pl.multiple_of(j * K_TILE, K_TILE)
        scores = lax.dot_general(
            k_scr[pl.ds(base, K_TILE), :],
            q2,
            (((1,), (1,)), ((), ())),
            preferred_element_type=jnp.float32,
        )
        key_pos = base + lax.broadcasted_iota(jnp.int32, (K_TILE, width), 0)
        allowed = (key_pos >= start) & (key_pos <= place)
        scores = jnp.where(allowed, scores, NEG)
        new_max = jnp.maximum(run_max, jnp.max(scores, axis=0, keepdims=True))
        expo = jnp.exp2(scores - new_max)
        factor = jnp.exp2(run_max - new_max)
        run_sum = run_sum * factor + jnp.sum(expo, axis=0, keepdims=True)
        acc = acc * factor + jnp.dot(
            vt_scr[:, pl.ds(base, K_TILE)],
            expo.astype(jnp.bfloat16),
            preferred_element_type=jnp.float32,
        )
        return new_max, run_sum, acc

    state = (
        jnp.full((1, width), NEG, jnp.float32),
        jnp.zeros((1, width), jnp.float32),
        jnp.zeros((HEAD_SIZE, width), jnp.float32),
    )
    stop = (first + Q_TILE + K_TILE - 1) // K_TILE
    _, run_sum, acc = lax.fori_loop(lo_ref[tile], stop, step, state)
    context = (acc / run_sum).T
    for g in range(group):
        out_ref[:, g * HEAD_SIZE : (g + 1) * HEAD_SIZE] = context[
            g * Q_TILE : (g + 1) * Q_TILE
        ].astype(jnp.bfloat16)


def attend(queries, start, blocks):
    rows, width = queries.shape
    back = len(blocks) - 1
    group = width // HEAD_SIZE
    tiles = rows // Q_TILE
    low = start[::Q_TILE] // K_TILE
    keys = (back + 1) * rows
    whole = lambda i, lo: (0, 0)
    return pl.pallas_call(
        partial(attention_kernel, back=back, group=group),
        out_shape=jax.ShapeDtypeStruct((rows, width), jnp.bfloat16),
        grid_spec=pltpu.PrefetchScalarGridSpec(
            num_scalar_prefetch=1,
            grid=(tiles,),
            in_specs=[
                pl.BlockSpec((Q_TILE, width), lambda i, lo: (i, 0)),
                pl.BlockSpec((1, Q_TILE), lambda i, lo: (0, i)),
            ]
            + [pl.BlockSpec((rows, 2 * HEAD_SIZE), whole) for _ in blocks],
            out_specs=pl.BlockSpec((Q_TILE, width), lambda i, lo: (i, 0)),
            scratch_shapes=[
                pltpu.VMEM((keys, HEAD_SIZE), jnp.bfloat16),
                pltpu.VMEM((HEAD_SIZE, keys), jnp.bfloat16),
            ],
        ),
        compiler_params=pltpu.CompilerParams(vmem_limit_bytes=32 * 1024 * 1024),
        cost_estimate=pl.CostEstimate(
            flops=2 * rows * width * keys, bytes_accessed=4 * rows * width, transcendentals=rows * keys
        ),
        name="attend",
    )(low, queries, start[None, :], *blocks)


def per_device(
    tokens, seg_ids, in_gain, q_weight, k_weight, value_weight, o_weight, out_gain, *, sizes
):
    rows, cols = tokens.shape
    model_width = in_gain.shape[0]
    nz, nseq = sizes["tensor"], sizes["seq"]
    plane = nseq * sizes["groups"]
    z = lax.axis_index("tensor")
    seq = lax.axis_index("seq")
    in_plane = lax.axis_index(PLANE)
    half = nz // 2
    side, within = z // half, z % half
    half_rows = half * cols

    ring = [(i, i // half * half + (i + 1) % half) for i in range(nz)]
    swap = [(i, (i + half) % nz) for i in range(nz)]
    turn = lambda k: [(i, (i + k) % nz) for i in range(nz)]

    x_blocks = [tokens]
    for _ in range(half - 1):
        x_blocks.append(lax.ppermute(x_blocks[-1], "tensor", ring))

    share = half_rows // plane

    def weight_rows(first, count):
        parts = [
            lax.dynamic_slice_in_dim(w, first, count, axis=0)
            for w in (q_weight, k_weight, value_weight)
        ]
        gains = lax.dynamic_slice_in_dim(in_gain, first, count, axis=0)
        joined = jnp.concatenate(parts, axis=1).astype(jnp.float32)
        return (joined * gains[:, None]).astype(jnp.bfloat16)

    sent = weight_rows((1 - side) * half_rows + in_plane * share, share)
    got = lax.ppermute(sent, "tensor", swap)
    far_weight = lax.all_gather(got, PLANE, axis=0, tiled=True)
    near_weight = weight_rows(side * half_rows, half_rows)

    o_rows = o_weight.shape[0]
    o_share = o_rows // plane
    moved = []
    for k in range(1, nz):
        target = (z + k) % nz
        piece = lax.dynamic_slice(
            o_weight, (in_plane * o_share, target * cols), (o_share, cols)
        )
        moved.append(lax.ppermute(piece, "tensor", turn(k)))
    gathered_o = lax.all_gather(jnp.stack(moved), PLANE, axis=1, tiled=True)
    own_o = lax.dynamic_slice_in_dim(o_weight, z * cols, cols, axis=1)
    o_all = jnp.concatenate([own_o, gathered_o.reshape((nz - 1) * o_rows, cols)], axis=0)

    back = -(-(nseq * rows // 2 - 1) // rows)
    all_ids = lax.all_gather(seg_ids, "seq", axis=0, tiled=True)
    start = jnp.sum((all_ids[None, :] < seg_ids[:, None]).astype(jnp.int32), axis=1)
    start = start - (seq - back) * rows

    token_places = seq * rows + jnp.arange(rows, dtype=jnp.int32)
    cosine, sine = rotation_table(token_places)

    squares = sum(
        jnp.sum(jnp.square(b.astype(jnp.float32)), axis=1, keepdims=True) for b in x_blocks
    )
    far_squares = lax.ppermute(squares, "tensor", swap)

    def project(weight):
        total = None
        for k, block in enumerate(x_blocks):
            source = (within + half - k) % half
            part = lax.dynamic_slice_in_dim(weight, source * cols, cols, axis=0)
            term = jnp.dot(block, part, preferred_element_type=jnp.float32)
            total = term if total is None else total + term
        return total

    partial_far = lax.ppermute(project(far_weight).astype(jnp.bfloat16), "tensor", swap)
    projected = project(near_weight) + partial_far.astype(jnp.float32)
    projected = projected * lax.rsqrt((squares + far_squares) / model_width + epsilon)

    q_width, k_width = q_weight.shape[1], k_weight.shape[1]
    scale = query_scale * math.log2(math.e)
    queries = rotate(projected[:, :q_width], cosine * scale, sine * scale).astype(jnp.bfloat16)
    keys = rotate(projected[:, q_width : q_width + k_width], cosine, sine)
    values = projected[:, q_width + k_width :]
    own_kv = jnp.concatenate([keys, values], axis=1).astype(jnp.bfloat16)

    blocks = [own_kv]
    for k in range(1, back + 1):
        blocks.insert(
            0, lax.ppermute(own_kv, "seq", [(i, i + k) for i in range(nseq - k)])
        )
    context = attend(queries, start, blocks)

    contexts = [context] + [lax.ppermute(context, "tensor", turn(k)) for k in range(1, nz)]
    branch = jnp.dot(
        jnp.concatenate(contexts, axis=1), o_all, preferred_element_type=jnp.float32
    )
    own_sq = jnp.sum(branch * branch, axis=1, keepdims=True)
    out_sq = own_sq
    for k in range(1, nz):
        out_sq = out_sq + lax.ppermute(own_sq, "tensor", turn(k))
    layer_out = (
        tokens.astype(jnp.float32)
        + branch * lax.rsqrt(out_sq / model_width + epsilon) * out_gain[None, :]
    )
    return layer_out.astype(jnp.bfloat16)


def solution(mesh):
    return jax.shard_map(
        partial(per_device, sizes=dict(mesh.shape)),
        mesh=mesh,
        in_specs=(
            P(("groups", "seq"), "tensor"),
            P(("groups", "seq")),
            P(),
            P(None, "tensor"),
            P(None, "tensor"),
            P(None, "tensor"),
            P("tensor", None),
            P("tensor"),
        ),
        out_specs=P(("groups", "seq"), "tensor"),
        check_vma=False,
    )
```

time: 368 us -> 203 us (0.55)
  waiting for transfers between devices: 242 us -> 101 us
  starting transfers between devices: 0.04 us -> 32.7 us
  blocking collectives: 35.3 us -> 5.15 us
  other arithmetic: 32.3 us -> 14.8 us
  matrix products: 24.1 us -> 14.8 us
  Pallas kernels: 0 us -> 6.82 us
  local copies, waits for them, and re-layouts: 18.5 us -> 12.6 us
    unnamed x3 -> x2, waiting for transfers between devices: 123 us -> 0.03 us
    all_gather x1 -> x2, waiting for transfers between devices: 119 us -> 0.02 us  [the longest x1 0.02 us: per_device(): far_weight = lax.all_gather(got, PLANE, axis=0, tiled=True)]
    ppermute x0 -> x15, waiting for transfers between devices: none -> 101 us  [the longest x1 29.2 us: per_device(): far_squares = lax.ppermute(squares, 'tensor', swap)]
    ppermute x0 -> x15, starting transfers between devices: none -> 32.6 us  [the longest x3 11.6 us: per_device(): out_sq = out_sq + lax.ppermute(own_sq, 'tensor', turn(k))]
    all_gather x3 -> x1, blocking collectives: 24.1 us -> 5.15 us  [per_device(): all_ids = lax.all_gather(seg_ids, 'seq', axis=0, tiled=True)]
    unnamed x20 -> x25, local copies, waits for them, and re-layouts: 17.6 us -> 4.77 us
    psum x1 -> x0, blocking collectives: 11.2 us -> none  [per_device(): out_sq = lax.psum(jnp.sum(branch_part * branch_part, axis=1), 'tensor')]
    dot_general x6 -> x5, matrix products: 24.1 us -> 14.8 us  [the longest x4 10.6 us: project(): term = jnp.dot(block, part, preferred_element_type=jnp.float32)]
  transfers between devices with their start and end apart: 2 -> 17, of which waited for: 2 -> 8; matrix products, arithmetic and copies ran while one was open for 2% -> 15% of each run, Pallas kernels for 0% -> 3%
where the time goes in v1:
time: 203 us; the launch traced here: 201 us
  waiting for transfers between devices  101 us (50%)
  starting transfers between devices  32.7 us (16%)
  other arithmetic  14.8 us (7%)
  matrix products  14.8 us (7%)
  between operations  13.7 us (7%)
  local copies, waits for them, and re-layouts  12.6 us (6%)
  Pallas kernels  6.82 us (3%)
  blocking collectives  5.15 us (3%)
    ppermute x1, waiting for transfers between devices, per_device(): far_squares = lax.ppermute(squares, 'tensor', swap)  29.2 us
    ppermute x3, waiting for transfers between devices, per_device(): lax.ppermute(context, 'tensor', turn(k))  24.3 us
    ppermute x3, waiting for transfers between devices, per_device(): moved.append(lax.ppermute(piece, 'tensor', turn(k)))  20.5 us
    ppermute x1, waiting for transfers between devices, per_device(): got = lax.ppermute(sent, 'tensor', swap)  13.5 us
    ppermute x3, starting transfers between devices, per_device(): out_sq = out_sq + lax.ppermute(own_sq, 'tensor', turn(k))  11.6 us
    ppermute x2, waiting for transfers between devices, per_device(): lax.ppermute(own_kv, 'seq', [(i, i + k) for i in range(nseq - k)])  11.4 us
    dot_general x4, matrix products, project(): term = jnp.dot(block, part, preferred_element_type=jnp.float32)  10.6 us
    pallas_call x1, Pallas kernels, attend(): pl.pallas_call(partial(attention_kernel, back=back, group=group), out_sha...  6.82 us
  transfers between devices with their start and end apart: 17, of which 8 were waited for; matrix products, arithmetic and copies ran while one was open for 15% of the time, Pallas kernels for 3%

profile of v1, /device:TPU:2, one launch (start us, length us, event | category | flops | bytes accessed | tf_op | source)
XLA Modules:
  0.0 201.5 jit_solution(10248288317233620753)
XLA Ops:
  10.1 2.7 %collective-permute-start.1 = (bf16[288,512]{1,0:T(8,128)(2,1)S(1)}, bf16[288,512]{1,0:T(8,128)(2,1)}, u32[]{:S(2)}, u32[]{:S(2)}) collective-permute-start(bf16[288,512]{1,0:T(8,128)(2,1)S(1)} %multiply_convert_fusion.1), channel_id=1, source_target_pairs={{0,2},{1,3},{2,0},{3,1},{4,6},{5,7},{6,4},{7,5},{8,10},{9,11},{10,... | collective-permute-start | bytes 884744 | tf_op jit(solution)/shard_map/ppermute | solution.py:167
  12.7 13.5 %collective-permute-done.1 = bf16[288,512]{1,0:T(8,128)(2,1)} collective-permute-done((bf16[288,512]{1,0:T(8,128)(2,1)S(1)}, bf16[288,512]{1,0:T(8,128)(2,1)}, u32[]{:S(2)}, u32[]{:S(2)}) %collective-permute-start.1) | collective-permute-done | bytes 294944 | tf_op jit(solution)/shard_map/ppermute | solution.py:167
  26.9 1.7 fusion.53
  30.0 2.1 %collective-permute-start.10 = (bf16[32,1152]{1,0:T(8,128)(2,1)}, bf16[32,1152]{1,0:T(8,128)(2,1)}, u32[]{:S(2)}, u32[]{:S(2)}) collective-permute-start(bf16[32,1152]{1,0:T(8,128)(2,1)} %get-tuple-element.7), channel_id=1, source_target_pairs={{0,2},{1,3},{2,0},{3,1},{4,6},{5,7},{6,4},{7,5},{8,10},{9,11},{10,... | collective-permute-start | bytes 221192 | tf_op jit(solution)/shard_map/ppermute | solution.py:179
  32.1 2.8 %collective-permute-start.11 = (bf16[32,1152]{1,0:T(8,128)(2,1)}, bf16[32,1152]{1,0:T(8,128)(2,1)}, u32[]{:S(2)}, u32[]{:S(2)}) collective-permute-start(bf16[32,1152]{1,0:T(8,128)(2,1)} %get-tuple-element.6), channel_id=1, source_target_pairs={{0,3},{1,0},{2,1},{3,2},{4,7},{5,4},{6,5},{7,6},{8,11},{9,8},{10,9... | collective-permute-start | bytes 221192 | tf_op jit(solution)/shard_map/ppermute | solution.py:179
  35.0 2.2 %constant_dynamic-slice_fusion.4 = (bf16[2304,128]{1,0:T(8,128)(2,1)}, bf16[2304,128]{1,0:T(8,128)(2,1)}) fusion(bf16[4608,128]{1,0:T(8,128)(2,1)S(1)} %copy-done.8, s32[]{:T(128)S(6)} %select_n.79, bf16[4608,128]{1,0:T(8,128)(2,1)} %param.12), kind=kLoop, calls=%fused_computation.74 | loop fusion | bytes 2359300 | tf_op jit(solution)/shard_map/dynamic_slice | solution.py:159
  38.6 5.1 %all-gather = s32[4,1,768]{2,1,0:T(1,128)S(1)} all-gather(s32[1,1,768]{2,1,0:T(1,128)S(1)} %reshape.42), channel_id=1, replica_groups=mesh['groups'=2,'seq'=4,'tensor'=4] {'seq'}, dimensions={0}, use_global_device_ids=true | all-gather | bytes 15360 | tf_op jit(solution)/shard_map/all_gather | solution.py:185
  43.8 1.7 convert_reduce_fusion
  45.5 2.3 %multiply_convert_fusion = bf16[2304,512]{1,0:T(8,128)(2,1)S(1)} fusion(bf16[2304,128]{1,0:T(8,128)(2,1)} %get-tuple-element.18, bf16[2304,128]{1,0:T(8,128)(2,1)} %get-tuple-element.19, bf16[2304,256]{1,0:T(8,128)(2,1)S(1)} %constant_dynamic-slice_fusion.6, f32[2304]{0:T(1024)S(1)} %dynamic_slice.51), kind=kLoop, calls=%fused_computation.1 | loop fusion | flops 9437184 | bytes 4727808 | tf_op jit(solution)/shard_map/convert_element_type | solution.py:164
  47.8 2.3 %fusion.20 = f32[512,768]{0,1:T(8,128)} fusion(bf16[768,1152]{1,0:T(8,128)(2,1)S(1)} %copy-done.3, bf16[2304,512]{1,0:T(8,128)(2,1)S(1)} %multiply_convert_fusion, s32[]{:T(128)S(6)} %select_n.82), kind=kOutput, calls=%fused_computation.28 | convolution fusion | flops 905969664 | bytes 4521988 | tf_op jit(solution)/shard_map/dot_general | solution.py:202
  50.6 20.5 %collective-permute-done.9 = bf16[32,1152]{1,0:T(8,128)(2,1)} collective-permute-done((bf16[32,1152]{1,0:T(8,128)(2,1)}, bf16[32,1152]{1,0:T(8,128)(2,1)}, u32[]{:S(2)}, u32[]{:S(2)}) %collective-permute-start.9) | collective-permute-done | bytes 73760 | tf_op jit(solution)/shard_map/ppermute | solution.py:179
  71.1 1.7 pad_maximum_fusion.2
  72.9 3.1 %fusion.15 = f32[512,768]{0,1:T(8,128)S(1)} fusion(bf16[768,1152]{1,0:T(8,128)(2,1)} %collective-permute-done, bf16[2304,512]{1,0:T(8,128)(2,1)} %all-gather.4.cloned.1.call-done, s32[]{:T(128)S(6)} %select_n.84), kind=kOutput, calls=%fused_computation.23 | convolution fusion | flops 905969664 | bytes 4521988 | tf_op jit(solution)/shard_map/dot_general | solution.py:202
  76.1 2.1 %fusion.14 = bf16[768,512]{1,0:T(8,128)(2,1)} fusion(f32[512,768]{0,1:T(8,128)S(1)} %fusion.15, bf16[768,1152]{1,0:T(8,128)(2,1)S(1)} %copy-done.4, bf16[2304,512]{1,0:T(8,128)(2,1)S(1)} %copy-done.11, s32[]{:T(128)S(6)} %select_n.82), kind=kOutput, calls=%fused_computation.22 | convolution fusion | flops 906756096 | bytes 5308420 | tf_op jit(solution)/shard_map/dot_general | solution.py:202
  78.1 3.1 %collective-permute-start.2 = (bf16[768,512]{1,0:T(8,128)(2,1)}, bf16[768,512]{1,0:T(8,128)(2,1)S(1)}, u32[]{:S(2)}, u32[]{:S(2)}) collective-permute-start(bf16[768,512]{1,0:T(8,128)(2,1)} %fusion.14), channel_id=1, source_target_pairs={{0,2},{1,3},{2,0},{3,1},{4,6},{5,7},{6,4},{7,5},{8,10},{9,11},{10,... | collective-permute-start | bytes 2359304 | tf_op jit(solution)/shard_map/ppermute | solution.py:206
  81.2 2.0 multiply_reduce_fusion.1
  83.3 3.1 %fusion.18 = f32[512,768]{0,1:T(8,128)S(1)} fusion(bf16[768,1152]{1,0:T(8,128)(2,1)} %collective-permute-done, bf16[2304,512]{1,0:T(8,128)(2,1)} %copy-done.6, s32[]{:T(128)S(6)} %select_n.84), kind=kOutput, calls=%fused_computation.26 | convolution fusion | flops 905969664 | bytes 4521988 | tf_op jit(solution)/shard_map/dot_general | solution.py:202
  86.4 29.2 %collective-permute-done.3 = f32[768,1]{0,1:T(1,128)S(1)} collective-permute-done((f32[768,1]{0,1:T(1,128)S(1)}, f32[768,1]{0,1:T(1,128)S(1)}, u32[]{:S(2)}, u32[]{:S(2)}) %collective-permute-start.3) | collective-permute-done | bytes 3104 | tf_op jit(solution)/shard_map/ppermute | solution.py:195
  116.0 2.7 %fusion.45 = (bf16[768,64]{1,0:T(8,128)(2,1)S(1)}, bf16[768,64]{1,0:T(8,128)(2,1)S(1)}, bf16[768,64]{1,0:T(8,128)(2,1)}, bf16[768,64]{1,0:T(8,128)(2,1)}, bf16[768,64]{1,0:T(8,128)(2,1)}, /*index=5*/bf16[768,64]{1,0:T(8,128)(2,1)}) fusion(f32[768,512]{1,0:T(8,128)S(1)} %fusion.13, f32[768]{0:T(1024)S(1)} %add_convert_fusion.1, f32[64]{0:T(128)S(1)} %multiply_power_fusion), kind=kLoop, calls=%fused_computation.56 | loop fusion | flops 1327104 | bytes 1772800 | tf_op jit(solution)/shard_map/convert
  120.3 1.9 collective-permute-start.5
  123.8 9.1 %collective-permute-done.4.rest_0_ = bf16[768,256]{1,0:T(8,128)(2,1)S(1)} collective-permute-done((bf16[768,256]{1,0:T(8,128)(2,1)S(1)}, bf16[768,256]{1,0:T(8,128)(2,1)S(1)}, u32[]{:S(2)}, u32[]{:S(2)}) %collective-permute-start.4) | collective-permute-done | bytes 393248 | tf_op jit(solution)/shard_map/ppermute | solution.py:220
  132.9 2.3 %collective-permute-done.5.rest_1_ = bf16[768,256]{1,0:T(8,128)(2,1)S(1)} collective-permute-done((bf16[768,256]{1,0:T(8,128)(2,1)S(1)}, bf16[768,256]{1,0:T(8,128)(2,1)S(1)}, u32[]{:S(2)}, u32[]{:S(2)}) %collective-permute-start.5) | collective-permute-done | bytes 393248 | tf_op jit(solution)/shard_map/ppermute | solution.py:220
  137.0 6.8 %attend.1 = bf16[768,256]{1,0:T(8,128)(2,1)S(1)} custom-call(s32[6]{0:T(128)S(1)} %and_select_fusion.lo_ref, bf16[768,256]{1,0:T(8,128)(2,1)S(1)} %pad_maximum_fusion.q_ref, s32[1,768]{1,0:T(1,128)S(1)} %sub.52.start_ref, bf16[768,256]{1,0:T(8,128)(2,1)S(1)} %collective-permute-done.4.rest_0_, bf16[768,256]{1,0:T(8,128)(2,1)S(1)} %copy-done.2, ...), custom_call_target="tpu_custom_call" | custom-call | flops 905969664 | bytes 786432 | tf_op jit(solution)/shard_map/attend/pallas_call | solution.py:108
  145.4 3.3 %collective-permute-start.7 = (bf16[768,256]{1,0:T(8,128)(2,1)S(1)}, bf16[768,256]{1,0:T(8,128)(2,1)S(1)}, u32[]{:S(2)}, u32[]{:S(2)}) collective-permute-start(bf16[768,256]{1,0:T(8,128)(2,1)S(1)} %attend.1), channel_id=1, source_target_pairs={{0,2},{1,3},{2,0},{3,1},{4,6},{5,7},{6,4},{7,5},{8,10},{9,11},{10,... | collective-permute-start | bytes 1179656 | tf_op jit(solution)/shard_map/ppermute | solution.py:224
  148.8 1.9 constant_dynamic-slice_fusion
  150.7 5.6 %collective-permute-done.6 = bf16[768,256]{1,0:T(8,128)(2,1)S(1)} collective-permute-done((bf16[768,256]{1,0:T(8,128)(2,1)S(1)}, bf16[768,256]{1,0:T(8,128)(2,1)S(1)}, u32[]{:S(2)}, u32[]{:S(2)}) %collective-permute-start.6) | collective-permute-done | bytes 393248 | tf_op jit(solution)/shard_map/ppermute | solution.py:224
  156.3 18.7 %collective-permute-done.7 = bf16[768,256]{1,0:T(8,128)(2,1)S(1)} collective-permute-done((bf16[768,256]{1,0:T(8,128)(2,1)S(1)}, bf16[768,256]{1,0:T(8,128)(2,1)S(1)}, u32[]{:S(2)}, u32[]{:S(2)}) %collective-permute-start.7) | collective-permute-done | bytes 393248 | tf_op jit(solution)/shard_map/ppermute | solution.py:224
  175.0 4.1 %multiply_reduce_fusion = (f32[768]{0:T(1024)S(1)}, f32[768,1152]{1,0:T(8,128)S(1)}) fusion(bf16[768,1152]{1,0:T(8,128)(2,1)} %bitcast.16, bf16[256,1152]{1,0:T(8,128)(2,1)} %constant_dynamic-slice_fusion, bf16[768,256]{1,0:T(8,128)(2,1)} %collective-permute-done.8, bf16[768,256]{1,0:T(8,128)(2,1)S(1)} %collective-permute-done.7, ...), kind=kOutput, calls=%fused_computation.6 | convolution fusion | flops 1824718080 | bytes 7474176 | tf_op jit(solution)/shard_map/dot_general | solution.py:225
  179.1 9.1 %collective-permute-start.12 = (f32[768,1]{0,1:T(1,128)S(1)}, f32[768,1]{0,1:T(1,128)S(1)}, u32[]{:S(2)}, u32[]{:S(2)}) collective-permute-start(f32[768,1]{0,1:T(1,128)S(1)} %broadcast_in_dim.2), channel_id=1, source_target_pairs={{0,1},{1,2},{2,3},{3,0},{4,5},{5,6},{6,7},{7,4},{8,9},{9,10},{10,1... | collective-permute-start | bytes 9224 | tf_op jit(solution)/shard_map/ppermute | solution.py:231
  188.3 2.4 %collective-permute-start.14 = (f32[768,1]{0,1:T(1,128)S(1)}, f32[768,1]{0,1:T(1,128)S(1)}, u32[]{:S(2)}, u32[]{:S(2)}) collective-permute-start(f32[768,1]{0,1:T(1,128)S(1)} %broadcast_in_dim.2), channel_id=1, source_target_pairs={{0,3},{1,0},{2,1},{3,2},{4,7},{5,4},{6,5},{7,6},{8,11},{9,8},{10,9... | collective-permute-start | bytes 9224 | tf_op jit(solution)/shard_map/ppermute | solution.py:231
  190.7 2.1 %collective-permute-done.13 = f32[768,1]{0,1:T(1,128)S(1)} collective-permute-done((f32[768,1]{0,1:T(1,128)S(1)}, f32[768,1]{0,1:T(1,128)S(1)}, u32[]{:S(2)}, u32[]{:S(2)}) %collective-permute-start.13) | collective-permute-done | bytes 3104 | tf_op jit(solution)/shard_map/ppermute | solution.py:231
  192.8 1.8 fusion.1
  (67 shorter events, 14.6 us)
Async XLA Ops:
  6.5 1.7 copy-start
  6.5 28.4 %copy-start.8 = (bf16[4608,128]{1,0:T(8,128)(2,1)S(1)}, bf16[4608,128]{1,0:T(8,128)(2,1)}, u32[]{:S(2)}) copy-start(bf16[4608,128]{1,0:T(8,128)(2,1)} %param.13) | copy-start | bytes 3538948
  6.5 66.3 %all-gather.4.cloned.1.call-start = ((), (), s32[]{:S(2)}) async-start(), calls=%async_computation | async-start | bytes 2654208 | tf_op jit(solution)/shard_map/all_gather | solution.py:168
  10.1 16.1 %collective-permute-start.1 = (bf16[288,512]{1,0:T(8,128)(2,1)S(1)}, bf16[288,512]{1,0:T(8,128)(2,1)}, u32[]{:S(2)}, u32[]{:S(2)}) collective-permute-start(bf16[288,512]{1,0:T(8,128)(2,1)S(1)} %multiply_convert_fusion.1), channel_id=1, source_target_pairs={{0,2},{1,3},{2,0},{3,1},{4,6},{5,7},{6,4},{7,5},{8,10},{9,11},{10,... | collective-permute-start | bytes 884744 | tf_op jit(solution)/shard_map/ppermute | solution.py:167
  26.2 124.5 %all-gather.6.cloned.1.call-start = ((), (), s32[]{:S(2)}) async-start(), calls=%async_computation.1 | async-start | bytes 1990656 | tf_op jit(solution)/shard_map/all_gather | solution.py:180
  26.3 46.6 %collective-permute-start = (bf16[768,1152]{1,0:T(8,128)(2,1)}, bf16[768,1152]{1,0:T(8,128)(2,1)}, u32[]{:S(2)}, u32[]{:S(2)}) collective-permute-start(bf16[768,1152]{1,0:T(8,128)(2,1)} %param.8), channel_id=1, source_target_pairs={{0,1},{1,0},{2,3},{3,2},{4,5},{5,4},{6,7},{7,6},{8,9},{9,8},{10,11... | collective-permute-start | bytes 5308424 | tf_op jit(solution)/shard_map/ppermute | solution.py:153
  28.6 42.6 %collective-permute-start.9 = (bf16[32,1152]{1,0:T(8,128)(2,1)}, bf16[32,1152]{1,0:T(8,128)(2,1)}, u32[]{:S(2)}, u32[]{:S(2)}) collective-permute-start(bf16[32,1152]{1,0:T(8,128)(2,1)} %get-tuple-element.5), channel_id=1, source_target_pairs={{0,1},{1,2},{2,3},{3,0},{4,5},{5,6},{6,7},{7,4},{8,9},{9,10},{10,1... | collective-permute-start | bytes 221192 | tf_op jit(solution)/shard_map/ppermute | solution.py:179
  30.0 41.1 %collective-permute-start.10 = (bf16[32,1152]{1,0:T(8,128)(2,1)}, bf16[32,1152]{1,0:T(8,128)(2,1)}, u32[]{:S(2)}, u32[]{:S(2)}) collective-permute-start(bf16[32,1152]{1,0:T(8,128)(2,1)} %get-tuple-element.7), channel_id=1, source_target_pairs={{0,2},{1,3},{2,0},{3,1},{4,6},{5,7},{6,4},{7,5},{8,10},{9,11},{10,... | collective-permute-start | bytes 221192 | tf_op jit(solution)/shard_map/ppermute | solution.py:179
  32.1 39.0 %collective-permute-start.11 = (bf16[32,1152]{1,0:T(8,128)(2,1)}, bf16[32,1152]{1,0:T(8,128)(2,1)}, u32[]{:S(2)}, u32[]{:S(2)}) collective-permute-start(bf16[32,1152]{1,0:T(8,128)(2,1)} %get-tuple-element.6), channel_id=1, source_target_pairs={{0,3},{1,0},{2,1},{3,2},{4,7},{5,4},{6,5},{7,6},{8,11},{9,8},{10,9... | collective-permute-start | bytes 221192 | tf_op jit(solution)/shard_map/ppermute | solution.py:179
  37.1 0.7 copy-start.9
  45.5 2.3 %copy-start.3 = (bf16[768,1152]{1,0:T(8,128)(2,1)S(1)}, bf16[768,1152]{1,0:T(8,128)(2,1)}, u32[]{:S(2)}) copy-start(bf16[768,1152]{1,0:T(8,128)(2,1)} %param.8) | copy-start | bytes 5308420
  47.8 2.3 %copy-start.6 = (bf16[2304,512]{1,0:T(8,128)(2,1)}, bf16[2304,512]{1,0:T(8,128)(2,1)S(1)}, u32[]{:S(2)}) copy-start(bf16[2304,512]{1,0:T(8,128)(2,1)S(1)} %multiply_convert_fusion) | copy-start | bytes 7077892
  72.9 3.2 %copy-start.4 = (bf16[768,1152]{1,0:T(8,128)(2,1)S(1)}, bf16[768,1152]{1,0:T(8,128)(2,1)}, u32[]{:S(2)}) copy-start(bf16[768,1152]{1,0:T(8,128)(2,1)} %param.8) | copy-start | bytes 5308420
  72.9 3.2 %copy-start.11 = (bf16[2304,512]{1,0:T(8,128)(2,1)S(1)}, bf16[2304,512]{1,0:T(8,128)(2,1)}, u32[]{:S(2)}) copy-start(bf16[2304,512]{1,0:T(8,128)(2,1)} %all-gather.4.cloned.1.call-done) | copy-start | bytes 7077892
  78.1 37.5 %collective-permute-start.2 = (bf16[768,512]{1,0:T(8,128)(2,1)}, bf16[768,512]{1,0:T(8,128)(2,1)S(1)}, u32[]{:S(2)}, u32[]{:S(2)}) collective-permute-start(bf16[768,512]{1,0:T(8,128)(2,1)} %fusion.14), channel_id=1, source_target_pairs={{0,2},{1,3},{2,0},{3,1},{4,6},{5,7},{6,4},{7,5},{8,10},{9,11},{10,... | collective-permute-start | bytes 2359304 | tf_op jit(solution)/shard_map/ppermute | solution.py:206
  83.2 32.4 %copy-start.7 = (f32[512,768]{0,1:T(8,128)S(1)}, f32[512,768]{0,1:T(8,128)}, u32[]{:S(2)}) copy-start(f32[512,768]{0,1:T(8,128)} %fusion.20) | copy-start | bytes 4718596
  83.2 32.4 %collective-permute-start.3 = (f32[768,1]{0,1:T(1,128)S(1)}, f32[768,1]{0,1:T(1,128)S(1)}, u32[]{:S(2)}, u32[]{:S(2)}) collective-permute-start(f32[768,1]{0,1:T(1,128)S(1)} %add.167), channel_id=1, source_target_pairs={{0,2},{1,3},{2,0},{3,1},{4,6},{5,7},{6,4},{7,5},{8,10},{9,11},{10,... | collective-permute-start | bytes 9224 | tf_op jit(solution)/shard_map/ppermute | solution.py:195
  119.0 13.9 %collective-permute-start.4 = (bf16[768,256]{1,0:T(8,128)(2,1)S(1)}, bf16[768,256]{1,0:T(8,128)(2,1)S(1)}, u32[]{:S(2)}, u32[]{:S(2)}) collective-permute-start(bf16[768,256]{1,0:T(8,128)(2,1)S(1)} %pad_maximum_fusion.1.rest_2_), channel_id=1, source_target_pairs={{0,8},{4,12},{1,9},{5,13},{2,10},{6,14},{3,11},{7,15},{16,24},{20,... | collective-permute-start | bytes 1179656 | tf_op jit(solution)/shard_map/ppermute | solution.py:220
  120.3 14.9 %collective-permute-start.5 = (bf16[768,256]{1,0:T(8,128)(2,1)S(1)}, bf16[768,256]{1,0:T(8,128)(2,1)S(1)}, u32[]{:S(2)}, u32[]{:S(2)}) collective-permute-start(bf16[768,256]{1,0:T(8,128)(2,1)S(1)} %pad_maximum_fusion.1.rest_2_), channel_id=1, source_target_pairs={{0,4},{4,8},{8,12},{1,5},{5,9},{9,13},{2,6},{6,10},{10,14},{3,7},{... | collective-permute-start | bytes 1179656 | tf_op jit(solution)/shard_map/ppermute | solution.py:220
  135.2 0.7 copy-start.1
  136.0 1.0 copy-start.2
  143.8 12.5 %collective-permute-start.6 = (bf16[768,256]{1,0:T(8,128)(2,1)S(1)}, bf16[768,256]{1,0:T(8,128)(2,1)S(1)}, u32[]{:S(2)}, u32[]{:S(2)}) collective-permute-start(bf16[768,256]{1,0:T(8,128)(2,1)S(1)} %attend.1), channel_id=1, source_target_pairs={{0,1},{1,2},{2,3},{3,0},{4,5},{5,6},{6,7},{7,4},{8,9},{9,10},{10,1... | collective-permute-start | bytes 1179656 | tf_op jit(solution)/shard_map/ppermute | solution.py:224
  145.4 29.5 %collective-permute-start.7 = (bf16[768,256]{1,0:T(8,128)(2,1)S(1)}, bf16[768,256]{1,0:T(8,128)(2,1)S(1)}, u32[]{:S(2)}, u32[]{:S(2)}) collective-permute-start(bf16[768,256]{1,0:T(8,128)(2,1)S(1)} %attend.1), channel_id=1, source_target_pairs={{0,2},{1,3},{2,0},{3,1},{4,6},{5,7},{6,4},{7,5},{8,10},{9,11},{10,... | collective-permute-start | bytes 1179656 | tf_op jit(solution)/shard_map/ppermute | solution.py:224
  148.8 26.2 %collective-permute-start.8 = (bf16[768,256]{1,0:T(8,128)(2,1)S(1)}, bf16[768,256]{1,0:T(8,128)(2,1)}, u32[]{:S(2)}, u32[]{:S(2)}) collective-permute-start(bf16[768,256]{1,0:T(8,128)(2,1)S(1)} %attend.1), channel_id=1, source_target_pairs={{0,3},{1,0},{2,1},{3,2},{4,7},{5,4},{6,5},{7,6},{8,11},{9,8},{10,9... | collective-permute-start | bytes 1179656 | tf_op jit(solution)/shard_map/ppermute | solution.py:224
  175.0 17.8 %copy-start.5 = (bf16[768,1152]{1,0:T(8,128)(2,1)S(1)}, bf16[768,1152]{1,0:T(8,128)(2,1)}, u32[]{:S(2)}) copy-start(bf16[768,1152]{1,0:T(8,128)(2,1)} %param.8) | copy-start | bytes 5308420
  175.0 17.8 %copy-start.10 = (f32[1152]{0:T(1024)S(1)}, f32[1152]{0:T(1024)}, u32[]{:S(2)}) copy-start(f32[1152]{0:T(1024)} %param.15) | copy-start | bytes 13828
  179.1 11.6 %collective-permute-start.12 = (f32[768,1]{0,1:T(1,128)S(1)}, f32[768,1]{0,1:T(1,128)S(1)}, u32[]{:S(2)}, u32[]{:S(2)}) collective-permute-start(f32[768,1]{0,1:T(1,128)S(1)} %broadcast_in_dim.2), channel_id=1, source_target_pairs={{0,1},{1,2},{2,3},{3,0},{4,5},{5,6},{6,7},{7,4},{8,9},{9,10},{10,1... | collective-permute-start | bytes 9224 | tf_op jit(solution)/shard_map/ppermute | solution.py:231
  188.3 4.5 %collective-permute-start.13 = (f32[768,1]{0,1:T(1,128)S(1)}, f32[768,1]{0,1:T(1,128)S(1)}, u32[]{:S(2)}, u32[]{:S(2)}) collective-permute-start(f32[768,1]{0,1:T(1,128)S(1)} %broadcast_in_dim.2), channel_id=1, source_target_pairs={{0,2},{1,3},{2,0},{3,1},{4,6},{5,7},{6,4},{7,5},{8,10},{9,11},{10,... | collective-permute-start | bytes 9224 | tf_op jit(solution)/shard_map/ppermute | solution.py:231
  188.3 4.5 %collective-permute-start.14 = (f32[768,1]{0,1:T(1,128)S(1)}, f32[768,1]{0,1:T(1,128)S(1)}, u32[]{:S(2)}, u32[]{:S(2)}) collective-permute-start(f32[768,1]{0,1:T(1,128)S(1)} %broadcast_in_dim.2), channel_id=1, source_target_pairs={{0,3},{1,0},{2,1},{3,2},{4,7},{5,4},{6,5},{7,6},{8,11},{9,8},{10,9... | collective-permute-start | bytes 9224 | tf_op jit(solution)/shard_map/ppermute | solution.py:231
Sparse Core Ops, SparseCore 0:
  26.3 30.1 all-gather.3
  73.0 28.4 all-gather.5

commit v2 on v1

--- a/solution.py
+++ b/solution.py
@@ -17,6 +17,7 @@
 NEG = -1e30
 Q_TILE = 128
 K_TILE = 256
+CHUNKS = 2
 
 
 def rotation_table(token_places):
@@ -37,7 +38,7 @@
     return jnp.concatenate(parts, axis=1)
 
 
-def attention_kernel(lo_ref, q_ref, start_ref, *rest, back, group):
+def attention_kernel(lo_ref, q_ref, start_ref, *rest, back, group, offset):
     kv_refs = rest[: back + 1]
     out_ref, k_scr, vt_scr = rest[back + 1 :]
     rows = kv_refs[0].shape[0]
@@ -56,19 +57,26 @@
     )
     width = group * Q_TILE
     start = jnp.concatenate([start_ref[...]] * group, axis=1)
-    first = back * rows + tile * Q_TILE
+    first = back * rows + offset + tile * Q_TILE
     place = first + lax.broadcasted_iota(jnp.int32, (1, Q_TILE), 1)
     place = jnp.concatenate([place] * group, axis=1)
 
-    def step(j, state):
-        run_max, run_sum, acc = state
+    def score(j):
         base = pl.multiple_of(j * K_TILE, K_TILE)
-        scores = lax.dot_general(
+        return lax.dot_general(
             k_scr[pl.ds(base, K_TILE), :],
             q2,
             (((1,), (1,)), ((), ())),
             preferred_element_type=jnp.float32,
         )
+
+    low = lo_ref[tile]
+    stop = (first + Q_TILE + K_TILE - 1) // K_TILE
+
+    def step(j, state):
+        scores, run_max, run_sum, acc = state
+        following = score(jnp.minimum(j + 1, stop - 1))
+        base = pl.multiple_of(j * K_TILE, K_TILE)
         key_pos = base + lax.broadcasted_iota(jnp.int32, (K_TILE, width), 0)
         allowed = (key_pos >= start) & (key_pos <= place)
         scores = jnp.where(allowed, scores, NEG)
@@ -81,15 +89,15 @@
             expo.astype(jnp.bfloat16),
             preferred_element_type=jnp.float32,
         )
-        return new_max, run_sum, acc
+        return following, new_max, run_sum, acc
 
     state = (
+        score(low),
         jnp.full((1, width), NEG, jnp.float32),
         jnp.zeros((1, width), jnp.float32),
         jnp.zeros((HEAD_SIZE, width), jnp.float32),
     )
-    stop = (first + Q_TILE + K_TILE - 1) // K_TILE
-    _, run_sum, acc = lax.fori_loop(lo_ref[tile], stop, step, state)
+    _, _, run_sum, acc = lax.fori_loop(low, stop, step, state)
     context = (acc / run_sum).T
     for g in range(group):
         out_ref[:, g * HEAD_SIZE : (g + 1) * HEAD_SIZE] = context[
@@ -97,25 +105,25 @@
         ].astype(jnp.bfloat16)
 
 
-def attend(queries, start, blocks):
+def attend(queries, start, blocks, offset):
     rows, width = queries.shape
+    block_rows = blocks[0].shape[0]
     back = len(blocks) - 1
     group = width // HEAD_SIZE
-    tiles = rows // Q_TILE
     low = start[::Q_TILE] // K_TILE
-    keys = (back + 1) * rows
+    keys = (back + 1) * block_rows
     whole = lambda i, lo: (0, 0)
     return pl.pallas_call(
-        partial(attention_kernel, back=back, group=group),
+        partial(attention_kernel, back=back, group=group, offset=offset),
         out_shape=jax.ShapeDtypeStruct((rows, width), jnp.bfloat16),
         grid_spec=pltpu.PrefetchScalarGridSpec(
             num_scalar_prefetch=1,
-            grid=(tiles,),
+            grid=(rows // Q_TILE,),
             in_specs=[
                 pl.BlockSpec((Q_TILE, width), lambda i, lo: (i, 0)),
                 pl.BlockSpec((1, Q_TILE), lambda i, lo: (0, i)),
             ]
-            + [pl.BlockSpec((rows, 2 * HEAD_SIZE), whole) for _ in blocks],
+            + [pl.BlockSpec((block_rows, 2 * HEAD_SIZE), whole) for _ in blocks],
             out_specs=pl.BlockSpec((Q_TILE, width), lambda i, lo: (i, 0)),
             scratch_shapes=[
                 pltpu.VMEM((keys, HEAD_SIZE), jnp.bfloat16),
@@ -128,6 +136,46 @@
         ),
         name="attend",
     )(low, queries, start[None, :], *blocks)
+
+
+def place_kernel(where_ref, own_ref, got_ref, out_ref):
+    piece = pl.program_id(0)
+    held = pl.num_programs(0) // 2
+
+    @pl.when(piece < held)
+    def _():
+        out_ref[...] = own_ref[0]
+
+    @pl.when(piece >= held)
+    def _():
+        out_ref[...] = got_ref[0]
+
+
+def spread(piece, plane, masks):
+    own = piece[None]
+    order = [0]
+    for mask in masks:
+        got = lax.ppermute(own, PLANE, [(i, i ^ mask) for i in range(plane)])
+        if mask != masks[-1]:
+            own = jnp.concatenate([own, got], axis=0)
+        order = order + [k ^ mask for k in order]
+    where = jnp.bitwise_xor(lax.axis_index(PLANE), jnp.array(order, jnp.int32))
+    held = own.shape[0]
+    rows, width = piece.shape
+    return pl.pallas_call(
+        place_kernel,
+        out_shape=jax.ShapeDtypeStruct((plane * rows, width), piece.dtype),
+        grid_spec=pltpu.PrefetchScalarGridSpec(
+            num_scalar_prefetch=1,
+            grid=(plane,),
+            in_specs=[
+                pl.BlockSpec((1, rows, width), lambda i, to: (jnp.minimum(i, held - 1), 0, 0)),
+                pl.BlockSpec((1, rows, width), lambda i, to: (jnp.maximum(i - held, 0), 0, 0)),
+            ],
+            out_specs=pl.BlockSpec((rows, width), lambda i, to: (to[i], 0)),
+        ),
+        name="place",
+    )(where, own, got)
 
 
 def per_device(
@@ -147,26 +195,34 @@
     ring = [(i, i // half * half + (i + 1) % half) for i in range(nz)]
     swap = [(i, (i + half) % nz) for i in range(nz)]
     turn = lambda k: [(i, (i + k) % nz) for i in range(nz)]
-
-    x_blocks = [tokens]
-    for _ in range(half - 1):
-        x_blocks.append(lax.ppermute(x_blocks[-1], "tensor", ring))
+    seq_bits = [1 << b for b in range(1, nseq.bit_length() - 1)]
+    group_bits = [nseq << b for b in range(sizes["groups"].bit_length() - 1)]
 
     share = half_rows // plane
-
-    def weight_rows(first, count):
-        parts = [
-            lax.dynamic_slice_in_dim(w, first, count, axis=0)
-            for w in (q_weight, k_weight, value_weight)
-        ]
+    far_first = (1 - side) * half_rows + in_plane * share
+    near_first = side * half_rows
+
+    def weight_rows(weights, first, count):
+        parts = [lax.dynamic_slice_in_dim(w, first, count, axis=0) for w in weights]
         gains = lax.dynamic_slice_in_dim(in_gain, first, count, axis=0)
         joined = jnp.concatenate(parts, axis=1).astype(jnp.float32)
         return (joined * gains[:, None]).astype(jnp.bfloat16)
 
-    sent = weight_rows((1 - side) * half_rows + in_plane * share, share)
-    got = lax.ppermute(sent, "tensor", swap)
-    far_weight = lax.all_gather(got, PLANE, axis=0, tiled=True)
-    near_weight = weight_rows(side * half_rows, half_rows)
+    kv_weights, q_weights = (k_weight, value_weight), (q_weight,)
+    far_kv = lax.ppermute(weight_rows(kv_weights, far_first, share), "tensor", swap)
+    far_q = lax.ppermute(weight_rows(q_weights, far_first, share), "tensor", swap)
+    far_kv = spread(far_kv, plane, seq_bits + group_bits + [1])
+    far_q = spread(far_q, plane, group_bits + seq_bits + [1])
+    near_kv = weight_rows(kv_weights, near_first, half_rows)
+    near_q = weight_rows(q_weights, near_first, half_rows)
+
+    chunk = rows // CHUNKS
+    x_chunks = []
+    for c in range(CHUNKS):
+        x_blocks = [tokens[c * chunk : (c + 1) * chunk]]
+        for _ in range(half - 1):
+            x_blocks.append(lax.ppermute(x_blocks[-1], "tensor", ring))
+        x_chunks.append(x_blocks)
 
     o_rows = o_weight.shape[0]
     o_share = o_rows // plane
@@ -189,12 +245,7 @@
     token_places = seq * rows + jnp.arange(rows, dtype=jnp.int32)
     cosine, sine = rotation_table(token_places)
 
-    squares = sum(
-        jnp.sum(jnp.square(b.astype(jnp.float32)), axis=1, keepdims=True) for b in x_blocks
-    )
-    far_squares = lax.ppermute(squares, "tensor", swap)
-
-    def project(weight):
+    def project(x_blocks, weight):
         total = None
         for k, block in enumerate(x_blocks):
             source = (within + half - k) % half
@@ -203,37 +254,54 @@
             total = term if total is None else total + term
         return total
 
-    partial_far = lax.ppermute(project(far_weight).astype(jnp.bfloat16), "tensor", swap)
-    projected = project(near_weight) + partial_far.astype(jnp.float32)
-    projected = projected * lax.rsqrt((squares + far_squares) / model_width + epsilon)
-
-    q_width, k_width = q_weight.shape[1], k_weight.shape[1]
-    scale = query_scale * math.log2(math.e)
-    queries = rotate(projected[:, :q_width], cosine * scale, sine * scale).astype(jnp.bfloat16)
-    keys = rotate(projected[:, q_width : q_width + k_width], cosine, sine)
-    values = projected[:, q_width + k_width :]
-    own_kv = jnp.concatenate([keys, values], axis=1).astype(jnp.bfloat16)
-
+    squares = [
+        sum(jnp.sum(jnp.square(b.astype(jnp.float32)), axis=1) for b in x_blocks)
+        for x_blocks in x_chunks
+    ]
+    squares = jnp.concatenate(squares)
+    squares = squares + lax.ppermute(squares, "tensor", swap)
+    factor = lax.rsqrt(squares / model_width + epsilon)[:, None]
+
+    def projections(far, near):
+        sums = []
+        for x_blocks in x_chunks:
+            other = project(x_blocks, far).astype(jnp.bfloat16)
+            other = lax.ppermute(other, "tensor", swap)
+            sums.append(project(x_blocks, near) + other.astype(jnp.float32))
+        return sums
+
+    projected_kv = jnp.concatenate(projections(far_kv, near_kv), axis=0) * factor
+    k_width = k_weight.shape[1]
+    keys = rotate(projected_kv[:, :k_width], cosine, sine)
+    own_kv = jnp.concatenate([keys, projected_kv[:, k_width:]], axis=1).astype(jnp.bfloat16)
     blocks = [own_kv]
     for k in range(1, back + 1):
         blocks.insert(
             0, lax.ppermute(own_kv, "seq", [(i, i + k) for i in range(nseq - k)])
         )
-    context = attend(queries, start, blocks)
-
-    contexts = [context] + [lax.ppermute(context, "tensor", turn(k)) for k in range(1, nz)]
-    branch = jnp.dot(
-        jnp.concatenate(contexts, axis=1), o_all, preferred_element_type=jnp.float32
-    )
-    own_sq = jnp.sum(branch * branch, axis=1, keepdims=True)
-    out_sq = own_sq
-    for k in range(1, nz):
-        out_sq = out_sq + lax.ppermute(own_sq, "tensor", turn(k))
-    layer_out = (
-        tokens.astype(jnp.float32)
-        + branch * lax.rsqrt(out_sq / model_width + epsilon) * out_gain[None, :]
-    )
-    return layer_out.astype(jnp.bfloat16)
+
+    scale = query_scale * math.log2(math.e)
+    outs = []
+    for c, projected_q in enumerate(projections(far_q, near_q)):
+        at = slice(c * chunk, (c + 1) * chunk)
+        queries = rotate(projected_q * factor[at], cosine[at] * scale, sine[at] * scale)
+        context = attend(queries.astype(jnp.bfloat16), start[at], blocks, c * chunk)
+
+        contexts = [context]
+        contexts += [lax.ppermute(context, "tensor", turn(k)) for k in range(1, nz)]
+        branch = jnp.dot(
+            jnp.concatenate(contexts, axis=1), o_all, preferred_element_type=jnp.float32
+        )
+        own_sq = jnp.sum(branch * branch, axis=1)
+        out_sq = own_sq
+        for k in range(1, nz):
+            out_sq = out_sq + lax.ppermute(own_sq, "tensor", turn(k))
+        out = (
+            tokens[at].astype(jnp.float32)
+            + branch * lax.rsqrt(out_sq / model_width + epsilon)[:, None] * out_gain[None, :]
+        )
+        outs.append(out.astype(jnp.bfloat16))
+    return jnp.concatenate(outs, axis=0)
 
 
 def solution(mesh):

time: 203 us -> 204 us (level)
  the two profiles are of different devices: /device:TPU:2 before, /device:TPU:6 now
where the time goes in v2:
time: 204 us; the launch traced here: 202 us
  waiting for transfers between devices  54.6 us (27%)
  starting transfers between devices  50.2 us (25%)
  other arithmetic  22.6 us (11%)
  Pallas kernels  20.6 us (10%)
  matrix products  20.5 us (10%)
  local copies, waits for them, and re-layouts  14.3 us (7%)
  between operations  14 us (7%)
  blocking collectives  5.15 us (3%)
    ppermute x4, waiting for transfers between devices, projections(): other = lax.ppermute(other, 'tensor', swap)  17.5 us
    dot_general x16, matrix products, project(): term = jnp.dot(block, part, preferred_element_type=jnp.float32)  15.1 us
    ppermute x3, waiting for transfers between devices, per_device(): moved.append(lax.ppermute(piece, 'tensor', turn(k)))  15.1 us
    ppermute x6, starting transfers between devices, per_device(): out_sq = out_sq + lax.ppermute(own_sq, 'tensor', turn(k))  14.2 us
    pallas_call x2, Pallas kernels, spread(): pl.pallas_call(place_kernel, out_shape=jax.ShapeDtypeStruct((plane * rows...  12.1 us
    ppermute x2, waiting for transfers between devices, per_device(): lax.ppermute(own_kv, 'seq', [(i, i + k) for i in range(nseq - k)])  11.2 us
    ppermute x6, starting transfers between devices, per_device(): contexts += [lax.ppermute(context, 'tensor', turn(k)) for k in range(1, nz)]  8.87 us
    pallas_call x2, Pallas kernels, attend(): pl.pallas_call(partial(attention_kernel, back=back, group=group, offset=o...  8.53 us
  transfers between devices with their start and end apart: 33, of which 13 were waited for; matrix products, arithmetic and copies ran while one was open for 25% of the time, Pallas kernels for 10%

profile of v2, /device:TPU:6, one launch (start us, length us, event | category | flops | bytes accessed | tf_op | source)
XLA Modules:
  0.0 201.9 jit_solution(9606070175054949939)
XLA Ops:
  10.0 2.6 %collective-permute-start.1 = (bf16[288,256]{1,0:T(8,128)(2,1)}, bf16[288,256]{1,0:T(8,128)(2,1)}, u32[]{:S(2)}, u32[]{:S(2)}) collective-permute-start(bf16[288,256]{1,0:T(8,128)(2,1)} %get-tuple-element.33), channel_id=1, source_target_pairs={{0,2},{1,3},{2,0},{3,1},{4,6},{5,7},{6,4},{7,5},{8,10},{9,11},{10,... | collective-permute-start | bytes 442376 | tf_op jit(solution)/shard_map/ppermute | solution.py:213
  12.6 2.8 %fusion.89 = (bf16[384,1152]{1,0:T(8,128)(2,1)}, bf16[384,1152]{1,0:T(8,128)(2,1)}) fusion(bf16[768,1152]{1,0:T(8,128)(2,1)} %param.10), kind=kLoop, calls=%fused_computation.160 | loop fusion | bytes 3538944 | tf_op jit(solution)/shard_map/slice | solution.py:300
  19.5 2.6 %collective-permute-start.20 = (bf16[32,1152]{1,0:T(8,128)(2,1)}, bf16[32,1152]{1,0:T(8,128)(2,1)}, u32[]{:S(2)}, u32[]{:S(2)}) collective-permute-start(bf16[32,1152]{1,0:T(8,128)(2,1)} %get-tuple-element.9), channel_id=1, source_target_pairs={{0,2},{1,3},{2,0},{3,1},{4,6},{5,7},{6,4},{7,5},{8,10},{9,11},{10,... | collective-permute-start | bytes 221192 | tf_op jit(solution)/shard_map/ppermute | solution.py:235
  22.0 2.1 %constant_dynamic-slice_fusion.3 = (bf16[2304,128]{1,0:T(8,128)(2,1)}, bf16[2304,128]{1,0:T(8,128)(2,1)}) fusion(bf16[4608,128]{1,0:T(8,128)(2,1)S(1)} %copy-done.14, s32[]{:T(128)S(6)} %select_n.120, bf16[4608,128]{1,0:T(8,128)(2,1)} %param.14), kind=kLoop, calls=%fused_computation.129 | loop fusion | bytes 2359300 | tf_op jit(solution)/shard_map/dynamic_slice | solution.py:206
  24.3 3.3 %multiply_convert_fusion = (bf16[2304,256]{1,0:T(8,128)(2,1)S(1)}, bf16[2304,256]{1,0:T(8,128)(2,1)}) fusion(bf16[2304,128]{1,0:T(8,128)(2,1)} %get-tuple-element.40, bf16[2304,128]{1,0:T(8,128)(2,1)} %get-tuple-element.41, f32[2304]{0:T(1024)S(1)} %dynamic_slice.71, bf16[4608,256]{1,0:T(8,128)(2,1)} %param.13, s32[]{:T(128)S(6)} %select_n.120), kind=kLoop, calls=%fused_computation.2 | loop fusion | flops 5308416 | bytes 4727812 | tf_op jit(solution)/shard_map/convert_element_type | solution.py:209
  30.0 2.3 %fusion.60 = f32[256,384]{0,1:T(8,128)} fusion(bf16[2304,256]{1,0:T(8,128)(2,1)} %get-tuple-element.25, s32[]{:T(128)S(6)} %select_n.123, bf16[768,1152]{1,0:T(8,128)(2,1)S(1)} %copy-done), kind=kOutput, calls=%fused_computation.86 | convolution fusion | flops 226492416 | bytes 1867780 | tf_op jit(solution)/shard_map/dot_general | solution.py:253
  34.7 5.1 %all-gather = s32[4,1,768]{2,1,0:T(1,128)S(1)} all-gather(s32[1,1,768]{2,1,0:T(1,128)S(1)} %reshape.27), channel_id=1, replica_groups=mesh['groups'=2,'seq'=4,'tensor'=4] {'seq'}, dimensions={0}, use_global_device_ids=true | all-gather | bytes 15360 | tf_op jit(solution)/shard_map/all_gather | solution.py:241
  41.6 1.9 constant_dynamic-slice_fusion
  47.5 12.4 %collective-permute-done.20 = bf16[32,1152]{1,0:T(8,128)(2,1)} collective-permute-done((bf16[32,1152]{1,0:T(8,128)(2,1)}, bf16[32,1152]{1,0:T(8,128)(2,1)}, u32[]{:S(2)}, u32[]{:S(2)}) %collective-permute-start.20) | collective-permute-done | bytes 73760 | tf_op jit(solution)/shard_map/ppermute | solution.py:235
  60.1 1.9 collective-permute-start.19
  65.7 2.4 %collective-permute-done.19 = bf16[32,1152]{1,0:T(8,128)(2,1)S(1)} collective-permute-done((bf16[32,1152]{1,0:T(8,128)(2,1)}, bf16[32,1152]{1,0:T(8,128)(2,1)S(1)}, u32[]{:S(2)}, u32[]{:S(2)}) %collective-permute-start.19) | collective-permute-done | bytes 73760 | tf_op jit(solution)/shard_map/ppermute | solution.py:235
  76.4 3.4 %collective-permute-start.7 = (f32[768]{0:T(1024)S(1)}, f32[768]{0:T(1024)S(1)}, u32[]{:S(2)}, u32[]{:S(2)}) collective-permute-start(f32[768]{0:T(1024)S(1)} %pad_maximum_fusion.12), channel_id=1, source_target_pairs={{0,2},{1,3},{2,0},{3,1},{4,6},{5,7},{6,4},{7,5},{8,10},{9,11},{10,... | collective-permute-start | bytes 9224 | tf_op jit(solution)/shard_map/ppermute | solution.py:262
  79.8 1.9 pad_maximum_fusion.5.own_ref
  83.1 6.0 %place.2 = bf16[2304,256]{1,0:T(8,128)(2,1)} custom-call(s32[8]{0:T(128)} %broadcast_xor_fusion.1.where_ref, bf16[4,288,256]{2,1,0:T(8,128)(2,1)} %copy-done.8, bf16[4,288,256]{2,1,0:T(8,128)(2,1)} %collective-permute-done.4.got_ref), custom_call_target="tpu_custom_call" | custom-call | tf_op jit(solution)/shard_map/place/pallas_call | solution.py:165
  91.9 4.3 %collective-permute-start.25 = (bf16[384,256]{1,0:T(8,128)(2,1)}, bf16[384,256]{1,0:T(8,128)(2,1)}, u32[]{:S(2)}, u32[]{:S(2)}) collective-permute-start(bf16[384,256]{1,0:T(8,128)(2,1)} %fusion.20), channel_id=1, source_target_pairs={{0,2},{1,3},{2,0},{3,1},{4,6},{5,7},{6,4},{7,5},{8,10},{9,11},{10,... | collective-permute-start | bytes 589832 | tf_op jit(solution)/shard_map/ppermute | solution.py:269
  96.3 6.0 %place.3 = bf16[2304,256]{1,0:T(8,128)(2,1)} custom-call(s32[8]{0:T(128)} %broadcast_xor_fusion.where_ref, bf16[4,288,256]{2,1,0:T(8,128)(2,1)} %pad_maximum_fusion.5.own_ref, bf16[4,288,256]{2,1,0:T(8,128)(2,1)} %collective-permute-done.11.got_ref), custom_call_target="tpu_custom_call" | custom-call | tf_op jit(solution)/shard_map/place/pallas_call | solution.py:165
  105.4 3.0 %collective-permute-start.13 = (bf16[384,256]{1,0:T(8,128)(2,1)S(1)}, bf16[384,256]{1,0:T(8,128)(2,1)S(1)}, u32[]{:S(2)}, u32[]{:S(2)}) collective-permute-start(bf16[384,256]{1,0:T(8,128)(2,1)S(1)} %fusion.21), channel_id=1, source_target_pairs={{0,2},{1,3},{2,0},{3,1},{4,6},{5,7},{6,4},{7,5},{8,10},{9,11},{10,... | collective-permute-start | bytes 589832 | tf_op jit(solution)/shard_map/ppermute | solution.py:269
  109.3 13.7 %collective-permute-done.12 = bf16[384,256]{1,0:T(8,128)(2,1)S(1)} collective-permute-done((bf16[384,256]{1,0:T(8,128)(2,1)S(1)}, bf16[384,256]{1,0:T(8,128)(2,1)S(1)}, u32[]{:S(2)}, u32[]{:S(2)}) %collective-permute-start.12) | collective-permute-done | bytes 196640 | tf_op jit(solution)/shard_map/ppermute | solution.py:269
  123.5 3.7 %collective-permute-done.13 = bf16[384,256]{1,0:T(8,128)(2,1)S(1)} collective-permute-done((bf16[384,256]{1,0:T(8,128)(2,1)S(1)}, bf16[384,256]{1,0:T(8,128)(2,1)S(1)}, u32[]{:S(2)}, u32[]{:S(2)}) %collective-permute-start.13) | collective-permute-done | bytes 196640 | tf_op jit(solution)/shard_map/ppermute | solution.py:269
  131.3 2.2 %collective-permute-start.15 = (bf16[768,256]{1,0:T(8,128)(2,1)S(1)}, bf16[768,256]{1,0:T(8,128)(2,1)S(1)}, u32[]{:S(2)}, u32[]{:S(2)}) collective-permute-start(bf16[768,256]{1,0:T(8,128)(2,1)S(1)} %pad_maximum_fusion.6.rest_2_), channel_id=1, source_target_pairs={{0,4},{4,8},{8,12},{1,5},{5,9},{9,13},{2,6},{6,10},{10,14},{3,7},{... | collective-permute-start | bytes 1179656 | tf_op jit(solution)/shard_map/ppermute | solution.py:280
  136.0 7.9 %collective-permute-done.14.rest_0_ = bf16[768,256]{1,0:T(8,128)(2,1)S(1)} collective-permute-done((bf16[768,256]{1,0:T(8,128)(2,1)S(1)}, bf16[768,256]{1,0:T(8,128)(2,1)S(1)}, u32[]{:S(2)}, u32[]{:S(2)}) %collective-permute-start.14) | collective-permute-done | bytes 393248 | tf_op jit(solution)/shard_map/ppermute | solution.py:280
  143.9 3.4 %collective-permute-done.15.rest_1_ = bf16[768,256]{1,0:T(8,128)(2,1)S(1)} collective-permute-done((bf16[768,256]{1,0:T(8,128)(2,1)S(1)}, bf16[768,256]{1,0:T(8,128)(2,1)S(1)}, u32[]{:S(2)}, u32[]{:S(2)}) %collective-permute-start.15) | collective-permute-done | bytes 393248 | tf_op jit(solution)/shard_map/ppermute | solution.py:280
  147.2 4.8 %attend.3 = bf16[384,256]{1,0:T(8,128)(2,1)S(1)} custom-call(s32[3]{0:T(128)S(1)} %get-tuple-element.38.lo_ref, bf16[384,256]{1,0:T(8,128)(2,1)S(1)} %pad_maximum_fusion.11.q_ref, s32[1,384]{1,0:T(1,128)S(1)} %broadcast_in_dim.11.start_ref, bf16[768,256]{1,0:T(8,128)(2,1)S(1)} %collective-permute-done.14.rest_0_, ...), custom_call_target="tpu_custom_call" | custom-call | flops 452984832 | bytes 393216 | tf_op jit(solution)/shard_map/attend/pallas_call | solution.py:116
  152.1 2.4 %collective-permute-start.27 = (bf16[384,256]{1,0:T(8,128)(2,1)S(1)}, bf16[384,256]{1,0:T(8,128)(2,1)S(1)}, u32[]{:S(2)}, u32[]{:S(2)}) collective-permute-start(bf16[384,256]{1,0:T(8,128)(2,1)S(1)} %attend.3), channel_id=1, source_target_pairs={{0,2},{1,3},{2,0},{3,1},{4,6},{5,7},{6,4},{7,5},{8,10},{9,11},{10,... | collective-permute-start | bytes 589832 | tf_op jit(solution)/shard_map/ppermute | solution.py:291
  156.5 3.7 %attend.2 = bf16[384,256]{1,0:T(8,128)(2,1)S(1)} custom-call(s32[3]{0:T(128)S(1)} %get-tuple-element.39.lo_ref, bf16[384,256]{1,0:T(8,128)(2,1)S(1)} %pad_maximum_fusion.10.q_ref, s32[1,384]{1,0:T(1,128)S(1)} %broadcast_in_dim.9.start_ref, bf16[768,256]{1,0:T(8,128)(2,1)S(1)} %collective-permute-done.14.rest_0_, ...), custom_call_target="tpu_custom_call" | custom-call | flops 452984832 | bytes 393216 | tf_op jit(solution)/shard_map/attend/pallas_call | solution.py:116
  162.4 2.8 %collective-permute-start.18 = (bf16[384,256]{1,0:T(8,128)(2,1)S(1)}, bf16[384,256]{1,0:T(8,128)(2,1)}, u32[]{:S(2)}, u32[]{:S(2)}) collective-permute-start(bf16[384,256]{1,0:T(8,128)(2,1)S(1)} %attend.2), channel_id=1, source_target_pairs={{0,3},{1,0},{2,1},{3,2},{4,7},{5,4},{6,5},{7,6},{8,11},{9,8},{10,9... | collective-permute-start | bytes 589832 | tf_op jit(solution)/shard_map/ppermute | solution.py:291
  165.2 6.0 %collective-permute-done.27 = bf16[384,256]{1,0:T(8,128)(2,1)S(1)} collective-permute-done((bf16[384,256]{1,0:T(8,128)(2,1)S(1)}, bf16[384,256]{1,0:T(8,128)(2,1)S(1)}, u32[]{:S(2)}, u32[]{:S(2)}) %collective-permute-start.27) | collective-permute-done | bytes 196640 | tf_op jit(solution)/shard_map/ppermute | solution.py:291
  171.3 3.1 %multiply_reduce_fusion = (f32[384]{0:T(512)S(1)}, f32[384,1152]{1,0:T(8,128)S(1)}) fusion(bf16[768,1152]{1,0:T(8,128)(2,1)} %bitcast.46, bf16[256,1152]{1,0:T(8,128)(2,1)} %constant_dynamic-slice_fusion, bf16[384,256]{1,0:T(8,128)(2,1)} %collective-permute-done.28, bf16[384,256]{1,0:T(8,128)(2,1)S(1)} %collective-permute-done.27, ...), kind=kOutput, calls=%fused_computation.13 | convolution fusion | flops 914718336 | bytes 4916736 | tf_op jit(solution)/shard_map/dot_general | solution.py:292
  174.4 7.4 %collective-permute-start.29 = (f32[384]{0:T(512)S(1)}, f32[384]{0:T(512)S(1)}, u32[]{:S(2)}, u32[]{:S(2)}) collective-permute-start(f32[384]{0:T(512)S(1)} %get-tuple-element.36), channel_id=1, source_target_pairs={{0,1},{1,2},{2,3},{3,0},{4,5},{5,6},{6,7},{7,4},{8,9},{9,10},{10,1... | collective-permute-start | bytes 4616 | tf_op jit(solution)/shard_map/ppermute | solution.py:298
  181.8 2.1 %collective-permute-start.30 = (f32[384]{0:T(512)S(1)}, f32[384]{0:T(512)S(1)}, u32[]{:S(2)}, u32[]{:S(2)}) collective-permute-start(f32[384]{0:T(512)S(1)} %get-tuple-element.36), channel_id=1, source_target_pairs={{0,2},{1,3},{2,0},{3,1},{4,6},{5,7},{6,4},{7,5},{8,10},{9,11},{10,... | collective-permute-start | bytes 4616 | tf_op jit(solution)/shard_map/ppermute | solution.py:298
  184.3 2.3 %multiply_reduce_fusion.1 = (f32[384]{0:T(512)S(1)}, f32[384,1152]{1,0:T(8,128)S(1)}) fusion(bf16[768,1152]{1,0:T(8,128)(2,1)S(1)} %bitcast.47, bf16[256,1152]{1,0:T(8,128)(2,1)S(1)} %copy-done.9, bf16[384,256]{1,0:T(8,128)(2,1)} %collective-permute-done.18, bf16[384,256]{1,0:T(8,128)(2,1)} %collective-permute-done.17, ...), kind=kOutput, calls=%fused_computation.14 | convolution fusion | flops 914718336 | bytes 4916736 | tf_op jit(solution)/shard_map/dot_general | solution.py:292
  186.6 1.9 collective-permute-start.22
  (167 shorter events, 56.0 us)
Async XLA Ops:
  6.5 164.7 %all-gather.3.cloned.1.call-start = ((), (), s32[]{:S(2)}) async-start(), calls=%async_computation | async-start | bytes 1990656 | tf_op jit(solution)/shard_map/all_gather | solution.py:236
  10.0 35.1 %collective-permute-start.1 = (bf16[288,256]{1,0:T(8,128)(2,1)}, bf16[288,256]{1,0:T(8,128)(2,1)}, u32[]{:S(2)}, u32[]{:S(2)}) collective-permute-start(bf16[288,256]{1,0:T(8,128)(2,1)} %get-tuple-element.33), channel_id=1, source_target_pairs={{0,2},{1,3},{2,0},{3,1},{4,6},{5,7},{6,4},{7,5},{8,10},{9,11},{10,... | collective-permute-start | bytes 442376 | tf_op jit(solution)/shard_map/ppermute | solution.py:213
  15.4 60.6 %collective-permute-start.6 = (bf16[384,1152]{1,0:T(8,128)(2,1)}, bf16[384,1152]{1,0:T(8,128)(2,1)S(1)}, u32[]{:S(2)}, u32[]{:S(2)}) collective-permute-start(bf16[384,1152]{1,0:T(8,128)(2,1)} %get-tuple-element.13), channel_id=1, source_target_pairs={{0,1},{1,0},{2,3},{3,2},{4,5},{5,4},{6,7},{7,6},{8,9},{9,8},{10,11... | collective-permute-start | bytes 2654216 | tf_op jit(solution)/shard_map/ppermute | solution.py:224
  17.0 58.1 %collective-permute-start = (bf16[384,1152]{1,0:T(8,128)(2,1)}, bf16[384,1152]{1,0:T(8,128)(2,1)S(1)}, u32[]{:S(2)}, u32[]{:S(2)}) collective-permute-start(bf16[384,1152]{1,0:T(8,128)(2,1)} %get-tuple-element.12), channel_id=1, source_target_pairs={{0,1},{1,0},{2,3},{3,2},{4,5},{5,4},{6,7},{7,6},{8,9},{9,8},{10,11... | collective-permute-start | bytes 2654216 | tf_op jit(solution)/shard_map/ppermute | solution.py:224
  17.5 46.2 %collective-permute-start.8 = (bf16[288,256]{1,0:T(8,128)(2,1)}, bf16[288,256]{1,0:T(8,128)(2,1)}, u32[]{:S(2)}, u32[]{:S(2)}) collective-permute-start(bf16[288,256]{1,0:T(8,128)(2,1)} %get-tuple-element.32), channel_id=1, source_target_pairs={{0,2},{1,3},{2,0},{3,1},{4,6},{5,7},{6,4},{7,5},{8,10},{9,11},{10,... | collective-permute-start | bytes 442376 | tf_op jit(solution)/shard_map/ppermute | solution.py:212
  19.5 40.4 %collective-permute-start.20 = (bf16[32,1152]{1,0:T(8,128)(2,1)}, bf16[32,1152]{1,0:T(8,128)(2,1)}, u32[]{:S(2)}, u32[]{:S(2)}) collective-permute-start(bf16[32,1152]{1,0:T(8,128)(2,1)} %get-tuple-element.9), channel_id=1, source_target_pairs={{0,2},{1,3},{2,0},{3,1},{4,6},{5,7},{6,4},{7,5},{8,10},{9,11},{10,... | collective-permute-start | bytes 221192 | tf_op jit(solution)/shard_map/ppermute | solution.py:235
  45.2 14.9 %collective-permute-start.2 = (bf16[1,288,256]{2,1,0:T(8,128)(2,1)}, bf16[1,288,256]{2,1,0:T(8,128)(2,1)}, u32[]{:S(2)}, u32[]{:S(2)}) collective-permute-start(bf16[1,288,256]{2,1,0:T(8,128)(2,1)} %bitcast.2), channel_id=1, source_target_pairs={{0,16},{4,20},{8,24},{12,28},{16,0},{20,4},{24,8},{28,12},{1,17},{... | collective-permute-start | bytes 442376 | tf_op jit(solution)/shard_map/ppermute | solution.py:158
  59.9 4.6 %collective-permute-start.21 = (bf16[32,1152]{1,0:T(8,128)(2,1)}, bf16[32,1152]{1,0:T(8,128)(2,1)S(1)}, u32[]{:S(2)}, u32[]{:S(2)}) collective-permute-start(bf16[32,1152]{1,0:T(8,128)(2,1)} %get-tuple-element.8), channel_id=1, source_target_pairs={{0,3},{1,0},{2,1},{3,2},{4,7},{5,4},{6,5},{7,6},{8,11},{9,8},{10,9... | collective-permute-start | bytes 221192 | tf_op jit(solution)/shard_map/ppermute | solution.py:235
  60.1 8.0 %collective-permute-start.19 = (bf16[32,1152]{1,0:T(8,128)(2,1)}, bf16[32,1152]{1,0:T(8,128)(2,1)S(1)}, u32[]{:S(2)}, u32[]{:S(2)}) collective-permute-start(bf16[32,1152]{1,0:T(8,128)(2,1)} %get-tuple-element.7), channel_id=1, source_target_pairs={{0,1},{1,2},{2,3},{3,0},{4,5},{5,6},{6,7},{7,4},{8,9},{9,10},{10,1... | collective-permute-start | bytes 221192 | tf_op jit(solution)/shard_map/ppermute | solution.py:235
  63.7 7.1 %collective-permute-start.9 = (bf16[1,288,256]{2,1,0:T(8,128)(2,1)}, bf16[1,288,256]{2,1,0:T(8,128)(2,1)}, u32[]{:S(2)}, u32[]{:S(2)}) collective-permute-start(bf16[1,288,256]{2,1,0:T(8,128)(2,1)} %bitcast.5), channel_id=1, source_target_pairs={{0,8},{4,12},{8,0},{12,4},{16,24},{20,28},{24,16},{28,20},{1,9},{5... | collective-permute-start | bytes 442376 | tf_op jit(solution)/shard_map/ppermute | solution.py:158
  64.5 9.4 %collective-permute-start.3 = (bf16[2,288,256]{2,1,0:T(8,128)(2,1)}, bf16[2,288,256]{2,1,0:T(8,128)(2,1)}, u32[]{:S(2)}, u32[]{:S(2)}) collective-permute-start(bf16[2,288,256]{2,1,0:T(8,128)(2,1)} %pad_maximum_fusion.7), channel_id=1, source_target_pairs={{0,8},{4,12},{8,0},{12,4},{16,24},{20,28},{24,16},{28,20},{1,9},{5... | collective-permute-start | bytes 884744 | tf_op jit(solution)/shard_map/ppermute | solution.py:158
  71.8 8.0 %collective-permute-start.10 = (bf16[2,288,256]{2,1,0:T(8,128)(2,1)S(1)}, bf16[2,288,256]{2,1,0:T(8,128)(2,1)S(1)}, u32[]{:S(2)}, u32[]{:S(2)}) collective-permute-start(bf16[2,288,256]{2,1,0:T(8,128)(2,1)S(1)} %pad_maximum_fusion.8), channel_id=1, source_target_pairs={{0,16},{4,20},{8,24},{12,28},{16,0},{20,4},{24,8},{28,12},{1,17},{... | collective-permute-start | bytes 884744 | tf_op jit(solution)/shard_map/ppermute | solution.py:158
  75.1 8.1 %collective-permute-start.4 = (bf16[4,288,256]{2,1,0:T(8,128)(2,1)S(1)}, bf16[4,288,256]{2,1,0:T(8,128)(2,1)}, u32[]{:S(2)}, u32[]{:S(2)}) collective-permute-start(bf16[4,288,256]{2,1,0:T(8,128)(2,1)S(1)} %pad_maximum_fusion.4.own_ref), channel_id=1, source_target_pairs={{0,4},{4,0},{8,12},{12,8},{16,20},{20,16},{24,28},{28,24},{1,5},{5... | collective-permute-start | bytes 1769480 | tf_op jit(solution)/shard_map/ppermute | solution.py:158
  76.4 5.6 %collective-permute-start.7 = (f32[768]{0:T(1024)S(1)}, f32[768]{0:T(1024)S(1)}, u32[]{:S(2)}, u32[]{:S(2)}) collective-permute-start(f32[768]{0:T(1024)S(1)} %pad_maximum_fusion.12), channel_id=1, source_target_pairs={{0,2},{1,3},{2,0},{3,1},{4,6},{5,7},{6,4},{7,5},{8,10},{9,11},{10,... | collective-permute-start | bytes 9224 | tf_op jit(solution)/shard_map/ppermute | solution.py:262
  81.7 14.6 %collective-permute-start.11 = (bf16[4,288,256]{2,1,0:T(8,128)(2,1)}, bf16[4,288,256]{2,1,0:T(8,128)(2,1)}, u32[]{:S(2)}, u32[]{:S(2)}) collective-permute-start(bf16[4,288,256]{2,1,0:T(8,128)(2,1)} %pad_maximum_fusion.5.own_ref), channel_id=1, source_target_pairs={{0,4},{4,0},{8,12},{12,8},{16,20},{20,16},{24,28},{28,24},{1,5},{5... | collective-permute-start | bytes 1769480 | tf_op jit(solution)/shard_map/ppermute | solution.py:158
  91.9 41.6 %collective-permute-start.25 = (bf16[384,256]{1,0:T(8,128)(2,1)}, bf16[384,256]{1,0:T(8,128)(2,1)}, u32[]{:S(2)}, u32[]{:S(2)}) collective-permute-start(bf16[384,256]{1,0:T(8,128)(2,1)} %fusion.20), channel_id=1, source_target_pairs={{0,2},{1,3},{2,0},{3,1},{4,6},{5,7},{6,4},{7,5},{8,10},{9,11},{10,... | collective-permute-start | bytes 589832 | tf_op jit(solution)/shard_map/ppermute | solution.py:269
  104.4 18.7 %collective-permute-start.12 = (bf16[384,256]{1,0:T(8,128)(2,1)S(1)}, bf16[384,256]{1,0:T(8,128)(2,1)S(1)}, u32[]{:S(2)}, u32[]{:S(2)}) collective-permute-start(bf16[384,256]{1,0:T(8,128)(2,1)S(1)} %fusion.22), channel_id=1, source_target_pairs={{0,2},{1,3},{2,0},{3,1},{4,6},{5,7},{6,4},{7,5},{8,10},{9,11},{10,... | collective-permute-start | bytes 589832 | tf_op jit(solution)/shard_map/ppermute | solution.py:269
  105.4 21.9 %collective-permute-start.13 = (bf16[384,256]{1,0:T(8,128)(2,1)S(1)}, bf16[384,256]{1,0:T(8,128)(2,1)S(1)}, u32[]{:S(2)}, u32[]{:S(2)}) collective-permute-start(bf16[384,256]{1,0:T(8,128)(2,1)S(1)} %fusion.21), channel_id=1, source_target_pairs={{0,2},{1,3},{2,0},{3,1},{4,6},{5,7},{6,4},{7,5},{8,10},{9,11},{10,... | collective-permute-start | bytes 589832 | tf_op jit(solution)/shard_map/ppermute | solution.py:269
  109.2 26.3 %collective-permute-start.5 = (bf16[384,256]{1,0:T(8,128)(2,1)S(1)}, bf16[384,256]{1,0:T(8,128)(2,1)S(1)}, u32[]{:S(2)}, u32[]{:S(2)}) collective-permute-start(bf16[384,256]{1,0:T(8,128)(2,1)S(1)} %fusion.23), channel_id=1, source_target_pairs={{0,2},{1,3},{2,0},{3,1},{4,6},{5,7},{6,4},{7,5},{8,10},{9,11},{10,... | collective-permute-start | bytes 589832 | tf_op jit(solution)/shard_map/ppermute | solution.py:269
  130.0 13.9 %collective-permute-start.14 = (bf16[768,256]{1,0:T(8,128)(2,1)S(1)}, bf16[768,256]{1,0:T(8,128)(2,1)S(1)}, u32[]{:S(2)}, u32[]{:S(2)}) collective-permute-start(bf16[768,256]{1,0:T(8,128)(2,1)S(1)} %pad_maximum_fusion.6.rest_2_), channel_id=1, source_target_pairs={{0,8},{4,12},{1,9},{5,13},{2,10},{6,14},{3,11},{7,15},{16,24},{20,... | collective-permute-start | bytes 1179656 | tf_op jit(solution)/shard_map/ppermute | solution.py:280
  131.3 15.9 %collective-permute-start.15 = (bf16[768,256]{1,0:T(8,128)(2,1)S(1)}, bf16[768,256]{1,0:T(8,128)(2,1)S(1)}, u32[]{:S(2)}, u32[]{:S(2)}) collective-permute-start(bf16[768,256]{1,0:T(8,128)(2,1)S(1)} %pad_maximum_fusion.6.rest_2_), channel_id=1, source_target_pairs={{0,4},{4,8},{8,12},{1,5},{5,9},{9,13},{2,6},{6,10},{10,14},{3,7},{... | collective-permute-start | bytes 1179656 | tf_op jit(solution)/shard_map/ppermute | solution.py:280
  152.1 10.3 %collective-permute-start.26 = (bf16[384,256]{1,0:T(8,128)(2,1)S(1)}, bf16[384,256]{1,0:T(8,128)(2,1)S(1)}, u32[]{:S(2)}, u32[]{:S(2)}) collective-permute-start(bf16[384,256]{1,0:T(8,128)(2,1)S(1)} %attend.3), channel_id=1, source_target_pairs={{0,1},{1,2},{2,3},{3,0},{4,5},{5,6},{6,7},{7,4},{8,9},{9,10},{10,1... | collective-permute-start | bytes 589832 | tf_op jit(solution)/shard_map/ppermute | solution.py:291
  152.1 19.1 %collective-permute-start.27 = (bf16[384,256]{1,0:T(8,128)(2,1)S(1)}, bf16[384,256]{1,0:T(8,128)(2,1)S(1)}, u32[]{:S(2)}, u32[]{:S(2)}) collective-permute-start(bf16[384,256]{1,0:T(8,128)(2,1)S(1)} %attend.3), channel_id=1, source_target_pairs={{0,2},{1,3},{2,0},{3,1},{4,6},{5,7},{6,4},{7,5},{8,10},{9,11},{10,... | collective-permute-start | bytes 589832 | tf_op jit(solution)/shard_map/ppermute | solution.py:291
  154.6 16.7 %collective-permute-start.28 = (bf16[384,256]{1,0:T(8,128)(2,1)S(1)}, bf16[384,256]{1,0:T(8,128)(2,1)}, u32[]{:S(2)}, u32[]{:S(2)}) collective-permute-start(bf16[384,256]{1,0:T(8,128)(2,1)S(1)} %attend.3), channel_id=1, source_target_pairs={{0,3},{1,0},{2,1},{3,2},{4,7},{5,4},{6,5},{7,6},{8,11},{9,8},{10,9... | collective-permute-start | bytes 589832 | tf_op jit(solution)/shard_map/ppermute | solution.py:291
  160.2 23.7 %collective-permute-start.16 = (bf16[384,256]{1,0:T(8,128)(2,1)S(1)}, bf16[384,256]{1,0:T(8,128)(2,1)S(1)}, u32[]{:S(2)}, u32[]{:S(2)}) collective-permute-start(bf16[384,256]{1,0:T(8,128)(2,1)S(1)} %attend.2), channel_id=1, source_target_pairs={{0,1},{1,2},{2,3},{3,0},{4,5},{5,6},{6,7},{7,4},{8,9},{9,10},{10,1... | collective-permute-start | bytes 589832 | tf_op jit(solution)/shard_map/ppermute | solution.py:291
  160.9 23.4 %collective-permute-start.17 = (bf16[384,256]{1,0:T(8,128)(2,1)S(1)}, bf16[384,256]{1,0:T(8,128)(2,1)}, u32[]{:S(2)}, u32[]{:S(2)}) collective-permute-start(bf16[384,256]{1,0:T(8,128)(2,1)S(1)} %attend.2), channel_id=1, source_target_pairs={{0,2},{1,3},{2,0},{3,1},{4,6},{5,7},{6,4},{7,5},{8,10},{9,11},{10,... | collective-permute-start | bytes 589832 | tf_op jit(solution)/shard_map/ppermute | solution.py:291
  162.4 21.9 %collective-permute-start.18 = (bf16[384,256]{1,0:T(8,128)(2,1)S(1)}, bf16[384,256]{1,0:T(8,128)(2,1)}, u32[]{:S(2)}, u32[]{:S(2)}) collective-permute-start(bf16[384,256]{1,0:T(8,128)(2,1)S(1)} %attend.2), channel_id=1, source_target_pairs={{0,3},{1,0},{2,1},{3,2},{4,7},{5,4},{6,5},{7,6},{8,11},{9,8},{10,9... | collective-permute-start | bytes 589832 | tf_op jit(solution)/shard_map/ppermute | solution.py:291
  174.4 15.1 %collective-permute-start.29 = (f32[384]{0:T(512)S(1)}, f32[384]{0:T(512)S(1)}, u32[]{:S(2)}, u32[]{:S(2)}) collective-permute-start(f32[384]{0:T(512)S(1)} %get-tuple-element.36), channel_id=1, source_target_pairs={{0,1},{1,2},{2,3},{3,0},{4,5},{5,6},{6,7},{7,4},{8,9},{9,10},{10,1... | collective-permute-start | bytes 4616 | tf_op jit(solution)/shard_map/ppermute | solution.py:298
  181.8 9.2 %collective-permute-start.30 = (f32[384]{0:T(512)S(1)}, f32[384]{0:T(512)S(1)}, u32[]{:S(2)}, u32[]{:S(2)}) collective-permute-start(f32[384]{0:T(512)S(1)} %get-tuple-element.36), channel_id=1, source_target_pairs={{0,2},{1,3},{2,0},{3,1},{4,6},{5,7},{6,4},{7,5},{8,10},{9,11},{10,... | collective-permute-start | bytes 4616 | tf_op jit(solution)/shard_map/ppermute | solution.py:298
  183.9 7.0 %collective-permute-start.31 = (f32[384]{0:T(512)S(1)}, f32[384]{0:T(512)S(1)}, u32[]{:S(2)}, u32[]{:S(2)}) collective-permute-start(f32[384]{0:T(512)S(1)} %get-tuple-element.36), channel_id=1, source_target_pairs={{0,3},{1,0},{2,1},{3,2},{4,7},{5,4},{6,5},{7,6},{8,11},{9,8},{10,9... | collective-permute-start | bytes 4616 | tf_op jit(solution)/shard_map/ppermute | solution.py:298
  186.6 5.4 %collective-permute-start.22 = (f32[384]{0:T(512)S(1)}, f32[384]{0:T(512)S(1)}, u32[]{:S(2)}, u32[]{:S(2)}) collective-permute-start(f32[384]{0:T(512)S(1)} %get-tuple-element.34), channel_id=1, source_target_pairs={{0,1},{1,2},{2,3},{3,0},{4,5},{5,6},{6,7},{7,4},{8,9},{9,10},{10,1... | collective-permute-start | bytes 4616 | tf_op jit(solution)/shard_map/ppermute | solution.py:298
  188.5 4.5 %collective-permute-start.23 = (f32[384]{0:T(512)S(1)}, f32[384]{0:T(512)S(1)}, u32[]{:S(2)}, u32[]{:S(2)}) collective-permute-start(f32[384]{0:T(512)S(1)} %get-tuple-element.34), channel_id=1, source_target_pairs={{0,2},{1,3},{2,0},{3,1},{4,6},{5,7},{6,4},{7,5},{8,10},{9,11},{10,... | collective-permute-start | bytes 4616 | tf_op jit(solution)/shard_map/ppermute | solution.py:298
  (32 other events, 211.6 us)
Sparse Core Ops, SparseCore 0:
  69.8 24.7 all-gather.2

commit v3 on v1

v3 whole, which is shorter than its diff:
```python
import math
from functools import partial

import jax
import jax.numpy as jnp
from jax import lax
from jax.experimental import pallas as pl
from jax.experimental.pallas import tpu as pltpu
from jax.sharding import PartitionSpec as P

HEAD_SIZE = 128
PLANE = ("groups", "seq")

epsilon = 1e-06
query_scale = 144.0 ** (-0.5)
rope_base = 10000.0
NEG = -1e30
Q_TILE = 128
K_TILE = 256
CHUNKS = 2
LANES = 128
TAIL = 16
F32, BF16 = jnp.float32, jnp.bfloat16
ANY = pl.BlockSpec(memory_space=pl.ANY)
HBM = pl.BlockSpec(memory_space=pltpu.HBM)
PARAMS = pltpu.CompilerParams(vmem_limit_bytes=48 * 1024 * 1024)


def shape(dims, dtype):
    return jax.ShapeDtypeStruct(dims, dtype)


def to_row(column):
    return jnp.broadcast_to(column, (column.shape[0], LANES)).T[0:1, :]


def to_column(row):
    return jnp.broadcast_to(row, (LANES, row.shape[1])).T


def rotation_table(token_places):
    half_dim = HEAD_SIZE // 2
    inverse = rope_base ** (-jnp.arange(half_dim, dtype=F32) / half_dim)
    angles = token_places.astype(F32)[:, None] * inverse[None, :]
    cosine, sine = jnp.cos(angles), jnp.sin(angles)
    return jnp.concatenate([cosine, cosine], 1), jnp.concatenate([-sine, sine], 1)


def rotate(vectors, cosine, sine):
    return vectors * cosine + pltpu.roll(vectors, HEAD_SIZE // 2, 1) * sine


def pack_kernel(at_ref, q_ref, k_ref, v_ref, kv_out, q_out, sems):
    share, width = q_out.shape[0], k_ref.shape[1]
    rows = pl.ds(pl.multiple_of(at_ref[0] * share, TAIL), share)
    copies = [
        pltpu.make_async_copy(k_ref.at[rows], kv_out.at[:, pl.ds(0, width)], sems.at[0]),
        pltpu.make_async_copy(v_ref.at[rows], kv_out.at[:, pl.ds(width, width)], sems.at[1]),
        pltpu.make_async_copy(q_ref.at[rows], q_out, sems.at[2]),
    ]
    for copy in copies:
        copy.start()
    for copy in copies:
        copy.wait()


def pack(at, q_weight, k_weight, v_weight, share):
    kv_width = k_weight.shape[1] + v_weight.shape[1]
    return pl.pallas_call(
        pack_kernel,
        out_shape=(shape((share, kv_width), BF16), shape((share, q_weight.shape[1]), BF16)),
        grid_spec=pltpu.PrefetchScalarGridSpec(
            num_scalar_prefetch=1,
            grid=(1,),
            in_specs=[HBM, HBM, HBM],
            out_specs=[ANY, ANY],
            scratch_shapes=[pltpu.SemaphoreType.DMA((3,))],
        ),
        compiler_params=pltpu.CompilerParams(vmem_limit_bytes=62 * 1024 * 1024),
        name="pack",
    )(at, q_weight, k_weight, v_weight)


def join_kernel(first_ref, second_ref, out_ref, sems):
    held = first_ref.shape[0]
    copies = [
        pltpu.make_async_copy(first_ref, out_ref.at[pl.ds(0, held)], sems.at[0]),
        pltpu.make_async_copy(second_ref, out_ref.at[pl.ds(held, held)], sems.at[1]),
    ]
    for copy in copies:
        copy.start()
    for copy in copies:
        copy.wait()


def join(first, second):
    return pl.pallas_call(
        join_kernel,
        out_shape=shape((2 * first.shape[0],) + first.shape[1:], first.dtype),
        in_specs=[ANY, ANY],
        out_specs=ANY,
        scratch_shapes=[pltpu.SemaphoreType.DMA((2,))],
        compiler_params=PARAMS,
        name="join",
    )(first, second)


def spread(piece, plane, masks):
    own = piece[None]
    order = [0]
    for mask in masks:
        got = lax.ppermute(own, PLANE, [(i, i ^ mask) for i in range(plane)])
        order = order + [k ^ mask for k in order]
        if mask != masks[-1]:
            own = join(own, got)
    where = jnp.bitwise_xor(lax.axis_index(PLANE), jnp.array(order, jnp.int32))
    return where, own, got


def prep_kernel(src_ref, gain_ref, *rest):
    x_refs, (out_ref, sq_ref) = rest[:-2], rest[-2:]
    total = 0.0
    for k, x_ref in enumerate(x_refs):
        x = x_ref[...].astype(F32)
        total = total + jnp.sum(x * x, axis=1, keepdims=True)
        out_ref[k] = (x * gain_ref[src_ref[k]]).astype(BF16)
    sq_ref[...] = to_row(total)


def prep(sources, gains, tokens, received, chunk, c):
    count, (nz, _, cols) = len(received) + 1, gains.shape
    return pl.pallas_call(
        prep_kernel,
        out_shape=(shape((count, chunk, cols), BF16), shape((1, chunk), F32)),
        grid_spec=pltpu.PrefetchScalarGridSpec(
            num_scalar_prefetch=1,
            grid=(1,),
            in_specs=[
                pl.BlockSpec((nz, 1, cols), lambda i, s: (0, 0, 0)),
                pl.BlockSpec((chunk, cols), lambda i, s: (c, 0)),
            ]
            + [pl.BlockSpec((chunk, cols), lambda i, s: (0, 0)) for _ in received],
            out_specs=[
                pl.BlockSpec((count, chunk, cols), lambda i, s: (0, 0, 0)),
                pl.BlockSpec((1, chunk), lambda i, s: (0, 0)),
            ],
        ),
        compiler_params=PARAMS,
        name="prep",
    )(sources, gains, tokens, *received)


def far_kernel(where_ref, src_ref, x_ref, *rest, with_sq):
    if with_sq:
        sq_ref, own_ref, got_ref, out_ref, weight, sems = rest
    else:
        own_ref, got_ref, out_ref, weight, sems = rest
    held, share, _ = own_ref.shape
    copies = []
    for i in range(2 * held):
        piece = own_ref.at[i] if i < held else got_ref.at[i - held]
        row = pl.multiple_of(where_ref[i] * share, TAIL)
        copies.append(
            pltpu.make_async_copy(piece, weight.at[pl.ds(row, share)], sems.at[i])
        )
    for copy in copies:
        copy.start()
    for copy in copies:
        copy.wait()
    count, chunk, cols = x_ref.shape
    total = None
    for k in range(count):
        row = pl.multiple_of(src_ref[k] * cols, TAIL)
        term = jnp.dot(x_ref[k], weight[pl.ds(row, cols), :], preferred_element_type=F32)
        total = term if total is None else total + term
    out_ref[:chunk, :] = total.astype(BF16)
    if with_sq:
        width = out_ref.shape[1]
        sq = sq_ref[...]
        high = sq.astype(BF16).astype(F32)
        lines = []
        for part in (high, sq - high):
            for at in range(0, chunk, width):
                line = part[:, at : at + width]
                if line.shape[1] < width:
                    line = jnp.concatenate(
                        [line, jnp.zeros((1, width - line.shape[1]), F32)], axis=1
                    )
                lines.append(line)
        lines.append(jnp.zeros((TAIL - len(lines), width), F32))
        out_ref[chunk:, :] = jnp.concatenate(lines, axis=0).astype(BF16)


def far_product(where, sources, x, pieces, sq):
    own, got = pieces
    held, share, width = own.shape
    count, chunk, cols = x.shape
    with_sq = sq is not None
    rows = chunk + (TAIL if with_sq else 0)
    extra = [pl.BlockSpec((1, chunk), lambda i, w, s: (0, 0))] if with_sq else []
    return pl.pallas_call(
        partial(far_kernel, with_sq=with_sq),
        out_shape=shape((rows, width), BF16),
        grid_spec=pltpu.PrefetchScalarGridSpec(
            num_scalar_prefetch=2,
            grid=(1,),
            in_specs=[pl.BlockSpec((count, chunk, cols), lambda i, w, s: (0, 0, 0))]
            + extra
            + [ANY, ANY],
            out_specs=pl.BlockSpec((rows, width), lambda i, w, s: (0, 0)),
            scratch_shapes=[
                pltpu.VMEM((2 * held * share, width), BF16),
                pltpu.SemaphoreType.DMA((2 * held,)),
            ],
        ),
        compiler_params=PARAMS,
        name="far",
    )(where, sources, x, *([sq] if with_sq else []), own, got)


def near_kernel(src_ref, x_ref, q_ref, k_ref, v_ref, after_ref, kv_out, q_out):
    step = pl.program_id(0)
    x = x_ref[0]
    width = k_ref.shape[1]
    dot = partial(jnp.dot, preferred_element_type=F32)

    @pl.when(step == 0)
    def _():
        kv_out[...] = jnp.zeros_like(kv_out)
        q_out[...] = jnp.zeros_like(q_out)

    kv_out[:, :width] += dot(x, k_ref[...])
    kv_out[:, width:] += dot(x, v_ref[...])
    q_out[...] += dot(x, q_ref[...])


def near_product(blocks, x, q_weight, k_weight, v_weight, after):
    count, chunk, cols = x.shape
    widths = [w.shape[1] for w in (q_weight, k_weight, v_weight)]
    kv_width = widths[1] + widths[2]
    return pl.pallas_call(
        near_kernel,
        out_shape=(shape((chunk, kv_width), F32), shape((chunk, widths[0]), F32)),
        grid_spec=pltpu.PrefetchScalarGridSpec(
            num_scalar_prefetch=1,
            grid=(count,),
            in_specs=[pl.BlockSpec((1, chunk, cols), lambda i, s: (i, 0, 0))]
            + [pl.BlockSpec((cols, w), lambda i, s: (s[i], 0)) for w in widths]
            + [ANY],
            out_specs=[
                pl.BlockSpec((chunk, kv_width), lambda i, s: (0, 0)),
                pl.BlockSpec((chunk, widths[0]), lambda i, s: (0, 0)),
            ],
        ),
        compiler_params=PARAMS,
        name="near",
    )(blocks, x, q_weight, k_weight, v_weight, after)


def keys_kernel(near_ref, far_ref, sq_ref, cos_ref, sin_ref, out_ref, sum_ref, *, model):
    chunk, width = near_ref.shape
    tail = far_ref[chunk:, :].astype(F32)
    lines = -(-chunk // width)
    total = sq_ref[...]
    for part in range(2):
        row = [tail[part * lines + i : part * lines + i + 1, :] for i in range(lines)]
        total = total + jnp.concatenate(row, axis=1)[:, :chunk]
    factor = to_column(lax.rsqrt(total / model + epsilon))
    sum_ref[...] = total
    for c in range(0, width, HEAD_SIZE):
        at = slice(c, c + HEAD_SIZE)
        part = (near_ref[:, at] + far_ref[:chunk, at].astype(F32)) * factor
        if c < width // 2:
            part = rotate(part, cos_ref[...], sin_ref[...])
        out_ref[:, at] = part.astype(BF16)


def keys_values(near, far, sq, cosine, sine, c, model):
    chunk, width = near.shape
    whole = lambda i: (0, 0)
    return pl.pallas_call(
        partial(keys_kernel, model=model),
        out_shape=(shape((chunk, width), BF16), shape((1, chunk), F32)),
        grid=(1,),
        in_specs=[
            pl.BlockSpec(near.shape, whole),
            pl.BlockSpec(far.shape, whole),
            pl.BlockSpec((1, chunk), whole),
            pl.BlockSpec((chunk, HEAD_SIZE), lambda i: (c, 0)),
            pl.BlockSpec((chunk, HEAD_SIZE), lambda i: (c, 0)),
        ],
        out_specs=[pl.BlockSpec((chunk, width), whole), pl.BlockSpec((1, chunk), whole)],
        compiler_params=PARAMS,
        name="keys",
    )(near, far, sq, cosine, sine)


def attention_kernel(
    lo_ref, near_ref, far_ref, sum_ref, cos_ref, sin_ref, start_ref, *rest, back, offset, model
):
    kv_refs, (out_ref, k_scr, vt_scr) = rest[:-3], rest[-3:]
    part_rows = kv_refs[0].shape[0]
    group = near_ref.shape[1] // HEAD_SIZE
    tile = pl.program_id(0)

    @pl.when(tile == 0)
    def _():
        for b, kv_ref in enumerate(kv_refs):
            at = slice(b * part_rows, (b + 1) * part_rows)
            k_scr[at, :] = kv_ref[:, :HEAD_SIZE]
            vt_scr[:, at] = kv_ref[:, HEAD_SIZE:].astype(F32).T.astype(BF16)

    scale = query_scale * math.log2(math.e)
    factor = to_column(lax.rsqrt(sum_ref[...] / model + epsilon) * scale)
    heads = []
    for c in range(0, group * HEAD_SIZE, HEAD_SIZE):
        at = slice(c, c + HEAD_SIZE)
        part = (near_ref[:, at] + far_ref[:, at].astype(F32)) * factor
        heads.append(rotate(part, cos_ref[...], sin_ref[...]).astype(BF16))
    q2 = jnp.concatenate(heads, axis=0)
    width = group * Q_TILE
    start = jnp.concatenate([start_ref[...]] * group, axis=1)
    first = back * part_rows * CHUNKS + offset + tile * Q_TILE
    place = first + lax.broadcasted_iota(jnp.int32, (1, Q_TILE), 1)
    place = jnp.concatenate([place] * group, axis=1)

    def score(j):
        base = pl.multiple_of(j * K_TILE, K_TILE)
        return lax.dot_general(
            k_scr[pl.ds(base, K_TILE), :],
            q2,
            (((1,), (1,)), ((), ())),
            preferred_element_type=F32,
        )

    low = lo_ref[tile]
    stop = (first + Q_TILE + K_TILE - 1) // K_TILE

    def step(j, state):
        scores, run_max, run_sum, acc = state
        following = score(jnp.minimum(j + 1, stop - 1))
        base = pl.multiple_of(j * K_TILE, K_TILE)
        key_pos = base + lax.broadcasted_iota(jnp.int32, (K_TILE, width), 0)
        allowed = (key_pos >= start) & (key_pos <= place)
        scores = jnp.where(allowed, scores, NEG)
        new_max = jnp.maximum(run_max, jnp.max(scores, axis=0, keepdims=True))
        expo = jnp.exp2(scores - new_max)
        factor = jnp.exp2(run_max - new_max)
        run_sum = run_sum * factor + jnp.sum(expo, axis=0, keepdims=True)
        acc = acc * factor + jnp.dot(
            vt_scr[:, pl.ds(base, K_TILE)], expo.astype(BF16), preferred_element_type=F32
        )
        return following, new_max, run_sum, acc

    state = (
        score(low),
        jnp.full((1, width), NEG, F32),
        jnp.zeros((1, width), F32),
        jnp.zeros((HEAD_SIZE, width), F32),
    )
    _, _, run_sum, acc = lax.fori_loop(low, stop, step, state)
    context = (acc / run_sum).T
    for g in range(group):
        out_ref[:, g * HEAD_SIZE : (g + 1) * HEAD_SIZE] = context[
            g * Q_TILE : (g + 1) * Q_TILE
        ].astype(BF16)


def attend(near, far, sums, cosine, sine, start, blocks, c, model):
    rows, width = near.shape
    part_rows = blocks[0].shape[0]
    back = len(blocks) // CHUNKS - 1
    tiles = rows // Q_TILE
    low = start[c * rows : (c + 1) * rows : Q_TILE] // K_TILE
    keys = len(blocks) * part_rows
    return pl.pallas_call(
        partial(attention_kernel, back=back, offset=c * rows, model=model),
        out_shape=shape((rows, width), BF16),
        grid_spec=pltpu.PrefetchScalarGridSpec(
            num_scalar_prefetch=1,
            grid=(tiles,),
            in_specs=[
                pl.BlockSpec((Q_TILE, width), lambda i, lo: (i, 0)),
                pl.BlockSpec((Q_TILE, width), lambda i, lo: (i, 0)),
                pl.BlockSpec((1, Q_TILE), lambda i, lo: (0, i)),
                pl.BlockSpec((Q_TILE, HEAD_SIZE), lambda i, lo: (c * tiles + i, 0)),
                pl.BlockSpec((Q_TILE, HEAD_SIZE), lambda i, lo: (c * tiles + i, 0)),
                pl.BlockSpec((1, Q_TILE), lambda i, lo: (0, c * tiles + i)),
            ]
            + [pl.BlockSpec(b.shape, lambda i, lo: (0, 0)) for b in blocks],
            out_specs=pl.BlockSpec((Q_TILE, width), lambda i, lo: (i, 0)),
            scratch_shapes=[
                pltpu.VMEM((keys, HEAD_SIZE), BF16),
                pltpu.VMEM((HEAD_SIZE, keys), BF16),
            ],
        ),
        compiler_params=PARAMS,
        name="attend",
    )(low, near, far, sums, cosine, sine, start[None, :], *blocks)


def output_kernel(z_ref, own_o_ref, o_ref, *rest):
    ctx_refs, (out_ref, sq_ref, acc) = rest[:-3], rest[-3:]
    step = pl.program_id(0)
    plane, _, share, tile = o_ref.shape
    total = jnp.dot(ctx_refs[0][...], own_o_ref[...], preferred_element_type=F32)
    for k, ctx_ref in enumerate(ctx_refs[1:]):
        weight = o_ref[:, k].reshape(plane * share, tile)
        total = total + jnp.dot(ctx_ref[...], weight, preferred_element_type=F32)
    out_ref[...] = total
    squares = jnp.sum(total * total, axis=1, keepdims=True)
    squares = jnp.broadcast_to(squares, acc.shape)

    @pl.when(step == 0)
    def _():
        acc[...] = squares

    @pl.when(step > 0)
    def _():
        acc[...] += squares

    @pl.when(step == pl.num_programs(0) - 1)
    def _():
        sq_ref[...] = acc[...].T[0:1, :]


def output_product(z, o_weight, gathered, contexts):
    chunk, width = contexts[0].shape
    plane, others, share, cols = gathered.shape
    tiles = 3 if cols % (3 * LANES) == 0 else 1
    tile = cols // tiles
    whole = lambda i, z: (0, 0)
    if cols % LANES:
        o_weight = lax.dynamic_slice_in_dim(o_weight, z[0] * cols, cols, axis=1)
        z = z * 0
    return pl.pallas_call(
        output_kernel,
        out_shape=(shape((chunk, cols), F32), shape((1, chunk), F32)),
        grid_spec=pltpu.PrefetchScalarGridSpec(
            num_scalar_prefetch=1,
            grid=(tiles,),
            in_specs=[
                pl.BlockSpec((width, tile), lambda i, z: (0, z[0] * tiles + i)),
                pl.BlockSpec((plane, others, share, tile), lambda i, z: (0, 0, 0, i)),
            ]
            + [pl.BlockSpec((chunk, width), whole) for _ in contexts],
            out_specs=[
                pl.BlockSpec((chunk, tile), lambda i, z: (0, i)),
                pl.BlockSpec((1, chunk), whole),
            ],
            scratch_shapes=[pltpu.VMEM((chunk, LANES), F32)],
        ),
        compiler_params=PARAMS,
        name="output",
    )(z, o_weight, gathered, *contexts)


def final_kernel(token_ref, branch_ref, gain_ref, *rest, model, others):
    sq_refs, out_ref = rest[:others], rest[-1]
    total = sq_refs[0][...]
    for sq_ref in sq_refs[1:]:
        total = total + sq_ref[...]
    factor = to_column(lax.rsqrt(total / model + epsilon))[:, 0:1]
    out = token_ref[...].astype(F32) + branch_ref[...] * factor * gain_ref[...]
    out_ref[...] = out.astype(BF16)


def finish(tokens, branch, out_gain, sums, previous, c, model):
    chunk, cols = branch.shape
    tiles = chunk // Q_TILE
    in_specs = [
        pl.BlockSpec((Q_TILE, cols), lambda i: (c * tiles + i, 0)),
        pl.BlockSpec((Q_TILE, cols), lambda i: (i, 0)),
        pl.BlockSpec((1, cols), lambda i: (0, 0)),
    ]
    in_specs += [pl.BlockSpec((1, Q_TILE), lambda i: (0, i)) for _ in sums]
    args = [tokens, branch, out_gain, *sums]
    aliases = {}
    if previous is not None:
        aliases = {len(args): 0}
        in_specs.append(ANY)
        args.append(previous)
    return pl.pallas_call(
        partial(final_kernel, model=model, others=len(sums)),
        out_shape=shape(tokens.shape, BF16),
        grid=(tiles,),
        in_specs=in_specs,
        out_specs=pl.BlockSpec((Q_TILE, cols), lambda i: (c * tiles + i, 0)),
        input_output_aliases=aliases,
        compiler_params=PARAMS,
        name="finish",
    )(*args)


def per_device(
    tokens, seg_ids, in_gain, q_weight, k_weight, value_weight, o_weight, out_gain, *, sizes
):
    rows, cols = tokens.shape
    model = in_gain.shape[0]
    nz, nseq = sizes["tensor"], sizes["seq"]
    plane = nseq * sizes["groups"]
    z = lax.axis_index("tensor")
    seq = lax.axis_index("seq")
    in_plane = lax.axis_index(PLANE)
    half = nz // 2
    side, within = z // half, z % half
    half_rows = half * cols

    ring = [(i, i // half * half + (i + 1) % half) for i in range(nz)]
    swap = [(i, (i + half) % nz) for i in range(nz)]
    turn = lambda k: [(i, (i + k) % nz) for i in range(nz)]
    seq_bits = [1 << b for b in range(1, nseq.bit_length() - 1)]
    group_bits = [nseq << b for b in range(sizes["groups"].bit_length() - 1)]

    share = half_rows // plane
    at = jnp.reshape((1 - side) * plane + in_plane, (1,))
    packed_kv, packed_q = pack(at, q_weight, k_weight, value_weight, share)
    far_kv = lax.ppermute(packed_kv, "tensor", swap)
    far_q = lax.ppermute(packed_q, "tensor", swap)
    where_kv, *far_kv = spread(far_kv, plane, seq_bits + group_bits + [1])
    where_q, *far_q = spread(far_q, plane, group_bits + seq_bits + [1])

    chunk = rows // CHUNKS
    sources = (within + half - jnp.arange(half, dtype=jnp.int32)) % half
    blocks_of = side * half + sources
    gains = in_gain.reshape(nz, 1, cols)
    received = []
    for c in range(CHUNKS):
        blocks = []
        held = tokens[c * chunk : (c + 1) * chunk]
        for _ in range(half - 1):
            held = lax.ppermute(held, "tensor", ring)
            blocks.append(held)
        received.append(blocks)

    o_share = o_weight.shape[0] // plane
    moved = []
    for k in range(1, nz):
        target = (z + k) % nz
        piece = lax.dynamic_slice(
            o_weight, (in_plane * o_share, target * cols), (o_share, cols)
        )
        moved.append(lax.ppermute(piece, "tensor", turn(k)))
    gathered_o = lax.all_gather(jnp.stack(moved), PLANE)

    back = -(-(nseq * rows // 2 - 1) // rows)
    earlier = lambda k: [(i, i + k) for i in range(nseq - k)]
    start = jnp.sum((seg_ids[None, :] < seg_ids[:, None]).astype(jnp.int32), axis=1)
    start = start + back * rows
    for k in range(1, back + 1):
        ids = lax.ppermute(seg_ids, "seq", earlier(k))
        ids = jnp.where(seq >= k, ids, -1)
        start = start - jnp.sum((ids[None, :] >= seg_ids[:, None]).astype(jnp.int32), axis=1)

    cosine, sine = rotation_table(seq * rows + jnp.arange(rows, dtype=jnp.int32))

    kv_parts, q_parts = [], []
    for c in range(CHUNKS):
        x, sq = prep(blocks_of, gains, tokens, received[c], chunk, c)
        sent_kv = far_product(where_kv, sources, x, far_kv, sq)
        sent_q = far_product(where_q, sources, x, far_q, None)
        got_kv = lax.ppermute(sent_kv, "tensor", swap)
        got_q = lax.ppermute(sent_q, "tensor", swap)
        near_kv, near_q = near_product(
            blocks_of, x, q_weight, k_weight, value_weight, sent_q
        )
        own_kv, sums = keys_values(near_kv, got_kv, sq, cosine, sine, c, model)
        kv_parts.append(own_kv)
        q_parts.append((near_q, got_q, sums))
    blocks = list(kv_parts)
    for k in range(1, back + 1):
        blocks = [lax.ppermute(part, "seq", earlier(k)) for part in kv_parts] + blocks

    out = None
    z_at = jnp.reshape(z, (1,))
    for c in range(CHUNKS):
        context = attend(*q_parts[c], cosine, sine, start, blocks, c, model)
        contexts = [context]
        contexts += [lax.ppermute(context, "tensor", turn(k)) for k in range(1, nz)]
        branch, own_sq = output_product(z_at, o_weight, gathered_o, contexts)
        sums = [own_sq]
        sums += [lax.ppermute(own_sq, "tensor", turn(k)) for k in range(1, nz)]
        out = finish(tokens, branch, out_gain[None, :], sums, out, c, model)
    return out


def solution(mesh):
    return jax.shard_map(
        partial(per_device, sizes=dict(mesh.shape)),
        mesh=mesh,
        in_specs=(
            P(("groups", "seq"), "tensor"),
            P(("groups", "seq")),
            P(),
            P(None, "tensor"),
            P(None, "tensor"),
            P(None, "tensor"),
            P("tensor", None),
            P("tensor"),
        ),
        out_specs=P(("groups", "seq"), "tensor"),
        check_vma=False,
    )
```

time: 203 us -> 193 us (0.951)
  waiting for transfers between devices: 101 us -> 31.8 us
  Pallas kernels: 6.82 us -> 69.5 us
  starting transfers between devices: 32.7 us -> 55.3 us
  matrix products: 14.8 us -> 0 us
  other arithmetic: 14.8 us -> 5.94 us
  blocking collectives: 5.15 us -> 0 us
    pallas_call x1 -> x21, Pallas kernels: 6.82 us -> 69.5 us  [the longest x4 12.5 us: far_product(): pl.pallas_call(partial(far_kernel, with_sq=with_sq), out_shape=shape((row...]
    ppermute x12 -> x32, waiting for transfers between devices: 80.5 us -> 28 us  [the longest x4 8.97 us: per_device(): lax.ppermute(part, 'seq', earlier(k))]
    ppermute x12 -> x32, starting transfers between devices: 26.2 us -> 49.7 us  [the longest x6 15.3 us: per_device(): sums += [lax.ppermute(own_sq, 'tensor', turn(k)) for k in range(1, nz)]]
    ppermute x3, waiting for transfers between devices: 20.5 us -> 3.82 us  [per_device(): moved.append(lax.ppermute(piece, 'tensor', turn(k)))]
    dot_general x5 -> x0, matrix products: 14.8 us -> none  [the longest x4 10.6 us: project(): term = jnp.dot(block, part, preferred_element_type=jnp.float32)]
    dynamic_slice x7 -> x0, local copies, waits for them, and re-layouts: 5.95 us -> none  [the longest x4 3.17 us: weight_rows(): lax.dynamic_slice_in_dim(w, first, count, axis=0)]
    slice x2 -> x3, local copies, waits for them, and re-layouts: 0.14 us -> 5.38 us  [the longest x1 2.77 us: per_device(): held = tokens[c * chunk:(c + 1) * chunk]]
    all_gather x1 -> x0, blocking collectives: 5.15 us -> none  [per_device(): all_ids = lax.all_gather(seg_ids, 'seq', axis=0, tiled=True)]
  transfers between devices with their start and end apart: 17 -> 36, of which waited for: 8 -> 13; matrix products, arithmetic and copies ran while one was open for 15% -> 7% of each run, Pallas kernels for 3% -> 35%
where the time goes in v3:
time: 193 us; the launch traced here: 191 us
  Pallas kernels  69.5 us (36%)
  starting transfers between devices  55.3 us (29%)
  waiting for transfers between devices  31.8 us (16%)
  local copies, waits for them, and re-layouts  14.2 us (7%)
  between operations  13.9 us (7%)
  other arithmetic  5.94 us (3%)
    ppermute x6, starting transfers between devices, per_device(): sums += [lax.ppermute(own_sq, 'tensor', turn(k)) for k in range(1, nz)]  15.3 us
    pallas_call x4, Pallas kernels, far_product(): pl.pallas_call(partial(far_kernel, with_sq=with_sq), out_shape=shape((row...  12.5 us
    pallas_call x4, Pallas kernels, join(): pl.pallas_call(join_kernel, out_shape=shape((2 * first.shape[0],) + first...  11.6 us
    pallas_call x2, Pallas kernels, attend(): pl.pallas_call(partial(attention_kernel, back=back, offset=c * rows, mode...  11.3 us
    pallas_call x1, Pallas kernels, pack(): pl.pallas_call(pack_kernel, out_shape=(shape((share, kv_width), BF16), sh...  10.1 us
    ppermute x4, waiting for transfers between devices, per_device(): lax.ppermute(part, 'seq', earlier(k))  8.97 us
    ppermute x6, starting transfers between devices, per_device(): contexts += [lax.ppermute(context, 'tensor', turn(k)) for k in range(1, nz)]  8.88 us
    pallas_call x2, Pallas kernels, near_product(): pl.pallas_call(near_kernel, out_shape=(shape((chunk, kv_width), F32), sha...  7.18 us
  transfers between devices with their start and end apart: 36, of which 13 were waited for; matrix products, arithmetic and copies ran while one was open for 7% of the time, Pallas kernels for 35%

profile of v3, /device:TPU:2, one launch (start us, length us, event | category | flops | bytes accessed | tf_op | source)
XLA Modules:
  0.0 190.7 jit_solution(5814824835617946460)
XLA Ops:
  9.1 2.6 %collective-permute-start.1 = (bf16[32,1152]{1,0:T(8,128)(2,1)S(1)}, bf16[32,1152]{1,0:T(8,128)(2,1)S(1)}, u32[]{:S(2)}, u32[]{:S(2)}) collective-permute-start(bf16[32,1152]{1,0:T(8,128)(2,1)S(1)} %get-tuple-element.46), channel_id=1, source_target_pairs={{0,2},{1,3},{2,0},{3,1},{4,6},{5,7},{6,4},{7,5},{8,10},{9,11},{10,... | collective-permute-start | bytes 221192 | tf_op jit(solution)/shard_map/ppermute | solution.py:543
  14.2 2.6 %collective-permute-done.1 = bf16[32,1152]{1,0:T(8,128)(2,1)S(1)} collective-permute-done((bf16[32,1152]{1,0:T(8,128)(2,1)S(1)}, bf16[32,1152]{1,0:T(8,128)(2,1)S(1)}, u32[]{:S(2)}, u32[]{:S(2)}) %collective-permute-start.1) | collective-permute-done | bytes 73760 | tf_op jit(solution)/shard_map/ppermute | solution.py:543
  17.7 2.8 %fusion.3 = (bf16[384,1152]{1,0:T(8,128)(2,1)}, bf16[384,1152]{1,0:T(8,128)(2,1)}) fusion(bf16[768,1152]{1,0:T(8,128)(2,1)} %token_ref.3), kind=kLoop, calls=%fused_computation.30 | loop fusion | bytes 3538944 | tf_op jit(solution)/shard_map/slice | solution.py:530
  22.3 10.1 %pack.1 = (bf16[288,256]{1,0:T(8,128)(2,1)}, bf16[288,256]{1,0:T(8,128)(2,1)}) custom-call(s32[1]{0:T(128)} %bitcast.5.at_ref, bf16[4608,256]{1,0:T(8,128)(2,1)} %q_ref.5, bf16[4608,128]{1,0:T(8,128)(2,1)} %k_ref.5, bf16[4608,128]{1,0:T(8,128)(2,1)} %v_ref.5), custom_call_target="tpu_custom_call" | custom-call | tf_op jit(solution)/shard_map/pack/pallas_call | solution.py:69
  32.3 2.0 %collective-permute-start.11 = (bf16[288,256]{1,0:T(8,128)(2,1)}, bf16[288,256]{1,0:T(8,128)(2,1)S(1)}, u32[]{:S(2)}, u32[]{:S(2)}) collective-permute-start(bf16[288,256]{1,0:T(8,128)(2,1)} %get-tuple-element.28), channel_id=1, source_target_pairs={{0,2},{1,3},{2,0},{3,1},{4,6},{5,7},{6,4},{7,5},{8,10},{9,11},{10,... | collective-permute-start | bytes 442376 | tf_op jit(solution)/shard_map/ppermute | solution.py:518
  38.9 6.9 %collective-permute-done.11 = bf16[288,256]{1,0:T(8,128)(2,1)S(1)} collective-permute-done((bf16[288,256]{1,0:T(8,128)(2,1)}, bf16[288,256]{1,0:T(8,128)(2,1)S(1)}, u32[]{:S(2)}, u32[]{:S(2)}) %collective-permute-start.11) | collective-permute-done | bytes 147488 | tf_op jit(solution)/shard_map/ppermute | solution.py:518
  46.8 2.1 %collective-permute-done.6 = bf16[288,256]{1,0:T(8,128)(2,1)S(1)} collective-permute-done((bf16[288,256]{1,0:T(8,128)(2,1)}, bf16[288,256]{1,0:T(8,128)(2,1)S(1)}, u32[]{:S(2)}, u32[]{:S(2)}) %collective-permute-start.6) | collective-permute-done | bytes 147488 | tf_op jit(solution)/shard_map/ppermute | solution.py:519
  59.8 2.0 %collective-permute-start.3 = (s32[768]{0:T(1024)S(1)}, s32[768]{0:T(1024)S(1)}, u32[]{:S(2)}, u32[]{:S(2)}) collective-permute-start(s32[768]{0:T(1024)S(1)} %copy-done.18), channel_id=1, source_target_pairs={{0,4},{4,8},{8,12},{1,5},{5,9},{9,13},{2,6},{6,10},{10,14},{3,7},{... | collective-permute-start | bytes 9224 | tf_op jit(solution)/shard_map/ppermute | solution.py:551
  62.1 2.7 %collective-permute-done.8.second_ref = bf16[2,288,256]{2,1,0:T(8,128)(2,1)} collective-permute-done((bf16[2,288,256]{2,1,0:T(8,128)(2,1)S(1)}, bf16[2,288,256]{2,1,0:T(8,128)(2,1)}, u32[]{:S(2)}, u32[]{:S(2)}) %collective-permute-start.8) | collective-permute-done | bytes 294944 | tf_op jit(solution)/shard_map/ppermute | solution.py:112
  64.7 10.1 %join.5.rest_0_ = bf16[4,288,256]{2,1,0:T(8,128)(2,1)} custom-call(bf16[2,288,256]{2,1,0:T(8,128)(2,1)S(1)} %join.4.first_ref, bf16[2,288,256]{2,1,0:T(8,128)(2,1)} %collective-permute-done.8.second_ref), custom_call_target="tpu_custom_call" | custom-call | tf_op jit(solution)/shard_map/join/pallas_call | solution.py:97
  77.0 2.4 %prep.2 = (bf16[2,384,1152]{2,1,0:T(8,128)(2,1)S(1)}, f32[1,384]{1,0:T(1,128)S(1)}) custom-call(s32[2]{0:T(128)S(1)} %broadcast_add_fusion.src_ref, f32[4,1,1152]{2,1,0:T(1,128)S(1)} %copy-done.10, bf16[768,1152]{1,0:T(8,128)(2,1)S(1)} %copy-done, bf16[384,1152]{1,0:T(8,128)(2,1)} %collective-permute-done.5.rest_1_), custom_call_target="tpu_custom_call" | custom-call | tf_op jit(solution)/shard_map/prep/pallas_call | solution.py:132
  79.4 3.5 %far.7 = bf16[400,256]{1,0:T(8,128)(2,1)} custom-call(s32[8]{0:T(128)S(1)} %copy-done.17, s32[2]{0:T(128)S(1)} %and_select_fusion.1.src_ref, bf16[2,384,1152]{2,1,0:T(8,128)(2,1)S(1)} %get-tuple-element.30.x_ref, f32[1,384]{1,0:T(1,128)S(1)} %get-tuple-element.32.rest_0_.sq_ref, bf16[4,288,256]{2,1,0:T(8,128)(2,1)S(1)} %join.7.rest_1_, ...), custom_call_target="tpu_custom_call" | custom-call | tf_op jit(solution)/shard_map/far/pallas_call | solution.py:201
  82.9 3.3 %collective-permute-start.17 = (bf16[400,256]{1,0:T(8,128)(2,1)}, bf16[400,256]{1,0:T(8,128)(2,1)}, u32[]{:S(2)}, u32[]{:S(2)}) collective-permute-start(bf16[400,256]{1,0:T(8,128)(2,1)} %far.7), channel_id=1, source_target_pairs={{0,2},{1,3},{2,0},{3,1},{4,6},{5,7},{6,4},{7,5},{8,10},{9,11},{10,... | collective-permute-start | bytes 614408 | tf_op jit(solution)/shard_map/ppermute | solution.py:562
  86.3 3.5 %far.5 = bf16[400,256]{1,0:T(8,128)(2,1)} custom-call(s32[8]{0:T(128)S(1)} %copy-done.17, s32[2]{0:T(128)S(1)} %and_select_fusion.1.src_ref, bf16[2,384,1152]{2,1,0:T(8,128)(2,1)S(1)} %get-tuple-element.23.x_ref, f32[1,384]{1,0:T(1,128)S(1)} %get-tuple-element.27.rest_0_.sq_ref, bf16[4,288,256]{2,1,0:T(8,128)(2,1)S(1)} %join.7.rest_1_, ...), custom_call_target="tpu_custom_call" | custom-call | tf_op jit(solution)/shard_map/far/pallas_call | solution.py:201
  95.8 2.9 %far.6.after_ref = bf16[384,256]{1,0:T(8,128)(2,1)S(1)} custom-call(s32[8]{0:T(128)S(1)} %copy-done.15, s32[2]{0:T(128)S(1)} %and_select_fusion.1.src_ref, bf16[2,384,1152]{2,1,0:T(8,128)(2,1)S(1)} %copy-done.2, bf16[4,288,256]{2,1,0:T(8,128)(2,1)} %join.5.rest_0_, bf16[4,288,256]{2,1,0:T(8,128)(2,1)} %collective-permute-done.9.rest_1_), custom_call_target="tpu_custom_call" | custom-call | tf_op jit(solution)/shard_map/far/pallas_call | solution.py:201
  100.0 3.6 %near.3 = (f32[384,256]{1,0:T(8,128)S(1)}, f32[384,256]{1,0:T(8,128)S(1)}) custom-call(s32[2]{0:T(128)S(1)} %broadcast_add_fusion.src_ref, bf16[2,384,1152]{2,1,0:T(8,128)(2,1)S(1)} %copy-done.3, bf16[4608,256]{1,0:T(8,128)(2,1)} %q_ref.5, bf16[4608,128]{1,0:T(8,128)(2,1)S(1)} %copy-done.4, bf16[4608,128]{1,0:T(8,128)(2,1)S(1)} %copy-done.5, ...), custom_call_target="tpu_custom_call" | custom-call | tf_op jit(solution)/shard_map/near/pallas_call | solution.py:241
  103.6 3.0 %collective-permute-start.28 = (bf16[384,256]{1,0:T(8,128)(2,1)S(1)}, bf16[384,256]{1,0:T(8,128)(2,1)S(1)}, u32[]{:S(2)}, u32[]{:S(2)}) collective-permute-start(bf16[384,256]{1,0:T(8,128)(2,1)S(1)} %far.6.after_ref), channel_id=1, source_target_pairs={{0,2},{1,3},{2,0},{3,1},{4,6},{5,7},{6,4},{7,5},{8,10},{9,11},{10,... | collective-permute-start | bytes 589832 | tf_op jit(solution)/shard_map/ppermute | solution.py:563
  106.6 2.6 %far.4.after_ref = bf16[384,256]{1,0:T(8,128)(2,1)S(1)} custom-call(s32[8]{0:T(128)S(1)} %copy-done.16, s32[2]{0:T(128)S(1)} %and_select_fusion.1.src_ref, bf16[2,384,1152]{2,1,0:T(8,128)(2,1)S(1)} %get-tuple-element.23.x_ref, bf16[4,288,256]{2,1,0:T(8,128)(2,1)} %join.5.rest_0_, bf16[4,288,256]{2,1,0:T(8,128)(2,1)} %collective-permute-done.9.rest_1_), custom_call_target="tpu_custom_call" | custom-call | tf_op jit(solution)/shard_map/far/pallas_call | solution.py:201
  109.2 3.6 %near.2 = (f32[384,256]{1,0:T(8,128)S(1)}, f32[384,256]{1,0:T(8,128)S(1)}) custom-call(s32[2]{0:T(128)S(1)} %broadcast_add_fusion.src_ref, bf16[2,384,1152]{2,1,0:T(8,128)(2,1)S(1)} %get-tuple-element.23.x_ref, bf16[4608,256]{1,0:T(8,128)(2,1)} %q_ref.5, bf16[4608,128]{1,0:T(8,128)(2,1)S(1)} %copy-done.4, bf16[4608,128]{1,0:T(8,128)(2,1)S(1)} %copy-done.5, ...), custom_call_target="tpu_custom_call" | custom-call | tf_op jit(solution)/shard_map/near/pallas_call | solution.py:241
  115.4 1.9 %collective-permute-start.20 = (bf16[384,256]{1,0:T(8,128)(2,1)S(1)}, bf16[384,256]{1,0:T(8,128)(2,1)S(1)}, u32[]{:S(2)}, u32[]{:S(2)}) collective-permute-start(bf16[384,256]{1,0:T(8,128)(2,1)S(1)} %get-tuple-element.33.rest_4_), channel_id=1, source_target_pairs={{0,4},{4,8},{8,12},{1,5},{5,9},{9,13},{2,6},{6,10},{10,14},{3,7},{... | collective-permute-start | bytes 589832 | tf_op jit(solution)/shard_map/ppermute | solution.py:572
  125.0 3.2 %collective-permute-done.19.rest_1_ = bf16[384,256]{1,0:T(8,128)(2,1)S(1)} collective-permute-done((bf16[384,256]{1,0:T(8,128)(2,1)S(1)}, bf16[384,256]{1,0:T(8,128)(2,1)S(1)}, u32[]{:S(2)}, u32[]{:S(2)}) %collective-permute-start.19) | collective-permute-done | bytes 196640 | tf_op jit(solution)/shard_map/ppermute | solution.py:572
  128.2 2.6 %collective-permute-done.21.rest_3_ = bf16[384,256]{1,0:T(8,128)(2,1)S(1)} collective-permute-done((bf16[384,256]{1,0:T(8,128)(2,1)S(1)}, bf16[384,256]{1,0:T(8,128)(2,1)S(1)}, u32[]{:S(2)}, u32[]{:S(2)}) %collective-permute-start.21) | collective-permute-done | bytes 196640 | tf_op jit(solution)/shard_map/ppermute | solution.py:572
  130.8 7.6 %attend.3.rest_0_ = bf16[384,256]{1,0:T(8,128)(2,1)S(1)} custom-call(s32[3]{0:T(128)S(1)} %and_select_fusion.lo_ref, f32[384,256]{1,0:T(8,128)S(1)} %get-tuple-element.37.near_ref, bf16[384,256]{1,0:T(8,128)(2,1)S(1)} %collective-permute-done.28.far_ref, f32[1,384]{1,0:T(1,128)S(1)} %get-tuple-element.38.sum_ref, f32[768,128]{1,0:T(8,128)S(1)} %copy-done.6, ...), custom_call_target="tpu_custom_call" | custom-call | tf_op jit(solution)/shard_map/attend/pallas_call | solution.py:376
  139.8 2.5 %collective-permute-start.31 = (bf16[384,256]{1,0:T(8,128)(2,1)S(1)}, bf16[384,256]{1,0:T(8,128)(2,1)S(1)}, u32[]{:S(2)}, u32[]{:S(2)}) collective-permute-start(bf16[384,256]{1,0:T(8,128)(2,1)S(1)} %attend.3.rest_0_), channel_id=1, source_target_pairs={{0,3},{1,0},{2,1},{3,2},{4,7},{5,4},{6,5},{7,6},{8,11},{9,8},{10,9... | collective-permute-start | bytes 589832 | tf_op jit(solution)/shard_map/ppermute | solution.py:579
  142.3 3.8 %attend.2.rest_0_ = bf16[384,256]{1,0:T(8,128)(2,1)S(1)} custom-call(s32[3]{0:T(128)S(1)} %and_select_fusion.2.lo_ref, f32[384,256]{1,0:T(8,128)S(1)} %get-tuple-element.25.near_ref, bf16[384,256]{1,0:T(8,128)(2,1)S(1)} %collective-permute-done.10.far_ref, f32[1,384]{1,0:T(1,128)S(1)} %get-tuple-element.29.sum_ref, f32[768,128]{1,0:T(8,128)S(1)} %copy-done.6, ...), custom_call_target="tpu_custom_call" | custom-call | tf_op jit(solution)/shard_map/attend/pallas_call | solution.py:376
  148.3 2.8 %collective-permute-start.24 = (bf16[384,256]{1,0:T(8,128)(2,1)S(1)}, bf16[384,256]{1,0:T(8,128)(2,1)S(1)}, u32[]{:S(2)}, u32[]{:S(2)}) collective-permute-start(bf16[384,256]{1,0:T(8,128)(2,1)S(1)} %attend.2.rest_0_), channel_id=1, source_target_pairs={{0,3},{1,0},{2,1},{3,2},{4,7},{5,4},{6,5},{7,6},{8,11},{9,8},{10,9... | collective-permute-start | bytes 589832 | tf_op jit(solution)/shard_map/ppermute | solution.py:579
  151.1 4.8 %collective-permute-done.30.rest_2_ = bf16[384,256]{1,0:T(8,128)(2,1)S(1)} collective-permute-done((bf16[384,256]{1,0:T(8,128)(2,1)S(1)}, bf16[384,256]{1,0:T(8,128)(2,1)S(1)}, u32[]{:S(2)}, u32[]{:S(2)}) %collective-permute-start.30) | collective-permute-done | bytes 196640 | tf_op jit(solution)/shard_map/ppermute | solution.py:579
  157.3 3.5 %output.3 = (f32[384,1152]{1,0:T(8,128)S(1)}, f32[1,384]{1,0:T(1,128)S(1)}) custom-call(s32[1]{0:T(128)} %bitcast.z_ref, bf16[256,4608]{1,0:T(8,128)(2,1)} %own_o_ref.3, bf16[8,3,32,1152]{3,2,1,0:T(8,128)(2,1)S(1)} %bitcast.8, bf16[384,256]{1,0:T(8,128)(2,1)S(1)} %attend.3.rest_0_, bf16[384,256]{1,0:T(8,128)(2,1)S(1)} %collective-permute-done.29.rest_1_, ...), custom_call_target="tpu_custom_call" | custom-call | tf_op jit(solution)/shard_map/output/pallas_call | solution.py:436
  160.9 9.0 %collective-permute-start.32 = (f32[1,384]{1,0:T(1,128)S(1)}, f32[1,384]{1,0:T(1,128)S(1)}, u32[]{:S(2)}, u32[]{:S(2)}) collective-permute-start(f32[1,384]{1,0:T(1,128)S(1)} %get-tuple-element.40.rest_0_), channel_id=1, source_target_pairs={{0,1},{1,2},{2,3},{3,0},{4,5},{5,6},{6,7},{7,4},{8,9},{9,10},{10,1... | collective-permute-start | bytes 4616 | tf_op jit(solution)/shard_map/ppermute | solution.py:582
  172.3 3.4 %output.2 = (f32[384,1152]{1,0:T(8,128)S(1)}, f32[1,384]{1,0:T(1,128)S(1)}) custom-call(s32[1]{0:T(128)} %bitcast.z_ref, bf16[256,4608]{1,0:T(8,128)(2,1)} %own_o_ref.3, bf16[8,3,32,1152]{3,2,1,0:T(8,128)(2,1)S(1)} %bitcast.9, bf16[384,256]{1,0:T(8,128)(2,1)S(1)} %attend.2.rest_0_, bf16[384,256]{1,0:T(8,128)(2,1)S(1)} %collective-permute-done.22.rest_1_, ...), custom_call_target="tpu_custom_call" | custom-call | tf_op jit(solution)/shard_map/output/pallas_call | solution.py:436
  176.3 2.0 %collective-permute-start.26 = (f32[1,384]{1,0:T(1,128)S(1)}, f32[1,384]{1,0:T(1,128)S(1)}, u32[]{:S(2)}, u32[]{:S(2)}) collective-permute-start(f32[1,384]{1,0:T(1,128)S(1)} %get-tuple-element.36.rest_0_), channel_id=1, source_target_pairs={{0,2},{1,3},{2,0},{3,1},{4,6},{5,7},{6,4},{7,5},{8,10},{9,11},{10,... | collective-permute-start | bytes 4616 | tf_op jit(solution)/shard_map/ppermute | solution.py:582
  179.7 1.9 %finish.2.rest_4_ = bf16[768,1152]{1,0:T(8,128)(2,1)} custom-call(bf16[768,1152]{1,0:T(8,128)(2,1)S(1)} %copy-done, f32[384,1152]{1,0:T(8,128)S(1)} %get-tuple-element.39.branch_ref, f32[1,1152]{1,0:T(1,128)S(1)} %broadcast_in_dim.14.gain_ref, f32[1,384]{1,0:T(1,128)S(1)} %get-tuple-element.40.rest_0_, f32[1,384]{1,0:T(1,128)S(1)} %collective-permute-done.32.rest_1_, ...), custom_call_target="tpu_custom_call" | custom-call | tf_op jit(solution)/shard_map/finish/pallas_call | solution.py:483
  (132 shorter events, 55.5 us)
Async XLA Ops:
  6.5 149.3 %all-gather.3.cloned.1.call-start = ((), (), s32[]{:S(2)}) async-start(), calls=%async_computation | async-start | bytes 1990656 | tf_op jit(solution)/shard_map/all_gather | solution.py:544
  7.5 6.7 %collective-permute-start = (bf16[32,1152]{1,0:T(8,128)(2,1)S(1)}, bf16[32,1152]{1,0:T(8,128)(2,1)S(1)}, u32[]{:S(2)}, u32[]{:S(2)}) collective-permute-start(bf16[32,1152]{1,0:T(8,128)(2,1)S(1)} %get-tuple-element.44), channel_id=1, source_target_pairs={{0,1},{1,2},{2,3},{3,0},{4,5},{5,6},{6,7},{7,4},{8,9},{9,10},{10,1... | collective-permute-start | bytes 221192 | tf_op jit(solution)/shard_map/ppermute | solution.py:543
  9.1 7.7 %collective-permute-start.1 = (bf16[32,1152]{1,0:T(8,128)(2,1)S(1)}, bf16[32,1152]{1,0:T(8,128)(2,1)S(1)}, u32[]{:S(2)}, u32[]{:S(2)}) collective-permute-start(bf16[32,1152]{1,0:T(8,128)(2,1)S(1)} %get-tuple-element.46), channel_id=1, source_target_pairs={{0,2},{1,3},{2,0},{3,1},{4,6},{5,7},{6,4},{7,5},{8,10},{9,11},{10,... | collective-permute-start | bytes 221192 | tf_op jit(solution)/shard_map/ppermute | solution.py:543
  20.4 55.3 %collective-permute-start.16 = (bf16[384,1152]{1,0:T(8,128)(2,1)}, bf16[384,1152]{1,0:T(8,128)(2,1)S(1)}, u32[]{:S(2)}, u32[]{:S(2)}) collective-permute-start(bf16[384,1152]{1,0:T(8,128)(2,1)} %get-tuple-element.47), channel_id=1, source_target_pairs={{0,1},{1,0},{2,3},{3,2},{4,5},{5,4},{6,7},{7,6},{8,9},{9,8},{10,11... | collective-permute-start | bytes 2654216 | tf_op jit(solution)/shard_map/ppermute | solution.py:532
  32.3 13.5 %collective-permute-start.11 = (bf16[288,256]{1,0:T(8,128)(2,1)}, bf16[288,256]{1,0:T(8,128)(2,1)S(1)}, u32[]{:S(2)}, u32[]{:S(2)}) collective-permute-start(bf16[288,256]{1,0:T(8,128)(2,1)} %get-tuple-element.28), channel_id=1, source_target_pairs={{0,2},{1,3},{2,0},{3,1},{4,6},{5,7},{6,4},{7,5},{8,10},{9,11},{10,... | collective-permute-start | bytes 442376 | tf_op jit(solution)/shard_map/ppermute | solution.py:518
  34.3 14.6 %collective-permute-start.6 = (bf16[288,256]{1,0:T(8,128)(2,1)}, bf16[288,256]{1,0:T(8,128)(2,1)S(1)}, u32[]{:S(2)}, u32[]{:S(2)}) collective-permute-start(bf16[288,256]{1,0:T(8,128)(2,1)} %get-tuple-element.24), channel_id=1, source_target_pairs={{0,2},{1,3},{2,0},{3,1},{4,6},{5,7},{6,4},{7,5},{8,10},{9,11},{10,... | collective-permute-start | bytes 442376 | tf_op jit(solution)/shard_map/ppermute | solution.py:519
  35.3 41.6 %collective-permute-start.5 = (bf16[384,1152]{1,0:T(8,128)(2,1)}, bf16[384,1152]{1,0:T(8,128)(2,1)}, u32[]{:S(2)}, u32[]{:S(2)}) collective-permute-start(bf16[384,1152]{1,0:T(8,128)(2,1)} %get-tuple-element.48), channel_id=1, source_target_pairs={{0,1},{1,0},{2,3},{3,2},{4,5},{5,4},{6,7},{7,6},{8,9},{9,8},{10,11... | collective-permute-start | bytes 2654216 | tf_op jit(solution)/shard_map/ppermute | solution.py:532
  35.5 26.5 %collective-permute-start.4 = (s32[768]{0:T(1024)S(1)}, s32[768]{0:T(1024)S(1)}, u32[]{:S(2)}, u32[]{:S(2)}) collective-permute-start(s32[768]{0:T(1024)S(1)} %copy-done.18), channel_id=1, source_target_pairs={{0,8},{4,12},{1,9},{5,13},{2,10},{6,14},{3,11},{7,15},{16,24},{20,... | collective-permute-start | bytes 9224 | tf_op jit(solution)/shard_map/ppermute | solution.py:551
  49.0 6.9 %collective-permute-start.7 = (bf16[1,288,256]{2,1,0:T(8,128)(2,1)S(1)}, bf16[1,288,256]{2,1,0:T(8,128)(2,1)}, u32[]{:S(2)}, u32[]{:S(2)}) collective-permute-start(bf16[1,288,256]{2,1,0:T(8,128)(2,1)S(1)} %bitcast.10), channel_id=1, source_target_pairs={{0,16},{4,20},{8,24},{12,28},{16,0},{20,4},{24,8},{28,12},{1,17},{... | collective-permute-start | bytes 442376 | tf_op jit(solution)/shard_map/ppermute | solution.py:112
  51.3 8.5 %collective-permute-start.13 = (bf16[2,288,256]{2,1,0:T(8,128)(2,1)S(1)}, bf16[2,288,256]{2,1,0:T(8,128)(2,1)S(1)}, u32[]{:S(2)}, u32[]{:S(2)}) collective-permute-start(bf16[2,288,256]{2,1,0:T(8,128)(2,1)S(1)} %join.6.first_ref), channel_id=1, source_target_pairs={{0,16},{4,20},{8,24},{12,28},{16,0},{20,4},{24,8},{28,12},{1,17},{... | collective-permute-start | bytes 884744 | tf_op jit(solution)/shard_map/ppermute | solution.py:112
  57.8 6.9 %collective-permute-start.8 = (bf16[2,288,256]{2,1,0:T(8,128)(2,1)S(1)}, bf16[2,288,256]{2,1,0:T(8,128)(2,1)}, u32[]{:S(2)}, u32[]{:S(2)}) collective-permute-start(bf16[2,288,256]{2,1,0:T(8,128)(2,1)S(1)} %join.4.first_ref), channel_id=1, source_target_pairs={{0,8},{4,12},{8,0},{12,4},{16,24},{20,28},{24,16},{28,20},{1,9},{5... | collective-permute-start | bytes 884744 | tf_op jit(solution)/shard_map/ppermute | solution.py:112
  59.8 15.1 %collective-permute-start.3 = (s32[768]{0:T(1024)S(1)}, s32[768]{0:T(1024)S(1)}, u32[]{:S(2)}, u32[]{:S(2)}) collective-permute-start(s32[768]{0:T(1024)S(1)} %copy-done.18), channel_id=1, source_target_pairs={{0,4},{4,8},{8,12},{1,5},{5,9},{9,13},{2,6},{6,10},{10,14},{3,7},{... | collective-permute-start | bytes 9224 | tf_op jit(solution)/shard_map/ppermute | solution.py:551
  62.0 17.4 %collective-permute-start.14 = (bf16[4,288,256]{2,1,0:T(8,128)(2,1)S(1)}, bf16[4,288,256]{2,1,0:T(8,128)(2,1)S(1)}, u32[]{:S(2)}, u32[]{:S(2)}) collective-permute-start(bf16[4,288,256]{2,1,0:T(8,128)(2,1)S(1)} %join.7.rest_1_), channel_id=1, source_target_pairs={{0,4},{4,0},{8,12},{12,8},{16,20},{20,16},{24,28},{28,24},{1,5},{5... | collective-permute-start | bytes 1769480 | tf_op jit(solution)/shard_map/ppermute | solution.py:112
  74.8 18.9 %collective-permute-start.9 = (bf16[4,288,256]{2,1,0:T(8,128)(2,1)}, bf16[4,288,256]{2,1,0:T(8,128)(2,1)}, u32[]{:S(2)}, u32[]{:S(2)}) collective-permute-start(bf16[4,288,256]{2,1,0:T(8,128)(2,1)} %join.5.rest_0_), channel_id=1, source_target_pairs={{0,4},{4,0},{8,12},{12,8},{16,20},{20,16},{24,28},{28,24},{1,5},{5... | collective-permute-start | bytes 1769480 | tf_op jit(solution)/shard_map/ppermute | solution.py:112
  82.9 29.9 %collective-permute-start.17 = (bf16[400,256]{1,0:T(8,128)(2,1)}, bf16[400,256]{1,0:T(8,128)(2,1)}, u32[]{:S(2)}, u32[]{:S(2)}) collective-permute-start(bf16[400,256]{1,0:T(8,128)(2,1)} %far.7), channel_id=1, source_target_pairs={{0,2},{1,3},{2,0},{3,1},{4,6},{5,7},{6,4},{7,5},{8,10},{9,11},{10,... | collective-permute-start | bytes 614408 | tf_op jit(solution)/shard_map/ppermute | solution.py:562
  89.8 27.5 %collective-permute-start.15 = (bf16[400,256]{1,0:T(8,128)(2,1)}, bf16[400,256]{1,0:T(8,128)(2,1)}, u32[]{:S(2)}, u32[]{:S(2)}) collective-permute-start(bf16[400,256]{1,0:T(8,128)(2,1)} %far.5), channel_id=1, source_target_pairs={{0,2},{1,3},{2,0},{3,1},{4,6},{5,7},{6,4},{7,5},{8,10},{9,11},{10,... | collective-permute-start | bytes 614408 | tf_op jit(solution)/shard_map/ppermute | solution.py:562
  103.6 18.2 %collective-permute-start.28 = (bf16[384,256]{1,0:T(8,128)(2,1)S(1)}, bf16[384,256]{1,0:T(8,128)(2,1)S(1)}, u32[]{:S(2)}, u32[]{:S(2)}) collective-permute-start(bf16[384,256]{1,0:T(8,128)(2,1)S(1)} %far.6.after_ref), channel_id=1, source_target_pairs={{0,2},{1,3},{2,0},{3,1},{4,6},{5,7},{6,4},{7,5},{8,10},{9,11},{10,... | collective-permute-start | bytes 589832 | tf_op jit(solution)/shard_map/ppermute | solution.py:563
  114.1 9.7 %collective-permute-start.18 = (bf16[384,256]{1,0:T(8,128)(2,1)S(1)}, bf16[384,256]{1,0:T(8,128)(2,1)S(1)}, u32[]{:S(2)}, u32[]{:S(2)}) collective-permute-start(bf16[384,256]{1,0:T(8,128)(2,1)S(1)} %get-tuple-element.33.rest_4_), channel_id=1, source_target_pairs={{0,8},{4,12},{1,9},{5,13},{2,10},{6,14},{3,11},{7,15},{16,24},{20,... | collective-permute-start | bytes 589832 | tf_op jit(solution)/shard_map/ppermute | solution.py:572
  115.4 9.6 %collective-permute-start.20 = (bf16[384,256]{1,0:T(8,128)(2,1)S(1)}, bf16[384,256]{1,0:T(8,128)(2,1)S(1)}, u32[]{:S(2)}, u32[]{:S(2)}) collective-permute-start(bf16[384,256]{1,0:T(8,128)(2,1)S(1)} %get-tuple-element.33.rest_4_), channel_id=1, source_target_pairs={{0,4},{4,8},{8,12},{1,5},{5,9},{9,13},{2,6},{6,10},{10,14},{3,7},{... | collective-permute-start | bytes 589832 | tf_op jit(solution)/shard_map/ppermute | solution.py:572
  118.5 9.7 %collective-permute-start.19 = (bf16[384,256]{1,0:T(8,128)(2,1)S(1)}, bf16[384,256]{1,0:T(8,128)(2,1)S(1)}, u32[]{:S(2)}, u32[]{:S(2)}) collective-permute-start(bf16[384,256]{1,0:T(8,128)(2,1)S(1)} %get-tuple-element.34.rest_5_), channel_id=1, source_target_pairs={{0,8},{4,12},{1,9},{5,13},{2,10},{6,14},{3,11},{7,15},{16,24},{20,... | collective-permute-start | bytes 589832 | tf_op jit(solution)/shard_map/ppermute | solution.py:572
  119.8 11.0 %collective-permute-start.21 = (bf16[384,256]{1,0:T(8,128)(2,1)S(1)}, bf16[384,256]{1,0:T(8,128)(2,1)S(1)}, u32[]{:S(2)}, u32[]{:S(2)}) collective-permute-start(bf16[384,256]{1,0:T(8,128)(2,1)S(1)} %get-tuple-element.34.rest_5_), channel_id=1, source_target_pairs={{0,4},{4,8},{8,12},{1,5},{5,9},{9,13},{2,6},{6,10},{10,14},{3,7},{... | collective-permute-start | bytes 589832 | tf_op jit(solution)/shard_map/ppermute | solution.py:572
  121.8 20.6 %collective-permute-start.10 = (bf16[384,256]{1,0:T(8,128)(2,1)S(1)}, bf16[384,256]{1,0:T(8,128)(2,1)S(1)}, u32[]{:S(2)}, u32[]{:S(2)}) collective-permute-start(bf16[384,256]{1,0:T(8,128)(2,1)S(1)} %far.4.after_ref), channel_id=1, source_target_pairs={{0,2},{1,3},{2,0},{3,1},{4,6},{5,7},{6,4},{7,5},{8,10},{9,11},{10,... | collective-permute-start | bytes 589832 | tf_op jit(solution)/shard_map/ppermute | solution.py:563
  138.4 9.8 %collective-permute-start.29 = (bf16[384,256]{1,0:T(8,128)(2,1)S(1)}, bf16[384,256]{1,0:T(8,128)(2,1)S(1)}, u32[]{:S(2)}, u32[]{:S(2)}) collective-permute-start(bf16[384,256]{1,0:T(8,128)(2,1)S(1)} %attend.3.rest_0_), channel_id=1, source_target_pairs={{0,1},{1,2},{2,3},{3,0},{4,5},{5,6},{6,7},{7,4},{8,9},{9,10},{10,1... | collective-permute-start | bytes 589832 | tf_op jit(solution)/shard_map/ppermute | solution.py:579
  138.5 17.4 %collective-permute-start.30 = (bf16[384,256]{1,0:T(8,128)(2,1)S(1)}, bf16[384,256]{1,0:T(8,128)(2,1)S(1)}, u32[]{:S(2)}, u32[]{:S(2)}) collective-permute-start(bf16[384,256]{1,0:T(8,128)(2,1)S(1)} %attend.3.rest_0_), channel_id=1, source_target_pairs={{0,2},{1,3},{2,0},{3,1},{4,6},{5,7},{6,4},{7,5},{8,10},{9,11},{10,... | collective-permute-start | bytes 589832 | tf_op jit(solution)/shard_map/ppermute | solution.py:579
  139.8 16.1 %collective-permute-start.31 = (bf16[384,256]{1,0:T(8,128)(2,1)S(1)}, bf16[384,256]{1,0:T(8,128)(2,1)S(1)}, u32[]{:S(2)}, u32[]{:S(2)}) collective-permute-start(bf16[384,256]{1,0:T(8,128)(2,1)S(1)} %attend.3.rest_0_), channel_id=1, source_target_pairs={{0,3},{1,0},{2,1},{3,2},{4,7},{5,4},{6,5},{7,6},{8,11},{9,8},{10,9... | collective-permute-start | bytes 589832 | tf_op jit(solution)/shard_map/ppermute | solution.py:579
  146.1 24.7 %collective-permute-start.22 = (bf16[384,256]{1,0:T(8,128)(2,1)S(1)}, bf16[384,256]{1,0:T(8,128)(2,1)S(1)}, u32[]{:S(2)}, u32[]{:S(2)}) collective-permute-start(bf16[384,256]{1,0:T(8,128)(2,1)S(1)} %attend.2.rest_0_), channel_id=1, source_target_pairs={{0,1},{1,2},{2,3},{3,0},{4,5},{5,6},{6,7},{7,4},{8,9},{9,10},{10,1... | collective-permute-start | bytes 589832 | tf_op jit(solution)/shard_map/ppermute | solution.py:579
  146.7 25.6 %collective-permute-start.23 = (bf16[384,256]{1,0:T(8,128)(2,1)S(1)}, bf16[384,256]{1,0:T(8,128)(2,1)S(1)}, u32[]{:S(2)}, u32[]{:S(2)}) collective-permute-start(bf16[384,256]{1,0:T(8,128)(2,1)S(1)} %attend.2.rest_0_), channel_id=1, source_target_pairs={{0,2},{1,3},{2,0},{3,1},{4,6},{5,7},{6,4},{7,5},{8,10},{9,11},{10,... | collective-permute-start | bytes 589832 | tf_op jit(solution)/shard_map/ppermute | solution.py:579
  148.3 24.1 %collective-permute-start.24 = (bf16[384,256]{1,0:T(8,128)(2,1)S(1)}, bf16[384,256]{1,0:T(8,128)(2,1)S(1)}, u32[]{:S(2)}, u32[]{:S(2)}) collective-permute-start(bf16[384,256]{1,0:T(8,128)(2,1)S(1)} %attend.2.rest_0_), channel_id=1, source_target_pairs={{0,3},{1,0},{2,1},{3,2},{4,7},{5,4},{6,5},{7,6},{8,11},{9,8},{10,9... | collective-permute-start | bytes 589832 | tf_op jit(solution)/shard_map/ppermute | solution.py:579
  160.9 17.4 %collective-permute-start.32 = (f32[1,384]{1,0:T(1,128)S(1)}, f32[1,384]{1,0:T(1,128)S(1)}, u32[]{:S(2)}, u32[]{:S(2)}) collective-permute-start(f32[1,384]{1,0:T(1,128)S(1)} %get-tuple-element.40.rest_0_), channel_id=1, source_target_pairs={{0,1},{1,2},{2,3},{3,0},{4,5},{5,6},{6,7},{7,4},{8,9},{9,10},{10,1... | collective-permute-start | bytes 4616 | tf_op jit(solution)/shard_map/ppermute | solution.py:582
  169.9 9.8 %collective-permute-start.33 = (f32[1,384]{1,0:T(1,128)S(1)}, f32[1,384]{1,0:T(1,128)S(1)}, u32[]{:S(2)}, u32[]{:S(2)}) collective-permute-start(f32[1,384]{1,0:T(1,128)S(1)} %get-tuple-element.40.rest_0_), channel_id=1, source_target_pairs={{0,2},{1,3},{2,0},{3,1},{4,6},{5,7},{6,4},{7,5},{8,10},{9,11},{10,... | collective-permute-start | bytes 4616 | tf_op jit(solution)/shard_map/ppermute | solution.py:582
  170.8 8.9 %collective-permute-start.34 = (f32[1,384]{1,0:T(1,128)S(1)}, f32[1,384]{1,0:T(1,128)S(1)}, u32[]{:S(2)}, u32[]{:S(2)}) collective-permute-start(f32[1,384]{1,0:T(1,128)S(1)} %get-tuple-element.40.rest_0_), channel_id=1, source_target_pairs={{0,3},{1,0},{2,1},{3,2},{4,7},{5,4},{6,5},{7,6},{8,11},{9,8},{10,9... | collective-permute-start | bytes 4616 | tf_op jit(solution)/shard_map/ppermute | solution.py:582
  175.8 5.8 %collective-permute-start.25 = (f32[1,384]{1,0:T(1,128)S(1)}, f32[1,384]{1,0:T(1,128)S(1)}, u32[]{:S(2)}, u32[]{:S(2)}) collective-permute-start(f32[1,384]{1,0:T(1,128)S(1)} %get-tuple-element.36.rest_0_), channel_id=1, source_target_pairs={{0,1},{1,2},{2,3},{3,0},{4,5},{5,6},{6,7},{7,4},{8,9},{9,10},{10,1... | collective-permute-start | bytes 4616 | tf_op jit(solution)/shard_map/ppermute | solution.py:582
  (28 other events, 226.4 us)
Sparse Core Ops, SparseCore 0:
  17.8 27.3 all-gather.2

commit v4 on v3

--- a/solution.py
+++ b/solution.py
@@ -23,7 +23,8 @@
 F32, BF16 = jnp.float32, jnp.bfloat16
 ANY = pl.BlockSpec(memory_space=pl.ANY)
 HBM = pl.BlockSpec(memory_space=pltpu.HBM)
-PARAMS = pltpu.CompilerParams(vmem_limit_bytes=48 * 1024 * 1024)
+PARAMS = pltpu.CompilerParams(vmem_limit_bytes=40 * 1024 * 1024)
+ALL_VMEM = pltpu.CompilerParams(vmem_limit_bytes=62 * 1024 * 1024)
 
 
 def shape(dims, dtype):
@@ -73,10 +74,13 @@
             num_scalar_prefetch=1,
             grid=(1,),
             in_specs=[HBM, HBM, HBM],
-            out_specs=[ANY, ANY],
+            out_specs=[
+                pl.BlockSpec((share, kv_width), lambda i, at: (0, 0)),
+                pl.BlockSpec((share, q_weight.shape[1]), lambda i, at: (0, 0)),
+            ],
             scratch_shapes=[pltpu.SemaphoreType.DMA((3,))],
         ),
-        compiler_params=pltpu.CompilerParams(vmem_limit_bytes=62 * 1024 * 1024),
+        compiler_params=ALL_VMEM,
         name="pack",
     )(at, q_weight, k_weight, v_weight)
 
@@ -98,7 +102,6 @@
         join_kernel,
         out_shape=shape((2 * first.shape[0],) + first.shape[1:], first.dtype),
         in_specs=[ANY, ANY],
-        out_specs=ANY,
         scratch_shapes=[pltpu.SemaphoreType.DMA((2,))],
         compiler_params=PARAMS,
         name="join",
@@ -113,8 +116,7 @@
         order = order + [k ^ mask for k in order]
         if mask != masks[-1]:
             own = join(own, got)
-    where = jnp.bitwise_xor(lax.axis_index(PLANE), jnp.array(order, jnp.int32))
-    return where, own, got
+    return order, own, got
 
 
 def prep_kernel(src_ref, gain_ref, *rest):
@@ -150,19 +152,17 @@
     )(sources, gains, tokens, *received)
 
 
-def far_kernel(where_ref, src_ref, x_ref, *rest, with_sq):
-    if with_sq:
-        sq_ref, own_ref, got_ref, out_ref, weight, sems = rest
-    else:
-        own_ref, got_ref, out_ref, weight, sems = rest
-    held, share, _ = own_ref.shape
-    copies = []
-    for i in range(2 * held):
-        piece = own_ref.at[i] if i < held else got_ref.at[i - held]
-        row = pl.multiple_of(where_ref[i] * share, TAIL)
-        copies.append(
-            pltpu.make_async_copy(piece, weight.at[pl.ds(row, share)], sems.at[i])
-        )
+def far_kernel(place_ref, src_ref, x_ref, sq_ref, *rest, orders):
+    pieces, (out_ref, weight, sems) = rest[:-3], rest[-3:]
+    copies, column = [], 0
+    for order, own_ref, got_ref in zip(orders, pieces[::2], pieces[1::2]):
+        held, share, width = own_ref.shape
+        for i, mask in enumerate(order):
+            piece = own_ref.at[i] if i < held else got_ref.at[i - held]
+            row = pl.multiple_of((place_ref[0] ^ mask) * share, TAIL)
+            there = weight.at[pl.ds(row, share), pl.ds(column, width)]
+            copies.append(pltpu.make_async_copy(piece, there, sems.at[len(copies)]))
+        column += width
     for copy in copies:
         copy.start()
     for copy in copies:
@@ -174,97 +174,98 @@
         term = jnp.dot(x_ref[k], weight[pl.ds(row, cols), :], preferred_element_type=F32)
         total = term if total is None else total + term
     out_ref[:chunk, :] = total.astype(BF16)
-    if with_sq:
-        width = out_ref.shape[1]
-        sq = sq_ref[...]
-        high = sq.astype(BF16).astype(F32)
-        lines = []
-        for part in (high, sq - high):
-            for at in range(0, chunk, width):
-                line = part[:, at : at + width]
-                if line.shape[1] < width:
-                    line = jnp.concatenate(
-                        [line, jnp.zeros((1, width - line.shape[1]), F32)], axis=1
-                    )
-                lines.append(line)
-        lines.append(jnp.zeros((TAIL - len(lines), width), F32))
-        out_ref[chunk:, :] = jnp.concatenate(lines, axis=0).astype(BF16)
-
-
-def far_product(where, sources, x, pieces, sq):
-    own, got = pieces
-    held, share, width = own.shape
+    sq = sq_ref[...]
+    high = sq.astype(BF16).astype(F32)
+    out_ref[chunk:, :] = lines_of((high, sq - high), out_ref.shape[1])
+
+
+def lines_of(rows, width):
+    lines = []
+    for row in rows:
+        for at in range(0, row.shape[1], width):
+            line = row[:, at : at + width]
+            if line.shape[1] < width:
+                rest = jnp.zeros((1, width - line.shape[1]), F32)
+                line = jnp.concatenate([line, rest], axis=1)
+            lines.append(line)
+    lines.append(jnp.zeros((TAIL - len(lines), width), F32))
+    return jnp.concatenate(lines, axis=0).astype(BF16)
+
+
+def rows_of(tail, count, length):
+    per_row = -(-length // tail.shape[1])
+    rows = []
+    for r in range(count):
+        lines = [tail[r * per_row + i : r * per_row + i + 1, :] for i in range(per_row)]
+        rows.append(jnp.concatenate(lines, axis=1)[:, :length])
+    return rows
+
+
+def far_product(place, sources, x, gathered, sq):
+    orders = [g[0] for g in gathered]
+    pieces = [piece for g in gathered for piece in g[1:]]
+    width = sum(g[1].shape[2] for g in gathered)
+    share = pieces[0].shape[1]
     count, chunk, cols = x.shape
-    with_sq = sq is not None
-    rows = chunk + (TAIL if with_sq else 0)
-    extra = [pl.BlockSpec((1, chunk), lambda i, w, s: (0, 0))] if with_sq else []
-    return pl.pallas_call(
-        partial(far_kernel, with_sq=with_sq),
-        out_shape=shape((rows, width), BF16),
+    return pl.pallas_call(
+        partial(far_kernel, orders=orders),
+        out_shape=shape((chunk + TAIL, width), BF16),
         grid_spec=pltpu.PrefetchScalarGridSpec(
             num_scalar_prefetch=2,
             grid=(1,),
-            in_specs=[pl.BlockSpec((count, chunk, cols), lambda i, w, s: (0, 0, 0))]
-            + extra
-            + [ANY, ANY],
-            out_specs=pl.BlockSpec((rows, width), lambda i, w, s: (0, 0)),
+            in_specs=[
+                pl.BlockSpec((count, chunk, cols), lambda i, p, s: (0, 0, 0)),
+                pl.BlockSpec((1, chunk), lambda i, p, s: (0, 0)),
+            ]
+            + [ANY for _ in pieces],
+            out_specs=pl.BlockSpec((chunk + TAIL, width), lambda i, p, s: (0, 0)),
             scratch_shapes=[
-                pltpu.VMEM((2 * held * share, width), BF16),
-                pltpu.SemaphoreType.DMA((2 * held,)),
+                pltpu.VMEM((len(orders[0]) * share, width), BF16),
+                pltpu.SemaphoreType.DMA((sum(len(o) for o in orders),)),
             ],
         ),
         compiler_params=PARAMS,
         name="far",
-    )(where, sources, x, *([sq] if with_sq else []), own, got)
-
-
-def near_kernel(src_ref, x_ref, q_ref, k_ref, v_ref, after_ref, kv_out, q_out):
-    step = pl.program_id(0)
+    )(place, sources, x, sq, *pieces)
+
+
+def near_kernel(src_ref, x_ref, k_ref, v_ref, q_ref, after_ref, out_ref):
     x = x_ref[0]
-    width = k_ref.shape[1]
-    dot = partial(jnp.dot, preferred_element_type=F32)
-
-    @pl.when(step == 0)
+
+    @pl.when(pl.program_id(0) == 0)
     def _():
-        kv_out[...] = jnp.zeros_like(kv_out)
-        q_out[...] = jnp.zeros_like(q_out)
-
-    kv_out[:, :width] += dot(x, k_ref[...])
-    kv_out[:, width:] += dot(x, v_ref[...])
-    q_out[...] += dot(x, q_ref[...])
-
-
-def near_product(blocks, x, q_weight, k_weight, v_weight, after):
+        out_ref[...] = jnp.zeros_like(out_ref)
+
+    column = 0
+    for ref in (k_ref, v_ref, q_ref):
+        at = slice(column, column + ref.shape[1])
+        out_ref[:, at] += jnp.dot(x, ref[...], preferred_element_type=F32)
+        column += ref.shape[1]
+
+
+def near_product(blocks, x, weights, after):
     count, chunk, cols = x.shape
-    widths = [w.shape[1] for w in (q_weight, k_weight, v_weight)]
-    kv_width = widths[1] + widths[2]
+    widths = [w.shape[1] for w in weights]
     return pl.pallas_call(
         near_kernel,
-        out_shape=(shape((chunk, kv_width), F32), shape((chunk, widths[0]), F32)),
+        out_shape=shape((chunk, sum(widths)), F32),
         grid_spec=pltpu.PrefetchScalarGridSpec(
             num_scalar_prefetch=1,
             grid=(count,),
             in_specs=[pl.BlockSpec((1, chunk, cols), lambda i, s: (i, 0, 0))]
             + [pl.BlockSpec((cols, w), lambda i, s: (s[i], 0)) for w in widths]
             + [ANY],
-            out_specs=[
-                pl.BlockSpec((chunk, kv_width), lambda i, s: (0, 0)),
-                pl.BlockSpec((chunk, widths[0]), lambda i, s: (0, 0)),
-            ],
+            out_specs=pl.BlockSpec((chunk, sum(widths)), lambda i, s: (0, 0)),
         ),
         compiler_params=PARAMS,
         name="near",
-    )(blocks, x, q_weight, k_weight, v_weight, after)
-
-
-def keys_kernel(near_ref, far_ref, sq_ref, cos_ref, sin_ref, out_ref, sum_ref, *, model):
+    )(blocks, x, *weights, after)
+
+
+def keys_kernel(near_ref, far_ref, sq_ref, id_ref, cos_ref, sin_ref, out_ref, sum_ref, *, model):
     chunk, width = near_ref.shape
     tail = far_ref[chunk:, :].astype(F32)
-    lines = -(-chunk // width)
-    total = sq_ref[...]
-    for part in range(2):
-        row = [tail[part * lines + i : part * lines + i + 1, :] for i in range(lines)]
-        total = total + jnp.concatenate(row, axis=1)[:, :chunk]
+    total = sum(rows_of(tail, 2, chunk), sq_ref[...])
     factor = to_column(lax.rsqrt(total / model + epsilon))
     sum_ref[...] = total
     for c in range(0, width, HEAD_SIZE):
@@ -272,34 +273,36 @@
         part = (near_ref[:, at] + far_ref[:chunk, at].astype(F32)) * factor
         if c < width // 2:
             part = rotate(part, cos_ref[...], sin_ref[...])
-        out_ref[:, at] = part.astype(BF16)
-
-
-def keys_values(near, far, sq, cosine, sine, c, model):
-    chunk, width = near.shape
+        out_ref[:chunk, at] = part.astype(BF16)
+    out_ref[chunk:, :] = lines_of((id_ref[...].astype(F32),), width)
+
+
+def keys_values(near, far, sq, ids, cosine, sine, c, width, model):
+    chunk = near.shape[0]
     whole = lambda i: (0, 0)
     return pl.pallas_call(
         partial(keys_kernel, model=model),
-        out_shape=(shape((chunk, width), BF16), shape((1, chunk), F32)),
+        out_shape=(shape((chunk + TAIL, width), BF16), shape((1, chunk), F32)),
         grid=(1,),
         in_specs=[
-            pl.BlockSpec(near.shape, whole),
+            pl.BlockSpec((chunk, width), whole),
             pl.BlockSpec(far.shape, whole),
             pl.BlockSpec((1, chunk), whole),
+            pl.BlockSpec((1, chunk), lambda i: (0, c)),
             pl.BlockSpec((chunk, HEAD_SIZE), lambda i: (c, 0)),
             pl.BlockSpec((chunk, HEAD_SIZE), lambda i: (c, 0)),
         ],
-        out_specs=[pl.BlockSpec((chunk, width), whole), pl.BlockSpec((1, chunk), whole)],
+        out_specs=[pl.BlockSpec((chunk + TAIL, width), whole), pl.BlockSpec((1, chunk), whole)],
         compiler_params=PARAMS,
         name="keys",
-    )(near, far, sq, cosine, sine)
+    )(near, far, sq, ids, cosine, sine)
 
 
 def attention_kernel(
-    lo_ref, near_ref, far_ref, sum_ref, cos_ref, sin_ref, start_ref, *rest, back, offset, model
+    seq_ref, near_ref, far_ref, sum_ref, cos_ref, sin_ref, id_ref, *rest, back, offset, model
 ):
-    kv_refs, (out_ref, k_scr, vt_scr) = rest[:-3], rest[-3:]
-    part_rows = kv_refs[0].shape[0]
+    kv_refs, (out_ref, k_scr, vt_scr, id_scr) = rest[:-4], rest[-4:]
+    part_rows = kv_refs[0].shape[0] - TAIL
     group = near_ref.shape[1] // HEAD_SIZE
     tile = pl.program_id(0)
 
@@ -307,8 +310,11 @@
     def _():
         for b, kv_ref in enumerate(kv_refs):
             at = slice(b * part_rows, (b + 1) * part_rows)
-            k_scr[at, :] = kv_ref[:, :HEAD_SIZE]
-            vt_scr[:, at] = kv_ref[:, HEAD_SIZE:].astype(F32).T.astype(BF16)
+            k_scr[at, :] = kv_ref[:part_rows, :HEAD_SIZE]
+            vt_scr[:, at] = kv_ref[:part_rows, HEAD_SIZE:].astype(F32).T.astype(BF16)
+            (ids,) = rows_of(kv_ref[part_rows:, :].astype(F32), 1, part_rows)
+            exists = b // CHUNKS >= back - seq_ref[0]
+            id_scr[at, :] = to_column(jnp.where(exists, ids, -1.0))
 
     scale = query_scale * math.log2(math.e)
     factor = to_column(lax.rsqrt(sum_ref[...] / model + epsilon) * scale)
@@ -319,7 +325,11 @@
         heads.append(rotate(part, cos_ref[...], sin_ref[...]).astype(BF16))
     q2 = jnp.concatenate(heads, axis=0)
     width = group * Q_TILE
-    start = jnp.concatenate([start_ref[...]] * group, axis=1)
+
+    before = (id_scr[...] < id_ref[...].astype(F32)).astype(F32)
+    start = jnp.sum(before, axis=0, keepdims=True).astype(jnp.int32)
+    low = jnp.min(start) // K_TILE
+    start = jnp.concatenate([start] * group, axis=1)
     first = back * part_rows * CHUNKS + offset + tile * Q_TILE
     place = first + lax.broadcasted_iota(jnp.int32, (1, Q_TILE), 1)
     place = jnp.concatenate([place] * group, axis=1)
@@ -333,7 +343,6 @@
             preferred_element_type=F32,
         )
 
-    low = lo_ref[tile]
     stop = (first + Q_TILE + K_TILE - 1) // K_TILE
 
     def step(j, state):
@@ -366,13 +375,13 @@
         ].astype(BF16)
 
 
-def attend(near, far, sums, cosine, sine, start, blocks, c, model):
-    rows, width = near.shape
-    part_rows = blocks[0].shape[0]
+def attend(seq, near, far, sums, cosine, sine, ids, blocks, c, width, model):
+    rows = near.shape[0]
+    part_rows = blocks[0].shape[0] - TAIL
     back = len(blocks) // CHUNKS - 1
     tiles = rows // Q_TILE
-    low = start[c * rows : (c + 1) * rows : Q_TILE] // K_TILE
     keys = len(blocks) * part_rows
+    last = near.shape[1] // width - 1
     return pl.pallas_call(
         partial(attention_kernel, back=back, offset=c * rows, model=model),
         out_shape=shape((rows, width), BF16),
@@ -380,23 +389,24 @@
             num_scalar_prefetch=1,
             grid=(tiles,),
             in_specs=[
-                pl.BlockSpec((Q_TILE, width), lambda i, lo: (i, 0)),
-                pl.BlockSpec((Q_TILE, width), lambda i, lo: (i, 0)),
-                pl.BlockSpec((1, Q_TILE), lambda i, lo: (0, i)),
-                pl.BlockSpec((Q_TILE, HEAD_SIZE), lambda i, lo: (c * tiles + i, 0)),
-                pl.BlockSpec((Q_TILE, HEAD_SIZE), lambda i, lo: (c * tiles + i, 0)),
-                pl.BlockSpec((1, Q_TILE), lambda i, lo: (0, c * tiles + i)),
+                pl.BlockSpec((Q_TILE, width), lambda i, s: (i, last)),
+                pl.BlockSpec((Q_TILE, width), lambda i, s: (i, last)),
+                pl.BlockSpec((1, Q_TILE), lambda i, s: (0, i)),
+                pl.BlockSpec((Q_TILE, HEAD_SIZE), lambda i, s: (c * tiles + i, 0)),
+                pl.BlockSpec((Q_TILE, HEAD_SIZE), lambda i, s: (c * tiles + i, 0)),
+                pl.BlockSpec((1, Q_TILE), lambda i, s: (0, c * tiles + i)),
             ]
-            + [pl.BlockSpec(b.shape, lambda i, lo: (0, 0)) for b in blocks],
-            out_specs=pl.BlockSpec((Q_TILE, width), lambda i, lo: (i, 0)),
+            + [pl.BlockSpec(b.shape, lambda i, s: (0, 0)) for b in blocks],
+            out_specs=pl.BlockSpec((Q_TILE, width), lambda i, s: (i, 0)),
             scratch_shapes=[
                 pltpu.VMEM((keys, HEAD_SIZE), BF16),
                 pltpu.VMEM((HEAD_SIZE, keys), BF16),
+                pltpu.VMEM((keys, LANES), F32),
             ],
         ),
         compiler_params=PARAMS,
         name="attend",
-    )(low, near, far, sums, cosine, sine, start[None, :], *blocks)
+    )(seq, near, far, sums, cosine, sine, ids, *blocks)
 
 
 def output_kernel(z_ref, own_o_ref, o_ref, *rest):
@@ -404,8 +414,8 @@
     step = pl.program_id(0)
     plane, _, share, tile = o_ref.shape
     total = jnp.dot(ctx_refs[0][...], own_o_ref[...], preferred_element_type=F32)
-    for k, ctx_ref in enumerate(ctx_refs[1:]):
-        weight = o_ref[:, k].reshape(plane * share, tile)
+    for i, ctx_ref in enumerate(ctx_refs[1:]):
+        weight = o_ref[:, z_ref[1 + i]].reshape(plane * share, tile)
         total = total + jnp.dot(ctx_ref[...], weight, preferred_element_type=F32)
     out_ref[...] = total
     squares = jnp.sum(total * total, axis=1, keepdims=True)
@@ -432,7 +442,7 @@
     whole = lambda i, z: (0, 0)
     if cols % LANES:
         o_weight = lax.dynamic_slice_in_dim(o_weight, z[0] * cols, cols, axis=1)
-        z = z * 0
+        z = z.at[0].set(0)
     return pl.pallas_call(
         output_kernel,
         out_shape=(shape((chunk, cols), F32), shape((1, chunk), F32)),
@@ -517,8 +527,8 @@
     packed_kv, packed_q = pack(at, q_weight, k_weight, value_weight, share)
     far_kv = lax.ppermute(packed_kv, "tensor", swap)
     far_q = lax.ppermute(packed_q, "tensor", swap)
-    where_kv, *far_kv = spread(far_kv, plane, seq_bits + group_bits + [1])
-    where_q, *far_q = spread(far_q, plane, group_bits + seq_bits + [1])
+    far_kv = spread(far_kv, plane, seq_bits + group_bits + [1])
+    far_q = spread(far_q, plane, group_bits + seq_bits + [1])
 
     chunk = rows // CHUNKS
     sources = (within + half - jnp.arange(half, dtype=jnp.int32)) % half
@@ -533,50 +543,60 @@
             blocks.append(held)
         received.append(blocks)
 
+    cosine, sine = rotation_table(seq * rows + jnp.arange(rows, dtype=jnp.int32))
+    ids = seg_ids[None, :]
+    weights = (k_weight, value_weight, q_weight)
+    kv_width = k_weight.shape[1] + value_weight.shape[1]
+    place = jnp.reshape(in_plane, (1,))
+    prepared, sent = [], []
+    for c in range(CHUNKS):
+        prepared.append(prep(blocks_of, gains, tokens, received[c], chunk, c))
+        sent.append(far_product(place, sources, prepared[c][0], [far_kv, far_q], prepared[c][1]))
+    kv_parts, q_parts = [], []
+    for c in range(CHUNKS):
+        x, sq = prepared[c]
+        got = lax.ppermute(sent[c], "tensor", swap)
+        near = near_product(blocks_of, x, weights, sent[-1])
+        own_kv, sums = keys_values(near, got, sq, ids, cosine, sine, c, kv_width, model)
+        kv_parts.append(own_kv)
+        q_parts.append((near, got, sums))
+
+    back = -(-(nseq * rows // 2 - 1) // rows)
+    blocks = list(kv_parts)
+    for k in range(1, back + 1):
+        earlier = [(i, i + k) for i in range(nseq - k)]
+        blocks = [lax.ppermute(part, "seq", earlier) for part in kv_parts] + blocks
+
     o_share = o_weight.shape[0] // plane
+    last = sent[-1][0, 0]
+    wait = (last != last).astype(jnp.int32)
     moved = []
     for k in range(1, nz):
         target = (z + k) % nz
         piece = lax.dynamic_slice(
-            o_weight, (in_plane * o_share, target * cols), (o_share, cols)
+            o_weight, (in_plane * o_share + wait, target * cols), (o_share, cols)
         )
         moved.append(lax.ppermute(piece, "tensor", turn(k)))
     gathered_o = lax.all_gather(jnp.stack(moved), PLANE)
 
-    back = -(-(nseq * rows // 2 - 1) // rows)
-    earlier = lambda k: [(i, i + k) for i in range(nseq - k)]
-    start = jnp.sum((seg_ids[None, :] < seg_ids[:, None]).astype(jnp.int32), axis=1)
-    start = start + back * rows
-    for k in range(1, back + 1):
-        ids = lax.ppermute(seg_ids, "seq", earlier(k))
-        ids = jnp.where(seq >= k, ids, -1)
-        start = start - jnp.sum((ids[None, :] >= seg_ids[:, None]).astype(jnp.int32), axis=1)
-
-    cosine, sine = rotation_table(seq * rows + jnp.arange(rows, dtype=jnp.int32))
-
-    kv_parts, q_parts = [], []
+    out = None
+    order = list(range(nz - 1))
+    if nz == 4:
+        order = [1, 0, 2, jnp.where(z < half, 0, 2)]
+    z_at = jnp.stack([z] + [jnp.int32(k) for k in order])
+    seq_at = jnp.reshape(seq, (1,))
+    q_width = q_weight.shape[1]
     for c in range(CHUNKS):
-        x, sq = prep(blocks_of, gains, tokens, received[c], chunk, c)
-        sent_kv = far_product(where_kv, sources, x, far_kv, sq)
-        sent_q = far_product(where_q, sources, x, far_q, None)
-        got_kv = lax.ppermute(sent_kv, "tensor", swap)
-        got_q = lax.ppermute(sent_q, "tensor", swap)
-        near_kv, near_q = near_product(
-            blocks_of, x, q_weight, k_weight, value_weight, sent_q
-        )
-        own_kv, sums = keys_values(near_kv, got_kv, sq, cosine, sine, c, model)
-        kv_parts.append(own_kv)
-        q_parts.append((near_q, got_q, sums))
-    blocks = list(kv_parts)
-    for k in range(1, back + 1):
-        blocks = [lax.ppermute(part, "seq", earlier(k)) for part in kv_parts] + blocks
-
-    out = None
-    z_at = jnp.reshape(z, (1,))
-    for c in range(CHUNKS):
-        context = attend(*q_parts[c], cosine, sine, start, blocks, c, model)
-        contexts = [context]
-        contexts += [lax.ppermute(context, "tensor", turn(k)) for k in range(1, nz)]
+        context = attend(seq_at, *q_parts[c], cosine, sine, ids, blocks, c, q_width, model)
+        if nz == 4:
+            opposite = lax.ppermute(context, "tensor", swap)
+            right = lax.ppermute(context, "tensor", [(0, 1), (1, 2), (2, 3)])
+            left = lax.ppermute(context, "tensor", [(1, 0), (2, 1), (3, 2)])
+            far_end = lax.ppermute(opposite, "tensor", [(2, 3), (1, 0)])
+            contexts = [context, opposite, right, left, far_end]
+        else:
+            contexts = [context]
+            contexts += [lax.ppermute(context, "tensor", turn(k)) for k in range(1, nz)]
         branch, own_sq = output_product(z_at, o_weight, gathered_o, contexts)
         sums = [own_sq]
         sums += [lax.ppermute(own_sq, "tensor", turn(k)) for k in range(1, nz)]

time: 193 us -> 215 us (1.11)
  waiting for transfers between devices: 31.8 us -> 95.2 us
  Pallas kernels: 69.5 us -> 41.3 us
  starting transfers between devices: 55.3 us -> 47.2 us
  other arithmetic: 5.94 us -> 2.46 us
  local copies, waits for them, and re-layouts: 14.2 us -> 11.6 us
    ppermute x2, waiting for transfers between devices: 0.02 us -> 27.5 us  [per_device(): held = lax.ppermute(held, 'tensor', ring)]
    ppermute x16 -> x14, waiting for transfers between devices: 13.8 us -> 39.3 us  [the longest x2 23 us: per_device(): got = lax.ppermute(sent[c], 'tensor', swap)]
    pallas_call x4, Pallas kernels: 11.6 us -> 2.66 us  [join(): pl.pallas_call(join_kernel, out_shape=shape((2 * first.shape[0],) + first...]
    pallas_call x1, Pallas kernels: 10.1 us -> 1.84 us  [pack(): pl.pallas_call(pack_kernel, out_shape=(shape((share, kv_width), BF16), sh...]
    pallas_call x6 -> x4, Pallas kernels: 19.7 us -> 12.3 us  [the longest x2 7.31 us: far_product(): pl.pallas_call(partial(far_kernel, orders=orders), out_shape=shape((chunk...]
    ppermute x6, starting transfers between devices: 15.3 us -> 10.1 us  [per_device(): sums += [lax.ppermute(own_sq, 'tensor', turn(k)) for k in range(1, nz)]]
    ppermute x1, waiting for transfers between devices: 6.9 us -> 11.2 us  [per_device(): far_kv = lax.ppermute(packed_kv, 'tensor', swap)]
    ppermute x6, waiting for transfers between devices: 0.31 us -> 3.41 us  [per_device(): sums += [lax.ppermute(own_sq, 'tensor', turn(k)) for k in range(1, nz)]]
  transfers between devices with their start and end apart: 36 -> 34, of which waited for: 13 -> 17; matrix products, arithmetic and copies ran while one was open for 7% -> 2% of each run, Pallas kernels for 35% -> 16%
where the time goes in v4:
time: 215 us; the launch traced here: 213 us
  waiting for transfers between devices  95.2 us (44%)
  starting transfers between devices  47.2 us (22%)
  Pallas kernels  41.3 us (19%)
  between operations  14.9 us (7%)
  local copies, waits for them, and re-layouts  11.6 us (5%)
  other arithmetic  2.46 us (1%)
    ppermute x2, waiting for transfers between devices, per_device(): held = lax.ppermute(held, 'tensor', ring)  27.5 us
    ppermute x2, waiting for transfers between devices, per_device(): got = lax.ppermute(sent[c], 'tensor', swap)  23 us
    ppermute x1, waiting for transfers between devices, per_device(): far_kv = lax.ppermute(packed_kv, 'tensor', swap)  11.2 us
    ppermute x6, starting transfers between devices, per_device(): sums += [lax.ppermute(own_sq, 'tensor', turn(k)) for k in range(1, nz)]  10.1 us
    ppermute x4, waiting for transfers between devices, per_device(): blocks = [lax.ppermute(part, 'seq', earlier) for part in kv_parts] + blocks  9.5 us
    pallas_call x2, Pallas kernels, attend(): pl.pallas_call(partial(attention_kernel, back=back, offset=c * rows, mode...  8.98 us
    pallas_call x2, Pallas kernels, output_product(): pl.pallas_call(output_kernel, out_shape=(shape((chunk, cols), F32), shape...  7.68 us
    unnamed x28, local copies, waits for them, and re-layouts  7.47 us
  transfers between devices with their start and end apart: 34, of which 17 were waited for; matrix products, arithmetic and copies ran while one was open for 2% of the time, Pallas kernels for 16%

profile of v4, /device:TPU:2, one launch (start us, length us, event | category | flops | bytes accessed | tf_op | source)
XLA Modules:
  0.0 212.6 jit_solution(11388495079454624452)
XLA Ops:
  8.4 2.7 %collective-permute-start.1 = (bf16[288,256]{1,0:T(8,128)(2,1)}, bf16[288,256]{1,0:T(8,128)(2,1)S(1)}, u32[]{:S(2)}, u32[]{:S(2)}) collective-permute-start(bf16[288,256]{1,0:T(8,128)(2,1)} %get-tuple-element.21), channel_id=1, source_target_pairs={{0,2},{1,3},{2,0},{3,1},{4,6},{5,7},{6,4},{7,5},{8,10},{9,11},{10,... | collective-permute-start | bytes 442376 | tf_op jit(solution)/shard_map/ppermute | solution.py:528
  11.4 11.2 %collective-permute-done.1 = bf16[288,256]{1,0:T(8,128)(2,1)S(1)} collective-permute-done((bf16[288,256]{1,0:T(8,128)(2,1)}, bf16[288,256]{1,0:T(8,128)(2,1)S(1)}, u32[]{:S(2)}, u32[]{:S(2)}) %collective-permute-start.1) | collective-permute-done | bytes 147488 | tf_op jit(solution)/shard_map/ppermute | solution.py:528
  22.8 1.8 collective-permute-done.5
  30.7 6.1 %collective-permute-done.3.second_ref = bf16[2,288,256]{2,1,0:T(8,128)(2,1)S(1)} collective-permute-done((bf16[2,288,256]{2,1,0:T(8,128)(2,1)S(1)}, bf16[2,288,256]{2,1,0:T(8,128)(2,1)S(1)}, u32[]{:S(2)}, u32[]{:S(2)}) %collective-permute-start.3) | collective-permute-done | bytes 294944 | tf_op jit(solution)/shard_map/ppermute | solution.py:115
  40.7 6.8 %collective-permute-done.rest_1_ = bf16[384,1152]{1,0:T(8,128)(2,1)S(1)} collective-permute-done((bf16[384,1152]{1,0:T(8,128)(2,1)S(1)}, bf16[384,1152]{1,0:T(8,128)(2,1)S(1)}, u32[]{:S(2)}, u32[]{:S(2)}) %collective-permute-start) | collective-permute-done | bytes 884768 | tf_op jit(solution)/shard_map/ppermute | solution.py:542
  51.5 3.6 %far.2.after_ref = bf16[400,512]{1,0:T(8,128)(2,1)S(1)} custom-call(s32[1]{0:T(128)} %bitcast.2.place_ref, s32[2]{0:T(128)S(1)} %and_select_fusion.src_ref, bf16[2,384,1152]{2,1,0:T(8,128)(2,1)S(1)} %get-tuple-element.19.x_ref, f32[1,384]{1,0:T(1,128)S(1)} %get-tuple-element.20.sq_ref, bf16[4,288,256]{2,1,0:T(8,128)(2,1)} %join.5.rest_0_, ...), custom_call_target="tpu_custom_call" | custom-call | tf_op jit(solution)/shard_map/far/pallas_call | solution.py:210
  60.4 2.8 %collective-permute-start.11 = (bf16[32,1152]{1,0:T(8,128)(2,1)S(1)}, bf16[32,1152]{1,0:T(8,128)(2,1)S(1)}, u32[]{:S(2)}, u32[]{:S(2)}) collective-permute-start(bf16[32,1152]{1,0:T(8,128)(2,1)S(1)} %get-tuple-element.34), channel_id=1, source_target_pairs={{0,3},{1,0},{2,1},{3,2},{4,7},{5,4},{6,5},{7,6},{8,11},{9,8},{10,9... | collective-permute-start | bytes 221192 | tf_op jit(solution)/shard_map/ppermute | solution.py:579
  64.0 2.3 %collective-permute-done.9 = bf16[32,1152]{1,0:T(8,128)(2,1)S(1)} collective-permute-done((bf16[32,1152]{1,0:T(8,128)(2,1)S(1)}, bf16[32,1152]{1,0:T(8,128)(2,1)S(1)}, u32[]{:S(2)}, u32[]{:S(2)}) %collective-permute-start.9) | collective-permute-done | bytes 73760 | tf_op jit(solution)/shard_map/ppermute | solution.py:579
  66.3 3.4 %collective-permute-done.10 = bf16[32,1152]{1,0:T(8,128)(2,1)S(1)} collective-permute-done((bf16[32,1152]{1,0:T(8,128)(2,1)S(1)}, bf16[32,1152]{1,0:T(8,128)(2,1)S(1)}, u32[]{:S(2)}, u32[]{:S(2)}) %collective-permute-start.10) | collective-permute-done | bytes 73760 | tf_op jit(solution)/shard_map/ppermute | solution.py:579
  70.5 20.7 %collective-permute-done.13.rest_1_ = bf16[384,1152]{1,0:T(8,128)(2,1)} collective-permute-done((bf16[384,1152]{1,0:T(8,128)(2,1)}, bf16[384,1152]{1,0:T(8,128)(2,1)}, u32[]{:S(2)}, u32[]{:S(2)}) %collective-permute-start.13) | collective-permute-done | bytes 884768 | tf_op jit(solution)/shard_map/ppermute | solution.py:542
  91.9 2.4 %prep.3 = (bf16[2,384,1152]{2,1,0:T(8,128)(2,1)S(1)}, f32[1,384]{1,0:T(1,128)S(1)}) custom-call(s32[2]{0:T(128)S(1)} %broadcast_add_fusion.src_ref, f32[4,1,1152]{2,1,0:T(1,128)S(1)} %copy-done.11, bf16[768,1152]{1,0:T(8,128)(2,1)S(1)} %copy-done, bf16[384,1152]{1,0:T(8,128)(2,1)} %collective-permute-done.13.rest_1_), custom_call_target="tpu_custom_call" | custom-call | tf_op jit(solution)/shard_map/prep/pallas_call | solution.py:134
  96.0 3.7 %far.3 = bf16[400,512]{1,0:T(8,128)(2,1)S(1)} custom-call(s32[1]{0:T(128)} %bitcast.2.place_ref, s32[2]{0:T(128)S(1)} %and_select_fusion.src_ref, bf16[2,384,1152]{2,1,0:T(8,128)(2,1)S(1)} %get-tuple-element.24.x_ref, f32[1,384]{1,0:T(1,128)S(1)} %get-tuple-element.25.sq_ref, bf16[4,288,256]{2,1,0:T(8,128)(2,1)} %join.5.rest_0_, ...), custom_call_target="tpu_custom_call" | custom-call | tf_op jit(solution)/shard_map/far/pallas_call | solution.py:210
  102.9 2.5 %near.3.near_ref = f32[384,512]{1,0:T(8,128)S(1)} custom-call(s32[2]{0:T(128)S(1)} %broadcast_add_fusion.src_ref, bf16[2,384,1152]{2,1,0:T(8,128)(2,1)S(1)} %get-tuple-element.24.x_ref, bf16[4608,128]{1,0:T(8,128)(2,1)S(1)} %copy-done.2, bf16[4608,128]{1,0:T(8,128)(2,1)S(1)} %copy-done.3, bf16[4608,256]{1,0:T(8,128)(2,1)S(1)} %copy-done.1, ...), custom_call_target="tpu_custom_call" | custom-call | tf_op jit(solution)/shard_map/near/pallas_call | solution.py:249
  105.4 2.5 %near.2.near_ref = f32[384,512]{1,0:T(8,128)S(1)} custom-call(s32[2]{0:T(128)S(1)} %broadcast_add_fusion.src_ref, bf16[2,384,1152]{2,1,0:T(8,128)(2,1)S(1)} %get-tuple-element.19.x_ref, bf16[4608,128]{1,0:T(8,128)(2,1)S(1)} %copy-done.2, bf16[4608,128]{1,0:T(8,128)(2,1)S(1)} %copy-done.3, bf16[4608,256]{1,0:T(8,128)(2,1)S(1)} %copy-done.1, ...), custom_call_target="tpu_custom_call" | custom-call | tf_op jit(solution)/shard_map/near/pallas_call | solution.py:249
  107.9 23.0 %collective-permute-done.14.far_ref = bf16[400,512]{1,0:T(8,128)(2,1)S(1)} collective-permute-done((bf16[400,512]{1,0:T(8,128)(2,1)S(1)}, bf16[400,512]{1,0:T(8,128)(2,1)S(1)}, u32[]{:S(2)}, u32[]{:S(2)}) %collective-permute-start.14) | collective-permute-done | bytes 409632 | tf_op jit(solution)/shard_map/ppermute | solution.py:558
  131.2 1.9 collective-permute-start.17
  134.7 1.9 collective-permute-start.18
  138.2 4.8 %collective-permute-done.15.rest_0_ = bf16[400,256]{1,0:T(8,128)(2,1)S(1)} collective-permute-done((bf16[400,256]{1,0:T(8,128)(2,1)S(1)}, bf16[400,256]{1,0:T(8,128)(2,1)S(1)}, u32[]{:S(2)}, u32[]{:S(2)}) %collective-permute-start.15) | collective-permute-done | bytes 204832 | tf_op jit(solution)/shard_map/ppermute | solution.py:568
  143.0 3.6 %collective-permute-done.18.rest_3_ = bf16[400,256]{1,0:T(8,128)(2,1)S(1)} collective-permute-done((bf16[400,256]{1,0:T(8,128)(2,1)S(1)}, bf16[400,256]{1,0:T(8,128)(2,1)S(1)}, u32[]{:S(2)}, u32[]{:S(2)}) %collective-permute-start.18) | collective-permute-done | bytes 204832 | tf_op jit(solution)/shard_map/ppermute | solution.py:568
  147.4 4.5 %attend.3.rest_0_ = bf16[384,256]{1,0:T(8,128)(2,1)S(1)} custom-call(s32[1]{0:T(128)} %bitcast.11.seq_ref, f32[384,512]{1,0:T(8,128)S(1)} %near.3.near_ref, bf16[400,512]{1,0:T(8,128)(2,1)S(1)} %collective-permute-done.14.far_ref, f32[1,384]{1,0:T(1,128)S(1)} %get-tuple-element.30.sum_ref, f32[768,128]{1,0:T(8,128)S(1)} %get-tuple-element.41.cos_ref, ...), custom_call_target="tpu_custom_call" | custom-call | tf_op jit(solution)/shard_map/attend/pallas_call | solution.py:385
  152.0 4.5 %attend.2.rest_0_ = bf16[384,256]{1,0:T(8,128)(2,1)S(1)} custom-call(s32[1]{0:T(128)} %bitcast.11.seq_ref, f32[384,512]{1,0:T(8,128)S(1)} %near.2.near_ref, bf16[400,512]{1,0:T(8,128)(2,1)S(1)} %collective-permute-done.12.far_ref, f32[1,384]{1,0:T(1,128)S(1)} %get-tuple-element.23.sum_ref, f32[768,128]{1,0:T(8,128)S(1)} %get-tuple-element.41.cos_ref, ...), custom_call_target="tpu_custom_call" | custom-call | tf_op jit(solution)/shard_map/attend/pallas_call | solution.py:385
  156.5 3.0 %collective-permute-start.19 = (bf16[384,256]{1,0:T(8,128)(2,1)S(1)}, bf16[384,256]{1,0:T(8,128)(2,1)S(1)}, u32[]{:S(2)}, u32[]{:S(2)}) collective-permute-start(bf16[384,256]{1,0:T(8,128)(2,1)S(1)} %attend.2.rest_0_), channel_id=1, source_target_pairs={{0,2},{1,3},{2,0},{3,1},{4,6},{5,7},{6,4},{7,5},{8,10},{9,11},{10,... | collective-permute-start | bytes 589832 | tf_op jit(solution)/shard_map/ppermute | solution.py:592
  160.7 4.7 %collective-permute-start.27 = (bf16[384,256]{1,0:T(8,128)(2,1)S(1)}, bf16[384,256]{1,0:T(8,128)(2,1)S(1)}, u32[]{:S(2)}, u32[]{:S(2)}) collective-permute-start(bf16[384,256]{1,0:T(8,128)(2,1)S(1)} %attend.3.rest_0_), channel_id=1, source_target_pairs={{0,1},{1,2},{2,3},{4,5},{5,6},{6,7},{8,9},{9,10},{10,11},{12,13},{... | collective-permute-start | bytes 589832 | tf_op jit(solution)/shard_map/ppermute | solution.py:593
  168.1 4.6 %collective-permute-done.19.rest_1_ = bf16[384,256]{1,0:T(8,128)(2,1)S(1)} collective-permute-done((bf16[384,256]{1,0:T(8,128)(2,1)S(1)}, bf16[384,256]{1,0:T(8,128)(2,1)S(1)}, u32[]{:S(2)}, u32[]{:S(2)}) %collective-permute-start.19) | collective-permute-done | bytes 196640 | tf_op jit(solution)/shard_map/ppermute | solution.py:592
  175.4 2.2 %collective-permute-done.29.rest_4_ = bf16[384,256]{1,0:T(8,128)(2,1)} collective-permute-done((bf16[384,256]{1,0:T(8,128)(2,1)S(1)}, bf16[384,256]{1,0:T(8,128)(2,1)}, u32[]{:S(2)}, u32[]{:S(2)}) %collective-permute-start.29) | collective-permute-done | bytes 196640 | tf_op jit(solution)/shard_map/ppermute | solution.py:595
  180.7 4.3 %output.3 = (f32[384,1152]{1,0:T(8,128)S(1)}, f32[1,384]{1,0:T(1,128)S(1)}) custom-call(s32[5]{0:T(128)S(1)} %stack.23.z_ref, bf16[256,4608]{1,0:T(8,128)(2,1)S(1)} %copy-done.4, bf16[8,3,32,1152]{3,2,1,0:T(8,128)(2,1)S(1)} %bitcast.12, bf16[384,256]{1,0:T(8,128)(2,1)S(1)} %attend.3.rest_0_, bf16[384,256]{1,0:T(8,128)(2,1)S(1)} %collective-permute-done.26.rest_1_, ...), custom_call_target="tpu_custom_call" | custom-call | tf_op jit(solution)/shard_map/output/pallas_call | solution.py:446
  185.0 5.1 %collective-permute-start.32 = (f32[1,384]{1,0:T(1,128)S(1)}, f32[1,384]{1,0:T(1,128)S(1)}, u32[]{:S(2)}, u32[]{:S(2)}) collective-permute-start(f32[1,384]{1,0:T(1,128)S(1)} %get-tuple-element.32.rest_0_), channel_id=1, source_target_pairs={{0,3},{1,0},{2,1},{3,2},{4,7},{5,4},{6,5},{7,6},{8,11},{9,8},{10,9... | collective-permute-start | bytes 4616 | tf_op jit(solution)/shard_map/ppermute | solution.py:602
  190.7 3.4 %output.2 = (f32[384,1152]{1,0:T(8,128)S(1)}, f32[1,384]{1,0:T(1,128)S(1)}) custom-call(s32[5]{0:T(128)S(1)} %stack.23.z_ref, bf16[256,4608]{1,0:T(8,128)(2,1)S(1)} %copy-done.4, bf16[8,3,32,1152]{3,2,1,0:T(8,128)(2,1)S(1)} %bitcast.13, bf16[384,256]{1,0:T(8,128)(2,1)S(1)} %attend.2.rest_0_, bf16[384,256]{1,0:T(8,128)(2,1)S(1)} %collective-permute-done.19.rest_1_, ...), custom_call_target="tpu_custom_call" | custom-call | tf_op jit(solution)/shard_map/output/pallas_call | solution.py:446
  194.2 3.2 %collective-permute-start.25 = (f32[1,384]{1,0:T(1,128)S(1)}, f32[1,384]{1,0:T(1,128)S(1)}, u32[]{:S(2)}, u32[]{:S(2)}) collective-permute-start(f32[1,384]{1,0:T(1,128)S(1)} %get-tuple-element.29.rest_0_), channel_id=1, source_target_pairs={{0,3},{1,0},{2,1},{3,2},{4,7},{5,4},{6,5},{7,6},{8,11},{9,8},{10,9... | collective-permute-start | bytes 4616 | tf_op jit(solution)/shard_map/ppermute | solution.py:602
  198.6 1.9 finish.2.rest_4_
  201.9 2.0 collective-permute-done.23.rest_1_
  203.9 1.9 finish.3
  (98 shorter events, 44.7 us)
Async XLA Ops:
  6.5 171.1 %all-gather.3.cloned.1.call-start = ((), (), s32[]{:S(2)}) async-start(), calls=%async_computation | async-start | bytes 1990656 | tf_op jit(solution)/shard_map/all_gather | solution.py:580
  8.4 14.2 %collective-permute-start.1 = (bf16[288,256]{1,0:T(8,128)(2,1)}, bf16[288,256]{1,0:T(8,128)(2,1)S(1)}, u32[]{:S(2)}, u32[]{:S(2)}) collective-permute-start(bf16[288,256]{1,0:T(8,128)(2,1)} %get-tuple-element.21), channel_id=1, source_target_pairs={{0,2},{1,3},{2,0},{3,1},{4,6},{5,7},{6,4},{7,5},{8,10},{9,11},{10,... | collective-permute-start | bytes 442376 | tf_op jit(solution)/shard_map/ppermute | solution.py:528
  11.0 13.6 %collective-permute-start.5 = (bf16[288,256]{1,0:T(8,128)(2,1)}, bf16[288,256]{1,0:T(8,128)(2,1)S(1)}, u32[]{:S(2)}, u32[]{:S(2)}) collective-permute-start(bf16[288,256]{1,0:T(8,128)(2,1)} %get-tuple-element.22), channel_id=1, source_target_pairs={{0,2},{1,3},{2,0},{3,1},{4,6},{5,7},{6,4},{7,5},{8,10},{9,11},{10,... | collective-permute-start | bytes 442376 | tf_op jit(solution)/shard_map/ppermute | solution.py:529
  22.6 5.4 %collective-permute-start.2 = (bf16[1,288,256]{2,1,0:T(8,128)(2,1)S(1)}, bf16[1,288,256]{2,1,0:T(8,128)(2,1)S(1)}, u32[]{:S(2)}, u32[]{:S(2)}) collective-permute-start(bf16[1,288,256]{2,1,0:T(8,128)(2,1)S(1)} %bitcast.16), channel_id=1, source_target_pairs={{0,8},{4,12},{8,0},{12,4},{16,24},{20,28},{24,16},{28,20},{1,9},{5... | collective-permute-start | bytes 442376 | tf_op jit(solution)/shard_map/ppermute | solution.py:115
  27.2 20.3 %collective-permute-start = (bf16[384,1152]{1,0:T(8,128)(2,1)S(1)}, bf16[384,1152]{1,0:T(8,128)(2,1)S(1)}, u32[]{:S(2)}, u32[]{:S(2)}) collective-permute-start(bf16[384,1152]{1,0:T(8,128)(2,1)S(1)} %get-tuple-element.37), channel_id=1, source_target_pairs={{0,1},{1,0},{2,3},{3,2},{4,5},{5,4},{6,7},{7,6},{8,9},{9,8},{10,11... | collective-permute-start | bytes 2654216 | tf_op jit(solution)/shard_map/ppermute | solution.py:542
  28.4 8.4 %collective-permute-start.3 = (bf16[2,288,256]{2,1,0:T(8,128)(2,1)S(1)}, bf16[2,288,256]{2,1,0:T(8,128)(2,1)S(1)}, u32[]{:S(2)}, u32[]{:S(2)}) collective-permute-start(bf16[2,288,256]{2,1,0:T(8,128)(2,1)S(1)} %join.4.first_ref), channel_id=1, source_target_pairs={{0,16},{4,20},{8,24},{12,28},{16,0},{20,4},{24,8},{28,12},{1,17},{... | collective-permute-start | bytes 884744 | tf_op jit(solution)/shard_map/ppermute | solution.py:115
  30.2 7.7 %collective-permute-start.7 = (bf16[2,288,256]{2,1,0:T(8,128)(2,1)S(1)}, bf16[2,288,256]{2,1,0:T(8,128)(2,1)S(1)}, u32[]{:S(2)}, u32[]{:S(2)}) collective-permute-start(bf16[2,288,256]{2,1,0:T(8,128)(2,1)S(1)} %join.6.first_ref), channel_id=1, source_target_pairs={{0,8},{4,12},{8,0},{12,4},{16,24},{20,28},{24,16},{28,20},{1,9},{5... | collective-permute-start | bytes 884744 | tf_op jit(solution)/shard_map/ppermute | solution.py:115
  37.8 13.8 %collective-permute-start.4 = (bf16[4,288,256]{2,1,0:T(8,128)(2,1)}, bf16[4,288,256]{2,1,0:T(8,128)(2,1)}, u32[]{:S(2)}, u32[]{:S(2)}) collective-permute-start(bf16[4,288,256]{2,1,0:T(8,128)(2,1)} %join.5.rest_0_), channel_id=1, source_target_pairs={{0,4},{4,0},{8,12},{12,8},{16,20},{20,16},{24,28},{28,24},{1,5},{5... | collective-permute-start | bytes 1769480 | tf_op jit(solution)/shard_map/ppermute | solution.py:115
  38.8 12.7 %collective-permute-start.8 = (bf16[4,288,256]{2,1,0:T(8,128)(2,1)}, bf16[4,288,256]{2,1,0:T(8,128)(2,1)}, u32[]{:S(2)}, u32[]{:S(2)}) collective-permute-start(bf16[4,288,256]{2,1,0:T(8,128)(2,1)} %join.7.rest_2_), channel_id=1, source_target_pairs={{0,4},{4,0},{8,12},{12,8},{16,20},{20,16},{24,28},{28,24},{1,5},{5... | collective-permute-start | bytes 1769480 | tf_op jit(solution)/shard_map/ppermute | solution.py:115
  58.6 7.6 %collective-permute-start.9 = (bf16[32,1152]{1,0:T(8,128)(2,1)S(1)}, bf16[32,1152]{1,0:T(8,128)(2,1)S(1)}, u32[]{:S(2)}, u32[]{:S(2)}) collective-permute-start(bf16[32,1152]{1,0:T(8,128)(2,1)S(1)} %get-tuple-element.33), channel_id=1, source_target_pairs={{0,1},{1,2},{2,3},{3,0},{4,5},{5,6},{6,7},{7,4},{8,9},{9,10},{10,1... | collective-permute-start | bytes 221192 | tf_op jit(solution)/shard_map/ppermute | solution.py:579
  60.4 5.9 %collective-permute-start.11 = (bf16[32,1152]{1,0:T(8,128)(2,1)S(1)}, bf16[32,1152]{1,0:T(8,128)(2,1)S(1)}, u32[]{:S(2)}, u32[]{:S(2)}) collective-permute-start(bf16[32,1152]{1,0:T(8,128)(2,1)S(1)} %get-tuple-element.34), channel_id=1, source_target_pairs={{0,3},{1,0},{2,1},{3,2},{4,7},{5,4},{6,5},{7,6},{8,11},{9,8},{10,9... | collective-permute-start | bytes 221192 | tf_op jit(solution)/shard_map/ppermute | solution.py:579
  63.2 6.5 %collective-permute-start.10 = (bf16[32,1152]{1,0:T(8,128)(2,1)S(1)}, bf16[32,1152]{1,0:T(8,128)(2,1)S(1)}, u32[]{:S(2)}, u32[]{:S(2)}) collective-permute-start(bf16[32,1152]{1,0:T(8,128)(2,1)S(1)} %get-tuple-element.35), channel_id=1, source_target_pairs={{0,2},{1,3},{2,0},{3,1},{4,6},{5,7},{6,4},{7,5},{8,10},{9,11},{10,... | collective-permute-start | bytes 221192 | tf_op jit(solution)/shard_map/ppermute | solution.py:579
  70.4 20.8 %collective-permute-start.13 = (bf16[384,1152]{1,0:T(8,128)(2,1)}, bf16[384,1152]{1,0:T(8,128)(2,1)}, u32[]{:S(2)}, u32[]{:S(2)}) collective-permute-start(bf16[384,1152]{1,0:T(8,128)(2,1)} %get-tuple-element.36), channel_id=1, source_target_pairs={{0,1},{1,0},{2,3},{3,2},{4,5},{5,4},{6,7},{7,6},{8,9},{9,8},{10,11... | collective-permute-start | bytes 2654216 | tf_op jit(solution)/shard_map/ppermute | solution.py:542
  94.3 40.1 %collective-permute-start.12 = (bf16[400,512]{1,0:T(8,128)(2,1)S(1)}, bf16[400,512]{1,0:T(8,128)(2,1)S(1)}, u32[]{:S(2)}, u32[]{:S(2)}) collective-permute-start(bf16[400,512]{1,0:T(8,128)(2,1)S(1)} %copy-done.7), channel_id=1, source_target_pairs={{0,2},{1,3},{2,0},{3,1},{4,6},{5,7},{6,4},{7,5},{8,10},{9,11},{10,... | collective-permute-start | bytes 1228808 | tf_op jit(solution)/shard_map/ppermute | solution.py:558
  99.8 31.1 %collective-permute-start.14 = (bf16[400,512]{1,0:T(8,128)(2,1)S(1)}, bf16[400,512]{1,0:T(8,128)(2,1)S(1)}, u32[]{:S(2)}, u32[]{:S(2)}) collective-permute-start(bf16[400,512]{1,0:T(8,128)(2,1)S(1)} %far.3), channel_id=1, source_target_pairs={{0,2},{1,3},{2,0},{3,1},{4,6},{5,7},{6,4},{7,5},{8,10},{9,11},{10,... | collective-permute-start | bytes 1228808 | tf_op jit(solution)/shard_map/ppermute | solution.py:558
  131.2 7.1 %collective-permute-start.17 = (bf16[400,256]{1,0:T(8,128)(2,1)S(1)}, bf16[400,256]{1,0:T(8,128)(2,1)S(1)}, u32[]{:S(2)}, u32[]{:S(2)}) collective-permute-start(bf16[400,256]{1,0:T(8,128)(2,1)S(1)} %get-tuple-element.26.rest_4_), channel_id=1, source_target_pairs={{0,4},{4,8},{8,12},{1,5},{5,9},{9,13},{2,6},{6,10},{10,14},{3,7},{... | collective-permute-start | bytes 614408 | tf_op jit(solution)/shard_map/ppermute | solution.py:568
  133.1 9.9 %collective-permute-start.15 = (bf16[400,256]{1,0:T(8,128)(2,1)S(1)}, bf16[400,256]{1,0:T(8,128)(2,1)S(1)}, u32[]{:S(2)}, u32[]{:S(2)}) collective-permute-start(bf16[400,256]{1,0:T(8,128)(2,1)S(1)} %get-tuple-element.26.rest_4_), channel_id=1, source_target_pairs={{0,8},{4,12},{1,9},{5,13},{2,10},{6,14},{3,11},{7,15},{16,24},{20,... | collective-permute-start | bytes 614408 | tf_op jit(solution)/shard_map/ppermute | solution.py:568
  134.7 12.0 %collective-permute-start.18 = (bf16[400,256]{1,0:T(8,128)(2,1)S(1)}, bf16[400,256]{1,0:T(8,128)(2,1)S(1)}, u32[]{:S(2)}, u32[]{:S(2)}) collective-permute-start(bf16[400,256]{1,0:T(8,128)(2,1)S(1)} %get-tuple-element.27.rest_5_), channel_id=1, source_target_pairs={{0,4},{4,8},{8,12},{1,5},{5,9},{9,13},{2,6},{6,10},{10,14},{3,7},{... | collective-permute-start | bytes 614408 | tf_op jit(solution)/shard_map/ppermute | solution.py:568
  136.6 10.8 %collective-permute-start.16 = (bf16[400,256]{1,0:T(8,128)(2,1)S(1)}, bf16[400,256]{1,0:T(8,128)(2,1)S(1)}, u32[]{:S(2)}, u32[]{:S(2)}) collective-permute-start(bf16[400,256]{1,0:T(8,128)(2,1)S(1)} %get-tuple-element.27.rest_5_), channel_id=1, source_target_pairs={{0,8},{4,12},{1,9},{5,13},{2,10},{6,14},{3,11},{7,15},{16,24},{20,... | collective-permute-start | bytes 614408 | tf_op jit(solution)/shard_map/ppermute | solution.py:568
  151.9 13.6 %collective-permute-start.26 = (bf16[384,256]{1,0:T(8,128)(2,1)S(1)}, bf16[384,256]{1,0:T(8,128)(2,1)S(1)}, u32[]{:S(2)}, u32[]{:S(2)}) collective-permute-start(bf16[384,256]{1,0:T(8,128)(2,1)S(1)} %attend.3.rest_0_), channel_id=1, source_target_pairs={{0,2},{1,3},{2,0},{3,1},{4,6},{5,7},{6,4},{7,5},{8,10},{9,11},{10,... | collective-permute-start | bytes 589832 | tf_op jit(solution)/shard_map/ppermute | solution.py:592
  156.5 16.2 %collective-permute-start.19 = (bf16[384,256]{1,0:T(8,128)(2,1)S(1)}, bf16[384,256]{1,0:T(8,128)(2,1)S(1)}, u32[]{:S(2)}, u32[]{:S(2)}) collective-permute-start(bf16[384,256]{1,0:T(8,128)(2,1)S(1)} %attend.2.rest_0_), channel_id=1, source_target_pairs={{0,2},{1,3},{2,0},{3,1},{4,6},{5,7},{6,4},{7,5},{8,10},{9,11},{10,... | collective-permute-start | bytes 589832 | tf_op jit(solution)/shard_map/ppermute | solution.py:592
  159.4 14.6 %collective-permute-start.28 = (bf16[384,256]{1,0:T(8,128)(2,1)S(1)}, bf16[384,256]{1,0:T(8,128)(2,1)S(1)}, u32[]{:S(2)}, u32[]{:S(2)}) collective-permute-start(bf16[384,256]{1,0:T(8,128)(2,1)S(1)} %attend.3.rest_0_), channel_id=1, source_target_pairs={{1,0},{2,1},{3,2},{5,4},{6,5},{7,6},{9,8},{10,9},{11,10},{13,12},{... | collective-permute-start | bytes 589832 | tf_op jit(solution)/shard_map/ppermute | solution.py:594
  160.7 14.7 %collective-permute-start.27 = (bf16[384,256]{1,0:T(8,128)(2,1)S(1)}, bf16[384,256]{1,0:T(8,128)(2,1)S(1)}, u32[]{:S(2)}, u32[]{:S(2)}) collective-permute-start(bf16[384,256]{1,0:T(8,128)(2,1)S(1)} %attend.3.rest_0_), channel_id=1, source_target_pairs={{0,1},{1,2},{2,3},{4,5},{5,6},{6,7},{8,9},{9,10},{10,11},{12,13},{... | collective-permute-start | bytes 589832 | tf_op jit(solution)/shard_map/ppermute | solution.py:593
  165.5 12.1 %collective-permute-start.29 = (bf16[384,256]{1,0:T(8,128)(2,1)S(1)}, bf16[384,256]{1,0:T(8,128)(2,1)}, u32[]{:S(2)}, u32[]{:S(2)}) collective-permute-start(bf16[384,256]{1,0:T(8,128)(2,1)S(1)} %collective-permute-done.26.rest_1_), channel_id=1, source_target_pairs={{2,3},{1,0},{6,7},{5,4},{10,11},{9,8},{14,15},{13,12},{18,19},{17,... | collective-permute-start | bytes 589832 | tf_op jit(solution)/shard_map/ppermute | solution.py:595
  166.8 23.3 %collective-permute-start.21 = (bf16[384,256]{1,0:T(8,128)(2,1)S(1)}, bf16[384,256]{1,0:T(8,128)(2,1)S(1)}, u32[]{:S(2)}, u32[]{:S(2)}) collective-permute-start(bf16[384,256]{1,0:T(8,128)(2,1)S(1)} %attend.2.rest_0_), channel_id=1, source_target_pairs={{1,0},{2,1},{3,2},{5,4},{6,5},{7,6},{9,8},{10,9},{11,10},{13,12},{... | collective-permute-start | bytes 589832 | tf_op jit(solution)/shard_map/ppermute | solution.py:594
  172.7 18.1 %collective-permute-start.20 = (bf16[384,256]{1,0:T(8,128)(2,1)S(1)}, bf16[384,256]{1,0:T(8,128)(2,1)S(1)}, u32[]{:S(2)}, u32[]{:S(2)}) collective-permute-start(bf16[384,256]{1,0:T(8,128)(2,1)S(1)} %attend.2.rest_0_), channel_id=1, source_target_pairs={{0,1},{1,2},{2,3},{4,5},{5,6},{6,7},{8,9},{9,10},{10,11},{12,13},{... | collective-permute-start | bytes 589832 | tf_op jit(solution)/shard_map/ppermute | solution.py:593
  174.0 16.8 %collective-permute-start.22 = (bf16[384,256]{1,0:T(8,128)(2,1)S(1)}, bf16[384,256]{1,0:T(8,128)(2,1)S(1)}, u32[]{:S(2)}, u32[]{:S(2)}) collective-permute-start(bf16[384,256]{1,0:T(8,128)(2,1)S(1)} %collective-permute-done.19.rest_1_), channel_id=1, source_target_pairs={{2,3},{1,0},{6,7},{5,4},{10,11},{9,8},{14,15},{13,12},{18,19},{17,... | collective-permute-start | bytes 589832 | tf_op jit(solution)/shard_map/ppermute | solution.py:595
  185.0 13.5 %collective-permute-start.32 = (f32[1,384]{1,0:T(1,128)S(1)}, f32[1,384]{1,0:T(1,128)S(1)}, u32[]{:S(2)}, u32[]{:S(2)}) collective-permute-start(f32[1,384]{1,0:T(1,128)S(1)} %get-tuple-element.32.rest_0_), channel_id=1, source_target_pairs={{0,3},{1,0},{2,1},{3,2},{4,7},{5,4},{6,5},{7,6},{8,11},{9,8},{10,9... | collective-permute-start | bytes 4616 | tf_op jit(solution)/shard_map/ppermute | solution.py:602
  190.1 8.5 %collective-permute-start.31 = (f32[1,384]{1,0:T(1,128)S(1)}, f32[1,384]{1,0:T(1,128)S(1)}, u32[]{:S(2)}, u32[]{:S(2)}) collective-permute-start(f32[1,384]{1,0:T(1,128)S(1)} %get-tuple-element.32.rest_0_), channel_id=1, source_target_pairs={{0,2},{1,3},{2,0},{3,1},{4,6},{5,7},{6,4},{7,5},{8,10},{9,11},{10,... | collective-permute-start | bytes 4616 | tf_op jit(solution)/shard_map/ppermute | solution.py:602
  190.1 8.5 %collective-permute-start.30 = (f32[1,384]{1,0:T(1,128)S(1)}, f32[1,384]{1,0:T(1,128)S(1)}, u32[]{:S(2)}, u32[]{:S(2)}) collective-permute-start(f32[1,384]{1,0:T(1,128)S(1)} %get-tuple-element.32.rest_0_), channel_id=1, source_target_pairs={{0,1},{1,2},{2,3},{3,0},{4,5},{5,6},{6,7},{7,4},{8,9},{9,10},{10,1... | collective-permute-start | bytes 4616 | tf_op jit(solution)/shard_map/ppermute | solution.py:602
  194.2 6.3 %collective-permute-start.25 = (f32[1,384]{1,0:T(1,128)S(1)}, f32[1,384]{1,0:T(1,128)S(1)}, u32[]{:S(2)}, u32[]{:S(2)}) collective-permute-start(f32[1,384]{1,0:T(1,128)S(1)} %get-tuple-element.29.rest_0_), channel_id=1, source_target_pairs={{0,3},{1,0},{2,1},{3,2},{4,7},{5,4},{6,5},{7,6},{8,11},{9,8},{10,9... | collective-permute-start | bytes 4616 | tf_op jit(solution)/shard_map/ppermute | solution.py:602
  198.5 5.4 %collective-permute-start.23 = (f32[1,384]{1,0:T(1,128)S(1)}, f32[1,384]{1,0:T(1,128)S(1)}, u32[]{:S(2)}, u32[]{:S(2)}) collective-permute-start(f32[1,384]{1,0:T(1,128)S(1)} %get-tuple-element.29.rest_0_), channel_id=1, source_target_pairs={{0,1},{1,2},{2,3},{3,0},{4,5},{5,6},{6,7},{7,4},{8,9},{9,10},{10,1... | collective-permute-start | bytes 4616 | tf_op jit(solution)/shard_map/ppermute | solution.py:602
  (16 other events, 95.9 us)
Sparse Core Ops, SparseCore 0:
  70.5 25.4 all-gather.2

commit v5 on v4

--- a/solution.py
+++ b/solution.py
@@ -121,62 +121,59 @@
 
 def prep_kernel(src_ref, gain_ref, *rest):
     x_refs, (out_ref, sq_ref) = rest[:-2], rest[-2:]
-    total = 0.0
     for k, x_ref in enumerate(x_refs):
         x = x_ref[...].astype(F32)
-        total = total + jnp.sum(x * x, axis=1, keepdims=True)
+        squares = jnp.sum(x * x, axis=1, keepdims=True)
+        total = squares if k == 0 else total + squares
         out_ref[k] = (x * gain_ref[src_ref[k]]).astype(BF16)
     sq_ref[...] = to_row(total)
 
 
-def prep(sources, gains, tokens, received, chunk, c):
-    count, (nz, _, cols) = len(received) + 1, gains.shape
+def prep(sources, gains, blocks):
+    rows, cols = blocks[0].shape
+    dims = (len(blocks), rows, cols)
     return pl.pallas_call(
         prep_kernel,
-        out_shape=(shape((count, chunk, cols), BF16), shape((1, chunk), F32)),
+        out_shape=(shape(dims, BF16), shape((1, rows), F32)),
         grid_spec=pltpu.PrefetchScalarGridSpec(
             num_scalar_prefetch=1,
             grid=(1,),
-            in_specs=[
-                pl.BlockSpec((nz, 1, cols), lambda i, s: (0, 0, 0)),
-                pl.BlockSpec((chunk, cols), lambda i, s: (c, 0)),
-            ]
-            + [pl.BlockSpec((chunk, cols), lambda i, s: (0, 0)) for _ in received],
+            in_specs=[pl.BlockSpec(gains.shape, lambda i, s: (0, 0, 0))]
+            + [pl.BlockSpec((rows, cols), lambda i, s: (0, 0)) for _ in blocks],
             out_specs=[
-                pl.BlockSpec((count, chunk, cols), lambda i, s: (0, 0, 0)),
-                pl.BlockSpec((1, chunk), lambda i, s: (0, 0)),
+                pl.BlockSpec(dims, lambda i, s: (0, 0, 0)),
+                pl.BlockSpec((1, rows), lambda i, s: (0, 0)),
             ],
         ),
         compiler_params=PARAMS,
         name="prep",
-    )(sources, gains, tokens, *received)
-
-
-def far_kernel(place_ref, src_ref, x_ref, sq_ref, *rest, orders):
-    pieces, (out_ref, weight, sems) = rest[:-3], rest[-3:]
-    copies, column = [], 0
-    for order, own_ref, got_ref in zip(orders, pieces[::2], pieces[1::2]):
-        held, share, width = own_ref.shape
-        for i, mask in enumerate(order):
-            piece = own_ref.at[i] if i < held else got_ref.at[i - held]
-            row = pl.multiple_of((place_ref[0] ^ mask) * share, TAIL)
-            there = weight.at[pl.ds(row, share), pl.ds(column, width)]
-            copies.append(pltpu.make_async_copy(piece, there, sems.at[len(copies)]))
-        column += width
+    )(sources, gains, *blocks)
+
+
+def far_kernel(place_ref, src_ref, x_ref, sq_ref, own_ref, got_ref, *rest, order, with_sq):
+    out_ref, weight, sems = rest[-3:]
+    held, share, width = own_ref.shape
+    copies = []
+    for i, mask in enumerate(order):
+        piece = own_ref.at[i] if i < held else got_ref.at[i - held]
+        row = pl.multiple_of((place_ref[0] ^ mask) * share, TAIL)
+        there = weight.at[pl.ds(row, share)]
+        copies.append(pltpu.make_async_copy(piece, there, sems.at[i]))
     for copy in copies:
         copy.start()
     for copy in copies:
         copy.wait()
-    count, chunk, cols = x_ref.shape
+    count, rows, cols = x_ref.shape
     total = None
     for k in range(count):
         row = pl.multiple_of(src_ref[k] * cols, TAIL)
         term = jnp.dot(x_ref[k], weight[pl.ds(row, cols), :], preferred_element_type=F32)
         total = term if total is None else total + term
-    out_ref[:chunk, :] = total.astype(BF16)
-    sq = sq_ref[...]
-    high = sq.astype(BF16).astype(F32)
-    out_ref[chunk:, :] = lines_of((high, sq - high), out_ref.shape[1])
+    out_ref[:rows, :] = total.astype(BF16)
+    if with_sq:
+        sq = sq_ref[...]
+        high = sq.astype(BF16).astype(F32)
+        out_ref[rows:, :] = lines_of((high, sq - high), width)
 
 
 def lines_of(rows, width):
@@ -201,32 +198,33 @@
     return rows
 
 
-def far_product(place, sources, x, gathered, sq):
-    orders = [g[0] for g in gathered]
-    pieces = [piece for g in gathered for piece in g[1:]]
-    width = sum(g[1].shape[2] for g in gathered)
-    share = pieces[0].shape[1]
-    count, chunk, cols = x.shape
-    return pl.pallas_call(
-        partial(far_kernel, orders=orders),
-        out_shape=shape((chunk + TAIL, width), BF16),
+def far_product(place, sources, x, sq, gathered, with_sq, after):
+    order, own, got = gathered
+    _, share, width = own.shape
+    rows = x.shape[1]
+    out_rows = rows + (TAIL if with_sq else 0)
+    return pl.pallas_call(
+        partial(far_kernel, order=order, with_sq=with_sq),
+        out_shape=shape((out_rows, width), BF16),
         grid_spec=pltpu.PrefetchScalarGridSpec(
             num_scalar_prefetch=2,
             grid=(1,),
             in_specs=[
-                pl.BlockSpec((count, chunk, cols), lambda i, p, s: (0, 0, 0)),
-                pl.BlockSpec((1, chunk), lambda i, p, s: (0, 0)),
+                pl.BlockSpec(x.shape, lambda i, p, s: (0, 0, 0)),
+                pl.BlockSpec((1, rows), lambda i, p, s: (0, 0)),
+                ANY,
+                ANY,
             ]
-            + [ANY for _ in pieces],
-            out_specs=pl.BlockSpec((chunk + TAIL, width), lambda i, p, s: (0, 0)),
+            + [ANY for _ in after],
+            out_specs=pl.BlockSpec((out_rows, width), lambda i, p, s: (0, 0)),
             scratch_shapes=[
-                pltpu.VMEM((len(orders[0]) * share, width), BF16),
-                pltpu.SemaphoreType.DMA((sum(len(o) for o in orders),)),
+                pltpu.VMEM((len(order) * share, width), BF16),
+                pltpu.SemaphoreType.DMA((len(order),)),
             ],
         ),
         compiler_params=PARAMS,
         name="far",
-    )(place, sources, x, sq, *pieces)
+    )(place, sources, x, sq, own, got, *after)
 
 
 def near_kernel(src_ref, x_ref, k_ref, v_ref, q_ref, after_ref, out_ref):
@@ -243,7 +241,7 @@
         column += ref.shape[1]
 
 
-def near_product(blocks, x, weights, after):
+def near_product(sources, x, weights, after):
     count, chunk, cols = x.shape
     widths = [w.shape[1] for w in weights]
     return pl.pallas_call(
@@ -259,10 +257,12 @@
         ),
         compiler_params=PARAMS,
         name="near",
-    )(blocks, x, *weights, after)
-
-
-def keys_kernel(near_ref, far_ref, sq_ref, id_ref, cos_ref, sin_ref, out_ref, sum_ref, *, model):
+    )(sources, x, *weights, after)
+
+
+def keys_kernel(
+    near_ref, far_ref, sq_ref, id_ref, cos_ref, sin_ref, out_ref, sum_ref, *, model
+):
     chunk, width = near_ref.shape
     tail = far_ref[chunk:, :].astype(F32)
     total = sum(rows_of(tail, 2, chunk), sq_ref[...])
@@ -277,7 +277,7 @@
     out_ref[chunk:, :] = lines_of((id_ref[...].astype(F32),), width)
 
 
-def keys_values(near, far, sq, ids, cosine, sine, c, width, model):
+def keys_values(near, far, sq, ids, cosine, sine, width, model):
     chunk = near.shape[0]
     whole = lambda i: (0, 0)
     return pl.pallas_call(
@@ -288,9 +288,9 @@
             pl.BlockSpec((chunk, width), whole),
             pl.BlockSpec(far.shape, whole),
             pl.BlockSpec((1, chunk), whole),
-            pl.BlockSpec((1, chunk), lambda i: (0, c)),
-            pl.BlockSpec((chunk, HEAD_SIZE), lambda i: (c, 0)),
-            pl.BlockSpec((chunk, HEAD_SIZE), lambda i: (c, 0)),
+            pl.BlockSpec((1, chunk), whole),
+            pl.BlockSpec((chunk, HEAD_SIZE), whole),
+            pl.BlockSpec((chunk, HEAD_SIZE), whole),
         ],
         out_specs=[pl.BlockSpec((chunk + TAIL, width), whole), pl.BlockSpec((1, chunk), whole)],
         compiler_params=PARAMS,
@@ -299,7 +299,7 @@
 
 
 def attention_kernel(
-    seq_ref, near_ref, far_ref, sum_ref, cos_ref, sin_ref, id_ref, *rest, back, offset, model
+    seq_ref, near_ref, far_ref, sum_ref, cos_ref, sin_ref, id_ref, after_ref, *rest, back, offset, model
 ):
     kv_refs, (out_ref, k_scr, vt_scr, id_scr) = rest[:-4], rest[-4:]
     part_rows = kv_refs[0].shape[0] - TAIL
@@ -313,7 +313,7 @@
             k_scr[at, :] = kv_ref[:part_rows, :HEAD_SIZE]
             vt_scr[:, at] = kv_ref[:part_rows, HEAD_SIZE:].astype(F32).T.astype(BF16)
             (ids,) = rows_of(kv_ref[part_rows:, :].astype(F32), 1, part_rows)
-            exists = b // CHUNKS >= back - seq_ref[0]
+            exists = b >= back - seq_ref[0]
             id_scr[at, :] = to_column(jnp.where(exists, ids, -1.0))
 
     scale = query_scale * math.log2(math.e)
@@ -330,7 +330,7 @@
     start = jnp.sum(before, axis=0, keepdims=True).astype(jnp.int32)
     low = jnp.min(start) // K_TILE
     start = jnp.concatenate([start] * group, axis=1)
-    first = back * part_rows * CHUNKS + offset + tile * Q_TILE
+    first = back * part_rows + offset + tile * Q_TILE
     place = first + lax.broadcasted_iota(jnp.int32, (1, Q_TILE), 1)
     place = jnp.concatenate([place] * group, axis=1)
 
@@ -375,10 +375,11 @@
         ].astype(BF16)
 
 
-def attend(seq, near, far, sums, cosine, sine, ids, blocks, c, width, model):
-    rows = near.shape[0]
+def attend(seq, near, far, sums, cosine, sine, ids, after, blocks, c, model):
+    rows = near.shape[0] // CHUNKS
+    width = far.shape[1]
     part_rows = blocks[0].shape[0] - TAIL
-    back = len(blocks) // CHUNKS - 1
+    back = len(blocks) - 1
     tiles = rows // Q_TILE
     keys = len(blocks) * part_rows
     last = near.shape[1] // width - 1
@@ -389,12 +390,13 @@
             num_scalar_prefetch=1,
             grid=(tiles,),
             in_specs=[
-                pl.BlockSpec((Q_TILE, width), lambda i, s: (i, last)),
-                pl.BlockSpec((Q_TILE, width), lambda i, s: (i, last)),
-                pl.BlockSpec((1, Q_TILE), lambda i, s: (0, i)),
+                pl.BlockSpec((Q_TILE, width), lambda i, s: (c * tiles + i, last)),
+                pl.BlockSpec((Q_TILE, width), lambda i, s: (c * tiles + i, 0)),
+                pl.BlockSpec((1, Q_TILE), lambda i, s: (0, c * tiles + i)),
                 pl.BlockSpec((Q_TILE, HEAD_SIZE), lambda i, s: (c * tiles + i, 0)),
                 pl.BlockSpec((Q_TILE, HEAD_SIZE), lambda i, s: (c * tiles + i, 0)),
                 pl.BlockSpec((1, Q_TILE), lambda i, s: (0, c * tiles + i)),
+                ANY,
             ]
             + [pl.BlockSpec(b.shape, lambda i, s: (0, 0)) for b in blocks],
             out_specs=pl.BlockSpec((Q_TILE, width), lambda i, s: (i, 0)),
@@ -405,17 +407,22 @@
             ],
         ),
         compiler_params=PARAMS,
+        cost_estimate=pl.CostEstimate(
+            flops=4 * rows * width * keys,
+            bytes_accessed=4 * keys * width,
+            transcendentals=rows * keys * width // HEAD_SIZE,
+        ),
         name="attend",
-    )(seq, near, far, sums, cosine, sine, ids, *blocks)
-
-
-def output_kernel(z_ref, own_o_ref, o_ref, *rest):
-    ctx_refs, (out_ref, sq_ref, acc) = rest[:-3], rest[-3:]
+    )(seq, near, far, sums, cosine, sine, ids, after, *blocks)
+
+
+def output_kernel(at_ref, own_o_ref, o_ref, *rest):
+    ctx_refs, (after_ref, out_ref, sq_ref, acc) = rest[:-4], rest[-4:]
     step = pl.program_id(0)
     plane, _, share, tile = o_ref.shape
     total = jnp.dot(ctx_refs[0][...], own_o_ref[...], preferred_element_type=F32)
     for i, ctx_ref in enumerate(ctx_refs[1:]):
-        weight = o_ref[:, z_ref[1 + i]].reshape(plane * share, tile)
+        weight = o_ref[:, at_ref[1 + i]].reshape(plane * share, tile)
         total = total + jnp.dot(ctx_ref[...], weight, preferred_element_type=F32)
     out_ref[...] = total
     squares = jnp.sum(total * total, axis=1, keepdims=True)
@@ -434,15 +441,14 @@
         sq_ref[...] = acc[...].T[0:1, :]
 
 
-def output_product(z, o_weight, gathered, contexts):
+def output_product(column, order, o_weight, gathered, contexts, after):
     chunk, width = contexts[0].shape
     plane, others, share, cols = gathered.shape
     tiles = 3 if cols % (3 * LANES) == 0 else 1
     tile = cols // tiles
-    whole = lambda i, z: (0, 0)
     if cols % LANES:
-        o_weight = lax.dynamic_slice_in_dim(o_weight, z[0] * cols, cols, axis=1)
-        z = z.at[0].set(0)
+        o_weight = lax.dynamic_slice_in_dim(o_weight, column * cols, cols, axis=1)
+        column = jnp.int32(0)
     return pl.pallas_call(
         output_kernel,
         out_shape=(shape((chunk, cols), F32), shape((1, chunk), F32)),
@@ -450,19 +456,20 @@
             num_scalar_prefetch=1,
             grid=(tiles,),
             in_specs=[
-                pl.BlockSpec((width, tile), lambda i, z: (0, z[0] * tiles + i)),
-                pl.BlockSpec((plane, others, share, tile), lambda i, z: (0, 0, 0, i)),
+                pl.BlockSpec((width, tile), lambda i, at: (0, at[0] * tiles + i)),
+                pl.BlockSpec((plane, others, share, tile), lambda i, at: (0, 0, 0, i)),
             ]
-            + [pl.BlockSpec((chunk, width), whole) for _ in contexts],
+            + [pl.BlockSpec((chunk, width), lambda i, at: (0, 0)) for _ in contexts]
+            + [ANY],
             out_specs=[
-                pl.BlockSpec((chunk, tile), lambda i, z: (0, i)),
-                pl.BlockSpec((1, chunk), whole),
+                pl.BlockSpec((chunk, tile), lambda i, at: (0, i)),
+                pl.BlockSpec((1, chunk), lambda i, at: (0, 0)),
             ],
             scratch_shapes=[pltpu.VMEM((chunk, LANES), F32)],
         ),
         compiler_params=PARAMS,
         name="output",
-    )(z, o_weight, gathered, *contexts)
+    )(jnp.stack([column] + order), o_weight, gathered, *contexts, after)
 
 
 def final_kernel(token_ref, branch_ref, gain_ref, *rest, model, others):
@@ -530,46 +537,34 @@
     far_kv = spread(far_kv, plane, seq_bits + group_bits + [1])
     far_q = spread(far_q, plane, group_bits + seq_bits + [1])
 
-    chunk = rows // CHUNKS
     sources = (within + half - jnp.arange(half, dtype=jnp.int32)) % half
-    blocks_of = side * half + sources
+    blocks = [tokens]
+    for _ in range(half - 1):
+        blocks.append(lax.ppermute(blocks[-1], "tensor", ring))
     gains = in_gain.reshape(nz, 1, cols)
-    received = []
-    for c in range(CHUNKS):
-        blocks = []
-        held = tokens[c * chunk : (c + 1) * chunk]
-        for _ in range(half - 1):
-            held = lax.ppermute(held, "tensor", ring)
-            blocks.append(held)
-        received.append(blocks)
-
+    x, sq = prep(side * half + sources, gains, blocks)
+
+    place = jnp.reshape(in_plane, (1,))
+    sent_kv = far_product(place, sources, x, sq, far_kv, True, [])
+    got_kv = lax.ppermute(sent_kv, "tensor", swap)
+    weights = (k_weight, value_weight, q_weight)
+    near = near_product(side * half + sources, x, weights, sent_kv)
+
+    sent_q = far_product(place, sources, x, sq, far_q, False, [near])
+    got_q = lax.ppermute(sent_q, "tensor", swap)
     cosine, sine = rotation_table(seq * rows + jnp.arange(rows, dtype=jnp.int32))
     ids = seg_ids[None, :]
-    weights = (k_weight, value_weight, q_weight)
     kv_width = k_weight.shape[1] + value_weight.shape[1]
-    place = jnp.reshape(in_plane, (1,))
-    prepared, sent = [], []
-    for c in range(CHUNKS):
-        prepared.append(prep(blocks_of, gains, tokens, received[c], chunk, c))
-        sent.append(far_product(place, sources, prepared[c][0], [far_kv, far_q], prepared[c][1]))
-    kv_parts, q_parts = [], []
-    for c in range(CHUNKS):
-        x, sq = prepared[c]
-        got = lax.ppermute(sent[c], "tensor", swap)
-        near = near_product(blocks_of, x, weights, sent[-1])
-        own_kv, sums = keys_values(near, got, sq, ids, cosine, sine, c, kv_width, model)
-        kv_parts.append(own_kv)
-        q_parts.append((near, got, sums))
+    own_kv, sums = keys_values(near, got_kv, sq, ids, cosine, sine, kv_width, model)
 
     back = -(-(nseq * rows // 2 - 1) // rows)
-    blocks = list(kv_parts)
+    kv_blocks = [own_kv]
     for k in range(1, back + 1):
         earlier = [(i, i + k) for i in range(nseq - k)]
-        blocks = [lax.ppermute(part, "seq", earlier) for part in kv_parts] + blocks
+        kv_blocks.insert(0, lax.ppermute(own_kv, "seq", earlier))
 
     o_share = o_weight.shape[0] // plane
-    last = sent[-1][0, 0]
-    wait = (last != last).astype(jnp.int32)
+    wait = (got_kv[0, 0] != got_kv[0, 0]).astype(jnp.int32)
     moved = []
     for k in range(1, nz):
         target = (z + k) % nz
@@ -580,27 +575,27 @@
     gathered_o = lax.all_gather(jnp.stack(moved), PLANE)
 
     out = None
-    order = list(range(nz - 1))
-    if nz == 4:
-        order = [1, 0, 2, jnp.where(z < half, 0, 2)]
-    z_at = jnp.stack([z] + [jnp.int32(k) for k in order])
     seq_at = jnp.reshape(seq, (1,))
-    q_width = q_weight.shape[1]
+    context, own_sq = place, place
     for c in range(CHUNKS):
-        context = attend(seq_at, *q_parts[c], cosine, sine, ids, blocks, c, q_width, model)
+        context = attend(
+            seq_at, near, got_q, sums, cosine, sine, ids, context, kv_blocks, c, model
+        )
         if nz == 4:
+            pairs = [(i, i ^ 1) for i in range(nz)]
             opposite = lax.ppermute(context, "tensor", swap)
-            right = lax.ppermute(context, "tensor", [(0, 1), (1, 2), (2, 3)])
-            left = lax.ppermute(context, "tensor", [(1, 0), (2, 1), (3, 2)])
-            far_end = lax.ppermute(opposite, "tensor", [(2, 3), (1, 0)])
-            contexts = [context, opposite, right, left, far_end]
+            beside = lax.ppermute(context, "tensor", pairs)
+            across = lax.ppermute(opposite, "tensor", pairs)
+            contexts = [context, opposite, beside, across]
+            order = [jnp.int32(1), 2 - 2 * (z % 2), 2 * (z % 2)]
         else:
             contexts = [context]
             contexts += [lax.ppermute(context, "tensor", turn(k)) for k in range(1, nz)]
-        branch, own_sq = output_product(z_at, o_weight, gathered_o, contexts)
-        sums = [own_sq]
-        sums += [lax.ppermute(own_sq, "tensor", turn(k)) for k in range(1, nz)]
-        out = finish(tokens, branch, out_gain[None, :], sums, out, c, model)
+            order = [jnp.int32(k) for k in range(nz - 1)]
+        branch, own_sq = output_product(z, order, o_weight, gathered_o, contexts, own_sq)
+        squares = [own_sq]
+        squares += [lax.ppermute(own_sq, "tensor", turn(k)) for k in range(1, nz)]
+        out = finish(tokens, branch, out_gain[None, :], squares, out, c, model)
     return out
 
 

time: 215 us -> 235 us (1.093)
  waiting for transfers between devices: 95.2 us -> 125 us
  starting transfers between devices: 47.2 us -> 35.3 us
    ppermute x1, waiting for transfers between devices: 11.2 us -> 36.9 us  [per_device(): far_kv = lax.ppermute(packed_kv, 'tensor', swap)]
    ppermute x20 -> x15, waiting for transfers between devices: 65.6 us -> 40.4 us  [the longest x1 18.9 us: per_device(): got_kv = lax.ppermute(sent_kv, 'tensor', swap)]
    ppermute x6, waiting for transfers between devices: 6.18 us -> 27.2 us  [spread(): got = lax.ppermute(own, PLANE, [(i, i ^ mask) for i in range(plane)])]
    ppermute x20 -> x15, starting transfers between devices: 31.6 us -> 20.2 us  [the longest x6 8.87 us: per_device(): squares += [lax.ppermute(own_sq, 'tensor', turn(k)) for k in range(1, nz)]]
    ppermute x1, waiting for transfers between devices: 1.85 us -> 6.96 us  [per_device(): far_q = lax.ppermute(packed_q, 'tensor', swap)]
    pallas_call x2, Pallas kernels: 8.98 us -> 12.9 us  [attend(): pl.pallas_call(partial(attention_kernel, back=back, offset=c * rows, mode...]
    ppermute x2, waiting for transfers between devices: 4.61 us -> 7.17 us  [per_device(): opposite = lax.ppermute(context, 'tensor', swap)]
    pallas_call x4 -> x3, Pallas kernels: 10.8 us -> 8.92 us  [the longest x2 7.23 us: far_product(): pl.pallas_call(partial(far_kernel, order=order, with_sq=with_sq), out_sha...]
  transfers between devices with their start and end apart: 34 -> 29, of which waited for: 17 -> 14; matrix products, arithmetic and copies ran while one was open for 2% -> 1% of each run, Pallas kernels for 16% -> 16%
where the time goes in v5:
time: 235 us; the launch traced here: 233 us
  waiting for transfers between devices  125 us (53%)
  Pallas kernels  43.5 us (19%)
  starting transfers between devices  35.3 us (15%)
  between operations  15.1 us (6%)
  local copies, waits for them, and re-layouts  11.4 us (5%)
  other arithmetic  2.55 us (1%)
    ppermute x1, waiting for transfers between devices, per_device(): far_kv = lax.ppermute(packed_kv, 'tensor', swap)  36.9 us
    ppermute x6, waiting for transfers between devices, spread(): got = lax.ppermute(own, PLANE, [(i, i ^ mask) for i in range(plane)])  27.2 us
    ppermute x1, waiting for transfers between devices, per_device(): got_kv = lax.ppermute(sent_kv, 'tensor', swap)  18.9 us
    ppermute x1, waiting for transfers between devices, per_device(): got_q = lax.ppermute(sent_q, 'tensor', swap)  15.1 us
    pallas_call x2, Pallas kernels, attend(): pl.pallas_call(partial(attention_kernel, back=back, offset=c * rows, mode...  12.9 us
    ppermute x6, starting transfers between devices, per_device(): squares += [lax.ppermute(own_sq, 'tensor', turn(k)) for k in range(1, nz)]  8.87 us
    unnamed x26, local copies, waits for them, and re-layouts  7.66 us
    pallas_call x2, Pallas kernels, far_product(): pl.pallas_call(partial(far_kernel, order=order, with_sq=with_sq), out_sha...  7.23 us
  transfers between devices with their start and end apart: 29, of which 14 were waited for; matrix products, arithmetic and copies ran while one was open for 1% of the time, Pallas kernels for 16%

profile of v5, /device:TPU:2, one launch (start us, length us, event | category | flops | bytes accessed | tf_op | source)
XLA Modules:
  0.0 233.0 jit_solution(1414392931781885350)
XLA Ops:
  9.9 2.7 %collective-permute-start.1 = (bf16[288,256]{1,0:T(8,128)(2,1)}, bf16[288,256]{1,0:T(8,128)(2,1)S(1)}, u32[]{:S(2)}, u32[]{:S(2)}) collective-permute-start(bf16[288,256]{1,0:T(8,128)(2,1)} %get-tuple-element.17), channel_id=1, source_target_pairs={{0,2},{1,3},{2,0},{3,1},{4,6},{5,7},{6,4},{7,5},{8,10},{9,11},{10,... | collective-permute-start | bytes 442376 | tf_op jit(solution)/shard_map/ppermute | solution.py:535
  12.5 36.9 %collective-permute-done.1 = bf16[288,256]{1,0:T(8,128)(2,1)S(1)} collective-permute-done((bf16[288,256]{1,0:T(8,128)(2,1)}, bf16[288,256]{1,0:T(8,128)(2,1)S(1)}, u32[]{:S(2)}, u32[]{:S(2)}) %collective-permute-start.1) | collective-permute-done | bytes 147488 | tf_op jit(solution)/shard_map/ppermute | solution.py:535
  50.0 4.6 %collective-permute-done.2.second_ref = bf16[1,288,256]{2,1,0:T(8,128)(2,1)S(1)} collective-permute-done((bf16[1,288,256]{2,1,0:T(8,128)(2,1)S(1)}, bf16[1,288,256]{2,1,0:T(8,128)(2,1)S(1)}, u32[]{:S(2)}, u32[]{:S(2)}) %collective-permute-start.2) | collective-permute-done | bytes 147488 | tf_op jit(solution)/shard_map/ppermute | solution.py:115
  56.6 5.2 %collective-permute-done.3.second_ref = bf16[2,288,256]{2,1,0:T(8,128)(2,1)S(1)} collective-permute-done((bf16[2,288,256]{2,1,0:T(8,128)(2,1)S(1)}, bf16[2,288,256]{2,1,0:T(8,128)(2,1)S(1)}, u32[]{:S(2)}, u32[]{:S(2)}) %collective-permute-start.3) | collective-permute-done | bytes 294944 | tf_op jit(solution)/shard_map/ppermute | solution.py:115
  70.1 3.9 %far.2.after_ref = bf16[784,256]{1,0:T(8,128)(2,1)} custom-call(s32[1]{0:T(128)} %bitcast.3.place_ref.after_ref.rest_4_, s32[2]{0:T(128)S(1)} %and_select_fusion.src_ref, bf16[2,768,1152]{2,1,0:T(8,128)(2,1)S(1)} %get-tuple-element.15.x_ref, f32[1,768]{1,0:T(1,128)S(1)} %get-tuple-element.16.sq_ref, bf16[4,288,256]{2,1,0:T(8,128)(2,1)} %join.5.own_ref, ...), custom_call_target="tpu_custom_call" | custom-call | tf_op jit(solution)/shard_map/far/pallas_call | solution.py:206
  74.0 3.3 %collective-permute-start.5 = (bf16[784,256]{1,0:T(8,128)(2,1)}, bf16[784,256]{1,0:T(8,128)(2,1)}, u32[]{:S(2)}, u32[]{:S(2)}) collective-permute-start(bf16[784,256]{1,0:T(8,128)(2,1)} %far.2.after_ref), channel_id=1, source_target_pairs={{0,2},{1,3},{2,0},{3,1},{4,6},{5,7},{6,4},{7,5},{8,10},{9,11},{10,... | collective-permute-start | bytes 1204232 | tf_op jit(solution)/shard_map/ppermute | solution.py:549
  77.3 18.9 %collective-permute-done.5.far_ref = bf16[784,256]{1,0:T(8,128)(2,1)} collective-permute-done((bf16[784,256]{1,0:T(8,128)(2,1)}, bf16[784,256]{1,0:T(8,128)(2,1)}, u32[]{:S(2)}, u32[]{:S(2)}) %collective-permute-start.5) | collective-permute-done | bytes 401440 | tf_op jit(solution)/shard_map/ppermute | solution.py:549
  100.0 2.5 %collective-permute-start.8 = (bf16[32,1152]{1,0:T(8,128)(2,1)S(1)}, bf16[32,1152]{1,0:T(8,128)(2,1)S(1)}, u32[]{:S(2)}, u32[]{:S(2)}) collective-permute-start(bf16[32,1152]{1,0:T(8,128)(2,1)S(1)} %get-tuple-element.26), channel_id=1, source_target_pairs={{0,3},{1,0},{2,1},{3,2},{4,7},{5,4},{6,5},{7,6},{8,11},{9,8},{10,9... | collective-permute-start | bytes 221192 | tf_op jit(solution)/shard_map/ppermute | solution.py:574
  103.1 2.1 collective-permute-done.8
  105.2 4.4 %collective-permute-done.7 = bf16[32,1152]{1,0:T(8,128)(2,1)S(1)} collective-permute-done((bf16[32,1152]{1,0:T(8,128)(2,1)S(1)}, bf16[32,1152]{1,0:T(8,128)(2,1)S(1)}, u32[]{:S(2)}, u32[]{:S(2)}) %collective-permute-start.7) | collective-permute-done | bytes 73760 | tf_op jit(solution)/shard_map/ppermute | solution.py:574
  110.3 1.9 collective-permute-start.9
  112.2 7.0 %collective-permute-done.9 = bf16[288,256]{1,0:T(8,128)(2,1)S(1)} collective-permute-done((bf16[288,256]{1,0:T(8,128)(2,1)}, bf16[288,256]{1,0:T(8,128)(2,1)S(1)}, u32[]{:S(2)}, u32[]{:S(2)}) %collective-permute-start.9) | collective-permute-done | bytes 147488 | tf_op jit(solution)/shard_map/ppermute | solution.py:536
  120.7 5.0 %collective-permute-done.10.second_ref = bf16[1,288,256]{2,1,0:T(8,128)(2,1)S(1)} collective-permute-done((bf16[1,288,256]{2,1,0:T(8,128)(2,1)S(1)}, bf16[1,288,256]{2,1,0:T(8,128)(2,1)S(1)}, u32[]{:S(2)}, u32[]{:S(2)}) %collective-permute-start.10) | collective-permute-done | bytes 147488 | tf_op jit(solution)/shard_map/ppermute | solution.py:115
  128.0 12.4 %collective-permute-done.11.second_ref = bf16[2,288,256]{2,1,0:T(8,128)(2,1)} collective-permute-done((bf16[2,288,256]{2,1,0:T(8,128)(2,1)}, bf16[2,288,256]{2,1,0:T(8,128)(2,1)}, u32[]{:S(2)}, u32[]{:S(2)}) %collective-permute-start.11) | collective-permute-done | bytes 294944 | tf_op jit(solution)/shard_map/ppermute | solution.py:115
  144.8 4.1 %near.1.rest_0_.near_ref = f32[768,512]{1,0:T(8,128)S(1)} custom-call(s32[2]{0:T(128)S(1)} %broadcast_add_fusion.src_ref, bf16[2,768,1152]{2,1,0:T(8,128)(2,1)S(1)} %get-tuple-element.15.x_ref, bf16[4608,128]{1,0:T(8,128)(2,1)S(1)} %copy-done.6, bf16[4608,128]{1,0:T(8,128)(2,1)S(1)} %copy-done.7, bf16[4608,256]{1,0:T(8,128)(2,1)S(1)} %copy-done.3, ...), custom_call_target="tpu_custom_call" | custom-call | tf_op jit(solution)/shard_map/near/pallas_call | solution.py:247
  151.5 2.6 %collective-permute-start.15 = (bf16[784,256]{1,0:T(8,128)(2,1)S(1)}, bf16[784,256]{1,0:T(8,128)(2,1)S(1)}, u32[]{:S(2)}, u32[]{:S(2)}) collective-permute-start(bf16[784,256]{1,0:T(8,128)(2,1)S(1)} %get-tuple-element.20.rest_2_), channel_id=1, source_target_pairs={{0,4},{4,8},{8,12},{1,5},{5,9},{9,13},{2,6},{6,10},{10,14},{3,7},{... | collective-permute-start | bytes 1204232 | tf_op jit(solution)/shard_map/ppermute | solution.py:564
  154.1 3.3 %far.3 = bf16[768,256]{1,0:T(8,128)(2,1)S(1)} custom-call(s32[1]{0:T(128)} %bitcast.3.place_ref.after_ref.rest_4_, s32[2]{0:T(128)S(1)} %and_select_fusion.src_ref, bf16[2,768,1152]{2,1,0:T(8,128)(2,1)S(1)} %get-tuple-element.15.x_ref, f32[1,768]{1,0:T(1,128)S(1)} %get-tuple-element.16.sq_ref, bf16[4,288,256]{2,1,0:T(8,128)(2,1)S(1)} %join.7.own_ref, ...), custom_call_target="tpu_custom_call" | custom-call | tf_op jit(solution)/shard_map/far/pallas_call | solution.py:206
  157.8 15.1 %collective-permute-done.13.far_ref = bf16[768,256]{1,0:T(8,128)(2,1)S(1)} collective-permute-done((bf16[768,256]{1,0:T(8,128)(2,1)S(1)}, bf16[768,256]{1,0:T(8,128)(2,1)S(1)}, u32[]{:S(2)}, u32[]{:S(2)}) %collective-permute-start.13) | collective-permute-done | bytes 393248 | tf_op jit(solution)/shard_map/ppermute | solution.py:554
  172.9 8.5 %attend.2.after_ref.rest_0_ = bf16[384,256]{1,0:T(8,128)(2,1)S(1)} custom-call(s32[1]{0:T(128)} %bitcast.11.seq_ref, f32[768,512]{1,0:T(8,128)S(1)} %near.1.rest_0_.near_ref, bf16[768,256]{1,0:T(8,128)(2,1)S(1)} %collective-permute-done.13.far_ref, f32[1,768]{1,0:T(1,128)S(1)} %get-tuple-element.19.sum_ref, f32[768,128]{1,0:T(8,128)S(1)} %get-tuple-element.31.cos_ref, ...), custom_call_target="tpu_custom_call" | custom-call | flops 905969664 | bytes 2359296 | tf_op jit(solution)/shard_map/attend/pallas_call | solution.py:386
  181.5 4.4 %attend.3.rest_0_ = bf16[384,256]{1,0:T(8,128)(2,1)S(1)} custom-call(s32[1]{0:T(128)} %bitcast.11.seq_ref, f32[768,512]{1,0:T(8,128)S(1)} %near.1.rest_0_.near_ref, bf16[768,256]{1,0:T(8,128)(2,1)S(1)} %collective-permute-done.13.far_ref, f32[1,768]{1,0:T(1,128)S(1)} %get-tuple-element.19.sum_ref, f32[768,128]{1,0:T(8,128)S(1)} %get-tuple-element.31.cos_ref, ...), custom_call_target="tpu_custom_call" | custom-call | flops 905969664 | bytes 2359296 | tf_op jit(solution)/shard_map/attend/pallas_call | solution.py:386
  185.9 3.0 %collective-permute-start.16 = (bf16[384,256]{1,0:T(8,128)(2,1)S(1)}, bf16[384,256]{1,0:T(8,128)(2,1)S(1)}, u32[]{:S(2)}, u32[]{:S(2)}) collective-permute-start(bf16[384,256]{1,0:T(8,128)(2,1)S(1)} %attend.3.rest_0_), channel_id=1, source_target_pairs={{0,2},{1,3},{2,0},{3,1},{4,6},{5,7},{6,4},{7,5},{8,10},{9,11},{10,... | collective-permute-start | bytes 589832 | tf_op jit(solution)/shard_map/ppermute | solution.py:586
  189.0 6.0 %collective-permute-done.19.rest_1_ = bf16[384,256]{1,0:T(8,128)(2,1)S(1)} collective-permute-done((bf16[384,256]{1,0:T(8,128)(2,1)S(1)}, bf16[384,256]{1,0:T(8,128)(2,1)S(1)}, u32[]{:S(2)}, u32[]{:S(2)}) %collective-permute-start.19) | collective-permute-done | bytes 196640 | tf_op jit(solution)/shard_map/ppermute | solution.py:586
  195.0 2.0 collective-permute-start.17
  198.3 2.2 collective-permute-done.20.rest_2_
  200.5 4.2 %collective-permute-done.21.rest_3_ = bf16[384,256]{1,0:T(8,128)(2,1)} collective-permute-done((bf16[384,256]{1,0:T(8,128)(2,1)S(1)}, bf16[384,256]{1,0:T(8,128)(2,1)}, u32[]{:S(2)}, u32[]{:S(2)}) %collective-permute-start.21) | collective-permute-done | bytes 196640 | tf_op jit(solution)/shard_map/ppermute | solution.py:588
  206.2 4.1 %output.2 = (f32[384,1152]{1,0:T(8,128)S(1)}, f32[1,384]{1,0:T(1,128)S(1)}) custom-call(s32[4]{0:T(128)S(1)} %pad_add_fusion.at_ref, bf16[256,4608]{1,0:T(8,128)(2,1)S(1)} %copy-done.2, bf16[8,3,32,1152]{3,2,1,0:T(8,128)(2,1)S(1)} %bitcast.13, bf16[384,256]{1,0:T(8,128)(2,1)S(1)} %attend.2.after_ref.rest_0_, ...), custom_call_target="tpu_custom_call" | custom-call | tf_op jit(solution)/shard_map/output/pallas_call | solution.py:452
  210.3 2.1 collective-permute-start.26
  212.4 1.7 collective-permute-start.27
  214.2 3.1 %output.3 = (f32[384,1152]{1,0:T(8,128)S(1)}, f32[1,384]{1,0:T(1,128)S(1)}) custom-call(s32[4]{0:T(128)S(1)} %pad_add_fusion.at_ref, bf16[256,4608]{1,0:T(8,128)(2,1)S(1)} %copy-done.2, bf16[8,3,32,1152]{3,2,1,0:T(8,128)(2,1)S(1)} %bitcast.14, bf16[384,256]{1,0:T(8,128)(2,1)S(1)} %attend.3.rest_0_, bf16[384,256]{1,0:T(8,128)(2,1)S(1)} %collective-permute-done.16.rest_1_, ...), custom_call_target="tpu_custom_call" | custom-call | tf_op jit(solution)/shard_map/output/pallas_call | solution.py:452
  219.4 2.8 %collective-permute-start.24 = (f32[1,384]{1,0:T(1,128)S(1)}, f32[1,384]{1,0:T(1,128)S(1)}, u32[]{:S(2)}, u32[]{:S(2)}) collective-permute-start(f32[1,384]{1,0:T(1,128)S(1)} %get-tuple-element.23.rest_0_), channel_id=1, source_target_pairs={{0,3},{1,0},{2,1},{3,2},{4,7},{5,4},{6,5},{7,6},{8,11},{9,8},{10,9... | collective-permute-start | bytes 4616 | tf_op jit(solution)/shard_map/ppermute | solution.py:597
  222.3 1.9 finish.2.rest_4_
  224.3 1.9 finish.3
  (82 shorter events, 34.2 us)
Async XLA Ops:
  6.5 198.2 %all-gather.3.cloned.1.call-start = ((), (), s32[]{:S(2)}) async-start(), calls=%async_computation | async-start | bytes 1990656 | tf_op jit(solution)/shard_map/all_gather | solution.py:575
  6.5 56.9 %collective-permute-start = (bf16[768,1152]{1,0:T(8,128)(2,1)}, bf16[768,1152]{1,0:T(8,128)(2,1)S(1)}, u32[]{:S(2)}, u32[]{:S(2)}) collective-permute-start(bf16[768,1152]{1,0:T(8,128)(2,1)} %token_ref.3), channel_id=1, source_target_pairs={{0,1},{1,0},{2,3},{3,2},{4,5},{5,4},{6,7},{7,6},{8,9},{9,8},{10,11... | collective-permute-start | bytes 5308424 | tf_op jit(solution)/shard_map/ppermute | solution.py:543
  9.8 53.0 %copy-start.11 = (f32[4608]{0:T(1024)S(1)}, f32[4608]{0:T(1024)}, u32[]{:S(2)}) copy-start(f32[4608]{0:T(1024)} %param.10) | copy-start | bytes 55300
  9.9 39.6 %collective-permute-start.1 = (bf16[288,256]{1,0:T(8,128)(2,1)}, bf16[288,256]{1,0:T(8,128)(2,1)S(1)}, u32[]{:S(2)}, u32[]{:S(2)}) collective-permute-start(bf16[288,256]{1,0:T(8,128)(2,1)} %get-tuple-element.17), channel_id=1, source_target_pairs={{0,2},{1,3},{2,0},{3,1},{4,6},{5,7},{6,4},{7,5},{8,10},{9,11},{10,... | collective-permute-start | bytes 442376 | tf_op jit(solution)/shard_map/ppermute | solution.py:535
  49.5 5.1 %collective-permute-start.2 = (bf16[1,288,256]{2,1,0:T(8,128)(2,1)S(1)}, bf16[1,288,256]{2,1,0:T(8,128)(2,1)S(1)}, u32[]{:S(2)}, u32[]{:S(2)}) collective-permute-start(bf16[1,288,256]{2,1,0:T(8,128)(2,1)S(1)} %bitcast.15), channel_id=1, source_target_pairs={{0,8},{4,12},{8,0},{12,4},{16,24},{20,28},{24,16},{28,20},{1,9},{5... | collective-permute-start | bytes 442376 | tf_op jit(solution)/shard_map/ppermute | solution.py:115
  55.0 6.8 %collective-permute-start.3 = (bf16[2,288,256]{2,1,0:T(8,128)(2,1)S(1)}, bf16[2,288,256]{2,1,0:T(8,128)(2,1)S(1)}, u32[]{:S(2)}, u32[]{:S(2)}) collective-permute-start(bf16[2,288,256]{2,1,0:T(8,128)(2,1)S(1)} %join.4.first_ref), channel_id=1, source_target_pairs={{0,16},{4,20},{8,24},{12,28},{16,0},{20,4},{24,8},{28,12},{1,17},{... | collective-permute-start | bytes 884744 | tf_op jit(solution)/shard_map/ppermute | solution.py:115
  62.7 7.3 %collective-permute-start.4 = (bf16[4,288,256]{2,1,0:T(8,128)(2,1)}, bf16[4,288,256]{2,1,0:T(8,128)(2,1)}, u32[]{:S(2)}, u32[]{:S(2)}) collective-permute-start(bf16[4,288,256]{2,1,0:T(8,128)(2,1)} %join.5.own_ref), channel_id=1, source_target_pairs={{0,4},{4,0},{8,12},{12,8},{16,20},{20,16},{24,28},{28,24},{1,5},{5... | collective-permute-start | bytes 1769480 | tf_op jit(solution)/shard_map/ppermute | solution.py:115
  74.0 22.2 %collective-permute-start.5 = (bf16[784,256]{1,0:T(8,128)(2,1)}, bf16[784,256]{1,0:T(8,128)(2,1)}, u32[]{:S(2)}, u32[]{:S(2)}) collective-permute-start(bf16[784,256]{1,0:T(8,128)(2,1)} %far.2.after_ref), channel_id=1, source_target_pairs={{0,2},{1,3},{2,0},{3,1},{4,6},{5,7},{6,4},{7,5},{8,10},{9,11},{10,... | collective-permute-start | bytes 1204232 | tf_op jit(solution)/shard_map/ppermute | solution.py:549
  100.0 5.2 %collective-permute-start.8 = (bf16[32,1152]{1,0:T(8,128)(2,1)S(1)}, bf16[32,1152]{1,0:T(8,128)(2,1)S(1)}, u32[]{:S(2)}, u32[]{:S(2)}) collective-permute-start(bf16[32,1152]{1,0:T(8,128)(2,1)S(1)} %get-tuple-element.26), channel_id=1, source_target_pairs={{0,3},{1,0},{2,1},{3,2},{4,7},{5,4},{6,5},{7,6},{8,11},{9,8},{10,9... | collective-permute-start | bytes 221192 | tf_op jit(solution)/shard_map/ppermute | solution.py:574
  102.5 7.1 %collective-permute-start.7 = (bf16[32,1152]{1,0:T(8,128)(2,1)S(1)}, bf16[32,1152]{1,0:T(8,128)(2,1)S(1)}, u32[]{:S(2)}, u32[]{:S(2)}) collective-permute-start(bf16[32,1152]{1,0:T(8,128)(2,1)S(1)} %get-tuple-element.27), channel_id=1, source_target_pairs={{0,2},{1,3},{2,0},{3,1},{4,6},{5,7},{6,4},{7,5},{8,10},{9,11},{10,... | collective-permute-start | bytes 221192 | tf_op jit(solution)/shard_map/ppermute | solution.py:574
  102.5 7.1 %collective-permute-start.6 = (bf16[32,1152]{1,0:T(8,128)(2,1)S(1)}, bf16[32,1152]{1,0:T(8,128)(2,1)S(1)}, u32[]{:S(2)}, u32[]{:S(2)}) collective-permute-start(bf16[32,1152]{1,0:T(8,128)(2,1)S(1)} %get-tuple-element.25), channel_id=1, source_target_pairs={{0,1},{1,2},{2,3},{3,0},{4,5},{5,6},{6,7},{7,4},{8,9},{9,10},{10,1... | collective-permute-start | bytes 221192 | tf_op jit(solution)/shard_map/ppermute | solution.py:574
  110.3 8.9 %collective-permute-start.9 = (bf16[288,256]{1,0:T(8,128)(2,1)}, bf16[288,256]{1,0:T(8,128)(2,1)S(1)}, u32[]{:S(2)}, u32[]{:S(2)}) collective-permute-start(bf16[288,256]{1,0:T(8,128)(2,1)} %get-tuple-element.18), channel_id=1, source_target_pairs={{0,2},{1,3},{2,0},{3,1},{4,6},{5,7},{6,4},{7,5},{8,10},{9,11},{10,... | collective-permute-start | bytes 442376 | tf_op jit(solution)/shard_map/ppermute | solution.py:536
  119.2 6.5 %collective-permute-start.10 = (bf16[1,288,256]{2,1,0:T(8,128)(2,1)S(1)}, bf16[1,288,256]{2,1,0:T(8,128)(2,1)S(1)}, u32[]{:S(2)}, u32[]{:S(2)}) collective-permute-start(bf16[1,288,256]{2,1,0:T(8,128)(2,1)S(1)} %bitcast.17), channel_id=1, source_target_pairs={{0,16},{4,20},{8,24},{12,28},{16,0},{20,4},{24,8},{28,12},{1,17},{... | collective-permute-start | bytes 442376 | tf_op jit(solution)/shard_map/ppermute | solution.py:115
  126.7 13.7 %collective-permute-start.11 = (bf16[2,288,256]{2,1,0:T(8,128)(2,1)}, bf16[2,288,256]{2,1,0:T(8,128)(2,1)}, u32[]{:S(2)}, u32[]{:S(2)}) collective-permute-start(bf16[2,288,256]{2,1,0:T(8,128)(2,1)} %join.6.first_ref), channel_id=1, source_target_pairs={{0,8},{4,12},{8,0},{12,4},{16,24},{20,28},{24,16},{28,20},{1,9},{5... | collective-permute-start | bytes 884744 | tf_op jit(solution)/shard_map/ppermute | solution.py:115
  141.6 12.5 %collective-permute-start.12 = (bf16[4,288,256]{2,1,0:T(8,128)(2,1)S(1)}, bf16[4,288,256]{2,1,0:T(8,128)(2,1)S(1)}, u32[]{:S(2)}, u32[]{:S(2)}) collective-permute-start(bf16[4,288,256]{2,1,0:T(8,128)(2,1)S(1)} %join.7.own_ref), channel_id=1, source_target_pairs={{0,4},{4,0},{8,12},{12,8},{16,20},{20,16},{24,28},{28,24},{1,5},{5... | collective-permute-start | bytes 1769480 | tf_op jit(solution)/shard_map/ppermute | solution.py:115
  150.2 22.7 %collective-permute-start.14 = (bf16[784,256]{1,0:T(8,128)(2,1)S(1)}, bf16[784,256]{1,0:T(8,128)(2,1)S(1)}, u32[]{:S(2)}, u32[]{:S(2)}) collective-permute-start(bf16[784,256]{1,0:T(8,128)(2,1)S(1)} %get-tuple-element.20.rest_2_), channel_id=1, source_target_pairs={{0,8},{4,12},{1,9},{5,13},{2,10},{6,14},{3,11},{7,15},{16,24},{20,... | collective-permute-start | bytes 1204232 | tf_op jit(solution)/shard_map/ppermute | solution.py:564
  151.5 21.4 %collective-permute-start.15 = (bf16[784,256]{1,0:T(8,128)(2,1)S(1)}, bf16[784,256]{1,0:T(8,128)(2,1)S(1)}, u32[]{:S(2)}, u32[]{:S(2)}) collective-permute-start(bf16[784,256]{1,0:T(8,128)(2,1)S(1)} %get-tuple-element.20.rest_2_), channel_id=1, source_target_pairs={{0,4},{4,8},{8,12},{1,5},{5,9},{9,13},{2,6},{6,10},{10,14},{3,7},{... | collective-permute-start | bytes 1204232 | tf_op jit(solution)/shard_map/ppermute | solution.py:564
  157.4 15.5 %collective-permute-start.13 = (bf16[768,256]{1,0:T(8,128)(2,1)S(1)}, bf16[768,256]{1,0:T(8,128)(2,1)S(1)}, u32[]{:S(2)}, u32[]{:S(2)}) collective-permute-start(bf16[768,256]{1,0:T(8,128)(2,1)S(1)} %far.3), channel_id=1, source_target_pairs={{0,2},{1,3},{2,0},{3,1},{4,6},{5,7},{6,4},{7,5},{8,10},{9,11},{10,... | collective-permute-start | bytes 1179656 | tf_op jit(solution)/shard_map/ppermute | solution.py:554
  181.4 23.3 %copy-start.2 = (bf16[256,4608]{1,0:T(8,128)(2,1)S(1)}, bf16[256,4608]{1,0:T(8,128)(2,1)}, u32[]{:S(2)}) copy-start(bf16[256,4608]{1,0:T(8,128)(2,1)} %own_o_ref.3) | copy-start | bytes 7077892
  181.4 13.5 %collective-permute-start.19 = (bf16[384,256]{1,0:T(8,128)(2,1)S(1)}, bf16[384,256]{1,0:T(8,128)(2,1)S(1)}, u32[]{:S(2)}, u32[]{:S(2)}) collective-permute-start(bf16[384,256]{1,0:T(8,128)(2,1)S(1)} %attend.2.after_ref.rest_0_), channel_id=1, source_target_pairs={{0,2},{1,3},{2,0},{3,1},{4,6},{5,7},{6,4},{7,5},{8,10},{9,11},{10,... | collective-permute-start | bytes 589832 | tf_op jit(solution)/shard_map/ppermute | solution.py:586
  185.9 12.3 %collective-permute-start.16 = (bf16[384,256]{1,0:T(8,128)(2,1)S(1)}, bf16[384,256]{1,0:T(8,128)(2,1)S(1)}, u32[]{:S(2)}, u32[]{:S(2)}) collective-permute-start(bf16[384,256]{1,0:T(8,128)(2,1)S(1)} %attend.3.rest_0_), channel_id=1, source_target_pairs={{0,2},{1,3},{2,0},{3,1},{4,6},{5,7},{6,4},{7,5},{8,10},{9,11},{10,... | collective-permute-start | bytes 589832 | tf_op jit(solution)/shard_map/ppermute | solution.py:586
  188.9 11.6 %collective-permute-start.20 = (bf16[384,256]{1,0:T(8,128)(2,1)S(1)}, bf16[384,256]{1,0:T(8,128)(2,1)}, u32[]{:S(2)}, u32[]{:S(2)}) collective-permute-start(bf16[384,256]{1,0:T(8,128)(2,1)S(1)} %attend.2.after_ref.rest_0_), channel_id=1, source_target_pairs={{0,1},{1,0},{2,3},{3,2},{4,5},{5,4},{6,7},{7,6},{8,9},{9,8},{10,11... | collective-permute-start | bytes 589832 | tf_op jit(solution)/shard_map/ppermute | solution.py:587
  195.0 9.7 %collective-permute-start.21 = (bf16[384,256]{1,0:T(8,128)(2,1)S(1)}, bf16[384,256]{1,0:T(8,128)(2,1)}, u32[]{:S(2)}, u32[]{:S(2)}) collective-permute-start(bf16[384,256]{1,0:T(8,128)(2,1)S(1)} %collective-permute-done.19.rest_1_), channel_id=1, source_target_pairs={{0,1},{1,0},{2,3},{3,2},{4,5},{5,4},{6,7},{7,6},{8,9},{9,8},{10,11... | collective-permute-start | bytes 589832 | tf_op jit(solution)/shard_map/ppermute | solution.py:588
  195.0 19.2 %collective-permute-start.17 = (bf16[384,256]{1,0:T(8,128)(2,1)S(1)}, bf16[384,256]{1,0:T(8,128)(2,1)S(1)}, u32[]{:S(2)}, u32[]{:S(2)}) collective-permute-start(bf16[384,256]{1,0:T(8,128)(2,1)S(1)} %attend.3.rest_0_), channel_id=1, source_target_pairs={{0,1},{1,0},{2,3},{3,2},{4,5},{5,4},{6,7},{7,6},{8,9},{9,8},{10,11... | collective-permute-start | bytes 589832 | tf_op jit(solution)/shard_map/ppermute | solution.py:587
  198.2 16.0 %collective-permute-start.18 = (bf16[384,256]{1,0:T(8,128)(2,1)S(1)}, bf16[384,256]{1,0:T(8,128)(2,1)S(1)}, u32[]{:S(2)}, u32[]{:S(2)}) collective-permute-start(bf16[384,256]{1,0:T(8,128)(2,1)S(1)} %collective-permute-done.16.rest_1_), channel_id=1, source_target_pairs={{0,1},{1,0},{2,3},{3,2},{4,5},{5,4},{6,7},{7,6},{8,9},{9,8},{10,11... | collective-permute-start | bytes 589832 | tf_op jit(solution)/shard_map/ppermute | solution.py:588
  210.3 12.0 %copy-start.1 = (bf16[768,1152]{1,0:T(8,128)(2,1)S(1)}, bf16[768,1152]{1,0:T(8,128)(2,1)}, u32[]{:S(2)}) copy-start(bf16[768,1152]{1,0:T(8,128)(2,1)} %token_ref.3) | copy-start | bytes 5308420
  210.3 9.2 %collective-permute-start.25 = (f32[1,384]{1,0:T(1,128)S(1)}, f32[1,384]{1,0:T(1,128)S(1)}, u32[]{:S(2)}, u32[]{:S(2)}) collective-permute-start(f32[1,384]{1,0:T(1,128)S(1)} %get-tuple-element.21.rest_4_.rest_0_), channel_id=1, source_target_pairs={{0,1},{1,2},{2,3},{3,0},{4,5},{5,6},{6,7},{7,4},{8,9},{9,10},{10,1... | collective-permute-start | bytes 4616 | tf_op jit(solution)/shard_map/ppermute | solution.py:597
  210.3 12.0 %collective-permute-start.26 = (f32[1,384]{1,0:T(1,128)S(1)}, f32[1,384]{1,0:T(1,128)S(1)}, u32[]{:S(2)}, u32[]{:S(2)}) collective-permute-start(f32[1,384]{1,0:T(1,128)S(1)} %get-tuple-element.21.rest_4_.rest_0_), channel_id=1, source_target_pairs={{0,2},{1,3},{2,0},{3,1},{4,6},{5,7},{6,4},{7,5},{8,10},{9,11},{10,... | collective-permute-start | bytes 4616 | tf_op jit(solution)/shard_map/ppermute | solution.py:597
  212.4 9.9 %collective-permute-start.27 = (f32[1,384]{1,0:T(1,128)S(1)}, f32[1,384]{1,0:T(1,128)S(1)}, u32[]{:S(2)}, u32[]{:S(2)}) collective-permute-start(f32[1,384]{1,0:T(1,128)S(1)} %get-tuple-element.21.rest_4_.rest_0_), channel_id=1, source_target_pairs={{0,3},{1,0},{2,1},{3,2},{4,7},{5,4},{6,5},{7,6},{8,11},{9,8},{10,9... | collective-permute-start | bytes 4616 | tf_op jit(solution)/shard_map/ppermute | solution.py:597
  217.3 7.0 %collective-permute-start.22 = (f32[1,384]{1,0:T(1,128)S(1)}, f32[1,384]{1,0:T(1,128)S(1)}, u32[]{:S(2)}, u32[]{:S(2)}) collective-permute-start(f32[1,384]{1,0:T(1,128)S(1)} %get-tuple-element.23.rest_0_), channel_id=1, source_target_pairs={{0,1},{1,2},{2,3},{3,0},{4,5},{5,6},{6,7},{7,4},{8,9},{9,10},{10,1... | collective-permute-start | bytes 4616 | tf_op jit(solution)/shard_map/ppermute | solution.py:597
  217.9 6.3 %collective-permute-start.23 = (f32[1,384]{1,0:T(1,128)S(1)}, f32[1,384]{1,0:T(1,128)S(1)}, u32[]{:S(2)}, u32[]{:S(2)}) collective-permute-start(f32[1,384]{1,0:T(1,128)S(1)} %get-tuple-element.23.rest_0_), channel_id=1, source_target_pairs={{0,2},{1,3},{2,0},{3,1},{4,6},{5,7},{6,4},{7,5},{8,10},{9,11},{10,... | collective-permute-start | bytes 4616 | tf_op jit(solution)/shard_map/ppermute | solution.py:597
  219.4 4.8 %collective-permute-start.24 = (f32[1,384]{1,0:T(1,128)S(1)}, f32[1,384]{1,0:T(1,128)S(1)}, u32[]{:S(2)}, u32[]{:S(2)}) collective-permute-start(f32[1,384]{1,0:T(1,128)S(1)} %get-tuple-element.23.rest_0_), channel_id=1, source_target_pairs={{0,3},{1,0},{2,1},{3,2},{4,7},{5,4},{6,5},{7,6},{8,11},{9,8},{10,9... | collective-permute-start | bytes 4616 | tf_op jit(solution)/shard_map/ppermute | solution.py:597
  (10 other events, 32.6 us)
Sparse Core Ops, SparseCore 0:
  110.4 30.6 all-gather.2

commit v6 on v5

--- a/solution.py
+++ b/solution.py
@@ -51,13 +51,14 @@
     return vectors * cosine + pltpu.roll(vectors, HEAD_SIZE // 2, 1) * sine
 
 
-def pack_kernel(at_ref, q_ref, k_ref, v_ref, kv_out, q_out, sems):
+def pack_kernel(at_ref, q_ref, k_ref, v_ref, x_ref, kv_out, q_out, x_out, sems):
     share, width = q_out.shape[0], k_ref.shape[1]
     rows = pl.ds(pl.multiple_of(at_ref[0] * share, TAIL), share)
     copies = [
         pltpu.make_async_copy(k_ref.at[rows], kv_out.at[:, pl.ds(0, width)], sems.at[0]),
         pltpu.make_async_copy(v_ref.at[rows], kv_out.at[:, pl.ds(width, width)], sems.at[1]),
         pltpu.make_async_copy(q_ref.at[rows], q_out, sems.at[2]),
+        pltpu.make_async_copy(x_ref.at[pl.ds(0, x_out.shape[0])], x_out, sems.at[3]),
     ]
     for copy in copies:
         copy.start()
@@ -65,81 +66,85 @@
         copy.wait()
 
 
-def pack(at, q_weight, k_weight, v_weight, share):
+def pack(at, q_weight, k_weight, v_weight, share, tokens, rows):
     kv_width = k_weight.shape[1] + v_weight.shape[1]
+    dims = [(share, kv_width), (share, q_weight.shape[1]), (rows, tokens.shape[1])]
     return pl.pallas_call(
         pack_kernel,
-        out_shape=(shape((share, kv_width), BF16), shape((share, q_weight.shape[1]), BF16)),
+        out_shape=tuple(shape(d, BF16) for d in dims),
         grid_spec=pltpu.PrefetchScalarGridSpec(
             num_scalar_prefetch=1,
             grid=(1,),
-            in_specs=[HBM, HBM, HBM],
-            out_specs=[
-                pl.BlockSpec((share, kv_width), lambda i, at: (0, 0)),
-                pl.BlockSpec((share, q_weight.shape[1]), lambda i, at: (0, 0)),
-            ],
-            scratch_shapes=[pltpu.SemaphoreType.DMA((3,))],
+            in_specs=[HBM, HBM, HBM, HBM],
+            out_specs=[pl.BlockSpec(d, lambda i, at: (0, 0)) for d in dims],
+            scratch_shapes=[pltpu.SemaphoreType.DMA((4,))],
         ),
         compiler_params=ALL_VMEM,
         name="pack",
-    )(at, q_weight, k_weight, v_weight)
-
-
-def join_kernel(first_ref, second_ref, out_ref, sems):
-    held = first_ref.shape[0]
-    copies = [
-        pltpu.make_async_copy(first_ref, out_ref.at[pl.ds(0, held)], sems.at[0]),
-        pltpu.make_async_copy(second_ref, out_ref.at[pl.ds(held, held)], sems.at[1]),
-    ]
+    )(at, q_weight, k_weight, v_weight, tokens)
+
+
+def stage_kernel(*refs, pairs, first, count):
+    outputs = pairs + (1 if count else 0)
+    ins, outs, sems = refs[: -outputs - 1], refs[-outputs - 1 : -1], refs[-1]
+    copies = []
+    for p in range(pairs):
+        held = ins[2 * p].shape[0]
+        for side in range(2):
+            there = outs[p].at[pl.ds(side * held, held)]
+            copies.append(
+                pltpu.make_async_copy(ins[2 * p + side], there, sems.at[len(copies)])
+            )
+    if count:
+        rows = ins[2 * pairs].at[pl.ds(first, count)]
+        copies.append(pltpu.make_async_copy(rows, outs[-1], sems.at[len(copies)]))
     for copy in copies:
         copy.start()
     for copy in copies:
         copy.wait()
 
 
-def join(first, second):
-    return pl.pallas_call(
-        join_kernel,
-        out_shape=shape((2 * first.shape[0],) + first.shape[1:], first.dtype),
-        in_specs=[ANY, ANY],
-        scratch_shapes=[pltpu.SemaphoreType.DMA((2,))],
-        compiler_params=PARAMS,
-        name="join",
-    )(first, second)
-
-
-def spread(piece, plane, masks):
-    own = piece[None]
-    order = [0]
-    for mask in masks:
-        got = lax.ppermute(own, PLANE, [(i, i ^ mask) for i in range(plane)])
-        order = order + [k ^ mask for k in order]
-        if mask != masks[-1]:
-            own = join(own, got)
-    return order, own, got
-
-
-def prep_kernel(src_ref, gain_ref, *rest):
+def stage(joined, tokens, first, count, after):
+    dims = [(2 * pair[0].shape[0],) + pair[0].shape[1:] for pair in joined]
+    if count:
+        dims.append((count, tokens.shape[1]))
+    return pl.pallas_call(
+        partial(stage_kernel, pairs=len(joined), first=first, count=count),
+        out_shape=tuple(shape(d, BF16) for d in dims),
+        in_specs=[ANY] * (2 * len(joined) + 1 + len(after)),
+        scratch_shapes=[pltpu.SemaphoreType.DMA((2 * len(joined) + 1,))],
+        compiler_params=PARAMS,
+        name="stage",
+    )(*[piece for pair in joined for piece in pair], tokens, *after)
+
+
+def prep_kernel(src_ref, gain_ref, *rest, cuts):
     x_refs, (out_ref, sq_ref) = rest[:-2], rest[-2:]
-    for k, x_ref in enumerate(x_refs):
-        x = x_ref[...].astype(F32)
-        squares = jnp.sum(x * x, axis=1, keepdims=True)
-        total = squares if k == 0 else total + squares
-        out_ref[k] = (x * gain_ref[src_ref[k]]).astype(BF16)
-    sq_ref[...] = to_row(total)
+    squares, at = [], 0
+    for k, pieces in enumerate(cuts):
+        column, row = [], 0
+        for x_ref in x_refs[at : at + pieces]:
+            x = x_ref[...].astype(F32)
+            column.append(jnp.sum(x * x, axis=1, keepdims=True))
+            out_ref[k, row : row + x.shape[0]] = (x * gain_ref[src_ref[k]]).astype(BF16)
+            row += x.shape[0]
+        squares.append(jnp.concatenate(column, axis=0))
+        at += pieces
+    sq_ref[...] = to_row(sum(squares[1:], squares[0]))
 
 
 def prep(sources, gains, blocks):
-    rows, cols = blocks[0].shape
+    rows, cols = blocks[0][0].shape
     dims = (len(blocks), rows, cols)
-    return pl.pallas_call(
-        prep_kernel,
+    pieces = [piece for block in blocks for piece in block]
+    return pl.pallas_call(
+        partial(prep_kernel, cuts=[len(block) for block in blocks]),
         out_shape=(shape(dims, BF16), shape((1, rows), F32)),
         grid_spec=pltpu.PrefetchScalarGridSpec(
             num_scalar_prefetch=1,
             grid=(1,),
             in_specs=[pl.BlockSpec(gains.shape, lambda i, s: (0, 0, 0))]
-            + [pl.BlockSpec((rows, cols), lambda i, s: (0, 0)) for _ in blocks],
+            + [pl.BlockSpec(piece.shape, lambda i, s: (0, 0)) for piece in pieces],
             out_specs=[
                 pl.BlockSpec(dims, lambda i, s: (0, 0, 0)),
                 pl.BlockSpec((1, rows), lambda i, s: (0, 0)),
@@ -147,7 +152,7 @@
         ),
         compiler_params=PARAMS,
         name="prep",
-    )(sources, gains, *blocks)
+    )(sources, gains, *pieces)
 
 
 def far_kernel(place_ref, src_ref, x_ref, sq_ref, own_ref, got_ref, *rest, order, with_sq):
@@ -261,7 +266,7 @@
 
 
 def keys_kernel(
-    near_ref, far_ref, sq_ref, id_ref, cos_ref, sin_ref, out_ref, sum_ref, *, model
+    near_ref, far_ref, sq_ref, id_ref, cos_ref, sin_ref, after_ref, out_ref, sum_ref, *, model
 ):
     chunk, width = near_ref.shape
     tail = far_ref[chunk:, :].astype(F32)
@@ -277,7 +282,7 @@
     out_ref[chunk:, :] = lines_of((id_ref[...].astype(F32),), width)
 
 
-def keys_values(near, far, sq, ids, cosine, sine, width, model):
+def keys_values(near, far, sq, ids, cosine, sine, after, width, model):
     chunk = near.shape[0]
     whole = lambda i: (0, 0)
     return pl.pallas_call(
@@ -291,11 +296,12 @@
             pl.BlockSpec((1, chunk), whole),
             pl.BlockSpec((chunk, HEAD_SIZE), whole),
             pl.BlockSpec((chunk, HEAD_SIZE), whole),
+            ANY,
         ],
         out_specs=[pl.BlockSpec((chunk + TAIL, width), whole), pl.BlockSpec((1, chunk), whole)],
         compiler_params=PARAMS,
         name="keys",
-    )(near, far, sq, ids, cosine, sine)
+    )(near, far, sq, ids, cosine, sine, after)
 
 
 def attention_kernel(
@@ -531,21 +537,48 @@
 
     share = half_rows // plane
     at = jnp.reshape((1 - side) * plane + in_plane, (1,))
-    packed_kv, packed_q = pack(at, q_weight, k_weight, value_weight, share)
-    far_kv = lax.ppermute(packed_kv, "tensor", swap)
-    far_q = lax.ppermute(packed_q, "tensor", swap)
-    far_kv = spread(far_kv, plane, seq_bits + group_bits + [1])
-    far_q = spread(far_q, plane, group_bits + seq_bits + [1])
+    inner = seq_bits + group_bits
+    masks_kv, masks_q = inner + [1], inner[::-1] + [1]
+    steps = len(masks_kv)
+    piece = rows // (steps + 1) // TAIL * TAIL
+    counts = [rows - steps * piece] + [piece] * steps
+    if counts[0] > piece:
+        counts = [rows - steps * (piece + TAIL)] + [piece + TAIL] * steps
+    packed_kv, packed_q, cut = pack(
+        at, q_weight, k_weight, value_weight, share, tokens, counts[0]
+    )
+    own_kv = lax.ppermute(packed_kv, "tensor", swap)[None]
+    own_q = lax.ppermute(packed_q, "tensor", swap)[None]
+    received = [lax.ppermute(cut, "tensor", ring)]
+    order_kv, order_q, first = [0], [0], counts[0]
+    for step, (mask_kv, mask_q) in enumerate(zip(masks_kv, masks_q)):
+        if step == 0:
+            (cut,) = stage([], tokens, first, counts[1], [own_kv, own_q, received[0]])
+        else:
+            own_kv, own_q, cut = stage(
+                [(own_kv, far_kv), (own_q, far_q)],
+                tokens,
+                first,
+                counts[step + 1],
+                [received[-1]],
+            )
+        first += counts[step + 1]
+        far_kv = lax.ppermute(own_kv, PLANE, [(i, i ^ mask_kv) for i in range(plane)])
+        far_q = lax.ppermute(own_q, PLANE, [(i, i ^ mask_q) for i in range(plane)])
+        received.append(lax.ppermute(cut, "tensor", ring))
+        order_kv = order_kv + [k ^ mask_kv for k in order_kv]
+        order_q = order_q + [k ^ mask_q for k in order_q]
+    far_kv, far_q = (order_kv, own_kv, far_kv), (order_q, own_q, far_q)
 
     sources = (within + half - jnp.arange(half, dtype=jnp.int32)) % half
-    blocks = [tokens]
-    for _ in range(half - 1):
-        blocks.append(lax.ppermute(blocks[-1], "tensor", ring))
+    blocks = [[tokens], received]
+    for _ in range(half - 2):
+        blocks.append([lax.ppermute(part, "tensor", ring) for part in blocks[-1]])
     gains = in_gain.reshape(nz, 1, cols)
     x, sq = prep(side * half + sources, gains, blocks)
 
     place = jnp.reshape(in_plane, (1,))
-    sent_kv = far_product(place, sources, x, sq, far_kv, True, [])
+    sent_kv = far_product(place, sources, x, sq, far_kv, True, [far_q[2]])
     got_kv = lax.ppermute(sent_kv, "tensor", swap)
     weights = (k_weight, value_weight, q_weight)
     near = near_product(side * half + sources, x, weights, sent_kv)
@@ -555,7 +588,9 @@
     cosine, sine = rotation_table(seq * rows + jnp.arange(rows, dtype=jnp.int32))
     ids = seg_ids[None, :]
     kv_width = k_weight.shape[1] + value_weight.shape[1]
-    own_kv, sums = keys_values(near, got_kv, sq, ids, cosine, sine, kv_width, model)
+    own_kv, sums = keys_values(
+        near, got_kv, sq, ids, cosine, sine, sent_q, kv_width, model
+    )
 
     back = -(-(nseq * rows // 2 - 1) // rows)
     kv_blocks = [own_kv]
@@ -564,7 +599,8 @@
         kv_blocks.insert(0, lax.ppermute(own_kv, "seq", earlier))
 
     o_share = o_weight.shape[0] // plane
-    wait = (got_kv[0, 0] != got_kv[0, 0]).astype(jnp.int32)
+    last = got_kv[0, 0] + sent_q[0, 0]
+    wait = (last != last).astype(jnp.int32)
     moved = []
     for k in range(1, nz):
         target = (z + k) % nz

time: 235 us -> 198 us (0.84)
  the two profiles are of different devices: /device:TPU:2 before, /device:TPU:0 now
where the time goes in v6:
time: 198 us
  waiting for transfers between devices  82.3 us (42%)
  starting transfers between devices  43.8 us (22%)
  Pallas kernels  40.4 us (20%)
  between operations  15 us (8%)
  local copies, waits for them, and re-layouts  13.5 us (7%)
  other arithmetic  2.57 us (1%)
    ppermute x1, waiting for transfers between devices, per_device(): got_q = lax.ppermute(sent_q, 'tensor', swap)  18.2 us
    ppermute x3, waiting for transfers between devices, per_device(): received.append(lax.ppermute(cut, 'tensor', ring))  14 us
    ppermute x1, waiting for transfers between devices, per_device(): own_kv = lax.ppermute(packed_kv, 'tensor', swap)[None]  11.1 us
    unnamed x34, local copies, waits for them, and re-layouts  10.5 us
    ppermute x2, waiting for transfers between devices, per_device(): opposite = lax.ppermute(context, 'tensor', swap)  10.2 us
    pallas_call x2, Pallas kernels, attend(): pl.pallas_call(partial(attention_kernel, back=back, offset=c * rows, mode...  9.05 us
    ppermute x6, starting transfers between devices, per_device(): squares += [lax.ppermute(own_sq, 'tensor', turn(k)) for k in range(1, nz)]  8.87 us
    pallas_call x2, Pallas kernels, far_product(): pl.pallas_call(partial(far_kernel, order=order, with_sq=with_sq), out_sha...  7.86 us
  transfers between devices with their start and end apart: 32, of which 17 were waited for; matrix products, arithmetic and copies ran while one was open for 1% of the time, Pallas kernels for 14%

profile of v6, /device:TPU:0, one launch (start us, length us, event | category | flops | bytes accessed | tf_op | source)
XLA Modules:
  0.0 197.5 jit_solution(4022974315799195460)
XLA Ops:
  6.5 2.2 %pack.1 = (bf16[288,256]{1,0:T(8,128)(2,1)}, bf16[288,256]{1,0:T(8,128)(2,1)}, bf16[192,1152]{1,0:T(8,128)(2,1)}) custom-call(s32[1]{0:T(128)} %bitcast.4.at_ref, bf16[4608,256]{1,0:T(8,128)(2,1)} %q_ref.3, bf16[4608,128]{1,0:T(8,128)(2,1)} %k_ref.3, bf16[4608,128]{1,0:T(8,128)(2,1)} %v_ref.3, bf16[768,1152]{1,0:T(8,128)(2,1)} %token_ref.3), custom_call_target="tpu_custom_call" | custom-call | tf_op jit(solution)/shard_map/pack/pallas_call | solution.py:72
  8.7 3.1 %collective-permute-start = (bf16[192,1152]{1,0:T(8,128)(2,1)}, bf16[192,1152]{1,0:T(8,128)(2,1)S(1)}, u32[]{:S(2)}, u32[]{:S(2)}) collective-permute-start(bf16[192,1152]{1,0:T(8,128)(2,1)} %get-tuple-element.22), channel_id=1, source_target_pairs={{0,1},{1,0},{2,3},{3,2},{4,5},{5,4},{6,7},{7,6},{8,9},{9,8},{10,11... | collective-permute-start | bytes 1327112 | tf_op jit(solution)/shard_map/ppermute | solution.py:552
  11.8 2.6 %collective-permute-start.1 = (bf16[288,256]{1,0:T(8,128)(2,1)}, bf16[288,256]{1,0:T(8,128)(2,1)S(1)}, u32[]{:S(2)}, u32[]{:S(2)}) collective-permute-start(bf16[288,256]{1,0:T(8,128)(2,1)} %get-tuple-element.23), channel_id=1, source_target_pairs={{0,2},{1,3},{2,0},{3,1},{4,6},{5,7},{6,4},{7,5},{8,10},{9,11},{10,... | collective-permute-start | bytes 442376 | tf_op jit(solution)/shard_map/ppermute | solution.py:550
  14.7 11.1 %collective-permute-done.1 = bf16[288,256]{1,0:T(8,128)(2,1)S(1)} collective-permute-done((bf16[288,256]{1,0:T(8,128)(2,1)}, bf16[288,256]{1,0:T(8,128)(2,1)S(1)}, u32[]{:S(2)}, u32[]{:S(2)}) %collective-permute-start.1) | collective-permute-done | bytes 147488 | tf_op jit(solution)/shard_map/ppermute | solution.py:550
  25.9 2.0 %collective-permute-done.2 = bf16[288,256]{1,0:T(8,128)(2,1)S(1)} collective-permute-done((bf16[288,256]{1,0:T(8,128)(2,1)}, bf16[288,256]{1,0:T(8,128)(2,1)S(1)}, u32[]{:S(2)}, u32[]{:S(2)}) %collective-permute-start.2) | collective-permute-done | bytes 147488 | tf_op jit(solution)/shard_map/ppermute | solution.py:551
  28.8 2.8 %collective-permute-start.3 = (bf16[192,1152]{1,0:T(8,128)(2,1)S(1)}, bf16[192,1152]{1,0:T(8,128)(2,1)S(1)}, u32[]{:S(2)}, u32[]{:S(2)}) collective-permute-start(bf16[192,1152]{1,0:T(8,128)(2,1)S(1)} %stage.3), channel_id=1, source_target_pairs={{0,1},{1,0},{2,3},{3,2},{4,5},{5,4},{6,7},{7,6},{8,9},{9,8},{10,11... | collective-permute-start | bytes 1327112 | tf_op jit(solution)/shard_map/ppermute | solution.py:568
  34.6 2.1 %collective-permute-done.4.refs_1_ = bf16[1,288,256]{2,1,0:T(8,128)(2,1)S(1)} collective-permute-done((bf16[1,288,256]{2,1,0:T(8,128)(2,1)S(1)}, bf16[1,288,256]{2,1,0:T(8,128)(2,1)S(1)}, u32[]{:S(2)}, u32[]{:S(2)}) %collective-permute-start.4) | collective-permute-done | bytes 147488 | tf_op jit(solution)/shard_map/ppermute | solution.py:566
  38.2 2.7 %collective-permute-done.3.refs_5_.rest_2_ = bf16[192,1152]{1,0:T(8,128)(2,1)S(1)} collective-permute-done((bf16[192,1152]{1,0:T(8,128)(2,1)S(1)}, bf16[192,1152]{1,0:T(8,128)(2,1)S(1)}, u32[]{:S(2)}, u32[]{:S(2)}) %collective-permute-start.3) | collective-permute-done | bytes 442400 | tf_op jit(solution)/shard_map/ppermute | solution.py:568
  46.8 3.7 %collective-permute-done.7.refs_1_ = bf16[2,288,256]{2,1,0:T(8,128)(2,1)S(1)} collective-permute-done((bf16[2,288,256]{2,1,0:T(8,128)(2,1)S(1)}, bf16[2,288,256]{2,1,0:T(8,128)(2,1)S(1)}, u32[]{:S(2)}, u32[]{:S(2)}) %collective-permute-start.7) | collective-permute-done | bytes 294944 | tf_op jit(solution)/shard_map/ppermute | solution.py:566
  56.2 10.9 %collective-permute-done.9.rest_4_ = bf16[192,1152]{1,0:T(8,128)(2,1)} collective-permute-done((bf16[192,1152]{1,0:T(8,128)(2,1)}, bf16[192,1152]{1,0:T(8,128)(2,1)}, u32[]{:S(2)}, u32[]{:S(2)}) %collective-permute-start.9) | collective-permute-done | bytes 442400 | tf_op jit(solution)/shard_map/ppermute | solution.py:568
  68.2 2.8 %prep.1 = (bf16[2,768,1152]{2,1,0:T(8,128)(2,1)S(1)}, f32[1,768]{1,0:T(1,128)S(1)}) custom-call(s32[2]{0:T(128)S(1)} %broadcast_add_fusion.src_ref, f32[4,1,1152]{2,1,0:T(1,128)S(1)} %reshape.28.gain_ref, bf16[768,1152]{1,0:T(8,128)(2,1)S(1)} %copy-done, bf16[192,1152]{1,0:T(8,128)(2,1)S(1)} %collective-permute-done.refs_3_.rest_1_, ...), custom_call_target="tpu_custom_call" | custom-call | tf_op jit(solution)/shard_map/prep/pallas_call | solution.py:140
  71.1 4.9 %far.2.after_ref = bf16[784,256]{1,0:T(8,128)(2,1)} custom-call(s32[1]{0:T(128)} %bitcast.3.place_ref.after_ref.rest_4_, s32[2]{0:T(128)S(1)} %and_select_fusion.src_ref, bf16[2,768,1152]{2,1,0:T(8,128)(2,1)S(1)} %get-tuple-element.29.x_ref, f32[1,768]{1,0:T(1,128)S(1)} %get-tuple-element.30.sq_ref, bf16[4,288,256]{2,1,0:T(8,128)(2,1)} %get-tuple-element.31.own_ref, ...), custom_call_target="tpu_custom_call" | custom-call | tf_op jit(solution)/shard_map/far/pallas_call | solution.py:211
  77.5 2.0 %copy-done.5 = bf16[2,768,1152]{2,1,0:T(8,128)(2,1)S(1)} copy-done((bf16[2,768,1152]{2,1,0:T(8,128)(2,1)S(1)}, bf16[2,768,1152]{2,1,0:T(8,128)(2,1)}, u32[]{:S(2)}) %copy-start.5) | copy-done | bytes 3538968
  82.4 4.1 %near.1.rest_0_.near_ref = f32[768,512]{1,0:T(8,128)S(1)} custom-call(s32[2]{0:T(128)S(1)} %broadcast_add_fusion.src_ref, bf16[2,768,1152]{2,1,0:T(8,128)(2,1)S(1)} %copy-done.5, bf16[4608,128]{1,0:T(8,128)(2,1)S(1)} %copy-done.10, bf16[4608,128]{1,0:T(8,128)(2,1)S(1)} %copy-done.11, bf16[4608,256]{1,0:T(8,128)(2,1)S(1)} %copy-done.8, ...), custom_call_target="tpu_custom_call" | custom-call | tf_op jit(solution)/shard_map/near/pallas_call | solution.py:252
  86.5 2.9 %far.3.after_ref = bf16[768,256]{1,0:T(8,128)(2,1)S(1)} custom-call(s32[1]{0:T(128)} %bitcast.3.place_ref.after_ref.rest_4_, s32[2]{0:T(128)S(1)} %and_select_fusion.src_ref, bf16[2,768,1152]{2,1,0:T(8,128)(2,1)S(1)} %copy-done.6, f32[1,768]{1,0:T(1,128)S(1)} %get-tuple-element.30.sq_ref, bf16[4,288,256]{2,1,0:T(8,128)(2,1)} %get-tuple-element.32.own_ref, ...), custom_call_target="tpu_custom_call" | custom-call | tf_op jit(solution)/shard_map/far/pallas_call | solution.py:211
  90.0 6.4 %collective-permute-done.12.far_ref = bf16[784,256]{1,0:T(8,128)(2,1)} collective-permute-done((bf16[784,256]{1,0:T(8,128)(2,1)}, bf16[784,256]{1,0:T(8,128)(2,1)}, u32[]{:S(2)}, u32[]{:S(2)}) %collective-permute-start.12) | collective-permute-done | bytes 401440 | tf_op jit(solution)/shard_map/ppermute | solution.py:582
  100.0 2.3 %collective-permute-start.15 = (bf16[32,1152]{1,0:T(8,128)(2,1)S(1)}, bf16[32,1152]{1,0:T(8,128)(2,1)S(1)}, u32[]{:S(2)}, u32[]{:S(2)}) collective-permute-start(bf16[32,1152]{1,0:T(8,128)(2,1)S(1)} %get-tuple-element.40), channel_id=1, source_target_pairs={{0,3},{1,0},{2,1},{3,2},{4,7},{5,4},{6,5},{7,6},{8,11},{9,8},{10,9... | collective-permute-start | bytes 221192 | tf_op jit(solution)/shard_map/ppermute | solution.py:610
  102.9 2.0 %collective-permute-done.15 = bf16[32,1152]{1,0:T(8,128)(2,1)S(1)} collective-permute-done((bf16[32,1152]{1,0:T(8,128)(2,1)S(1)}, bf16[32,1152]{1,0:T(8,128)(2,1)S(1)}, u32[]{:S(2)}, u32[]{:S(2)}) %collective-permute-start.15) | collective-permute-done | bytes 73760 | tf_op jit(solution)/shard_map/ppermute | solution.py:610
  105.0 4.5 %collective-permute-done.14 = bf16[32,1152]{1,0:T(8,128)(2,1)S(1)} collective-permute-done((bf16[32,1152]{1,0:T(8,128)(2,1)S(1)}, bf16[32,1152]{1,0:T(8,128)(2,1)S(1)}, u32[]{:S(2)}, u32[]{:S(2)}) %collective-permute-start.14) | collective-permute-done | bytes 73760 | tf_op jit(solution)/shard_map/ppermute | solution.py:610
  114.8 3.4 %collective-permute-start.17 = (bf16[784,256]{1,0:T(8,128)(2,1)S(1)}, bf16[784,256]{1,0:T(8,128)(2,1)S(1)}, u32[]{:S(2)}, u32[]{:S(2)}) collective-permute-start(bf16[784,256]{1,0:T(8,128)(2,1)S(1)} %get-tuple-element.34.rest_2_), channel_id=1, source_target_pairs={{0,8},{4,12},{1,9},{5,13},{2,10},{6,14},{3,11},{7,15},{16,24},{20,... | collective-permute-start | bytes 1204232 | tf_op jit(solution)/shard_map/ppermute | solution.py:599
  121.6 18.2 %collective-permute-done.16.far_ref = bf16[768,256]{1,0:T(8,128)(2,1)S(1)} collective-permute-done((bf16[768,256]{1,0:T(8,128)(2,1)S(1)}, bf16[768,256]{1,0:T(8,128)(2,1)S(1)}, u32[]{:S(2)}, u32[]{:S(2)}) %collective-permute-start.16) | collective-permute-done | bytes 393248 | tf_op jit(solution)/shard_map/ppermute | solution.py:587
  139.9 4.4 %attend.2.after_ref.rest_0_ = bf16[384,256]{1,0:T(8,128)(2,1)S(1)} custom-call(s32[1]{0:T(128)} %bitcast.12.seq_ref, f32[768,512]{1,0:T(8,128)S(1)} %copy-done.2, bf16[768,256]{1,0:T(8,128)(2,1)S(1)} %collective-permute-done.16.far_ref, f32[1,768]{1,0:T(1,128)S(1)} %get-tuple-element.33.sum_ref, f32[768,128]{1,0:T(8,128)S(1)} %get-tuple-element.45.cos_ref, ...), custom_call_target="tpu_custom_call" | custom-call | flops 905969664 | bytes 2359296 | tf_op jit(solution)/shard_map/attend/pallas_call | solution.py:392
  144.3 4.7 %attend.3.rest_0_ = bf16[384,256]{1,0:T(8,128)(2,1)S(1)} custom-call(s32[1]{0:T(128)} %bitcast.12.seq_ref, f32[768,512]{1,0:T(8,128)S(1)} %copy-done.3, bf16[768,256]{1,0:T(8,128)(2,1)S(1)} %collective-permute-done.16.far_ref, f32[1,768]{1,0:T(1,128)S(1)} %get-tuple-element.33.sum_ref, f32[768,128]{1,0:T(8,128)S(1)} %get-tuple-element.45.cos_ref, ...), custom_call_target="tpu_custom_call" | custom-call | flops 905969664 | bytes 2359296 | tf_op jit(solution)/shard_map/attend/pallas_call | solution.py:392
  149.0 3.0 %collective-permute-start.19 = (bf16[384,256]{1,0:T(8,128)(2,1)S(1)}, bf16[384,256]{1,0:T(8,128)(2,1)S(1)}, u32[]{:S(2)}, u32[]{:S(2)}) collective-permute-start(bf16[384,256]{1,0:T(8,128)(2,1)S(1)} %attend.3.rest_0_), channel_id=1, source_target_pairs={{0,2},{1,3},{2,0},{3,1},{4,6},{5,7},{6,4},{7,5},{8,10},{9,11},{10,... | collective-permute-start | bytes 589832 | tf_op jit(solution)/shard_map/ppermute | solution.py:622
  152.0 7.8 %collective-permute-done.22.rest_1_ = bf16[384,256]{1,0:T(8,128)(2,1)S(1)} collective-permute-done((bf16[384,256]{1,0:T(8,128)(2,1)S(1)}, bf16[384,256]{1,0:T(8,128)(2,1)S(1)}, u32[]{:S(2)}, u32[]{:S(2)}) %collective-permute-start.22) | collective-permute-done | bytes 196640 | tf_op jit(solution)/shard_map/ppermute | solution.py:622
  159.8 2.0 %collective-permute-start.20 = (bf16[384,256]{1,0:T(8,128)(2,1)S(1)}, bf16[384,256]{1,0:T(8,128)(2,1)S(1)}, u32[]{:S(2)}, u32[]{:S(2)}) collective-permute-start(bf16[384,256]{1,0:T(8,128)(2,1)S(1)} %attend.3.rest_0_), channel_id=1, source_target_pairs={{0,1},{1,0},{2,3},{3,2},{4,5},{5,4},{6,7},{7,6},{8,9},{9,8},{10,11... | collective-permute-start | bytes 589832 | tf_op jit(solution)/shard_map/ppermute | solution.py:623
  161.8 2.4 %collective-permute-done.19.rest_1_ = bf16[384,256]{1,0:T(8,128)(2,1)S(1)} collective-permute-done((bf16[384,256]{1,0:T(8,128)(2,1)S(1)}, bf16[384,256]{1,0:T(8,128)(2,1)S(1)}, u32[]{:S(2)}, u32[]{:S(2)}) %collective-permute-start.19) | collective-permute-done | bytes 196640 | tf_op jit(solution)/shard_map/ppermute | solution.py:622
  164.3 4.2 %collective-permute-done.24.rest_3_ = bf16[384,256]{1,0:T(8,128)(2,1)S(1)} collective-permute-done((bf16[384,256]{1,0:T(8,128)(2,1)S(1)}, bf16[384,256]{1,0:T(8,128)(2,1)S(1)}, u32[]{:S(2)}, u32[]{:S(2)}) %collective-permute-start.24) | collective-permute-done | bytes 196640 | tf_op jit(solution)/shard_map/ppermute | solution.py:624
  171.6 3.1 %output.2 = (f32[384,1152]{1,0:T(8,128)S(1)}, f32[1,384]{1,0:T(1,128)S(1)}) custom-call(s32[4]{0:T(128)S(1)} %pad_add_fusion.at_ref, bf16[256,4608]{1,0:T(8,128)(2,1)S(1)} %copy-done.7, bf16[8,3,32,1152]{3,2,1,0:T(8,128)(2,1)S(1)} %bitcast.13, bf16[384,256]{1,0:T(8,128)(2,1)S(1)} %attend.2.after_ref.rest_0_, ...), custom_call_target="tpu_custom_call" | custom-call | tf_op jit(solution)/shard_map/output/pallas_call | solution.py:458
  174.8 2.8 %collective-permute-start.29 = (f32[1,384]{1,0:T(1,128)S(1)}, f32[1,384]{1,0:T(1,128)S(1)}, u32[]{:S(2)}, u32[]{:S(2)}) collective-permute-start(f32[1,384]{1,0:T(1,128)S(1)} %get-tuple-element.35.rest_4_.rest_0_), channel_id=1, source_target_pairs={{0,2},{1,3},{2,0},{3,1},{4,6},{5,7},{6,4},{7,5},{8,10},{9,11},{10,... | collective-permute-start | bytes 4616 | tf_op jit(solution)/shard_map/ppermute | solution.py:633
  178.6 3.1 %output.3 = (f32[384,1152]{1,0:T(8,128)S(1)}, f32[1,384]{1,0:T(1,128)S(1)}) custom-call(s32[4]{0:T(128)S(1)} %pad_add_fusion.at_ref, bf16[256,4608]{1,0:T(8,128)(2,1)S(1)} %copy-done.7, bf16[8,3,32,1152]{3,2,1,0:T(8,128)(2,1)S(1)} %bitcast.14, bf16[384,256]{1,0:T(8,128)(2,1)S(1)} %attend.3.rest_0_, bf16[384,256]{1,0:T(8,128)(2,1)S(1)} %collective-permute-done.19.rest_1_, ...), custom_call_target="tpu_custom_call" | custom-call | tf_op jit(solution)/shard_map/output/pallas_call | solution.py:458
  183.9 2.8 %collective-permute-start.27 = (f32[1,384]{1,0:T(1,128)S(1)}, f32[1,384]{1,0:T(1,128)S(1)}, u32[]{:S(2)}, u32[]{:S(2)}) collective-permute-start(f32[1,384]{1,0:T(1,128)S(1)} %get-tuple-element.37.rest_0_), channel_id=1, source_target_pairs={{0,3},{1,0},{2,1},{3,2},{4,7},{5,4},{6,5},{7,6},{8,11},{9,8},{10,9... | collective-permute-start | bytes 4616 | tf_op jit(solution)/shard_map/ppermute | solution.py:633
  (96 shorter events, 45.4 us)
Async XLA Ops:
  6.5 162.0 %all-gather.3.cloned.1.call-start = ((), (), s32[]{:S(2)}) async-start(), calls=%async_computation | async-start | bytes 1990656 | tf_op jit(solution)/shard_map/all_gather | solution.py:611
  8.7 19.8 %collective-permute-start = (bf16[192,1152]{1,0:T(8,128)(2,1)}, bf16[192,1152]{1,0:T(8,128)(2,1)S(1)}, u32[]{:S(2)}, u32[]{:S(2)}) collective-permute-start(bf16[192,1152]{1,0:T(8,128)(2,1)} %get-tuple-element.22), channel_id=1, source_target_pairs={{0,1},{1,0},{2,3},{3,2},{4,5},{5,4},{6,7},{7,6},{8,9},{9,8},{10,11... | collective-permute-start | bytes 1327112 | tf_op jit(solution)/shard_map/ppermute | solution.py:552
  11.8 14.0 %collective-permute-start.1 = (bf16[288,256]{1,0:T(8,128)(2,1)}, bf16[288,256]{1,0:T(8,128)(2,1)S(1)}, u32[]{:S(2)}, u32[]{:S(2)}) collective-permute-start(bf16[288,256]{1,0:T(8,128)(2,1)} %get-tuple-element.23), channel_id=1, source_target_pairs={{0,2},{1,3},{2,0},{3,1},{4,6},{5,7},{6,4},{7,5},{8,10},{9,11},{10,... | collective-permute-start | bytes 442376 | tf_op jit(solution)/shard_map/ppermute | solution.py:550
  14.4 13.5 %collective-permute-start.2 = (bf16[288,256]{1,0:T(8,128)(2,1)}, bf16[288,256]{1,0:T(8,128)(2,1)S(1)}, u32[]{:S(2)}, u32[]{:S(2)}) collective-permute-start(bf16[288,256]{1,0:T(8,128)(2,1)} %get-tuple-element.24), channel_id=1, source_target_pairs={{0,2},{1,3},{2,0},{3,1},{4,6},{5,7},{6,4},{7,5},{8,10},{9,11},{10,... | collective-permute-start | bytes 442376 | tf_op jit(solution)/shard_map/ppermute | solution.py:551
  28.8 12.1 %collective-permute-start.3 = (bf16[192,1152]{1,0:T(8,128)(2,1)S(1)}, bf16[192,1152]{1,0:T(8,128)(2,1)S(1)}, u32[]{:S(2)}, u32[]{:S(2)}) collective-permute-start(bf16[192,1152]{1,0:T(8,128)(2,1)S(1)} %stage.3), channel_id=1, source_target_pairs={{0,1},{1,0},{2,3},{3,2},{4,5},{5,4},{6,7},{7,6},{8,9},{9,8},{10,11... | collective-permute-start | bytes 1327112 | tf_op jit(solution)/shard_map/ppermute | solution.py:568
  31.6 5.1 %collective-permute-start.4 = (bf16[1,288,256]{2,1,0:T(8,128)(2,1)S(1)}, bf16[1,288,256]{2,1,0:T(8,128)(2,1)S(1)}, u32[]{:S(2)}, u32[]{:S(2)}) collective-permute-start(bf16[1,288,256]{2,1,0:T(8,128)(2,1)S(1)} %bitcast.16), channel_id=1, source_target_pairs={{0,8},{4,12},{8,0},{12,4},{16,24},{20,28},{24,16},{28,20},{1,9},{5... | collective-permute-start | bytes 442376 | tf_op jit(solution)/shard_map/ppermute | solution.py:566
  33.1 5.1 %collective-permute-start.5 = (bf16[1,288,256]{2,1,0:T(8,128)(2,1)S(1)}, bf16[1,288,256]{2,1,0:T(8,128)(2,1)S(1)}, u32[]{:S(2)}, u32[]{:S(2)}) collective-permute-start(bf16[1,288,256]{2,1,0:T(8,128)(2,1)S(1)} %bitcast.19), channel_id=1, source_target_pairs={{0,16},{4,20},{8,24},{12,28},{16,0},{20,4},{24,8},{28,12},{1,17},{... | collective-permute-start | bytes 442376 | tf_op jit(solution)/shard_map/ppermute | solution.py:567
  42.0 10.5 %collective-permute-start.6 = (bf16[192,1152]{1,0:T(8,128)(2,1)S(1)}, bf16[192,1152]{1,0:T(8,128)(2,1)S(1)}, u32[]{:S(2)}, u32[]{:S(2)}) collective-permute-start(bf16[192,1152]{1,0:T(8,128)(2,1)S(1)} %get-tuple-element.25), channel_id=1, source_target_pairs={{0,1},{1,0},{2,3},{3,2},{4,5},{5,4},{6,7},{7,6},{8,9},{9,8},{10,11... | collective-permute-start | bytes 1327112 | tf_op jit(solution)/shard_map/ppermute | solution.py:568
  43.8 6.7 %collective-permute-start.7 = (bf16[2,288,256]{2,1,0:T(8,128)(2,1)S(1)}, bf16[2,288,256]{2,1,0:T(8,128)(2,1)S(1)}, u32[]{:S(2)}, u32[]{:S(2)}) collective-permute-start(bf16[2,288,256]{2,1,0:T(8,128)(2,1)S(1)} %get-tuple-element.26.refs_0_), channel_id=1, source_target_pairs={{0,16},{4,20},{8,24},{12,28},{16,0},{20,4},{24,8},{28,12},{1,17},{... | collective-permute-start | bytes 884744 | tf_op jit(solution)/shard_map/ppermute | solution.py:566
  45.3 6.7 %collective-permute-start.8 = (bf16[2,288,256]{2,1,0:T(8,128)(2,1)S(1)}, bf16[2,288,256]{2,1,0:T(8,128)(2,1)S(1)}, u32[]{:S(2)}, u32[]{:S(2)}) collective-permute-start(bf16[2,288,256]{2,1,0:T(8,128)(2,1)S(1)} %get-tuple-element.27.refs_2_), channel_id=1, source_target_pairs={{0,8},{4,12},{8,0},{12,4},{16,24},{20,28},{24,16},{28,20},{1,9},{5... | collective-permute-start | bytes 884744 | tf_op jit(solution)/shard_map/ppermute | solution.py:567
  54.1 16.9 %collective-permute-start.10 = (bf16[4,288,256]{2,1,0:T(8,128)(2,1)}, bf16[4,288,256]{2,1,0:T(8,128)(2,1)}, u32[]{:S(2)}, u32[]{:S(2)}) collective-permute-start(bf16[4,288,256]{2,1,0:T(8,128)(2,1)} %get-tuple-element.31.own_ref), channel_id=1, source_target_pairs={{0,4},{4,0},{8,12},{12,8},{16,20},{20,16},{24,28},{28,24},{1,5},{5... | collective-permute-start | bytes 1769480 | tf_op jit(solution)/shard_map/ppermute | solution.py:566
  54.2 16.8 %collective-permute-start.11 = (bf16[4,288,256]{2,1,0:T(8,128)(2,1)}, bf16[4,288,256]{2,1,0:T(8,128)(2,1)S(1)}, u32[]{:S(2)}, u32[]{:S(2)}) collective-permute-start(bf16[4,288,256]{2,1,0:T(8,128)(2,1)} %get-tuple-element.32.own_ref), channel_id=1, source_target_pairs={{0,4},{4,0},{8,12},{12,8},{16,20},{20,16},{24,28},{28,24},{1,5},{5... | collective-permute-start | bytes 1769480 | tf_op jit(solution)/shard_map/ppermute | solution.py:567
  54.7 12.5 %collective-permute-start.9 = (bf16[192,1152]{1,0:T(8,128)(2,1)}, bf16[192,1152]{1,0:T(8,128)(2,1)}, u32[]{:S(2)}, u32[]{:S(2)}) collective-permute-start(bf16[192,1152]{1,0:T(8,128)(2,1)} %get-tuple-element.28), channel_id=1, source_target_pairs={{0,1},{1,0},{2,3},{3,2},{4,5},{5,4},{6,7},{7,6},{8,9},{9,8},{10,11... | collective-permute-start | bytes 1327112 | tf_op jit(solution)/shard_map/ppermute | solution.py:568
  76.0 20.3 %collective-permute-start.12 = (bf16[784,256]{1,0:T(8,128)(2,1)}, bf16[784,256]{1,0:T(8,128)(2,1)}, u32[]{:S(2)}, u32[]{:S(2)}) collective-permute-start(bf16[784,256]{1,0:T(8,128)(2,1)} %far.2.after_ref), channel_id=1, source_target_pairs={{0,2},{1,3},{2,0},{3,1},{4,6},{5,7},{6,4},{7,5},{8,10},{9,11},{10,... | collective-permute-start | bytes 1204232 | tf_op jit(solution)/shard_map/ppermute | solution.py:582
  100.0 5.0 %collective-permute-start.15 = (bf16[32,1152]{1,0:T(8,128)(2,1)S(1)}, bf16[32,1152]{1,0:T(8,128)(2,1)S(1)}, u32[]{:S(2)}, u32[]{:S(2)}) collective-permute-start(bf16[32,1152]{1,0:T(8,128)(2,1)S(1)} %get-tuple-element.40), channel_id=1, source_target_pairs={{0,3},{1,0},{2,1},{3,2},{4,7},{5,4},{6,5},{7,6},{8,11},{9,8},{10,9... | collective-permute-start | bytes 221192 | tf_op jit(solution)/shard_map/ppermute | solution.py:610
  102.3 7.2 %collective-permute-start.14 = (bf16[32,1152]{1,0:T(8,128)(2,1)S(1)}, bf16[32,1152]{1,0:T(8,128)(2,1)S(1)}, u32[]{:S(2)}, u32[]{:S(2)}) collective-permute-start(bf16[32,1152]{1,0:T(8,128)(2,1)S(1)} %get-tuple-element.41), channel_id=1, source_target_pairs={{0,2},{1,3},{2,0},{3,1},{4,6},{5,7},{6,4},{7,5},{8,10},{9,11},{10,... | collective-permute-start | bytes 221192 | tf_op jit(solution)/shard_map/ppermute | solution.py:610
  102.3 7.2 %collective-permute-start.13 = (bf16[32,1152]{1,0:T(8,128)(2,1)S(1)}, bf16[32,1152]{1,0:T(8,128)(2,1)S(1)}, u32[]{:S(2)}, u32[]{:S(2)}) collective-permute-start(bf16[32,1152]{1,0:T(8,128)(2,1)S(1)} %get-tuple-element.39), channel_id=1, source_target_pairs={{0,1},{1,2},{2,3},{3,0},{4,5},{5,6},{6,7},{7,4},{8,9},{9,10},{10,1... | collective-permute-start | bytes 221192 | tf_op jit(solution)/shard_map/ppermute | solution.py:610
  114.8 25.1 %collective-permute-start.17 = (bf16[784,256]{1,0:T(8,128)(2,1)S(1)}, bf16[784,256]{1,0:T(8,128)(2,1)S(1)}, u32[]{:S(2)}, u32[]{:S(2)}) collective-permute-start(bf16[784,256]{1,0:T(8,128)(2,1)S(1)} %get-tuple-element.34.rest_2_), channel_id=1, source_target_pairs={{0,8},{4,12},{1,9},{5,13},{2,10},{6,14},{3,11},{7,15},{16,24},{20,... | collective-permute-start | bytes 1204232 | tf_op jit(solution)/shard_map/ppermute | solution.py:599
  118.2 21.6 %collective-permute-start.18 = (bf16[784,256]{1,0:T(8,128)(2,1)S(1)}, bf16[784,256]{1,0:T(8,128)(2,1)S(1)}, u32[]{:S(2)}, u32[]{:S(2)}) collective-permute-start(bf16[784,256]{1,0:T(8,128)(2,1)S(1)} %get-tuple-element.34.rest_2_), channel_id=1, source_target_pairs={{0,4},{4,8},{8,12},{1,5},{5,9},{9,13},{2,6},{6,10},{10,14},{3,7},{... | collective-permute-start | bytes 1204232 | tf_op jit(solution)/shard_map/ppermute | solution.py:599
  119.7 20.1 %collective-permute-start.16 = (bf16[768,256]{1,0:T(8,128)(2,1)S(1)}, bf16[768,256]{1,0:T(8,128)(2,1)S(1)}, u32[]{:S(2)}, u32[]{:S(2)}) collective-permute-start(bf16[768,256]{1,0:T(8,128)(2,1)S(1)} %far.3.after_ref), channel_id=1, source_target_pairs={{0,2},{1,3},{2,0},{3,1},{4,6},{5,7},{6,4},{7,5},{8,10},{9,11},{10,... | collective-permute-start | bytes 1179656 | tf_op jit(solution)/shard_map/ppermute | solution.py:587
  144.2 15.5 %collective-permute-start.22 = (bf16[384,256]{1,0:T(8,128)(2,1)S(1)}, bf16[384,256]{1,0:T(8,128)(2,1)S(1)}, u32[]{:S(2)}, u32[]{:S(2)}) collective-permute-start(bf16[384,256]{1,0:T(8,128)(2,1)S(1)} %attend.2.after_ref.rest_0_), channel_id=1, source_target_pairs={{0,2},{1,3},{2,0},{3,1},{4,6},{5,7},{6,4},{7,5},{8,10},{9,11},{10,... | collective-permute-start | bytes 589832 | tf_op jit(solution)/shard_map/ppermute | solution.py:622
  149.0 15.1 %collective-permute-start.19 = (bf16[384,256]{1,0:T(8,128)(2,1)S(1)}, bf16[384,256]{1,0:T(8,128)(2,1)S(1)}, u32[]{:S(2)}, u32[]{:S(2)}) collective-permute-start(bf16[384,256]{1,0:T(8,128)(2,1)S(1)} %attend.3.rest_0_), channel_id=1, source_target_pairs={{0,2},{1,3},{2,0},{3,1},{4,6},{5,7},{6,4},{7,5},{8,10},{9,11},{10,... | collective-permute-start | bytes 589832 | tf_op jit(solution)/shard_map/ppermute | solution.py:622
  152.0 12.3 %collective-permute-start.23 = (bf16[384,256]{1,0:T(8,128)(2,1)S(1)}, bf16[384,256]{1,0:T(8,128)(2,1)S(1)}, u32[]{:S(2)}, u32[]{:S(2)}) collective-permute-start(bf16[384,256]{1,0:T(8,128)(2,1)S(1)} %attend.2.after_ref.rest_0_), channel_id=1, source_target_pairs={{0,1},{1,0},{2,3},{3,2},{4,5},{5,4},{6,7},{7,6},{8,9},{9,8},{10,11... | collective-permute-start | bytes 589832 | tf_op jit(solution)/shard_map/ppermute | solution.py:623
  159.8 8.7 %collective-permute-start.24 = (bf16[384,256]{1,0:T(8,128)(2,1)S(1)}, bf16[384,256]{1,0:T(8,128)(2,1)S(1)}, u32[]{:S(2)}, u32[]{:S(2)}) collective-permute-start(bf16[384,256]{1,0:T(8,128)(2,1)S(1)} %collective-permute-done.22.rest_1_), channel_id=1, source_target_pairs={{0,1},{1,0},{2,3},{3,2},{4,5},{5,4},{6,7},{7,6},{8,9},{9,8},{10,11... | collective-permute-start | bytes 589832 | tf_op jit(solution)/shard_map/ppermute | solution.py:624
  159.8 18.9 %collective-permute-start.20 = (bf16[384,256]{1,0:T(8,128)(2,1)S(1)}, bf16[384,256]{1,0:T(8,128)(2,1)S(1)}, u32[]{:S(2)}, u32[]{:S(2)}) collective-permute-start(bf16[384,256]{1,0:T(8,128)(2,1)S(1)} %attend.3.rest_0_), channel_id=1, source_target_pairs={{0,1},{1,0},{2,3},{3,2},{4,5},{5,4},{6,7},{7,6},{8,9},{9,8},{10,11... | collective-permute-start | bytes 589832 | tf_op jit(solution)/shard_map/ppermute | solution.py:623
  164.1 14.5 %collective-permute-start.21 = (bf16[384,256]{1,0:T(8,128)(2,1)S(1)}, bf16[384,256]{1,0:T(8,128)(2,1)S(1)}, u32[]{:S(2)}, u32[]{:S(2)}) collective-permute-start(bf16[384,256]{1,0:T(8,128)(2,1)S(1)} %collective-permute-done.19.rest_1_), channel_id=1, source_target_pairs={{0,1},{1,0},{2,3},{3,2},{4,5},{5,4},{6,7},{7,6},{8,9},{9,8},{10,11... | collective-permute-start | bytes 589832 | tf_op jit(solution)/shard_map/ppermute | solution.py:624
  174.8 9.2 %collective-permute-start.28 = (f32[1,384]{1,0:T(1,128)S(1)}, f32[1,384]{1,0:T(1,128)S(1)}, u32[]{:S(2)}, u32[]{:S(2)}) collective-permute-start(f32[1,384]{1,0:T(1,128)S(1)} %get-tuple-element.35.rest_4_.rest_0_), channel_id=1, source_target_pairs={{0,1},{1,2},{2,3},{3,0},{4,5},{5,6},{6,7},{7,4},{8,9},{9,10},{10,1... | collective-permute-start | bytes 4616 | tf_op jit(solution)/shard_map/ppermute | solution.py:633
  174.8 11.9 %collective-permute-start.29 = (f32[1,384]{1,0:T(1,128)S(1)}, f32[1,384]{1,0:T(1,128)S(1)}, u32[]{:S(2)}, u32[]{:S(2)}) collective-permute-start(f32[1,384]{1,0:T(1,128)S(1)} %get-tuple-element.35.rest_4_.rest_0_), channel_id=1, source_target_pairs={{0,2},{1,3},{2,0},{3,1},{4,6},{5,7},{6,4},{7,5},{8,10},{9,11},{10,... | collective-permute-start | bytes 4616 | tf_op jit(solution)/shard_map/ppermute | solution.py:633
  177.6 9.2 %collective-permute-start.30 = (f32[1,384]{1,0:T(1,128)S(1)}, f32[1,384]{1,0:T(1,128)S(1)}, u32[]{:S(2)}, u32[]{:S(2)}) collective-permute-start(f32[1,384]{1,0:T(1,128)S(1)} %get-tuple-element.35.rest_4_.rest_0_), channel_id=1, source_target_pairs={{0,3},{1,0},{2,1},{3,2},{4,7},{5,4},{6,5},{7,6},{8,11},{9,8},{10,9... | collective-permute-start | bytes 4616 | tf_op jit(solution)/shard_map/ppermute | solution.py:633
  181.7 7.0 %collective-permute-start.25 = (f32[1,384]{1,0:T(1,128)S(1)}, f32[1,384]{1,0:T(1,128)S(1)}, u32[]{:S(2)}, u32[]{:S(2)}) collective-permute-start(f32[1,384]{1,0:T(1,128)S(1)} %get-tuple-element.37.rest_0_), channel_id=1, source_target_pairs={{0,1},{1,2},{2,3},{3,0},{4,5},{5,6},{6,7},{7,4},{8,9},{9,10},{10,1... | collective-permute-start | bytes 4616 | tf_op jit(solution)/shard_map/ppermute | solution.py:633
  182.8 5.9 %collective-permute-start.26 = (f32[1,384]{1,0:T(1,128)S(1)}, f32[1,384]{1,0:T(1,128)S(1)}, u32[]{:S(2)}, u32[]{:S(2)}) collective-permute-start(f32[1,384]{1,0:T(1,128)S(1)} %get-tuple-element.37.rest_0_), channel_id=1, source_target_pairs={{0,2},{1,3},{2,0},{3,1},{4,6},{5,7},{6,4},{7,5},{8,10},{9,11},{10,... | collective-permute-start | bytes 4616 | tf_op jit(solution)/shard_map/ppermute | solution.py:633
  183.9 4.8 %collective-permute-start.27 = (f32[1,384]{1,0:T(1,128)S(1)}, f32[1,384]{1,0:T(1,128)S(1)}, u32[]{:S(2)}, u32[]{:S(2)}) collective-permute-start(f32[1,384]{1,0:T(1,128)S(1)} %get-tuple-element.37.rest_0_), channel_id=1, source_target_pairs={{0,3},{1,0},{2,1},{3,2},{4,7},{5,4},{6,5},{7,6},{8,11},{9,8},{10,9... | collective-permute-start | bytes 4616 | tf_op jit(solution)/shard_map/ppermute | solution.py:633
  (17 other events, 115.0 us)
Sparse Core Ops, SparseCore 0:
  110.4 28.2 all-gather.2

commit v7 on v6

--- a/solution.py
+++ b/solution.py
@@ -23,7 +23,9 @@
 F32, BF16 = jnp.float32, jnp.bfloat16
 ANY = pl.BlockSpec(memory_space=pl.ANY)
 HBM = pl.BlockSpec(memory_space=pltpu.HBM)
-PARAMS = pltpu.CompilerParams(vmem_limit_bytes=40 * 1024 * 1024)
+VMEM = pl.BlockSpec(memory_space=pltpu.VMEM)
+DOCUMENTS = 8
+PARAMS = pltpu.CompilerParams(vmem_limit_bytes=24 * 1024 * 1024)
 ALL_VMEM = pltpu.CompilerParams(vmem_limit_bytes=62 * 1024 * 1024)
 
 
@@ -118,6 +120,37 @@
     )(*[piece for pair in joined for piece in pair], tokens, *after)
 
 
+def cut_kernel(at_ref, o_ref, after_ref, *rest):
+    outs, sems = rest[:-1], rest[-1]
+    copies = []
+    for i, out in enumerate(outs):
+        rows = pl.ds(pl.multiple_of(at_ref[0], TAIL), out.shape[0])
+        columns = pl.ds(pl.multiple_of(at_ref[1 + i], LANES), out.shape[1])
+        copies.append(pltpu.make_async_copy(o_ref.at[rows, columns], out, sems.at[i]))
+    for copy in copies:
+        copy.start()
+    for copy in copies:
+        copy.wait()
+
+
+def cut_pieces(row, columns, o_weight, share, cols, after):
+    if cols % LANES:
+        return [lax.dynamic_slice(o_weight, (row, c), (share, cols)) for c in columns]
+    return pl.pallas_call(
+        cut_kernel,
+        out_shape=tuple(shape((share, cols), BF16) for _ in columns),
+        grid_spec=pltpu.PrefetchScalarGridSpec(
+            num_scalar_prefetch=1,
+            grid=(1,),
+            in_specs=[ANY, ANY],
+            out_specs=[VMEM for _ in columns],
+            scratch_shapes=[pltpu.SemaphoreType.DMA((len(columns),))],
+        ),
+        compiler_params=PARAMS,
+        name="cut",
+    )(jnp.stack([row] + columns), o_weight, after)
+
+
 def prep_kernel(src_ref, gain_ref, *rest, cuts):
     x_refs, (out_ref, sq_ref) = rest[:-2], rest[-2:]
     squares, at = [], 0
@@ -143,12 +176,8 @@
         grid_spec=pltpu.PrefetchScalarGridSpec(
             num_scalar_prefetch=1,
             grid=(1,),
-            in_specs=[pl.BlockSpec(gains.shape, lambda i, s: (0, 0, 0))]
-            + [pl.BlockSpec(piece.shape, lambda i, s: (0, 0)) for piece in pieces],
-            out_specs=[
-                pl.BlockSpec(dims, lambda i, s: (0, 0, 0)),
-                pl.BlockSpec((1, rows), lambda i, s: (0, 0)),
-            ],
+            in_specs=[VMEM] + [VMEM for _ in pieces],
+            out_specs=[VMEM, VMEM],
         ),
         compiler_params=PARAMS,
         name="prep",
@@ -214,14 +243,8 @@
         grid_spec=pltpu.PrefetchScalarGridSpec(
             num_scalar_prefetch=2,
             grid=(1,),
-            in_specs=[
-                pl.BlockSpec(x.shape, lambda i, p, s: (0, 0, 0)),
-                pl.BlockSpec((1, rows), lambda i, p, s: (0, 0)),
-                ANY,
-                ANY,
-            ]
-            + [ANY for _ in after],
-            out_specs=pl.BlockSpec((out_rows, width), lambda i, p, s: (0, 0)),
+            in_specs=[VMEM, VMEM, ANY, ANY] + [ANY for _ in after],
+            out_specs=VMEM,
             scratch_shapes=[
                 pltpu.VMEM((len(order) * share, width), BF16),
                 pltpu.SemaphoreType.DMA((len(order),)),
@@ -233,7 +256,7 @@
 
 
 def near_kernel(src_ref, x_ref, k_ref, v_ref, q_ref, after_ref, out_ref):
-    x = x_ref[0]
+    x = x_ref[pl.program_id(0)]
 
     @pl.when(pl.program_id(0) == 0)
     def _():
@@ -255,10 +278,10 @@
         grid_spec=pltpu.PrefetchScalarGridSpec(
             num_scalar_prefetch=1,
             grid=(count,),
-            in_specs=[pl.BlockSpec((1, chunk, cols), lambda i, s: (i, 0, 0))]
+            in_specs=[VMEM]
             + [pl.BlockSpec((cols, w), lambda i, s: (s[i], 0)) for w in widths]
             + [ANY],
-            out_specs=pl.BlockSpec((chunk, sum(widths)), lambda i, s: (0, 0)),
+            out_specs=VMEM,
         ),
         compiler_params=PARAMS,
         name="near",
@@ -268,37 +291,30 @@
 def keys_kernel(
     near_ref, far_ref, sq_ref, id_ref, cos_ref, sin_ref, after_ref, out_ref, sum_ref, *, model
 ):
-    chunk, width = near_ref.shape
-    tail = far_ref[chunk:, :].astype(F32)
-    total = sum(rows_of(tail, 2, chunk), sq_ref[...])
+    rows, width = near_ref.shape[0], far_ref.shape[1]
+    tail = far_ref[rows:, :].astype(F32)
+    total = sum(rows_of(tail, 2, rows), sq_ref[...])
     factor = to_column(lax.rsqrt(total / model + epsilon))
     sum_ref[...] = total
-    for c in range(0, width, HEAD_SIZE):
-        at = slice(c, c + HEAD_SIZE)
-        part = (near_ref[:, at] + far_ref[:chunk, at].astype(F32)) * factor
-        if c < width // 2:
-            part = rotate(part, cos_ref[...], sin_ref[...])
-        out_ref[:chunk, at] = part.astype(BF16)
-    out_ref[chunk:, :] = lines_of((id_ref[...].astype(F32),), width)
-
-
-def keys_values(near, far, sq, ids, cosine, sine, after, width, model):
-    chunk = near.shape[0]
-    whole = lambda i: (0, 0)
+    keys, values = slice(0, HEAD_SIZE), slice(HEAD_SIZE, 2 * HEAD_SIZE)
+    part = (near_ref[:, keys] + far_ref[:rows, keys].astype(F32)) * factor
+    part = rotate(part, cos_ref[...], sin_ref[...]).astype(BF16)
+    out_ref[: rows // 2, keys] = part[: rows // 2]
+    out_ref[: rows // 2, values] = part[rows // 2 :]
+    part = (near_ref[:, values] + far_ref[:rows, values].astype(F32)) * factor
+    part = part.T.astype(BF16)
+    for i, at in enumerate(range(0, rows, width)):
+        row = rows // 2 + i * HEAD_SIZE
+        out_ref[row : row + HEAD_SIZE, :] = part[:, at : at + width]
+    out_ref[rows:, :] = lines_of((id_ref[...].astype(F32),), width)
+
+
+def keys_values(near, far, sq, ids, cosine, sine, after, model):
     return pl.pallas_call(
         partial(keys_kernel, model=model),
-        out_shape=(shape((chunk + TAIL, width), BF16), shape((1, chunk), F32)),
-        grid=(1,),
-        in_specs=[
-            pl.BlockSpec((chunk, width), whole),
-            pl.BlockSpec(far.shape, whole),
-            pl.BlockSpec((1, chunk), whole),
-            pl.BlockSpec((1, chunk), whole),
-            pl.BlockSpec((chunk, HEAD_SIZE), whole),
-            pl.BlockSpec((chunk, HEAD_SIZE), whole),
-            ANY,
-        ],
-        out_specs=[pl.BlockSpec((chunk + TAIL, width), whole), pl.BlockSpec((1, chunk), whole)],
+        out_shape=(shape(far.shape, BF16), shape(sq.shape, F32)),
+        in_specs=[VMEM] * 6 + [ANY],
+        out_specs=[VMEM, VMEM],
         compiler_params=PARAMS,
         name="keys",
     )(near, far, sq, ids, cosine, sine, after)
@@ -307,20 +323,29 @@
 def attention_kernel(
     seq_ref, near_ref, far_ref, sum_ref, cos_ref, sin_ref, id_ref, after_ref, *rest, back, offset, model
 ):
-    kv_refs, (out_ref, k_scr, vt_scr, id_scr) = rest[:-4], rest[-4:]
-    part_rows = kv_refs[0].shape[0] - TAIL
+    kv_refs, (out_ref, k_scr, vt_scr, count_scr) = rest[:-4], rest[-4:]
+    part_rows, message = kv_refs[0].shape[0] - TAIL, kv_refs[0].shape[1]
     group = near_ref.shape[1] // HEAD_SIZE
     tile = pl.program_id(0)
 
     @pl.when(tile == 0)
     def _():
+        counts = [jnp.zeros((1, 1), F32) for _ in range(DOCUMENTS)]
         for b, kv_ref in enumerate(kv_refs):
-            at = slice(b * part_rows, (b + 1) * part_rows)
-            k_scr[at, :] = kv_ref[:part_rows, :HEAD_SIZE]
-            vt_scr[:, at] = kv_ref[:part_rows, HEAD_SIZE:].astype(F32).T.astype(BF16)
+            row, half = b * part_rows, part_rows // 2
+            k_scr[row : row + half, :] = kv_ref[:half, :HEAD_SIZE]
+            k_scr[row + half : row + part_rows, :] = kv_ref[:half, HEAD_SIZE:]
+            for i, at in enumerate(range(0, part_rows, message)):
+                first = half + i * HEAD_SIZE
+                vt_scr[:, row + at : row + at + message] = kv_ref[first : first + HEAD_SIZE, :]
             (ids,) = rows_of(kv_ref[part_rows:, :].astype(F32), 1, part_rows)
             exists = b >= back - seq_ref[0]
-            id_scr[at, :] = to_column(jnp.where(exists, ids, -1.0))
+            ids = jnp.where(exists, ids, -1.0)
+            for d in range(DOCUMENTS):
+                below = (ids < d).astype(F32)
+                counts[d] = counts[d] + jnp.sum(below, axis=1, keepdims=True)
+        for d in range(DOCUMENTS):
+            count_scr[d : d + 1, :] = jnp.broadcast_to(counts[d], (1, LANES))
 
     scale = query_scale * math.log2(math.e)
     factor = to_column(lax.rsqrt(sum_ref[...] / model + epsilon) * scale)
@@ -332,8 +357,10 @@
     q2 = jnp.concatenate(heads, axis=0)
     width = group * Q_TILE
 
-    before = (id_scr[...] < id_ref[...].astype(F32)).astype(F32)
-    start = jnp.sum(before, axis=0, keepdims=True).astype(jnp.int32)
+    start = jnp.zeros((1, Q_TILE), F32)
+    for d in range(DOCUMENTS):
+        start = jnp.where(id_ref[...] == d, count_scr[d : d + 1, :], start)
+    start = start.astype(jnp.int32)
     low = jnp.min(start) // K_TILE
     start = jnp.concatenate([start] * group, axis=1)
     first = back * part_rows + offset + tile * Q_TILE
@@ -404,12 +431,12 @@
                 pl.BlockSpec((1, Q_TILE), lambda i, s: (0, c * tiles + i)),
                 ANY,
             ]
-            + [pl.BlockSpec(b.shape, lambda i, s: (0, 0)) for b in blocks],
+            + [VMEM for _ in blocks],
             out_specs=pl.BlockSpec((Q_TILE, width), lambda i, s: (i, 0)),
             scratch_shapes=[
                 pltpu.VMEM((keys, HEAD_SIZE), BF16),
                 pltpu.VMEM((HEAD_SIZE, keys), BF16),
-                pltpu.VMEM((keys, LANES), F32),
+                pltpu.VMEM((DOCUMENTS, LANES), F32),
             ],
         ),
         compiler_params=PARAMS,
@@ -568,6 +595,12 @@
         received.append(lax.ppermute(cut, "tensor", ring))
         order_kv = order_kv + [k ^ mask_kv for k in order_kv]
         order_q = order_q + [k ^ mask_q for k in order_q]
+    o_share = o_weight.shape[0] // plane
+    columns = [(z + k) % nz * cols for k in range(1, nz)]
+    pieces = cut_pieces(in_plane * o_share, columns, o_weight, o_share, cols, own_q)
+    moved = [lax.ppermute(p, "tensor", turn(k + 1)) for k, p in enumerate(pieces)]
+    moved = jnp.stack(moved)
+    gathered_o = lax.all_gather(moved, PLANE)
     far_kv, far_q = (order_kv, own_kv, far_kv), (order_q, own_q, far_q)
 
     sources = (within + half - jnp.arange(half, dtype=jnp.int32)) % half
@@ -578,19 +611,16 @@
     x, sq = prep(side * half + sources, gains, blocks)
 
     place = jnp.reshape(in_plane, (1,))
-    sent_kv = far_product(place, sources, x, sq, far_kv, True, [far_q[2]])
+    sent_kv = far_product(place, sources, x, sq, far_kv, True, [far_q[2], moved])
     got_kv = lax.ppermute(sent_kv, "tensor", swap)
     weights = (k_weight, value_weight, q_weight)
-    near = near_product(side * half + sources, x, weights, sent_kv)
-
-    sent_q = far_product(place, sources, x, sq, far_q, False, [near])
+
+    sent_q = far_product(place, sources, x, sq, far_q, False, [sent_kv])
     got_q = lax.ppermute(sent_q, "tensor", swap)
+    near = near_product(side * half + sources, x, weights, sent_q)
     cosine, sine = rotation_table(seq * rows + jnp.arange(rows, dtype=jnp.int32))
     ids = seg_ids[None, :]
-    kv_width = k_weight.shape[1] + value_weight.shape[1]
-    own_kv, sums = keys_values(
-        near, got_kv, sq, ids, cosine, sine, sent_q, kv_width, model
-    )
+    own_kv, sums = keys_values(near, got_kv, sq, ids, cosine, sine, sent_q, model)
 
     back = -(-(nseq * rows // 2 - 1) // rows)
     kv_blocks = [own_kv]
@@ -598,21 +628,9 @@
         earlier = [(i, i + k) for i in range(nseq - k)]
         kv_blocks.insert(0, lax.ppermute(own_kv, "seq", earlier))
 
-    o_share = o_weight.shape[0] // plane
-    last = got_kv[0, 0] + sent_q[0, 0]
-    wait = (last != last).astype(jnp.int32)
-    moved = []
-    for k in range(1, nz):
-        target = (z + k) % nz
-        piece = lax.dynamic_slice(
-            o_weight, (in_plane * o_share + wait, target * cols), (o_share, cols)
-        )
-        moved.append(lax.ppermute(piece, "tensor", turn(k)))
-    gathered_o = lax.all_gather(jnp.stack(moved), PLANE)
-
     out = None
     seq_at = jnp.reshape(seq, (1,))
-    context, own_sq = place, place
+    context, own_sq = gathered_o, place
     for c in range(CHUNKS):
         context = attend(
             seq_at, near, got_q, sums, cosine, sine, ids, context, kv_blocks, c, model

time: 198 us -> 203 us (1.025)
  the two profiles are of different devices: /device:TPU:0 before, /device:TPU:2 now
where the time goes in v7:
time: 203 us; the launch traced here: 200 us
  waiting for transfers between devices  84.7 us (42%)
  Pallas kernels  40.3 us (20%)
  starting transfers between devices  35.7 us (18%)
  local copies, waits for them, and re-layouts  23 us (11%)
  between operations  13.8 us (7%)
  other arithmetic  2.64 us (1%)
    unnamed x80, local copies, waits for them, and re-layouts  23 us
    ppermute x1, waiting for transfers between devices, per_device(): got_q = lax.ppermute(sent_q, 'tensor', swap)  17.2 us
    ppermute x3, waiting for transfers between devices, per_device(): received.append(lax.ppermute(cut, 'tensor', ring))  15.9 us
    ppermute x1, waiting for transfers between devices, per_device(): own_kv = lax.ppermute(packed_kv, 'tensor', swap)[None]  11.1 us
    pallas_call x2, Pallas kernels, attend(): pl.pallas_call(partial(attention_kernel, back=back, offset=c * rows, mode...  10.6 us
    ppermute x1, waiting for transfers between devices, per_device(): got_kv = lax.ppermute(sent_kv, 'tensor', swap)  9.88 us
    ppermute x2, waiting for transfers between devices, per_device(): opposite = lax.ppermute(context, 'tensor', swap)  9.8 us
    ppermute x6, starting transfers between devices, per_device(): squares += [lax.ppermute(own_sq, 'tensor', turn(k)) for k in range(1, nz)]  8.87 us
  transfers between devices with their start and end apart: 32, of which 17 were waited for; matrix products, arithmetic and copies ran while one was open for 1% of the time, Pallas kernels for 14%

profile of v7, /device:TPU:2, one launch (start us, length us, event | category | flops | bytes accessed | tf_op | source)
XLA Modules:
  0.0 200.2 jit_solution(2541453335384091687)
XLA Ops:
  6.5 2.2 %pack.1 = (bf16[288,256]{1,0:T(8,128)(2,1)}, bf16[288,256]{1,0:T(8,128)(2,1)}, bf16[192,1152]{1,0:T(8,128)(2,1)}) custom-call(s32[1]{0:T(128)} %bitcast.7.at_ref, bf16[4608,256]{1,0:T(8,128)(2,1)} %q_ref.3, bf16[4608,128]{1,0:T(8,128)(2,1)} %k_ref.3, bf16[4608,128]{1,0:T(8,128)(2,1)} %v_ref.3, bf16[768,1152]{1,0:T(8,128)(2,1)} %token_ref.3), custom_call_target="tpu_custom_call" | custom-call | tf_op jit(solution)/shard_map/pack/pallas_call | solution.py:74
  10.4 2.6 %collective-permute-start = (bf16[288,256]{1,0:T(8,128)(2,1)}, bf16[288,256]{1,0:T(8,128)(2,1)S(1)}, u32[]{:S(2)}, u32[]{:S(2)}) collective-permute-start(bf16[288,256]{1,0:T(8,128)(2,1)} %get-tuple-element.25), channel_id=1, source_target_pairs={{0,2},{1,3},{2,0},{3,1},{4,6},{5,7},{6,4},{7,5},{8,10},{9,11},{10,... | collective-permute-start | bytes 442376 | tf_op jit(solution)/shard_map/ppermute | solution.py:577
  13.3 11.1 %collective-permute-done = bf16[288,256]{1,0:T(8,128)(2,1)S(1)} collective-permute-done((bf16[288,256]{1,0:T(8,128)(2,1)}, bf16[288,256]{1,0:T(8,128)(2,1)S(1)}, u32[]{:S(2)}, u32[]{:S(2)}) %collective-permute-start) | collective-permute-done | bytes 147488 | tf_op jit(solution)/shard_map/ppermute | solution.py:577
  24.4 2.0 %collective-permute-done.2 = bf16[288,256]{1,0:T(8,128)(2,1)S(1)} collective-permute-done((bf16[288,256]{1,0:T(8,128)(2,1)}, bf16[288,256]{1,0:T(8,128)(2,1)S(1)}, u32[]{:S(2)}, u32[]{:S(2)}) %collective-permute-start.2) | collective-permute-done | bytes 147488 | tf_op jit(solution)/shard_map/ppermute | solution.py:578
  27.5 2.7 %collective-permute-start.5 = (bf16[192,1152]{1,0:T(8,128)(2,1)S(1)}, bf16[192,1152]{1,0:T(8,128)(2,1)S(1)}, u32[]{:S(2)}, u32[]{:S(2)}) collective-permute-start(bf16[192,1152]{1,0:T(8,128)(2,1)S(1)} %stage.3), channel_id=1, source_target_pairs={{0,1},{1,0},{2,3},{3,2},{4,5},{5,4},{6,7},{7,6},{8,9},{9,8},{10,11... | collective-permute-start | bytes 1327112 | tf_op jit(solution)/shard_map/ppermute | solution.py:595
  32.2 3.1 %collective-permute-done.1.refs_1_ = bf16[1,288,256]{2,1,0:T(8,128)(2,1)S(1)} collective-permute-done((bf16[1,288,256]{2,1,0:T(8,128)(2,1)S(1)}, bf16[1,288,256]{2,1,0:T(8,128)(2,1)S(1)}, u32[]{:S(2)}, u32[]{:S(2)}) %collective-permute-start.1) | collective-permute-done | bytes 147488 | tf_op jit(solution)/shard_map/ppermute | solution.py:593
  35.8 3.6 %collective-permute-done.5.refs_5_.rest_2_ = bf16[192,1152]{1,0:T(8,128)(2,1)S(1)} collective-permute-done((bf16[192,1152]{1,0:T(8,128)(2,1)S(1)}, bf16[192,1152]{1,0:T(8,128)(2,1)S(1)}, u32[]{:S(2)}, u32[]{:S(2)}) %collective-permute-start.5) | collective-permute-done | bytes 442400 | tf_op jit(solution)/shard_map/ppermute | solution.py:595
  41.3 1.8 collective-permute-start.8
  45.2 4.6 %collective-permute-done.6.refs_1_ = bf16[2,288,256]{2,1,0:T(8,128)(2,1)S(1)} collective-permute-done((bf16[2,288,256]{2,1,0:T(8,128)(2,1)S(1)}, bf16[2,288,256]{2,1,0:T(8,128)(2,1)S(1)}, u32[]{:S(2)}, u32[]{:S(2)}) %collective-permute-start.6) | collective-permute-done | bytes 294944 | tf_op jit(solution)/shard_map/ppermute | solution.py:593
  56.1 2.4 %collective-permute-start.11 = (bf16[32,1152]{1,0:T(8,128)(2,1)S(1)}, bf16[32,1152]{1,0:T(8,128)(2,1)S(1)}, u32[]{:S(2)}, u32[]{:S(2)}) collective-permute-start(bf16[32,1152]{1,0:T(8,128)(2,1)S(1)} %get-tuple-element.34), channel_id=1, source_target_pairs={{0,3},{1,0},{2,1},{3,2},{4,7},{5,4},{6,5},{7,6},{8,11},{9,8},{10,9... | collective-permute-start | bytes 221192 | tf_op jit(solution)/shard_map/ppermute | solution.py:601
  61.3 2.5 %collective-permute-done.10 = bf16[32,1152]{1,0:T(8,128)(2,1)S(1)} collective-permute-done((bf16[32,1152]{1,0:T(8,128)(2,1)S(1)}, bf16[32,1152]{1,0:T(8,128)(2,1)S(1)}, u32[]{:S(2)}, u32[]{:S(2)}) %collective-permute-start.10) | collective-permute-done | bytes 73760 | tf_op jit(solution)/shard_map/ppermute | solution.py:601
  66.5 12.3 %collective-permute-done.12.rest_4_ = bf16[192,1152]{1,0:T(8,128)(2,1)S(1)} collective-permute-done((bf16[192,1152]{1,0:T(8,128)(2,1)}, bf16[192,1152]{1,0:T(8,128)(2,1)S(1)}, u32[]{:S(2)}, u32[]{:S(2)}) %collective-permute-start.12) | collective-permute-done | bytes 442400 | tf_op jit(solution)/shard_map/ppermute | solution.py:595
  81.8 1.8 prep.1
  83.7 3.7 %far.2.rest_0_ = bf16[784,256]{1,0:T(8,128)(2,1)S(1)} custom-call(s32[1]{0:T(128)} %bitcast.15.place_ref.rest_4_, s32[2]{0:T(128)S(1)} %and_select_fusion.src_ref, bf16[2,768,1152]{2,1,0:T(8,128)(2,1)S(1)} %get-tuple-element.36.x_ref, f32[1,768]{1,0:T(1,128)S(1)} %get-tuple-element.37.sq_ref, bf16[4,288,256]{2,1,0:T(8,128)(2,1)S(1)} %copy-done.27, ...), custom_call_target="tpu_custom_call" | custom-call | tf_op jit(solution)/shard_map/far/pallas_call | solution.py:240
  90.1 3.3 %far.3.after_ref = bf16[768,256]{1,0:T(8,128)(2,1)S(1)} custom-call(s32[1]{0:T(128)} %bitcast.15.place_ref.rest_4_, s32[2]{0:T(128)S(1)} %and_select_fusion.src_ref, bf16[2,768,1152]{2,1,0:T(8,128)(2,1)S(1)} %get-tuple-element.36.x_ref, f32[1,768]{1,0:T(1,128)S(1)} %get-tuple-element.37.sq_ref, bf16[4,288,256]{2,1,0:T(8,128)(2,1)S(1)} %copy-done.12, ...), custom_call_target="tpu_custom_call" | custom-call | tf_op jit(solution)/shard_map/far/pallas_call | solution.py:240
  93.4 4.1 %near.1.near_ref = f32[768,512]{1,0:T(8,128)S(1)} custom-call(s32[2]{0:T(128)S(1)} %broadcast_add_fusion.src_ref, bf16[2,768,1152]{2,1,0:T(8,128)(2,1)S(1)} %get-tuple-element.36.x_ref, bf16[4608,128]{1,0:T(8,128)(2,1)S(1)} %copy-done.9, bf16[4608,128]{1,0:T(8,128)(2,1)S(1)} %copy-done.10, bf16[4608,256]{1,0:T(8,128)(2,1)S(1)} %copy-done.8, ...), custom_call_target="tpu_custom_call" | custom-call | tf_op jit(solution)/shard_map/near/pallas_call | solution.py:275
  97.5 9.9 %collective-permute-done.16.far_ref = bf16[784,256]{1,0:T(8,128)(2,1)S(1)} collective-permute-done((bf16[784,256]{1,0:T(8,128)(2,1)S(1)}, bf16[784,256]{1,0:T(8,128)(2,1)S(1)}, u32[]{:S(2)}, u32[]{:S(2)}) %collective-permute-start.16) | collective-permute-done | bytes 401440 | tf_op jit(solution)/shard_map/ppermute | solution.py:615
  110.3 1.9 collective-permute-start.18
  112.3 17.2 %collective-permute-done.15.far_ref = bf16[768,256]{1,0:T(8,128)(2,1)S(1)} collective-permute-done((bf16[768,256]{1,0:T(8,128)(2,1)S(1)}, bf16[768,256]{1,0:T(8,128)(2,1)S(1)}, u32[]{:S(2)}, u32[]{:S(2)}) %collective-permute-start.15) | collective-permute-done | bytes 393248 | tf_op jit(solution)/shard_map/ppermute | solution.py:619
  137.7 4.7 %attend.2.after_ref.rest_0_ = bf16[384,256]{1,0:T(8,128)(2,1)S(1)} custom-call(s32[1]{0:T(128)} %bitcast.14.seq_ref, f32[768,512]{1,0:T(8,128)S(1)} %copy-done.2, bf16[768,256]{1,0:T(8,128)(2,1)S(1)} %copy-done.25, f32[1,768]{1,0:T(1,128)S(1)} %get-tuple-element.39.sum_ref, f32[768,128]{1,0:T(8,128)S(1)} %get-tuple-element.48.cos_ref, ...), custom_call_target="tpu_custom_call" | custom-call | flops 905969664 | bytes 2359296 | tf_op jit(solution)/shard_map/attend/pallas_call | solution.py:419
  142.5 5.9 %attend.3.rest_0_ = bf16[384,256]{1,0:T(8,128)(2,1)S(1)} custom-call(s32[1]{0:T(128)} %bitcast.14.seq_ref, f32[768,512]{1,0:T(8,128)S(1)} %copy-done.2, bf16[768,256]{1,0:T(8,128)(2,1)S(1)} %copy-done.25, f32[1,768]{1,0:T(1,128)S(1)} %get-tuple-element.39.sum_ref, f32[768,128]{1,0:T(8,128)S(1)} %get-tuple-element.48.cos_ref, ...), custom_call_target="tpu_custom_call" | custom-call | flops 905969664 | bytes 2359296 | tf_op jit(solution)/shard_map/attend/pallas_call | solution.py:419
  148.4 2.9 %collective-permute-start.19 = (bf16[384,256]{1,0:T(8,128)(2,1)S(1)}, bf16[384,256]{1,0:T(8,128)(2,1)S(1)}, u32[]{:S(2)}, u32[]{:S(2)}) collective-permute-start(bf16[384,256]{1,0:T(8,128)(2,1)S(1)} %attend.3.rest_0_), channel_id=1, source_target_pairs={{0,2},{1,3},{2,0},{3,1},{4,6},{5,7},{6,4},{7,5},{8,10},{9,11},{10,... | collective-permute-start | bytes 589832 | tf_op jit(solution)/shard_map/ppermute | solution.py:640
  151.7 7.2 %collective-permute-done.22.rest_1_ = bf16[384,256]{1,0:T(8,128)(2,1)} collective-permute-done((bf16[384,256]{1,0:T(8,128)(2,1)S(1)}, bf16[384,256]{1,0:T(8,128)(2,1)}, u32[]{:S(2)}, u32[]{:S(2)}) %collective-permute-start.22) | collective-permute-done | bytes 196640 | tf_op jit(solution)/shard_map/ppermute | solution.py:640
  158.8 2.1 %collective-permute-start.20 = (bf16[384,256]{1,0:T(8,128)(2,1)S(1)}, bf16[384,256]{1,0:T(8,128)(2,1)S(1)}, u32[]{:S(2)}, u32[]{:S(2)}) collective-permute-start(bf16[384,256]{1,0:T(8,128)(2,1)S(1)} %attend.3.rest_0_), channel_id=1, source_target_pairs={{0,1},{1,0},{2,3},{3,2},{4,5},{5,4},{6,7},{7,6},{8,9},{9,8},{10,11... | collective-permute-start | bytes 589832 | tf_op jit(solution)/shard_map/ppermute | solution.py:641
  160.9 2.6 %collective-permute-done.19.rest_1_ = bf16[384,256]{1,0:T(8,128)(2,1)S(1)} collective-permute-done((bf16[384,256]{1,0:T(8,128)(2,1)S(1)}, bf16[384,256]{1,0:T(8,128)(2,1)S(1)}, u32[]{:S(2)}, u32[]{:S(2)}) %collective-permute-start.19) | collective-permute-done | bytes 196640 | tf_op jit(solution)/shard_map/ppermute | solution.py:640
  164.3 3.5 %collective-permute-done.24.rest_3_ = bf16[384,256]{1,0:T(8,128)(2,1)S(1)} collective-permute-done((bf16[384,256]{1,0:T(8,128)(2,1)}, bf16[384,256]{1,0:T(8,128)(2,1)S(1)}, u32[]{:S(2)}, u32[]{:S(2)}) %collective-permute-start.24) | collective-permute-done | bytes 196640 | tf_op jit(solution)/shard_map/ppermute | solution.py:642
  173.5 4.0 %output.2 = (f32[384,1152]{1,0:T(8,128)S(1)}, f32[1,384]{1,0:T(1,128)S(1)}) custom-call(s32[4]{0:T(128)S(1)} %pad_add_fusion.at_ref, bf16[256,4608]{1,0:T(8,128)(2,1)S(1)} %copy-done.4, bf16[8,3,32,1152]{3,2,1,0:T(8,128)(2,1)S(1)} %bitcast.17, bf16[384,256]{1,0:T(8,128)(2,1)S(1)} %attend.2.after_ref.rest_0_, ...), custom_call_target="tpu_custom_call" | custom-call | tf_op jit(solution)/shard_map/output/pallas_call | solution.py:485
  177.5 2.4 %collective-permute-start.29 = (f32[1,384]{1,0:T(1,128)S(1)}, f32[1,384]{1,0:T(1,128)S(1)}, u32[]{:S(2)}, u32[]{:S(2)}) collective-permute-start(f32[1,384]{1,0:T(1,128)S(1)} %get-tuple-element.41.rest_4_.rest_0_), channel_id=1, source_target_pairs={{0,2},{1,3},{2,0},{3,1},{4,6},{5,7},{6,4},{7,5},{8,10},{9,11},{10,... | collective-permute-start | bytes 4616 | tf_op jit(solution)/shard_map/ppermute | solution.py:651
  181.3 3.1 %output.3 = (f32[384,1152]{1,0:T(8,128)S(1)}, f32[1,384]{1,0:T(1,128)S(1)}) custom-call(s32[4]{0:T(128)S(1)} %pad_add_fusion.at_ref, bf16[256,4608]{1,0:T(8,128)(2,1)S(1)} %copy-done.4, bf16[8,3,32,1152]{3,2,1,0:T(8,128)(2,1)S(1)} %bitcast.18, bf16[384,256]{1,0:T(8,128)(2,1)S(1)} %attend.3.rest_0_, bf16[384,256]{1,0:T(8,128)(2,1)S(1)} %collective-permute-done.19.rest_1_, ...), custom_call_target="tpu_custom_call" | custom-call | tf_op jit(solution)/shard_map/output/pallas_call | solution.py:485
  186.6 2.8 %collective-permute-start.27 = (f32[1,384]{1,0:T(1,128)S(1)}, f32[1,384]{1,0:T(1,128)S(1)}, u32[]{:S(2)}, u32[]{:S(2)}) collective-permute-start(f32[1,384]{1,0:T(1,128)S(1)} %get-tuple-element.43.rest_0_), channel_id=1, source_target_pairs={{0,3},{1,0},{2,1},{3,2},{4,7},{5,4},{6,5},{7,6},{8,11},{9,8},{10,9... | collective-permute-start | bytes 4616 | tf_op jit(solution)/shard_map/ppermute | solution.py:651
  189.5 1.9 finish.2.rest_4_
  191.4 1.9 finish.3
  (141 shorter events, 48.5 us)
Async XLA Ops:
  6.5 125.3 %all-gather.3.cloned.1.call-start = ((), (), s32[]{:S(2)}) async-start(), calls=%async_computation | async-start | bytes 1990656 | tf_op jit(solution)/shard_map/all_gather | solution.py:603
  8.7 18.5 %collective-permute-start.4 = (bf16[192,1152]{1,0:T(8,128)(2,1)}, bf16[192,1152]{1,0:T(8,128)(2,1)S(1)}, u32[]{:S(2)}, u32[]{:S(2)}) collective-permute-start(bf16[192,1152]{1,0:T(8,128)(2,1)} %get-tuple-element.27), channel_id=1, source_target_pairs={{0,1},{1,0},{2,3},{3,2},{4,5},{5,4},{6,7},{7,6},{8,9},{9,8},{10,11... | collective-permute-start | bytes 1327112 | tf_op jit(solution)/shard_map/ppermute | solution.py:579
  10.4 14.0 %collective-permute-start = (bf16[288,256]{1,0:T(8,128)(2,1)}, bf16[288,256]{1,0:T(8,128)(2,1)S(1)}, u32[]{:S(2)}, u32[]{:S(2)}) collective-permute-start(bf16[288,256]{1,0:T(8,128)(2,1)} %get-tuple-element.25), channel_id=1, source_target_pairs={{0,2},{1,3},{2,0},{3,1},{4,6},{5,7},{6,4},{7,5},{8,10},{9,11},{10,... | collective-permute-start | bytes 442376 | tf_op jit(solution)/shard_map/ppermute | solution.py:577
  13.0 13.5 %collective-permute-start.2 = (bf16[288,256]{1,0:T(8,128)(2,1)}, bf16[288,256]{1,0:T(8,128)(2,1)S(1)}, u32[]{:S(2)}, u32[]{:S(2)}) collective-permute-start(bf16[288,256]{1,0:T(8,128)(2,1)} %get-tuple-element.26), channel_id=1, source_target_pairs={{0,2},{1,3},{2,0},{3,1},{4,6},{5,7},{6,4},{7,5},{8,10},{9,11},{10,... | collective-permute-start | bytes 442376 | tf_op jit(solution)/shard_map/ppermute | solution.py:578
  27.5 12.0 %collective-permute-start.5 = (bf16[192,1152]{1,0:T(8,128)(2,1)S(1)}, bf16[192,1152]{1,0:T(8,128)(2,1)S(1)}, u32[]{:S(2)}, u32[]{:S(2)}) collective-permute-start(bf16[192,1152]{1,0:T(8,128)(2,1)S(1)} %stage.3), channel_id=1, source_target_pairs={{0,1},{1,0},{2,3},{3,2},{4,5},{5,4},{6,7},{7,6},{8,9},{9,8},{10,11... | collective-permute-start | bytes 1327112 | tf_op jit(solution)/shard_map/ppermute | solution.py:595
  30.2 5.1 %collective-permute-start.1 = (bf16[1,288,256]{2,1,0:T(8,128)(2,1)S(1)}, bf16[1,288,256]{2,1,0:T(8,128)(2,1)S(1)}, u32[]{:S(2)}, u32[]{:S(2)}) collective-permute-start(bf16[1,288,256]{2,1,0:T(8,128)(2,1)S(1)} %bitcast.20), channel_id=1, source_target_pairs={{0,8},{4,12},{8,0},{12,4},{16,24},{20,28},{24,16},{28,20},{1,9},{5... | collective-permute-start | bytes 442376 | tf_op jit(solution)/shard_map/ppermute | solution.py:593
  30.7 5.1 %collective-permute-start.3 = (bf16[1,288,256]{2,1,0:T(8,128)(2,1)S(1)}, bf16[1,288,256]{2,1,0:T(8,128)(2,1)S(1)}, u32[]{:S(2)}, u32[]{:S(2)}) collective-permute-start(bf16[1,288,256]{2,1,0:T(8,128)(2,1)S(1)} %bitcast.23), channel_id=1, source_target_pairs={{0,16},{4,20},{8,24},{12,28},{16,0},{20,4},{24,8},{28,12},{1,17},{... | collective-permute-start | bytes 442376 | tf_op jit(solution)/shard_map/ppermute | solution.py:594
  41.3 10.7 %collective-permute-start.8 = (bf16[192,1152]{1,0:T(8,128)(2,1)}, bf16[192,1152]{1,0:T(8,128)(2,1)S(1)}, u32[]{:S(2)}, u32[]{:S(2)}) collective-permute-start(bf16[192,1152]{1,0:T(8,128)(2,1)} %get-tuple-element.30), channel_id=1, source_target_pairs={{0,1},{1,0},{2,3},{3,2},{4,5},{5,4},{6,7},{7,6},{8,9},{9,8},{10,11... | collective-permute-start | bytes 1327112 | tf_op jit(solution)/shard_map/ppermute | solution.py:595
  43.1 6.7 %collective-permute-start.6 = (bf16[2,288,256]{2,1,0:T(8,128)(2,1)S(1)}, bf16[2,288,256]{2,1,0:T(8,128)(2,1)S(1)}, u32[]{:S(2)}, u32[]{:S(2)}) collective-permute-start(bf16[2,288,256]{2,1,0:T(8,128)(2,1)S(1)} %get-tuple-element.28.refs_0_), channel_id=1, source_target_pairs={{0,16},{4,20},{8,24},{12,28},{16,0},{20,4},{24,8},{28,12},{1,17},{... | collective-permute-start | bytes 884744 | tf_op jit(solution)/shard_map/ppermute | solution.py:593
  44.6 6.7 %collective-permute-start.7 = (bf16[2,288,256]{2,1,0:T(8,128)(2,1)S(1)}, bf16[2,288,256]{2,1,0:T(8,128)(2,1)S(1)}, u32[]{:S(2)}, u32[]{:S(2)}) collective-permute-start(bf16[2,288,256]{2,1,0:T(8,128)(2,1)S(1)} %get-tuple-element.29.refs_2_), channel_id=1, source_target_pairs={{0,8},{4,12},{8,0},{12,4},{16,24},{20,28},{24,16},{28,20},{1,9},{5... | collective-permute-start | bytes 884744 | tf_op jit(solution)/shard_map/ppermute | solution.py:594
  56.1 5.2 %collective-permute-start.11 = (bf16[32,1152]{1,0:T(8,128)(2,1)S(1)}, bf16[32,1152]{1,0:T(8,128)(2,1)S(1)}, u32[]{:S(2)}, u32[]{:S(2)}) collective-permute-start(bf16[32,1152]{1,0:T(8,128)(2,1)S(1)} %get-tuple-element.34), channel_id=1, source_target_pairs={{0,3},{1,0},{2,1},{3,2},{4,7},{5,4},{6,5},{7,6},{8,11},{9,8},{10,9... | collective-permute-start | bytes 221192 | tf_op jit(solution)/shard_map/ppermute | solution.py:601
  58.5 5.3 %collective-permute-start.10 = (bf16[32,1152]{1,0:T(8,128)(2,1)S(1)}, bf16[32,1152]{1,0:T(8,128)(2,1)S(1)}, u32[]{:S(2)}, u32[]{:S(2)}) collective-permute-start(bf16[32,1152]{1,0:T(8,128)(2,1)S(1)} %get-tuple-element.33), channel_id=1, source_target_pairs={{0,2},{1,3},{2,0},{3,1},{4,6},{5,7},{6,4},{7,5},{8,10},{9,11},{10,... | collective-permute-start | bytes 221192 | tf_op jit(solution)/shard_map/ppermute | solution.py:601
  59.0 6.2 %collective-permute-start.9 = (bf16[32,1152]{1,0:T(8,128)(2,1)S(1)}, bf16[32,1152]{1,0:T(8,128)(2,1)S(1)}, u32[]{:S(2)}, u32[]{:S(2)}) collective-permute-start(bf16[32,1152]{1,0:T(8,128)(2,1)S(1)} %get-tuple-element.32), channel_id=1, source_target_pairs={{0,1},{1,2},{2,3},{3,0},{4,5},{5,6},{6,7},{7,4},{8,9},{9,10},{10,1... | collective-permute-start | bytes 221192 | tf_op jit(solution)/shard_map/ppermute | solution.py:601
  65.9 17.8 %collective-permute-start.13 = (bf16[4,288,256]{2,1,0:T(8,128)(2,1)S(1)}, bf16[4,288,256]{2,1,0:T(8,128)(2,1)S(1)}, u32[]{:S(2)}, u32[]{:S(2)}) collective-permute-start(bf16[4,288,256]{2,1,0:T(8,128)(2,1)S(1)} %get-tuple-element.31.after_ref.own_ref), channel_id=1, source_target_pairs={{0,4},{4,0},{8,12},{12,8},{16,20},{20,16},{24,28},{28,24},{1,5},{5... | collective-permute-start | bytes 1769480 | tf_op jit(solution)/shard_map/ppermute | solution.py:594
  65.9 17.7 %collective-permute-start.14 = (bf16[4,288,256]{2,1,0:T(8,128)(2,1)}, bf16[4,288,256]{2,1,0:T(8,128)(2,1)}, u32[]{:S(2)}, u32[]{:S(2)}) collective-permute-start(bf16[4,288,256]{2,1,0:T(8,128)(2,1)} %copy-done.26), channel_id=1, source_target_pairs={{0,4},{4,0},{8,12},{12,8},{16,20},{20,16},{24,28},{28,24},{1,5},{5... | collective-permute-start | bytes 1769480 | tf_op jit(solution)/shard_map/ppermute | solution.py:593
  66.4 12.4 %collective-permute-start.12 = (bf16[192,1152]{1,0:T(8,128)(2,1)}, bf16[192,1152]{1,0:T(8,128)(2,1)S(1)}, u32[]{:S(2)}, u32[]{:S(2)}) collective-permute-start(bf16[192,1152]{1,0:T(8,128)(2,1)} %copy-done.36), channel_id=1, source_target_pairs={{0,1},{1,0},{2,3},{3,2},{4,5},{5,4},{6,7},{7,6},{8,9},{9,8},{10,11... | collective-permute-start | bytes 1327112 | tf_op jit(solution)/shard_map/ppermute | solution.py:595
  87.4 20.0 %collective-permute-start.16 = (bf16[784,256]{1,0:T(8,128)(2,1)S(1)}, bf16[784,256]{1,0:T(8,128)(2,1)S(1)}, u32[]{:S(2)}, u32[]{:S(2)}) collective-permute-start(bf16[784,256]{1,0:T(8,128)(2,1)S(1)} %far.2.rest_0_), channel_id=1, source_target_pairs={{0,2},{1,3},{2,0},{3,1},{4,6},{5,7},{6,4},{7,5},{8,10},{9,11},{10,... | collective-permute-start | bytes 1204232 | tf_op jit(solution)/shard_map/ppermute | solution.py:615
  109.0 21.3 %collective-permute-start.17 = (bf16[784,256]{1,0:T(8,128)(2,1)S(1)}, bf16[784,256]{1,0:T(8,128)(2,1)S(1)}, u32[]{:S(2)}, u32[]{:S(2)}) collective-permute-start(bf16[784,256]{1,0:T(8,128)(2,1)S(1)} %get-tuple-element.40.rest_2_), channel_id=1, source_target_pairs={{0,8},{4,12},{1,9},{5,13},{2,10},{6,14},{3,11},{7,15},{16,24},{20,... | collective-permute-start | bytes 1204232 | tf_op jit(solution)/shard_map/ppermute | solution.py:629
  110.3 20.8 %collective-permute-start.18 = (bf16[784,256]{1,0:T(8,128)(2,1)S(1)}, bf16[784,256]{1,0:T(8,128)(2,1)S(1)}, u32[]{:S(2)}, u32[]{:S(2)}) collective-permute-start(bf16[784,256]{1,0:T(8,128)(2,1)S(1)} %get-tuple-element.40.rest_2_), channel_id=1, source_target_pairs={{0,4},{4,8},{8,12},{1,5},{5,9},{9,13},{2,6},{6,10},{10,14},{3,7},{... | collective-permute-start | bytes 1204232 | tf_op jit(solution)/shard_map/ppermute | solution.py:629
  112.2 17.3 %collective-permute-start.15 = (bf16[768,256]{1,0:T(8,128)(2,1)S(1)}, bf16[768,256]{1,0:T(8,128)(2,1)S(1)}, u32[]{:S(2)}, u32[]{:S(2)}) collective-permute-start(bf16[768,256]{1,0:T(8,128)(2,1)S(1)} %far.3.after_ref), channel_id=1, source_target_pairs={{0,2},{1,3},{2,0},{3,1},{4,6},{5,7},{6,4},{7,5},{8,10},{9,11},{10,... | collective-permute-start | bytes 1179656 | tf_op jit(solution)/shard_map/ppermute | solution.py:619
  142.4 16.4 %collective-permute-start.22 = (bf16[384,256]{1,0:T(8,128)(2,1)S(1)}, bf16[384,256]{1,0:T(8,128)(2,1)}, u32[]{:S(2)}, u32[]{:S(2)}) collective-permute-start(bf16[384,256]{1,0:T(8,128)(2,1)S(1)} %attend.2.after_ref.rest_0_), channel_id=1, source_target_pairs={{0,2},{1,3},{2,0},{3,1},{4,6},{5,7},{6,4},{7,5},{8,10},{9,11},{10,... | collective-permute-start | bytes 589832 | tf_op jit(solution)/shard_map/ppermute | solution.py:640
  148.4 15.2 %collective-permute-start.19 = (bf16[384,256]{1,0:T(8,128)(2,1)S(1)}, bf16[384,256]{1,0:T(8,128)(2,1)S(1)}, u32[]{:S(2)}, u32[]{:S(2)}) collective-permute-start(bf16[384,256]{1,0:T(8,128)(2,1)S(1)} %attend.3.rest_0_), channel_id=1, source_target_pairs={{0,2},{1,3},{2,0},{3,1},{4,6},{5,7},{6,4},{7,5},{8,10},{9,11},{10,... | collective-permute-start | bytes 589832 | tf_op jit(solution)/shard_map/ppermute | solution.py:640
  151.3 12.3 %collective-permute-start.23 = (bf16[384,256]{1,0:T(8,128)(2,1)S(1)}, bf16[384,256]{1,0:T(8,128)(2,1)S(1)}, u32[]{:S(2)}, u32[]{:S(2)}) collective-permute-start(bf16[384,256]{1,0:T(8,128)(2,1)S(1)} %attend.2.after_ref.rest_0_), channel_id=1, source_target_pairs={{0,1},{1,0},{2,3},{3,2},{4,5},{5,4},{6,7},{7,6},{8,9},{9,8},{10,11... | collective-permute-start | bytes 589832 | tf_op jit(solution)/shard_map/ppermute | solution.py:641
  158.8 9.0 %collective-permute-start.24 = (bf16[384,256]{1,0:T(8,128)(2,1)}, bf16[384,256]{1,0:T(8,128)(2,1)S(1)}, u32[]{:S(2)}, u32[]{:S(2)}) collective-permute-start(bf16[384,256]{1,0:T(8,128)(2,1)} %collective-permute-done.22.rest_1_), channel_id=1, source_target_pairs={{0,1},{1,0},{2,3},{3,2},{4,5},{5,4},{6,7},{7,6},{8,9},{9,8},{10,11... | collective-permute-start | bytes 589832 | tf_op jit(solution)/shard_map/ppermute | solution.py:642
  158.8 22.5 %collective-permute-start.20 = (bf16[384,256]{1,0:T(8,128)(2,1)S(1)}, bf16[384,256]{1,0:T(8,128)(2,1)S(1)}, u32[]{:S(2)}, u32[]{:S(2)}) collective-permute-start(bf16[384,256]{1,0:T(8,128)(2,1)S(1)} %attend.3.rest_0_), channel_id=1, source_target_pairs={{0,1},{1,0},{2,3},{3,2},{4,5},{5,4},{6,7},{7,6},{8,9},{9,8},{10,11... | collective-permute-start | bytes 589832 | tf_op jit(solution)/shard_map/ppermute | solution.py:641
  163.5 17.8 %collective-permute-start.21 = (bf16[384,256]{1,0:T(8,128)(2,1)S(1)}, bf16[384,256]{1,0:T(8,128)(2,1)S(1)}, u32[]{:S(2)}, u32[]{:S(2)}) collective-permute-start(bf16[384,256]{1,0:T(8,128)(2,1)S(1)} %collective-permute-done.19.rest_1_), channel_id=1, source_target_pairs={{0,1},{1,0},{2,3},{3,2},{4,5},{5,4},{6,7},{7,6},{8,9},{9,8},{10,11... | collective-permute-start | bytes 589832 | tf_op jit(solution)/shard_map/ppermute | solution.py:642
  177.5 9.2 %collective-permute-start.28 = (f32[1,384]{1,0:T(1,128)S(1)}, f32[1,384]{1,0:T(1,128)S(1)}, u32[]{:S(2)}, u32[]{:S(2)}) collective-permute-start(f32[1,384]{1,0:T(1,128)S(1)} %get-tuple-element.41.rest_4_.rest_0_), channel_id=1, source_target_pairs={{0,1},{1,2},{2,3},{3,0},{4,5},{5,6},{6,7},{7,4},{8,9},{9,10},{10,1... | collective-permute-start | bytes 4616 | tf_op jit(solution)/shard_map/ppermute | solution.py:651
  177.5 12.0 %collective-permute-start.29 = (f32[1,384]{1,0:T(1,128)S(1)}, f32[1,384]{1,0:T(1,128)S(1)}, u32[]{:S(2)}, u32[]{:S(2)}) collective-permute-start(f32[1,384]{1,0:T(1,128)S(1)} %get-tuple-element.41.rest_4_.rest_0_), channel_id=1, source_target_pairs={{0,2},{1,3},{2,0},{3,1},{4,6},{5,7},{6,4},{7,5},{8,10},{9,11},{10,... | collective-permute-start | bytes 4616 | tf_op jit(solution)/shard_map/ppermute | solution.py:651
  179.9 9.6 %collective-permute-start.30 = (f32[1,384]{1,0:T(1,128)S(1)}, f32[1,384]{1,0:T(1,128)S(1)}, u32[]{:S(2)}, u32[]{:S(2)}) collective-permute-start(f32[1,384]{1,0:T(1,128)S(1)} %get-tuple-element.41.rest_4_.rest_0_), channel_id=1, source_target_pairs={{0,3},{1,0},{2,1},{3,2},{4,7},{5,4},{6,5},{7,6},{8,11},{9,8},{10,9... | collective-permute-start | bytes 4616 | tf_op jit(solution)/shard_map/ppermute | solution.py:651
  184.5 7.0 %collective-permute-start.25 = (f32[1,384]{1,0:T(1,128)S(1)}, f32[1,384]{1,0:T(1,128)S(1)}, u32[]{:S(2)}, u32[]{:S(2)}) collective-permute-start(f32[1,384]{1,0:T(1,128)S(1)} %get-tuple-element.43.rest_0_), channel_id=1, source_target_pairs={{0,1},{1,2},{2,3},{3,0},{4,5},{5,6},{6,7},{7,4},{8,9},{9,10},{10,1... | collective-permute-start | bytes 4616 | tf_op jit(solution)/shard_map/ppermute | solution.py:651
  185.1 6.3 %collective-permute-start.26 = (f32[1,384]{1,0:T(1,128)S(1)}, f32[1,384]{1,0:T(1,128)S(1)}, u32[]{:S(2)}, u32[]{:S(2)}) collective-permute-start(f32[1,384]{1,0:T(1,128)S(1)} %get-tuple-element.43.rest_0_), channel_id=1, source_target_pairs={{0,2},{1,3},{2,0},{3,1},{4,6},{5,7},{6,4},{7,5},{8,10},{9,11},{10,... | collective-permute-start | bytes 4616 | tf_op jit(solution)/shard_map/ppermute | solution.py:651
  186.6 4.8 %collective-permute-start.27 = (f32[1,384]{1,0:T(1,128)S(1)}, f32[1,384]{1,0:T(1,128)S(1)}, u32[]{:S(2)}, u32[]{:S(2)}) collective-permute-start(f32[1,384]{1,0:T(1,128)S(1)} %get-tuple-element.43.rest_0_), channel_id=1, source_target_pairs={{0,3},{1,0},{2,1},{3,2},{4,7},{5,4},{6,5},{7,6},{8,11},{9,8},{10,9... | collective-permute-start | bytes 4616 | tf_op jit(solution)/shard_map/ppermute | solution.py:651
  (40 other events, 150.2 us)
Sparse Core Ops, SparseCore 0:
  66.0 24.8 all-gather.2

commit v8 on v7

--- a/solution.py
+++ b/solution.py
@@ -25,7 +25,7 @@
 HBM = pl.BlockSpec(memory_space=pltpu.HBM)
 VMEM = pl.BlockSpec(memory_space=pltpu.VMEM)
 DOCUMENTS = 8
-PARAMS = pltpu.CompilerParams(vmem_limit_bytes=24 * 1024 * 1024)
+PARAMS = pltpu.CompilerParams(vmem_limit_bytes=48 * 1024 * 1024)
 ALL_VMEM = pltpu.CompilerParams(vmem_limit_bytes=62 * 1024 * 1024)
 
 
@@ -176,8 +176,12 @@
         grid_spec=pltpu.PrefetchScalarGridSpec(
             num_scalar_prefetch=1,
             grid=(1,),
-            in_specs=[VMEM] + [VMEM for _ in pieces],
-            out_specs=[VMEM, VMEM],
+            in_specs=[pl.BlockSpec(gains.shape, lambda i, s: (0, 0, 0))]
+            + [pl.BlockSpec(piece.shape, lambda i, s: (0, 0)) for piece in pieces],
+            out_specs=[
+                pl.BlockSpec(dims, lambda i, s: (0, 0, 0)),
+                pl.BlockSpec((1, rows), lambda i, s: (0, 0)),
+            ],
         ),
         compiler_params=PARAMS,
         name="prep",
@@ -243,8 +247,14 @@
         grid_spec=pltpu.PrefetchScalarGridSpec(
             num_scalar_prefetch=2,
             grid=(1,),
-            in_specs=[VMEM, VMEM, ANY, ANY] + [ANY for _ in after],
-            out_specs=VMEM,
+            in_specs=[
+                pl.BlockSpec(x.shape, lambda i, p, s: (0, 0, 0)),
+                pl.BlockSpec((1, rows), lambda i, p, s: (0, 0)),
+                ANY,
+                ANY,
+            ]
+            + [ANY for _ in after],
+            out_specs=pl.BlockSpec((out_rows, width), lambda i, p, s: (0, 0)),
             scratch_shapes=[
                 pltpu.VMEM((len(order) * share, width), BF16),
                 pltpu.SemaphoreType.DMA((len(order),)),
@@ -256,7 +266,7 @@
 
 
 def near_kernel(src_ref, x_ref, k_ref, v_ref, q_ref, after_ref, out_ref):
-    x = x_ref[pl.program_id(0)]
+    x = x_ref[0]
 
     @pl.when(pl.program_id(0) == 0)
     def _():
@@ -278,10 +288,10 @@
         grid_spec=pltpu.PrefetchScalarGridSpec(
             num_scalar_prefetch=1,
             grid=(count,),
-            in_specs=[VMEM]
+            in_specs=[pl.BlockSpec((1, chunk, cols), lambda i, s: (i, 0, 0))]
             + [pl.BlockSpec((cols, w), lambda i, s: (s[i], 0)) for w in widths]
             + [ANY],
-            out_specs=VMEM,
+            out_specs=pl.BlockSpec((chunk, sum(widths)), lambda i, s: (0, 0)),
         ),
         compiler_params=PARAMS,
         name="near",
@@ -289,32 +299,33 @@
 
 
 def keys_kernel(
-    near_ref, far_ref, sq_ref, id_ref, cos_ref, sin_ref, after_ref, out_ref, sum_ref, *, model
+    near_ref, far_ref, sq_ref, id_ref, cos_ref, sin_ref, after_ref, k_out, vt_out, sum_ref, *, model
 ):
-    rows, width = near_ref.shape[0], far_ref.shape[1]
+    rows = near_ref.shape[0]
     tail = far_ref[rows:, :].astype(F32)
     total = sum(rows_of(tail, 2, rows), sq_ref[...])
     factor = to_column(lax.rsqrt(total / model + epsilon))
     sum_ref[...] = total
     keys, values = slice(0, HEAD_SIZE), slice(HEAD_SIZE, 2 * HEAD_SIZE)
     part = (near_ref[:, keys] + far_ref[:rows, keys].astype(F32)) * factor
-    part = rotate(part, cos_ref[...], sin_ref[...]).astype(BF16)
-    out_ref[: rows // 2, keys] = part[: rows // 2]
-    out_ref[: rows // 2, values] = part[rows // 2 :]
+    k_out[:rows, :] = rotate(part, cos_ref[...], sin_ref[...]).astype(BF16)
+    k_out[rows:, :] = lines_of((id_ref[...].astype(F32),), HEAD_SIZE)
     part = (near_ref[:, values] + far_ref[:rows, values].astype(F32)) * factor
-    part = part.T.astype(BF16)
-    for i, at in enumerate(range(0, rows, width)):
-        row = rows // 2 + i * HEAD_SIZE
-        out_ref[row : row + HEAD_SIZE, :] = part[:, at : at + width]
-    out_ref[rows:, :] = lines_of((id_ref[...].astype(F32),), width)
+    vt_out[...] = part.T.astype(BF16)
 
 
 def keys_values(near, far, sq, ids, cosine, sine, after, model):
+    rows, width = near.shape[0], far.shape[1]
+    whole = lambda i: (0, 0)
+    dims = [(rows + TAIL, HEAD_SIZE), (HEAD_SIZE, rows), (1, rows)]
     return pl.pallas_call(
         partial(keys_kernel, model=model),
-        out_shape=(shape(far.shape, BF16), shape(sq.shape, F32)),
-        in_specs=[VMEM] * 6 + [ANY],
-        out_specs=[VMEM, VMEM],
+        out_shape=tuple(shape(d, t) for d, t in zip(dims, (BF16, BF16, F32))),
+        grid=(1,),
+        in_specs=[pl.BlockSpec((rows, width), whole)]
+        + [pl.BlockSpec(a.shape, whole) for a in (far, sq, ids, cosine, sine)]
+        + [ANY],
+        out_specs=[pl.BlockSpec(d, whole) for d in dims],
         compiler_params=PARAMS,
         name="keys",
     )(near, far, sq, ids, cosine, sine, after)
@@ -324,21 +335,18 @@
     seq_ref, near_ref, far_ref, sum_ref, cos_ref, sin_ref, id_ref, after_ref, *rest, back, offset, model
 ):
     kv_refs, (out_ref, k_scr, vt_scr, count_scr) = rest[:-4], rest[-4:]
-    part_rows, message = kv_refs[0].shape[0] - TAIL, kv_refs[0].shape[1]
+    part_rows = kv_refs[1].shape[1]
     group = near_ref.shape[1] // HEAD_SIZE
     tile = pl.program_id(0)
 
     @pl.when(tile == 0)
     def _():
         counts = [jnp.zeros((1, 1), F32) for _ in range(DOCUMENTS)]
-        for b, kv_ref in enumerate(kv_refs):
-            row, half = b * part_rows, part_rows // 2
-            k_scr[row : row + half, :] = kv_ref[:half, :HEAD_SIZE]
-            k_scr[row + half : row + part_rows, :] = kv_ref[:half, HEAD_SIZE:]
-            for i, at in enumerate(range(0, part_rows, message)):
-                first = half + i * HEAD_SIZE
-                vt_scr[:, row + at : row + at + message] = kv_ref[first : first + HEAD_SIZE, :]
-            (ids,) = rows_of(kv_ref[part_rows:, :].astype(F32), 1, part_rows)
+        for b, (k_ref, vt_ref) in enumerate(zip(kv_refs[::2], kv_refs[1::2])):
+            at = slice(b * part_rows, (b + 1) * part_rows)
+            k_scr[at, :] = k_ref[:part_rows, :]
+            vt_scr[:, at] = vt_ref[...]
+            (ids,) = rows_of(k_ref[part_rows:, :].astype(F32), 1, part_rows)
             exists = b >= back - seq_ref[0]
             ids = jnp.where(exists, ids, -1.0)
             for d in range(DOCUMENTS):
@@ -411,10 +419,10 @@
 def attend(seq, near, far, sums, cosine, sine, ids, after, blocks, c, model):
     rows = near.shape[0] // CHUNKS
     width = far.shape[1]
-    part_rows = blocks[0].shape[0] - TAIL
     back = len(blocks) - 1
     tiles = rows // Q_TILE
-    keys = len(blocks) * part_rows
+    keys = len(blocks) * near.shape[0]
+    blocks = [part for block in blocks for part in block]
     last = near.shape[1] // width - 1
     return pl.pallas_call(
         partial(attention_kernel, back=back, offset=c * rows, model=model),
@@ -431,7 +439,7 @@
                 pl.BlockSpec((1, Q_TILE), lambda i, s: (0, c * tiles + i)),
                 ANY,
             ]
-            + [VMEM for _ in blocks],
+            + [pl.BlockSpec(b.shape, lambda i, s: (0, 0)) for b in blocks],
             out_specs=pl.BlockSpec((Q_TILE, width), lambda i, s: (i, 0)),
             scratch_shapes=[
                 pltpu.VMEM((keys, HEAD_SIZE), BF16),
@@ -587,7 +595,7 @@
                 tokens,
                 first,
                 counts[step + 1],
-                [received[-1]],
+                received[-2:-1],
             )
         first += counts[step + 1]
         far_kv = lax.ppermute(own_kv, PLANE, [(i, i ^ mask_kv) for i in range(plane)])
@@ -595,12 +603,6 @@
         received.append(lax.ppermute(cut, "tensor", ring))
         order_kv = order_kv + [k ^ mask_kv for k in order_kv]
         order_q = order_q + [k ^ mask_q for k in order_q]
-    o_share = o_weight.shape[0] // plane
-    columns = [(z + k) % nz * cols for k in range(1, nz)]
-    pieces = cut_pieces(in_plane * o_share, columns, o_weight, o_share, cols, own_q)
-    moved = [lax.ppermute(p, "tensor", turn(k + 1)) for k, p in enumerate(pieces)]
-    moved = jnp.stack(moved)
-    gathered_o = lax.all_gather(moved, PLANE)
     far_kv, far_q = (order_kv, own_kv, far_kv), (order_q, own_q, far_q)
 
     sources = (within + half - jnp.arange(half, dtype=jnp.int32)) % half
@@ -611,7 +613,7 @@
     x, sq = prep(side * half + sources, gains, blocks)
 
     place = jnp.reshape(in_plane, (1,))
-    sent_kv = far_product(place, sources, x, sq, far_kv, True, [far_q[2], moved])
+    sent_kv = far_product(place, sources, x, sq, far_kv, True, [far_q[2]])
     got_kv = lax.ppermute(sent_kv, "tensor", swap)
     weights = (k_weight, value_weight, q_weight)
 
@@ -620,17 +622,24 @@
     near = near_product(side * half + sources, x, weights, sent_q)
     cosine, sine = rotation_table(seq * rows + jnp.arange(rows, dtype=jnp.int32))
     ids = seg_ids[None, :]
-    own_kv, sums = keys_values(near, got_kv, sq, ids, cosine, sine, sent_q, model)
+    *own_kv, sums = keys_values(near, got_kv, sq, ids, cosine, sine, sent_q, model)
 
     back = -(-(nseq * rows // 2 - 1) // rows)
     kv_blocks = [own_kv]
     for k in range(1, back + 1):
         earlier = [(i, i + k) for i in range(nseq - k)]
-        kv_blocks.insert(0, lax.ppermute(own_kv, "seq", earlier))
+        kv_blocks.insert(0, [lax.ppermute(part, "seq", earlier) for part in own_kv])
+
+    o_share = o_weight.shape[0] // plane
+    columns = [(z + k) % nz * cols for k in range(1, nz)]
+    pieces = cut_pieces(in_plane * o_share, columns, o_weight, o_share, cols, own_kv[0])
+    moved = [lax.ppermute(p, "tensor", turn(k + 1)) for k, p in enumerate(pieces)]
+    moved = jnp.stack(moved)
+    gathered_o = lax.all_gather(moved, PLANE)
 
     out = None
     seq_at = jnp.reshape(seq, (1,))
-    context, own_sq = gathered_o, place
+    context, own_sq = moved, place
     for c in range(CHUNKS):
         context = attend(
             seq_at, near, got_q, sums, cosine, sine, ids, context, kv_blocks, c, model

time: 203 us -> 189 us (0.931); the launches traced: 200 us -> 189 us
  local copies, waits for them, and re-layouts: 23 us -> 7.63 us
  waiting for transfers between devices: 84.7 us -> 78 us
  starting transfers between devices: 35.7 us -> 41.3 us
  Pallas kernels: 40.3 us -> 45.4 us
    unnamed x80 -> x34, local copies, waits for them, and re-layouts: 23 us -> 7.6 us
    ppermute x1, waiting for transfers between devices: 17.2 us -> 10.8 us  [per_device(): got_q = lax.ppermute(sent_q, 'tensor', swap)]
    ppermute x2, waiting for transfers between devices: 9.8 us -> 4.83 us  [per_device(): opposite = lax.ppermute(context, 'tensor', swap)]
    ppermute x3, waiting for transfers between devices: 15.9 us -> 19.9 us  [per_device(): received.append(lax.ppermute(cut, 'tensor', ring))]
    ppermute x2 -> x4, starting transfers between devices: 3.2 us -> 6.41 us  [per_device(): kv_blocks.insert(0, [lax.ppermute(part, 'seq', earlier) for part in own_kv])]
    ppermute x2, waiting for transfers between devices: 0.01 us -> 3.11 us  [per_device(): beside = lax.ppermute(context, 'tensor', pairs)]
    ppermute x3, starting transfers between devices: 4.47 us -> 6.99 us  [per_device(): received.append(lax.ppermute(cut, 'tensor', ring))]
    ppermute x3, waiting for transfers between devices: 7.69 us -> 5.39 us  [per_device(): lax.ppermute(own_kv, PLANE, [(i, i ^ mask_kv) for i in range(plane)])]
  transfers between devices with their start and end apart: 32 -> 34, of which waited for: 17 -> 15; matrix products, arithmetic and copies ran while one was open for 1% -> 1% of each run, Pallas kernels for 14% -> 19%
where the time goes in v8:
time: 189 us
  waiting for transfers between devices  78 us (41%)
  Pallas kernels  45.4 us (24%)
  starting transfers between devices  41.3 us (22%)
  between operations  13.7 us (7%)
  local copies, waits for them, and re-layouts  7.63 us (4%)
  other arithmetic  2.64 us (1%)
    ppermute x3, waiting for transfers between devices, per_device(): received.append(lax.ppermute(cut, 'tensor', ring))  19.9 us
    pallas_call x2, Pallas kernels, attend(): pl.pallas_call(partial(attention_kernel, back=back, offset=c * rows, mode...  12.1 us
    ppermute x1, waiting for transfers between devices, per_device(): own_kv = lax.ppermute(packed_kv, 'tensor', swap)[None]  11.1 us
    ppermute x1, waiting for transfers between devices, per_device(): got_q = lax.ppermute(sent_q, 'tensor', swap)  10.8 us
    ppermute x6, starting transfers between devices, per_device(): squares += [lax.ppermute(own_sq, 'tensor', turn(k)) for k in range(1, nz)]  8.89 us
    pallas_call x2, Pallas kernels, output_product(): pl.pallas_call(output_kernel, out_shape=(shape((chunk, cols), F32), shape...  8.06 us
    ppermute x1, waiting for transfers between devices, per_device(): got_kv = lax.ppermute(sent_kv, 'tensor', swap)  7.83 us
    unnamed x34, local copies, waits for them, and re-layouts  7.6 us
  transfers between devices with their start and end apart: 34, of which 15 were waited for; matrix products, arithmetic and copies ran while one was open for 1% of the time, Pallas kernels for 19%

profile of v8, /device:TPU:2, one launch (start us, length us, event | category | flops | bytes accessed | tf_op | source)
XLA Modules:
  0.0 188.7 jit_solution(3847391419822776224)
XLA Ops:
  6.5 2.2 %pack.1 = (bf16[288,256]{1,0:T(8,128)(2,1)}, bf16[288,256]{1,0:T(8,128)(2,1)}, bf16[192,1152]{1,0:T(8,128)(2,1)}) custom-call(s32[1]{0:T(128)} %bitcast.7.at_ref, bf16[4608,256]{1,0:T(8,128)(2,1)} %q_ref.3, bf16[4608,128]{1,0:T(8,128)(2,1)} %k_ref.3, bf16[4608,128]{1,0:T(8,128)(2,1)} %v_ref.3, bf16[768,1152]{1,0:T(8,128)(2,1)} %token_ref.3), custom_call_target="tpu_custom_call" | custom-call | tf_op jit(solution)/shard_map/pack/pallas_call | solution.py:74
  10.4 2.6 %collective-permute-start.1 = (bf16[288,256]{1,0:T(8,128)(2,1)}, bf16[288,256]{1,0:T(8,128)(2,1)S(1)}, u32[]{:S(2)}, u32[]{:S(2)}) collective-permute-start(bf16[288,256]{1,0:T(8,128)(2,1)} %get-tuple-element.27), channel_id=1, source_target_pairs={{0,2},{1,3},{2,0},{3,1},{4,6},{5,7},{6,4},{7,5},{8,10},{9,11},{10,... | collective-permute-start | bytes 442376 | tf_op jit(solution)/shard_map/ppermute | solution.py:585
  13.3 11.1 %collective-permute-done.1 = bf16[288,256]{1,0:T(8,128)(2,1)S(1)} collective-permute-done((bf16[288,256]{1,0:T(8,128)(2,1)}, bf16[288,256]{1,0:T(8,128)(2,1)S(1)}, u32[]{:S(2)}, u32[]{:S(2)}) %collective-permute-start.1) | collective-permute-done | bytes 147488 | tf_op jit(solution)/shard_map/ppermute | solution.py:585
  28.2 3.5 %collective-permute-start.3 = (bf16[192,1152]{1,0:T(8,128)(2,1)S(1)}, bf16[192,1152]{1,0:T(8,128)(2,1)S(1)}, u32[]{:S(2)}, u32[]{:S(2)}) collective-permute-start(bf16[192,1152]{1,0:T(8,128)(2,1)S(1)} %stage.3), channel_id=1, source_target_pairs={{0,1},{1,0},{2,3},{3,2},{4,5},{5,4},{6,7},{7,6},{8,9},{9,8},{10,11... | collective-permute-start | bytes 1327112 | tf_op jit(solution)/shard_map/ppermute | solution.py:603
  35.4 5.4 %collective-permute-done.7.refs_1_ = bf16[2,288,256]{2,1,0:T(8,128)(2,1)S(1)} collective-permute-done((bf16[2,288,256]{2,1,0:T(8,128)(2,1)S(1)}, bf16[2,288,256]{2,1,0:T(8,128)(2,1)S(1)}, u32[]{:S(2)}, u32[]{:S(2)}) %collective-permute-start.7) | collective-permute-done | bytes 294944 | tf_op jit(solution)/shard_map/ppermute | solution.py:601
  44.5 3.5 %collective-permute-start.6 = (bf16[192,1152]{1,0:T(8,128)(2,1)}, bf16[192,1152]{1,0:T(8,128)(2,1)S(1)}, u32[]{:S(2)}, u32[]{:S(2)}) collective-permute-start(bf16[192,1152]{1,0:T(8,128)(2,1)} %copy-done.12), channel_id=1, source_target_pairs={{0,1},{1,0},{2,3},{3,2},{4,5},{5,4},{6,7},{7,6},{8,9},{9,8},{10,11... | collective-permute-start | bytes 1327112 | tf_op jit(solution)/shard_map/ppermute | solution.py:603
  48.1 11.1 %collective-permute-done.6.rest_3_ = bf16[192,1152]{1,0:T(8,128)(2,1)S(1)} collective-permute-done((bf16[192,1152]{1,0:T(8,128)(2,1)}, bf16[192,1152]{1,0:T(8,128)(2,1)S(1)}, u32[]{:S(2)}, u32[]{:S(2)}) %collective-permute-start.6) | collective-permute-done | bytes 442400 | tf_op jit(solution)/shard_map/ppermute | solution.py:603
  59.2 8.8 %collective-permute-done.9.rest_4_ = bf16[192,1152]{1,0:T(8,128)(2,1)S(1)} collective-permute-done((bf16[192,1152]{1,0:T(8,128)(2,1)}, bf16[192,1152]{1,0:T(8,128)(2,1)S(1)}, u32[]{:S(2)}, u32[]{:S(2)}) %collective-permute-start.9) | collective-permute-done | bytes 442400 | tf_op jit(solution)/shard_map/ppermute | solution.py:603
  68.0 3.3 %prep.1 = (bf16[2,768,1152]{2,1,0:T(8,128)(2,1)}, f32[1,768]{1,0:T(1,128)S(1)}) custom-call(s32[2]{0:T(128)S(1)} %broadcast_add_fusion.src_ref, f32[4,1,1152]{2,1,0:T(1,128)S(1)} %reshape.23.gain_ref, bf16[768,1152]{1,0:T(8,128)(2,1)S(1)} %copy-done, bf16[192,1152]{1,0:T(8,128)(2,1)S(1)} %collective-permute-done.refs_3_.refs_5_.rest_1_, ...), custom_call_target="tpu_custom_call" | custom-call | tf_op jit(solution)/shard_map/prep/pallas_call | solution.py:173
  71.3 2.2 %copy-done.1 = bf16[2,768,1152]{2,1,0:T(8,128)(2,1)S(1)} copy-done((bf16[2,768,1152]{2,1,0:T(8,128)(2,1)S(1)}, bf16[2,768,1152]{2,1,0:T(8,128)(2,1)}, u32[]{:S(2)}) %copy-start.1) | copy-done | bytes 3538968
  73.5 3.1 %far.2.rest_0_ = bf16[784,256]{1,0:T(8,128)(2,1)S(1)} custom-call(s32[1]{0:T(128)} %bitcast.10.place_ref.rest_4_, s32[2]{0:T(128)S(1)} %and_select_fusion.src_ref, bf16[2,768,1152]{2,1,0:T(8,128)(2,1)S(1)} %copy-done.1, f32[1,768]{1,0:T(1,128)S(1)} %get-tuple-element.34.sq_ref, bf16[4,288,256]{2,1,0:T(8,128)(2,1)} %get-tuple-element.36.own_ref, ...), custom_call_target="tpu_custom_call" | custom-call | tf_op jit(solution)/shard_map/far/pallas_call | solution.py:244
  80.2 3.1 %far.3.after_ref = bf16[768,256]{1,0:T(8,128)(2,1)S(1)} custom-call(s32[1]{0:T(128)} %bitcast.10.place_ref.rest_4_, s32[2]{0:T(128)S(1)} %and_select_fusion.src_ref, bf16[2,768,1152]{2,1,0:T(8,128)(2,1)S(1)} %copy-done.1, f32[1,768]{1,0:T(1,128)S(1)} %get-tuple-element.34.sq_ref, bf16[4,288,256]{2,1,0:T(8,128)(2,1)} %get-tuple-element.35.own_ref, ...), custom_call_target="tpu_custom_call" | custom-call | tf_op jit(solution)/shard_map/far/pallas_call | solution.py:244
  83.3 5.7 %near.1.near_ref = f32[768,512]{1,0:T(8,128)S(1)} custom-call(s32[2]{0:T(128)S(1)} %broadcast_add_fusion.src_ref, bf16[2,768,1152]{2,1,0:T(8,128)(2,1)} %get-tuple-element.33.x_ref, bf16[4608,128]{1,0:T(8,128)(2,1)S(1)} %copy-done.7, bf16[4608,128]{1,0:T(8,128)(2,1)S(1)} %copy-done.8, bf16[4608,256]{1,0:T(8,128)(2,1)} %q_ref.3, ...), custom_call_target="tpu_custom_call" | custom-call | tf_op jit(solution)/shard_map/near/pallas_call | solution.py:285
  89.1 7.8 %collective-permute-done.12.far_ref = bf16[784,256]{1,0:T(8,128)(2,1)S(1)} collective-permute-done((bf16[784,256]{1,0:T(8,128)(2,1)S(1)}, bf16[784,256]{1,0:T(8,128)(2,1)S(1)}, u32[]{:S(2)}, u32[]{:S(2)}) %collective-permute-start.12) | collective-permute-done | bytes 401440 | tf_op jit(solution)/shard_map/ppermute | solution.py:617
  100.1 2.5 %collective-permute-done.15 = bf16[32,1152]{1,0:T(8,128)(2,1)S(1)} collective-permute-done((bf16[32,1152]{1,0:T(8,128)(2,1)S(1)}, bf16[32,1152]{1,0:T(8,128)(2,1)S(1)}, u32[]{:S(2)}, u32[]{:S(2)}) %collective-permute-start.15) | collective-permute-done | bytes 73760 | tf_op jit(solution)/shard_map/ppermute | solution.py:636
  102.6 3.8 %collective-permute-done.14 = bf16[32,1152]{1,0:T(8,128)(2,1)S(1)} collective-permute-done((bf16[32,1152]{1,0:T(8,128)(2,1)S(1)}, bf16[32,1152]{1,0:T(8,128)(2,1)S(1)}, u32[]{:S(2)}, u32[]{:S(2)}) %collective-permute-start.14) | collective-permute-done | bytes 73760 | tf_op jit(solution)/shard_map/ppermute | solution.py:636
  109.6 1.9 %collective-permute-start.19 = (bf16[784,128]{1,0:T(8,128)(2,1)S(1)}, bf16[784,128]{1,0:T(8,128)(2,1)S(1)}, u32[]{:S(2)}, u32[]{:S(2)}) collective-permute-start(bf16[784,128]{1,0:T(8,128)(2,1)S(1)} %get-tuple-element.37.after_ref.rest_4_), channel_id=1, source_target_pairs={{0,4},{4,8},{8,12},{1,5},{5,9},{9,13},{2,6},{6,10},{10,14},{3,7},{... | collective-permute-start | bytes 602120 | tf_op jit(solution)/shard_map/ppermute | solution.py:631
  112.9 1.9 %collective-permute-start.20 = (bf16[128,768]{1,0:T(8,128)(2,1)S(1)}, bf16[128,768]{1,0:T(8,128)(2,1)S(1)}, u32[]{:S(2)}, u32[]{:S(2)}) collective-permute-start(bf16[128,768]{1,0:T(8,128)(2,1)S(1)} %get-tuple-element.42.rest_5_), channel_id=1, source_target_pairs={{0,4},{4,8},{8,12},{1,5},{5,9},{9,13},{2,6},{6,10},{10,14},{3,7},{... | collective-permute-start | bytes 589832 | tf_op jit(solution)/shard_map/ppermute | solution.py:631
  114.8 10.8 %collective-permute-done.16.far_ref = bf16[768,256]{1,0:T(8,128)(2,1)S(1)} collective-permute-done((bf16[768,256]{1,0:T(8,128)(2,1)S(1)}, bf16[768,256]{1,0:T(8,128)(2,1)S(1)}, u32[]{:S(2)}, u32[]{:S(2)}) %collective-permute-start.16) | collective-permute-done | bytes 393248 | tf_op jit(solution)/shard_map/ppermute | solution.py:621
  125.6 2.1 %collective-permute-done.20.rest_3_ = bf16[128,768]{1,0:T(8,128)(2,1)S(1)} collective-permute-done((bf16[128,768]{1,0:T(8,128)(2,1)S(1)}, bf16[128,768]{1,0:T(8,128)(2,1)S(1)}, u32[]{:S(2)}, u32[]{:S(2)}) %collective-permute-start.20) | collective-permute-done | bytes 196640 | tf_op jit(solution)/shard_map/ppermute | solution.py:631
  130.1 5.5 %attend.2.after_ref.rest_0_ = bf16[384,256]{1,0:T(8,128)(2,1)S(1)} custom-call(s32[1]{0:T(128)} %bitcast.15.seq_ref, f32[768,512]{1,0:T(8,128)S(1)} %copy-done.3, bf16[768,256]{1,0:T(8,128)(2,1)S(1)} %collective-permute-done.16.far_ref, f32[1,768]{1,0:T(1,128)S(1)} %get-tuple-element.41.sum_ref, f32[768,128]{1,0:T(8,128)S(1)} %get-tuple-element.50.cos_ref, ...), custom_call_target="tpu_custom_call" | custom-call | flops 905969664 | bytes 2359296 | tf_op jit(solution)/shard_map/attend/pallas_call | solution.py:427
  137.0 6.6 %attend.3.rest_0_ = bf16[384,256]{1,0:T(8,128)(2,1)S(1)} custom-call(s32[1]{0:T(128)} %bitcast.15.seq_ref, f32[768,512]{1,0:T(8,128)S(1)} %copy-done.3, bf16[768,256]{1,0:T(8,128)(2,1)S(1)} %collective-permute-done.16.far_ref, f32[1,768]{1,0:T(1,128)S(1)} %get-tuple-element.41.sum_ref, f32[768,128]{1,0:T(8,128)S(1)} %get-tuple-element.50.cos_ref, ...), custom_call_target="tpu_custom_call" | custom-call | flops 905969664 | bytes 2359296 | tf_op jit(solution)/shard_map/attend/pallas_call | solution.py:427
  145.3 3.9 %collective-permute-done.24.rest_1_ = bf16[384,256]{1,0:T(8,128)(2,1)} collective-permute-done((bf16[384,256]{1,0:T(8,128)(2,1)S(1)}, bf16[384,256]{1,0:T(8,128)(2,1)}, u32[]{:S(2)}, u32[]{:S(2)}) %collective-permute-start.24) | collective-permute-done | bytes 196640 | tf_op jit(solution)/shard_map/ppermute | solution.py:649
  149.1 2.0 %collective-permute-start.22 = (bf16[384,256]{1,0:T(8,128)(2,1)S(1)}, bf16[384,256]{1,0:T(8,128)(2,1)S(1)}, u32[]{:S(2)}, u32[]{:S(2)}) collective-permute-start(bf16[384,256]{1,0:T(8,128)(2,1)S(1)} %attend.3.rest_0_), channel_id=1, source_target_pairs={{0,1},{1,0},{2,3},{3,2},{4,5},{5,4},{6,7},{7,6},{8,9},{9,8},{10,11... | collective-permute-start | bytes 589832 | tf_op jit(solution)/shard_map/ppermute | solution.py:650
  152.2 3.1 %collective-permute-done.25.rest_2_ = bf16[384,256]{1,0:T(8,128)(2,1)S(1)} collective-permute-done((bf16[384,256]{1,0:T(8,128)(2,1)S(1)}, bf16[384,256]{1,0:T(8,128)(2,1)S(1)}, u32[]{:S(2)}, u32[]{:S(2)}) %collective-permute-start.25) | collective-permute-done | bytes 196640 | tf_op jit(solution)/shard_map/ppermute | solution.py:650
  155.3 4.2 %collective-permute-done.26.rest_3_ = bf16[384,256]{1,0:T(8,128)(2,1)S(1)} collective-permute-done((bf16[384,256]{1,0:T(8,128)(2,1)}, bf16[384,256]{1,0:T(8,128)(2,1)S(1)}, u32[]{:S(2)}, u32[]{:S(2)}) %collective-permute-start.26) | collective-permute-done | bytes 196640 | tf_op jit(solution)/shard_map/ppermute | solution.py:651
  161.0 4.1 %output.2 = (f32[384,1152]{1,0:T(8,128)S(1)}, f32[1,384]{1,0:T(1,128)S(1)}) custom-call(s32[4]{0:T(128)S(1)} %pad_add_fusion.at_ref, bf16[256,4608]{1,0:T(8,128)(2,1)} %own_o_ref.3, bf16[8,3,32,1152]{3,2,1,0:T(8,128)(2,1)S(1)} %bitcast.16, bf16[384,256]{1,0:T(8,128)(2,1)S(1)} %attend.2.after_ref.rest_0_, bf16[384,256]{1,0:T(8,128)(2,1)} %collective-permute-done.24.rest_1_, ...), custom_call_target="tpu_custom_call" | custom-call | tf_op jit(solution)/shard_map/output/pallas_call | solution.py:493
  165.6 3.4 %collective-permute-start.32 = (f32[1,384]{1,0:T(1,128)S(1)}, f32[1,384]{1,0:T(1,128)S(1)}, u32[]{:S(2)}, u32[]{:S(2)}) collective-permute-start(f32[1,384]{1,0:T(1,128)S(1)} %get-tuple-element.43.rest_4_.rest_0_), channel_id=1, source_target_pairs={{0,3},{1,0},{2,1},{3,2},{4,7},{5,4},{6,5},{7,6},{8,11},{9,8},{10,9... | collective-permute-start | bytes 4616 | tf_op jit(solution)/shard_map/ppermute | solution.py:660
  169.0 4.0 %output.3 = (f32[384,1152]{1,0:T(8,128)S(1)}, f32[1,384]{1,0:T(1,128)S(1)}) custom-call(s32[4]{0:T(128)S(1)} %pad_add_fusion.at_ref, bf16[256,4608]{1,0:T(8,128)(2,1)} %own_o_ref.3, bf16[8,3,32,1152]{3,2,1,0:T(8,128)(2,1)S(1)} %bitcast.17, bf16[384,256]{1,0:T(8,128)(2,1)S(1)} %attend.3.rest_0_, bf16[384,256]{1,0:T(8,128)(2,1)S(1)} %collective-permute-done.21.rest_1_, ...), custom_call_target="tpu_custom_call" | custom-call | tf_op jit(solution)/shard_map/output/pallas_call | solution.py:493
  175.2 2.8 %collective-permute-start.29 = (f32[1,384]{1,0:T(1,128)S(1)}, f32[1,384]{1,0:T(1,128)S(1)}, u32[]{:S(2)}, u32[]{:S(2)}) collective-permute-start(f32[1,384]{1,0:T(1,128)S(1)} %get-tuple-element.45.rest_0_), channel_id=1, source_target_pairs={{0,3},{1,0},{2,1},{3,2},{4,7},{5,4},{6,5},{7,6},{8,11},{9,8},{10,9... | collective-permute-start | bytes 4616 | tf_op jit(solution)/shard_map/ppermute | solution.py:660
  178.0 1.9 %finish.2.rest_4_ = bf16[768,1152]{1,0:T(8,128)(2,1)} custom-call(bf16[768,1152]{1,0:T(8,128)(2,1)S(1)} %copy-done, f32[384,1152]{1,0:T(8,128)S(1)} %get-tuple-element.46.branch_ref, f32[1,1152]{1,0:T(1,128)S(1)} %broadcast_in_dim.18.gain_ref, f32[1,384]{1,0:T(1,128)S(1)} %get-tuple-element.43.rest_4_.rest_0_, f32[1,384]{1,0:T(1,128)S(1)} %collective-permute-done.30.rest_1_, ...), custom_call_target="tpu_custom_call" | custom-call | tf_op jit(solution)/shard_map/finish/pallas_call | solution.py:541
  180.0 1.9 %finish.3 = bf16[768,1152]{1,0:T(8,128)(2,1)} custom-call(bf16[768,1152]{1,0:T(8,128)(2,1)S(1)} %copy-done, f32[384,1152]{1,0:T(8,128)S(1)} %get-tuple-element.44.branch_ref, f32[1,1152]{1,0:T(1,128)S(1)} %broadcast_in_dim.18.gain_ref, f32[1,384]{1,0:T(1,128)S(1)} %get-tuple-element.45.rest_0_, ...), custom_call_target="tpu_custom_call", output_to_operand_aliasing={{}: (7, {})} | custom-call | tf_op jit(solution)/shard_map/finish/pallas_call | solution.py:541
  (99 shorter events, 35.0 us)
Async XLA Ops:
  6.5 153.0 %all-gather.3.cloned.1.call-start = ((), (), s32[]{:S(2)}) async-start(), calls=%async_computation | async-start | bytes 1990656 | tf_op jit(solution)/shard_map/all_gather | solution.py:638
  8.7 19.2 %collective-permute-start = (bf16[192,1152]{1,0:T(8,128)(2,1)}, bf16[192,1152]{1,0:T(8,128)(2,1)S(1)}, u32[]{:S(2)}, u32[]{:S(2)}) collective-permute-start(bf16[192,1152]{1,0:T(8,128)(2,1)} %get-tuple-element.26), channel_id=1, source_target_pairs={{0,1},{1,0},{2,3},{3,2},{4,5},{5,4},{6,7},{7,6},{8,9},{9,8},{10,11... | collective-permute-start | bytes 1327112 | tf_op jit(solution)/shard_map/ppermute | solution.py:587
  10.4 14.0 %collective-permute-start.1 = (bf16[288,256]{1,0:T(8,128)(2,1)}, bf16[288,256]{1,0:T(8,128)(2,1)S(1)}, u32[]{:S(2)}, u32[]{:S(2)}) collective-permute-start(bf16[288,256]{1,0:T(8,128)(2,1)} %get-tuple-element.27), channel_id=1, source_target_pairs={{0,2},{1,3},{2,0},{3,1},{4,6},{5,7},{6,4},{7,5},{8,10},{9,11},{10,... | collective-permute-start | bytes 442376 | tf_op jit(solution)/shard_map/ppermute | solution.py:585
  13.0 13.5 %collective-permute-start.2 = (bf16[288,256]{1,0:T(8,128)(2,1)}, bf16[288,256]{1,0:T(8,128)(2,1)S(1)}, u32[]{:S(2)}, u32[]{:S(2)}) collective-permute-start(bf16[288,256]{1,0:T(8,128)(2,1)} %get-tuple-element.28), channel_id=1, source_target_pairs={{0,2},{1,3},{2,0},{3,1},{4,6},{5,7},{6,4},{7,5},{8,10},{9,11},{10,... | collective-permute-start | bytes 442376 | tf_op jit(solution)/shard_map/ppermute | solution.py:586
  24.4 7.3 %collective-permute-start.4 = (bf16[1,288,256]{2,1,0:T(8,128)(2,1)S(1)}, bf16[1,288,256]{2,1,0:T(8,128)(2,1)S(1)}, u32[]{:S(2)}, u32[]{:S(2)}) collective-permute-start(bf16[1,288,256]{2,1,0:T(8,128)(2,1)S(1)} %bitcast.18), channel_id=1, source_target_pairs={{0,8},{4,12},{8,0},{12,4},{16,24},{20,28},{24,16},{28,20},{1,9},{5... | collective-permute-start | bytes 442376 | tf_op jit(solution)/shard_map/ppermute | solution.py:601
  26.4 5.2 %collective-permute-start.5 = (bf16[1,288,256]{2,1,0:T(8,128)(2,1)S(1)}, bf16[1,288,256]{2,1,0:T(8,128)(2,1)S(1)}, u32[]{:S(2)}, u32[]{:S(2)}) collective-permute-start(bf16[1,288,256]{2,1,0:T(8,128)(2,1)S(1)} %bitcast.21), channel_id=1, source_target_pairs={{0,16},{4,20},{8,24},{12,28},{16,0},{20,4},{24,8},{28,12},{1,17},{... | collective-permute-start | bytes 442376 | tf_op jit(solution)/shard_map/ppermute | solution.py:602
  28.2 13.4 %collective-permute-start.3 = (bf16[192,1152]{1,0:T(8,128)(2,1)S(1)}, bf16[192,1152]{1,0:T(8,128)(2,1)S(1)}, u32[]{:S(2)}, u32[]{:S(2)}) collective-permute-start(bf16[192,1152]{1,0:T(8,128)(2,1)S(1)} %stage.3), channel_id=1, source_target_pairs={{0,1},{1,0},{2,3},{3,2},{4,5},{5,4},{6,7},{7,6},{8,9},{9,8},{10,11... | collective-permute-start | bytes 1327112 | tf_op jit(solution)/shard_map/ppermute | solution.py:603
  33.5 7.3 %collective-permute-start.7 = (bf16[2,288,256]{2,1,0:T(8,128)(2,1)S(1)}, bf16[2,288,256]{2,1,0:T(8,128)(2,1)S(1)}, u32[]{:S(2)}, u32[]{:S(2)}) collective-permute-start(bf16[2,288,256]{2,1,0:T(8,128)(2,1)S(1)} %get-tuple-element.30.refs_0_), channel_id=1, source_target_pairs={{0,16},{4,20},{8,24},{12,28},{16,0},{20,4},{24,8},{28,12},{1,17},{... | collective-permute-start | bytes 884744 | tf_op jit(solution)/shard_map/ppermute | solution.py:601
  34.9 6.7 %collective-permute-start.8 = (bf16[2,288,256]{2,1,0:T(8,128)(2,1)S(1)}, bf16[2,288,256]{2,1,0:T(8,128)(2,1)S(1)}, u32[]{:S(2)}, u32[]{:S(2)}) collective-permute-start(bf16[2,288,256]{2,1,0:T(8,128)(2,1)S(1)} %get-tuple-element.31.refs_2_), channel_id=1, source_target_pairs={{0,8},{4,12},{8,0},{12,4},{16,24},{20,28},{24,16},{28,20},{1,9},{5... | collective-permute-start | bytes 884744 | tf_op jit(solution)/shard_map/ppermute | solution.py:602
  44.0 27.3 %collective-permute-start.10 = (bf16[4,288,256]{2,1,0:T(8,128)(2,1)}, bf16[4,288,256]{2,1,0:T(8,128)(2,1)S(1)}, u32[]{:S(2)}, u32[]{:S(2)}) collective-permute-start(bf16[4,288,256]{2,1,0:T(8,128)(2,1)} %get-tuple-element.35.own_ref), channel_id=1, source_target_pairs={{0,4},{4,0},{8,12},{12,8},{16,20},{20,16},{24,28},{28,24},{1,5},{5... | collective-permute-start | bytes 1769480 | tf_op jit(solution)/shard_map/ppermute | solution.py:602
  44.0 27.3 %collective-permute-start.11 = (bf16[4,288,256]{2,1,0:T(8,128)(2,1)}, bf16[4,288,256]{2,1,0:T(8,128)(2,1)}, u32[]{:S(2)}, u32[]{:S(2)}) collective-permute-start(bf16[4,288,256]{2,1,0:T(8,128)(2,1)} %get-tuple-element.36.own_ref), channel_id=1, source_target_pairs={{0,4},{4,0},{8,12},{12,8},{16,20},{20,16},{24,28},{28,24},{1,5},{5... | collective-permute-start | bytes 1769480 | tf_op jit(solution)/shard_map/ppermute | solution.py:601
  44.5 14.6 %collective-permute-start.6 = (bf16[192,1152]{1,0:T(8,128)(2,1)}, bf16[192,1152]{1,0:T(8,128)(2,1)S(1)}, u32[]{:S(2)}, u32[]{:S(2)}) collective-permute-start(bf16[192,1152]{1,0:T(8,128)(2,1)} %copy-done.12), channel_id=1, source_target_pairs={{0,1},{1,0},{2,3},{3,2},{4,5},{5,4},{6,7},{7,6},{8,9},{9,8},{10,11... | collective-permute-start | bytes 1327112 | tf_op jit(solution)/shard_map/ppermute | solution.py:603
  48.0 20.0 %collective-permute-start.9 = (bf16[192,1152]{1,0:T(8,128)(2,1)}, bf16[192,1152]{1,0:T(8,128)(2,1)S(1)}, u32[]{:S(2)}, u32[]{:S(2)}) collective-permute-start(bf16[192,1152]{1,0:T(8,128)(2,1)} %copy-done.13), channel_id=1, source_target_pairs={{0,1},{1,0},{2,3},{3,2},{4,5},{5,4},{6,7},{7,6},{8,9},{9,8},{10,11... | collective-permute-start | bytes 1327112 | tf_op jit(solution)/shard_map/ppermute | solution.py:603
  76.7 20.2 %collective-permute-start.12 = (bf16[784,256]{1,0:T(8,128)(2,1)S(1)}, bf16[784,256]{1,0:T(8,128)(2,1)S(1)}, u32[]{:S(2)}, u32[]{:S(2)}) collective-permute-start(bf16[784,256]{1,0:T(8,128)(2,1)S(1)} %far.2.rest_0_), channel_id=1, source_target_pairs={{0,2},{1,3},{2,0},{3,1},{4,6},{5,7},{6,4},{7,5},{8,10},{9,11},{10,... | collective-permute-start | bytes 1204232 | tf_op jit(solution)/shard_map/ppermute | solution.py:617
  99.4 7.0 %collective-permute-start.14 = (bf16[32,1152]{1,0:T(8,128)(2,1)S(1)}, bf16[32,1152]{1,0:T(8,128)(2,1)S(1)}, u32[]{:S(2)}, u32[]{:S(2)}) collective-permute-start(bf16[32,1152]{1,0:T(8,128)(2,1)S(1)} %get-tuple-element.39), channel_id=1, source_target_pairs={{0,2},{1,3},{2,0},{3,1},{4,6},{5,7},{6,4},{7,5},{8,10},{9,11},{10,... | collective-permute-start | bytes 221192 | tf_op jit(solution)/shard_map/ppermute | solution.py:636
  99.4 7.0 %collective-permute-start.13 = (bf16[32,1152]{1,0:T(8,128)(2,1)S(1)}, bf16[32,1152]{1,0:T(8,128)(2,1)S(1)}, u32[]{:S(2)}, u32[]{:S(2)}) collective-permute-start(bf16[32,1152]{1,0:T(8,128)(2,1)S(1)} %get-tuple-element.38), channel_id=1, source_target_pairs={{0,1},{1,2},{2,3},{3,0},{4,5},{5,6},{6,7},{7,4},{8,9},{9,10},{10,1... | collective-permute-start | bytes 221192 | tf_op jit(solution)/shard_map/ppermute | solution.py:636
  107.2 18.3 %collective-permute-start.16 = (bf16[768,256]{1,0:T(8,128)(2,1)S(1)}, bf16[768,256]{1,0:T(8,128)(2,1)S(1)}, u32[]{:S(2)}, u32[]{:S(2)}) collective-permute-start(bf16[768,256]{1,0:T(8,128)(2,1)S(1)} %far.3.after_ref), channel_id=1, source_target_pairs={{0,2},{1,3},{2,0},{3,1},{4,6},{5,7},{6,4},{7,5},{8,10},{9,11},{10,... | collective-permute-start | bytes 1179656 | tf_op jit(solution)/shard_map/ppermute | solution.py:621
  108.3 19.4 %collective-permute-start.17 = (bf16[784,128]{1,0:T(8,128)(2,1)S(1)}, bf16[784,128]{1,0:T(8,128)(2,1)S(1)}, u32[]{:S(2)}, u32[]{:S(2)}) collective-permute-start(bf16[784,128]{1,0:T(8,128)(2,1)S(1)} %get-tuple-element.37.after_ref.rest_4_), channel_id=1, source_target_pairs={{0,8},{4,12},{1,9},{5,13},{2,10},{6,14},{3,11},{7,15},{16,24},{20,... | collective-permute-start | bytes 602120 | tf_op jit(solution)/shard_map/ppermute | solution.py:631
  109.6 18.1 %collective-permute-start.19 = (bf16[784,128]{1,0:T(8,128)(2,1)S(1)}, bf16[784,128]{1,0:T(8,128)(2,1)S(1)}, u32[]{:S(2)}, u32[]{:S(2)}) collective-permute-start(bf16[784,128]{1,0:T(8,128)(2,1)S(1)} %get-tuple-element.37.after_ref.rest_4_), channel_id=1, source_target_pairs={{0,4},{4,8},{8,12},{1,5},{5,9},{9,13},{2,6},{6,10},{10,14},{3,7},{... | collective-permute-start | bytes 602120 | tf_op jit(solution)/shard_map/ppermute | solution.py:631
  111.6 14.0 %collective-permute-start.18 = (bf16[128,768]{1,0:T(8,128)(2,1)S(1)}, bf16[128,768]{1,0:T(8,128)(2,1)S(1)}, u32[]{:S(2)}, u32[]{:S(2)}) collective-permute-start(bf16[128,768]{1,0:T(8,128)(2,1)S(1)} %get-tuple-element.42.rest_5_), channel_id=1, source_target_pairs={{0,8},{4,12},{1,9},{5,13},{2,10},{6,14},{3,11},{7,15},{16,24},{20,... | collective-permute-start | bytes 589832 | tf_op jit(solution)/shard_map/ppermute | solution.py:631
  112.9 14.9 %collective-permute-start.20 = (bf16[128,768]{1,0:T(8,128)(2,1)S(1)}, bf16[128,768]{1,0:T(8,128)(2,1)S(1)}, u32[]{:S(2)}, u32[]{:S(2)}) collective-permute-start(bf16[128,768]{1,0:T(8,128)(2,1)S(1)} %get-tuple-element.42.rest_5_), channel_id=1, source_target_pairs={{0,4},{4,8},{8,12},{1,5},{5,9},{9,13},{2,6},{6,10},{10,14},{3,7},{... | collective-permute-start | bytes 589832 | tf_op jit(solution)/shard_map/ppermute | solution.py:631
  135.6 13.5 %collective-permute-start.24 = (bf16[384,256]{1,0:T(8,128)(2,1)S(1)}, bf16[384,256]{1,0:T(8,128)(2,1)}, u32[]{:S(2)}, u32[]{:S(2)}) collective-permute-start(bf16[384,256]{1,0:T(8,128)(2,1)S(1)} %attend.2.after_ref.rest_0_), channel_id=1, source_target_pairs={{0,2},{1,3},{2,0},{3,1},{4,6},{5,7},{6,4},{7,5},{8,10},{9,11},{10,... | collective-permute-start | bytes 589832 | tf_op jit(solution)/shard_map/ppermute | solution.py:649
  143.6 8.6 %collective-permute-start.21 = (bf16[384,256]{1,0:T(8,128)(2,1)S(1)}, bf16[384,256]{1,0:T(8,128)(2,1)S(1)}, u32[]{:S(2)}, u32[]{:S(2)}) collective-permute-start(bf16[384,256]{1,0:T(8,128)(2,1)S(1)} %attend.3.rest_0_), channel_id=1, source_target_pairs={{0,2},{1,3},{2,0},{3,1},{4,6},{5,7},{6,4},{7,5},{8,10},{9,11},{10,... | collective-permute-start | bytes 589832 | tf_op jit(solution)/shard_map/ppermute | solution.py:649
  145.3 10.0 %collective-permute-start.25 = (bf16[384,256]{1,0:T(8,128)(2,1)S(1)}, bf16[384,256]{1,0:T(8,128)(2,1)S(1)}, u32[]{:S(2)}, u32[]{:S(2)}) collective-permute-start(bf16[384,256]{1,0:T(8,128)(2,1)S(1)} %attend.2.after_ref.rest_0_), channel_id=1, source_target_pairs={{0,1},{1,0},{2,3},{3,2},{4,5},{5,4},{6,7},{7,6},{8,9},{9,8},{10,11... | collective-permute-start | bytes 589832 | tf_op jit(solution)/shard_map/ppermute | solution.py:650
  149.1 10.4 %collective-permute-start.26 = (bf16[384,256]{1,0:T(8,128)(2,1)}, bf16[384,256]{1,0:T(8,128)(2,1)S(1)}, u32[]{:S(2)}, u32[]{:S(2)}) collective-permute-start(bf16[384,256]{1,0:T(8,128)(2,1)} %collective-permute-done.24.rest_1_), channel_id=1, source_target_pairs={{0,1},{1,0},{2,3},{3,2},{4,5},{5,4},{6,7},{7,6},{8,9},{9,8},{10,11... | collective-permute-start | bytes 589832 | tf_op jit(solution)/shard_map/ppermute | solution.py:651
  149.1 19.9 %collective-permute-start.22 = (bf16[384,256]{1,0:T(8,128)(2,1)S(1)}, bf16[384,256]{1,0:T(8,128)(2,1)S(1)}, u32[]{:S(2)}, u32[]{:S(2)}) collective-permute-start(bf16[384,256]{1,0:T(8,128)(2,1)S(1)} %attend.3.rest_0_), channel_id=1, source_target_pairs={{0,1},{1,0},{2,3},{3,2},{4,5},{5,4},{6,7},{7,6},{8,9},{9,8},{10,11... | collective-permute-start | bytes 589832 | tf_op jit(solution)/shard_map/ppermute | solution.py:650
  152.1 16.9 %collective-permute-start.23 = (bf16[384,256]{1,0:T(8,128)(2,1)S(1)}, bf16[384,256]{1,0:T(8,128)(2,1)S(1)}, u32[]{:S(2)}, u32[]{:S(2)}) collective-permute-start(bf16[384,256]{1,0:T(8,128)(2,1)S(1)} %collective-permute-done.21.rest_1_), channel_id=1, source_target_pairs={{0,1},{1,0},{2,3},{3,2},{4,5},{5,4},{6,7},{7,6},{8,9},{9,8},{10,11... | collective-permute-start | bytes 589832 | tf_op jit(solution)/shard_map/ppermute | solution.py:651
  165.1 10.0 %collective-permute-start.30 = (f32[1,384]{1,0:T(1,128)S(1)}, f32[1,384]{1,0:T(1,128)S(1)}, u32[]{:S(2)}, u32[]{:S(2)}) collective-permute-start(f32[1,384]{1,0:T(1,128)S(1)} %get-tuple-element.43.rest_4_.rest_0_), channel_id=1, source_target_pairs={{0,1},{1,2},{2,3},{3,0},{4,5},{5,6},{6,7},{7,4},{8,9},{9,10},{10,1... | collective-permute-start | bytes 4616 | tf_op jit(solution)/shard_map/ppermute | solution.py:660
  165.2 12.8 %collective-permute-start.31 = (f32[1,384]{1,0:T(1,128)S(1)}, f32[1,384]{1,0:T(1,128)S(1)}, u32[]{:S(2)}, u32[]{:S(2)}) collective-permute-start(f32[1,384]{1,0:T(1,128)S(1)} %get-tuple-element.43.rest_4_.rest_0_), channel_id=1, source_target_pairs={{0,2},{1,3},{2,0},{3,1},{4,6},{5,7},{6,4},{7,5},{8,10},{9,11},{10,... | collective-permute-start | bytes 4616 | tf_op jit(solution)/shard_map/ppermute | solution.py:660
  165.6 12.4 %collective-permute-start.32 = (f32[1,384]{1,0:T(1,128)S(1)}, f32[1,384]{1,0:T(1,128)S(1)}, u32[]{:S(2)}, u32[]{:S(2)}) collective-permute-start(f32[1,384]{1,0:T(1,128)S(1)} %get-tuple-element.43.rest_4_.rest_0_), channel_id=1, source_target_pairs={{0,3},{1,0},{2,1},{3,2},{4,7},{5,4},{6,5},{7,6},{8,11},{9,8},{10,9... | collective-permute-start | bytes 4616 | tf_op jit(solution)/shard_map/ppermute | solution.py:660
  173.0 7.0 %collective-permute-start.27 = (f32[1,384]{1,0:T(1,128)S(1)}, f32[1,384]{1,0:T(1,128)S(1)}, u32[]{:S(2)}, u32[]{:S(2)}) collective-permute-start(f32[1,384]{1,0:T(1,128)S(1)} %get-tuple-element.45.rest_0_), channel_id=1, source_target_pairs={{0,1},{1,2},{2,3},{3,0},{4,5},{5,6},{6,7},{7,4},{8,9},{9,10},{10,1... | collective-permute-start | bytes 4616 | tf_op jit(solution)/shard_map/ppermute | solution.py:660
  173.6 6.4 %collective-permute-start.28 = (f32[1,384]{1,0:T(1,128)S(1)}, f32[1,384]{1,0:T(1,128)S(1)}, u32[]{:S(2)}, u32[]{:S(2)}) collective-permute-start(f32[1,384]{1,0:T(1,128)S(1)} %get-tuple-element.45.rest_0_), channel_id=1, source_target_pairs={{0,2},{1,3},{2,0},{3,1},{4,6},{5,7},{6,4},{7,5},{8,10},{9,11},{10,... | collective-permute-start | bytes 4616 | tf_op jit(solution)/shard_map/ppermute | solution.py:660
  (19 other events, 105.8 us)
Sparse Core Ops, SparseCore 0:
  107.3 26.7 all-gather.2

commit v9 on v8

--- a/solution.py
+++ b/solution.py
@@ -151,46 +151,40 @@
     )(jnp.stack([row] + columns), o_weight, after)
 
 
-def prep_kernel(src_ref, gain_ref, *rest, cuts):
-    x_refs, (out_ref, sq_ref) = rest[:-2], rest[-2:]
-    squares, at = [], 0
-    for k, pieces in enumerate(cuts):
-        column, row = [], 0
-        for x_ref in x_refs[at : at + pieces]:
-            x = x_ref[...].astype(F32)
-            column.append(jnp.sum(x * x, axis=1, keepdims=True))
-            out_ref[k, row : row + x.shape[0]] = (x * gain_ref[src_ref[k]]).astype(BF16)
-            row += x.shape[0]
-        squares.append(jnp.concatenate(column, axis=0))
-        at += pieces
-    sq_ref[...] = to_row(sum(squares[1:], squares[0]))
-
-
-def prep(sources, gains, blocks):
-    rows, cols = blocks[0][0].shape
-    dims = (len(blocks), rows, cols)
-    pieces = [piece for block in blocks for piece in block]
-    return pl.pallas_call(
-        partial(prep_kernel, cuts=[len(block) for block in blocks]),
-        out_shape=(shape(dims, BF16), shape((1, rows), F32)),
+def lay_kernel(place_ref, own_ref, got_ref, out_ref, sems, *, order):
+    held, others, share, _ = own_ref.shape
+    copies = []
+    for i, mask in enumerate(order):
+        piece = own_ref.at[i] if i < held else got_ref.at[i - held]
+        row = pl.multiple_of((place_ref[0] ^ mask) * share, TAIL)
+        there = out_ref.at[:, pl.ds(row, share)]
+        copies.append(pltpu.make_async_copy(piece, there, sems.at[i]))
+    for copy in copies:
+        copy.start()
+    for copy in copies:
+        copy.wait()
+
+
+def lay_pieces(place, order, own, got):
+    _, others, share, cols = own.shape
+    dims = (others, len(order) * share, cols)
+    return pl.pallas_call(
+        partial(lay_kernel, order=order),
+        out_shape=shape(dims, BF16),
         grid_spec=pltpu.PrefetchScalarGridSpec(
             num_scalar_prefetch=1,
             grid=(1,),
-            in_specs=[pl.BlockSpec(gains.shape, lambda i, s: (0, 0, 0))]
-            + [pl.BlockSpec(piece.shape, lambda i, s: (0, 0)) for piece in pieces],
-            out_specs=[
-                pl.BlockSpec(dims, lambda i, s: (0, 0, 0)),
-                pl.BlockSpec((1, rows), lambda i, s: (0, 0)),
-            ],
-        ),
-        compiler_params=PARAMS,
-        name="prep",
-    )(sources, gains, *pieces)
-
-
-def far_kernel(place_ref, src_ref, x_ref, sq_ref, own_ref, got_ref, *rest, order, with_sq):
-    out_ref, weight, sems = rest[-3:]
-    held, share, width = own_ref.shape
+            in_specs=[ANY, ANY],
+            out_specs=pl.BlockSpec(dims, lambda i, p: (0, 0, 0)),
+            scratch_shapes=[pltpu.SemaphoreType.DMA((len(order),))],
+        ),
+        compiler_params=PARAMS,
+        name="lay",
+    )(place, own, got)
+
+
+def place_weights(place_ref, own_ref, got_ref, weight, sems, order):
+    held, share, _ = own_ref.shape
     copies = []
     for i, mask in enumerate(order):
         piece = own_ref.at[i] if i < held else got_ref.at[i - held]
@@ -199,19 +193,75 @@
         copies.append(pltpu.make_async_copy(piece, there, sems.at[i]))
     for copy in copies:
         copy.start()
-    for copy in copies:
-        copy.wait()
-    count, rows, cols = x_ref.shape
+    return copies
+
+
+def far_sum(src_ref, x_ref, weight):
+    count, _, cols = x_ref.shape
     total = None
     for k in range(count):
         row = pl.multiple_of(src_ref[k] * cols, TAIL)
         term = jnp.dot(x_ref[k], weight[pl.ds(row, cols), :], preferred_element_type=F32)
         total = term if total is None else total + term
-    out_ref[:rows, :] = total.astype(BF16)
-    if with_sq:
-        sq = sq_ref[...]
-        high = sq.astype(BF16).astype(F32)
-        out_ref[rows:, :] = lines_of((high, sq - high), width)
+    return total
+
+
+def far_kv_kernel(place_ref, src_ref, gain_ref, own_ref, got_ref, *rest, order, cuts):
+    x_refs, (out_ref, x_out, sq_ref, weight, sems) = rest[: sum(cuts)], rest[-5:]
+    copies = place_weights(place_ref, own_ref, got_ref, weight, sems, order)
+    rows = x_out.shape[1]
+    columns, at = [], 0
+    for k, pieces in enumerate(cuts):
+        gain = gain_ref[place_ref[1] + src_ref[k]]
+        column, row = [], 0
+        for x_ref in x_refs[at : at + pieces]:
+            x = x_ref[...].astype(F32)
+            column.append(jnp.sum(x * x, axis=1, keepdims=True))
+            x_out[k, row : row + x.shape[0]] = (x * gain).astype(BF16)
+            row += x.shape[0]
+        columns.append(jnp.concatenate(column, axis=0))
+        at += pieces
+    sq = to_row(sum(columns[1:], columns[0]))
+    sq_ref[...] = sq
+    for copy in copies:
+        copy.wait()
+    out_ref[:rows, :] = far_sum(src_ref, x_out, weight).astype(BF16)
+    high = sq.astype(BF16).astype(F32)
+    out_ref[rows:, :] = lines_of((high, sq - high), out_ref.shape[1])
+
+
+def far_kv_product(place, sources, gains, blocks, gathered, after):
+    order, own, got = gathered
+    _, share, width = own.shape
+    rows, cols = blocks[0][0].shape
+    pieces = [piece for block in blocks for piece in block]
+    dims = [(rows + TAIL, width), (len(blocks), rows, cols), (1, rows)]
+    whole = lambda d: pl.BlockSpec(d, lambda i, p, s: (0,) * len(d))
+    return pl.pallas_call(
+        partial(far_kv_kernel, order=order, cuts=[len(block) for block in blocks]),
+        out_shape=tuple(shape(d, t) for d, t in zip(dims, (BF16, BF16, F32))),
+        grid_spec=pltpu.PrefetchScalarGridSpec(
+            num_scalar_prefetch=2,
+            grid=(1,),
+            in_specs=[whole(gains.shape), ANY, ANY]
+            + [whole(piece.shape) for piece in pieces]
+            + [ANY for _ in after],
+            out_specs=[whole(d) for d in dims],
+            scratch_shapes=[
+                pltpu.VMEM((len(order) * share, width), BF16),
+                pltpu.SemaphoreType.DMA((len(order),)),
+            ],
+        ),
+        compiler_params=PARAMS,
+        name="far_kv",
+    )(place, sources, gains, own, got, *pieces, *after)
+
+
+def far_kernel(place_ref, src_ref, x_ref, own_ref, got_ref, *rest, order):
+    out_ref, weight, sems = rest[-3:]
+    for copy in place_weights(place_ref, own_ref, got_ref, weight, sems, order):
+        copy.wait()
+    out_ref[...] = far_sum(src_ref, x_ref, weight).astype(BF16)
 
 
 def lines_of(rows, width):
@@ -236,25 +286,19 @@
     return rows
 
 
-def far_product(place, sources, x, sq, gathered, with_sq, after):
+def far_product(place, sources, x, gathered, after):
     order, own, got = gathered
     _, share, width = own.shape
     rows = x.shape[1]
-    out_rows = rows + (TAIL if with_sq else 0)
-    return pl.pallas_call(
-        partial(far_kernel, order=order, with_sq=with_sq),
-        out_shape=shape((out_rows, width), BF16),
+    return pl.pallas_call(
+        partial(far_kernel, order=order),
+        out_shape=shape((rows, width), BF16),
         grid_spec=pltpu.PrefetchScalarGridSpec(
             num_scalar_prefetch=2,
             grid=(1,),
-            in_specs=[
-                pl.BlockSpec(x.shape, lambda i, p, s: (0, 0, 0)),
-                pl.BlockSpec((1, rows), lambda i, p, s: (0, 0)),
-                ANY,
-                ANY,
-            ]
+            in_specs=[pl.BlockSpec(x.shape, lambda i, p, s: (0, 0, 0)), ANY, ANY]
             + [ANY for _ in after],
-            out_specs=pl.BlockSpec((out_rows, width), lambda i, p, s: (0, 0)),
+            out_specs=pl.BlockSpec((rows, width), lambda i, p, s: (0, 0)),
             scratch_shapes=[
                 pltpu.VMEM((len(order) * share, width), BF16),
                 pltpu.SemaphoreType.DMA((len(order),)),
@@ -262,7 +306,7 @@
         ),
         compiler_params=PARAMS,
         name="far",
-    )(place, sources, x, sq, own, got, *after)
+    )(place, sources, x, own, got, *after)
 
 
 def near_kernel(src_ref, x_ref, k_ref, v_ref, q_ref, after_ref, out_ref):
@@ -299,8 +343,9 @@
 
 
 def keys_kernel(
-    near_ref, far_ref, sq_ref, id_ref, cos_ref, sin_ref, after_ref, k_out, vt_out, sum_ref, *, model
+    near_ref, far_ref, sq_ref, id_ref, cos_ref, sin_ref, *rest, model
 ):
+    k_out, vt_out, sum_ref = rest[-3:]
     rows = near_ref.shape[0]
     tail = far_ref[rows:, :].astype(F32)
     total = sum(rows_of(tail, 2, rows), sq_ref[...])
@@ -324,11 +369,11 @@
         grid=(1,),
         in_specs=[pl.BlockSpec((rows, width), whole)]
         + [pl.BlockSpec(a.shape, whole) for a in (far, sq, ids, cosine, sine)]
-        + [ANY],
+        + [ANY for _ in after],
         out_specs=[pl.BlockSpec(d, whole) for d in dims],
         compiler_params=PARAMS,
         name="keys",
-    )(near, far, sq, ids, cosine, sine, after)
+    )(near, far, sq, ids, cosine, sine, *after)
 
 
 def attention_kernel(
@@ -460,10 +505,9 @@
 def output_kernel(at_ref, own_o_ref, o_ref, *rest):
     ctx_refs, (after_ref, out_ref, sq_ref, acc) = rest[:-4], rest[-4:]
     step = pl.program_id(0)
-    plane, _, share, tile = o_ref.shape
     total = jnp.dot(ctx_refs[0][...], own_o_ref[...], preferred_element_type=F32)
     for i, ctx_ref in enumerate(ctx_refs[1:]):
-        weight = o_ref[:, at_ref[1 + i]].reshape(plane * share, tile)
+        weight = o_ref[at_ref[1 + i]]
         total = total + jnp.dot(ctx_ref[...], weight, preferred_element_type=F32)
     out_ref[...] = total
     squares = jnp.sum(total * total, axis=1, keepdims=True)
@@ -484,7 +528,7 @@
 
 def output_product(column, order, o_weight, gathered, contexts, after):
     chunk, width = contexts[0].shape
-    plane, others, share, cols = gathered.shape
+    others, _, cols = gathered.shape
     tiles = 3 if cols % (3 * LANES) == 0 else 1
     tile = cols // tiles
     if cols % LANES:
@@ -498,7 +542,7 @@
             grid=(tiles,),
             in_specs=[
                 pl.BlockSpec((width, tile), lambda i, at: (0, at[0] * tiles + i)),
-                pl.BlockSpec((plane, others, share, tile), lambda i, at: (0, 0, 0, i)),
+                pl.BlockSpec((others, width, tile), lambda i, at: (0, 0, i)),
             ]
             + [pl.BlockSpec((chunk, width), lambda i, at: (0, 0)) for _ in contexts]
             + [ANY],
@@ -574,11 +618,9 @@
     at = jnp.reshape((1 - side) * plane + in_plane, (1,))
     inner = seq_bits + group_bits
     masks_kv, masks_q = inner + [1], inner[::-1] + [1]
-    steps = len(masks_kv)
-    piece = rows // (steps + 1) // TAIL * TAIL
-    counts = [rows - steps * piece] + [piece] * steps
-    if counts[0] > piece:
-        counts = [rows - steps * (piece + TAIL)] + [piece + TAIL] * steps
+    last = len(masks_kv) - 1
+    third = rows // 3 // TAIL * TAIL
+    counts = [rows - 2 * third, third, third]
     packed_kv, packed_q, cut = pack(
         at, q_weight, k_weight, value_weight, share, tokens, counts[0]
     )
@@ -587,42 +629,64 @@
     received = [lax.ppermute(cut, "tensor", ring)]
     order_kv, order_q, first = [0], [0], counts[0]
     for step, (mask_kv, mask_q) in enumerate(zip(masks_kv, masks_q)):
+        after, count = [], 0
         if step == 0:
-            (cut,) = stage([], tokens, first, counts[1], [own_kv, own_q, received[0]])
+            pairs, after = [], [own_kv, own_q, received[0]]
         else:
-            own_kv, own_q, cut = stage(
-                [(own_kv, far_kv), (own_q, far_q)],
-                tokens,
-                first,
-                counts[step + 1],
-                received[-2:-1],
-            )
-        first += counts[step + 1]
+            pairs = [(own_kv, far_kv), (own_q, far_q)]
+        if step < 2:
+            count = counts[1 + step]
+        if step == last:
+            o_share = o_weight.shape[0] // plane
+            columns = [(z + k) % nz * cols for k in range(1, nz)]
+            pieces = cut_pieces(in_plane * o_share, columns, o_weight, o_share, cols, own_kv)
+            moved = [lax.ppermute(p, "tensor", turn(k + 1)) for k, p in enumerate(pieces)]
+            own_o = jnp.stack(moved)[None]
+            after = [received[1], own_o]
+        outs = stage(pairs, tokens, first, count, after)
+        if pairs:
+            own_kv, own_q = outs[:2]
+        if count:
+            received.append(lax.ppermute(outs[-1], "tensor", ring))
+        first += count
         far_kv = lax.ppermute(own_kv, PLANE, [(i, i ^ mask_kv) for i in range(plane)])
         far_q = lax.ppermute(own_q, PLANE, [(i, i ^ mask_q) for i in range(plane)])
-        received.append(lax.ppermute(cut, "tensor", ring))
         order_kv = order_kv + [k ^ mask_kv for k in order_kv]
         order_q = order_q + [k ^ mask_q for k in order_q]
     far_kv, far_q = (order_kv, own_kv, far_kv), (order_q, own_q, far_q)
+
+    def double(own, step, after):
+        if step > 0:
+            (own,) = stage([own], tokens, 0, 0, after)
+        return own, lax.ppermute(own, PLANE, [(i, i ^ masks_kv[step]) for i in range(plane)])
+
+    pair_o = double(own_o, 0, [])
+    for step in range(1, last - 1):
+        pair_o = double(pair_o, step, [])
 
     sources = (within + half - jnp.arange(half, dtype=jnp.int32)) % half
     blocks = [[tokens], received]
     for _ in range(half - 2):
         blocks.append([lax.ppermute(part, "tensor", ring) for part in blocks[-1]])
     gains = in_gain.reshape(nz, 1, cols)
-    x, sq = prep(side * half + sources, gains, blocks)
-
-    place = jnp.reshape(in_plane, (1,))
-    sent_kv = far_product(place, sources, x, sq, far_kv, True, [far_q[2]])
+    place = jnp.stack([in_plane, side * half])
+    sent_kv, x, sq = far_kv_product(
+        place, sources, gains, blocks, far_kv, [far_q[2], pair_o[1]]
+    )
     got_kv = lax.ppermute(sent_kv, "tensor", swap)
+    pair_o = double(pair_o, last - 1, [sent_kv])
     weights = (k_weight, value_weight, q_weight)
 
-    sent_q = far_product(place, sources, x, sq, far_q, False, [sent_kv])
+    sent_q = far_product(place, sources, x, far_q, [sent_kv])
     got_q = lax.ppermute(sent_q, "tensor", swap)
     near = near_product(side * half + sources, x, weights, sent_q)
     cosine, sine = rotation_table(seq * rows + jnp.arange(rows, dtype=jnp.int32))
     ids = seg_ids[None, :]
-    *own_kv, sums = keys_values(near, got_kv, sq, ids, cosine, sine, sent_q, model)
+    *own_kv, sums = keys_values(
+        near, got_kv, sq, ids, cosine, sine, [sent_q, pair_o[1]], model
+    )
+    pair_o = double(pair_o, last, [own_kv[0]])
+    gathered_o = lay_pieces(place, order_kv, *pair_o)
 
     back = -(-(nseq * rows // 2 - 1) // rows)
     kv_blocks = [own_kv]
@@ -630,29 +694,22 @@
         earlier = [(i, i + k) for i in range(nseq - k)]
         kv_blocks.insert(0, [lax.ppermute(part, "seq", earlier) for part in own_kv])
 
-    o_share = o_weight.shape[0] // plane
-    columns = [(z + k) % nz * cols for k in range(1, nz)]
-    pieces = cut_pieces(in_plane * o_share, columns, o_weight, o_share, cols, own_kv[0])
-    moved = [lax.ppermute(p, "tensor", turn(k + 1)) for k, p in enumerate(pieces)]
-    moved = jnp.stack(moved)
-    gathered_o = lax.all_gather(moved, PLANE)
-
     out = None
     seq_at = jnp.reshape(seq, (1,))
-    context, own_sq = moved, place
+    after, own_sq = pair_o[1], place
     for c in range(CHUNKS):
         context = attend(
-            seq_at, near, got_q, sums, cosine, sine, ids, context, kv_blocks, c, model
+            seq_at, near, got_q, sums, cosine, sine, ids, after, kv_blocks, c, model
         )
         if nz == 4:
             pairs = [(i, i ^ 1) for i in range(nz)]
             opposite = lax.ppermute(context, "tensor", swap)
             beside = lax.ppermute(context, "tensor", pairs)
             across = lax.ppermute(opposite, "tensor", pairs)
-            contexts = [context, opposite, beside, across]
+            contexts, after = [context, opposite, beside, across], beside
             order = [jnp.int32(1), 2 - 2 * (z % 2), 2 * (z % 2)]
         else:
-            contexts = [context]
+            contexts, after = [context], context
             contexts += [lax.ppermute(context, "tensor", turn(k)) for k in range(1, nz)]
             order = [jnp.int32(k) for k in range(nz - 1)]
         branch, own_sq = output_product(z, order, o_weight, gathered_o, contexts, own_sq)

time: 189 us -> 169 us (0.89)
  between operations: 13.7 us -> 0.46 us
  local copies, waits for them, and re-layouts: 7.63 us -> 2.32 us
  waiting for transfers between devices: 78 us -> 72.9 us
  Pallas kernels: 45.4 us -> 49.4 us
    ppermute x3 -> x5, waiting for transfers between devices: 19.9 us -> 7.38 us  [the longest x3 7.37 us: double(): lax.ppermute(own, PLANE, [(i, i ^ masks_kv[step]) for i in range(plane)])]
    unnamed x34 -> x32, local copies, waits for them, and re-layouts: 7.6 us -> 2.29 us
    ppermute x2, waiting for transfers between devices: 4.22 us -> 0.01 us  [per_device(): across = lax.ppermute(opposite, 'tensor', pairs)]
    ppermute x3, waiting for transfers between devices: 0.82 us -> 4.97 us  [per_device(): far_q = lax.ppermute(own_q, PLANE, [(i, i ^ mask_q) for i in range(plane)])]
    ppermute x1, waiting for transfers between devices: 10.8 us -> 14.8 us  [per_device(): got_q = lax.ppermute(sent_q, 'tensor', swap)]
    ppermute x3, waiting for transfers between devices: 6.36 us -> 3.14 us  [per_device(): lax.ppermute(p, 'tensor', turn(k + 1))]
    ppermute x1, waiting for transfers between devices: 11.1 us -> 14.3 us  [per_device(): own_kv = lax.ppermute(packed_kv, 'tensor', swap)[None]]
    ppermute x4, waiting for transfers between devices: 2.16 us -> 5 us  [per_device(): kv_blocks.insert(0, [lax.ppermute(part, 'seq', earlier) for part in own_kv])]
  transfers between devices with their start and end apart: 34 -> 35, of which waited for: 15 -> 16; matrix products, arithmetic and copies ran while one was open for 1% -> 1% of each run, Pallas kernels for 19% -> 19%
where the time goes in v9:
time: 169 us; the launch traced here: 168 us
  waiting for transfers between devices  72.9 us (43%)
  Pallas kernels  49.4 us (29%)
  starting transfers between devices  41.2 us (24%)
  local copies, waits for them, and re-layouts  2.32 us (1%)
  other arithmetic  2.02 us (1%)
    ppermute x1, waiting for transfers between devices, per_device(): got_q = lax.ppermute(sent_q, 'tensor', swap)  14.8 us
    ppermute x1, waiting for transfers between devices, per_device(): own_kv = lax.ppermute(packed_kv, 'tensor', swap)[None]  14.3 us
    pallas_call x2, Pallas kernels, attend(): pl.pallas_call(partial(attention_kernel, back=back, offset=c * rows, mode...  12.1 us
    ppermute x6, starting transfers between devices, per_device(): squares += [lax.ppermute(own_sq, 'tensor', turn(k)) for k in range(1, nz)]  9.53 us
    pallas_call x2, Pallas kernels, output_product(): pl.pallas_call(output_kernel, out_shape=(shape((chunk, cols), F32), shape...  8.39 us
    ppermute x3, waiting for transfers between devices, double(): lax.ppermute(own, PLANE, [(i, i ^ masks_kv[step]) for i in range(plane)])  7.37 us
    ppermute x4, starting transfers between devices, per_device(): kv_blocks.insert(0, [lax.ppermute(part, 'seq', earlier) for part in own_kv])  6.87 us
    ppermute x1, waiting for transfers between devices, per_device(): got_kv = lax.ppermute(sent_kv, 'tensor', swap)  6.42 us
  transfers between devices with their start and end apart: 35, of which 16 were waited for; matrix products, arithmetic and copies ran while one was open for 1% of the time, Pallas kernels for 19%

profile of v9, /device:TPU:2, one launch (start us, length us, event | category | flops | bytes accessed | tf_op | source)
XLA Modules:
  0.0 168.3 jit_solution(14470813961988397968)
XLA Ops:
  0.0 2.3 %pack.1 = (bf16[288,256]{1,0:T(8,128)(2,1)}, bf16[288,256]{1,0:T(8,128)(2,1)}, bf16[256,1152]{1,0:T(8,128)(2,1)}) custom-call(s32[1]{0:T(128)} %bitcast.9.at_ref, bf16[4608,256]{1,0:T(8,128)(2,1)} %q_ref.3, bf16[4608,128]{1,0:T(8,128)(2,1)} %k_ref.3, bf16[4608,128]{1,0:T(8,128)(2,1)} %v_ref.3, bf16[768,1152]{1,0:T(8,128)(2,1)} %token_ref.3), custom_call_target="tpu_custom_call" | custom-call | tf_op jit(solution)/shard_map/pack/pallas_call | solution.py:74
  3.9 2.6 %collective-permute-start = (bf16[288,256]{1,0:T(8,128)(2,1)}, bf16[288,256]{1,0:T(8,128)(2,1)S(1)}, u32[]{:S(2)}, u32[]{:S(2)}) collective-permute-start(bf16[288,256]{1,0:T(8,128)(2,1)} %get-tuple-element.26), channel_id=1, source_target_pairs={{0,2},{1,3},{2,0},{3,1},{4,6},{5,7},{6,4},{7,5},{8,10},{9,11},{10,... | collective-permute-start | bytes 442376 | tf_op jit(solution)/shard_map/ppermute | solution.py:627
  6.9 14.3 %collective-permute-done = bf16[288,256]{1,0:T(8,128)(2,1)S(1)} collective-permute-done((bf16[288,256]{1,0:T(8,128)(2,1)}, bf16[288,256]{1,0:T(8,128)(2,1)S(1)}, u32[]{:S(2)}, u32[]{:S(2)}) %collective-permute-start) | collective-permute-done | bytes 147488 | tf_op jit(solution)/shard_map/ppermute | solution.py:627
  21.1 2.0 %collective-permute-done.2 = bf16[288,256]{1,0:T(8,128)(2,1)S(1)} collective-permute-done((bf16[288,256]{1,0:T(8,128)(2,1)}, bf16[288,256]{1,0:T(8,128)(2,1)S(1)}, u32[]{:S(2)}, u32[]{:S(2)}) %collective-permute-start.2) | collective-permute-done | bytes 147488 | tf_op jit(solution)/shard_map/ppermute | solution.py:628
  24.9 2.7 %collective-permute-start.11 = (bf16[256,1152]{1,0:T(8,128)(2,1)}, bf16[256,1152]{1,0:T(8,128)(2,1)S(1)}, u32[]{:S(2)}, u32[]{:S(2)}) collective-permute-start(bf16[256,1152]{1,0:T(8,128)(2,1)} %stage.6), channel_id=1, source_target_pairs={{0,1},{1,0},{2,3},{3,2},{4,5},{5,4},{6,7},{7,6},{8,9},{9,8},{10,11... | collective-permute-start | bytes 1769480 | tf_op jit(solution)/shard_map/ppermute | solution.py:650
  29.7 3.0 %collective-permute-done.1.refs_1_ = bf16[1,288,256]{2,1,0:T(8,128)(2,1)S(1)} collective-permute-done((bf16[1,288,256]{2,1,0:T(8,128)(2,1)S(1)}, bf16[1,288,256]{2,1,0:T(8,128)(2,1)S(1)}, u32[]{:S(2)}, u32[]{:S(2)}) %collective-permute-start.1) | collective-permute-done | bytes 147488 | tf_op jit(solution)/shard_map/ppermute | solution.py:652
  33.4 2.3 %stage.5 = (bf16[2,288,256]{2,1,0:T(8,128)(2,1)S(1)}, bf16[2,288,256]{2,1,0:T(8,128)(2,1)S(1)}, bf16[256,1152]{1,0:T(8,128)(2,1)}) custom-call(bf16[1,288,256]{2,1,0:T(8,128)(2,1)S(1)} %bitcast.20, bf16[1,288,256]{2,1,0:T(8,128)(2,1)S(1)} %collective-permute-done.1.refs_1_, bf16[1,288,256]{2,1,0:T(8,128)(2,1)S(1)} %bitcast.23, ...), custom_call_target="tpu_custom_call" | custom-call | tf_op jit(solution)/shard_map/stage/pallas_call | solution.py:113
  38.0 1.9 %collective-permute-start.4 = (bf16[32,1152]{1,0:T(8,128)(2,1)S(1)}, bf16[32,1152]{1,0:T(8,128)(2,1)S(1)}, u32[]{:S(2)}, u32[]{:S(2)}) collective-permute-start(bf16[32,1152]{1,0:T(8,128)(2,1)S(1)} %get-tuple-element.29), channel_id=1, source_target_pairs={{0,1},{1,2},{2,3},{3,0},{4,5},{5,6},{6,7},{7,4},{8,9},{9,10},{10,1... | collective-permute-start | bytes 221192 | tf_op jit(solution)/shard_map/ppermute | solution.py:643
  41.5 2.8 %collective-permute-done.6 = bf16[32,1152]{1,0:T(8,128)(2,1)S(1)} collective-permute-done((bf16[32,1152]{1,0:T(8,128)(2,1)S(1)}, bf16[32,1152]{1,0:T(8,128)(2,1)S(1)}, u32[]{:S(2)}, u32[]{:S(2)}) %collective-permute-start.6) | collective-permute-done | bytes 73760 | tf_op jit(solution)/shard_map/ppermute | solution.py:643
  46.7 4.3 %collective-permute-done.9.refs_3_ = bf16[2,288,256]{2,1,0:T(8,128)(2,1)S(1)} collective-permute-done((bf16[2,288,256]{2,1,0:T(8,128)(2,1)S(1)}, bf16[2,288,256]{2,1,0:T(8,128)(2,1)S(1)}, u32[]{:S(2)}, u32[]{:S(2)}) %collective-permute-start.9) | collective-permute-done | bytes 294944 | tf_op jit(solution)/shard_map/ppermute | solution.py:653
  53.1 7.4 %collective-permute-done.7.rest_5_.refs_1_ = bf16[1,3,32,1152]{3,2,1,0:T(8,128)(2,1)S(1)} collective-permute-done((bf16[1,3,32,1152]{3,2,1,0:T(8,128)(2,1)S(1)}, bf16[1,3,32,1152]{3,2,1,0:T(8,128)(2,1)S(1)}, u32[]{:S(2)}, u32[]{:S(2)}) %collective-permute-start.7) | collective-permute-done | bytes 221216 | tf_op jit(solution)/shard_map/ppermute | solution.py:661
  61.6 5.7 %far_kv.1 = (bf16[784,256]{1,0:T(8,128)(2,1)S(1)}, bf16[2,768,1152]{2,1,0:T(8,128)(2,1)}, f32[1,768]{1,0:T(1,128)S(1)}) custom-call(s32[2]{0:T(128)S(1)} %get-tuple-element.51.place_ref.rest_4_, s32[2]{0:T(128)S(1)} %get-tuple-element.50.src_ref, f32[4,1,1152]{2,1,0:T(1,128)S(1)} %reshape.21.gain_ref, bf16[4,288,256]{2,1,0:T(8,128)(2,1)} %get-tuple-element.34.own_ref, ...), custom_call_target="tpu_custom_call" | custom-call | tf_op jit(solution)/shard_map/far_kv/pallas_call | solution.py:240
  72.1 3.1 %far.1.after_ref.rest_0_ = bf16[768,256]{1,0:T(8,128)(2,1)S(1)} custom-call(s32[2]{0:T(128)S(1)} %get-tuple-element.51.place_ref.rest_4_, s32[2]{0:T(128)S(1)} %get-tuple-element.50.src_ref, bf16[2,768,1152]{2,1,0:T(8,128)(2,1)S(1)} %copy-done.2, bf16[4,288,256]{2,1,0:T(8,128)(2,1)} %get-tuple-element.36.own_ref, ...), custom_call_target="tpu_custom_call" | custom-call | tf_op jit(solution)/shard_map/far/pallas_call | solution.py:293
  75.2 5.7 %near.1.near_ref = f32[768,512]{1,0:T(8,128)S(1)} custom-call(s32[2]{0:T(128)S(1)} %broadcast_add_fusion.src_ref, bf16[2,768,1152]{2,1,0:T(8,128)(2,1)} %get-tuple-element.38.x_ref, bf16[4608,128]{1,0:T(8,128)(2,1)S(1)} %copy-done.3, bf16[4608,128]{1,0:T(8,128)(2,1)S(1)} %copy-done.4, bf16[4608,256]{1,0:T(8,128)(2,1)} %q_ref.3, ...), custom_call_target="tpu_custom_call" | custom-call | tf_op jit(solution)/shard_map/near/pallas_call | solution.py:329
  80.9 6.4 %collective-permute-done.16.far_ref = bf16[784,256]{1,0:T(8,128)(2,1)S(1)} collective-permute-done((bf16[784,256]{1,0:T(8,128)(2,1)S(1)}, bf16[784,256]{1,0:T(8,128)(2,1)S(1)}, u32[]{:S(2)}, u32[]{:S(2)}) %collective-permute-start.16) | collective-permute-done | bytes 401440 | tf_op jit(solution)/shard_map/ppermute | solution.py:676
  89.8 2.3 %collective-permute-start.21 = (bf16[784,128]{1,0:T(8,128)(2,1)S(1)}, bf16[784,128]{1,0:T(8,128)(2,1)S(1)}, u32[]{:S(2)}, u32[]{:S(2)}) collective-permute-start(bf16[784,128]{1,0:T(8,128)(2,1)S(1)} %get-tuple-element.40.refs_3_.rest_4_), channel_id=1, source_target_pairs={{0,4},{4,8},{8,12},{1,5},{5,9},{9,13},{2,6},{6,10},{10,14},{3,7},{... | collective-permute-start | bytes 602120 | tf_op jit(solution)/shard_map/ppermute | solution.py:695
  93.4 14.8 %collective-permute-done.18.far_ref = bf16[768,256]{1,0:T(8,128)(2,1)S(1)} collective-permute-done((bf16[768,256]{1,0:T(8,128)(2,1)S(1)}, bf16[768,256]{1,0:T(8,128)(2,1)S(1)}, u32[]{:S(2)}, u32[]{:S(2)}) %collective-permute-start.18) | collective-permute-done | bytes 393248 | tf_op jit(solution)/shard_map/ppermute | solution.py:681
  108.2 2.0 %collective-permute-start.22 = (bf16[128,768]{1,0:T(8,128)(2,1)S(1)}, bf16[128,768]{1,0:T(8,128)(2,1)S(1)}, u32[]{:S(2)}, u32[]{:S(2)}) collective-permute-start(bf16[128,768]{1,0:T(8,128)(2,1)S(1)} %get-tuple-element.42.rest_5_), channel_id=1, source_target_pairs={{0,4},{4,8},{8,12},{1,5},{5,9},{9,13},{2,6},{6,10},{10,14},{3,7},{... | collective-permute-start | bytes 589832 | tf_op jit(solution)/shard_map/ppermute | solution.py:695
  110.2 5.0 %collective-permute-done.22.rest_3_ = bf16[128,768]{1,0:T(8,128)(2,1)S(1)} collective-permute-done((bf16[128,768]{1,0:T(8,128)(2,1)S(1)}, bf16[128,768]{1,0:T(8,128)(2,1)S(1)}, u32[]{:S(2)}, u32[]{:S(2)}) %collective-permute-start.22) | collective-permute-done | bytes 196640 | tf_op jit(solution)/shard_map/ppermute | solution.py:695
  115.2 6.4 %attend.2.rest_0_ = bf16[384,256]{1,0:T(8,128)(2,1)S(1)} custom-call(s32[1]{0:T(128)} %bitcast.16.seq_ref, f32[768,512]{1,0:T(8,128)S(1)} %near.1.near_ref, bf16[768,256]{1,0:T(8,128)(2,1)S(1)} %collective-permute-done.18.far_ref, f32[1,768]{1,0:T(1,128)S(1)} %get-tuple-element.41.sum_ref, f32[768,128]{1,0:T(8,128)S(1)} %get-tuple-element.52.cos_ref, ...), custom_call_target="tpu_custom_call" | custom-call | flops 905969664 | bytes 2359296 | tf_op jit(solution)/shard_map/attend/pallas_call | solution.py:472
  121.7 2.8 %collective-permute-start.27 = (bf16[384,256]{1,0:T(8,128)(2,1)S(1)}, bf16[384,256]{1,0:T(8,128)(2,1)}, u32[]{:S(2)}, u32[]{:S(2)}) collective-permute-start(bf16[384,256]{1,0:T(8,128)(2,1)S(1)} %attend.2.rest_0_), channel_id=1, source_target_pairs={{0,2},{1,3},{2,0},{3,1},{4,6},{5,7},{6,4},{7,5},{8,10},{9,11},{10,... | collective-permute-start | bytes 589832 | tf_op jit(solution)/shard_map/ppermute | solution.py:706
  124.4 4.8 %collective-permute-done.23.after_ref.rest_2_ = bf16[384,256]{1,0:T(8,128)(2,1)S(1)} collective-permute-done((bf16[384,256]{1,0:T(8,128)(2,1)S(1)}, bf16[384,256]{1,0:T(8,128)(2,1)S(1)}, u32[]{:S(2)}, u32[]{:S(2)}) %collective-permute-start.23) | collective-permute-done | bytes 196640 | tf_op jit(solution)/shard_map/ppermute | solution.py:707
  129.2 5.8 %attend.3.rest_0_ = bf16[384,256]{1,0:T(8,128)(2,1)S(1)} custom-call(s32[1]{0:T(128)} %bitcast.16.seq_ref, f32[768,512]{1,0:T(8,128)S(1)} %near.1.near_ref, bf16[768,256]{1,0:T(8,128)(2,1)S(1)} %collective-permute-done.18.far_ref, f32[1,768]{1,0:T(1,128)S(1)} %get-tuple-element.41.sum_ref, f32[768,128]{1,0:T(8,128)S(1)} %get-tuple-element.52.cos_ref, ...), custom_call_target="tpu_custom_call" | custom-call | flops 905969664 | bytes 2359296 | tf_op jit(solution)/shard_map/attend/pallas_call | solution.py:472
  135.5 2.5 %collective-permute-start.28 = (bf16[384,256]{1,0:T(8,128)(2,1)}, bf16[384,256]{1,0:T(8,128)(2,1)}, u32[]{:S(2)}, u32[]{:S(2)}) collective-permute-start(bf16[384,256]{1,0:T(8,128)(2,1)} %collective-permute-done.27.rest_1_), channel_id=1, source_target_pairs={{0,1},{1,0},{2,3},{3,2},{4,5},{5,4},{6,7},{7,6},{8,9},{9,8},{10,11... | collective-permute-start | bytes 589832 | tf_op jit(solution)/shard_map/ppermute | solution.py:708
  138.0 5.6 %collective-permute-done.24.rest_1_ = bf16[384,256]{1,0:T(8,128)(2,1)S(1)} collective-permute-done((bf16[384,256]{1,0:T(8,128)(2,1)S(1)}, bf16[384,256]{1,0:T(8,128)(2,1)S(1)}, u32[]{:S(2)}, u32[]{:S(2)}) %collective-permute-start.24) | collective-permute-done | bytes 196640 | tf_op jit(solution)/shard_map/ppermute | solution.py:706
  146.3 4.2 %output.2 = (f32[384,1152]{1,0:T(8,128)S(1)}, f32[1,384]{1,0:T(1,128)S(1)}) custom-call(s32[4]{0:T(128)S(1)} %pad_add_fusion.at_ref, bf16[256,4608]{1,0:T(8,128)(2,1)} %own_o_ref.3, bf16[3,256,1152]{2,1,0:T(8,128)(2,1)S(1)} %lay.1.o_ref, bf16[384,256]{1,0:T(8,128)(2,1)S(1)} %copy-done.10, bf16[384,256]{1,0:T(8,128)(2,1)} %collective-permute-done.27.rest_1_, ...), custom_call_target="tpu_custom_call" | custom-call | tf_op jit(solution)/shard_map/output/pallas_call | solution.py:537
  150.5 2.1 %collective-permute-start.32 = (f32[1,384]{1,0:T(1,128)S(1)}, f32[1,384]{1,0:T(1,128)S(1)}, u32[]{:S(2)}, u32[]{:S(2)}) collective-permute-start(f32[1,384]{1,0:T(1,128)S(1)} %get-tuple-element.43.rest_4_.rest_0_), channel_id=1, source_target_pairs={{0,1},{1,2},{2,3},{3,0},{4,5},{5,6},{6,7},{7,4},{8,9},{9,10},{10,1... | collective-permute-start | bytes 4616 | tf_op jit(solution)/shard_map/ppermute | solution.py:717
  153.3 2.8 %collective-permute-start.34 = (f32[1,384]{1,0:T(1,128)S(1)}, f32[1,384]{1,0:T(1,128)S(1)}, u32[]{:S(2)}, u32[]{:S(2)}) collective-permute-start(f32[1,384]{1,0:T(1,128)S(1)} %get-tuple-element.43.rest_4_.rest_0_), channel_id=1, source_target_pairs={{0,3},{1,0},{2,1},{3,2},{4,7},{5,4},{6,5},{7,6},{8,11},{9,8},{10,9... | collective-permute-start | bytes 4616 | tf_op jit(solution)/shard_map/ppermute | solution.py:717
  156.2 4.2 %output.3 = (f32[384,1152]{1,0:T(8,128)S(1)}, f32[1,384]{1,0:T(1,128)S(1)}) custom-call(s32[4]{0:T(128)S(1)} %pad_add_fusion.at_ref, bf16[256,4608]{1,0:T(8,128)(2,1)} %own_o_ref.3, bf16[3,256,1152]{2,1,0:T(8,128)(2,1)S(1)} %lay.1.o_ref, bf16[384,256]{1,0:T(8,128)(2,1)S(1)} %attend.3.rest_0_, bf16[384,256]{1,0:T(8,128)(2,1)S(1)} %collective-permute-done.24.rest_1_, ...), custom_call_target="tpu_custom_call" | custom-call | tf_op jit(solution)/shard_map/output/pallas_call | solution.py:537
  161.8 2.5 %collective-permute-start.31 = (f32[1,384]{1,0:T(1,128)S(1)}, f32[1,384]{1,0:T(1,128)S(1)}, u32[]{:S(2)}, u32[]{:S(2)}) collective-permute-start(f32[1,384]{1,0:T(1,128)S(1)} %get-tuple-element.45.rest_0_), channel_id=1, source_target_pairs={{0,3},{1,0},{2,1},{3,2},{4,7},{5,4},{6,5},{7,6},{8,11},{9,8},{10,9... | collective-permute-start | bytes 4616 | tf_op jit(solution)/shard_map/ppermute | solution.py:717
  164.3 1.9 %finish.2.rest_4_ = bf16[768,1152]{1,0:T(8,128)(2,1)} custom-call(bf16[768,1152]{1,0:T(8,128)(2,1)S(1)} %copy-done, f32[384,1152]{1,0:T(8,128)S(1)} %get-tuple-element.46.branch_ref, f32[1,1152]{1,0:T(1,128)S(1)} %broadcast_in_dim.22.gain_ref, f32[1,384]{1,0:T(1,128)S(1)} %get-tuple-element.43.rest_4_.rest_0_, f32[1,384]{1,0:T(1,128)S(1)} %collective-permute-done.32.rest_1_, ...), custom_call_target="tpu_custom_call" | custom-call | tf_op jit(solution)/shard_map/finish/pallas_call | solution.py:585
  166.4 1.9 %finish.3 = bf16[768,1152]{1,0:T(8,128)(2,1)} custom-call(bf16[768,1152]{1,0:T(8,128)(2,1)S(1)} %copy-done, f32[384,1152]{1,0:T(8,128)S(1)} %get-tuple-element.44.branch_ref, f32[1,1152]{1,0:T(1,128)S(1)} %broadcast_in_dim.22.gain_ref, f32[1,384]{1,0:T(1,128)S(1)} %get-tuple-element.45.rest_0_, ...), custom_call_target="tpu_custom_call", output_to_operand_aliasing={{}: (7, {})} | custom-call | tf_op jit(solution)/shard_map/finish/pallas_call | solution.py:585
  (100 shorter events, 29.8 us)
Async XLA Ops:
  2.3 21.7 %collective-permute-start.10 = (bf16[256,1152]{1,0:T(8,128)(2,1)}, bf16[256,1152]{1,0:T(8,128)(2,1)S(1)}, u32[]{:S(2)}, u32[]{:S(2)}) collective-permute-start(bf16[256,1152]{1,0:T(8,128)(2,1)} %get-tuple-element.33), channel_id=1, source_target_pairs={{0,1},{1,0},{2,3},{3,2},{4,5},{5,4},{6,7},{7,6},{8,9},{9,8},{10,11... | collective-permute-start | bytes 1769480 | tf_op jit(solution)/shard_map/ppermute | solution.py:629
  3.9 17.2 %collective-permute-start = (bf16[288,256]{1,0:T(8,128)(2,1)}, bf16[288,256]{1,0:T(8,128)(2,1)S(1)}, u32[]{:S(2)}, u32[]{:S(2)}) collective-permute-start(bf16[288,256]{1,0:T(8,128)(2,1)} %get-tuple-element.26), channel_id=1, source_target_pairs={{0,2},{1,3},{2,0},{3,1},{4,6},{5,7},{6,4},{7,5},{8,10},{9,11},{10,... | collective-permute-start | bytes 442376 | tf_op jit(solution)/shard_map/ppermute | solution.py:627
  6.5 16.6 %collective-permute-start.2 = (bf16[288,256]{1,0:T(8,128)(2,1)}, bf16[288,256]{1,0:T(8,128)(2,1)S(1)}, u32[]{:S(2)}, u32[]{:S(2)}) collective-permute-start(bf16[288,256]{1,0:T(8,128)(2,1)} %get-tuple-element.27), channel_id=1, source_target_pairs={{0,2},{1,3},{2,0},{3,1},{4,6},{5,7},{6,4},{7,5},{8,10},{9,11},{10,... | collective-permute-start | bytes 442376 | tf_op jit(solution)/shard_map/ppermute | solution.py:628
  24.9 26.1 %collective-permute-start.11 = (bf16[256,1152]{1,0:T(8,128)(2,1)}, bf16[256,1152]{1,0:T(8,128)(2,1)S(1)}, u32[]{:S(2)}, u32[]{:S(2)}) collective-permute-start(bf16[256,1152]{1,0:T(8,128)(2,1)} %stage.6), channel_id=1, source_target_pairs={{0,1},{1,0},{2,3},{3,2},{4,5},{5,4},{6,7},{7,6},{8,9},{9,8},{10,11... | collective-permute-start | bytes 1769480 | tf_op jit(solution)/shard_map/ppermute | solution.py:650
  36.3 8.0 %collective-permute-start.6 = (bf16[32,1152]{1,0:T(8,128)(2,1)S(1)}, bf16[32,1152]{1,0:T(8,128)(2,1)S(1)}, u32[]{:S(2)}, u32[]{:S(2)}) collective-permute-start(bf16[32,1152]{1,0:T(8,128)(2,1)S(1)} %get-tuple-element.31), channel_id=1, source_target_pairs={{0,3},{1,0},{2,1},{3,2},{4,7},{5,4},{6,5},{7,6},{8,11},{9,8},{10,9... | collective-permute-start | bytes 221192 | tf_op jit(solution)/shard_map/ppermute | solution.py:643
  37.7 6.6 %collective-permute-start.5 = (bf16[32,1152]{1,0:T(8,128)(2,1)S(1)}, bf16[32,1152]{1,0:T(8,128)(2,1)S(1)}, u32[]{:S(2)}, u32[]{:S(2)}) collective-permute-start(bf16[32,1152]{1,0:T(8,128)(2,1)S(1)} %get-tuple-element.30), channel_id=1, source_target_pairs={{0,2},{1,3},{2,0},{3,1},{4,6},{5,7},{6,4},{7,5},{8,10},{9,11},{10,... | collective-permute-start | bytes 221192 | tf_op jit(solution)/shard_map/ppermute | solution.py:643
  38.0 8.1 %collective-permute-start.4 = (bf16[32,1152]{1,0:T(8,128)(2,1)S(1)}, bf16[32,1152]{1,0:T(8,128)(2,1)S(1)}, u32[]{:S(2)}, u32[]{:S(2)}) collective-permute-start(bf16[32,1152]{1,0:T(8,128)(2,1)S(1)} %get-tuple-element.29), channel_id=1, source_target_pairs={{0,1},{1,2},{2,3},{3,0},{4,5},{5,6},{6,7},{7,4},{8,9},{9,10},{10,1... | collective-permute-start | bytes 221192 | tf_op jit(solution)/shard_map/ppermute | solution.py:643
  40.0 6.7 %collective-permute-start.8 = (bf16[2,288,256]{2,1,0:T(8,128)(2,1)S(1)}, bf16[2,288,256]{2,1,0:T(8,128)(2,1)S(1)}, u32[]{:S(2)}, u32[]{:S(2)}) collective-permute-start(bf16[2,288,256]{2,1,0:T(8,128)(2,1)S(1)} %get-tuple-element.28.after_ref.refs_0_), channel_id=1, source_target_pairs={{0,16},{4,20},{8,24},{12,28},{16,0},{20,4},{24,8},{28,12},{1,17},{... | collective-permute-start | bytes 884744 | tf_op jit(solution)/shard_map/ppermute | solution.py:652
  44.3 6.7 %collective-permute-start.9 = (bf16[2,288,256]{2,1,0:T(8,128)(2,1)S(1)}, bf16[2,288,256]{2,1,0:T(8,128)(2,1)S(1)}, u32[]{:S(2)}, u32[]{:S(2)}) collective-permute-start(bf16[2,288,256]{2,1,0:T(8,128)(2,1)S(1)} %get-tuple-element.32.refs_2_), channel_id=1, source_target_pairs={{0,8},{4,12},{8,0},{12,4},{16,24},{20,28},{24,16},{28,20},{1,9},{5... | collective-permute-start | bytes 884744 | tf_op jit(solution)/shard_map/ppermute | solution.py:653
  44.3 16.2 %collective-permute-start.13 = (bf16[256,1152]{1,0:T(8,128)(2,1)}, bf16[256,1152]{1,0:T(8,128)(2,1)}, u32[]{:S(2)}, u32[]{:S(2)}) collective-permute-start(bf16[256,1152]{1,0:T(8,128)(2,1)} %get-tuple-element.35), channel_id=1, source_target_pairs={{0,1},{1,0},{2,3},{3,2},{4,5},{5,4},{6,7},{7,6},{8,9},{9,8},{10,11... | collective-permute-start | bytes 1769480 | tf_op jit(solution)/shard_map/ppermute | solution.py:650
  52.4 8.1 %collective-permute-start.12 = (bf16[4,288,256]{2,1,0:T(8,128)(2,1)}, bf16[4,288,256]{2,1,0:T(8,128)(2,1)}, u32[]{:S(2)}, u32[]{:S(2)}) collective-permute-start(bf16[4,288,256]{2,1,0:T(8,128)(2,1)} %get-tuple-element.34.own_ref), channel_id=1, source_target_pairs={{0,4},{4,0},{8,12},{12,8},{16,20},{20,16},{24,28},{28,24},{1,5},{5... | collective-permute-start | bytes 1769480 | tf_op jit(solution)/shard_map/ppermute | solution.py:652
  52.5 8.0 %collective-permute-start.14 = (bf16[4,288,256]{2,1,0:T(8,128)(2,1)}, bf16[4,288,256]{2,1,0:T(8,128)(2,1)S(1)}, u32[]{:S(2)}, u32[]{:S(2)}) collective-permute-start(bf16[4,288,256]{2,1,0:T(8,128)(2,1)} %get-tuple-element.36.own_ref), channel_id=1, source_target_pairs={{0,4},{4,0},{8,12},{12,8},{16,20},{20,16},{24,28},{28,24},{1,5},{5... | collective-permute-start | bytes 1769480 | tf_op jit(solution)/shard_map/ppermute | solution.py:653
  53.1 7.4 %collective-permute-start.7 = (bf16[1,3,32,1152]{3,2,1,0:T(8,128)(2,1)S(1)}, bf16[1,3,32,1152]{3,2,1,0:T(8,128)(2,1)S(1)}, u32[]{:S(2)}, u32[]{:S(2)}) collective-permute-start(bf16[1,3,32,1152]{3,2,1,0:T(8,128)(2,1)S(1)} %maximum_bitcast_fusion.refs_6_.refs_0_), channel_id=1, source_target_pairs={{0,8},{4,12},{8,0},{12,4},{16,24},{20,28},{24,16},{28,20},{1,9},{5... | collective-permute-start | bytes 663560 | tf_op jit(solution)/shard_map/ppermute | solution.py:661
  67.3 20.0 %collective-permute-start.16 = (bf16[784,256]{1,0:T(8,128)(2,1)S(1)}, bf16[784,256]{1,0:T(8,128)(2,1)S(1)}, u32[]{:S(2)}, u32[]{:S(2)}) collective-permute-start(bf16[784,256]{1,0:T(8,128)(2,1)S(1)} %get-tuple-element.37.refs_3_.rest_0_), channel_id=1, source_target_pairs={{0,2},{1,3},{2,0},{3,1},{4,6},{5,7},{6,4},{7,5},{8,10},{9,11},{10,... | collective-permute-start | bytes 1204232 | tf_op jit(solution)/shard_map/ppermute | solution.py:676
  68.7 18.6 %collective-permute-start.15 = (bf16[2,3,32,1152]{3,2,1,0:T(8,128)(2,1)S(1)}, bf16[2,3,32,1152]{3,2,1,0:T(8,128)(2,1)S(1)}, u32[]{:S(2)}, u32[]{:S(2)}) collective-permute-start(bf16[2,3,32,1152]{3,2,1,0:T(8,128)(2,1)S(1)} %stage.8.refs_0_), channel_id=1, source_target_pairs={{0,16},{4,20},{8,24},{12,28},{16,0},{20,4},{24,8},{28,12},{1,17},{... | collective-permute-start | bytes 1327112 | tf_op jit(solution)/shard_map/ppermute | solution.py:661
  88.3 26.9 %collective-permute-start.17 = (bf16[4,3,32,1152]{3,2,1,0:T(8,128)(2,1)S(1)}, bf16[4,3,32,1152]{3,2,1,0:T(8,128)(2,1)S(1)}, u32[]{:S(2)}, u32[]{:S(2)}) collective-permute-start(bf16[4,3,32,1152]{3,2,1,0:T(8,128)(2,1)S(1)} %stage.9.own_ref), channel_id=1, source_target_pairs={{0,4},{4,0},{8,12},{12,8},{16,20},{20,16},{24,28},{28,24},{1,5},{5... | collective-permute-start | bytes 2654216 | tf_op jit(solution)/shard_map/ppermute | solution.py:661
  88.4 19.8 %collective-permute-start.18 = (bf16[768,256]{1,0:T(8,128)(2,1)S(1)}, bf16[768,256]{1,0:T(8,128)(2,1)S(1)}, u32[]{:S(2)}, u32[]{:S(2)}) collective-permute-start(bf16[768,256]{1,0:T(8,128)(2,1)S(1)} %far.1.after_ref.rest_0_), channel_id=1, source_target_pairs={{0,2},{1,3},{2,0},{3,1},{4,6},{5,7},{6,4},{7,5},{8,10},{9,11},{10,... | collective-permute-start | bytes 1179656 | tf_op jit(solution)/shard_map/ppermute | solution.py:681
  88.5 26.7 %collective-permute-start.19 = (bf16[784,128]{1,0:T(8,128)(2,1)S(1)}, bf16[784,128]{1,0:T(8,128)(2,1)S(1)}, u32[]{:S(2)}, u32[]{:S(2)}) collective-permute-start(bf16[784,128]{1,0:T(8,128)(2,1)S(1)} %get-tuple-element.40.refs_3_.rest_4_), channel_id=1, source_target_pairs={{0,8},{4,12},{1,9},{5,13},{2,10},{6,14},{3,11},{7,15},{16,24},{20,... | collective-permute-start | bytes 602120 | tf_op jit(solution)/shard_map/ppermute | solution.py:695
  89.8 25.4 %collective-permute-start.21 = (bf16[784,128]{1,0:T(8,128)(2,1)S(1)}, bf16[784,128]{1,0:T(8,128)(2,1)S(1)}, u32[]{:S(2)}, u32[]{:S(2)}) collective-permute-start(bf16[784,128]{1,0:T(8,128)(2,1)S(1)} %get-tuple-element.40.refs_3_.rest_4_), channel_id=1, source_target_pairs={{0,4},{4,8},{8,12},{1,5},{5,9},{9,13},{2,6},{6,10},{10,14},{3,7},{... | collective-permute-start | bytes 602120 | tf_op jit(solution)/shard_map/ppermute | solution.py:695
  92.1 18.1 %collective-permute-start.20 = (bf16[128,768]{1,0:T(8,128)(2,1)S(1)}, bf16[128,768]{1,0:T(8,128)(2,1)S(1)}, u32[]{:S(2)}, u32[]{:S(2)}) collective-permute-start(bf16[128,768]{1,0:T(8,128)(2,1)S(1)} %get-tuple-element.42.rest_5_), channel_id=1, source_target_pairs={{0,8},{4,12},{1,9},{5,13},{2,10},{6,14},{3,11},{7,15},{16,24},{20,... | collective-permute-start | bytes 589832 | tf_op jit(solution)/shard_map/ppermute | solution.py:695
  108.2 7.0 %collective-permute-start.22 = (bf16[128,768]{1,0:T(8,128)(2,1)S(1)}, bf16[128,768]{1,0:T(8,128)(2,1)S(1)}, u32[]{:S(2)}, u32[]{:S(2)}) collective-permute-start(bf16[128,768]{1,0:T(8,128)(2,1)S(1)} %get-tuple-element.42.rest_5_), channel_id=1, source_target_pairs={{0,4},{4,8},{8,12},{1,5},{5,9},{9,13},{2,6},{6,10},{10,14},{3,7},{... | collective-permute-start | bytes 589832 | tf_op jit(solution)/shard_map/ppermute | solution.py:695
  121.6 7.6 %collective-permute-start.23 = (bf16[384,256]{1,0:T(8,128)(2,1)S(1)}, bf16[384,256]{1,0:T(8,128)(2,1)S(1)}, u32[]{:S(2)}, u32[]{:S(2)}) collective-permute-start(bf16[384,256]{1,0:T(8,128)(2,1)S(1)} %attend.2.rest_0_), channel_id=1, source_target_pairs={{0,1},{1,0},{2,3},{3,2},{4,5},{5,4},{6,7},{7,6},{8,9},{9,8},{10,11... | collective-permute-start | bytes 589832 | tf_op jit(solution)/shard_map/ppermute | solution.py:707
  121.7 13.8 %collective-permute-start.27 = (bf16[384,256]{1,0:T(8,128)(2,1)S(1)}, bf16[384,256]{1,0:T(8,128)(2,1)}, u32[]{:S(2)}, u32[]{:S(2)}) collective-permute-start(bf16[384,256]{1,0:T(8,128)(2,1)S(1)} %attend.2.rest_0_), channel_id=1, source_target_pairs={{0,2},{1,3},{2,0},{3,1},{4,6},{5,7},{6,4},{7,5},{8,10},{9,11},{10,... | collective-permute-start | bytes 589832 | tf_op jit(solution)/shard_map/ppermute | solution.py:706
  135.0 8.6 %collective-permute-start.24 = (bf16[384,256]{1,0:T(8,128)(2,1)S(1)}, bf16[384,256]{1,0:T(8,128)(2,1)S(1)}, u32[]{:S(2)}, u32[]{:S(2)}) collective-permute-start(bf16[384,256]{1,0:T(8,128)(2,1)S(1)} %attend.3.rest_0_), channel_id=1, source_target_pairs={{0,2},{1,3},{2,0},{3,1},{4,6},{5,7},{6,4},{7,5},{8,10},{9,11},{10,... | collective-permute-start | bytes 589832 | tf_op jit(solution)/shard_map/ppermute | solution.py:706
  135.5 10.8 %collective-permute-start.28 = (bf16[384,256]{1,0:T(8,128)(2,1)}, bf16[384,256]{1,0:T(8,128)(2,1)}, u32[]{:S(2)}, u32[]{:S(2)}) collective-permute-start(bf16[384,256]{1,0:T(8,128)(2,1)} %collective-permute-done.27.rest_1_), channel_id=1, source_target_pairs={{0,1},{1,0},{2,3},{3,2},{4,5},{5,4},{6,7},{7,6},{8,9},{9,8},{10,11... | collective-permute-start | bytes 589832 | tf_op jit(solution)/shard_map/ppermute | solution.py:708
  138.0 18.2 %collective-permute-start.25 = (bf16[384,256]{1,0:T(8,128)(2,1)S(1)}, bf16[384,256]{1,0:T(8,128)(2,1)}, u32[]{:S(2)}, u32[]{:S(2)}) collective-permute-start(bf16[384,256]{1,0:T(8,128)(2,1)S(1)} %attend.3.rest_0_), channel_id=1, source_target_pairs={{0,1},{1,0},{2,3},{3,2},{4,5},{5,4},{6,7},{7,6},{8,9},{9,8},{10,11... | collective-permute-start | bytes 589832 | tf_op jit(solution)/shard_map/ppermute | solution.py:707
  143.6 12.6 %collective-permute-start.26 = (bf16[384,256]{1,0:T(8,128)(2,1)S(1)}, bf16[384,256]{1,0:T(8,128)(2,1)}, u32[]{:S(2)}, u32[]{:S(2)}) collective-permute-start(bf16[384,256]{1,0:T(8,128)(2,1)S(1)} %collective-permute-done.24.rest_1_), channel_id=1, source_target_pairs={{0,1},{1,0},{2,3},{3,2},{4,5},{5,4},{6,7},{7,6},{8,9},{9,8},{10,11... | collective-permute-start | bytes 589832 | tf_op jit(solution)/shard_map/ppermute | solution.py:708
  150.5 11.3 %collective-permute-start.32 = (f32[1,384]{1,0:T(1,128)S(1)}, f32[1,384]{1,0:T(1,128)S(1)}, u32[]{:S(2)}, u32[]{:S(2)}) collective-permute-start(f32[1,384]{1,0:T(1,128)S(1)} %get-tuple-element.43.rest_4_.rest_0_), channel_id=1, source_target_pairs={{0,1},{1,2},{2,3},{3,0},{4,5},{5,6},{6,7},{7,4},{8,9},{9,10},{10,1... | collective-permute-start | bytes 4616 | tf_op jit(solution)/shard_map/ppermute | solution.py:717
  152.6 11.7 %collective-permute-start.33 = (f32[1,384]{1,0:T(1,128)S(1)}, f32[1,384]{1,0:T(1,128)S(1)}, u32[]{:S(2)}, u32[]{:S(2)}) collective-permute-start(f32[1,384]{1,0:T(1,128)S(1)} %get-tuple-element.43.rest_4_.rest_0_), channel_id=1, source_target_pairs={{0,2},{1,3},{2,0},{3,1},{4,6},{5,7},{6,4},{7,5},{8,10},{9,11},{10,... | collective-permute-start | bytes 4616 | tf_op jit(solution)/shard_map/ppermute | solution.py:717
  153.3 11.0 %collective-permute-start.34 = (f32[1,384]{1,0:T(1,128)S(1)}, f32[1,384]{1,0:T(1,128)S(1)}, u32[]{:S(2)}, u32[]{:S(2)}) collective-permute-start(f32[1,384]{1,0:T(1,128)S(1)} %get-tuple-element.43.rest_4_.rest_0_), channel_id=1, source_target_pairs={{0,3},{1,0},{2,1},{3,2},{4,7},{5,4},{6,5},{7,6},{8,11},{9,8},{10,9... | collective-permute-start | bytes 4616 | tf_op jit(solution)/shard_map/ppermute | solution.py:717
  160.4 5.8 %collective-permute-start.29 = (f32[1,384]{1,0:T(1,128)S(1)}, f32[1,384]{1,0:T(1,128)S(1)}, u32[]{:S(2)}, u32[]{:S(2)}) collective-permute-start(f32[1,384]{1,0:T(1,128)S(1)} %get-tuple-element.45.rest_0_), channel_id=1, source_target_pairs={{0,1},{1,2},{2,3},{3,0},{4,5},{5,6},{6,7},{7,4},{8,9},{9,10},{10,1... | collective-permute-start | bytes 4616 | tf_op jit(solution)/shard_map/ppermute | solution.py:717
  160.4 5.8 %collective-permute-start.30 = (f32[1,384]{1,0:T(1,128)S(1)}, f32[1,384]{1,0:T(1,128)S(1)}, u32[]{:S(2)}, u32[]{:S(2)}) collective-permute-start(f32[1,384]{1,0:T(1,128)S(1)} %get-tuple-element.45.rest_0_), channel_id=1, source_target_pairs={{0,2},{1,3},{2,0},{3,1},{4,6},{5,7},{6,4},{7,5},{8,10},{9,11},{10,... | collective-permute-start | bytes 4616 | tf_op jit(solution)/shard_map/ppermute | solution.py:717
  (19 other events, 110.6 us)

commit v10 on v9

--- a/solution.py
+++ b/solution.py
@@ -309,7 +309,8 @@
     )(place, sources, x, own, got, *after)
 
 
-def near_kernel(src_ref, x_ref, k_ref, v_ref, q_ref, after_ref, out_ref):
+def near_kernel(src_ref, x_ref, k_ref, v_ref, q_ref, *rest):
+    out_ref = rest[-1]
     x = x_ref[0]
 
     @pl.when(pl.program_id(0) == 0)
@@ -334,64 +335,93 @@
             grid=(count,),
             in_specs=[pl.BlockSpec((1, chunk, cols), lambda i, s: (i, 0, 0))]
             + [pl.BlockSpec((cols, w), lambda i, s: (s[i], 0)) for w in widths]
-            + [ANY],
+            + [ANY for _ in after],
             out_specs=pl.BlockSpec((chunk, sum(widths)), lambda i, s: (0, 0)),
         ),
         compiler_params=PARAMS,
         name="near",
-    )(sources, x, *weights, after)
-
-
-def keys_kernel(
-    near_ref, far_ref, sq_ref, id_ref, cos_ref, sin_ref, *rest, model
-):
-    k_out, vt_out, sum_ref = rest[-3:]
-    rows = near_ref.shape[0]
+    )(sources, x, *weights, *after)
+
+
+def keys_kernel(near_ref, far_ref, sq_ref, id_ref, cos_ref, sin_ref, *rest, model):
+    out_ref, sum_ref = rest[-2:]
+    rows, width = near_ref.shape[0], far_ref.shape[1]
     tail = far_ref[rows:, :].astype(F32)
     total = sum(rows_of(tail, 2, rows), sq_ref[...])
     factor = to_column(lax.rsqrt(total / model + epsilon))
     sum_ref[...] = total
     keys, values = slice(0, HEAD_SIZE), slice(HEAD_SIZE, 2 * HEAD_SIZE)
     part = (near_ref[:, keys] + far_ref[:rows, keys].astype(F32)) * factor
-    k_out[:rows, :] = rotate(part, cos_ref[...], sin_ref[...]).astype(BF16)
-    k_out[rows:, :] = lines_of((id_ref[...].astype(F32),), HEAD_SIZE)
+    part = rotate(part, cos_ref[...], sin_ref[...]).astype(BF16)
+    out_ref[: rows // 2, keys] = part[: rows // 2]
+    out_ref[: rows // 2, values] = part[rows // 2 :]
     part = (near_ref[:, values] + far_ref[:rows, values].astype(F32)) * factor
-    vt_out[...] = part.T.astype(BF16)
+    part = part.T.astype(BF16)
+    for i, at in enumerate(range(0, rows, width)):
+        row = rows // 2 + i * HEAD_SIZE
+        out_ref[row : row + HEAD_SIZE, :] = part[:, at : at + width]
+    out_ref[rows:, :] = lines_of((id_ref[...].astype(F32),), width)
 
 
 def keys_values(near, far, sq, ids, cosine, sine, after, model):
     rows, width = near.shape[0], far.shape[1]
     whole = lambda i: (0, 0)
-    dims = [(rows + TAIL, HEAD_SIZE), (HEAD_SIZE, rows), (1, rows)]
     return pl.pallas_call(
         partial(keys_kernel, model=model),
-        out_shape=tuple(shape(d, t) for d, t in zip(dims, (BF16, BF16, F32))),
+        out_shape=(shape(far.shape, BF16), shape(sq.shape, F32)),
         grid=(1,),
         in_specs=[pl.BlockSpec((rows, width), whole)]
         + [pl.BlockSpec(a.shape, whole) for a in (far, sq, ids, cosine, sine)]
         + [ANY for _ in after],
-        out_specs=[pl.BlockSpec(d, whole) for d in dims],
+        out_specs=[pl.BlockSpec(far.shape, whole), pl.BlockSpec(sq.shape, whole)],
         compiler_params=PARAMS,
         name="keys",
     )(near, far, sq, ids, cosine, sine, *after)
 
 
-def attention_kernel(
-    seq_ref, near_ref, far_ref, sum_ref, cos_ref, sin_ref, id_ref, after_ref, *rest, back, offset, model
-):
+def queries_kernel(near_ref, far_ref, sum_ref, cos_ref, sin_ref, out_ref, *, model):
+    scale = query_scale * math.log2(math.e)
+    factor = to_column(lax.rsqrt(sum_ref[...] / model + epsilon) * scale)
+    for c in range(0, out_ref.shape[1], HEAD_SIZE):
+        at = slice(c, c + HEAD_SIZE)
+        part = (near_ref[:, at] + far_ref[:, at].astype(F32)) * factor
+        out_ref[:, at] = rotate(part, cos_ref[...], sin_ref[...]).astype(BF16)
+
+
+def finished_queries(near, far, sums, cosine, sine, model):
+    rows, width = far.shape
+    last = near.shape[1] // width - 1
+    whole = lambda i: (0, 0)
+    return pl.pallas_call(
+        partial(queries_kernel, model=model),
+        out_shape=shape((rows, width), BF16),
+        grid=(1,),
+        in_specs=[pl.BlockSpec((rows, width), lambda i: (0, last))]
+        + [pl.BlockSpec(a.shape, whole) for a in (far, sums, cosine, sine)],
+        out_specs=pl.BlockSpec((rows, width), whole),
+        compiler_params=PARAMS,
+        cost_estimate=pl.CostEstimate(flops=5 * 10**10, bytes_accessed=10**8, transcendentals=0),
+        name="queries",
+    )(near, far, sums, cosine, sine)
+
+
+def attention_kernel(seq_ref, q_ref, id_ref, after_ref, *rest, back, offset):
     kv_refs, (out_ref, k_scr, vt_scr, count_scr) = rest[:-4], rest[-4:]
-    part_rows = kv_refs[1].shape[1]
-    group = near_ref.shape[1] // HEAD_SIZE
+    part_rows, message = kv_refs[0].shape[0] - TAIL, kv_refs[0].shape[1]
+    group = q_ref.shape[1] // HEAD_SIZE
     tile = pl.program_id(0)
 
     @pl.when(tile == 0)
     def _():
         counts = [jnp.zeros((1, 1), F32) for _ in range(DOCUMENTS)]
-        for b, (k_ref, vt_ref) in enumerate(zip(kv_refs[::2], kv_refs[1::2])):
-            at = slice(b * part_rows, (b + 1) * part_rows)
-            k_scr[at, :] = k_ref[:part_rows, :]
-            vt_scr[:, at] = vt_ref[...]
-            (ids,) = rows_of(k_ref[part_rows:, :].astype(F32), 1, part_rows)
+        for b, kv_ref in enumerate(kv_refs):
+            row, half = b * part_rows, part_rows // 2
+            k_scr[row : row + half, :] = kv_ref[:half, :HEAD_SIZE]
+            k_scr[row + half : row + part_rows, :] = kv_ref[:half, HEAD_SIZE:]
+            for i, at in enumerate(range(0, part_rows, message)):
+                first = half + i * HEAD_SIZE
+                vt_scr[:, row + at : row + at + message] = kv_ref[first : first + HEAD_SIZE, :]
+            (ids,) = rows_of(kv_ref[part_rows:, :].astype(F32), 1, part_rows)
             exists = b >= back - seq_ref[0]
             ids = jnp.where(exists, ids, -1.0)
             for d in range(DOCUMENTS):
@@ -400,13 +430,7 @@
         for d in range(DOCUMENTS):
             count_scr[d : d + 1, :] = jnp.broadcast_to(counts[d], (1, LANES))
 
-    scale = query_scale * math.log2(math.e)
-    factor = to_column(lax.rsqrt(sum_ref[...] / model + epsilon) * scale)
-    heads = []
-    for c in range(0, group * HEAD_SIZE, HEAD_SIZE):
-        at = slice(c, c + HEAD_SIZE)
-        part = (near_ref[:, at] + far_ref[:, at].astype(F32)) * factor
-        heads.append(rotate(part, cos_ref[...], sin_ref[...]).astype(BF16))
+    heads = [q_ref[:, c : c + HEAD_SIZE] for c in range(0, group * HEAD_SIZE, HEAD_SIZE)]
     q2 = jnp.concatenate(heads, axis=0)
     width = group * Q_TILE
 
@@ -461,26 +485,19 @@
         ].astype(BF16)
 
 
-def attend(seq, near, far, sums, cosine, sine, ids, after, blocks, c, model):
-    rows = near.shape[0] // CHUNKS
-    width = far.shape[1]
+def attend(seq, queries, ids, after, blocks, c):
+    rows, width = queries.shape[0] // CHUNKS, queries.shape[1]
     back = len(blocks) - 1
     tiles = rows // Q_TILE
-    keys = len(blocks) * near.shape[0]
-    blocks = [part for block in blocks for part in block]
-    last = near.shape[1] // width - 1
-    return pl.pallas_call(
-        partial(attention_kernel, back=back, offset=c * rows, model=model),
+    keys = len(blocks) * queries.shape[0]
+    return pl.pallas_call(
+        partial(attention_kernel, back=back, offset=c * rows),
         out_shape=shape((rows, width), BF16),
         grid_spec=pltpu.PrefetchScalarGridSpec(
             num_scalar_prefetch=1,
             grid=(tiles,),
             in_specs=[
-                pl.BlockSpec((Q_TILE, width), lambda i, s: (c * tiles + i, last)),
                 pl.BlockSpec((Q_TILE, width), lambda i, s: (c * tiles + i, 0)),
-                pl.BlockSpec((1, Q_TILE), lambda i, s: (0, c * tiles + i)),
-                pl.BlockSpec((Q_TILE, HEAD_SIZE), lambda i, s: (c * tiles + i, 0)),
-                pl.BlockSpec((Q_TILE, HEAD_SIZE), lambda i, s: (c * tiles + i, 0)),
                 pl.BlockSpec((1, Q_TILE), lambda i, s: (0, c * tiles + i)),
                 ANY,
             ]
@@ -499,11 +516,11 @@
             transcendentals=rows * keys * width // HEAD_SIZE,
         ),
         name="attend",
-    )(seq, near, far, sums, cosine, sine, ids, after, *blocks)
+    )(seq, queries, ids, after, *blocks)
 
 
 def output_kernel(at_ref, own_o_ref, o_ref, *rest):
-    ctx_refs, (after_ref, out_ref, sq_ref, acc) = rest[:-4], rest[-4:]
+    ctx_refs, (before_ref, out_ref, sq_ref, acc) = rest[:-4], rest[-4:]
     step = pl.program_id(0)
     total = jnp.dot(ctx_refs[0][...], own_o_ref[...], preferred_element_type=F32)
     for i, ctx_ref in enumerate(ctx_refs[1:]):
@@ -523,10 +540,13 @@
 
     @pl.when(step == pl.num_programs(0) - 1)
     def _():
-        sq_ref[...] = acc[...].T[0:1, :]
-
-
-def output_product(column, order, o_weight, gathered, contexts, after):
+        done = sq_ref.shape[1] - acc.shape[0]
+        if done:
+            sq_ref[:, :done] = before_ref[...]
+        sq_ref[:, done:] = acc[...].T[0:1, :]
+
+
+def output_product(column, order, o_weight, gathered, contexts, before, c):
     chunk, width = contexts[0].shape
     others, _, cols = gathered.shape
     tiles = 3 if cols % (3 * LANES) == 0 else 1
@@ -536,7 +556,7 @@
         column = jnp.int32(0)
     return pl.pallas_call(
         output_kernel,
-        out_shape=(shape((chunk, cols), F32), shape((1, chunk), F32)),
+        out_shape=(shape((chunk, cols), F32), shape((1, (c + 1) * chunk), F32)),
         grid_spec=pltpu.PrefetchScalarGridSpec(
             num_scalar_prefetch=1,
             grid=(tiles,),
@@ -545,53 +565,50 @@
                 pl.BlockSpec((others, width, tile), lambda i, at: (0, 0, i)),
             ]
             + [pl.BlockSpec((chunk, width), lambda i, at: (0, 0)) for _ in contexts]
-            + [ANY],
+            + [pl.BlockSpec(before.shape, lambda i, at: (0, 0))],
             out_specs=[
                 pl.BlockSpec((chunk, tile), lambda i, at: (0, i)),
-                pl.BlockSpec((1, chunk), lambda i, at: (0, 0)),
+                pl.BlockSpec((1, (c + 1) * chunk), lambda i, at: (0, 0)),
             ],
             scratch_shapes=[pltpu.VMEM((chunk, LANES), F32)],
         ),
         compiler_params=PARAMS,
         name="output",
-    )(jnp.stack([column] + order), o_weight, gathered, *contexts, after)
-
-
-def final_kernel(token_ref, branch_ref, gain_ref, *rest, model, others):
-    sq_refs, out_ref = rest[:others], rest[-1]
+    )(jnp.stack([column] + order), o_weight, gathered, *contexts, before)
+
+
+def final_kernel(token_ref, gain_ref, *rest, model):
+    branch_refs, sq_refs, out_ref = rest[:CHUNKS], rest[CHUNKS:-1], rest[-1]
     total = sq_refs[0][...]
     for sq_ref in sq_refs[1:]:
         total = total + sq_ref[...]
     factor = to_column(lax.rsqrt(total / model + epsilon))[:, 0:1]
-    out = token_ref[...].astype(F32) + branch_ref[...] * factor * gain_ref[...]
-    out_ref[...] = out.astype(BF16)
-
-
-def finish(tokens, branch, out_gain, sums, previous, c, model):
-    chunk, cols = branch.shape
-    tiles = chunk // Q_TILE
-    in_specs = [
-        pl.BlockSpec((Q_TILE, cols), lambda i: (c * tiles + i, 0)),
-        pl.BlockSpec((Q_TILE, cols), lambda i: (i, 0)),
-        pl.BlockSpec((1, cols), lambda i: (0, 0)),
-    ]
-    in_specs += [pl.BlockSpec((1, Q_TILE), lambda i: (0, i)) for _ in sums]
-    args = [tokens, branch, out_gain, *sums]
-    aliases = {}
-    if previous is not None:
-        aliases = {len(args): 0}
-        in_specs.append(ANY)
-        args.append(previous)
-    return pl.pallas_call(
-        partial(final_kernel, model=model, others=len(sums)),
+    for c in range(CHUNKS):
+
+        @pl.when(pl.program_id(0) * CHUNKS // pl.num_programs(0) == c)
+        def _():
+            out = token_ref[...].astype(F32) + branch_refs[c][...] * factor * gain_ref[...]
+            out_ref[...] = out.astype(BF16)
+
+
+def finish(tokens, branches, out_gain, sums, model):
+    rows, cols = tokens.shape
+    tiles = rows // CHUNKS // Q_TILE
+    held = lambda c: lambda i: (jnp.clip(i - c * tiles, 0, tiles - 1), 0)
+    return pl.pallas_call(
+        partial(final_kernel, model=model),
         out_shape=shape(tokens.shape, BF16),
-        grid=(tiles,),
-        in_specs=in_specs,
-        out_specs=pl.BlockSpec((Q_TILE, cols), lambda i: (c * tiles + i, 0)),
-        input_output_aliases=aliases,
+        grid=(CHUNKS * tiles,),
+        in_specs=[
+            pl.BlockSpec((Q_TILE, cols), lambda i: (i, 0)),
+            pl.BlockSpec((1, cols), lambda i: (0, 0)),
+        ]
+        + [pl.BlockSpec((Q_TILE, cols), held(c)) for c in range(CHUNKS)]
+        + [pl.BlockSpec((1, Q_TILE), lambda i: (0, i)) for _ in sums],
+        out_specs=pl.BlockSpec((Q_TILE, cols), lambda i: (i, 0)),
         compiler_params=PARAMS,
         name="finish",
-    )(*args)
+    )(tokens, out_gain, *branches, *sums)
 
 
 def per_device(
@@ -619,8 +636,8 @@
     inner = seq_bits + group_bits
     masks_kv, masks_q = inner + [1], inner[::-1] + [1]
     last = len(masks_kv) - 1
-    third = rows // 3 // TAIL * TAIL
-    counts = [rows - 2 * third, third, third]
+    eighth = rows // 48 * 8
+    counts = [eighth, rows // 2 + TAIL, rows - eighth - rows // 2 - TAIL]
     packed_kv, packed_q, cut = pack(
         at, q_weight, k_weight, value_weight, share, tokens, counts[0]
     )
@@ -637,12 +654,7 @@
         if step < 2:
             count = counts[1 + step]
         if step == last:
-            o_share = o_weight.shape[0] // plane
-            columns = [(z + k) % nz * cols for k in range(1, nz)]
-            pieces = cut_pieces(in_plane * o_share, columns, o_weight, o_share, cols, own_kv)
-            moved = [lax.ppermute(p, "tensor", turn(k + 1)) for k, p in enumerate(pieces)]
-            own_o = jnp.stack(moved)[None]
-            after = [received[1], own_o]
+            after = [received[1]]
         outs = stage(pairs, tokens, first, count, after)
         if pairs:
             own_kv, own_q = outs[:2]
@@ -655,14 +667,16 @@
         order_q = order_q + [k ^ mask_q for k in order_q]
     far_kv, far_q = (order_kv, own_kv, far_kv), (order_q, own_q, far_q)
 
+    o_share = o_weight.shape[0] // plane
+    columns = [(z + k) % nz * cols for k in range(1, nz)]
+    pieces = cut_pieces(in_plane * o_share, columns, o_weight, o_share, cols, own_kv)
+    moved = [lax.ppermute(p, "tensor", turn(k + 1)) for k, p in enumerate(pieces)]
+    own_o = jnp.stack(moved)[None]
+
     def double(own, step, after):
         if step > 0:
             (own,) = stage([own], tokens, 0, 0, after)
         return own, lax.ppermute(own, PLANE, [(i, i ^ masks_kv[step]) for i in range(plane)])
-
-    pair_o = double(own_o, 0, [])
-    for step in range(1, last - 1):
-        pair_o = double(pair_o, step, [])
 
     sources = (within + half - jnp.arange(half, dtype=jnp.int32)) % half
     blocks = [[tokens], received]
@@ -671,52 +685,56 @@
     gains = in_gain.reshape(nz, 1, cols)
     place = jnp.stack([in_plane, side * half])
     sent_kv, x, sq = far_kv_product(
-        place, sources, gains, blocks, far_kv, [far_q[2], pair_o[1]]
+        place, sources, gains, blocks, far_kv, [far_q[2], own_o]
     )
     got_kv = lax.ppermute(sent_kv, "tensor", swap)
-    pair_o = double(pair_o, last - 1, [sent_kv])
+    pair_o = double(own_o, 0, [])
+    for step in range(1, last - 1):
+        pair_o = double(pair_o, step, [])
     weights = (k_weight, value_weight, q_weight)
 
     sent_q = far_product(place, sources, x, far_q, [sent_kv])
     got_q = lax.ppermute(sent_q, "tensor", swap)
-    near = near_product(side * half + sources, x, weights, sent_q)
+    near = near_product(side * half + sources, x, weights, [sent_q, pair_o[1]])
+    pair_o = double(pair_o, last - 1, [near])
     cosine, sine = rotation_table(seq * rows + jnp.arange(rows, dtype=jnp.int32))
     ids = seg_ids[None, :]
-    *own_kv, sums = keys_values(
-        near, got_kv, sq, ids, cosine, sine, [sent_q, pair_o[1]], model
+    own_kv, sums = keys_values(
+        near, got_kv, sq, ids, cosine, sine, [sent_q], model
     )
-    pair_o = double(pair_o, last, [own_kv[0]])
+    pair_o = double(pair_o, last, [own_kv])
     gathered_o = lay_pieces(place, order_kv, *pair_o)
 
     back = -(-(nseq * rows // 2 - 1) // rows)
     kv_blocks = [own_kv]
     for k in range(1, back + 1):
         earlier = [(i, i + k) for i in range(nseq - k)]
-        kv_blocks.insert(0, [lax.ppermute(part, "seq", earlier) for part in own_kv])
-
-    out = None
+        kv_blocks.insert(0, lax.ppermute(own_kv, "seq", earlier))
+
+    queries = finished_queries(near, got_q, sums, cosine, sine, model)
     seq_at = jnp.reshape(seq, (1,))
-    after, own_sq = pair_o[1], place
+    branches, own_sq, after = [], sums, own_kv
     for c in range(CHUNKS):
-        context = attend(
-            seq_at, near, got_q, sums, cosine, sine, ids, after, kv_blocks, c, model
-        )
+        context = attend(seq_at, queries, ids, after, kv_blocks, c)
+        after = gathered_o
         if nz == 4:
             pairs = [(i, i ^ 1) for i in range(nz)]
             opposite = lax.ppermute(context, "tensor", swap)
             beside = lax.ppermute(context, "tensor", pairs)
             across = lax.ppermute(opposite, "tensor", pairs)
-            contexts, after = [context, opposite, beside, across], beside
+            contexts = [context, opposite, beside, across]
             order = [jnp.int32(1), 2 - 2 * (z % 2), 2 * (z % 2)]
         else:
-            contexts, after = [context], context
+            contexts = [context]
             contexts += [lax.ppermute(context, "tensor", turn(k)) for k in range(1, nz)]
             order = [jnp.int32(k) for k in range(nz - 1)]
-        branch, own_sq = output_product(z, order, o_weight, gathered_o, contexts, own_sq)
-        squares = [own_sq]
-        squares += [lax.ppermute(own_sq, "tensor", turn(k)) for k in range(1, nz)]
-        out = finish(tokens, branch, out_gain[None, :], squares, out, c, model)
-    return out
+        branch, own_sq = output_product(
+            z, order, o_weight, gathered_o, contexts, own_sq, c
+        )
+        branches.append(branch)
+    squares = [own_sq]
+    squares += [lax.ppermute(own_sq, "tensor", turn(k)) for k in range(1, nz)]
+    return finish(tokens, branches, out_gain[None, :], squares, model)
 
 
 def solution(mesh):

time: 169 us -> 165 us (0.976); the launches traced: 168 us -> 163 us
  Pallas kernels: 49.4 us -> 45.6 us
  starting transfers between devices: 41.2 us -> 37.6 us
  local copies, waits for them, and re-layouts: 2.32 us -> 5.31 us
  waiting for transfers between devices: 72.9 us -> 70.7 us
    ppermute x3, waiting for transfers between devices: 3.14 us -> 15.9 us  [per_device(): lax.ppermute(p, 'tensor', turn(k + 1))]
    ppermute x1, waiting for transfers between devices: 14.8 us -> 3.87 us  [per_device(): got_q = lax.ppermute(sent_q, 'tensor', swap)]
    ppermute x3, waiting for transfers between devices: 7.37 us -> 0.01 us  [double(): lax.ppermute(own, PLANE, [(i, i ^ masks_kv[step]) for i in range(plane)])]
    ppermute x1, waiting for transfers between devices: 14.3 us -> 8.01 us  [per_device(): own_kv = lax.ppermute(packed_kv, 'tensor', swap)[None]]
    ppermute x2, waiting for transfers between devices: 4.78 us -> 0.01 us  [per_device(): beside = lax.ppermute(context, 'tensor', pairs)]
    ppermute x6 -> x3, starting transfers between devices: 9.53 us -> 5.49 us  [per_device(): squares += [lax.ppermute(own_sq, 'tensor', turn(k)) for k in range(1, nz)]]
    ppermute x4 -> x2, waiting for transfers between devices: 5 us -> 8.93 us  [per_device(): kv_blocks.insert(0, lax.ppermute(own_kv, 'seq', earlier))]
    ppermute x1, waiting for transfers between devices: 6.42 us -> 10.1 us  [per_device(): got_kv = lax.ppermute(sent_kv, 'tensor', swap)]
  transfers between devices with their start and end apart: 35 -> 30, of which waited for: 16 -> 19; matrix products, arithmetic and copies ran while one was open for 1% -> 2% of each run, Pallas kernels for 19% -> 20%
where the time goes in v10:
time: 165 us; the launch traced here: 163 us
  waiting for transfers between devices  70.7 us (43%)
  Pallas kernels  45.6 us (28%)
  starting transfers between devices  37.6 us (23%)
  local copies, waits for them, and re-layouts  5.31 us (3%)
  other arithmetic  2.89 us (2%)
    ppermute x3, waiting for transfers between devices, per_device(): lax.ppermute(p, 'tensor', turn(k + 1))  15.9 us
    ppermute x1, waiting for transfers between devices, per_device(): got_kv = lax.ppermute(sent_kv, 'tensor', swap)  10.1 us
    pallas_call x2, Pallas kernels, attend(): pl.pallas_call(partial(attention_kernel, back=back, offset=c * rows), out...  9.8 us
    ppermute x2, waiting for transfers between devices, per_device(): kv_blocks.insert(0, lax.ppermute(own_kv, 'seq', earlier))  8.93 us
    ppermute x1, waiting for transfers between devices, per_device(): own_kv = lax.ppermute(packed_kv, 'tensor', swap)[None]  8.01 us
    pallas_call x2, Pallas kernels, output_product(): pl.pallas_call(output_kernel, out_shape=(shape((chunk, cols), F32), shape...  7.94 us
    ppermute x3, waiting for transfers between devices, per_device(): lax.ppermute(own_kv, PLANE, [(i, i ^ mask_kv) for i in range(plane)])  6.72 us
    pallas_call x5, Pallas kernels, stage(): pl.pallas_call(partial(stage_kernel, pairs=len(joined), first=first, coun...  6.09 us
  transfers between devices with their start and end apart: 30, of which 19 were waited for; matrix products, arithmetic and copies ran while one was open for 2% of the time, Pallas kernels for 20%

profile of v10, /device:TPU:2, one launch (start us, length us, event | category | flops | bytes accessed | tf_op | source)
XLA Modules:
  0.0 162.5 jit_solution(1050506478975885975)
XLA Ops:
  0.0 2.1 %pack.1 = (bf16[288,256]{1,0:T(8,128)(2,1)}, bf16[288,256]{1,0:T(8,128)(2,1)}, bf16[128,1152]{1,0:T(8,128)(2,1)}) custom-call(s32[1]{0:T(128)} %bitcast.9.at_ref, bf16[4608,256]{1,0:T(8,128)(2,1)} %q_ref.3, bf16[4608,128]{1,0:T(8,128)(2,1)} %k_ref.3, bf16[4608,128]{1,0:T(8,128)(2,1)} %v_ref.3, bf16[768,1152]{1,0:T(8,128)(2,1)} %token_ref.1), custom_call_target="tpu_custom_call" | custom-call | tf_op jit(solution)/shard_map/pack/pallas_call | solution.py:74
  3.7 2.6 %collective-permute-start = (bf16[288,256]{1,0:T(8,128)(2,1)}, bf16[288,256]{1,0:T(8,128)(2,1)S(1)}, u32[]{:S(2)}, u32[]{:S(2)}) collective-permute-start(bf16[288,256]{1,0:T(8,128)(2,1)} %get-tuple-element.25), channel_id=1, source_target_pairs={{0,2},{1,3},{2,0},{3,1},{4,6},{5,7},{6,4},{7,5},{8,10},{9,11},{10,... | collective-permute-start | bytes 442376 | tf_op jit(solution)/shard_map/ppermute | solution.py:644
  6.7 8.0 %collective-permute-done = bf16[288,256]{1,0:T(8,128)(2,1)S(1)} collective-permute-done((bf16[288,256]{1,0:T(8,128)(2,1)}, bf16[288,256]{1,0:T(8,128)(2,1)S(1)}, u32[]{:S(2)}, u32[]{:S(2)}) %collective-permute-start) | collective-permute-done | bytes 147488 | tf_op jit(solution)/shard_map/ppermute | solution.py:644
  14.7 5.0 %collective-permute-done.2 = bf16[288,256]{1,0:T(8,128)(2,1)S(1)} collective-permute-done((bf16[288,256]{1,0:T(8,128)(2,1)}, bf16[288,256]{1,0:T(8,128)(2,1)S(1)}, u32[]{:S(2)}, u32[]{:S(2)}) %collective-permute-start.2) | collective-permute-done | bytes 147488 | tf_op jit(solution)/shard_map/ppermute | solution.py:645
  23.4 3.1 %collective-permute-done.1.refs_1_ = bf16[1,288,256]{2,1,0:T(8,128)(2,1)S(1)} collective-permute-done((bf16[1,288,256]{2,1,0:T(8,128)(2,1)S(1)}, bf16[1,288,256]{2,1,0:T(8,128)(2,1)S(1)}, u32[]{:S(2)}, u32[]{:S(2)}) %collective-permute-start.1) | collective-permute-done | bytes 147488 | tf_op jit(solution)/shard_map/ppermute | solution.py:664
  32.5 3.6 %collective-permute-done.4.refs_1_ = bf16[2,288,256]{2,1,0:T(8,128)(2,1)S(1)} collective-permute-done((bf16[2,288,256]{2,1,0:T(8,128)(2,1)S(1)}, bf16[2,288,256]{2,1,0:T(8,128)(2,1)S(1)}, u32[]{:S(2)}, u32[]{:S(2)}) %collective-permute-start.4) | collective-permute-done | bytes 294944 | tf_op jit(solution)/shard_map/ppermute | solution.py:664
  38.0 3.1 %collective-permute-done.7.refs_5_.rest_2_ = bf16[400,1152]{1,0:T(8,128)(2,1)S(1)} collective-permute-done((bf16[400,1152]{1,0:T(8,128)(2,1)}, bf16[400,1152]{1,0:T(8,128)(2,1)S(1)}, u32[]{:S(2)}, u32[]{:S(2)}) %collective-permute-start.7) | collective-permute-done | bytes 921632 | tf_op jit(solution)/shard_map/ppermute | solution.py:662
  41.1 2.2 %stage.7 = (bf16[4,288,256]{2,1,0:T(8,128)(2,1)}, bf16[4,288,256]{2,1,0:T(8,128)(2,1)}) custom-call(bf16[2,288,256]{2,1,0:T(8,128)(2,1)S(1)} %get-tuple-element.27.refs_0_, bf16[2,288,256]{2,1,0:T(8,128)(2,1)S(1)} %collective-permute-done.4.refs_1_, bf16[2,288,256]{2,1,0:T(8,128)(2,1)} %get-tuple-element.28.refs_2_, ...), custom_call_target="tpu_custom_call" | custom-call | tf_op jit(solution)/shard_map/stage/pallas_call | solution.py:113
  46.8 2.2 %collective-permute-start.9 = (bf16[32,1152]{1,0:T(8,128)(2,1)S(1)}, bf16[32,1152]{1,0:T(8,128)(2,1)S(1)}, u32[]{:S(2)}, u32[]{:S(2)}) collective-permute-start(bf16[32,1152]{1,0:T(8,128)(2,1)S(1)} %get-tuple-element.32), channel_id=1, source_target_pairs={{0,2},{1,3},{2,0},{3,1},{4,6},{5,7},{6,4},{7,5},{8,10},{9,11},{10,... | collective-permute-start | bytes 221192 | tf_op jit(solution)/shard_map/ppermute | solution.py:673
  49.0 2.0 %collective-permute-done.8 = bf16[32,1152]{1,0:T(8,128)(2,1)} collective-permute-done((bf16[32,1152]{1,0:T(8,128)(2,1)S(1)}, bf16[32,1152]{1,0:T(8,128)(2,1)}, u32[]{:S(2)}, u32[]{:S(2)}) %collective-permute-start.8) | collective-permute-done | bytes 73760 | tf_op jit(solution)/shard_map/ppermute | solution.py:673
  51.1 10.5 %collective-permute-done.9 = bf16[32,1152]{1,0:T(8,128)(2,1)S(1)} collective-permute-done((bf16[32,1152]{1,0:T(8,128)(2,1)S(1)}, bf16[32,1152]{1,0:T(8,128)(2,1)S(1)}, u32[]{:S(2)}, u32[]{:S(2)}) %collective-permute-start.9) | collective-permute-done | bytes 73760 | tf_op jit(solution)/shard_map/ppermute | solution.py:673
  61.6 3.4 %collective-permute-done.10 = bf16[32,1152]{1,0:T(8,128)(2,1)S(1)} collective-permute-done((bf16[32,1152]{1,0:T(8,128)(2,1)S(1)}, bf16[32,1152]{1,0:T(8,128)(2,1)S(1)}, u32[]{:S(2)}, u32[]{:S(2)}) %collective-permute-start.10) | collective-permute-done | bytes 73760 | tf_op jit(solution)/shard_map/ppermute | solution.py:673
  67.5 4.7 %far_kv.1 = (bf16[784,256]{1,0:T(8,128)(2,1)S(1)}, bf16[2,768,1152]{2,1,0:T(8,128)(2,1)}, f32[1,768]{1,0:T(1,128)S(1)}) custom-call(s32[2]{0:T(128)S(1)} %get-tuple-element.49.place_ref, s32[2]{0:T(128)S(1)} %get-tuple-element.48.src_ref, f32[4,1,1152]{2,1,0:T(1,128)S(1)} %reshape.21.gain_ref, bf16[4,288,256]{2,1,0:T(8,128)(2,1)} %get-tuple-element.30.after_ref.own_ref, ...), custom_call_target="tpu_custom_call" | custom-call | tf_op jit(solution)/shard_map/far_kv/pallas_call | solution.py:240
  73.1 2.0 %copy-done.5 = bf16[2,768,1152]{2,1,0:T(8,128)(2,1)S(1)} copy-done((bf16[2,768,1152]{2,1,0:T(8,128)(2,1)S(1)}, bf16[2,768,1152]{2,1,0:T(8,128)(2,1)}, u32[]{:S(2)}) %copy-start.5) | copy-done | bytes 3538968
  75.1 3.1 %far.1.rest_0_ = bf16[768,256]{1,0:T(8,128)(2,1)S(1)} custom-call(s32[2]{0:T(128)S(1)} %get-tuple-element.49.place_ref, s32[2]{0:T(128)S(1)} %get-tuple-element.48.src_ref, bf16[2,768,1152]{2,1,0:T(8,128)(2,1)S(1)} %copy-done.5, bf16[4,288,256]{2,1,0:T(8,128)(2,1)} %get-tuple-element.35.own_ref, ...), custom_call_target="tpu_custom_call" | custom-call | tf_op jit(solution)/shard_map/far/pallas_call | solution.py:293
  78.2 2.2 %collective-permute-start.18 = (bf16[768,256]{1,0:T(8,128)(2,1)S(1)}, bf16[768,256]{1,0:T(8,128)(2,1)S(1)}, u32[]{:S(2)}, u32[]{:S(2)}) collective-permute-start(bf16[768,256]{1,0:T(8,128)(2,1)S(1)} %far.1.rest_0_), channel_id=1, source_target_pairs={{0,2},{1,3},{2,0},{3,1},{4,6},{5,7},{6,4},{7,5},{8,10},{9,11},{10,... | collective-permute-start | bytes 1179656 | tf_op jit(solution)/shard_map/ppermute | solution.py:697
  80.4 5.7 %near.1.refs_3_.near_ref = f32[768,512]{1,0:T(8,128)S(1)} custom-call(s32[2]{0:T(128)S(1)} %broadcast_add_fusion.src_ref, bf16[2,768,1152]{2,1,0:T(8,128)(2,1)} %get-tuple-element.36.x_ref, bf16[4608,128]{1,0:T(8,128)(2,1)S(1)} %copy-done.6, bf16[4608,128]{1,0:T(8,128)(2,1)S(1)} %copy-done.7, bf16[4608,256]{1,0:T(8,128)(2,1)} %q_ref.3, ...), custom_call_target="tpu_custom_call" | custom-call | tf_op jit(solution)/shard_map/near/pallas_call | solution.py:330
  90.1 10.1 %collective-permute-done.16.far_ref = bf16[784,256]{1,0:T(8,128)(2,1)S(1)} collective-permute-done((bf16[784,256]{1,0:T(8,128)(2,1)S(1)}, bf16[784,256]{1,0:T(8,128)(2,1)S(1)}, u32[]{:S(2)}, u32[]{:S(2)}) %collective-permute-start.16) | collective-permute-done | bytes 401440 | tf_op jit(solution)/shard_map/ppermute | solution.py:690
  101.9 2.1 %collective-permute-start.20 = (bf16[784,256]{1,0:T(8,128)(2,1)S(1)}, bf16[784,256]{1,0:T(8,128)(2,1)S(1)}, u32[]{:S(2)}, u32[]{:S(2)}) collective-permute-start(bf16[784,256]{1,0:T(8,128)(2,1)S(1)} %get-tuple-element.39.refs_3_.after_ref.rest_2_), channel_id=1, source_target_pairs={{0,4},{4,8},{8,12},{1,5},{5,9},{9,13},{2,6},{6,10},{10,14},{3,7},{... | collective-permute-start | bytes 1204232 | tf_op jit(solution)/shard_map/ppermute | solution.py:712
  104.6 3.9 %collective-permute-done.18.far_ref = bf16[768,256]{1,0:T(8,128)(2,1)S(1)} collective-permute-done((bf16[768,256]{1,0:T(8,128)(2,1)S(1)}, bf16[768,256]{1,0:T(8,128)(2,1)S(1)}, u32[]{:S(2)}, u32[]{:S(2)}) %collective-permute-start.18) | collective-permute-done | bytes 393248 | tf_op jit(solution)/shard_map/ppermute | solution.py:697
  109.0 5.7 %collective-permute-done.19.rest_0_ = bf16[784,256]{1,0:T(8,128)(2,1)S(1)} collective-permute-done((bf16[784,256]{1,0:T(8,128)(2,1)S(1)}, bf16[784,256]{1,0:T(8,128)(2,1)S(1)}, u32[]{:S(2)}, u32[]{:S(2)}) %collective-permute-start.19) | collective-permute-done | bytes 401440 | tf_op jit(solution)/shard_map/ppermute | solution.py:712
  114.7 3.3 %collective-permute-done.20.rest_1_ = bf16[784,256]{1,0:T(8,128)(2,1)S(1)} collective-permute-done((bf16[784,256]{1,0:T(8,128)(2,1)S(1)}, bf16[784,256]{1,0:T(8,128)(2,1)S(1)}, u32[]{:S(2)}, u32[]{:S(2)}) %collective-permute-start.20) | collective-permute-done | bytes 401440 | tf_op jit(solution)/shard_map/ppermute | solution.py:712
  117.9 6.9 %attend.2.rest_0_ = bf16[384,256]{1,0:T(8,128)(2,1)S(1)} custom-call(s32[1]{0:T(128)} %bitcast.16.seq_ref, bf16[768,256]{1,0:T(8,128)(2,1)S(1)} %queries.1.q_ref, s32[1,768]{1,0:T(1,128)S(1)} %broadcast_in_dim.21.id_ref, bf16[784,256]{1,0:T(8,128)(2,1)S(1)} %get-tuple-element.39.refs_3_.after_ref.rest_2_, ...), custom_call_target="tpu_custom_call" | custom-call | flops 905969664 | bytes 2359296 | tf_op jit(solution)/shard_map/attend/pallas_call | solution.py:493
  126.4 2.9 %attend.3.rest_0_ = bf16[384,256]{1,0:T(8,128)(2,1)S(1)} custom-call(s32[1]{0:T(128)} %bitcast.16.seq_ref, bf16[768,256]{1,0:T(8,128)(2,1)S(1)} %queries.1.q_ref, s32[1,768]{1,0:T(1,128)S(1)} %broadcast_in_dim.21.id_ref, bf16[3,256,1152]{2,1,0:T(8,128)(2,1)S(1)} %lay.1.o_ref.after_ref, bf16[784,256]{1,0:T(8,128)(2,1)S(1)} %collective-permute-done.19.rest_0_, ...), custom_call_target="tpu_custom_call" | custom-call | flops 905969664 | bytes 2359296 | tf_op jit(solution)/shard_map/attend/pallas_call | solution.py:493
  129.3 3.0 %collective-permute-start.24 = (bf16[384,256]{1,0:T(8,128)(2,1)S(1)}, bf16[384,256]{1,0:T(8,128)(2,1)S(1)}, u32[]{:S(2)}, u32[]{:S(2)}) collective-permute-start(bf16[384,256]{1,0:T(8,128)(2,1)S(1)} %attend.3.rest_0_), channel_id=1, source_target_pairs={{0,2},{1,3},{2,0},{3,1},{4,6},{5,7},{6,4},{7,5},{8,10},{9,11},{10,... | collective-permute-start | bytes 589832 | tf_op jit(solution)/shard_map/ppermute | solution.py:722
  135.4 2.2 %collective-permute-done.24.rest_1_ = bf16[384,256]{1,0:T(8,128)(2,1)S(1)} collective-permute-done((bf16[384,256]{1,0:T(8,128)(2,1)S(1)}, bf16[384,256]{1,0:T(8,128)(2,1)S(1)}, u32[]{:S(2)}, u32[]{:S(2)}) %collective-permute-start.24) | collective-permute-done | bytes 196640 | tf_op jit(solution)/shard_map/ppermute | solution.py:722
  137.6 3.2 %collective-permute-start.26 = (bf16[384,256]{1,0:T(8,128)(2,1)S(1)}, bf16[384,256]{1,0:T(8,128)(2,1)S(1)}, u32[]{:S(2)}, u32[]{:S(2)}) collective-permute-start(bf16[384,256]{1,0:T(8,128)(2,1)S(1)} %collective-permute-done.24.rest_1_), channel_id=1, source_target_pairs={{0,1},{1,0},{2,3},{3,2},{4,5},{5,4},{6,7},{7,6},{8,9},{9,8},{10,11... | collective-permute-start | bytes 589832 | tf_op jit(solution)/shard_map/ppermute | solution.py:724
  140.9 2.1 %collective-permute-done.23.rest_3_ = bf16[384,256]{1,0:T(8,128)(2,1)S(1)} collective-permute-done((bf16[384,256]{1,0:T(8,128)(2,1)S(1)}, bf16[384,256]{1,0:T(8,128)(2,1)S(1)}, u32[]{:S(2)}, u32[]{:S(2)}) %collective-permute-start.23) | collective-permute-done | bytes 196640 | tf_op jit(solution)/shard_map/ppermute | solution.py:724
  144.5 4.0 %output.2 = (f32[384,1152]{1,0:T(8,128)S(1)}, f32[1,384]{1,0:T(1,128)S(1)}) custom-call(s32[4]{0:T(128)S(1)} %pad_add_fusion.at_ref, bf16[256,4608]{1,0:T(8,128)(2,1)} %own_o_ref.3, bf16[3,256,1152]{2,1,0:T(8,128)(2,1)S(1)} %copy-done.2, bf16[384,256]{1,0:T(8,128)(2,1)S(1)} %attend.2.rest_0_, bf16[384,256]{1,0:T(8,128)(2,1)S(1)} %collective-permute-done.21.rest_1_, ...), custom_call_target="tpu_custom_call" | custom-call | tf_op jit(solution)/shard_map/output/pallas_call | solution.py:557
  148.5 4.0 %output.3 = (f32[384,1152]{1,0:T(8,128)S(1)}, f32[1,768]{1,0:T(1,128)S(1)}) custom-call(s32[4]{0:T(128)S(1)} %pad_add_fusion.at_ref, bf16[256,4608]{1,0:T(8,128)(2,1)} %own_o_ref.3, bf16[3,256,1152]{2,1,0:T(8,128)(2,1)S(1)} %copy-done.3, bf16[384,256]{1,0:T(8,128)(2,1)S(1)} %attend.3.rest_0_, bf16[384,256]{1,0:T(8,128)(2,1)S(1)} %collective-permute-done.24.rest_1_, ...), custom_call_target="tpu_custom_call" | custom-call | tf_op jit(solution)/shard_map/output/pallas_call | solution.py:557
  155.3 2.6 %collective-permute-start.29 = (f32[1,768]{1,0:T(1,128)S(1)}, f32[1,768]{1,0:T(1,128)S(1)}, u32[]{:S(2)}, u32[]{:S(2)}) collective-permute-start(f32[1,768]{1,0:T(1,128)S(1)} %get-tuple-element.44.rest_2_), channel_id=1, source_target_pairs={{0,3},{1,0},{2,1},{3,2},{4,7},{5,4},{6,5},{7,6},{8,11},{9,8},{10,9... | collective-permute-start | bytes 9224 | tf_op jit(solution)/shard_map/ppermute | solution.py:736
  159.3 3.2 %finish.1 = bf16[768,1152]{1,0:T(8,128)(2,1)} custom-call(bf16[768,1152]{1,0:T(8,128)(2,1)S(1)} %copy-done, f32[1,1152]{1,0:T(1,128)S(1)} %broadcast_in_dim.17.gain_ref, f32[384,1152]{1,0:T(8,128)S(1)} %get-tuple-element.41.rest_0_, f32[384,1152]{1,0:T(8,128)S(1)} %get-tuple-element.43.rest_1_, f32[1,768]{1,0:T(1,128)S(1)} %get-tuple-element.44.rest_2_, ...), custom_call_target="tpu_custom_call" | custom-call | tf_op jit(solution)/shard_map/finish/pallas_call | solution.py:598
  (86 shorter events, 37.6 us)
Async XLA Ops:
  0.0 19.7 %copy-start = (bf16[768,1152]{1,0:T(8,128)(2,1)S(1)}, bf16[768,1152]{1,0:T(8,128)(2,1)}, u32[]{:S(2)}) copy-start(bf16[768,1152]{1,0:T(8,128)(2,1)} %token_ref.1) | copy-start | bytes 5308420
  2.1 17.6 %collective-permute-start.6 = (bf16[128,1152]{1,0:T(8,128)(2,1)}, bf16[128,1152]{1,0:T(8,128)(2,1)S(1)}, u32[]{:S(2)}, u32[]{:S(2)}) collective-permute-start(bf16[128,1152]{1,0:T(8,128)(2,1)} %get-tuple-element.29), channel_id=1, source_target_pairs={{0,1},{1,0},{2,3},{3,2},{4,5},{5,4},{6,7},{7,6},{8,9},{9,8},{10,11... | collective-permute-start | bytes 884744 | tf_op jit(solution)/shard_map/ppermute | solution.py:646
  3.7 10.9 %collective-permute-start = (bf16[288,256]{1,0:T(8,128)(2,1)}, bf16[288,256]{1,0:T(8,128)(2,1)S(1)}, u32[]{:S(2)}, u32[]{:S(2)}) collective-permute-start(bf16[288,256]{1,0:T(8,128)(2,1)} %get-tuple-element.25), channel_id=1, source_target_pairs={{0,2},{1,3},{2,0},{3,1},{4,6},{5,7},{6,4},{7,5},{8,10},{9,11},{10,... | collective-permute-start | bytes 442376 | tf_op jit(solution)/shard_map/ppermute | solution.py:644
  6.3 13.4 %collective-permute-start.2 = (bf16[288,256]{1,0:T(8,128)(2,1)}, bf16[288,256]{1,0:T(8,128)(2,1)S(1)}, u32[]{:S(2)}, u32[]{:S(2)}) collective-permute-start(bf16[288,256]{1,0:T(8,128)(2,1)} %get-tuple-element.26), channel_id=1, source_target_pairs={{0,2},{1,3},{2,0},{3,1},{4,6},{5,7},{6,4},{7,5},{8,10},{9,11},{10,... | collective-permute-start | bytes 442376 | tf_op jit(solution)/shard_map/ppermute | solution.py:645
  20.9 20.2 %collective-permute-start.7 = (bf16[400,1152]{1,0:T(8,128)(2,1)}, bf16[400,1152]{1,0:T(8,128)(2,1)S(1)}, u32[]{:S(2)}, u32[]{:S(2)}) collective-permute-start(bf16[400,1152]{1,0:T(8,128)(2,1)} %stage.6), channel_id=1, source_target_pairs={{0,1},{1,0},{2,3},{3,2},{4,5},{5,4},{6,7},{7,6},{8,9},{9,8},{10,11... | collective-permute-start | bytes 2764808 | tf_op jit(solution)/shard_map/ppermute | solution.py:662
  21.4 5.1 %collective-permute-start.1 = (bf16[1,288,256]{2,1,0:T(8,128)(2,1)S(1)}, bf16[1,288,256]{2,1,0:T(8,128)(2,1)S(1)}, u32[]{:S(2)}, u32[]{:S(2)}) collective-permute-start(bf16[1,288,256]{2,1,0:T(8,128)(2,1)S(1)} %bitcast.19), channel_id=1, source_target_pairs={{0,8},{4,12},{8,0},{12,4},{16,24},{20,28},{24,16},{28,20},{1,9},{5... | collective-permute-start | bytes 442376 | tf_op jit(solution)/shard_map/ppermute | solution.py:664
  21.9 5.1 %collective-permute-start.3 = (bf16[1,288,256]{2,1,0:T(8,128)(2,1)S(1)}, bf16[1,288,256]{2,1,0:T(8,128)(2,1)S(1)}, u32[]{:S(2)}, u32[]{:S(2)}) collective-permute-start(bf16[1,288,256]{2,1,0:T(8,128)(2,1)S(1)} %bitcast.22), channel_id=1, source_target_pairs={{0,16},{4,20},{8,24},{12,28},{16,0},{20,4},{24,8},{28,12},{1,17},{... | collective-permute-start | bytes 442376 | tf_op jit(solution)/shard_map/ppermute | solution.py:665
  29.5 6.7 %collective-permute-start.4 = (bf16[2,288,256]{2,1,0:T(8,128)(2,1)S(1)}, bf16[2,288,256]{2,1,0:T(8,128)(2,1)S(1)}, u32[]{:S(2)}, u32[]{:S(2)}) collective-permute-start(bf16[2,288,256]{2,1,0:T(8,128)(2,1)S(1)} %get-tuple-element.27.refs_0_), channel_id=1, source_target_pairs={{0,16},{4,20},{8,24},{12,28},{16,0},{20,4},{24,8},{28,12},{1,17},{... | collective-permute-start | bytes 884744 | tf_op jit(solution)/shard_map/ppermute | solution.py:664
  31.0 7.0 %collective-permute-start.5 = (bf16[2,288,256]{2,1,0:T(8,128)(2,1)}, bf16[2,288,256]{2,1,0:T(8,128)(2,1)}, u32[]{:S(2)}, u32[]{:S(2)}) collective-permute-start(bf16[2,288,256]{2,1,0:T(8,128)(2,1)} %get-tuple-element.28.refs_2_), channel_id=1, source_target_pairs={{0,8},{4,12},{8,0},{12,4},{16,24},{20,28},{24,16},{28,20},{1,9},{5... | collective-permute-start | bytes 884744 | tf_op jit(solution)/shard_map/ppermute | solution.py:665
  32.5 10.8 %copy-start.4 = (bf16[256,4608]{1,0:T(8,128)(2,1)S(1)}, bf16[256,4608]{1,0:T(8,128)(2,1)}, u32[]{:S(2)}) copy-start(bf16[256,4608]{1,0:T(8,128)(2,1)} %own_o_ref.3) | copy-start | bytes 7077892
  44.0 7.0 %collective-permute-start.8 = (bf16[32,1152]{1,0:T(8,128)(2,1)S(1)}, bf16[32,1152]{1,0:T(8,128)(2,1)}, u32[]{:S(2)}, u32[]{:S(2)}) collective-permute-start(bf16[32,1152]{1,0:T(8,128)(2,1)S(1)} %get-tuple-element.31), channel_id=1, source_target_pairs={{0,1},{1,2},{2,3},{3,0},{4,5},{5,6},{6,7},{7,4},{8,9},{9,10},{10,1... | collective-permute-start | bytes 221192 | tf_op jit(solution)/shard_map/ppermute | solution.py:673
  45.8 20.8 %collective-permute-start.12 = (bf16[4,288,256]{2,1,0:T(8,128)(2,1)}, bf16[4,288,256]{2,1,0:T(8,128)(2,1)}, u32[]{:S(2)}, u32[]{:S(2)}) collective-permute-start(bf16[4,288,256]{2,1,0:T(8,128)(2,1)} %get-tuple-element.30.after_ref.own_ref), channel_id=1, source_target_pairs={{0,4},{4,0},{8,12},{12,8},{16,20},{20,16},{24,28},{28,24},{1,5},{5... | collective-permute-start | bytes 1769480 | tf_op jit(solution)/shard_map/ppermute | solution.py:664
  45.8 20.8 %collective-permute-start.14 = (bf16[4,288,256]{2,1,0:T(8,128)(2,1)}, bf16[4,288,256]{2,1,0:T(8,128)(2,1)S(1)}, u32[]{:S(2)}, u32[]{:S(2)}) collective-permute-start(bf16[4,288,256]{2,1,0:T(8,128)(2,1)} %get-tuple-element.35.own_ref), channel_id=1, source_target_pairs={{0,4},{4,0},{8,12},{12,8},{16,20},{20,16},{24,28},{28,24},{1,5},{5... | collective-permute-start | bytes 1769480 | tf_op jit(solution)/shard_map/ppermute | solution.py:665
  46.3 20.2 %collective-permute-start.13 = (bf16[240,1152]{1,0:T(8,128)(2,1)}, bf16[240,1152]{1,0:T(8,128)(2,1)S(1)}, u32[]{:S(2)}, u32[]{:S(2)}) collective-permute-start(bf16[240,1152]{1,0:T(8,128)(2,1)} %copy-done.10), channel_id=1, source_target_pairs={{0,1},{1,0},{2,3},{3,2},{4,5},{5,4},{6,7},{7,6},{8,9},{9,8},{10,11... | collective-permute-start | bytes 1658888 | tf_op jit(solution)/shard_map/ppermute | solution.py:662
  46.8 14.7 %collective-permute-start.9 = (bf16[32,1152]{1,0:T(8,128)(2,1)S(1)}, bf16[32,1152]{1,0:T(8,128)(2,1)S(1)}, u32[]{:S(2)}, u32[]{:S(2)}) collective-permute-start(bf16[32,1152]{1,0:T(8,128)(2,1)S(1)} %get-tuple-element.32), channel_id=1, source_target_pairs={{0,2},{1,3},{2,0},{3,1},{4,6},{5,7},{6,4},{7,5},{8,10},{9,11},{10,... | collective-permute-start | bytes 221192 | tf_op jit(solution)/shard_map/ppermute | solution.py:673
  51.0 14.0 %collective-permute-start.10 = (bf16[32,1152]{1,0:T(8,128)(2,1)S(1)}, bf16[32,1152]{1,0:T(8,128)(2,1)S(1)}, u32[]{:S(2)}, u32[]{:S(2)}) collective-permute-start(bf16[32,1152]{1,0:T(8,128)(2,1)S(1)} %get-tuple-element.33), channel_id=1, source_target_pairs={{0,3},{1,0},{2,1},{3,2},{4,7},{5,4},{6,5},{7,6},{8,11},{9,8},{10,9... | collective-permute-start | bytes 221192 | tf_op jit(solution)/shard_map/ppermute | solution.py:673
  65.9 14.5 %collective-permute-start.11 = (bf16[1,3,32,1152]{3,2,1,0:T(8,128)(2,1)S(1)}, bf16[1,3,32,1152]{3,2,1,0:T(8,128)(2,1)S(1)}, u32[]{:S(2)}, u32[]{:S(2)}) collective-permute-start(bf16[1,3,32,1152]{3,2,1,0:T(8,128)(2,1)S(1)} %maximum_bitcast_fusion.rest_5_.refs_0_), channel_id=1, source_target_pairs={{0,8},{4,12},{8,0},{12,4},{16,24},{20,28},{24,16},{28,20},{1,9},{5... | collective-permute-start | bytes 663560 | tf_op jit(solution)/shard_map/ppermute | solution.py:679
  72.3 27.9 %collective-permute-start.16 = (bf16[784,256]{1,0:T(8,128)(2,1)S(1)}, bf16[784,256]{1,0:T(8,128)(2,1)S(1)}, u32[]{:S(2)}, u32[]{:S(2)}) collective-permute-start(bf16[784,256]{1,0:T(8,128)(2,1)S(1)} %get-tuple-element.37.rest_0_), channel_id=1, source_target_pairs={{0,2},{1,3},{2,0},{3,1},{4,6},{5,7},{6,4},{7,5},{8,10},{9,11},{10,... | collective-permute-start | bytes 1204232 | tf_op jit(solution)/shard_map/ppermute | solution.py:690
  78.2 30.3 %collective-permute-start.18 = (bf16[768,256]{1,0:T(8,128)(2,1)S(1)}, bf16[768,256]{1,0:T(8,128)(2,1)S(1)}, u32[]{:S(2)}, u32[]{:S(2)}) collective-permute-start(bf16[768,256]{1,0:T(8,128)(2,1)S(1)} %far.1.rest_0_), channel_id=1, source_target_pairs={{0,2},{1,3},{2,0},{3,1},{4,6},{5,7},{6,4},{7,5},{8,10},{9,11},{10,... | collective-permute-start | bytes 1179656 | tf_op jit(solution)/shard_map/ppermute | solution.py:697
  86.7 17.3 %collective-permute-start.15 = (bf16[2,3,32,1152]{3,2,1,0:T(8,128)(2,1)S(1)}, bf16[2,3,32,1152]{3,2,1,0:T(8,128)(2,1)S(1)}, u32[]{:S(2)}, u32[]{:S(2)}) collective-permute-start(bf16[2,3,32,1152]{3,2,1,0:T(8,128)(2,1)S(1)} %stage.8.refs_0_), channel_id=1, source_target_pairs={{0,16},{4,20},{8,24},{12,28},{16,0},{20,4},{24,8},{28,12},{1,17},{... | collective-permute-start | bytes 1327112 | tf_op jit(solution)/shard_map/ppermute | solution.py:679
  100.6 14.1 %collective-permute-start.19 = (bf16[784,256]{1,0:T(8,128)(2,1)S(1)}, bf16[784,256]{1,0:T(8,128)(2,1)S(1)}, u32[]{:S(2)}, u32[]{:S(2)}) collective-permute-start(bf16[784,256]{1,0:T(8,128)(2,1)S(1)} %get-tuple-element.39.refs_3_.after_ref.rest_2_), channel_id=1, source_target_pairs={{0,8},{4,12},{1,9},{5,13},{2,10},{6,14},{3,11},{7,15},{16,24},{20,... | collective-permute-start | bytes 1204232 | tf_op jit(solution)/shard_map/ppermute | solution.py:712
  101.9 16.0 %collective-permute-start.20 = (bf16[784,256]{1,0:T(8,128)(2,1)S(1)}, bf16[784,256]{1,0:T(8,128)(2,1)S(1)}, u32[]{:S(2)}, u32[]{:S(2)}) collective-permute-start(bf16[784,256]{1,0:T(8,128)(2,1)S(1)} %get-tuple-element.39.refs_3_.after_ref.rest_2_), channel_id=1, source_target_pairs={{0,4},{4,8},{8,12},{1,5},{5,9},{9,13},{2,6},{6,10},{10,14},{3,7},{... | collective-permute-start | bytes 1204232 | tf_op jit(solution)/shard_map/ppermute | solution.py:712
  104.6 20.4 %collective-permute-start.17 = (bf16[4,3,32,1152]{3,2,1,0:T(8,128)(2,1)S(1)}, bf16[4,3,32,1152]{3,2,1,0:T(8,128)(2,1)S(1)}, u32[]{:S(2)}, u32[]{:S(2)}) collective-permute-start(bf16[4,3,32,1152]{3,2,1,0:T(8,128)(2,1)S(1)} %stage.9.own_ref), channel_id=1, source_target_pairs={{0,4},{4,0},{8,12},{12,8},{16,20},{20,16},{24,28},{28,24},{1,5},{5... | collective-permute-start | bytes 2654216 | tf_op jit(solution)/shard_map/ppermute | solution.py:679
  124.9 8.5 %collective-permute-start.21 = (bf16[384,256]{1,0:T(8,128)(2,1)S(1)}, bf16[384,256]{1,0:T(8,128)(2,1)S(1)}, u32[]{:S(2)}, u32[]{:S(2)}) collective-permute-start(bf16[384,256]{1,0:T(8,128)(2,1)S(1)} %attend.2.rest_0_), channel_id=1, source_target_pairs={{0,2},{1,3},{2,0},{3,1},{4,6},{5,7},{6,4},{7,5},{8,10},{9,11},{10,... | collective-permute-start | bytes 589832 | tf_op jit(solution)/shard_map/ppermute | solution.py:722
  129.3 8.3 %collective-permute-start.24 = (bf16[384,256]{1,0:T(8,128)(2,1)S(1)}, bf16[384,256]{1,0:T(8,128)(2,1)S(1)}, u32[]{:S(2)}, u32[]{:S(2)}) collective-permute-start(bf16[384,256]{1,0:T(8,128)(2,1)S(1)} %attend.3.rest_0_), channel_id=1, source_target_pairs={{0,2},{1,3},{2,0},{3,1},{4,6},{5,7},{6,4},{7,5},{8,10},{9,11},{10,... | collective-permute-start | bytes 589832 | tf_op jit(solution)/shard_map/ppermute | solution.py:722
  132.2 8.7 %collective-permute-start.22 = (bf16[384,256]{1,0:T(8,128)(2,1)S(1)}, bf16[384,256]{1,0:T(8,128)(2,1)S(1)}, u32[]{:S(2)}, u32[]{:S(2)}) collective-permute-start(bf16[384,256]{1,0:T(8,128)(2,1)S(1)} %attend.2.rest_0_), channel_id=1, source_target_pairs={{0,1},{1,0},{2,3},{3,2},{4,5},{5,4},{6,7},{7,6},{8,9},{9,8},{10,11... | collective-permute-start | bytes 589832 | tf_op jit(solution)/shard_map/ppermute | solution.py:723
  133.4 9.6 %collective-permute-start.23 = (bf16[384,256]{1,0:T(8,128)(2,1)S(1)}, bf16[384,256]{1,0:T(8,128)(2,1)S(1)}, u32[]{:S(2)}, u32[]{:S(2)}) collective-permute-start(bf16[384,256]{1,0:T(8,128)(2,1)S(1)} %collective-permute-done.21.rest_1_), channel_id=1, source_target_pairs={{0,1},{1,0},{2,3},{3,2},{4,5},{5,4},{6,7},{7,6},{8,9},{9,8},{10,11... | collective-permute-start | bytes 589832 | tf_op jit(solution)/shard_map/ppermute | solution.py:724
  134.3 14.2 %collective-permute-start.25 = (bf16[384,256]{1,0:T(8,128)(2,1)S(1)}, bf16[384,256]{1,0:T(8,128)(2,1)S(1)}, u32[]{:S(2)}, u32[]{:S(2)}) collective-permute-start(bf16[384,256]{1,0:T(8,128)(2,1)S(1)} %attend.3.rest_0_), channel_id=1, source_target_pairs={{0,1},{1,0},{2,3},{3,2},{4,5},{5,4},{6,7},{7,6},{8,9},{9,8},{10,11... | collective-permute-start | bytes 589832 | tf_op jit(solution)/shard_map/ppermute | solution.py:723
  137.6 10.9 %collective-permute-start.26 = (bf16[384,256]{1,0:T(8,128)(2,1)S(1)}, bf16[384,256]{1,0:T(8,128)(2,1)S(1)}, u32[]{:S(2)}, u32[]{:S(2)}) collective-permute-start(bf16[384,256]{1,0:T(8,128)(2,1)S(1)} %collective-permute-done.24.rest_1_), channel_id=1, source_target_pairs={{0,1},{1,0},{2,3},{3,2},{4,5},{5,4},{6,7},{7,6},{8,9},{9,8},{10,11... | collective-permute-start | bytes 589832 | tf_op jit(solution)/shard_map/ppermute | solution.py:724
  152.4 5.5 %collective-permute-start.27 = (f32[1,768]{1,0:T(1,128)S(1)}, f32[1,768]{1,0:T(1,128)S(1)}, u32[]{:S(2)}, u32[]{:S(2)}) collective-permute-start(f32[1,768]{1,0:T(1,128)S(1)} %get-tuple-element.44.rest_2_), channel_id=1, source_target_pairs={{0,1},{1,2},{2,3},{3,0},{4,5},{5,6},{6,7},{7,4},{8,9},{9,10},{10,1... | collective-permute-start | bytes 9224 | tf_op jit(solution)/shard_map/ppermute | solution.py:736
  154.3 4.5 %collective-permute-start.28 = (f32[1,768]{1,0:T(1,128)S(1)}, f32[1,768]{1,0:T(1,128)S(1)}, u32[]{:S(2)}, u32[]{:S(2)}) collective-permute-start(f32[1,768]{1,0:T(1,128)S(1)} %get-tuple-element.44.rest_2_), channel_id=1, source_target_pairs={{0,2},{1,3},{2,0},{3,1},{4,6},{5,7},{6,4},{7,5},{8,10},{9,11},{10,... | collective-permute-start | bytes 9224 | tf_op jit(solution)/shard_map/ppermute | solution.py:736
  155.3 4.0 %collective-permute-start.29 = (f32[1,768]{1,0:T(1,128)S(1)}, f32[1,768]{1,0:T(1,128)S(1)}, u32[]{:S(2)}, u32[]{:S(2)}) collective-permute-start(f32[1,768]{1,0:T(1,128)S(1)} %get-tuple-element.44.rest_2_), channel_id=1, source_target_pairs={{0,3},{1,0},{2,1},{3,2},{4,7},{5,4},{6,5},{7,6},{8,11},{9,8},{10,9... | collective-permute-start | bytes 9224 | tf_op jit(solution)/shard_map/ppermute | solution.py:736
  (12 other events, 46.4 us)

commit v11 on v10

--- a/solution.py
+++ b/solution.py
@@ -25,6 +25,7 @@
 HBM = pl.BlockSpec(memory_space=pltpu.HBM)
 VMEM = pl.BlockSpec(memory_space=pltpu.VMEM)
 DOCUMENTS = 8
+HIDE = 5 * 10**10
 PARAMS = pltpu.CompilerParams(vmem_limit_bytes=48 * 1024 * 1024)
 ALL_VMEM = pltpu.CompilerParams(vmem_limit_bytes=62 * 1024 * 1024)
 
@@ -106,7 +107,7 @@
         copy.wait()
 
 
-def stage(joined, tokens, first, count, after):
+def stage(joined, tokens, first, count, after, flops=0):
     dims = [(2 * pair[0].shape[0],) + pair[0].shape[1:] for pair in joined]
     if count:
         dims.append((count, tokens.shape[1]))
@@ -116,6 +117,7 @@
         in_specs=[ANY] * (2 * len(joined) + 1 + len(after)),
         scratch_shapes=[pltpu.SemaphoreType.DMA((2 * len(joined) + 1,))],
         compiler_params=PARAMS,
+        cost_estimate=pl.CostEstimate(flops=flops, bytes_accessed=flops // 500, transcendentals=0),
         name="stage",
     )(*[piece for pair in joined for piece in pair], tokens, *after)
 
@@ -400,7 +402,7 @@
         + [pl.BlockSpec(a.shape, whole) for a in (far, sums, cosine, sine)],
         out_specs=pl.BlockSpec((rows, width), whole),
         compiler_params=PARAMS,
-        cost_estimate=pl.CostEstimate(flops=5 * 10**10, bytes_accessed=10**8, transcendentals=0),
+        cost_estimate=pl.CostEstimate(flops=HIDE, bytes_accessed=10**8, transcendentals=0),
         name="queries",
     )(near, far, sums, cosine, sine)
 
@@ -519,13 +521,20 @@
     )(seq, queries, ids, after, *blocks)
 
 
-def output_kernel(at_ref, own_o_ref, o_ref, *rest):
+def first_output_kernel(at_ref, own_o_ref, o_ref, *rest):
+    ctx_refs, out_ref = rest[:-2], rest[-1]
+    total = jnp.dot(ctx_refs[0][...], own_o_ref[...], preferred_element_type=F32)
+    for i, ctx_ref in enumerate(ctx_refs[1:]):
+        total = total + jnp.dot(ctx_ref[...], o_ref[at_ref[1 + i]], preferred_element_type=F32)
+    out_ref[...] = total
+
+
+def last_output_kernel(at_ref, part_ref, o_ref, *rest):
     ctx_refs, (before_ref, out_ref, sq_ref, acc) = rest[:-4], rest[-4:]
     step = pl.program_id(0)
-    total = jnp.dot(ctx_refs[0][...], own_o_ref[...], preferred_element_type=F32)
-    for i, ctx_ref in enumerate(ctx_refs[1:]):
-        weight = o_ref[at_ref[1 + i]]
-        total = total + jnp.dot(ctx_ref[...], weight, preferred_element_type=F32)
+    total = part_ref[...]
+    for i, ctx_ref in enumerate(ctx_refs):
+        total = total + jnp.dot(ctx_ref[...], o_ref[at_ref[i]], preferred_element_type=F32)
     out_ref[...] = total
     squares = jnp.sum(total * total, axis=1, keepdims=True)
     squares = jnp.broadcast_to(squares, acc.shape)
@@ -546,22 +555,50 @@
         sq_ref[:, done:] = acc[...].T[0:1, :]
 
 
-def output_product(column, order, o_weight, gathered, contexts, before, c):
+def column_tiles(cols):
+    tiles = 3 if cols % (3 * LANES) == 0 else 1
+    return tiles, cols // tiles
+
+
+def first_output(column, order, o_weight, gathered, contexts, after):
     chunk, width = contexts[0].shape
     others, _, cols = gathered.shape
-    tiles = 3 if cols % (3 * LANES) == 0 else 1
-    tile = cols // tiles
+    tiles, tile = column_tiles(cols)
     if cols % LANES:
         o_weight = lax.dynamic_slice_in_dim(o_weight, column * cols, cols, axis=1)
         column = jnp.int32(0)
     return pl.pallas_call(
-        output_kernel,
-        out_shape=(shape((chunk, cols), F32), shape((1, (c + 1) * chunk), F32)),
+        first_output_kernel,
+        out_shape=shape((chunk, cols), F32),
         grid_spec=pltpu.PrefetchScalarGridSpec(
             num_scalar_prefetch=1,
             grid=(tiles,),
             in_specs=[
                 pl.BlockSpec((width, tile), lambda i, at: (0, at[0] * tiles + i)),
+                pl.BlockSpec((others, width, tile), lambda i, at: (0, 0, i)),
+            ]
+            + [pl.BlockSpec((chunk, width), lambda i, at: (0, 0)) for _ in contexts]
+            + [ANY],
+            out_specs=pl.BlockSpec((chunk, tile), lambda i, at: (0, i)),
+        ),
+        compiler_params=PARAMS,
+        cost_estimate=pl.CostEstimate(flops=HIDE, bytes_accessed=10**8, transcendentals=0),
+        name="first_output",
+    )(jnp.stack([column] + order), o_weight, gathered, *contexts, after)
+
+
+def last_output(order, part, gathered, contexts, before, c):
+    chunk, width = contexts[0].shape
+    others, _, cols = gathered.shape
+    tiles, tile = column_tiles(cols)
+    return pl.pallas_call(
+        last_output_kernel,
+        out_shape=(shape((chunk, cols), F32), shape((1, (c + 1) * chunk), F32)),
+        grid_spec=pltpu.PrefetchScalarGridSpec(
+            num_scalar_prefetch=1,
+            grid=(tiles,),
+            in_specs=[
+                pl.BlockSpec((chunk, tile), lambda i, at: (0, i)),
                 pl.BlockSpec((others, width, tile), lambda i, at: (0, 0, i)),
             ]
             + [pl.BlockSpec((chunk, width), lambda i, at: (0, 0)) for _ in contexts]
@@ -573,8 +610,8 @@
             scratch_shapes=[pltpu.VMEM((chunk, LANES), F32)],
         ),
         compiler_params=PARAMS,
-        name="output",
-    )(jnp.stack([column] + order), o_weight, gathered, *contexts, before)
+        name="last_output",
+    )(jnp.stack(order), part, gathered, *contexts, before)
 
 
 def final_kernel(token_ref, gain_ref, *rest, model):
@@ -637,13 +674,18 @@
     masks_kv, masks_q = inner + [1], inner[::-1] + [1]
     last = len(masks_kv) - 1
     eighth = rows // 48 * 8
-    counts = [eighth, rows // 2 + TAIL, rows - eighth - rows // 2 - TAIL]
+    counts = [eighth, rows // 2 - 2 * TAIL, rows // 2 + 2 * TAIL - eighth]
     packed_kv, packed_q, cut = pack(
         at, q_weight, k_weight, value_weight, share, tokens, counts[0]
     )
     own_kv = lax.ppermute(packed_kv, "tensor", swap)[None]
     own_q = lax.ppermute(packed_q, "tensor", swap)[None]
     received = [lax.ppermute(cut, "tensor", ring)]
+    o_share = o_weight.shape[0] // plane
+    columns = [(z + k) % nz * cols for k in range(1, nz)]
+    pieces = cut_pieces(in_plane * o_share, columns, o_weight, o_share, cols, own_kv)
+    moved = [lax.ppermute(p, "tensor", turn(k + 1)) for k, p in enumerate(pieces)]
+
     order_kv, order_q, first = [0], [0], counts[0]
     for step, (mask_kv, mask_q) in enumerate(zip(masks_kv, masks_q)):
         after, count = [], 0
@@ -654,8 +696,8 @@
         if step < 2:
             count = counts[1 + step]
         if step == last:
-            after = [received[1]]
-        outs = stage(pairs, tokens, first, count, after)
+            after = [received[1]] + moved
+        outs = stage(pairs, tokens, first, count, after, HIDE if step == last else 0)
         if pairs:
             own_kv, own_q = outs[:2]
         if count:
@@ -667,10 +709,6 @@
         order_q = order_q + [k ^ mask_q for k in order_q]
     far_kv, far_q = (order_kv, own_kv, far_kv), (order_q, own_q, far_q)
 
-    o_share = o_weight.shape[0] // plane
-    columns = [(z + k) % nz * cols for k in range(1, nz)]
-    pieces = cut_pieces(in_plane * o_share, columns, o_weight, o_share, cols, own_kv)
-    moved = [lax.ppermute(p, "tensor", turn(k + 1)) for k, p in enumerate(pieces)]
     own_o = jnp.stack(moved)[None]
 
     def double(own, step, after):
@@ -685,7 +723,7 @@
     gains = in_gain.reshape(nz, 1, cols)
     place = jnp.stack([in_plane, side * half])
     sent_kv, x, sq = far_kv_product(
-        place, sources, gains, blocks, far_kv, [far_q[2], own_o]
+        place, sources, gains, blocks, far_kv, [far_q[2]]
     )
     got_kv = lax.ppermute(sent_kv, "tensor", swap)
     pair_o = double(own_o, 0, [])
@@ -693,14 +731,15 @@
         pair_o = double(pair_o, step, [])
     weights = (k_weight, value_weight, q_weight)
 
-    sent_q = far_product(place, sources, x, far_q, [sent_kv])
+    near = near_product(side * half + sources, x, weights, [sent_kv])
+
+    sent_q = far_product(place, sources, x, far_q, [near])
     got_q = lax.ppermute(sent_q, "tensor", swap)
-    near = near_product(side * half + sources, x, weights, [sent_q, pair_o[1]])
-    pair_o = double(pair_o, last - 1, [near])
+    pair_o = double(pair_o, last - 1, [sent_q])
     cosine, sine = rotation_table(seq * rows + jnp.arange(rows, dtype=jnp.int32))
     ids = seg_ids[None, :]
     own_kv, sums = keys_values(
-        near, got_kv, sq, ids, cosine, sine, [sent_q], model
+        near, got_kv, sq, ids, cosine, sine, [sent_q, pair_o[0]], model
     )
     pair_o = double(pair_o, last, [own_kv])
     gathered_o = lay_pieces(place, order_kv, *pair_o)
@@ -713,7 +752,7 @@
 
     queries = finished_queries(near, got_q, sums, cosine, sine, model)
     seq_at = jnp.reshape(seq, (1,))
-    branches, own_sq, after = [], sums, own_kv
+    early, late, after = [], [], own_kv
     for c in range(CHUNKS):
         context = attend(seq_at, queries, ids, after, kv_blocks, c)
         after = gathered_o
@@ -722,15 +761,18 @@
             opposite = lax.ppermute(context, "tensor", swap)
             beside = lax.ppermute(context, "tensor", pairs)
             across = lax.ppermute(opposite, "tensor", pairs)
-            contexts = [context, opposite, beside, across]
-            order = [jnp.int32(1), 2 - 2 * (z % 2), 2 * (z % 2)]
+            early.append([context, beside])
+            late.append([opposite, across])
+            order = [2 - 2 * (z % 2), jnp.int32(1), 2 * (z % 2)]
         else:
-            contexts = [context]
-            contexts += [lax.ppermute(context, "tensor", turn(k)) for k in range(1, nz)]
+            early.append([context])
+            late.append([lax.ppermute(context, "tensor", turn(k)) for k in range(1, nz)])
             order = [jnp.int32(k) for k in range(nz - 1)]
-        branch, own_sq = output_product(
-            z, order, o_weight, gathered_o, contexts, own_sq, c
-        )
+    split = len(early[0]) - 1
+    branches, own_sq = [], sums
+    for c in range(CHUNKS):
+        part = first_output(z, order[:split], o_weight, gathered_o, early[c], context)
+        branch, own_sq = last_output(order[split:], part, gathered_o, late[c], own_sq, c)
         branches.append(branch)
     squares = [own_sq]
     squares += [lax.ppermute(own_sq, "tensor", turn(k)) for k in range(1, nz)]

time: 165 us -> 160 us (0.970); the launches traced: 163 us -> 160 us
  Pallas kernels: 45.6 us -> 56.5 us
  waiting for transfers between devices: 70.7 us -> 63.1 us
  starting transfers between devices: 37.6 us -> 34.7 us
  local copies, waits for them, and re-layouts: 5.31 us -> 3.14 us
    ppermute x3, waiting for transfers between devices: 15.9 us -> 8.64 us  [per_device(): lax.ppermute(p, 'tensor', turn(k + 1))]
    ppermute x2, waiting for transfers between devices: 3.33 us -> 8.49 us  [per_device(): opposite = lax.ppermute(context, 'tensor', swap)]
    ppermute x1, waiting for transfers between devices: 3.87 us -> 0.01 us  [per_device(): got_q = lax.ppermute(sent_q, 'tensor', swap)]
    ppermute x2, starting transfers between devices: 4.08 us -> 0.34 us  [per_device(): across = lax.ppermute(opposite, 'tensor', pairs)]
    ppermute x2, starting transfers between devices: 1.17 us -> 4.84 us  [per_device(): beside = lax.ppermute(context, 'tensor', pairs)]
    ppermute x3, waiting for transfers between devices: 6.72 us -> 3.09 us  [per_device(): lax.ppermute(own_kv, PLANE, [(i, i ^ mask_kv) for i in range(plane)])]
    pallas_call x2 -> x4, Pallas kernels: 7.94 us -> 11.5 us  [the longest x2 6.46 us: first_output(): pl.pallas_call(first_output_kernel, out_shape=shape((chunk, cols), F32),...]
    ppermute x2, waiting for transfers between devices: 3.08 us -> 6.47 us  [per_device(): received.append(lax.ppermute(outs[-1], 'tensor', ring))]
  transfers between devices with their start and end apart: 30 -> 30, of which waited for: 19 -> 15; matrix products, arithmetic and copies ran while one was open for 2% -> 1% of each run, Pallas kernels for 20% -> 30%
where the time goes in v11:
time: 160 us
  waiting for transfers between devices  63.1 us (39%)
  Pallas kernels  56.5 us (35%)
  starting transfers between devices  34.7 us (22%)
  local copies, waits for them, and re-layouts  3.14 us (2%)
  other arithmetic  2.09 us (1%)
    pallas_call x2, Pallas kernels, attend(): pl.pallas_call(partial(attention_kernel, back=back, offset=c * rows), out...  11.4 us
    ppermute x1, waiting for transfers between devices, per_device(): got_kv = lax.ppermute(sent_kv, 'tensor', swap)  9.42 us
    ppermute x3, waiting for transfers between devices, per_device(): lax.ppermute(p, 'tensor', turn(k + 1))  8.64 us
    ppermute x2, waiting for transfers between devices, per_device(): kv_blocks.insert(0, lax.ppermute(own_kv, 'seq', earlier))  8.64 us
    ppermute x2, waiting for transfers between devices, per_device(): opposite = lax.ppermute(context, 'tensor', swap)  8.49 us
    ppermute x1, waiting for transfers between devices, per_device(): own_kv = lax.ppermute(packed_kv, 'tensor', swap)[None]  8.01 us
    ppermute x2, waiting for transfers between devices, per_device(): received.append(lax.ppermute(outs[-1], 'tensor', ring))  6.47 us
    pallas_call x2, Pallas kernels, first_output(): pl.pallas_call(first_output_kernel, out_shape=shape((chunk, cols), F32),...  6.46 us
  transfers between devices with their start and end apart: 30, of which 15 were waited for; matrix products, arithmetic and copies ran while one was open for 1% of the time, Pallas kernels for 30%

profile of v11, /device:TPU:2, one launch (start us, length us, event | category | flops | bytes accessed | tf_op | source)
XLA Modules:
  0.0 159.9 jit_solution(11758403260333265128)
XLA Ops:
  0.0 2.1 %pack.1 = (bf16[288,256]{1,0:T(8,128)(2,1)}, bf16[288,256]{1,0:T(8,128)(2,1)}, bf16[128,1152]{1,0:T(8,128)(2,1)}) custom-call(s32[1]{0:T(128)} %bitcast.9.at_ref, bf16[4608,256]{1,0:T(8,128)(2,1)} %q_ref.3, bf16[4608,128]{1,0:T(8,128)(2,1)} %k_ref.3, bf16[4608,128]{1,0:T(8,128)(2,1)} %v_ref.3, bf16[768,1152]{1,0:T(8,128)(2,1)} %token_ref.1), custom_call_target="tpu_custom_call" | custom-call | tf_op jit(solution)/shard_map/pack/pallas_call | solution.py:75
  3.7 2.6 %collective-permute-start = (bf16[288,256]{1,0:T(8,128)(2,1)}, bf16[288,256]{1,0:T(8,128)(2,1)S(1)}, u32[]{:S(2)}, u32[]{:S(2)}) collective-permute-start(bf16[288,256]{1,0:T(8,128)(2,1)} %get-tuple-element.25), channel_id=1, source_target_pairs={{0,2},{1,3},{2,0},{3,1},{4,6},{5,7},{6,4},{7,5},{8,10},{9,11},{10,... | collective-permute-start | bytes 442376 | tf_op jit(solution)/shard_map/ppermute | solution.py:681
  6.7 8.0 %collective-permute-done = bf16[288,256]{1,0:T(8,128)(2,1)S(1)} collective-permute-done((bf16[288,256]{1,0:T(8,128)(2,1)}, bf16[288,256]{1,0:T(8,128)(2,1)S(1)}, u32[]{:S(2)}, u32[]{:S(2)}) %collective-permute-start) | collective-permute-done | bytes 147488 | tf_op jit(solution)/shard_map/ppermute | solution.py:681
  14.7 5.0 %collective-permute-done.6 = bf16[288,256]{1,0:T(8,128)(2,1)S(1)} collective-permute-done((bf16[288,256]{1,0:T(8,128)(2,1)}, bf16[288,256]{1,0:T(8,128)(2,1)S(1)}, u32[]{:S(2)}, u32[]{:S(2)}) %collective-permute-start.6) | collective-permute-done | bytes 147488 | tf_op jit(solution)/shard_map/ppermute | solution.py:682
  22.4 3.1 %collective-permute-done.5.refs_1_ = bf16[1,288,256]{2,1,0:T(8,128)(2,1)S(1)} collective-permute-done((bf16[1,288,256]{2,1,0:T(8,128)(2,1)S(1)}, bf16[1,288,256]{2,1,0:T(8,128)(2,1)S(1)}, u32[]{:S(2)}, u32[]{:S(2)}) %collective-permute-start.5) | collective-permute-done | bytes 147488 | tf_op jit(solution)/shard_map/ppermute | solution.py:706
  26.0 2.0 %stage.5 = (bf16[2,288,256]{2,1,0:T(8,128)(2,1)}, bf16[2,288,256]{2,1,0:T(8,128)(2,1)}, bf16[288,1152]{1,0:T(8,128)(2,1)}) custom-call(bf16[1,288,256]{2,1,0:T(8,128)(2,1)S(1)} %bitcast.20, bf16[1,288,256]{2,1,0:T(8,128)(2,1)S(1)} %collective-permute-done.5.refs_1_, bf16[1,288,256]{2,1,0:T(8,128)(2,1)S(1)} %bitcast.24, ...), custom_call_target="tpu_custom_call" | custom-call | tf_op jit(solution)/shard_map/stage/pallas_call | solution.py:114
  31.2 1.7 %copy-done.6 = bf16[256,4608]{1,0:T(8,128)(2,1)S(1)} copy-done((bf16[256,4608]{1,0:T(8,128)(2,1)S(1)}, bf16[256,4608]{1,0:T(8,128)(2,1)}, u32[]{:S(2)}) %copy-start.6) | copy-done | bytes 2359320
  36.3 5.5 %collective-permute-done.1.refs_6_ = bf16[32,1152]{1,0:T(8,128)(2,1)S(1)} collective-permute-done((bf16[32,1152]{1,0:T(8,128)(2,1)S(1)}, bf16[32,1152]{1,0:T(8,128)(2,1)S(1)}, u32[]{:S(2)}, u32[]{:S(2)}) %collective-permute-start.1) | collective-permute-done | bytes 73760 | tf_op jit(solution)/shard_map/ppermute | solution.py:687
  41.9 1.9 %collective-permute-start.13 = (bf16[288,1152]{1,0:T(8,128)(2,1)}, bf16[288,1152]{1,0:T(8,128)(2,1)}, u32[]{:S(2)}, u32[]{:S(2)}) collective-permute-start(bf16[288,1152]{1,0:T(8,128)(2,1)} %get-tuple-element.34), channel_id=1, source_target_pairs={{0,1},{1,0},{2,3},{3,2},{4,5},{5,4},{6,7},{7,6},{8,9},{9,8},{10,11... | collective-permute-start | bytes 1990664 | tf_op jit(solution)/shard_map/ppermute | solution.py:704
  43.8 3.2 %collective-permute-done.3.refs_8_ = bf16[32,1152]{1,0:T(8,128)(2,1)S(1)} collective-permute-done((bf16[32,1152]{1,0:T(8,128)(2,1)S(1)}, bf16[32,1152]{1,0:T(8,128)(2,1)S(1)}, u32[]{:S(2)}, u32[]{:S(2)}) %collective-permute-start.3) | collective-permute-done | bytes 73760 | tf_op jit(solution)/shard_map/ppermute | solution.py:687
  47.0 2.3 %stage.7 = (bf16[4,288,256]{2,1,0:T(8,128)(2,1)}, bf16[4,288,256]{2,1,0:T(8,128)(2,1)}) custom-call(bf16[2,288,256]{2,1,0:T(8,128)(2,1)} %get-tuple-element.30.refs_0_, bf16[2,288,256]{2,1,0:T(8,128)(2,1)} %collective-permute-done.8.refs_1_, bf16[2,288,256]{2,1,0:T(8,128)(2,1)} %get-tuple-element.31.refs_2_, ...), custom_call_target="tpu_custom_call" | custom-call | flops 49999998976 | bytes 100000000 | tf_op jit(solution)/shard_map/stage/pallas_call | solution.py:114
  50.6 6.5 %collective-permute-done.13.rest_3_ = bf16[288,1152]{1,0:T(8,128)(2,1)} collective-permute-done((bf16[288,1152]{1,0:T(8,128)(2,1)}, bf16[288,1152]{1,0:T(8,128)(2,1)}, u32[]{:S(2)}, u32[]{:S(2)}) %collective-permute-start.13) | collective-permute-done | bytes 663584 | tf_op jit(solution)/shard_map/ppermute | solution.py:704
  57.1 6.4 %far_kv.1 = (bf16[784,256]{1,0:T(8,128)(2,1)}, bf16[2,768,1152]{2,1,0:T(8,128)(2,1)}, f32[1,768]{1,0:T(1,128)S(1)}) custom-call(s32[2]{0:T(128)S(1)} %get-tuple-element.49.place_ref, s32[2]{0:T(128)S(1)} %get-tuple-element.48.src_ref, f32[4,1,1152]{2,1,0:T(1,128)S(1)} %reshape.21.gain_ref, bf16[4,288,256]{2,1,0:T(8,128)(2,1)} %get-tuple-element.33.own_ref, ...), custom_call_target="tpu_custom_call" | custom-call | tf_op jit(solution)/shard_map/far_kv/pallas_call | solution.py:242
  63.5 1.8 %collective-permute-start.16 = (bf16[784,256]{1,0:T(8,128)(2,1)}, bf16[784,256]{1,0:T(8,128)(2,1)}, u32[]{:S(2)}, u32[]{:S(2)}) collective-permute-start(bf16[784,256]{1,0:T(8,128)(2,1)} %get-tuple-element.37.rest_0_), channel_id=1, source_target_pairs={{0,2},{1,3},{2,0},{3,1},{4,6},{5,7},{6,4},{7,5},{8,10},{9,11},{10,... | collective-permute-start | bytes 1204232 | tf_op jit(solution)/shard_map/ppermute | solution.py:728
  65.3 5.7 %near.1.rest_0_.near_ref = f32[768,512]{1,0:T(8,128)S(1)} custom-call(s32[2]{0:T(128)S(1)} %broadcast_add_fusion.src_ref, bf16[2,768,1152]{2,1,0:T(8,128)(2,1)} %get-tuple-element.36.x_ref, bf16[4608,128]{1,0:T(8,128)(2,1)S(1)} %copy-done.4, bf16[4608,128]{1,0:T(8,128)(2,1)S(1)} %copy-done.5, bf16[4608,256]{1,0:T(8,128)(2,1)} %q_ref.3, ...), custom_call_target="tpu_custom_call" | custom-call | tf_op jit(solution)/shard_map/near/pallas_call | solution.py:332
  71.0 4.9 %far.1.refs_3_.rest_0_ = bf16[768,256]{1,0:T(8,128)(2,1)S(1)} custom-call(s32[2]{0:T(128)S(1)} %get-tuple-element.49.place_ref, s32[2]{0:T(128)S(1)} %get-tuple-element.48.src_ref, bf16[2,768,1152]{2,1,0:T(8,128)(2,1)} %get-tuple-element.36.x_ref, bf16[4,288,256]{2,1,0:T(8,128)(2,1)} %get-tuple-element.35.own_ref, ...), custom_call_target="tpu_custom_call" | custom-call | tf_op jit(solution)/shard_map/far/pallas_call | solution.py:295
  80.7 9.4 %collective-permute-done.16.far_ref = bf16[784,256]{1,0:T(8,128)(2,1)} collective-permute-done((bf16[784,256]{1,0:T(8,128)(2,1)}, bf16[784,256]{1,0:T(8,128)(2,1)}, u32[]{:S(2)}, u32[]{:S(2)}) %collective-permute-start.16) | collective-permute-done | bytes 401440 | tf_op jit(solution)/shard_map/ppermute | solution.py:728
  94.4 2.1 %collective-permute-start.20 = (bf16[784,256]{1,0:T(8,128)(2,1)S(1)}, bf16[784,256]{1,0:T(8,128)(2,1)S(1)}, u32[]{:S(2)}, u32[]{:S(2)}) collective-permute-start(bf16[784,256]{1,0:T(8,128)(2,1)S(1)} %get-tuple-element.39.refs_3_.after_ref.rest_2_), channel_id=1, source_target_pairs={{0,4},{4,8},{8,12},{1,5},{5,9},{9,13},{2,6},{6,10},{10,14},{3,7},{... | collective-permute-start | bytes 1204232 | tf_op jit(solution)/shard_map/ppermute | solution.py:751
  99.4 7.8 %collective-permute-done.19.rest_0_ = bf16[784,256]{1,0:T(8,128)(2,1)S(1)} collective-permute-done((bf16[784,256]{1,0:T(8,128)(2,1)S(1)}, bf16[784,256]{1,0:T(8,128)(2,1)S(1)}, u32[]{:S(2)}, u32[]{:S(2)}) %collective-permute-start.19) | collective-permute-done | bytes 401440 | tf_op jit(solution)/shard_map/ppermute | solution.py:751
  108.1 6.9 %attend.2.rest_0_ = bf16[384,256]{1,0:T(8,128)(2,1)S(1)} custom-call(s32[1]{0:T(128)} %bitcast.16.seq_ref, bf16[768,256]{1,0:T(8,128)(2,1)S(1)} %queries.1.q_ref, s32[1,768]{1,0:T(1,128)S(1)} %broadcast_in_dim.21.id_ref, bf16[784,256]{1,0:T(8,128)(2,1)S(1)} %get-tuple-element.39.refs_3_.after_ref.rest_2_, ...), custom_call_target="tpu_custom_call" | custom-call | flops 905969664 | bytes 2359296 | tf_op jit(solution)/shard_map/attend/pallas_call | solution.py:495
  115.2 2.8 %collective-permute-start.21 = (bf16[384,256]{1,0:T(8,128)(2,1)S(1)}, bf16[384,256]{1,0:T(8,128)(2,1)S(1)}, u32[]{:S(2)}, u32[]{:S(2)}) collective-permute-start(bf16[384,256]{1,0:T(8,128)(2,1)S(1)} %attend.2.rest_0_), channel_id=1, source_target_pairs={{0,1},{1,0},{2,3},{3,2},{4,5},{5,4},{6,7},{7,6},{8,9},{9,8},{10,11... | collective-permute-start | bytes 589832 | tf_op jit(solution)/shard_map/ppermute | solution.py:762
  118.0 6.7 %collective-permute-done.22.rest_0_ = bf16[384,256]{1,0:T(8,128)(2,1)S(1)} collective-permute-done((bf16[384,256]{1,0:T(8,128)(2,1)S(1)}, bf16[384,256]{1,0:T(8,128)(2,1)S(1)}, u32[]{:S(2)}, u32[]{:S(2)}) %collective-permute-start.22) | collective-permute-done | bytes 196640 | tf_op jit(solution)/shard_map/ppermute | solution.py:761
  126.2 4.5 %attend.3.rest_2_.rest_0_ = bf16[384,256]{1,0:T(8,128)(2,1)S(1)} custom-call(s32[1]{0:T(128)} %bitcast.16.seq_ref, bf16[768,256]{1,0:T(8,128)(2,1)S(1)} %queries.1.q_ref, s32[1,768]{1,0:T(1,128)S(1)} %broadcast_in_dim.21.id_ref, bf16[3,256,1152]{2,1,0:T(8,128)(2,1)S(1)} %lay.1.after_ref.o_ref, bf16[784,256]{1,0:T(8,128)(2,1)S(1)} %collective-permute-done.19.rest_0_, ...), custom_call_target="tpu_custom_call" | custom-call | flops 905969664 | bytes 2359296 | tf_op jit(solution)/shard_map/attend/pallas_call | solution.py:495
  130.7 2.1 %collective-permute-start.24 = (bf16[384,256]{1,0:T(8,128)(2,1)S(1)}, bf16[384,256]{1,0:T(8,128)(2,1)S(1)}, u32[]{:S(2)}, u32[]{:S(2)}) collective-permute-start(bf16[384,256]{1,0:T(8,128)(2,1)S(1)} %attend.3.rest_2_.rest_0_), channel_id=1, source_target_pairs={{0,1},{1,0},{2,3},{3,2},{4,5},{5,4},{6,7},{7,6},{8,9},{9,8},{10,11... | collective-permute-start | bytes 589832 | tf_op jit(solution)/shard_map/ppermute | solution.py:762
  134.0 3.2 %first_output.2.part_ref = f32[384,1152]{1,0:T(8,128)S(1)} custom-call(s32[2]{0:T(128)S(1)} %pad_add_fusion.1.at_ref, bf16[256,4608]{1,0:T(8,128)(2,1)} %own_o_ref.3, bf16[3,256,1152]{2,1,0:T(8,128)(2,1)S(1)} %lay.1.after_ref.o_ref, bf16[384,256]{1,0:T(8,128)(2,1)S(1)} %attend.2.rest_0_, bf16[384,256]{1,0:T(8,128)(2,1)S(1)} %collective-permute-done.21.rest_1_, ...), custom_call_target="tpu_custom_call" | custom-call | flops 49999998976 | bytes 100000000 | tf_op jit(solution)/shard_map/first_output/pallas_call | solution.py:570
  137.3 2.5 %last_output.2 = (f32[384,1152]{1,0:T(8,128)S(1)}, f32[1,384]{1,0:T(1,128)S(1)}) custom-call(s32[2]{0:T(128)S(1)} %pad_add_fusion.at_ref, f32[384,1152]{1,0:T(8,128)S(1)} %first_output.2.part_ref, bf16[3,256,1152]{2,1,0:T(8,128)(2,1)S(1)} %lay.1.after_ref.o_ref, bf16[384,256]{1,0:T(8,128)(2,1)S(1)} %collective-permute-done.22.rest_0_, ...), custom_call_target="tpu_custom_call" | custom-call | tf_op jit(solution)/shard_map/last_output/pallas_call | solution.py:594
  139.8 1.7 %collective-permute-done.25.rest_0_ = bf16[384,256]{1,0:T(8,128)(2,1)S(1)} collective-permute-done((bf16[384,256]{1,0:T(8,128)(2,1)S(1)}, bf16[384,256]{1,0:T(8,128)(2,1)S(1)}, u32[]{:S(2)}, u32[]{:S(2)}) %collective-permute-start.25) | collective-permute-done | bytes 196640 | tf_op jit(solution)/shard_map/ppermute | solution.py:761
  141.9 3.2 %first_output.3.part_ref = f32[384,1152]{1,0:T(8,128)S(1)} custom-call(s32[2]{0:T(128)S(1)} %pad_add_fusion.1.at_ref, bf16[256,4608]{1,0:T(8,128)(2,1)} %own_o_ref.3, bf16[3,256,1152]{2,1,0:T(8,128)(2,1)S(1)} %lay.1.after_ref.o_ref, bf16[384,256]{1,0:T(8,128)(2,1)S(1)} %attend.3.rest_2_.rest_0_, bf16[384,256]{1,0:T(8,128)(2,1)S(1)} %collective-permute-done.24.rest_1_, ...), custom_call_target="tpu_custom_call" | custom-call | flops 49999998976 | bytes 100000000 | tf_op jit(solution)/shard_map/first_output/pallas_call | solution.py:570
  145.1 2.1 %collective-permute-done.26.rest_1_ = bf16[384,256]{1,0:T(8,128)(2,1)S(1)} collective-permute-done((bf16[384,256]{1,0:T(8,128)(2,1)S(1)}, bf16[384,256]{1,0:T(8,128)(2,1)S(1)}, u32[]{:S(2)}, u32[]{:S(2)}) %collective-permute-start.26) | collective-permute-done | bytes 196640 | tf_op jit(solution)/shard_map/ppermute | solution.py:763
  147.2 2.5 %last_output.3 = (f32[384,1152]{1,0:T(8,128)S(1)}, f32[1,768]{1,0:T(1,128)S(1)}) custom-call(s32[2]{0:T(128)S(1)} %pad_add_fusion.at_ref, f32[384,1152]{1,0:T(8,128)S(1)} %first_output.3.part_ref, bf16[3,256,1152]{2,1,0:T(8,128)(2,1)S(1)} %lay.1.after_ref.o_ref, bf16[384,256]{1,0:T(8,128)(2,1)S(1)} %collective-permute-done.25.rest_0_, ...), custom_call_target="tpu_custom_call" | custom-call | tf_op jit(solution)/shard_map/last_output/pallas_call | solution.py:594
  150.2 2.9 %collective-permute-start.28 = (f32[1,768]{1,0:T(1,128)S(1)}, f32[1,768]{1,0:T(1,128)S(1)}, u32[]{:S(2)}, u32[]{:S(2)}) collective-permute-start(f32[1,768]{1,0:T(1,128)S(1)} %get-tuple-element.44.rest_2_), channel_id=1, source_target_pairs={{0,2},{1,3},{2,0},{3,1},{4,6},{5,7},{6,4},{7,5},{8,10},{9,11},{10,... | collective-permute-start | bytes 9224 | tf_op jit(solution)/shard_map/ppermute | solution.py:778
  156.6 3.2 %finish.1 = bf16[768,1152]{1,0:T(8,128)(2,1)} custom-call(bf16[768,1152]{1,0:T(8,128)(2,1)S(1)} %copy-done, f32[1,1152]{1,0:T(1,128)S(1)} %broadcast_in_dim.17.gain_ref, f32[384,1152]{1,0:T(8,128)S(1)} %get-tuple-element.41.rest_0_, f32[384,1152]{1,0:T(8,128)S(1)} %get-tuple-element.43.rest_1_, f32[1,768]{1,0:T(1,128)S(1)} %get-tuple-element.44.rest_2_, ...), custom_call_target="tpu_custom_call" | custom-call | tf_op jit(solution)/shard_map/finish/pallas_call | solution.py:635
  (81 shorter events, 33.1 us)
Async XLA Ops:
  0.0 19.7 %copy-start = (bf16[768,1152]{1,0:T(8,128)(2,1)S(1)}, bf16[768,1152]{1,0:T(8,128)(2,1)}, u32[]{:S(2)}) copy-start(bf16[768,1152]{1,0:T(8,128)(2,1)} %token_ref.1) | copy-start | bytes 5308420
  2.1 17.6 %collective-permute-start.10 = (bf16[128,1152]{1,0:T(8,128)(2,1)}, bf16[128,1152]{1,0:T(8,128)(2,1)S(1)}, u32[]{:S(2)}, u32[]{:S(2)}) collective-permute-start(bf16[128,1152]{1,0:T(8,128)(2,1)} %get-tuple-element.32), channel_id=1, source_target_pairs={{0,1},{1,0},{2,3},{3,2},{4,5},{5,4},{6,7},{7,6},{8,9},{9,8},{10,11... | collective-permute-start | bytes 884744 | tf_op jit(solution)/shard_map/ppermute | solution.py:683
  3.7 10.9 %collective-permute-start = (bf16[288,256]{1,0:T(8,128)(2,1)}, bf16[288,256]{1,0:T(8,128)(2,1)S(1)}, u32[]{:S(2)}, u32[]{:S(2)}) collective-permute-start(bf16[288,256]{1,0:T(8,128)(2,1)} %get-tuple-element.25), channel_id=1, source_target_pairs={{0,2},{1,3},{2,0},{3,1},{4,6},{5,7},{6,4},{7,5},{8,10},{9,11},{10,... | collective-permute-start | bytes 442376 | tf_op jit(solution)/shard_map/ppermute | solution.py:681
  6.3 13.4 %collective-permute-start.6 = (bf16[288,256]{1,0:T(8,128)(2,1)}, bf16[288,256]{1,0:T(8,128)(2,1)S(1)}, u32[]{:S(2)}, u32[]{:S(2)}) collective-permute-start(bf16[288,256]{1,0:T(8,128)(2,1)} %get-tuple-element.29), channel_id=1, source_target_pairs={{0,2},{1,3},{2,0},{3,1},{4,6},{5,7},{6,4},{7,5},{8,10},{9,11},{10,... | collective-permute-start | bytes 442376 | tf_op jit(solution)/shard_map/ppermute | solution.py:682
  19.8 27.2 %collective-permute-start.11 = (bf16[352,1152]{1,0:T(8,128)(2,1)S(1)}, bf16[352,1152]{1,0:T(8,128)(2,1)}, u32[]{:S(2)}, u32[]{:S(2)}) collective-permute-start(bf16[352,1152]{1,0:T(8,128)(2,1)S(1)} %stage.6), channel_id=1, source_target_pairs={{0,1},{1,0},{2,3},{3,2},{4,5},{5,4},{6,7},{7,6},{8,9},{9,8},{10,11... | collective-permute-start | bytes 2433032 | tf_op jit(solution)/shard_map/ppermute | solution.py:704
  20.3 5.1 %collective-permute-start.5 = (bf16[1,288,256]{2,1,0:T(8,128)(2,1)S(1)}, bf16[1,288,256]{2,1,0:T(8,128)(2,1)S(1)}, u32[]{:S(2)}, u32[]{:S(2)}) collective-permute-start(bf16[1,288,256]{2,1,0:T(8,128)(2,1)S(1)} %bitcast.19), channel_id=1, source_target_pairs={{0,8},{4,12},{8,0},{12,4},{16,24},{20,28},{24,16},{28,20},{1,9},{5... | collective-permute-start | bytes 442376 | tf_op jit(solution)/shard_map/ppermute | solution.py:706
  20.8 5.1 %collective-permute-start.7 = (bf16[1,288,256]{2,1,0:T(8,128)(2,1)S(1)}, bf16[1,288,256]{2,1,0:T(8,128)(2,1)S(1)}, u32[]{:S(2)}, u32[]{:S(2)}) collective-permute-start(bf16[1,288,256]{2,1,0:T(8,128)(2,1)S(1)} %bitcast.23), channel_id=1, source_target_pairs={{0,16},{4,20},{8,24},{12,28},{16,0},{20,4},{24,8},{28,12},{1,17},{... | collective-permute-start | bytes 442376 | tf_op jit(solution)/shard_map/ppermute | solution.py:707
  28.0 18.9 %collective-permute-start.8 = (bf16[2,288,256]{2,1,0:T(8,128)(2,1)}, bf16[2,288,256]{2,1,0:T(8,128)(2,1)}, u32[]{:S(2)}, u32[]{:S(2)}) collective-permute-start(bf16[2,288,256]{2,1,0:T(8,128)(2,1)} %get-tuple-element.30.refs_0_), channel_id=1, source_target_pairs={{0,16},{4,20},{8,24},{12,28},{16,0},{20,4},{24,8},{28,12},{1,17},{... | collective-permute-start | bytes 884744 | tf_op jit(solution)/shard_map/ppermute | solution.py:706
  29.6 17.4 %collective-permute-start.9 = (bf16[2,288,256]{2,1,0:T(8,128)(2,1)}, bf16[2,288,256]{2,1,0:T(8,128)(2,1)}, u32[]{:S(2)}, u32[]{:S(2)}) collective-permute-start(bf16[2,288,256]{2,1,0:T(8,128)(2,1)} %get-tuple-element.31.refs_2_), channel_id=1, source_target_pairs={{0,8},{4,12},{8,0},{12,4},{16,24},{20,28},{24,16},{28,20},{1,9},{5... | collective-permute-start | bytes 884744 | tf_op jit(solution)/shard_map/ppermute | solution.py:707
  33.5 8.3 %collective-permute-start.1 = (bf16[32,1152]{1,0:T(8,128)(2,1)S(1)}, bf16[32,1152]{1,0:T(8,128)(2,1)S(1)}, u32[]{:S(2)}, u32[]{:S(2)}) collective-permute-start(bf16[32,1152]{1,0:T(8,128)(2,1)S(1)} %get-tuple-element.26), channel_id=1, source_target_pairs={{0,1},{1,2},{2,3},{3,0},{4,5},{5,6},{6,7},{7,4},{8,9},{9,10},{10,1... | collective-permute-start | bytes 221192 | tf_op jit(solution)/shard_map/ppermute | solution.py:687
  35.1 6.8 %collective-permute-start.2 = (bf16[32,1152]{1,0:T(8,128)(2,1)S(1)}, bf16[32,1152]{1,0:T(8,128)(2,1)S(1)}, u32[]{:S(2)}, u32[]{:S(2)}) collective-permute-start(bf16[32,1152]{1,0:T(8,128)(2,1)S(1)} %get-tuple-element.27), channel_id=1, source_target_pairs={{0,2},{1,3},{2,0},{3,1},{4,6},{5,7},{6,4},{7,5},{8,10},{9,11},{10,... | collective-permute-start | bytes 221192 | tf_op jit(solution)/shard_map/ppermute | solution.py:687
  41.7 5.2 %collective-permute-start.3 = (bf16[32,1152]{1,0:T(8,128)(2,1)S(1)}, bf16[32,1152]{1,0:T(8,128)(2,1)S(1)}, u32[]{:S(2)}, u32[]{:S(2)}) collective-permute-start(bf16[32,1152]{1,0:T(8,128)(2,1)S(1)} %get-tuple-element.28), channel_id=1, source_target_pairs={{0,3},{1,0},{2,1},{3,2},{4,7},{5,4},{6,5},{7,6},{8,11},{9,8},{10,9... | collective-permute-start | bytes 221192 | tf_op jit(solution)/shard_map/ppermute | solution.py:687
  41.9 15.2 %collective-permute-start.13 = (bf16[288,1152]{1,0:T(8,128)(2,1)}, bf16[288,1152]{1,0:T(8,128)(2,1)}, u32[]{:S(2)}, u32[]{:S(2)}) collective-permute-start(bf16[288,1152]{1,0:T(8,128)(2,1)} %get-tuple-element.34), channel_id=1, source_target_pairs={{0,1},{1,0},{2,3},{3,2},{4,5},{5,4},{6,7},{7,6},{8,9},{9,8},{10,11... | collective-permute-start | bytes 1990664 | tf_op jit(solution)/shard_map/ppermute | solution.py:704
  49.3 7.8 %collective-permute-start.12 = (bf16[4,288,256]{2,1,0:T(8,128)(2,1)}, bf16[4,288,256]{2,1,0:T(8,128)(2,1)}, u32[]{:S(2)}, u32[]{:S(2)}) collective-permute-start(bf16[4,288,256]{2,1,0:T(8,128)(2,1)} %get-tuple-element.33.own_ref), channel_id=1, source_target_pairs={{0,4},{4,0},{8,12},{12,8},{16,20},{20,16},{24,28},{28,24},{1,5},{5... | collective-permute-start | bytes 1769480 | tf_op jit(solution)/shard_map/ppermute | solution.py:706
  49.3 7.7 %collective-permute-start.14 = (bf16[4,288,256]{2,1,0:T(8,128)(2,1)}, bf16[4,288,256]{2,1,0:T(8,128)(2,1)S(1)}, u32[]{:S(2)}, u32[]{:S(2)}) collective-permute-start(bf16[4,288,256]{2,1,0:T(8,128)(2,1)} %get-tuple-element.35.own_ref), channel_id=1, source_target_pairs={{0,4},{4,0},{8,12},{12,8},{16,20},{20,16},{24,28},{28,24},{1,5},{5... | collective-permute-start | bytes 1769480 | tf_op jit(solution)/shard_map/ppermute | solution.py:707
  50.0 27.2 %collective-permute-start.4 = (bf16[1,3,32,1152]{3,2,1,0:T(8,128)(2,1)S(1)}, bf16[1,3,32,1152]{3,2,1,0:T(8,128)(2,1)S(1)}, u32[]{:S(2)}, u32[]{:S(2)}) collective-permute-start(bf16[1,3,32,1152]{3,2,1,0:T(8,128)(2,1)S(1)} %maximum_bitcast_fusion.refs_0_), channel_id=1, source_target_pairs={{0,8},{4,12},{8,0},{12,4},{16,24},{20,28},{24,16},{28,20},{1,9},{5... | collective-permute-start | bytes 663560 | tf_op jit(solution)/shard_map/ppermute | solution.py:717
  57.1 8.2 %copy-start.4 = (bf16[4608,128]{1,0:T(8,128)(2,1)S(1)}, bf16[4608,128]{1,0:T(8,128)(2,1)}, u32[]{:S(2)}) copy-start(bf16[4608,128]{1,0:T(8,128)(2,1)} %k_ref.3) | copy-start | bytes 3538948
  63.5 26.7 %collective-permute-start.16 = (bf16[784,256]{1,0:T(8,128)(2,1)}, bf16[784,256]{1,0:T(8,128)(2,1)}, u32[]{:S(2)}, u32[]{:S(2)}) collective-permute-start(bf16[784,256]{1,0:T(8,128)(2,1)} %get-tuple-element.37.rest_0_), channel_id=1, source_target_pairs={{0,2},{1,3},{2,0},{3,1},{4,6},{5,7},{6,4},{7,5},{8,10},{9,11},{10,... | collective-permute-start | bytes 1204232 | tf_op jit(solution)/shard_map/ppermute | solution.py:728
  76.0 22.0 %collective-permute-start.18 = (bf16[768,256]{1,0:T(8,128)(2,1)S(1)}, bf16[768,256]{1,0:T(8,128)(2,1)}, u32[]{:S(2)}, u32[]{:S(2)}) collective-permute-start(bf16[768,256]{1,0:T(8,128)(2,1)S(1)} %far.1.refs_3_.rest_0_), channel_id=1, source_target_pairs={{0,2},{1,3},{2,0},{3,1},{4,6},{5,7},{6,4},{7,5},{8,10},{9,11},{10,... | collective-permute-start | bytes 1179656 | tf_op jit(solution)/shard_map/ppermute | solution.py:737
  77.8 18.8 %collective-permute-start.15 = (bf16[2,3,32,1152]{3,2,1,0:T(8,128)(2,1)S(1)}, bf16[2,3,32,1152]{3,2,1,0:T(8,128)(2,1)}, u32[]{:S(2)}, u32[]{:S(2)}) collective-permute-start(bf16[2,3,32,1152]{3,2,1,0:T(8,128)(2,1)S(1)} %stage.8.rest_1_.refs_0_), channel_id=1, source_target_pairs={{0,16},{4,20},{8,24},{12,28},{16,0},{20,4},{24,8},{28,12},{1,17},{... | collective-permute-start | bytes 1327112 | tf_op jit(solution)/shard_map/ppermute | solution.py:717
  93.0 14.3 %collective-permute-start.19 = (bf16[784,256]{1,0:T(8,128)(2,1)S(1)}, bf16[784,256]{1,0:T(8,128)(2,1)S(1)}, u32[]{:S(2)}, u32[]{:S(2)}) collective-permute-start(bf16[784,256]{1,0:T(8,128)(2,1)S(1)} %get-tuple-element.39.refs_3_.after_ref.rest_2_), channel_id=1, source_target_pairs={{0,8},{4,12},{1,9},{5,13},{2,10},{6,14},{3,11},{7,15},{16,24},{20,... | collective-permute-start | bytes 1204232 | tf_op jit(solution)/shard_map/ppermute | solution.py:751
  94.4 13.6 %collective-permute-start.20 = (bf16[784,256]{1,0:T(8,128)(2,1)S(1)}, bf16[784,256]{1,0:T(8,128)(2,1)S(1)}, u32[]{:S(2)}, u32[]{:S(2)}) collective-permute-start(bf16[784,256]{1,0:T(8,128)(2,1)S(1)} %get-tuple-element.39.refs_3_.after_ref.rest_2_), channel_id=1, source_target_pairs={{0,4},{4,8},{8,12},{1,5},{5,9},{9,13},{2,6},{6,10},{10,14},{3,7},{... | collective-permute-start | bytes 1204232 | tf_op jit(solution)/shard_map/ppermute | solution.py:751
  97.9 26.9 %collective-permute-start.17 = (bf16[4,3,32,1152]{3,2,1,0:T(8,128)(2,1)S(1)}, bf16[4,3,32,1152]{3,2,1,0:T(8,128)(2,1)S(1)}, u32[]{:S(2)}, u32[]{:S(2)}) collective-permute-start(bf16[4,3,32,1152]{3,2,1,0:T(8,128)(2,1)S(1)} %stage.9.own_ref), channel_id=1, source_target_pairs={{0,4},{4,0},{8,12},{12,8},{16,20},{20,16},{24,28},{28,24},{1,5},{5... | collective-permute-start | bytes 2654216 | tf_op jit(solution)/shard_map/ppermute | solution.py:717
  115.0 9.7 %collective-permute-start.22 = (bf16[384,256]{1,0:T(8,128)(2,1)S(1)}, bf16[384,256]{1,0:T(8,128)(2,1)S(1)}, u32[]{:S(2)}, u32[]{:S(2)}) collective-permute-start(bf16[384,256]{1,0:T(8,128)(2,1)S(1)} %attend.2.rest_0_), channel_id=1, source_target_pairs={{0,2},{1,3},{2,0},{3,1},{4,6},{5,7},{6,4},{7,5},{8,10},{9,11},{10,... | collective-permute-start | bytes 589832 | tf_op jit(solution)/shard_map/ppermute | solution.py:761
  115.2 18.9 %collective-permute-start.21 = (bf16[384,256]{1,0:T(8,128)(2,1)S(1)}, bf16[384,256]{1,0:T(8,128)(2,1)S(1)}, u32[]{:S(2)}, u32[]{:S(2)}) collective-permute-start(bf16[384,256]{1,0:T(8,128)(2,1)S(1)} %attend.2.rest_0_), channel_id=1, source_target_pairs={{0,1},{1,0},{2,3},{3,2},{4,5},{5,4},{6,7},{7,6},{8,9},{9,8},{10,11... | collective-permute-start | bytes 589832 | tf_op jit(solution)/shard_map/ppermute | solution.py:762
  124.7 12.5 %collective-permute-start.23 = (bf16[384,256]{1,0:T(8,128)(2,1)S(1)}, bf16[384,256]{1,0:T(8,128)(2,1)S(1)}, u32[]{:S(2)}, u32[]{:S(2)}) collective-permute-start(bf16[384,256]{1,0:T(8,128)(2,1)S(1)} %collective-permute-done.22.rest_0_), channel_id=1, source_target_pairs={{0,1},{1,0},{2,3},{3,2},{4,5},{5,4},{6,7},{7,6},{8,9},{9,8},{10,11... | collective-permute-start | bytes 589832 | tf_op jit(solution)/shard_map/ppermute | solution.py:763
  130.7 11.2 %collective-permute-start.24 = (bf16[384,256]{1,0:T(8,128)(2,1)S(1)}, bf16[384,256]{1,0:T(8,128)(2,1)S(1)}, u32[]{:S(2)}, u32[]{:S(2)}) collective-permute-start(bf16[384,256]{1,0:T(8,128)(2,1)S(1)} %attend.3.rest_2_.rest_0_), channel_id=1, source_target_pairs={{0,1},{1,0},{2,3},{3,2},{4,5},{5,4},{6,7},{7,6},{8,9},{9,8},{10,11... | collective-permute-start | bytes 589832 | tf_op jit(solution)/shard_map/ppermute | solution.py:762
  132.8 8.8 %collective-permute-start.25 = (bf16[384,256]{1,0:T(8,128)(2,1)S(1)}, bf16[384,256]{1,0:T(8,128)(2,1)S(1)}, u32[]{:S(2)}, u32[]{:S(2)}) collective-permute-start(bf16[384,256]{1,0:T(8,128)(2,1)S(1)} %attend.3.rest_2_.rest_0_), channel_id=1, source_target_pairs={{0,2},{1,3},{2,0},{3,1},{4,6},{5,7},{6,4},{7,5},{8,10},{9,11},{10,... | collective-permute-start | bytes 589832 | tf_op jit(solution)/shard_map/ppermute | solution.py:761
  141.6 5.7 %collective-permute-start.26 = (bf16[384,256]{1,0:T(8,128)(2,1)S(1)}, bf16[384,256]{1,0:T(8,128)(2,1)S(1)}, u32[]{:S(2)}, u32[]{:S(2)}) collective-permute-start(bf16[384,256]{1,0:T(8,128)(2,1)S(1)} %collective-permute-done.25.rest_0_), channel_id=1, source_target_pairs={{0,1},{1,0},{2,3},{3,2},{4,5},{5,4},{6,7},{7,6},{8,9},{9,8},{10,11... | collective-permute-start | bytes 589832 | tf_op jit(solution)/shard_map/ppermute | solution.py:763
  149.8 5.4 %collective-permute-start.27 = (f32[1,768]{1,0:T(1,128)S(1)}, f32[1,768]{1,0:T(1,128)S(1)}, u32[]{:S(2)}, u32[]{:S(2)}) collective-permute-start(f32[1,768]{1,0:T(1,128)S(1)} %get-tuple-element.44.rest_2_), channel_id=1, source_target_pairs={{0,1},{1,2},{2,3},{3,0},{4,5},{5,6},{6,7},{7,4},{8,9},{9,10},{10,1... | collective-permute-start | bytes 9224 | tf_op jit(solution)/shard_map/ppermute | solution.py:778
  150.2 5.1 %collective-permute-start.28 = (f32[1,768]{1,0:T(1,128)S(1)}, f32[1,768]{1,0:T(1,128)S(1)}, u32[]{:S(2)}, u32[]{:S(2)}) collective-permute-start(f32[1,768]{1,0:T(1,128)S(1)} %get-tuple-element.44.rest_2_), channel_id=1, source_target_pairs={{0,2},{1,3},{2,0},{3,1},{4,6},{5,7},{6,4},{7,5},{8,10},{9,11},{10,... | collective-permute-start | bytes 9224 | tf_op jit(solution)/shard_map/ppermute | solution.py:778
  153.0 3.6 %collective-permute-start.29 = (f32[1,768]{1,0:T(1,128)S(1)}, f32[1,768]{1,0:T(1,128)S(1)}, u32[]{:S(2)}, u32[]{:S(2)}) collective-permute-start(f32[1,768]{1,0:T(1,128)S(1)} %get-tuple-element.44.rest_2_), channel_id=1, source_target_pairs={{0,3},{1,0},{2,1},{3,2},{4,7},{5,4},{6,5},{7,6},{8,11},{9,8},{10,9... | collective-permute-start | bytes 9224 | tf_op jit(solution)/shard_map/ppermute | solution.py:778
  (8 other events, 38.8 us)

commit v12 on v11

--- a/solution.py
+++ b/solution.py
@@ -87,6 +87,22 @@
     )(at, q_weight, k_weight, v_weight, tokens)
 
 
+def gate_kernel(x_ref, after_ref, out_ref):
+    pass
+
+
+def gate(x, after):
+    return pl.pallas_call(
+        gate_kernel,
+        out_shape=shape(x.shape, x.dtype),
+        in_specs=[ANY, ANY],
+        out_specs=ANY,
+        input_output_aliases={0: 0},
+        compiler_params=PARAMS,
+        name="gate",
+    )(x, after)
+
+
 def stage_kernel(*refs, pairs, first, count):
     outputs = pairs + (1 if count else 0)
     ins, outs, sems = refs[: -outputs - 1], refs[-outputs - 1 : -1], refs[-1]
@@ -208,15 +224,23 @@
     return total
 
 
-def far_kv_kernel(place_ref, src_ref, gain_ref, own_ref, got_ref, *rest, order, cuts):
-    x_refs, (out_ref, x_out, sq_ref, weight, sems) = rest[: sum(cuts)], rest[-5:]
+def far_kv_kernel(
+    place_ref, src_ref, gain_ref, own_ref, got_ref, token_ref, *rest, order, cuts, first
+):
+    x_refs, (out_ref, x_out, sq_ref, weight, tokens, sems) = rest[: sum(cuts)], rest[-6:]
+    rows = x_out.shape[1]
     copies = place_weights(place_ref, own_ref, got_ref, weight, sems, order)
-    rows = x_out.shape[1]
+    mine = pltpu.make_async_copy(
+        token_ref.at[pl.ds(first, rows)], tokens, sems.at[len(order)]
+    )
+    mine.start()
     columns, at = [], 0
-    for k, pieces in enumerate(cuts):
+    for k, pieces in [(k + 1, pieces) for k, pieces in enumerate(cuts)] + [(0, 1)]:
+        if k == 0:
+            mine.wait()
         gain = gain_ref[place_ref[1] + src_ref[k]]
         column, row = [], 0
-        for x_ref in x_refs[at : at + pieces]:
+        for x_ref in x_refs[at : at + pieces] if k else [tokens]:
             x = x_ref[...].astype(F32)
             column.append(jnp.sum(x * x, axis=1, keepdims=True))
             x_out[k, row : row + x.shape[0]] = (x * gain).astype(BF16)
@@ -232,38 +256,46 @@
     out_ref[rows:, :] = lines_of((high, sq - high), out_ref.shape[1])
 
 
-def far_kv_product(place, sources, gains, blocks, gathered, after):
+def far_kv_product(place, sources, gains, tokens, first, blocks, gathered, after):
     order, own, got = gathered
     _, share, width = own.shape
-    rows, cols = blocks[0][0].shape
+    cols = tokens.shape[1]
+    rows = sum(piece.shape[0] for piece in blocks[0])
     pieces = [piece for block in blocks for piece in block]
-    dims = [(rows + TAIL, width), (len(blocks), rows, cols), (1, rows)]
+    dims = [(rows + TAIL, width), (len(blocks) + 1, rows, cols), (1, rows)]
     whole = lambda d: pl.BlockSpec(d, lambda i, p, s: (0,) * len(d))
     return pl.pallas_call(
-        partial(far_kv_kernel, order=order, cuts=[len(block) for block in blocks]),
+        partial(
+            far_kv_kernel, order=order, cuts=[len(block) for block in blocks], first=first
+        ),
         out_shape=tuple(shape(d, t) for d, t in zip(dims, (BF16, BF16, F32))),
         grid_spec=pltpu.PrefetchScalarGridSpec(
             num_scalar_prefetch=2,
             grid=(1,),
-            in_specs=[whole(gains.shape), ANY, ANY]
+            in_specs=[whole(gains.shape), ANY, ANY, ANY]
             + [whole(piece.shape) for piece in pieces]
             + [ANY for _ in after],
             out_specs=[whole(d) for d in dims],
             scratch_shapes=[
                 pltpu.VMEM((len(order) * share, width), BF16),
-                pltpu.SemaphoreType.DMA((len(order),)),
+                pltpu.VMEM((rows, cols), BF16),
+                pltpu.SemaphoreType.DMA((len(order) + 1,)),
             ],
         ),
         compiler_params=PARAMS,
         name="far_kv",
-    )(place, sources, gains, own, got, *pieces, *after)
-
-
-def far_kernel(place_ref, src_ref, x_ref, own_ref, got_ref, *rest, order):
-    out_ref, weight, sems = rest[-3:]
+    )(place, sources, gains, own, got, tokens, *pieces, *after)
+
+
+def far_kernel(place_ref, src_ref, own_ref, got_ref, *rest, order, groups):
+    x_refs, (out_ref, weight, sems) = rest[:groups], rest[-3:]
     for copy in place_weights(place_ref, own_ref, got_ref, weight, sems, order):
         copy.wait()
-    out_ref[...] = far_sum(src_ref, x_ref, weight).astype(BF16)
+    row = 0
+    for x_ref in x_refs:
+        rows = x_ref.shape[1]
+        out_ref[row : row + rows, :] = far_sum(src_ref, x_ref, weight).astype(BF16)
+        row += rows
 
 
 def lines_of(rows, width):
@@ -288,17 +320,18 @@
     return rows
 
 
-def far_product(place, sources, x, gathered, after):
+def far_product(place, sources, xs, gathered, after):
     order, own, got = gathered
     _, share, width = own.shape
-    rows = x.shape[1]
-    return pl.pallas_call(
-        partial(far_kernel, order=order),
+    rows = sum(x.shape[1] for x in xs)
+    return pl.pallas_call(
+        partial(far_kernel, order=order, groups=len(xs)),
         out_shape=shape((rows, width), BF16),
         grid_spec=pltpu.PrefetchScalarGridSpec(
             num_scalar_prefetch=2,
             grid=(1,),
-            in_specs=[pl.BlockSpec(x.shape, lambda i, p, s: (0, 0, 0)), ANY, ANY]
+            in_specs=[ANY, ANY]
+            + [pl.BlockSpec(x.shape, lambda i, p, s: (0, 0, 0)) for x in xs]
             + [ANY for _ in after],
             out_specs=pl.BlockSpec((rows, width), lambda i, p, s: (0, 0)),
             scratch_shapes=[
@@ -308,7 +341,7 @@
         ),
         compiler_params=PARAMS,
         name="far",
-    )(place, sources, x, own, got, *after)
+    )(place, sources, own, got, *xs, *after)
 
 
 def near_kernel(src_ref, x_ref, k_ref, v_ref, q_ref, *rest):
@@ -345,66 +378,81 @@
     )(sources, x, *weights, *after)
 
 
-def keys_kernel(near_ref, far_ref, sq_ref, id_ref, cos_ref, sin_ref, *rest, model):
+def keys_kernel(id_ref, cos_ref, sin_ref, *rest, model, groups):
+    near_refs, far_refs, sq_refs = (rest[g * groups : (g + 1) * groups] for g in range(3))
     out_ref, sum_ref = rest[-2:]
-    rows, width = near_ref.shape[0], far_ref.shape[1]
-    tail = far_ref[rows:, :].astype(F32)
-    total = sum(rows_of(tail, 2, rows), sq_ref[...])
-    factor = to_column(lax.rsqrt(total / model + epsilon))
-    sum_ref[...] = total
+    width, rows = out_ref.shape[1], out_ref.shape[0] - TAIL
     keys, values = slice(0, HEAD_SIZE), slice(HEAD_SIZE, 2 * HEAD_SIZE)
-    part = (near_ref[:, keys] + far_ref[:rows, keys].astype(F32)) * factor
-    part = rotate(part, cos_ref[...], sin_ref[...]).astype(BF16)
+    key_parts, value_parts, first = [], [], 0
+    for near_ref, far_ref, sq_ref in zip(near_refs, far_refs, sq_refs):
+        count = near_ref.shape[0]
+        at = slice(first, first + count)
+        tail = far_ref[count:, :].astype(F32)
+        total = sum(rows_of(tail, 2, count), sq_ref[...])
+        factor = to_column(lax.rsqrt(total / model + epsilon))
+        sum_ref[:, at] = total
+        part = (near_ref[:, keys] + far_ref[:count, keys].astype(F32)) * factor
+        key_parts.append(rotate(part, cos_ref[at, :], sin_ref[at, :]).astype(BF16))
+        part = (near_ref[:, values] + far_ref[:count, values].astype(F32)) * factor
+        value_parts.append(part.T.astype(BF16))
+        first += count
+    part = jnp.concatenate(key_parts, axis=0)
     out_ref[: rows // 2, keys] = part[: rows // 2]
     out_ref[: rows // 2, values] = part[rows // 2 :]
-    part = (near_ref[:, values] + far_ref[:rows, values].astype(F32)) * factor
-    part = part.T.astype(BF16)
+    part = jnp.concatenate(value_parts, axis=1)
     for i, at in enumerate(range(0, rows, width)):
         row = rows // 2 + i * HEAD_SIZE
         out_ref[row : row + HEAD_SIZE, :] = part[:, at : at + width]
     out_ref[rows:, :] = lines_of((id_ref[...].astype(F32),), width)
 
 
-def keys_values(near, far, sq, ids, cosine, sine, after, model):
-    rows, width = near.shape[0], far.shape[1]
+def keys_values(nears, fars, sqs, ids, cosine, sine, after, model):
+    rows, width = cosine.shape[0], fars[0].shape[1]
     whole = lambda i: (0, 0)
-    return pl.pallas_call(
-        partial(keys_kernel, model=model),
-        out_shape=(shape(far.shape, BF16), shape(sq.shape, F32)),
+    dims = [(rows + TAIL, width), (1, rows)]
+    return pl.pallas_call(
+        partial(keys_kernel, model=model, groups=len(nears)),
+        out_shape=tuple(shape(d, t) for d, t in zip(dims, (BF16, F32))),
         grid=(1,),
-        in_specs=[pl.BlockSpec((rows, width), whole)]
-        + [pl.BlockSpec(a.shape, whole) for a in (far, sq, ids, cosine, sine)]
+        in_specs=[pl.BlockSpec(a.shape, whole) for a in (ids, cosine, sine)]
+        + [pl.BlockSpec((near.shape[0], width), whole) for near in nears]
+        + [pl.BlockSpec(a.shape, whole) for a in (*fars, *sqs)]
         + [ANY for _ in after],
-        out_specs=[pl.BlockSpec(far.shape, whole), pl.BlockSpec(sq.shape, whole)],
+        out_specs=[pl.BlockSpec(d, whole) for d in dims],
         compiler_params=PARAMS,
         name="keys",
-    )(near, far, sq, ids, cosine, sine, *after)
-
-
-def queries_kernel(near_ref, far_ref, sum_ref, cos_ref, sin_ref, out_ref, *, model):
+    )(ids, cosine, sine, *nears, *fars, *sqs, *after)
+
+
+def queries_kernel(far_ref, sum_ref, cos_ref, sin_ref, *rest, model):
+    near_refs, out_ref = rest[:-1], rest[-1]
     scale = query_scale * math.log2(math.e)
-    factor = to_column(lax.rsqrt(sum_ref[...] / model + epsilon) * scale)
-    for c in range(0, out_ref.shape[1], HEAD_SIZE):
-        at = slice(c, c + HEAD_SIZE)
-        part = (near_ref[:, at] + far_ref[:, at].astype(F32)) * factor
-        out_ref[:, at] = rotate(part, cos_ref[...], sin_ref[...]).astype(BF16)
-
-
-def finished_queries(near, far, sums, cosine, sine, model):
+    first = 0
+    for near_ref in near_refs:
+        rows = slice(first, first + near_ref.shape[0])
+        factor = to_column(lax.rsqrt(sum_ref[:, rows] / model + epsilon) * scale)
+        for c in range(0, out_ref.shape[1], HEAD_SIZE):
+            at = slice(c, c + HEAD_SIZE)
+            part = (near_ref[:, at] + far_ref[rows, at].astype(F32)) * factor
+            out_ref[rows, at] = rotate(part, cos_ref[rows, :], sin_ref[rows, :]).astype(BF16)
+        first += near_ref.shape[0]
+
+
+def finished_queries(nears, far, sums, cosine, sine, model):
     rows, width = far.shape
-    last = near.shape[1] // width - 1
+    last = nears[0].shape[1] // width - 1
     whole = lambda i: (0, 0)
     return pl.pallas_call(
         partial(queries_kernel, model=model),
         out_shape=shape((rows, width), BF16),
         grid=(1,),
-        in_specs=[pl.BlockSpec((rows, width), lambda i: (0, last))]
-        + [pl.BlockSpec(a.shape, whole) for a in (far, sums, cosine, sine)],
+        in_specs=[pl.BlockSpec(a.shape, whole) for a in (far, sums, cosine, sine)]
+        + [pl.BlockSpec((near.shape[0], width), lambda i: (0, last)) for near in nears],
         out_specs=pl.BlockSpec((rows, width), whole),
         compiler_params=PARAMS,
         cost_estimate=pl.CostEstimate(flops=HIDE, bytes_accessed=10**8, transcendentals=0),
         name="queries",
-    )(near, far, sums, cosine, sine)
+    )(far, sums, cosine, sine, *nears)
 
 
 def attention_kernel(seq_ref, q_ref, id_ref, after_ref, *rest, back, offset):
@@ -673,8 +721,7 @@
     inner = seq_bits + group_bits
     masks_kv, masks_q = inner + [1], inner[::-1] + [1]
     last = len(masks_kv) - 1
-    eighth = rows // 48 * 8
-    counts = [eighth, rows // 2 - 2 * TAIL, rows // 2 + 2 * TAIL - eighth]
+    counts = [rows // 6, rows // 2 - rows // 6, rows // 2]
     packed_kv, packed_q, cut = pack(
         at, q_weight, k_weight, value_weight, share, tokens, counts[0]
     )
@@ -717,29 +764,38 @@
         return own, lax.ppermute(own, PLANE, [(i, i ^ masks_kv[step]) for i in range(plane)])
 
     sources = (within + half - jnp.arange(half, dtype=jnp.int32)) % half
-    blocks = [[tokens], received]
-    for _ in range(half - 2):
-        blocks.append([lax.ppermute(part, "tensor", ring) for part in blocks[-1]])
     gains = in_gain.reshape(nz, 1, cols)
     place = jnp.stack([in_plane, side * half])
-    sent_kv, x, sq = far_kv_product(
-        place, sources, gains, blocks, far_kv, [far_q[2]]
-    )
-    got_kv = lax.ppermute(sent_kv, "tensor", swap)
+    weights = (k_weight, value_weight, q_weight)
     pair_o = double(own_o, 0, [])
     for step in range(1, last - 1):
         pair_o = double(pair_o, step, [])
-    weights = (k_weight, value_weight, q_weight)
-
-    near = near_product(side * half + sources, x, weights, [sent_kv])
-
-    sent_q = far_product(place, sources, x, far_q, [near])
+    xs, sqs, got_kv, nears, first, after = [], [], [], [], 0, [far_q[2]]
+    for pieces in (received[:2], received[2:]):
+        blocks = [pieces]
+        for _ in range(half - 2):
+            blocks.append([lax.ppermute(part, "tensor", ring) for part in blocks[-1]])
+        sent_kv, x, sq = far_kv_product(
+            place, sources, gains, tokens, first, blocks, far_kv, after
+        )
+        xs.append(x)
+        sqs.append(sq)
+        got_kv.append(lax.ppermute(sent_kv, "tensor", swap))
+        if not first:
+            nears.append(near_product(side * half + sources, x, weights, [sent_kv]))
+            after = nears
+        first += x.shape[1]
+
+    after = [sent_kv, got_kv[0]]
+    nears.append(near_product(side * half + sources, xs[1], weights, after))
+
+    sent_q = far_product(place, sources, xs, far_q, [nears[1]])
     got_q = lax.ppermute(sent_q, "tensor", swap)
     pair_o = double(pair_o, last - 1, [sent_q])
     cosine, sine = rotation_table(seq * rows + jnp.arange(rows, dtype=jnp.int32))
     ids = seg_ids[None, :]
     own_kv, sums = keys_values(
-        near, got_kv, sq, ids, cosine, sine, [sent_q, pair_o[0]], model
+        nears, got_kv, sqs, ids, cosine, sine, [sent_q, pair_o[0]], model
     )
     pair_o = double(pair_o, last, [own_kv])
     gathered_o = lay_pieces(place, order_kv, *pair_o)
@@ -750,16 +806,20 @@
         earlier = [(i, i + k) for i in range(nseq - k)]
         kv_blocks.insert(0, lax.ppermute(own_kv, "seq", earlier))
 
-    queries = finished_queries(near, got_q, sums, cosine, sine, model)
+    queries = finished_queries(nears, got_q, sums, cosine, sine, model)
     seq_at = jnp.reshape(seq, (1,))
-    early, late, after = [], [], own_kv
+    contexts, after = [], own_kv
     for c in range(CHUNKS):
-        context = attend(seq_at, queries, ids, after, kv_blocks, c)
+        contexts.append(attend(seq_at, queries, ids, after, kv_blocks, c))
         after = gathered_o
+    early, late = [], []
+    for c, context in enumerate(contexts):
         if nz == 4:
             pairs = [(i, i ^ 1) for i in range(nz)]
             opposite = lax.ppermute(context, "tensor", swap)
             beside = lax.ppermute(context, "tensor", pairs)
+            if c + 1 < CHUNKS:
+                opposite = gate(opposite, contexts[c + 1])
             across = lax.ppermute(opposite, "tensor", pairs)
             early.append([context, beside])
             late.append([opposite, across])
@@ -771,7 +831,7 @@
     split = len(early[0]) - 1
     branches, own_sq = [], sums
     for c in range(CHUNKS):
-        part = first_output(z, order[:split], o_weight, gathered_o, early[c], context)
+        part = first_output(z, order[:split], o_weight, gathered_o, early[c], contexts[-1])
         branch, own_sq = last_output(order[split:], part, gathered_o, late[c], own_sq, c)
         branches.append(branch)
     squares = [own_sq]

time: 160 us -> 170 us (1.062)
  starting transfers between devices: 34.7 us -> 38.2 us
  local copies, waits for them, and re-layouts: 3.14 us -> 5.63 us
  Pallas kernels: 56.5 us -> 58.2 us
    ppermute x1 -> x2, waiting for transfers between devices: 9.42 us -> 24.4 us  [per_device(): got_kv.append(lax.ppermute(sent_kv, 'tensor', swap))]
    ppermute x2, waiting for transfers between devices: 8.49 us -> 0.55 us  [per_device(): opposite = lax.ppermute(context, 'tensor', swap)]
    ppermute x2, waiting for transfers between devices: 6.47 us -> 0.01 us  [per_device(): received.append(lax.ppermute(outs[-1], 'tensor', ring))]
    ppermute x2, waiting for transfers between devices: 8.64 us -> 12.9 us  [per_device(): kv_blocks.insert(0, lax.ppermute(own_kv, 'seq', earlier))]
    pallas_call x1 -> x2, Pallas kernels: 6.36 us -> 10.5 us  [far_kv_product(): pl.pallas_call(partial(far_kv_kernel, order=order, cuts=[len(block) for b...]
    ppermute x2, starting transfers between devices: 0.34 us -> 3.85 us  [per_device(): across = lax.ppermute(opposite, 'tensor', pairs)]
    pallas_call x2 -> x3, Pallas kernels: 6.34 us -> 3.39 us  [the longest x1 2.94 us: far_product(): pl.pallas_call(partial(far_kernel, order=order, groups=len(xs)), out_shap...]
    ppermute x2, starting transfers between devices: 4.84 us -> 2.16 us  [per_device(): beside = lax.ppermute(context, 'tensor', pairs)]
  transfers between devices with their start and end apart: 30 -> 31, of which waited for: 15 -> 16; matrix products, arithmetic and copies ran while one was open for 1% -> 1% of each run, Pallas kernels for 30% -> 29%
where the time goes in v12:
time: 170 us; the launch traced here: 169 us
  waiting for transfers between devices  64 us (38%)
  Pallas kernels  58.2 us (34%)
  starting transfers between devices  38.2 us (22%)
  local copies, waits for them, and re-layouts  5.63 us (3%)
  other arithmetic  2.08 us (1%)
    ppermute x2, waiting for transfers between devices, per_device(): got_kv.append(lax.ppermute(sent_kv, 'tensor', swap))  24.4 us
    ppermute x2, waiting for transfers between devices, per_device(): kv_blocks.insert(0, lax.ppermute(own_kv, 'seq', earlier))  12.9 us
    pallas_call x2, Pallas kernels, attend(): pl.pallas_call(partial(attention_kernel, back=back, offset=c * rows), out...  11.7 us
    pallas_call x2, Pallas kernels, far_kv_product(): pl.pallas_call(partial(far_kv_kernel, order=order, cuts=[len(block) for b...  10.5 us
    ppermute x1, waiting for transfers between devices, per_device(): own_kv = lax.ppermute(packed_kv, 'tensor', swap)[None]  8.01 us
    pallas_call x2, Pallas kernels, near_product(): pl.pallas_call(near_kernel, out_shape=shape((chunk, sum(widths)), F32), g...  7.15 us
    pallas_call x2, Pallas kernels, first_output(): pl.pallas_call(first_output_kernel, out_shape=shape((chunk, cols), F32),...  6.48 us
    ppermute x3, waiting for transfers between devices, per_device(): lax.ppermute(p, 'tensor', turn(k + 1))  6.42 us
  transfers between devices with their start and end apart: 31, of which 16 were waited for; matrix products, arithmetic and copies ran while one was open for 1% of the time, Pallas kernels for 29%

profile of v12, /device:TPU:2, one launch (start us, length us, event | category | flops | bytes accessed | tf_op | source)
XLA Modules:
  0.0 168.5 jit_solution(5860007380942016030)
XLA Ops:
  0.0 2.1 %pack.1 = (bf16[288,256]{1,0:T(8,128)(2,1)}, bf16[288,256]{1,0:T(8,128)(2,1)}, bf16[128,1152]{1,0:T(8,128)(2,1)}) custom-call(s32[1]{0:T(128)} %bitcast.9.at_ref, bf16[4608,256]{1,0:T(8,128)(2,1)} %q_ref.5, bf16[4608,128]{1,0:T(8,128)(2,1)} %k_ref.5, bf16[4608,128]{1,0:T(8,128)(2,1)} %v_ref.5, bf16[768,1152]{1,0:T(8,128)(2,1)} %token_ref.5), custom_call_target="tpu_custom_call" | custom-call | tf_op jit(solution)/shard_map/pack/pallas_call | solution.py:75
  3.7 2.6 %collective-permute-start = (bf16[288,256]{1,0:T(8,128)(2,1)}, bf16[288,256]{1,0:T(8,128)(2,1)S(1)}, u32[]{:S(2)}, u32[]{:S(2)}) collective-permute-start(bf16[288,256]{1,0:T(8,128)(2,1)} %get-tuple-element.28), channel_id=1, source_target_pairs={{0,2},{1,3},{2,0},{3,1},{4,6},{5,7},{6,4},{7,5},{8,10},{9,11},{10,... | collective-permute-start | bytes 442376 | tf_op jit(solution)/shard_map/ppermute | solution.py:728
  6.7 8.0 %collective-permute-done = bf16[288,256]{1,0:T(8,128)(2,1)S(1)} collective-permute-done((bf16[288,256]{1,0:T(8,128)(2,1)}, bf16[288,256]{1,0:T(8,128)(2,1)S(1)}, u32[]{:S(2)}, u32[]{:S(2)}) %collective-permute-start) | collective-permute-done | bytes 147488 | tf_op jit(solution)/shard_map/ppermute | solution.py:728
  14.7 5.0 %collective-permute-done.6 = bf16[288,256]{1,0:T(8,128)(2,1)S(1)} collective-permute-done((bf16[288,256]{1,0:T(8,128)(2,1)}, bf16[288,256]{1,0:T(8,128)(2,1)S(1)}, u32[]{:S(2)}, u32[]{:S(2)}) %collective-permute-start.6) | collective-permute-done | bytes 147488 | tf_op jit(solution)/shard_map/ppermute | solution.py:729
  23.2 3.1 %collective-permute-done.5.refs_1_ = bf16[1,288,256]{2,1,0:T(8,128)(2,1)S(1)} collective-permute-done((bf16[1,288,256]{2,1,0:T(8,128)(2,1)S(1)}, bf16[1,288,256]{2,1,0:T(8,128)(2,1)S(1)}, u32[]{:S(2)}, u32[]{:S(2)}) %collective-permute-start.5) | collective-permute-done | bytes 147488 | tf_op jit(solution)/shard_map/ppermute | solution.py:753
  26.9 2.1 %stage.5 = (bf16[2,288,256]{2,1,0:T(8,128)(2,1)}, bf16[2,288,256]{2,1,0:T(8,128)(2,1)}, bf16[384,1152]{1,0:T(8,128)(2,1)}) custom-call(bf16[1,288,256]{2,1,0:T(8,128)(2,1)S(1)} %bitcast.20, bf16[1,288,256]{2,1,0:T(8,128)(2,1)S(1)} %collective-permute-done.5.refs_1_, bf16[1,288,256]{2,1,0:T(8,128)(2,1)S(1)} %bitcast.24, ...), custom_call_target="tpu_custom_call" | custom-call | tf_op jit(solution)/shard_map/stage/pallas_call | solution.py:130
  37.2 3.6 %collective-permute-done.1.refs_6_ = bf16[32,1152]{1,0:T(8,128)(2,1)S(1)} collective-permute-done((bf16[32,1152]{1,0:T(8,128)(2,1)S(1)}, bf16[32,1152]{1,0:T(8,128)(2,1)S(1)}, u32[]{:S(2)}, u32[]{:S(2)}) %collective-permute-start.1) | collective-permute-done | bytes 73760 | tf_op jit(solution)/shard_map/ppermute | solution.py:734
  41.5 2.2 %collective-permute-start.14 = (bf16[384,1152]{1,0:T(8,128)(2,1)}, bf16[384,1152]{1,0:T(8,128)(2,1)}, u32[]{:S(2)}, u32[]{:S(2)}) collective-permute-start(bf16[384,1152]{1,0:T(8,128)(2,1)} %get-tuple-element.39), channel_id=1, source_target_pairs={{0,1},{1,0},{2,3},{3,2},{4,5},{5,4},{6,7},{7,6},{8,9},{9,8},{10,11... | collective-permute-start | bytes 2654216 | tf_op jit(solution)/shard_map/ppermute | solution.py:751
  43.7 2.3 %collective-permute-done.3.refs_8_ = bf16[32,1152]{1,0:T(8,128)(2,1)S(1)} collective-permute-done((bf16[32,1152]{1,0:T(8,128)(2,1)S(1)}, bf16[32,1152]{1,0:T(8,128)(2,1)S(1)}, u32[]{:S(2)}, u32[]{:S(2)}) %collective-permute-start.3) | collective-permute-done | bytes 73760 | tf_op jit(solution)/shard_map/ppermute | solution.py:734
  47.9 2.0 %stage.7 = (bf16[4,288,256]{2,1,0:T(8,128)(2,1)S(1)}, bf16[4,288,256]{2,1,0:T(8,128)(2,1)}) custom-call(bf16[2,288,256]{2,1,0:T(8,128)(2,1)} %get-tuple-element.33.refs_0_, bf16[2,288,256]{2,1,0:T(8,128)(2,1)S(1)} %collective-permute-done.8.refs_1_, bf16[2,288,256]{2,1,0:T(8,128)(2,1)} %get-tuple-element.34.refs_2_, ...), custom_call_target="tpu_custom_call" | custom-call | flops 49999998976 | bytes 100000000 | tf_op jit(solution)/shard_map/stage/pallas_call | solution.py:130
  54.8 4.7 %far_kv.2 = (bf16[400,256]{1,0:T(8,128)(2,1)S(1)}, bf16[2,384,1152]{2,1,0:T(8,128)(2,1)S(1)}, f32[1,384]{1,0:T(1,128)S(1)}) custom-call(s32[2]{0:T(128)S(1)} %get-tuple-element.55.place_ref, s32[2]{0:T(128)S(1)} %get-tuple-element.54.src_ref, f32[4,1,1152]{2,1,0:T(1,128)S(1)} %reshape.21.gain_ref, bf16[4,288,256]{2,1,0:T(8,128)(2,1)S(1)} %get-tuple-element.37.own_ref, ...), custom_call_target="tpu_custom_call" | custom-call | tf_op jit(solution)/shard_map/far_kv/pallas_call | solution.py:267
  60.7 3.6 %near.2.rest_1_.rest_0_ = f32[384,512]{1,0:T(8,128)S(1)} custom-call(s32[2]{0:T(128)S(1)} %broadcast_add_fusion.src_ref, bf16[2,384,1152]{2,1,0:T(8,128)(2,1)S(1)} %get-tuple-element.38.x_ref.rest_0_, bf16[4608,128]{1,0:T(8,128)(2,1)S(1)} %copy-done.2, bf16[4608,128]{1,0:T(8,128)(2,1)S(1)} %copy-done.3, bf16[4608,256]{1,0:T(8,128)(2,1)} %q_ref.5, ...), custom_call_target="tpu_custom_call" | custom-call | tf_op jit(solution)/shard_map/near/pallas_call | solution.py:365
  64.3 5.7 %far_kv.3 = (bf16[400,256]{1,0:T(8,128)(2,1)S(1)}, bf16[2,384,1152]{2,1,0:T(8,128)(2,1)S(1)}, f32[1,384]{1,0:T(1,128)S(1)}) custom-call(s32[2]{0:T(128)S(1)} %get-tuple-element.55.place_ref, s32[2]{0:T(128)S(1)} %get-tuple-element.54.src_ref, f32[4,1,1152]{2,1,0:T(1,128)S(1)} %reshape.21.gain_ref, bf16[4,288,256]{2,1,0:T(8,128)(2,1)S(1)} %get-tuple-element.37.own_ref, ...), custom_call_target="tpu_custom_call" | custom-call | tf_op jit(solution)/shard_map/far_kv/pallas_call | solution.py:267
  71.3 3.6 %near.3.rest_2_.rest_1_ = f32[384,512]{1,0:T(8,128)S(1)} custom-call(s32[2]{0:T(128)S(1)} %broadcast_add_fusion.src_ref, bf16[2,384,1152]{2,1,0:T(8,128)(2,1)S(1)} %get-tuple-element.41.x_ref.rest_1_, bf16[4608,128]{1,0:T(8,128)(2,1)S(1)} %copy-done.2, bf16[4608,128]{1,0:T(8,128)(2,1)S(1)} %copy-done.3, bf16[4608,256]{1,0:T(8,128)(2,1)} %q_ref.5, ...), custom_call_target="tpu_custom_call" | custom-call | tf_op jit(solution)/shard_map/near/pallas_call | solution.py:365
  74.9 2.9 %far.1.refs_3_.rest_6_ = bf16[768,256]{1,0:T(8,128)(2,1)S(1)} custom-call(s32[2]{0:T(128)S(1)} %get-tuple-element.55.place_ref, s32[2]{0:T(128)S(1)} %get-tuple-element.54.src_ref, bf16[4,288,256]{2,1,0:T(8,128)(2,1)} %get-tuple-element.36.own_ref, bf16[4,288,256]{2,1,0:T(8,128)(2,1)S(1)} %collective-permute-done.12.rest_2_.got_ref, ...), custom_call_target="tpu_custom_call" | custom-call | tf_op jit(solution)/shard_map/far/pallas_call | solution.py:327
  81.2 2.4 %collective-permute-start.17 = (bf16[400,256]{1,0:T(8,128)(2,1)S(1)}, bf16[400,256]{1,0:T(8,128)(2,1)S(1)}, u32[]{:S(2)}, u32[]{:S(2)}) collective-permute-start(bf16[400,256]{1,0:T(8,128)(2,1)S(1)} %get-tuple-element.42.rest_0_), channel_id=1, source_target_pairs={{0,2},{1,3},{2,0},{3,1},{4,6},{5,7},{6,4},{7,5},{8,10},{9,11},{10,... | collective-permute-start | bytes 614408 | tf_op jit(solution)/shard_map/ppermute | solution.py:783
  83.9 23.1 %collective-permute-done.17.rest_3_ = bf16[400,256]{1,0:T(8,128)(2,1)S(1)} collective-permute-done((bf16[400,256]{1,0:T(8,128)(2,1)S(1)}, bf16[400,256]{1,0:T(8,128)(2,1)S(1)}, u32[]{:S(2)}, u32[]{:S(2)}) %collective-permute-start.17) | collective-permute-done | bytes 204832 | tf_op jit(solution)/shard_map/ppermute | solution.py:783
  108.8 2.1 %collective-permute-start.21 = (bf16[784,256]{1,0:T(8,128)(2,1)S(1)}, bf16[784,256]{1,0:T(8,128)(2,1)S(1)}, u32[]{:S(2)}, u32[]{:S(2)}) collective-permute-start(bf16[784,256]{1,0:T(8,128)(2,1)S(1)} %get-tuple-element.45.refs_3_.after_ref.rest_2_), channel_id=1, source_target_pairs={{0,4},{4,8},{8,12},{1,5},{5,9},{9,13},{2,6},{6,10},{10,14},{3,7},{... | collective-permute-start | bytes 1204232 | tf_op jit(solution)/shard_map/ppermute | solution.py:807
  112.0 9.5 %collective-permute-done.20.rest_0_ = bf16[784,256]{1,0:T(8,128)(2,1)S(1)} collective-permute-done((bf16[784,256]{1,0:T(8,128)(2,1)S(1)}, bf16[784,256]{1,0:T(8,128)(2,1)S(1)}, u32[]{:S(2)}, u32[]{:S(2)}) %collective-permute-start.20) | collective-permute-done | bytes 401440 | tf_op jit(solution)/shard_map/ppermute | solution.py:807
  121.6 3.4 %collective-permute-done.21.rest_1_ = bf16[784,256]{1,0:T(8,128)(2,1)S(1)} collective-permute-done((bf16[784,256]{1,0:T(8,128)(2,1)S(1)}, bf16[784,256]{1,0:T(8,128)(2,1)S(1)}, u32[]{:S(2)}, u32[]{:S(2)}) %collective-permute-start.21) | collective-permute-done | bytes 401440 | tf_op jit(solution)/shard_map/ppermute | solution.py:807
  124.9 6.1 %attend.2.rest_0_ = bf16[384,256]{1,0:T(8,128)(2,1)S(1)} custom-call(s32[1]{0:T(128)} %bitcast.16.seq_ref, bf16[768,256]{1,0:T(8,128)(2,1)S(1)} %queries.1.q_ref, s32[1,768]{1,0:T(1,128)S(1)} %broadcast_in_dim.21.id_ref, bf16[784,256]{1,0:T(8,128)(2,1)S(1)} %get-tuple-element.45.refs_3_.after_ref.rest_2_, ...), custom_call_target="tpu_custom_call" | custom-call | flops 905969664 | bytes 2359296 | tf_op jit(solution)/shard_map/attend/pallas_call | solution.py:543
  131.1 1.9 %collective-permute-start.22 = (bf16[384,256]{1,0:T(8,128)(2,1)S(1)}, bf16[384,256]{1,0:T(8,128)(2,1)S(1)}, u32[]{:S(2)}, u32[]{:S(2)}) collective-permute-start(bf16[384,256]{1,0:T(8,128)(2,1)S(1)} %attend.2.rest_0_), channel_id=1, source_target_pairs={{0,1},{1,0},{2,3},{3,2},{4,5},{5,4},{6,7},{7,6},{8,9},{9,8},{10,11... | collective-permute-start | bytes 589832 | tf_op jit(solution)/shard_map/ppermute | solution.py:820
  134.6 5.6 %attend.3.rest_2_.after_ref.rest_0_ = bf16[384,256]{1,0:T(8,128)(2,1)S(1)} custom-call(s32[1]{0:T(128)} %bitcast.16.seq_ref, bf16[768,256]{1,0:T(8,128)(2,1)S(1)} %queries.1.q_ref, s32[1,768]{1,0:T(1,128)S(1)} %broadcast_in_dim.21.id_ref, bf16[3,256,1152]{2,1,0:T(8,128)(2,1)S(1)} %lay.1.after_ref.o_ref, ...), custom_call_target="tpu_custom_call" | custom-call | flops 905969664 | bytes 2359296 | tf_op jit(solution)/shard_map/attend/pallas_call | solution.py:543
  140.4 2.8 %collective-permute-start.26 = (bf16[384,256]{1,0:T(8,128)(2,1)S(1)}, bf16[384,256]{1,0:T(8,128)(2,1)S(1)}, u32[]{:S(2)}, u32[]{:S(2)}) collective-permute-start(bf16[384,256]{1,0:T(8,128)(2,1)S(1)} %attend.3.rest_2_.after_ref.rest_0_), channel_id=1, source_target_pairs={{0,2},{1,3},{2,0},{3,1},{4,6},{5,7},{6,4},{7,5},{8,10},{9,11},{10,... | collective-permute-start | bytes 589832 | tf_op jit(solution)/shard_map/ppermute | solution.py:819
  143.3 3.2 %first_output.2.part_ref = f32[384,1152]{1,0:T(8,128)S(1)} custom-call(s32[2]{0:T(128)S(1)} %pad_add_fusion.1.at_ref, bf16[256,4608]{1,0:T(8,128)(2,1)} %own_o_ref.3, bf16[3,256,1152]{2,1,0:T(8,128)(2,1)S(1)} %lay.1.after_ref.o_ref, bf16[384,256]{1,0:T(8,128)(2,1)S(1)} %attend.2.rest_0_, bf16[384,256]{1,0:T(8,128)(2,1)S(1)} %collective-permute-done.22.rest_1_, ...), custom_call_target="tpu_custom_call" | custom-call | flops 49999998976 | bytes 100000000 | tf_op jit(solution)/shard_map/first_output/pallas_call | solution.py:618
  147.1 3.8 %collective-permute-start.27 = (bf16[384,256]{1,0:T(8,128)(2,1)S(1)}, bf16[384,256]{1,0:T(8,128)(2,1)S(1)}, u32[]{:S(2)}, u32[]{:S(2)}) collective-permute-start(bf16[384,256]{1,0:T(8,128)(2,1)S(1)} %collective-permute-done.26.rest_0_), channel_id=1, source_target_pairs={{0,1},{1,0},{2,3},{3,2},{4,5},{5,4},{6,7},{7,6},{8,9},{9,8},{10,11... | collective-permute-start | bytes 589832 | tf_op jit(solution)/shard_map/ppermute | solution.py:823
  150.9 3.2 %first_output.3.part_ref = f32[384,1152]{1,0:T(8,128)S(1)} custom-call(s32[2]{0:T(128)S(1)} %pad_add_fusion.1.at_ref, bf16[256,4608]{1,0:T(8,128)(2,1)} %own_o_ref.3, bf16[3,256,1152]{2,1,0:T(8,128)(2,1)S(1)} %lay.1.after_ref.o_ref, bf16[384,256]{1,0:T(8,128)(2,1)S(1)} %attend.3.rest_2_.after_ref.rest_0_, ...), custom_call_target="tpu_custom_call" | custom-call | flops 49999998976 | bytes 100000000 | tf_op jit(solution)/shard_map/first_output/pallas_call | solution.py:618
  154.1 2.5 %last_output.2 = (f32[384,1152]{1,0:T(8,128)S(1)}, f32[1,384]{1,0:T(1,128)S(1)}) custom-call(s32[2]{0:T(128)S(1)} %pad_add_fusion.at_ref, f32[384,1152]{1,0:T(8,128)S(1)} %first_output.2.part_ref, bf16[3,256,1152]{2,1,0:T(8,128)(2,1)S(1)} %lay.1.after_ref.o_ref, bf16[384,256]{1,0:T(8,128)(2,1)S(1)} %gate.1.rest_0_, ...), custom_call_target="tpu_custom_call" | custom-call | tf_op jit(solution)/shard_map/last_output/pallas_call | solution.py:642
  156.7 2.5 %last_output.3 = (f32[384,1152]{1,0:T(8,128)S(1)}, f32[1,768]{1,0:T(1,128)S(1)}) custom-call(s32[2]{0:T(128)S(1)} %pad_add_fusion.at_ref, f32[384,1152]{1,0:T(8,128)S(1)} %first_output.3.part_ref, bf16[3,256,1152]{2,1,0:T(8,128)(2,1)S(1)} %lay.1.after_ref.o_ref, bf16[384,256]{1,0:T(8,128)(2,1)S(1)} %collective-permute-done.26.rest_0_, ...), custom_call_target="tpu_custom_call" | custom-call | tf_op jit(solution)/shard_map/last_output/pallas_call | solution.py:642
  159.3 1.7 %collective-permute-start.29 = (f32[1,768]{1,0:T(1,128)S(1)}, f32[1,768]{1,0:T(1,128)S(1)}, u32[]{:S(2)}, u32[]{:S(2)}) collective-permute-start(f32[1,768]{1,0:T(1,128)S(1)} %get-tuple-element.50.rest_2_), channel_id=1, source_target_pairs={{0,2},{1,3},{2,0},{3,1},{4,6},{5,7},{6,4},{7,5},{8,10},{9,11},{10,... | collective-permute-start | bytes 9224 | tf_op jit(solution)/shard_map/ppermute | solution.py:838
  161.0 2.4 %collective-permute-start.30 = (f32[1,768]{1,0:T(1,128)S(1)}, f32[1,768]{1,0:T(1,128)S(1)}, u32[]{:S(2)}, u32[]{:S(2)}) collective-permute-start(f32[1,768]{1,0:T(1,128)S(1)} %get-tuple-element.50.rest_2_), channel_id=1, source_target_pairs={{0,3},{1,0},{2,1},{3,2},{4,7},{5,4},{6,5},{7,6},{8,11},{9,8},{10,9... | collective-permute-start | bytes 9224 | tf_op jit(solution)/shard_map/ppermute | solution.py:838
  165.3 3.3 %finish.1 = bf16[768,1152]{1,0:T(8,128)(2,1)} custom-call(bf16[768,1152]{1,0:T(8,128)(2,1)S(1)} %copy-done.1, f32[1,1152]{1,0:T(1,128)S(1)} %broadcast_in_dim.17.gain_ref, f32[384,1152]{1,0:T(8,128)S(1)} %get-tuple-element.47.rest_0_, f32[384,1152]{1,0:T(8,128)S(1)} %get-tuple-element.49.rest_1_, f32[1,768]{1,0:T(1,128)S(1)} %get-tuple-element.50.rest_2_, ...), custom_call_target="tpu_custom_call" | custom-call | tf_op jit(solution)/shard_map/finish/pallas_call | solution.py:683
  (92 shorter events, 34.9 us)
Async XLA Ops:
  0.0 19.7 %copy-start = (bf16[768,1152]{1,0:T(8,128)(2,1)S(1)}, bf16[768,1152]{1,0:T(8,128)(2,1)}, u32[]{:S(2)}) copy-start(bf16[768,1152]{1,0:T(8,128)(2,1)} %token_ref.5) | copy-start | bytes 5308420
  2.1 17.6 %collective-permute-start.10 = (bf16[128,1152]{1,0:T(8,128)(2,1)}, bf16[128,1152]{1,0:T(8,128)(2,1)S(1)}, u32[]{:S(2)}, u32[]{:S(2)}) collective-permute-start(bf16[128,1152]{1,0:T(8,128)(2,1)} %get-tuple-element.35), channel_id=1, source_target_pairs={{0,1},{1,0},{2,3},{3,2},{4,5},{5,4},{6,7},{7,6},{8,9},{9,8},{10,11... | collective-permute-start | bytes 884744 | tf_op jit(solution)/shard_map/ppermute | solution.py:730
  3.7 10.9 %collective-permute-start = (bf16[288,256]{1,0:T(8,128)(2,1)}, bf16[288,256]{1,0:T(8,128)(2,1)S(1)}, u32[]{:S(2)}, u32[]{:S(2)}) collective-permute-start(bf16[288,256]{1,0:T(8,128)(2,1)} %get-tuple-element.28), channel_id=1, source_target_pairs={{0,2},{1,3},{2,0},{3,1},{4,6},{5,7},{6,4},{7,5},{8,10},{9,11},{10,... | collective-permute-start | bytes 442376 | tf_op jit(solution)/shard_map/ppermute | solution.py:728
  6.3 13.4 %collective-permute-start.6 = (bf16[288,256]{1,0:T(8,128)(2,1)}, bf16[288,256]{1,0:T(8,128)(2,1)S(1)}, u32[]{:S(2)}, u32[]{:S(2)}) collective-permute-start(bf16[288,256]{1,0:T(8,128)(2,1)} %get-tuple-element.32), channel_id=1, source_target_pairs={{0,2},{1,3},{2,0},{3,1},{4,6},{5,7},{6,4},{7,5},{8,10},{9,11},{10,... | collective-permute-start | bytes 442376 | tf_op jit(solution)/shard_map/ppermute | solution.py:729
  20.7 25.3 %collective-permute-start.11 = (bf16[256,1152]{1,0:T(8,128)(2,1)}, bf16[256,1152]{1,0:T(8,128)(2,1)S(1)}, u32[]{:S(2)}, u32[]{:S(2)}) collective-permute-start(bf16[256,1152]{1,0:T(8,128)(2,1)} %stage.6), channel_id=1, source_target_pairs={{0,1},{1,0},{2,3},{3,2},{4,5},{5,4},{6,7},{7,6},{8,9},{9,8},{10,11... | collective-permute-start | bytes 1769480 | tf_op jit(solution)/shard_map/ppermute | solution.py:751
  21.2 5.1 %collective-permute-start.5 = (bf16[1,288,256]{2,1,0:T(8,128)(2,1)S(1)}, bf16[1,288,256]{2,1,0:T(8,128)(2,1)S(1)}, u32[]{:S(2)}, u32[]{:S(2)}) collective-permute-start(bf16[1,288,256]{2,1,0:T(8,128)(2,1)S(1)} %bitcast.19), channel_id=1, source_target_pairs={{0,8},{4,12},{8,0},{12,4},{16,24},{20,28},{24,16},{28,20},{1,9},{5... | collective-permute-start | bytes 442376 | tf_op jit(solution)/shard_map/ppermute | solution.py:753
  21.7 5.1 %collective-permute-start.7 = (bf16[1,288,256]{2,1,0:T(8,128)(2,1)S(1)}, bf16[1,288,256]{2,1,0:T(8,128)(2,1)S(1)}, u32[]{:S(2)}, u32[]{:S(2)}) collective-permute-start(bf16[1,288,256]{2,1,0:T(8,128)(2,1)S(1)} %bitcast.23), channel_id=1, source_target_pairs={{0,16},{4,20},{8,24},{12,28},{16,0},{20,4},{24,8},{28,12},{1,17},{... | collective-permute-start | bytes 442376 | tf_op jit(solution)/shard_map/ppermute | solution.py:754
  28.9 17.1 %collective-permute-start.8 = (bf16[2,288,256]{2,1,0:T(8,128)(2,1)}, bf16[2,288,256]{2,1,0:T(8,128)(2,1)S(1)}, u32[]{:S(2)}, u32[]{:S(2)}) collective-permute-start(bf16[2,288,256]{2,1,0:T(8,128)(2,1)} %get-tuple-element.33.refs_0_), channel_id=1, source_target_pairs={{0,16},{4,20},{8,24},{12,28},{16,0},{20,4},{24,8},{28,12},{1,17},{... | collective-permute-start | bytes 884744 | tf_op jit(solution)/shard_map/ppermute | solution.py:753
  30.5 15.5 %collective-permute-start.9 = (bf16[2,288,256]{2,1,0:T(8,128)(2,1)}, bf16[2,288,256]{2,1,0:T(8,128)(2,1)S(1)}, u32[]{:S(2)}, u32[]{:S(2)}) collective-permute-start(bf16[2,288,256]{2,1,0:T(8,128)(2,1)} %get-tuple-element.34.refs_2_), channel_id=1, source_target_pairs={{0,8},{4,12},{8,0},{12,4},{16,24},{20,28},{24,16},{28,20},{1,9},{5... | collective-permute-start | bytes 884744 | tf_op jit(solution)/shard_map/ppermute | solution.py:754
  34.4 6.4 %collective-permute-start.1 = (bf16[32,1152]{1,0:T(8,128)(2,1)S(1)}, bf16[32,1152]{1,0:T(8,128)(2,1)S(1)}, u32[]{:S(2)}, u32[]{:S(2)}) collective-permute-start(bf16[32,1152]{1,0:T(8,128)(2,1)S(1)} %get-tuple-element.29), channel_id=1, source_target_pairs={{0,1},{1,2},{2,3},{3,0},{4,5},{5,6},{6,7},{7,4},{8,9},{9,10},{10,1... | collective-permute-start | bytes 221192 | tf_op jit(solution)/shard_map/ppermute | solution.py:734
  36.0 5.5 %collective-permute-start.2 = (bf16[32,1152]{1,0:T(8,128)(2,1)S(1)}, bf16[32,1152]{1,0:T(8,128)(2,1)S(1)}, u32[]{:S(2)}, u32[]{:S(2)}) collective-permute-start(bf16[32,1152]{1,0:T(8,128)(2,1)S(1)} %get-tuple-element.30), channel_id=1, source_target_pairs={{0,2},{1,3},{2,0},{3,1},{4,6},{5,7},{6,4},{7,5},{8,10},{9,11},{10,... | collective-permute-start | bytes 221192 | tf_op jit(solution)/shard_map/ppermute | solution.py:734
  40.8 5.2 %collective-permute-start.3 = (bf16[32,1152]{1,0:T(8,128)(2,1)S(1)}, bf16[32,1152]{1,0:T(8,128)(2,1)S(1)}, u32[]{:S(2)}, u32[]{:S(2)}) collective-permute-start(bf16[32,1152]{1,0:T(8,128)(2,1)S(1)} %get-tuple-element.31), channel_id=1, source_target_pairs={{0,3},{1,0},{2,1},{3,2},{4,7},{5,4},{6,5},{7,6},{8,11},{9,8},{10,9... | collective-permute-start | bytes 221192 | tf_op jit(solution)/shard_map/ppermute | solution.py:734
  41.5 22.8 %collective-permute-start.14 = (bf16[384,1152]{1,0:T(8,128)(2,1)}, bf16[384,1152]{1,0:T(8,128)(2,1)}, u32[]{:S(2)}, u32[]{:S(2)}) collective-permute-start(bf16[384,1152]{1,0:T(8,128)(2,1)} %get-tuple-element.39), channel_id=1, source_target_pairs={{0,1},{1,0},{2,3},{3,2},{4,5},{5,4},{6,7},{7,6},{8,9},{9,8},{10,11... | collective-permute-start | bytes 2654216 | tf_op jit(solution)/shard_map/ppermute | solution.py:751
  49.9 2.3 %collective-permute-start.12 = (bf16[4,288,256]{2,1,0:T(8,128)(2,1)}, bf16[4,288,256]{2,1,0:T(8,128)(2,1)S(1)}, u32[]{:S(2)}, u32[]{:S(2)}) collective-permute-start(bf16[4,288,256]{2,1,0:T(8,128)(2,1)} %get-tuple-element.36.own_ref), channel_id=1, source_target_pairs={{0,4},{4,0},{8,12},{12,8},{16,20},{20,16},{24,28},{28,24},{1,5},{5... | collective-permute-start | bytes 1769480 | tf_op jit(solution)/shard_map/ppermute | solution.py:754
  50.0 2.8 %collective-permute-start.13 = (bf16[4,288,256]{2,1,0:T(8,128)(2,1)S(1)}, bf16[4,288,256]{2,1,0:T(8,128)(2,1)S(1)}, u32[]{:S(2)}, u32[]{:S(2)}) collective-permute-start(bf16[4,288,256]{2,1,0:T(8,128)(2,1)S(1)} %get-tuple-element.37.own_ref), channel_id=1, source_target_pairs={{0,4},{4,0},{8,12},{12,8},{16,20},{20,16},{24,28},{28,24},{1,5},{5... | collective-permute-start | bytes 1769480 | tf_op jit(solution)/shard_map/ppermute | solution.py:753
  50.6 27.9 %collective-permute-start.4 = (bf16[1,3,32,1152]{3,2,1,0:T(8,128)(2,1)S(1)}, bf16[1,3,32,1152]{3,2,1,0:T(8,128)(2,1)S(1)}, u32[]{:S(2)}, u32[]{:S(2)}) collective-permute-start(bf16[1,3,32,1152]{3,2,1,0:T(8,128)(2,1)S(1)} %maximum_bitcast_fusion.refs_0_), channel_id=1, source_target_pairs={{0,8},{4,12},{8,0},{12,4},{16,24},{20,28},{24,16},{28,20},{1,9},{5... | collective-permute-start | bytes 663560 | tf_op jit(solution)/shard_map/ppermute | solution.py:764
  59.6 11.8 %collective-permute-start.15 = (bf16[400,256]{1,0:T(8,128)(2,1)S(1)}, bf16[400,256]{1,0:T(8,128)(2,1)S(1)}, u32[]{:S(2)}, u32[]{:S(2)}) collective-permute-start(bf16[400,256]{1,0:T(8,128)(2,1)S(1)} %get-tuple-element.40.rest_0_), channel_id=1, source_target_pairs={{0,2},{1,3},{2,0},{3,1},{4,6},{5,7},{6,4},{7,5},{8,10},{9,11},{10,... | collective-permute-start | bytes 614408 | tf_op jit(solution)/shard_map/ppermute | solution.py:783
  77.9 33.7 %collective-permute-start.19 = (bf16[768,256]{1,0:T(8,128)(2,1)S(1)}, bf16[768,256]{1,0:T(8,128)(2,1)S(1)}, u32[]{:S(2)}, u32[]{:S(2)}) collective-permute-start(bf16[768,256]{1,0:T(8,128)(2,1)S(1)} %far.1.refs_3_.rest_6_), channel_id=1, source_target_pairs={{0,2},{1,3},{2,0},{3,1},{4,6},{5,7},{6,4},{7,5},{8,10},{9,11},{10,... | collective-permute-start | bytes 1179656 | tf_op jit(solution)/shard_map/ppermute | solution.py:793
  79.2 31.8 %collective-permute-start.16 = (bf16[2,3,32,1152]{3,2,1,0:T(8,128)(2,1)S(1)}, bf16[2,3,32,1152]{3,2,1,0:T(8,128)(2,1)S(1)}, u32[]{:S(2)}, u32[]{:S(2)}) collective-permute-start(bf16[2,3,32,1152]{3,2,1,0:T(8,128)(2,1)S(1)} %stage.8.rest_7_.refs_0_), channel_id=1, source_target_pairs={{0,16},{4,20},{8,24},{12,28},{16,0},{20,4},{24,8},{28,12},{1,17},{... | collective-permute-start | bytes 1327112 | tf_op jit(solution)/shard_map/ppermute | solution.py:764
  81.2 25.9 %collective-permute-start.17 = (bf16[400,256]{1,0:T(8,128)(2,1)S(1)}, bf16[400,256]{1,0:T(8,128)(2,1)S(1)}, u32[]{:S(2)}, u32[]{:S(2)}) collective-permute-start(bf16[400,256]{1,0:T(8,128)(2,1)S(1)} %get-tuple-element.42.rest_0_), channel_id=1, source_target_pairs={{0,2},{1,3},{2,0},{3,1},{4,6},{5,7},{6,4},{7,5},{8,10},{9,11},{10,... | collective-permute-start | bytes 614408 | tf_op jit(solution)/shard_map/ppermute | solution.py:783
  107.5 14.0 %collective-permute-start.20 = (bf16[784,256]{1,0:T(8,128)(2,1)S(1)}, bf16[784,256]{1,0:T(8,128)(2,1)S(1)}, u32[]{:S(2)}, u32[]{:S(2)}) collective-permute-start(bf16[784,256]{1,0:T(8,128)(2,1)S(1)} %get-tuple-element.45.refs_3_.after_ref.rest_2_), channel_id=1, source_target_pairs={{0,8},{4,12},{1,9},{5,13},{2,10},{6,14},{3,11},{7,15},{16,24},{20,... | collective-permute-start | bytes 1204232 | tf_op jit(solution)/shard_map/ppermute | solution.py:807
  108.8 16.1 %collective-permute-start.21 = (bf16[784,256]{1,0:T(8,128)(2,1)S(1)}, bf16[784,256]{1,0:T(8,128)(2,1)S(1)}, u32[]{:S(2)}, u32[]{:S(2)}) collective-permute-start(bf16[784,256]{1,0:T(8,128)(2,1)S(1)} %get-tuple-element.45.refs_3_.after_ref.rest_2_), channel_id=1, source_target_pairs={{0,4},{4,8},{8,12},{1,5},{5,9},{9,13},{2,6},{6,10},{10,14},{3,7},{... | collective-permute-start | bytes 1204232 | tf_op jit(solution)/shard_map/ppermute | solution.py:807
  111.5 21.7 %collective-permute-start.18 = (bf16[4,3,32,1152]{3,2,1,0:T(8,128)(2,1)S(1)}, bf16[4,3,32,1152]{3,2,1,0:T(8,128)(2,1)S(1)}, u32[]{:S(2)}, u32[]{:S(2)}) collective-permute-start(bf16[4,3,32,1152]{3,2,1,0:T(8,128)(2,1)S(1)} %stage.9.own_ref), channel_id=1, source_target_pairs={{0,4},{4,0},{8,12},{12,8},{16,20},{20,16},{24,28},{28,24},{1,5},{5... | collective-permute-start | bytes 2654216 | tf_op jit(solution)/shard_map/ppermute | solution.py:764
  131.1 12.2 %collective-permute-start.23 = (bf16[384,256]{1,0:T(8,128)(2,1)S(1)}, bf16[384,256]{1,0:T(8,128)(2,1)S(1)}, u32[]{:S(2)}, u32[]{:S(2)}) collective-permute-start(bf16[384,256]{1,0:T(8,128)(2,1)S(1)} %attend.2.rest_0_), channel_id=1, source_target_pairs={{0,2},{1,3},{2,0},{3,1},{4,6},{5,7},{6,4},{7,5},{8,10},{9,11},{10,... | collective-permute-start | bytes 589832 | tf_op jit(solution)/shard_map/ppermute | solution.py:819
  131.1 12.2 %collective-permute-start.22 = (bf16[384,256]{1,0:T(8,128)(2,1)S(1)}, bf16[384,256]{1,0:T(8,128)(2,1)S(1)}, u32[]{:S(2)}, u32[]{:S(2)}) collective-permute-start(bf16[384,256]{1,0:T(8,128)(2,1)S(1)} %attend.2.rest_0_), channel_id=1, source_target_pairs={{0,1},{1,0},{2,3},{3,2},{4,5},{5,4},{6,7},{7,6},{8,9},{9,8},{10,11... | collective-permute-start | bytes 589832 | tf_op jit(solution)/shard_map/ppermute | solution.py:820
  140.2 10.7 %collective-permute-start.25 = (bf16[384,256]{1,0:T(8,128)(2,1)S(1)}, bf16[384,256]{1,0:T(8,128)(2,1)S(1)}, u32[]{:S(2)}, u32[]{:S(2)}) collective-permute-start(bf16[384,256]{1,0:T(8,128)(2,1)S(1)} %attend.3.rest_2_.after_ref.rest_0_), channel_id=1, source_target_pairs={{0,1},{1,0},{2,3},{3,2},{4,5},{5,4},{6,7},{7,6},{8,9},{9,8},{10,11... | collective-permute-start | bytes 589832 | tf_op jit(solution)/shard_map/ppermute | solution.py:820
  140.4 6.7 %collective-permute-start.26 = (bf16[384,256]{1,0:T(8,128)(2,1)S(1)}, bf16[384,256]{1,0:T(8,128)(2,1)S(1)}, u32[]{:S(2)}, u32[]{:S(2)}) collective-permute-start(bf16[384,256]{1,0:T(8,128)(2,1)S(1)} %attend.3.rest_2_.after_ref.rest_0_), channel_id=1, source_target_pairs={{0,2},{1,3},{2,0},{3,1},{4,6},{5,7},{6,4},{7,5},{8,10},{9,11},{10,... | collective-permute-start | bytes 589832 | tf_op jit(solution)/shard_map/ppermute | solution.py:819
  143.2 10.9 %collective-permute-start.24 = (bf16[384,256]{1,0:T(8,128)(2,1)S(1)}, bf16[384,256]{1,0:T(8,128)(2,1)S(1)}, u32[]{:S(2)}, u32[]{:S(2)}) collective-permute-start(bf16[384,256]{1,0:T(8,128)(2,1)S(1)} %gate.1.rest_0_), channel_id=1, source_target_pairs={{0,1},{1,0},{2,3},{3,2},{4,5},{5,4},{6,7},{7,6},{8,9},{9,8},{10,11... | collective-permute-start | bytes 589832 | tf_op jit(solution)/shard_map/ppermute | solution.py:823
  147.1 9.6 %collective-permute-start.27 = (bf16[384,256]{1,0:T(8,128)(2,1)S(1)}, bf16[384,256]{1,0:T(8,128)(2,1)S(1)}, u32[]{:S(2)}, u32[]{:S(2)}) collective-permute-start(bf16[384,256]{1,0:T(8,128)(2,1)S(1)} %collective-permute-done.26.rest_0_), channel_id=1, source_target_pairs={{0,1},{1,0},{2,3},{3,2},{4,5},{5,4},{6,7},{7,6},{8,9},{9,8},{10,11... | collective-permute-start | bytes 589832 | tf_op jit(solution)/shard_map/ppermute | solution.py:823
  159.2 5.4 %collective-permute-start.28 = (f32[1,768]{1,0:T(1,128)S(1)}, f32[1,768]{1,0:T(1,128)S(1)}, u32[]{:S(2)}, u32[]{:S(2)}) collective-permute-start(f32[1,768]{1,0:T(1,128)S(1)} %get-tuple-element.50.rest_2_), channel_id=1, source_target_pairs={{0,1},{1,2},{2,3},{3,0},{4,5},{5,6},{6,7},{7,4},{8,9},{9,10},{10,1... | collective-permute-start | bytes 9224 | tf_op jit(solution)/shard_map/ppermute | solution.py:838
  159.3 5.4 %collective-permute-start.29 = (f32[1,768]{1,0:T(1,128)S(1)}, f32[1,768]{1,0:T(1,128)S(1)}, u32[]{:S(2)}, u32[]{:S(2)}) collective-permute-start(f32[1,768]{1,0:T(1,128)S(1)} %get-tuple-element.50.rest_2_), channel_id=1, source_target_pairs={{0,2},{1,3},{2,0},{3,1},{4,6},{5,7},{6,4},{7,5},{8,10},{9,11},{10,... | collective-permute-start | bytes 9224 | tf_op jit(solution)/shard_map/ppermute | solution.py:838
  161.0 4.2 %collective-permute-start.30 = (f32[1,768]{1,0:T(1,128)S(1)}, f32[1,768]{1,0:T(1,128)S(1)}, u32[]{:S(2)}, u32[]{:S(2)}) collective-permute-start(f32[1,768]{1,0:T(1,128)S(1)} %get-tuple-element.50.rest_2_), channel_id=1, source_target_pairs={{0,3},{1,0},{2,1},{3,2},{4,7},{5,4},{6,5},{7,6},{8,11},{9,8},{10,9... | collective-permute-start | bytes 9224 | tf_op jit(solution)/shard_map/ppermute | solution.py:838
  (12 other events, 42.2 us)

commit v13 on v11

--- a/solution.py
+++ b/solution.py
@@ -85,6 +85,22 @@
         compiler_params=ALL_VMEM,
         name="pack",
     )(at, q_weight, k_weight, v_weight, tokens)
+
+
+def gate_kernel(x_ref, after_ref, out_ref):
+    pass
+
+
+def gate(x, after):
+    return pl.pallas_call(
+        gate_kernel,
+        out_shape=shape(x.shape, x.dtype),
+        in_specs=[ANY, ANY],
+        out_specs=ANY,
+        input_output_aliases={0: 0},
+        compiler_params=PARAMS,
+        name="gate",
+    )(x, after)
 
 
 def stage_kernel(*refs, pairs, first, count):
@@ -734,7 +750,7 @@
     near = near_product(side * half + sources, x, weights, [sent_kv])
 
     sent_q = far_product(place, sources, x, far_q, [near])
-    got_q = lax.ppermute(sent_q, "tensor", swap)
+    got_q = lax.ppermute(gate(sent_q, got_kv), "tensor", swap)
     pair_o = double(pair_o, last - 1, [sent_q])
     cosine, sine = rotation_table(seq * rows + jnp.arange(rows, dtype=jnp.int32))
     ids = seg_ids[None, :]
@@ -752,14 +768,18 @@
 
     queries = finished_queries(near, got_q, sums, cosine, sine, model)
     seq_at = jnp.reshape(seq, (1,))
-    early, late, after = [], [], own_kv
+    contexts, after = [], own_kv
     for c in range(CHUNKS):
-        context = attend(seq_at, queries, ids, after, kv_blocks, c)
+        contexts.append(attend(seq_at, queries, ids, after, kv_blocks, c))
         after = gathered_o
+    early, late = [], []
+    for c, context in enumerate(contexts):
         if nz == 4:
             pairs = [(i, i ^ 1) for i in range(nz)]
             opposite = lax.ppermute(context, "tensor", swap)
             beside = lax.ppermute(context, "tensor", pairs)
+            if c + 1 < CHUNKS:
+                opposite = gate(opposite, contexts[c + 1])
             across = lax.ppermute(opposite, "tensor", pairs)
             early.append([context, beside])
             late.append([opposite, across])
@@ -771,7 +791,7 @@
     split = len(early[0]) - 1
     branches, own_sq = [], sums
     for c in range(CHUNKS):
-        part = first_output(z, order[:split], o_weight, gathered_o, early[c], context)
+        part = first_output(z, order[:split], o_weight, gathered_o, early[c], contexts[-1])
         branch, own_sq = last_output(order[split:], part, gathered_o, late[c], own_sq, c)
         branches.append(branch)
     squares = [own_sq]

time: 160 us -> 147 us (0.919)
  waiting for transfers between devices: 63.1 us -> 49.2 us
    ppermute x1, waiting for transfers between devices: 0.01 us -> 10.6 us  [per_device(): got_q = lax.ppermute(gate(sent_q, got_kv), 'tensor', swap)]
    ppermute x1, waiting for transfers between devices: 9.42 us -> 0.01 us  [per_device(): got_kv = lax.ppermute(sent_kv, 'tensor', swap)]
    ppermute x2, waiting for transfers between devices: 8.64 us -> 0.01 us  [per_device(): kv_blocks.insert(0, lax.ppermute(own_kv, 'seq', earlier))]
    ppermute x2, waiting for transfers between devices: 8.49 us -> 3.48 us  [per_device(): opposite = lax.ppermute(context, 'tensor', swap)]
    ppermute x2, starting transfers between devices: 0.34 us -> 3.12 us  [per_device(): across = lax.ppermute(opposite, 'tensor', pairs)]
    ppermute x2, starting transfers between devices: 4.84 us -> 2.24 us  [per_device(): beside = lax.ppermute(context, 'tensor', pairs)]
    ppermute x2, waiting for transfers between devices: 2.09 us -> 0.01 us  [per_device(): across = lax.ppermute(opposite, 'tensor', pairs)]
    unnamed x20 -> x30, local copies, waits for them, and re-layouts: 3.11 us -> 3.87 us
  transfers between devices with their start and end apart: 30 -> 30, of which waited for: 15 -> 12; matrix products, arithmetic and copies ran while one was open for 1% -> 1% of each run, Pallas kernels for 30% -> 28%
where the time goes in v13:
time: 147 us
  Pallas kernels  55.3 us (38%)
  waiting for transfers between devices  49.2 us (33%)
  starting transfers between devices  36 us (24%)
  local copies, waits for them, and re-layouts  3.9 us (3%)
  other arithmetic  2.08 us (1%)
    pallas_call x2, Pallas kernels, attend(): pl.pallas_call(partial(attention_kernel, back=back, offset=c * rows), out...  11.5 us
    ppermute x1, waiting for transfers between devices, per_device(): got_q = lax.ppermute(gate(sent_q, got_kv), 'tensor', swap)  10.6 us
    ppermute x3, waiting for transfers between devices, per_device(): lax.ppermute(p, 'tensor', turn(k + 1))  8.64 us
    ppermute x1, waiting for transfers between devices, per_device(): own_kv = lax.ppermute(packed_kv, 'tensor', swap)[None]  8.01 us
    ppermute x2, waiting for transfers between devices, per_device(): received.append(lax.ppermute(outs[-1], 'tensor', ring))  7.07 us
    pallas_call x2, Pallas kernels, first_output(): pl.pallas_call(first_output_kernel, out_shape=shape((chunk, cols), F32),...  6.47 us
    pallas_call x5, Pallas kernels, stage(): pl.pallas_call(partial(stage_kernel, pairs=len(joined), first=first, coun...  6.31 us
    pallas_call x1, Pallas kernels, far_kv_product(): pl.pallas_call(partial(far_kv_kernel, order=order, cuts=[len(block) for b...  6.03 us
  transfers between devices with their start and end apart: 30, of which 12 were waited for; matrix products, arithmetic and copies ran while one was open for 1% of the time, Pallas kernels for 28%

profile of v13, /device:TPU:2, one launch (start us, length us, event | category | flops | bytes accessed | tf_op | source)
XLA Modules:
  0.0 146.9 jit_solution(2844073812184767440)
XLA Ops:
  0.0 2.1 %pack.1 = (bf16[288,256]{1,0:T(8,128)(2,1)}, bf16[288,256]{1,0:T(8,128)(2,1)}, bf16[128,1152]{1,0:T(8,128)(2,1)}) custom-call(s32[1]{0:T(128)} %bitcast.9.at_ref, bf16[4608,256]{1,0:T(8,128)(2,1)} %q_ref.3, bf16[4608,128]{1,0:T(8,128)(2,1)} %k_ref.3, bf16[4608,128]{1,0:T(8,128)(2,1)} %v_ref.3, bf16[768,1152]{1,0:T(8,128)(2,1)} %token_ref.1), custom_call_target="tpu_custom_call" | custom-call | tf_op jit(solution)/shard_map/pack/pallas_call | solution.py:75
  2.1 1.6 %collective-permute-start.10 = (bf16[128,1152]{1,0:T(8,128)(2,1)}, bf16[128,1152]{1,0:T(8,128)(2,1)S(1)}, u32[]{:S(2)}, u32[]{:S(2)}) collective-permute-start(bf16[128,1152]{1,0:T(8,128)(2,1)} %get-tuple-element.32), channel_id=1, source_target_pairs={{0,1},{1,0},{2,3},{3,2},{4,5},{5,4},{6,7},{7,6},{8,9},{9,8},{10,11... | collective-permute-start | bytes 884744 | tf_op jit(solution)/shard_map/ppermute | solution.py:699
  3.7 2.6 %collective-permute-start = (bf16[288,256]{1,0:T(8,128)(2,1)}, bf16[288,256]{1,0:T(8,128)(2,1)S(1)}, u32[]{:S(2)}, u32[]{:S(2)}) collective-permute-start(bf16[288,256]{1,0:T(8,128)(2,1)} %get-tuple-element.25), channel_id=1, source_target_pairs={{0,2},{1,3},{2,0},{3,1},{4,6},{5,7},{6,4},{7,5},{8,10},{9,11},{10,... | collective-permute-start | bytes 442376 | tf_op jit(solution)/shard_map/ppermute | solution.py:697
  6.7 8.0 %collective-permute-done = bf16[288,256]{1,0:T(8,128)(2,1)S(1)} collective-permute-done((bf16[288,256]{1,0:T(8,128)(2,1)}, bf16[288,256]{1,0:T(8,128)(2,1)S(1)}, u32[]{:S(2)}, u32[]{:S(2)}) %collective-permute-start) | collective-permute-done | bytes 147488 | tf_op jit(solution)/shard_map/ppermute | solution.py:697
  14.7 5.0 %collective-permute-done.6 = bf16[288,256]{1,0:T(8,128)(2,1)S(1)} collective-permute-done((bf16[288,256]{1,0:T(8,128)(2,1)}, bf16[288,256]{1,0:T(8,128)(2,1)S(1)}, u32[]{:S(2)}, u32[]{:S(2)}) %collective-permute-start.6) | collective-permute-done | bytes 147488 | tf_op jit(solution)/shard_map/ppermute | solution.py:698
  22.4 3.1 %collective-permute-done.5.refs_1_ = bf16[1,288,256]{2,1,0:T(8,128)(2,1)S(1)} collective-permute-done((bf16[1,288,256]{2,1,0:T(8,128)(2,1)S(1)}, bf16[1,288,256]{2,1,0:T(8,128)(2,1)S(1)}, u32[]{:S(2)}, u32[]{:S(2)}) %collective-permute-start.5) | collective-permute-done | bytes 147488 | tf_op jit(solution)/shard_map/ppermute | solution.py:722
  26.0 2.0 %stage.5 = (bf16[2,288,256]{2,1,0:T(8,128)(2,1)}, bf16[2,288,256]{2,1,0:T(8,128)(2,1)}, bf16[288,1152]{1,0:T(8,128)(2,1)}) custom-call(bf16[1,288,256]{2,1,0:T(8,128)(2,1)S(1)} %bitcast.20, bf16[1,288,256]{2,1,0:T(8,128)(2,1)S(1)} %collective-permute-done.5.refs_1_, bf16[1,288,256]{2,1,0:T(8,128)(2,1)S(1)} %bitcast.24, ...), custom_call_target="tpu_custom_call" | custom-call | tf_op jit(solution)/shard_map/stage/pallas_call | solution.py:130
  31.2 1.7 %copy-done.5 = bf16[256,4608]{1,0:T(8,128)(2,1)S(1)} copy-done((bf16[256,4608]{1,0:T(8,128)(2,1)S(1)}, bf16[256,4608]{1,0:T(8,128)(2,1)}, u32[]{:S(2)}) %copy-start.5) | copy-done | bytes 2359320
  33.5 1.6 %collective-permute-start.1 = (bf16[32,1152]{1,0:T(8,128)(2,1)S(1)}, bf16[32,1152]{1,0:T(8,128)(2,1)S(1)}, u32[]{:S(2)}, u32[]{:S(2)}) collective-permute-start(bf16[32,1152]{1,0:T(8,128)(2,1)S(1)} %get-tuple-element.26), channel_id=1, source_target_pairs={{0,1},{1,2},{2,3},{3,0},{4,5},{5,6},{6,7},{7,4},{8,9},{9,10},{10,1... | collective-permute-start | bytes 221192 | tf_op jit(solution)/shard_map/ppermute | solution.py:703
  36.3 5.5 %collective-permute-done.1.refs_6_ = bf16[32,1152]{1,0:T(8,128)(2,1)S(1)} collective-permute-done((bf16[32,1152]{1,0:T(8,128)(2,1)S(1)}, bf16[32,1152]{1,0:T(8,128)(2,1)S(1)}, u32[]{:S(2)}, u32[]{:S(2)}) %collective-permute-start.1) | collective-permute-done | bytes 73760 | tf_op jit(solution)/shard_map/ppermute | solution.py:703
  41.9 1.9 %collective-permute-start.13 = (bf16[288,1152]{1,0:T(8,128)(2,1)}, bf16[288,1152]{1,0:T(8,128)(2,1)}, u32[]{:S(2)}, u32[]{:S(2)}) collective-permute-start(bf16[288,1152]{1,0:T(8,128)(2,1)} %get-tuple-element.34), channel_id=1, source_target_pairs={{0,1},{1,0},{2,3},{3,2},{4,5},{5,4},{6,7},{7,6},{8,9},{9,8},{10,11... | collective-permute-start | bytes 1990664 | tf_op jit(solution)/shard_map/ppermute | solution.py:720
  43.8 3.2 %collective-permute-done.3.refs_8_ = bf16[32,1152]{1,0:T(8,128)(2,1)S(1)} collective-permute-done((bf16[32,1152]{1,0:T(8,128)(2,1)S(1)}, bf16[32,1152]{1,0:T(8,128)(2,1)S(1)}, u32[]{:S(2)}, u32[]{:S(2)}) %collective-permute-start.3) | collective-permute-done | bytes 73760 | tf_op jit(solution)/shard_map/ppermute | solution.py:703
  47.0 2.3 %stage.7 = (bf16[4,288,256]{2,1,0:T(8,128)(2,1)}, bf16[4,288,256]{2,1,0:T(8,128)(2,1)}) custom-call(bf16[2,288,256]{2,1,0:T(8,128)(2,1)} %get-tuple-element.30.refs_0_, bf16[2,288,256]{2,1,0:T(8,128)(2,1)} %collective-permute-done.8.refs_1_, bf16[2,288,256]{2,1,0:T(8,128)(2,1)} %get-tuple-element.31.refs_2_, ...), custom_call_target="tpu_custom_call" | custom-call | flops 49999998976 | bytes 100000000 | tf_op jit(solution)/shard_map/stage/pallas_call | solution.py:130
  50.0 7.1 %collective-permute-done.13.rest_3_ = bf16[288,1152]{1,0:T(8,128)(2,1)} collective-permute-done((bf16[288,1152]{1,0:T(8,128)(2,1)}, bf16[288,1152]{1,0:T(8,128)(2,1)}, u32[]{:S(2)}, u32[]{:S(2)}) %collective-permute-start.13) | collective-permute-done | bytes 663584 | tf_op jit(solution)/shard_map/ppermute | solution.py:720
  57.1 6.0 %far_kv.1 = (bf16[784,256]{1,0:T(8,128)(2,1)S(1)}, bf16[2,768,1152]{2,1,0:T(8,128)(2,1)}, f32[1,768]{1,0:T(1,128)S(1)}) custom-call(s32[2]{0:T(128)S(1)} %get-tuple-element.49.place_ref, s32[2]{0:T(128)S(1)} %get-tuple-element.48.src_ref, f32[4,1,1152]{2,1,0:T(1,128)S(1)} %reshape.21.gain_ref, bf16[4,288,256]{2,1,0:T(8,128)(2,1)} %get-tuple-element.33.own_ref, ...), custom_call_target="tpu_custom_call" | custom-call | tf_op jit(solution)/shard_map/far_kv/pallas_call | solution.py:258
  63.1 1.9 %collective-permute-start.16 = (bf16[784,256]{1,0:T(8,128)(2,1)S(1)}, bf16[784,256]{1,0:T(8,128)(2,1)S(1)}, u32[]{:S(2)}, u32[]{:S(2)}) collective-permute-start(bf16[784,256]{1,0:T(8,128)(2,1)S(1)} %get-tuple-element.37.rest_0_), channel_id=1, source_target_pairs={{0,2},{1,3},{2,0},{3,1},{4,6},{5,7},{6,4},{7,5},{8,10},{9,11},{10,... | collective-permute-start | bytes 1204232 | tf_op jit(solution)/shard_map/ppermute | solution.py:744
  67.1 5.7 %near.1.rest_0_.near_ref = f32[768,512]{1,0:T(8,128)S(1)} custom-call(s32[2]{0:T(128)S(1)} %broadcast_add_fusion.src_ref, bf16[2,768,1152]{2,1,0:T(8,128)(2,1)} %get-tuple-element.36.x_ref, bf16[4608,128]{1,0:T(8,128)(2,1)S(1)} %copy-done.3, bf16[4608,128]{1,0:T(8,128)(2,1)S(1)} %copy-done.4, bf16[4608,256]{1,0:T(8,128)(2,1)} %q_ref.3, ...), custom_call_target="tpu_custom_call" | custom-call | tf_op jit(solution)/shard_map/near/pallas_call | solution.py:348
  72.8 4.9 %far.1.refs_3_.rest_0_.x_ref = bf16[768,256]{1,0:T(8,128)(2,1)S(1)} custom-call(s32[2]{0:T(128)S(1)} %get-tuple-element.49.place_ref, s32[2]{0:T(128)S(1)} %get-tuple-element.48.src_ref, bf16[2,768,1152]{2,1,0:T(8,128)(2,1)} %get-tuple-element.36.x_ref, bf16[4,288,256]{2,1,0:T(8,128)(2,1)} %get-tuple-element.35.own_ref, ...), custom_call_target="tpu_custom_call" | custom-call | tf_op jit(solution)/shard_map/far/pallas_call | solution.py:311
  84.2 2.1 %collective-permute-start.20 = (bf16[784,256]{1,0:T(8,128)(2,1)}, bf16[784,256]{1,0:T(8,128)(2,1)S(1)}, u32[]{:S(2)}, u32[]{:S(2)}) collective-permute-start(bf16[784,256]{1,0:T(8,128)(2,1)} %copy-done.6), channel_id=1, source_target_pairs={{0,4},{4,8},{8,12},{1,5},{5,9},{9,13},{2,6},{6,10},{10,14},{3,7},{... | collective-permute-start | bytes 1204232 | tf_op jit(solution)/shard_map/ppermute | solution.py:767
  89.2 10.6 %collective-permute-done.18.far_ref = bf16[768,256]{1,0:T(8,128)(2,1)} collective-permute-done((bf16[768,256]{1,0:T(8,128)(2,1)S(1)}, bf16[768,256]{1,0:T(8,128)(2,1)}, u32[]{:S(2)}, u32[]{:S(2)}) %collective-permute-start.18) | collective-permute-done | bytes 393248 | tf_op jit(solution)/shard_map/ppermute | solution.py:753
  101.4 7.0 %attend.2.rest_0_ = bf16[384,256]{1,0:T(8,128)(2,1)S(1)} custom-call(s32[1]{0:T(128)} %bitcast.16.seq_ref, bf16[768,256]{1,0:T(8,128)(2,1)S(1)} %queries.1.q_ref, s32[1,768]{1,0:T(1,128)S(1)} %broadcast_in_dim.21.id_ref, bf16[784,256]{1,0:T(8,128)(2,1)S(1)} %copy-done.7, bf16[784,256]{1,0:T(8,128)(2,1)S(1)} %collective-permute-done.19.rest_0_, ...), custom_call_target="tpu_custom_call" | custom-call | flops 905969664 | bytes 2359296 | tf_op jit(solution)/shard_map/attend/pallas_call | solution.py:511
  108.5 2.2 %collective-permute-start.21 = (bf16[384,256]{1,0:T(8,128)(2,1)S(1)}, bf16[384,256]{1,0:T(8,128)(2,1)S(1)}, u32[]{:S(2)}, u32[]{:S(2)}) collective-permute-start(bf16[384,256]{1,0:T(8,128)(2,1)S(1)} %attend.2.rest_0_), channel_id=1, source_target_pairs={{0,1},{1,0},{2,3},{3,2},{4,5},{5,4},{6,7},{7,6},{8,9},{9,8},{10,11... | collective-permute-start | bytes 589832 | tf_op jit(solution)/shard_map/ppermute | solution.py:780
  112.1 4.5 %attend.3.rest_2_.after_ref.rest_0_ = bf16[384,256]{1,0:T(8,128)(2,1)S(1)} custom-call(s32[1]{0:T(128)} %bitcast.16.seq_ref, bf16[768,256]{1,0:T(8,128)(2,1)S(1)} %queries.1.q_ref, s32[1,768]{1,0:T(1,128)S(1)} %broadcast_in_dim.21.id_ref, bf16[3,256,1152]{2,1,0:T(8,128)(2,1)S(1)} %lay.1.after_ref.o_ref, ...), custom_call_target="tpu_custom_call" | custom-call | flops 905969664 | bytes 2359296 | tf_op jit(solution)/shard_map/attend/pallas_call | solution.py:511
  116.7 2.8 %collective-permute-start.25 = (bf16[384,256]{1,0:T(8,128)(2,1)S(1)}, bf16[384,256]{1,0:T(8,128)(2,1)S(1)}, u32[]{:S(2)}, u32[]{:S(2)}) collective-permute-start(bf16[384,256]{1,0:T(8,128)(2,1)S(1)} %attend.3.rest_2_.after_ref.rest_0_), channel_id=1, source_target_pairs={{0,2},{1,3},{2,0},{3,1},{4,6},{5,7},{6,4},{7,5},{8,10},{9,11},{10,... | collective-permute-start | bytes 589832 | tf_op jit(solution)/shard_map/ppermute | solution.py:779
  119.5 3.2 %first_output.2.part_ref = f32[384,1152]{1,0:T(8,128)S(1)} custom-call(s32[2]{0:T(128)S(1)} %pad_add_fusion.1.at_ref, bf16[256,4608]{1,0:T(8,128)(2,1)} %own_o_ref.3, bf16[3,256,1152]{2,1,0:T(8,128)(2,1)S(1)} %lay.1.after_ref.o_ref, bf16[384,256]{1,0:T(8,128)(2,1)S(1)} %attend.2.rest_0_, bf16[384,256]{1,0:T(8,128)(2,1)S(1)} %collective-permute-done.21.rest_1_, ...), custom_call_target="tpu_custom_call" | custom-call | flops 49999998976 | bytes 100000000 | tf_op jit(solution)/shard_map/first_output/pallas_call | solution.py:586
  122.8 3.5 %collective-permute-done.25.rest_0_ = bf16[384,256]{1,0:T(8,128)(2,1)S(1)} collective-permute-done((bf16[384,256]{1,0:T(8,128)(2,1)S(1)}, bf16[384,256]{1,0:T(8,128)(2,1)S(1)}, u32[]{:S(2)}, u32[]{:S(2)}) %collective-permute-start.25) | collective-permute-done | bytes 196640 | tf_op jit(solution)/shard_map/ppermute | solution.py:779
  126.3 3.0 %collective-permute-start.26 = (bf16[384,256]{1,0:T(8,128)(2,1)S(1)}, bf16[384,256]{1,0:T(8,128)(2,1)S(1)}, u32[]{:S(2)}, u32[]{:S(2)}) collective-permute-start(bf16[384,256]{1,0:T(8,128)(2,1)S(1)} %collective-permute-done.25.rest_0_), channel_id=1, source_target_pairs={{0,1},{1,0},{2,3},{3,2},{4,5},{5,4},{6,7},{7,6},{8,9},{9,8},{10,11... | collective-permute-start | bytes 589832 | tf_op jit(solution)/shard_map/ppermute | solution.py:783
  129.3 3.2 %first_output.3.part_ref = f32[384,1152]{1,0:T(8,128)S(1)} custom-call(s32[2]{0:T(128)S(1)} %pad_add_fusion.1.at_ref, bf16[256,4608]{1,0:T(8,128)(2,1)} %own_o_ref.3, bf16[3,256,1152]{2,1,0:T(8,128)(2,1)S(1)} %lay.1.after_ref.o_ref, bf16[384,256]{1,0:T(8,128)(2,1)S(1)} %attend.3.rest_2_.after_ref.rest_0_, ...), custom_call_target="tpu_custom_call" | custom-call | flops 49999998976 | bytes 100000000 | tf_op jit(solution)/shard_map/first_output/pallas_call | solution.py:586
  132.6 2.5 %last_output.2 = (f32[384,1152]{1,0:T(8,128)S(1)}, f32[1,384]{1,0:T(1,128)S(1)}) custom-call(s32[2]{0:T(128)S(1)} %pad_add_fusion.at_ref, f32[384,1152]{1,0:T(8,128)S(1)} %first_output.2.part_ref, bf16[3,256,1152]{2,1,0:T(8,128)(2,1)S(1)} %lay.1.after_ref.o_ref, bf16[384,256]{1,0:T(8,128)(2,1)S(1)} %gate.3.rest_0_, ...), custom_call_target="tpu_custom_call" | custom-call | tf_op jit(solution)/shard_map/last_output/pallas_call | solution.py:610
  135.1 2.5 %last_output.3 = (f32[384,1152]{1,0:T(8,128)S(1)}, f32[1,768]{1,0:T(1,128)S(1)}) custom-call(s32[2]{0:T(128)S(1)} %pad_add_fusion.at_ref, f32[384,1152]{1,0:T(8,128)S(1)} %first_output.3.part_ref, bf16[3,256,1152]{2,1,0:T(8,128)(2,1)S(1)} %lay.1.after_ref.o_ref, bf16[384,256]{1,0:T(8,128)(2,1)S(1)} %collective-permute-done.25.rest_0_, ...), custom_call_target="tpu_custom_call" | custom-call | tf_op jit(solution)/shard_map/last_output/pallas_call | solution.py:610
  137.7 2.4 %collective-permute-start.28 = (f32[1,768]{1,0:T(1,128)S(1)}, f32[1,768]{1,0:T(1,128)S(1)}, u32[]{:S(2)}, u32[]{:S(2)}) collective-permute-start(f32[1,768]{1,0:T(1,128)S(1)} %get-tuple-element.44.rest_2_), channel_id=1, source_target_pairs={{0,2},{1,3},{2,0},{3,1},{4,6},{5,7},{6,4},{7,5},{8,10},{9,11},{10,... | collective-permute-start | bytes 9224 | tf_op jit(solution)/shard_map/ppermute | solution.py:798
  143.7 3.3 %finish.1 = bf16[768,1152]{1,0:T(8,128)(2,1)} custom-call(bf16[768,1152]{1,0:T(8,128)(2,1)S(1)} %copy-done, f32[1,1152]{1,0:T(1,128)S(1)} %broadcast_in_dim.17.gain_ref, f32[384,1152]{1,0:T(8,128)S(1)} %get-tuple-element.41.rest_0_, f32[384,1152]{1,0:T(8,128)S(1)} %get-tuple-element.43.rest_1_, f32[1,768]{1,0:T(1,128)S(1)} %get-tuple-element.44.rest_2_, ...), custom_call_target="tpu_custom_call" | custom-call | tf_op jit(solution)/shard_map/finish/pallas_call | solution.py:651
  (93 shorter events, 27.6 us)
Async XLA Ops:
  0.0 19.7 %copy-start = (bf16[768,1152]{1,0:T(8,128)(2,1)S(1)}, bf16[768,1152]{1,0:T(8,128)(2,1)}, u32[]{:S(2)}) copy-start(bf16[768,1152]{1,0:T(8,128)(2,1)} %token_ref.1) | copy-start | bytes 5308420
  2.1 17.6 %collective-permute-start.10 = (bf16[128,1152]{1,0:T(8,128)(2,1)}, bf16[128,1152]{1,0:T(8,128)(2,1)S(1)}, u32[]{:S(2)}, u32[]{:S(2)}) collective-permute-start(bf16[128,1152]{1,0:T(8,128)(2,1)} %get-tuple-element.32), channel_id=1, source_target_pairs={{0,1},{1,0},{2,3},{3,2},{4,5},{5,4},{6,7},{7,6},{8,9},{9,8},{10,11... | collective-permute-start | bytes 884744 | tf_op jit(solution)/shard_map/ppermute | solution.py:699
  3.7 10.9 %collective-permute-start = (bf16[288,256]{1,0:T(8,128)(2,1)}, bf16[288,256]{1,0:T(8,128)(2,1)S(1)}, u32[]{:S(2)}, u32[]{:S(2)}) collective-permute-start(bf16[288,256]{1,0:T(8,128)(2,1)} %get-tuple-element.25), channel_id=1, source_target_pairs={{0,2},{1,3},{2,0},{3,1},{4,6},{5,7},{6,4},{7,5},{8,10},{9,11},{10,... | collective-permute-start | bytes 442376 | tf_op jit(solution)/shard_map/ppermute | solution.py:697
  6.3 13.4 %collective-permute-start.6 = (bf16[288,256]{1,0:T(8,128)(2,1)}, bf16[288,256]{1,0:T(8,128)(2,1)S(1)}, u32[]{:S(2)}, u32[]{:S(2)}) collective-permute-start(bf16[288,256]{1,0:T(8,128)(2,1)} %get-tuple-element.29), channel_id=1, source_target_pairs={{0,2},{1,3},{2,0},{3,1},{4,6},{5,7},{6,4},{7,5},{8,10},{9,11},{10,... | collective-permute-start | bytes 442376 | tf_op jit(solution)/shard_map/ppermute | solution.py:698
  19.8 27.2 %collective-permute-start.11 = (bf16[352,1152]{1,0:T(8,128)(2,1)S(1)}, bf16[352,1152]{1,0:T(8,128)(2,1)}, u32[]{:S(2)}, u32[]{:S(2)}) collective-permute-start(bf16[352,1152]{1,0:T(8,128)(2,1)S(1)} %stage.6), channel_id=1, source_target_pairs={{0,1},{1,0},{2,3},{3,2},{4,5},{5,4},{6,7},{7,6},{8,9},{9,8},{10,11... | collective-permute-start | bytes 2433032 | tf_op jit(solution)/shard_map/ppermute | solution.py:720
  20.3 5.1 %collective-permute-start.5 = (bf16[1,288,256]{2,1,0:T(8,128)(2,1)S(1)}, bf16[1,288,256]{2,1,0:T(8,128)(2,1)S(1)}, u32[]{:S(2)}, u32[]{:S(2)}) collective-permute-start(bf16[1,288,256]{2,1,0:T(8,128)(2,1)S(1)} %bitcast.19), channel_id=1, source_target_pairs={{0,8},{4,12},{8,0},{12,4},{16,24},{20,28},{24,16},{28,20},{1,9},{5... | collective-permute-start | bytes 442376 | tf_op jit(solution)/shard_map/ppermute | solution.py:722
  20.8 5.1 %collective-permute-start.7 = (bf16[1,288,256]{2,1,0:T(8,128)(2,1)S(1)}, bf16[1,288,256]{2,1,0:T(8,128)(2,1)S(1)}, u32[]{:S(2)}, u32[]{:S(2)}) collective-permute-start(bf16[1,288,256]{2,1,0:T(8,128)(2,1)S(1)} %bitcast.23), channel_id=1, source_target_pairs={{0,16},{4,20},{8,24},{12,28},{16,0},{20,4},{24,8},{28,12},{1,17},{... | collective-permute-start | bytes 442376 | tf_op jit(solution)/shard_map/ppermute | solution.py:723
  28.0 18.9 %collective-permute-start.8 = (bf16[2,288,256]{2,1,0:T(8,128)(2,1)}, bf16[2,288,256]{2,1,0:T(8,128)(2,1)}, u32[]{:S(2)}, u32[]{:S(2)}) collective-permute-start(bf16[2,288,256]{2,1,0:T(8,128)(2,1)} %get-tuple-element.30.refs_0_), channel_id=1, source_target_pairs={{0,16},{4,20},{8,24},{12,28},{16,0},{20,4},{24,8},{28,12},{1,17},{... | collective-permute-start | bytes 884744 | tf_op jit(solution)/shard_map/ppermute | solution.py:722
  29.6 17.4 %collective-permute-start.9 = (bf16[2,288,256]{2,1,0:T(8,128)(2,1)}, bf16[2,288,256]{2,1,0:T(8,128)(2,1)}, u32[]{:S(2)}, u32[]{:S(2)}) collective-permute-start(bf16[2,288,256]{2,1,0:T(8,128)(2,1)} %get-tuple-element.31.refs_2_), channel_id=1, source_target_pairs={{0,8},{4,12},{8,0},{12,4},{16,24},{20,28},{24,16},{28,20},{1,9},{5... | collective-permute-start | bytes 884744 | tf_op jit(solution)/shard_map/ppermute | solution.py:723
  33.5 8.3 %collective-permute-start.1 = (bf16[32,1152]{1,0:T(8,128)(2,1)S(1)}, bf16[32,1152]{1,0:T(8,128)(2,1)S(1)}, u32[]{:S(2)}, u32[]{:S(2)}) collective-permute-start(bf16[32,1152]{1,0:T(8,128)(2,1)S(1)} %get-tuple-element.26), channel_id=1, source_target_pairs={{0,1},{1,2},{2,3},{3,0},{4,5},{5,6},{6,7},{7,4},{8,9},{9,10},{10,1... | collective-permute-start | bytes 221192 | tf_op jit(solution)/shard_map/ppermute | solution.py:703
  35.1 6.8 %collective-permute-start.2 = (bf16[32,1152]{1,0:T(8,128)(2,1)S(1)}, bf16[32,1152]{1,0:T(8,128)(2,1)S(1)}, u32[]{:S(2)}, u32[]{:S(2)}) collective-permute-start(bf16[32,1152]{1,0:T(8,128)(2,1)S(1)} %get-tuple-element.27), channel_id=1, source_target_pairs={{0,2},{1,3},{2,0},{3,1},{4,6},{5,7},{6,4},{7,5},{8,10},{9,11},{10,... | collective-permute-start | bytes 221192 | tf_op jit(solution)/shard_map/ppermute | solution.py:703
  41.7 5.2 %collective-permute-start.3 = (bf16[32,1152]{1,0:T(8,128)(2,1)S(1)}, bf16[32,1152]{1,0:T(8,128)(2,1)S(1)}, u32[]{:S(2)}, u32[]{:S(2)}) collective-permute-start(bf16[32,1152]{1,0:T(8,128)(2,1)S(1)} %get-tuple-element.28), channel_id=1, source_target_pairs={{0,3},{1,0},{2,1},{3,2},{4,7},{5,4},{6,5},{7,6},{8,11},{9,8},{10,9... | collective-permute-start | bytes 221192 | tf_op jit(solution)/shard_map/ppermute | solution.py:703
  41.9 15.2 %collective-permute-start.13 = (bf16[288,1152]{1,0:T(8,128)(2,1)}, bf16[288,1152]{1,0:T(8,128)(2,1)}, u32[]{:S(2)}, u32[]{:S(2)}) collective-permute-start(bf16[288,1152]{1,0:T(8,128)(2,1)} %get-tuple-element.34), channel_id=1, source_target_pairs={{0,1},{1,0},{2,3},{3,2},{4,5},{5,4},{6,7},{7,6},{8,9},{9,8},{10,11... | collective-permute-start | bytes 1990664 | tf_op jit(solution)/shard_map/ppermute | solution.py:720
  49.3 7.8 %collective-permute-start.12 = (bf16[4,288,256]{2,1,0:T(8,128)(2,1)}, bf16[4,288,256]{2,1,0:T(8,128)(2,1)}, u32[]{:S(2)}, u32[]{:S(2)}) collective-permute-start(bf16[4,288,256]{2,1,0:T(8,128)(2,1)} %get-tuple-element.33.own_ref), channel_id=1, source_target_pairs={{0,4},{4,0},{8,12},{12,8},{16,20},{20,16},{24,28},{28,24},{1,5},{5... | collective-permute-start | bytes 1769480 | tf_op jit(solution)/shard_map/ppermute | solution.py:722
  49.4 7.7 %collective-permute-start.14 = (bf16[4,288,256]{2,1,0:T(8,128)(2,1)}, bf16[4,288,256]{2,1,0:T(8,128)(2,1)S(1)}, u32[]{:S(2)}, u32[]{:S(2)}) collective-permute-start(bf16[4,288,256]{2,1,0:T(8,128)(2,1)} %get-tuple-element.35.own_ref), channel_id=1, source_target_pairs={{0,4},{4,0},{8,12},{12,8},{16,20},{20,16},{24,28},{28,24},{1,5},{5... | collective-permute-start | bytes 1769480 | tf_op jit(solution)/shard_map/ppermute | solution.py:723
  63.1 17.2 %collective-permute-start.16 = (bf16[784,256]{1,0:T(8,128)(2,1)S(1)}, bf16[784,256]{1,0:T(8,128)(2,1)S(1)}, u32[]{:S(2)}, u32[]{:S(2)}) collective-permute-start(bf16[784,256]{1,0:T(8,128)(2,1)S(1)} %get-tuple-element.37.rest_0_), channel_id=1, source_target_pairs={{0,2},{1,3},{2,0},{3,1},{4,6},{5,7},{6,4},{7,5},{8,10},{9,11},{10,... | collective-permute-start | bytes 1204232 | tf_op jit(solution)/shard_map/ppermute | solution.py:744
  65.0 12.8 %collective-permute-start.4 = (bf16[1,3,32,1152]{3,2,1,0:T(8,128)(2,1)S(1)}, bf16[1,3,32,1152]{3,2,1,0:T(8,128)(2,1)S(1)}, u32[]{:S(2)}, u32[]{:S(2)}) collective-permute-start(bf16[1,3,32,1152]{3,2,1,0:T(8,128)(2,1)S(1)} %maximum_bitcast_fusion.refs_0_), channel_id=1, source_target_pairs={{0,8},{4,12},{8,0},{12,4},{16,24},{20,28},{24,16},{28,20},{1,9},{5... | collective-permute-start | bytes 663560 | tf_op jit(solution)/shard_map/ppermute | solution.py:733
  78.4 8.5 %collective-permute-start.15 = (bf16[2,3,32,1152]{3,2,1,0:T(8,128)(2,1)S(1)}, bf16[2,3,32,1152]{3,2,1,0:T(8,128)(2,1)}, u32[]{:S(2)}, u32[]{:S(2)}) collective-permute-start(bf16[2,3,32,1152]{3,2,1,0:T(8,128)(2,1)S(1)} %stage.8.rest_1_.refs_0_), channel_id=1, source_target_pairs={{0,16},{4,20},{8,24},{12,28},{16,0},{20,4},{24,8},{28,12},{1,17},{... | collective-permute-start | bytes 1327112 | tf_op jit(solution)/shard_map/ppermute | solution.py:733
  81.9 17.9 %collective-permute-start.18 = (bf16[768,256]{1,0:T(8,128)(2,1)S(1)}, bf16[768,256]{1,0:T(8,128)(2,1)}, u32[]{:S(2)}, u32[]{:S(2)}) collective-permute-start(bf16[768,256]{1,0:T(8,128)(2,1)S(1)} %gate.2), channel_id=1, source_target_pairs={{0,2},{1,3},{2,0},{3,1},{4,6},{5,7},{6,4},{7,5},{8,10},{9,11},{10,... | collective-permute-start | bytes 1179656 | tf_op jit(solution)/shard_map/ppermute | solution.py:753
  82.7 17.1 %copy-start.2 = (f32[768,512]{1,0:T(8,128)S(1)}, f32[768,512]{1,0:T(8,128)}, u32[]{:S(2)}) copy-start(f32[768,512]{1,0:T(8,128)} %copy-done.1) | copy-start | bytes 4718596
  82.7 18.6 %collective-permute-start.19 = (bf16[784,256]{1,0:T(8,128)(2,1)}, bf16[784,256]{1,0:T(8,128)(2,1)S(1)}, u32[]{:S(2)}, u32[]{:S(2)}) collective-permute-start(bf16[784,256]{1,0:T(8,128)(2,1)} %copy-done.6), channel_id=1, source_target_pairs={{0,8},{4,12},{1,9},{5,13},{2,10},{6,14},{3,11},{7,15},{16,24},{20,... | collective-permute-start | bytes 1204232 | tf_op jit(solution)/shard_map/ppermute | solution.py:767
  84.2 17.2 %collective-permute-start.20 = (bf16[784,256]{1,0:T(8,128)(2,1)}, bf16[784,256]{1,0:T(8,128)(2,1)S(1)}, u32[]{:S(2)}, u32[]{:S(2)}) collective-permute-start(bf16[784,256]{1,0:T(8,128)(2,1)} %copy-done.6), channel_id=1, source_target_pairs={{0,4},{4,8},{8,12},{1,5},{5,9},{9,13},{2,6},{6,10},{10,14},{3,7},{... | collective-permute-start | bytes 1204232 | tf_op jit(solution)/shard_map/ppermute | solution.py:767
  89.2 21.5 %collective-permute-start.17 = (bf16[4,3,32,1152]{3,2,1,0:T(8,128)(2,1)S(1)}, bf16[4,3,32,1152]{3,2,1,0:T(8,128)(2,1)S(1)}, u32[]{:S(2)}, u32[]{:S(2)}) collective-permute-start(bf16[4,3,32,1152]{3,2,1,0:T(8,128)(2,1)S(1)} %stage.9.own_ref), channel_id=1, source_target_pairs={{0,4},{4,0},{8,12},{12,8},{16,20},{20,16},{24,28},{28,24},{1,5},{5... | collective-permute-start | bytes 2654216 | tf_op jit(solution)/shard_map/ppermute | solution.py:733
  108.4 11.1 %collective-permute-start.22 = (bf16[384,256]{1,0:T(8,128)(2,1)S(1)}, bf16[384,256]{1,0:T(8,128)(2,1)S(1)}, u32[]{:S(2)}, u32[]{:S(2)}) collective-permute-start(bf16[384,256]{1,0:T(8,128)(2,1)S(1)} %attend.2.rest_0_), channel_id=1, source_target_pairs={{0,2},{1,3},{2,0},{3,1},{4,6},{5,7},{6,4},{7,5},{8,10},{9,11},{10,... | collective-permute-start | bytes 589832 | tf_op jit(solution)/shard_map/ppermute | solution.py:779
  108.5 11.1 %collective-permute-start.21 = (bf16[384,256]{1,0:T(8,128)(2,1)S(1)}, bf16[384,256]{1,0:T(8,128)(2,1)S(1)}, u32[]{:S(2)}, u32[]{:S(2)}) collective-permute-start(bf16[384,256]{1,0:T(8,128)(2,1)S(1)} %attend.2.rest_0_), channel_id=1, source_target_pairs={{0,1},{1,0},{2,3},{3,2},{4,5},{5,4},{6,7},{7,6},{8,9},{9,8},{10,11... | collective-permute-start | bytes 589832 | tf_op jit(solution)/shard_map/ppermute | solution.py:780
  116.6 12.7 %collective-permute-start.24 = (bf16[384,256]{1,0:T(8,128)(2,1)S(1)}, bf16[384,256]{1,0:T(8,128)(2,1)S(1)}, u32[]{:S(2)}, u32[]{:S(2)}) collective-permute-start(bf16[384,256]{1,0:T(8,128)(2,1)S(1)} %attend.3.rest_2_.after_ref.rest_0_), channel_id=1, source_target_pairs={{0,1},{1,0},{2,3},{3,2},{4,5},{5,4},{6,7},{7,6},{8,9},{9,8},{10,11... | collective-permute-start | bytes 589832 | tf_op jit(solution)/shard_map/ppermute | solution.py:780
  116.7 9.6 %collective-permute-start.25 = (bf16[384,256]{1,0:T(8,128)(2,1)S(1)}, bf16[384,256]{1,0:T(8,128)(2,1)S(1)}, u32[]{:S(2)}, u32[]{:S(2)}) collective-permute-start(bf16[384,256]{1,0:T(8,128)(2,1)S(1)} %attend.3.rest_2_.after_ref.rest_0_), channel_id=1, source_target_pairs={{0,2},{1,3},{2,0},{3,1},{4,6},{5,7},{6,4},{7,5},{8,10},{9,11},{10,... | collective-permute-start | bytes 589832 | tf_op jit(solution)/shard_map/ppermute | solution.py:779
  119.5 13.1 %collective-permute-start.23 = (bf16[384,256]{1,0:T(8,128)(2,1)S(1)}, bf16[384,256]{1,0:T(8,128)(2,1)S(1)}, u32[]{:S(2)}, u32[]{:S(2)}) collective-permute-start(bf16[384,256]{1,0:T(8,128)(2,1)S(1)} %gate.3.rest_0_), channel_id=1, source_target_pairs={{0,1},{1,0},{2,3},{3,2},{4,5},{5,4},{6,7},{7,6},{8,9},{9,8},{10,11... | collective-permute-start | bytes 589832 | tf_op jit(solution)/shard_map/ppermute | solution.py:783
  126.3 8.8 %collective-permute-start.26 = (bf16[384,256]{1,0:T(8,128)(2,1)S(1)}, bf16[384,256]{1,0:T(8,128)(2,1)S(1)}, u32[]{:S(2)}, u32[]{:S(2)}) collective-permute-start(bf16[384,256]{1,0:T(8,128)(2,1)S(1)} %collective-permute-done.25.rest_0_), channel_id=1, source_target_pairs={{0,1},{1,0},{2,3},{3,2},{4,5},{5,4},{6,7},{7,6},{8,9},{9,8},{10,11... | collective-permute-start | bytes 589832 | tf_op jit(solution)/shard_map/ppermute | solution.py:783
  137.7 5.4 %collective-permute-start.27 = (f32[1,768]{1,0:T(1,128)S(1)}, f32[1,768]{1,0:T(1,128)S(1)}, u32[]{:S(2)}, u32[]{:S(2)}) collective-permute-start(f32[1,768]{1,0:T(1,128)S(1)} %get-tuple-element.44.rest_2_), channel_id=1, source_target_pairs={{0,1},{1,2},{2,3},{3,0},{4,5},{5,6},{6,7},{7,4},{8,9},{9,10},{10,1... | collective-permute-start | bytes 9224 | tf_op jit(solution)/shard_map/ppermute | solution.py:798
  137.7 5.4 %collective-permute-start.28 = (f32[1,768]{1,0:T(1,128)S(1)}, f32[1,768]{1,0:T(1,128)S(1)}, u32[]{:S(2)}, u32[]{:S(2)}) collective-permute-start(f32[1,768]{1,0:T(1,128)S(1)} %get-tuple-element.44.rest_2_), channel_id=1, source_target_pairs={{0,2},{1,3},{2,0},{3,1},{4,6},{5,7},{6,4},{7,5},{8,10},{9,11},{10,... | collective-permute-start | bytes 9224 | tf_op jit(solution)/shard_map/ppermute | solution.py:798
  140.1 3.6 %collective-permute-start.29 = (f32[1,768]{1,0:T(1,128)S(1)}, f32[1,768]{1,0:T(1,128)S(1)}, u32[]{:S(2)}, u32[]{:S(2)}) collective-permute-start(f32[1,768]{1,0:T(1,128)S(1)} %get-tuple-element.44.rest_2_), channel_id=1, source_target_pairs={{0,3},{1,0},{2,1},{3,2},{4,7},{5,4},{6,5},{7,6},{8,11},{9,8},{10,9... | collective-permute-start | bytes 9224 | tf_op jit(solution)/shard_map/ppermute | solution.py:798
  (13 other events, 67.4 us)

commit v14 on v13

--- a/solution.py
+++ b/solution.py
@@ -473,13 +473,17 @@
 
     stop = (first + Q_TILE + K_TILE - 1) // K_TILE
 
-    def step(j, state):
+    clear = jnp.minimum((jnp.max(start) + K_TILE - 1) // K_TILE, stop)
+    edge = jnp.maximum((first + 1) // K_TILE, clear)
+
+    def step(j, state, masked):
         scores, run_max, run_sum, acc = state
         following = score(jnp.minimum(j + 1, stop - 1))
         base = pl.multiple_of(j * K_TILE, K_TILE)
-        key_pos = base + lax.broadcasted_iota(jnp.int32, (K_TILE, width), 0)
-        allowed = (key_pos >= start) & (key_pos <= place)
-        scores = jnp.where(allowed, scores, NEG)
+        if masked:
+            key_pos = base + lax.broadcasted_iota(jnp.int32, (K_TILE, width), 0)
+            allowed = (key_pos >= start) & (key_pos <= place)
+            scores = jnp.where(allowed, scores, NEG)
         new_max = jnp.maximum(run_max, jnp.max(scores, axis=0, keepdims=True))
         expo = jnp.exp2(scores - new_max)
         factor = jnp.exp2(run_max - new_max)
@@ -495,7 +499,9 @@
         jnp.zeros((1, width), F32),
         jnp.zeros((HEAD_SIZE, width), F32),
     )
-    _, _, run_sum, acc = lax.fori_loop(low, stop, step, state)
+    state = lax.fori_loop(low, clear, partial(step, masked=True), state)
+    state = lax.fori_loop(clear, edge, partial(step, masked=False), state)
+    _, _, run_sum, acc = lax.fori_loop(edge, stop, partial(step, masked=True), state)
     context = (acc / run_sum).T
     for g in range(group):
         out_ref[:, g * HEAD_SIZE : (g + 1) * HEAD_SIZE] = context[

time: 147 us -> 147 us (level); the launches traced: 147 us -> 145 us
  waiting for transfers between devices: 49.2 us -> 54.2 us
  Pallas kernels: 55.3 us -> 50.7 us
  starting transfers between devices: 36 us -> 34.2 us
    pallas_call x2, Pallas kernels: 11.5 us -> 6.85 us  [attend(): pl.pallas_call(partial(attention_kernel, back=back, offset=c * rows), out...]
    ppermute x2, waiting for transfers between devices: 0.01 us -> 4.48 us  [per_device(): beside = lax.ppermute(context, 'tensor', pairs)]
    ppermute x2, waiting for transfers between devices: 0.01 us -> 2.24 us  [per_device(): across = lax.ppermute(opposite, 'tensor', pairs)]
    ppermute x2, waiting for transfers between devices: 3.48 us -> 1.39 us  [per_device(): opposite = lax.ppermute(context, 'tensor', swap)]
    ppermute x2, starting transfers between devices: 3.12 us -> 1.25 us  [per_device(): across = lax.ppermute(opposite, 'tensor', pairs)]
  transfers between devices with their start and end apart: 30 -> 30, of which waited for: 12 -> 15; matrix products, arithmetic and copies ran while one was open for 1% -> 1% of each run, Pallas kernels for 28% -> 25%
where the time goes in v14:
time: 147 us; the launch traced here: 145 us
  waiting for transfers between devices  54.2 us (37%)
  Pallas kernels  50.7 us (34%)
  starting transfers between devices  34.2 us (23%)
  local copies, waits for them, and re-layouts  3.9 us (3%)
  other arithmetic  2.08 us (1%)
    ppermute x1, waiting for transfers between devices, per_device(): got_q = lax.ppermute(gate(sent_q, got_kv), 'tensor', swap)  10.6 us
    ppermute x3, waiting for transfers between devices, per_device(): lax.ppermute(p, 'tensor', turn(k + 1))  8.64 us
    ppermute x1, waiting for transfers between devices, per_device(): own_kv = lax.ppermute(packed_kv, 'tensor', swap)[None]  8.01 us
    ppermute x2, waiting for transfers between devices, per_device(): received.append(lax.ppermute(outs[-1], 'tensor', ring))  7.07 us
    pallas_call x2, Pallas kernels, attend(): pl.pallas_call(partial(attention_kernel, back=back, offset=c * rows), out...  6.85 us
    pallas_call x2, Pallas kernels, first_output(): pl.pallas_call(first_output_kernel, out_shape=shape((chunk, cols), F32),...  6.47 us
    pallas_call x5, Pallas kernels, stage(): pl.pallas_call(partial(stage_kernel, pairs=len(joined), first=first, coun...  6.31 us
    pallas_call x1, Pallas kernels, far_kv_product(): pl.pallas_call(partial(far_kv_kernel, order=order, cuts=[len(block) for b...  6.03 us
  transfers between devices with their start and end apart: 30, of which 15 were waited for; matrix products, arithmetic and copies ran while one was open for 1% of the time, Pallas kernels for 25%

profile of v14, /device:TPU:2, one launch (start us, length us, event | category | flops | bytes accessed | tf_op | source)
XLA Modules:
  0.0 145.5 jit_solution(11423550269573210574)
XLA Ops:
  0.0 2.1 %pack.1 = (bf16[288,256]{1,0:T(8,128)(2,1)}, bf16[288,256]{1,0:T(8,128)(2,1)}, bf16[128,1152]{1,0:T(8,128)(2,1)}) custom-call(s32[1]{0:T(128)} %bitcast.9.at_ref, bf16[4608,256]{1,0:T(8,128)(2,1)} %q_ref.3, bf16[4608,128]{1,0:T(8,128)(2,1)} %k_ref.3, bf16[4608,128]{1,0:T(8,128)(2,1)} %v_ref.3, bf16[768,1152]{1,0:T(8,128)(2,1)} %token_ref.1), custom_call_target="tpu_custom_call" | custom-call | tf_op jit(solution)/shard_map/pack/pallas_call | solution.py:75
  2.1 1.6 %collective-permute-start.10 = (bf16[128,1152]{1,0:T(8,128)(2,1)}, bf16[128,1152]{1,0:T(8,128)(2,1)S(1)}, u32[]{:S(2)}, u32[]{:S(2)}) collective-permute-start(bf16[128,1152]{1,0:T(8,128)(2,1)} %get-tuple-element.32), channel_id=1, source_target_pairs={{0,1},{1,0},{2,3},{3,2},{4,5},{5,4},{6,7},{7,6},{8,9},{9,8},{10,11... | collective-permute-start | bytes 884744 | tf_op jit(solution)/shard_map/ppermute | solution.py:705
  3.7 2.6 %collective-permute-start = (bf16[288,256]{1,0:T(8,128)(2,1)}, bf16[288,256]{1,0:T(8,128)(2,1)S(1)}, u32[]{:S(2)}, u32[]{:S(2)}) collective-permute-start(bf16[288,256]{1,0:T(8,128)(2,1)} %get-tuple-element.25), channel_id=1, source_target_pairs={{0,2},{1,3},{2,0},{3,1},{4,6},{5,7},{6,4},{7,5},{8,10},{9,11},{10,... | collective-permute-start | bytes 442376 | tf_op jit(solution)/shard_map/ppermute | solution.py:703
  6.7 8.0 %collective-permute-done = bf16[288,256]{1,0:T(8,128)(2,1)S(1)} collective-permute-done((bf16[288,256]{1,0:T(8,128)(2,1)}, bf16[288,256]{1,0:T(8,128)(2,1)S(1)}, u32[]{:S(2)}, u32[]{:S(2)}) %collective-permute-start) | collective-permute-done | bytes 147488 | tf_op jit(solution)/shard_map/ppermute | solution.py:703
  14.7 5.0 %collective-permute-done.6 = bf16[288,256]{1,0:T(8,128)(2,1)S(1)} collective-permute-done((bf16[288,256]{1,0:T(8,128)(2,1)}, bf16[288,256]{1,0:T(8,128)(2,1)S(1)}, u32[]{:S(2)}, u32[]{:S(2)}) %collective-permute-start.6) | collective-permute-done | bytes 147488 | tf_op jit(solution)/shard_map/ppermute | solution.py:704
  22.4 3.1 %collective-permute-done.5.refs_1_ = bf16[1,288,256]{2,1,0:T(8,128)(2,1)S(1)} collective-permute-done((bf16[1,288,256]{2,1,0:T(8,128)(2,1)S(1)}, bf16[1,288,256]{2,1,0:T(8,128)(2,1)S(1)}, u32[]{:S(2)}, u32[]{:S(2)}) %collective-permute-start.5) | collective-permute-done | bytes 147488 | tf_op jit(solution)/shard_map/ppermute | solution.py:728
  26.0 2.0 %stage.5 = (bf16[2,288,256]{2,1,0:T(8,128)(2,1)}, bf16[2,288,256]{2,1,0:T(8,128)(2,1)}, bf16[288,1152]{1,0:T(8,128)(2,1)}) custom-call(bf16[1,288,256]{2,1,0:T(8,128)(2,1)S(1)} %bitcast.20, bf16[1,288,256]{2,1,0:T(8,128)(2,1)S(1)} %collective-permute-done.5.refs_1_, bf16[1,288,256]{2,1,0:T(8,128)(2,1)S(1)} %bitcast.24, ...), custom_call_target="tpu_custom_call" | custom-call | tf_op jit(solution)/shard_map/stage/pallas_call | solution.py:130
  31.2 1.7 %copy-done.5 = bf16[256,4608]{1,0:T(8,128)(2,1)S(1)} copy-done((bf16[256,4608]{1,0:T(8,128)(2,1)S(1)}, bf16[256,4608]{1,0:T(8,128)(2,1)}, u32[]{:S(2)}) %copy-start.5) | copy-done | bytes 2359320
  33.5 1.6 %collective-permute-start.1 = (bf16[32,1152]{1,0:T(8,128)(2,1)S(1)}, bf16[32,1152]{1,0:T(8,128)(2,1)S(1)}, u32[]{:S(2)}, u32[]{:S(2)}) collective-permute-start(bf16[32,1152]{1,0:T(8,128)(2,1)S(1)} %get-tuple-element.26), channel_id=1, source_target_pairs={{0,1},{1,2},{2,3},{3,0},{4,5},{5,6},{6,7},{7,4},{8,9},{9,10},{10,1... | collective-permute-start | bytes 221192 | tf_op jit(solution)/shard_map/ppermute | solution.py:709
  36.3 5.5 %collective-permute-done.1.refs_6_ = bf16[32,1152]{1,0:T(8,128)(2,1)S(1)} collective-permute-done((bf16[32,1152]{1,0:T(8,128)(2,1)S(1)}, bf16[32,1152]{1,0:T(8,128)(2,1)S(1)}, u32[]{:S(2)}, u32[]{:S(2)}) %collective-permute-start.1) | collective-permute-done | bytes 73760 | tf_op jit(solution)/shard_map/ppermute | solution.py:709
  41.9 1.9 %collective-permute-start.13 = (bf16[288,1152]{1,0:T(8,128)(2,1)}, bf16[288,1152]{1,0:T(8,128)(2,1)}, u32[]{:S(2)}, u32[]{:S(2)}) collective-permute-start(bf16[288,1152]{1,0:T(8,128)(2,1)} %get-tuple-element.34), channel_id=1, source_target_pairs={{0,1},{1,0},{2,3},{3,2},{4,5},{5,4},{6,7},{7,6},{8,9},{9,8},{10,11... | collective-permute-start | bytes 1990664 | tf_op jit(solution)/shard_map/ppermute | solution.py:726
  43.8 3.2 %collective-permute-done.3.refs_8_ = bf16[32,1152]{1,0:T(8,128)(2,1)S(1)} collective-permute-done((bf16[32,1152]{1,0:T(8,128)(2,1)S(1)}, bf16[32,1152]{1,0:T(8,128)(2,1)S(1)}, u32[]{:S(2)}, u32[]{:S(2)}) %collective-permute-start.3) | collective-permute-done | bytes 73760 | tf_op jit(solution)/shard_map/ppermute | solution.py:709
  47.0 2.3 %stage.7 = (bf16[4,288,256]{2,1,0:T(8,128)(2,1)}, bf16[4,288,256]{2,1,0:T(8,128)(2,1)}) custom-call(bf16[2,288,256]{2,1,0:T(8,128)(2,1)} %get-tuple-element.30.refs_0_, bf16[2,288,256]{2,1,0:T(8,128)(2,1)} %collective-permute-done.8.refs_1_, bf16[2,288,256]{2,1,0:T(8,128)(2,1)} %get-tuple-element.31.refs_2_, ...), custom_call_target="tpu_custom_call" | custom-call | flops 49999998976 | bytes 100000000 | tf_op jit(solution)/shard_map/stage/pallas_call | solution.py:130
  50.0 7.1 %collective-permute-done.13.rest_3_ = bf16[288,1152]{1,0:T(8,128)(2,1)} collective-permute-done((bf16[288,1152]{1,0:T(8,128)(2,1)}, bf16[288,1152]{1,0:T(8,128)(2,1)}, u32[]{:S(2)}, u32[]{:S(2)}) %collective-permute-start.13) | collective-permute-done | bytes 663584 | tf_op jit(solution)/shard_map/ppermute | solution.py:726
  57.1 6.0 %far_kv.1 = (bf16[784,256]{1,0:T(8,128)(2,1)S(1)}, bf16[2,768,1152]{2,1,0:T(8,128)(2,1)}, f32[1,768]{1,0:T(1,128)S(1)}) custom-call(s32[2]{0:T(128)S(1)} %get-tuple-element.49.place_ref, s32[2]{0:T(128)S(1)} %get-tuple-element.48.src_ref, f32[4,1,1152]{2,1,0:T(1,128)S(1)} %reshape.21.gain_ref, bf16[4,288,256]{2,1,0:T(8,128)(2,1)} %get-tuple-element.33.own_ref, ...), custom_call_target="tpu_custom_call" | custom-call | tf_op jit(solution)/shard_map/far_kv/pallas_call | solution.py:258
  63.1 1.9 %collective-permute-start.16 = (bf16[784,256]{1,0:T(8,128)(2,1)S(1)}, bf16[784,256]{1,0:T(8,128)(2,1)S(1)}, u32[]{:S(2)}, u32[]{:S(2)}) collective-permute-start(bf16[784,256]{1,0:T(8,128)(2,1)S(1)} %get-tuple-element.37.rest_0_), channel_id=1, source_target_pairs={{0,2},{1,3},{2,0},{3,1},{4,6},{5,7},{6,4},{7,5},{8,10},{9,11},{10,... | collective-permute-start | bytes 1204232 | tf_op jit(solution)/shard_map/ppermute | solution.py:750
  67.1 5.7 %near.1.rest_0_.near_ref = f32[768,512]{1,0:T(8,128)S(1)} custom-call(s32[2]{0:T(128)S(1)} %broadcast_add_fusion.src_ref, bf16[2,768,1152]{2,1,0:T(8,128)(2,1)} %get-tuple-element.36.x_ref, bf16[4608,128]{1,0:T(8,128)(2,1)S(1)} %copy-done.3, bf16[4608,128]{1,0:T(8,128)(2,1)S(1)} %copy-done.4, bf16[4608,256]{1,0:T(8,128)(2,1)} %q_ref.3, ...), custom_call_target="tpu_custom_call" | custom-call | tf_op jit(solution)/shard_map/near/pallas_call | solution.py:348
  72.8 4.9 %far.1.refs_3_.rest_0_.x_ref = bf16[768,256]{1,0:T(8,128)(2,1)S(1)} custom-call(s32[2]{0:T(128)S(1)} %get-tuple-element.49.place_ref, s32[2]{0:T(128)S(1)} %get-tuple-element.48.src_ref, bf16[2,768,1152]{2,1,0:T(8,128)(2,1)} %get-tuple-element.36.x_ref, bf16[4,288,256]{2,1,0:T(8,128)(2,1)} %get-tuple-element.35.own_ref, ...), custom_call_target="tpu_custom_call" | custom-call | tf_op jit(solution)/shard_map/far/pallas_call | solution.py:311
  78.4 1.6 %collective-permute-start.15 = (bf16[2,3,32,1152]{3,2,1,0:T(8,128)(2,1)S(1)}, bf16[2,3,32,1152]{3,2,1,0:T(8,128)(2,1)}, u32[]{:S(2)}, u32[]{:S(2)}) collective-permute-start(bf16[2,3,32,1152]{3,2,1,0:T(8,128)(2,1)S(1)} %stage.8.rest_1_.refs_0_), channel_id=1, source_target_pairs={{0,16},{4,20},{8,24},{12,28},{16,0},{20,4},{24,8},{28,12},{1,17},{... | collective-permute-start | bytes 1327112 | tf_op jit(solution)/shard_map/ppermute | solution.py:739
  84.2 2.1 %collective-permute-start.20 = (bf16[784,256]{1,0:T(8,128)(2,1)}, bf16[784,256]{1,0:T(8,128)(2,1)S(1)}, u32[]{:S(2)}, u32[]{:S(2)}) collective-permute-start(bf16[784,256]{1,0:T(8,128)(2,1)} %copy-done.6), channel_id=1, source_target_pairs={{0,4},{4,8},{8,12},{1,5},{5,9},{9,13},{2,6},{6,10},{10,14},{3,7},{... | collective-permute-start | bytes 1204232 | tf_op jit(solution)/shard_map/ppermute | solution.py:773
  89.2 10.6 %collective-permute-done.18.far_ref = bf16[768,256]{1,0:T(8,128)(2,1)} collective-permute-done((bf16[768,256]{1,0:T(8,128)(2,1)S(1)}, bf16[768,256]{1,0:T(8,128)(2,1)}, u32[]{:S(2)}, u32[]{:S(2)}) %collective-permute-start.18) | collective-permute-done | bytes 393248 | tf_op jit(solution)/shard_map/ppermute | solution.py:759
  101.4 3.1 %attend.2.rest_0_ = bf16[384,256]{1,0:T(8,128)(2,1)S(1)} custom-call(s32[1]{0:T(128)} %bitcast.16.seq_ref, bf16[768,256]{1,0:T(8,128)(2,1)S(1)} %queries.1.q_ref, s32[1,768]{1,0:T(1,128)S(1)} %broadcast_in_dim.21.id_ref, bf16[784,256]{1,0:T(8,128)(2,1)S(1)} %copy-done.7, bf16[784,256]{1,0:T(8,128)(2,1)S(1)} %collective-permute-done.19.rest_0_, ...), custom_call_target="tpu_custom_call" | custom-call | flops 905969664 | bytes 2359296 | tf_op jit(solution)/shard_map/attend/pallas_call | solution.py:517
  104.6 2.2 %collective-permute-start.21 = (bf16[384,256]{1,0:T(8,128)(2,1)S(1)}, bf16[384,256]{1,0:T(8,128)(2,1)S(1)}, u32[]{:S(2)}, u32[]{:S(2)}) collective-permute-start(bf16[384,256]{1,0:T(8,128)(2,1)S(1)} %attend.2.rest_0_), channel_id=1, source_target_pairs={{0,1},{1,0},{2,3},{3,2},{4,5},{5,4},{6,7},{7,6},{8,9},{9,8},{10,11... | collective-permute-start | bytes 589832 | tf_op jit(solution)/shard_map/ppermute | solution.py:786
  108.3 3.7 %attend.3.rest_2_.after_ref.rest_0_ = bf16[384,256]{1,0:T(8,128)(2,1)S(1)} custom-call(s32[1]{0:T(128)} %bitcast.16.seq_ref, bf16[768,256]{1,0:T(8,128)(2,1)S(1)} %queries.1.q_ref, s32[1,768]{1,0:T(1,128)S(1)} %broadcast_in_dim.21.id_ref, bf16[3,256,1152]{2,1,0:T(8,128)(2,1)S(1)} %lay.1.after_ref.o_ref, ...), custom_call_target="tpu_custom_call" | custom-call | flops 905969664 | bytes 2359296 | tf_op jit(solution)/shard_map/attend/pallas_call | solution.py:517
  112.1 2.8 %collective-permute-start.25 = (bf16[384,256]{1,0:T(8,128)(2,1)S(1)}, bf16[384,256]{1,0:T(8,128)(2,1)S(1)}, u32[]{:S(2)}, u32[]{:S(2)}) collective-permute-start(bf16[384,256]{1,0:T(8,128)(2,1)S(1)} %attend.3.rest_2_.after_ref.rest_0_), channel_id=1, source_target_pairs={{0,2},{1,3},{2,0},{3,1},{4,6},{5,7},{6,4},{7,5},{8,10},{9,11},{10,... | collective-permute-start | bytes 589832 | tf_op jit(solution)/shard_map/ppermute | solution.py:785
  116.2 4.5 %collective-permute-done.21.rest_1_ = bf16[384,256]{1,0:T(8,128)(2,1)S(1)} collective-permute-done((bf16[384,256]{1,0:T(8,128)(2,1)S(1)}, bf16[384,256]{1,0:T(8,128)(2,1)S(1)}, u32[]{:S(2)}, u32[]{:S(2)}) %collective-permute-start.21) | collective-permute-done | bytes 196640 | tf_op jit(solution)/shard_map/ppermute | solution.py:786
  120.7 3.2 %first_output.2.part_ref = f32[384,1152]{1,0:T(8,128)S(1)} custom-call(s32[2]{0:T(128)S(1)} %pad_add_fusion.1.at_ref, bf16[256,4608]{1,0:T(8,128)(2,1)} %own_o_ref.3, bf16[3,256,1152]{2,1,0:T(8,128)(2,1)S(1)} %lay.1.after_ref.o_ref, bf16[384,256]{1,0:T(8,128)(2,1)S(1)} %attend.2.rest_0_, bf16[384,256]{1,0:T(8,128)(2,1)S(1)} %collective-permute-done.21.rest_1_, ...), custom_call_target="tpu_custom_call" | custom-call | flops 49999998976 | bytes 100000000 | tf_op jit(solution)/shard_map/first_output/pallas_call | solution.py:592
  125.2 3.2 %first_output.3.part_ref = f32[384,1152]{1,0:T(8,128)S(1)} custom-call(s32[2]{0:T(128)S(1)} %pad_add_fusion.1.at_ref, bf16[256,4608]{1,0:T(8,128)(2,1)} %own_o_ref.3, bf16[3,256,1152]{2,1,0:T(8,128)(2,1)S(1)} %lay.1.after_ref.o_ref, bf16[384,256]{1,0:T(8,128)(2,1)S(1)} %attend.3.rest_2_.after_ref.rest_0_, ...), custom_call_target="tpu_custom_call" | custom-call | flops 49999998976 | bytes 100000000 | tf_op jit(solution)/shard_map/first_output/pallas_call | solution.py:592
  129.1 2.5 %last_output.2 = (f32[384,1152]{1,0:T(8,128)S(1)}, f32[1,384]{1,0:T(1,128)S(1)}) custom-call(s32[2]{0:T(128)S(1)} %pad_add_fusion.at_ref, f32[384,1152]{1,0:T(8,128)S(1)} %first_output.2.part_ref, bf16[3,256,1152]{2,1,0:T(8,128)(2,1)S(1)} %lay.1.after_ref.o_ref, bf16[384,256]{1,0:T(8,128)(2,1)S(1)} %gate.3.rest_0_, ...), custom_call_target="tpu_custom_call" | custom-call | tf_op jit(solution)/shard_map/last_output/pallas_call | solution.py:616
  133.2 2.5 %last_output.3 = (f32[384,1152]{1,0:T(8,128)S(1)}, f32[1,768]{1,0:T(1,128)S(1)}) custom-call(s32[2]{0:T(128)S(1)} %pad_add_fusion.at_ref, f32[384,1152]{1,0:T(8,128)S(1)} %first_output.3.part_ref, bf16[3,256,1152]{2,1,0:T(8,128)(2,1)S(1)} %lay.1.after_ref.o_ref, bf16[384,256]{1,0:T(8,128)(2,1)S(1)} %collective-permute-done.25.rest_0_, ...), custom_call_target="tpu_custom_call" | custom-call | tf_op jit(solution)/shard_map/last_output/pallas_call | solution.py:616
  136.0 2.6 %collective-permute-start.28 = (f32[1,768]{1,0:T(1,128)S(1)}, f32[1,768]{1,0:T(1,128)S(1)}, u32[]{:S(2)}, u32[]{:S(2)}) collective-permute-start(f32[1,768]{1,0:T(1,128)S(1)} %get-tuple-element.44.rest_2_), channel_id=1, source_target_pairs={{0,2},{1,3},{2,0},{3,1},{4,6},{5,7},{6,4},{7,5},{8,10},{9,11},{10,... | collective-permute-start | bytes 9224 | tf_op jit(solution)/shard_map/ppermute | solution.py:804
  142.2 3.3 %finish.1 = bf16[768,1152]{1,0:T(8,128)(2,1)} custom-call(bf16[768,1152]{1,0:T(8,128)(2,1)S(1)} %copy-done, f32[1,1152]{1,0:T(1,128)S(1)} %broadcast_in_dim.17.gain_ref, f32[384,1152]{1,0:T(8,128)S(1)} %get-tuple-element.41.rest_0_, f32[384,1152]{1,0:T(8,128)S(1)} %get-tuple-element.43.rest_1_, f32[1,768]{1,0:T(1,128)S(1)} %get-tuple-element.44.rest_2_, ...), custom_call_target="tpu_custom_call" | custom-call | tf_op jit(solution)/shard_map/finish/pallas_call | solution.py:657
  (93 shorter events, 31.0 us)
Async XLA Ops:
  0.0 19.7 %copy-start = (bf16[768,1152]{1,0:T(8,128)(2,1)S(1)}, bf16[768,1152]{1,0:T(8,128)(2,1)}, u32[]{:S(2)}) copy-start(bf16[768,1152]{1,0:T(8,128)(2,1)} %token_ref.1) | copy-start | bytes 5308420
  2.1 17.6 %collective-permute-start.10 = (bf16[128,1152]{1,0:T(8,128)(2,1)}, bf16[128,1152]{1,0:T(8,128)(2,1)S(1)}, u32[]{:S(2)}, u32[]{:S(2)}) collective-permute-start(bf16[128,1152]{1,0:T(8,128)(2,1)} %get-tuple-element.32), channel_id=1, source_target_pairs={{0,1},{1,0},{2,3},{3,2},{4,5},{5,4},{6,7},{7,6},{8,9},{9,8},{10,11... | collective-permute-start | bytes 884744 | tf_op jit(solution)/shard_map/ppermute | solution.py:705
  3.7 10.9 %collective-permute-start = (bf16[288,256]{1,0:T(8,128)(2,1)}, bf16[288,256]{1,0:T(8,128)(2,1)S(1)}, u32[]{:S(2)}, u32[]{:S(2)}) collective-permute-start(bf16[288,256]{1,0:T(8,128)(2,1)} %get-tuple-element.25), channel_id=1, source_target_pairs={{0,2},{1,3},{2,0},{3,1},{4,6},{5,7},{6,4},{7,5},{8,10},{9,11},{10,... | collective-permute-start | bytes 442376 | tf_op jit(solution)/shard_map/ppermute | solution.py:703
  6.3 13.4 %collective-permute-start.6 = (bf16[288,256]{1,0:T(8,128)(2,1)}, bf16[288,256]{1,0:T(8,128)(2,1)S(1)}, u32[]{:S(2)}, u32[]{:S(2)}) collective-permute-start(bf16[288,256]{1,0:T(8,128)(2,1)} %get-tuple-element.29), channel_id=1, source_target_pairs={{0,2},{1,3},{2,0},{3,1},{4,6},{5,7},{6,4},{7,5},{8,10},{9,11},{10,... | collective-permute-start | bytes 442376 | tf_op jit(solution)/shard_map/ppermute | solution.py:704
  19.8 27.2 %collective-permute-start.11 = (bf16[352,1152]{1,0:T(8,128)(2,1)S(1)}, bf16[352,1152]{1,0:T(8,128)(2,1)}, u32[]{:S(2)}, u32[]{:S(2)}) collective-permute-start(bf16[352,1152]{1,0:T(8,128)(2,1)S(1)} %stage.6), channel_id=1, source_target_pairs={{0,1},{1,0},{2,3},{3,2},{4,5},{5,4},{6,7},{7,6},{8,9},{9,8},{10,11... | collective-permute-start | bytes 2433032 | tf_op jit(solution)/shard_map/ppermute | solution.py:726
  20.3 5.1 %collective-permute-start.5 = (bf16[1,288,256]{2,1,0:T(8,128)(2,1)S(1)}, bf16[1,288,256]{2,1,0:T(8,128)(2,1)S(1)}, u32[]{:S(2)}, u32[]{:S(2)}) collective-permute-start(bf16[1,288,256]{2,1,0:T(8,128)(2,1)S(1)} %bitcast.19), channel_id=1, source_target_pairs={{0,8},{4,12},{8,0},{12,4},{16,24},{20,28},{24,16},{28,20},{1,9},{5... | collective-permute-start | bytes 442376 | tf_op jit(solution)/shard_map/ppermute | solution.py:728
  20.8 5.1 %collective-permute-start.7 = (bf16[1,288,256]{2,1,0:T(8,128)(2,1)S(1)}, bf16[1,288,256]{2,1,0:T(8,128)(2,1)S(1)}, u32[]{:S(2)}, u32[]{:S(2)}) collective-permute-start(bf16[1,288,256]{2,1,0:T(8,128)(2,1)S(1)} %bitcast.23), channel_id=1, source_target_pairs={{0,16},{4,20},{8,24},{12,28},{16,0},{20,4},{24,8},{28,12},{1,17},{... | collective-permute-start | bytes 442376 | tf_op jit(solution)/shard_map/ppermute | solution.py:729
  28.0 18.9 %collective-permute-start.8 = (bf16[2,288,256]{2,1,0:T(8,128)(2,1)}, bf16[2,288,256]{2,1,0:T(8,128)(2,1)}, u32[]{:S(2)}, u32[]{:S(2)}) collective-permute-start(bf16[2,288,256]{2,1,0:T(8,128)(2,1)} %get-tuple-element.30.refs_0_), channel_id=1, source_target_pairs={{0,16},{4,20},{8,24},{12,28},{16,0},{20,4},{24,8},{28,12},{1,17},{... | collective-permute-start | bytes 884744 | tf_op jit(solution)/shard_map/ppermute | solution.py:728
  29.6 17.4 %collective-permute-start.9 = (bf16[2,288,256]{2,1,0:T(8,128)(2,1)}, bf16[2,288,256]{2,1,0:T(8,128)(2,1)}, u32[]{:S(2)}, u32[]{:S(2)}) collective-permute-start(bf16[2,288,256]{2,1,0:T(8,128)(2,1)} %get-tuple-element.31.refs_2_), channel_id=1, source_target_pairs={{0,8},{4,12},{8,0},{12,4},{16,24},{20,28},{24,16},{28,20},{1,9},{5... | collective-permute-start | bytes 884744 | tf_op jit(solution)/shard_map/ppermute | solution.py:729
  33.5 8.3 %collective-permute-start.1 = (bf16[32,1152]{1,0:T(8,128)(2,1)S(1)}, bf16[32,1152]{1,0:T(8,128)(2,1)S(1)}, u32[]{:S(2)}, u32[]{:S(2)}) collective-permute-start(bf16[32,1152]{1,0:T(8,128)(2,1)S(1)} %get-tuple-element.26), channel_id=1, source_target_pairs={{0,1},{1,2},{2,3},{3,0},{4,5},{5,6},{6,7},{7,4},{8,9},{9,10},{10,1... | collective-permute-start | bytes 221192 | tf_op jit(solution)/shard_map/ppermute | solution.py:709
  35.1 6.8 %collective-permute-start.2 = (bf16[32,1152]{1,0:T(8,128)(2,1)S(1)}, bf16[32,1152]{1,0:T(8,128)(2,1)S(1)}, u32[]{:S(2)}, u32[]{:S(2)}) collective-permute-start(bf16[32,1152]{1,0:T(8,128)(2,1)S(1)} %get-tuple-element.27), channel_id=1, source_target_pairs={{0,2},{1,3},{2,0},{3,1},{4,6},{5,7},{6,4},{7,5},{8,10},{9,11},{10,... | collective-permute-start | bytes 221192 | tf_op jit(solution)/shard_map/ppermute | solution.py:709
  41.7 5.2 %collective-permute-start.3 = (bf16[32,1152]{1,0:T(8,128)(2,1)S(1)}, bf16[32,1152]{1,0:T(8,128)(2,1)S(1)}, u32[]{:S(2)}, u32[]{:S(2)}) collective-permute-start(bf16[32,1152]{1,0:T(8,128)(2,1)S(1)} %get-tuple-element.28), channel_id=1, source_target_pairs={{0,3},{1,0},{2,1},{3,2},{4,7},{5,4},{6,5},{7,6},{8,11},{9,8},{10,9... | collective-permute-start | bytes 221192 | tf_op jit(solution)/shard_map/ppermute | solution.py:709
  41.9 15.2 %collective-permute-start.13 = (bf16[288,1152]{1,0:T(8,128)(2,1)}, bf16[288,1152]{1,0:T(8,128)(2,1)}, u32[]{:S(2)}, u32[]{:S(2)}) collective-permute-start(bf16[288,1152]{1,0:T(8,128)(2,1)} %get-tuple-element.34), channel_id=1, source_target_pairs={{0,1},{1,0},{2,3},{3,2},{4,5},{5,4},{6,7},{7,6},{8,9},{9,8},{10,11... | collective-permute-start | bytes 1990664 | tf_op jit(solution)/shard_map/ppermute | solution.py:726
  49.3 7.8 %collective-permute-start.12 = (bf16[4,288,256]{2,1,0:T(8,128)(2,1)}, bf16[4,288,256]{2,1,0:T(8,128)(2,1)}, u32[]{:S(2)}, u32[]{:S(2)}) collective-permute-start(bf16[4,288,256]{2,1,0:T(8,128)(2,1)} %get-tuple-element.33.own_ref), channel_id=1, source_target_pairs={{0,4},{4,0},{8,12},{12,8},{16,20},{20,16},{24,28},{28,24},{1,5},{5... | collective-permute-start | bytes 1769480 | tf_op jit(solution)/shard_map/ppermute | solution.py:728
  49.4 7.7 %collective-permute-start.14 = (bf16[4,288,256]{2,1,0:T(8,128)(2,1)}, bf16[4,288,256]{2,1,0:T(8,128)(2,1)S(1)}, u32[]{:S(2)}, u32[]{:S(2)}) collective-permute-start(bf16[4,288,256]{2,1,0:T(8,128)(2,1)} %get-tuple-element.35.own_ref), channel_id=1, source_target_pairs={{0,4},{4,0},{8,12},{12,8},{16,20},{20,16},{24,28},{28,24},{1,5},{5... | collective-permute-start | bytes 1769480 | tf_op jit(solution)/shard_map/ppermute | solution.py:729
  63.1 17.2 %collective-permute-start.16 = (bf16[784,256]{1,0:T(8,128)(2,1)S(1)}, bf16[784,256]{1,0:T(8,128)(2,1)S(1)}, u32[]{:S(2)}, u32[]{:S(2)}) collective-permute-start(bf16[784,256]{1,0:T(8,128)(2,1)S(1)} %get-tuple-element.37.rest_0_), channel_id=1, source_target_pairs={{0,2},{1,3},{2,0},{3,1},{4,6},{5,7},{6,4},{7,5},{8,10},{9,11},{10,... | collective-permute-start | bytes 1204232 | tf_op jit(solution)/shard_map/ppermute | solution.py:750
  65.0 12.8 %collective-permute-start.4 = (bf16[1,3,32,1152]{3,2,1,0:T(8,128)(2,1)S(1)}, bf16[1,3,32,1152]{3,2,1,0:T(8,128)(2,1)S(1)}, u32[]{:S(2)}, u32[]{:S(2)}) collective-permute-start(bf16[1,3,32,1152]{3,2,1,0:T(8,128)(2,1)S(1)} %maximum_bitcast_fusion.refs_0_), channel_id=1, source_target_pairs={{0,8},{4,12},{8,0},{12,4},{16,24},{20,28},{24,16},{28,20},{1,9},{5... | collective-permute-start | bytes 663560 | tf_op jit(solution)/shard_map/ppermute | solution.py:739
  78.4 8.5 %collective-permute-start.15 = (bf16[2,3,32,1152]{3,2,1,0:T(8,128)(2,1)S(1)}, bf16[2,3,32,1152]{3,2,1,0:T(8,128)(2,1)}, u32[]{:S(2)}, u32[]{:S(2)}) collective-permute-start(bf16[2,3,32,1152]{3,2,1,0:T(8,128)(2,1)S(1)} %stage.8.rest_1_.refs_0_), channel_id=1, source_target_pairs={{0,16},{4,20},{8,24},{12,28},{16,0},{20,4},{24,8},{28,12},{1,17},{... | collective-permute-start | bytes 1327112 | tf_op jit(solution)/shard_map/ppermute | solution.py:739
  81.9 17.9 %collective-permute-start.18 = (bf16[768,256]{1,0:T(8,128)(2,1)S(1)}, bf16[768,256]{1,0:T(8,128)(2,1)}, u32[]{:S(2)}, u32[]{:S(2)}) collective-permute-start(bf16[768,256]{1,0:T(8,128)(2,1)S(1)} %gate.2), channel_id=1, source_target_pairs={{0,2},{1,3},{2,0},{3,1},{4,6},{5,7},{6,4},{7,5},{8,10},{9,11},{10,... | collective-permute-start | bytes 1179656 | tf_op jit(solution)/shard_map/ppermute | solution.py:759
  82.7 17.1 %copy-start.2 = (f32[768,512]{1,0:T(8,128)S(1)}, f32[768,512]{1,0:T(8,128)}, u32[]{:S(2)}) copy-start(f32[768,512]{1,0:T(8,128)} %copy-done.1) | copy-start | bytes 4718596
  82.7 18.6 %collective-permute-start.19 = (bf16[784,256]{1,0:T(8,128)(2,1)}, bf16[784,256]{1,0:T(8,128)(2,1)S(1)}, u32[]{:S(2)}, u32[]{:S(2)}) collective-permute-start(bf16[784,256]{1,0:T(8,128)(2,1)} %copy-done.6), channel_id=1, source_target_pairs={{0,8},{4,12},{1,9},{5,13},{2,10},{6,14},{3,11},{7,15},{16,24},{20,... | collective-permute-start | bytes 1204232 | tf_op jit(solution)/shard_map/ppermute | solution.py:773
  84.2 17.2 %collective-permute-start.20 = (bf16[784,256]{1,0:T(8,128)(2,1)}, bf16[784,256]{1,0:T(8,128)(2,1)S(1)}, u32[]{:S(2)}, u32[]{:S(2)}) collective-permute-start(bf16[784,256]{1,0:T(8,128)(2,1)} %copy-done.6), channel_id=1, source_target_pairs={{0,4},{4,8},{8,12},{1,5},{5,9},{9,13},{2,6},{6,10},{10,14},{3,7},{... | collective-permute-start | bytes 1204232 | tf_op jit(solution)/shard_map/ppermute | solution.py:773
  89.2 17.7 %collective-permute-start.17 = (bf16[4,3,32,1152]{3,2,1,0:T(8,128)(2,1)S(1)}, bf16[4,3,32,1152]{3,2,1,0:T(8,128)(2,1)S(1)}, u32[]{:S(2)}, u32[]{:S(2)}) collective-permute-start(bf16[4,3,32,1152]{3,2,1,0:T(8,128)(2,1)S(1)} %stage.9.own_ref), channel_id=1, source_target_pairs={{0,4},{4,0},{8,12},{12,8},{16,20},{20,16},{24,28},{28,24},{1,5},{5... | collective-permute-start | bytes 2654216 | tf_op jit(solution)/shard_map/ppermute | solution.py:739
  104.5 11.7 %collective-permute-start.22 = (bf16[384,256]{1,0:T(8,128)(2,1)S(1)}, bf16[384,256]{1,0:T(8,128)(2,1)S(1)}, u32[]{:S(2)}, u32[]{:S(2)}) collective-permute-start(bf16[384,256]{1,0:T(8,128)(2,1)S(1)} %attend.2.rest_0_), channel_id=1, source_target_pairs={{0,2},{1,3},{2,0},{3,1},{4,6},{5,7},{6,4},{7,5},{8,10},{9,11},{10,... | collective-permute-start | bytes 589832 | tf_op jit(solution)/shard_map/ppermute | solution.py:785
  104.6 16.1 %collective-permute-start.21 = (bf16[384,256]{1,0:T(8,128)(2,1)S(1)}, bf16[384,256]{1,0:T(8,128)(2,1)S(1)}, u32[]{:S(2)}, u32[]{:S(2)}) collective-permute-start(bf16[384,256]{1,0:T(8,128)(2,1)S(1)} %attend.2.rest_0_), channel_id=1, source_target_pairs={{0,1},{1,0},{2,3},{3,2},{4,5},{5,4},{6,7},{7,6},{8,9},{9,8},{10,11... | collective-permute-start | bytes 589832 | tf_op jit(solution)/shard_map/ppermute | solution.py:786
  112.0 13.2 %collective-permute-start.24 = (bf16[384,256]{1,0:T(8,128)(2,1)S(1)}, bf16[384,256]{1,0:T(8,128)(2,1)S(1)}, u32[]{:S(2)}, u32[]{:S(2)}) collective-permute-start(bf16[384,256]{1,0:T(8,128)(2,1)S(1)} %attend.3.rest_2_.after_ref.rest_0_), channel_id=1, source_target_pairs={{0,1},{1,0},{2,3},{3,2},{4,5},{5,4},{6,7},{7,6},{8,9},{9,8},{10,11... | collective-permute-start | bytes 589832 | tf_op jit(solution)/shard_map/ppermute | solution.py:786
  112.1 11.9 %collective-permute-start.25 = (bf16[384,256]{1,0:T(8,128)(2,1)S(1)}, bf16[384,256]{1,0:T(8,128)(2,1)S(1)}, u32[]{:S(2)}, u32[]{:S(2)}) collective-permute-start(bf16[384,256]{1,0:T(8,128)(2,1)S(1)} %attend.3.rest_2_.after_ref.rest_0_), channel_id=1, source_target_pairs={{0,2},{1,3},{2,0},{3,1},{4,6},{5,7},{6,4},{7,5},{8,10},{9,11},{10,... | collective-permute-start | bytes 589832 | tf_op jit(solution)/shard_map/ppermute | solution.py:785
  116.2 12.9 %collective-permute-start.23 = (bf16[384,256]{1,0:T(8,128)(2,1)S(1)}, bf16[384,256]{1,0:T(8,128)(2,1)S(1)}, u32[]{:S(2)}, u32[]{:S(2)}) collective-permute-start(bf16[384,256]{1,0:T(8,128)(2,1)S(1)} %gate.3.rest_0_), channel_id=1, source_target_pairs={{0,1},{1,0},{2,3},{3,2},{4,5},{5,4},{6,7},{7,6},{8,9},{9,8},{10,11... | collective-permute-start | bytes 589832 | tf_op jit(solution)/shard_map/ppermute | solution.py:789
  124.0 9.3 %collective-permute-start.26 = (bf16[384,256]{1,0:T(8,128)(2,1)S(1)}, bf16[384,256]{1,0:T(8,128)(2,1)S(1)}, u32[]{:S(2)}, u32[]{:S(2)}) collective-permute-start(bf16[384,256]{1,0:T(8,128)(2,1)S(1)} %collective-permute-done.25.rest_0_), channel_id=1, source_target_pairs={{0,1},{1,0},{2,3},{3,2},{4,5},{5,4},{6,7},{7,6},{8,9},{9,8},{10,11... | collective-permute-start | bytes 589832 | tf_op jit(solution)/shard_map/ppermute | solution.py:789
  135.8 5.4 %collective-permute-start.27 = (f32[1,768]{1,0:T(1,128)S(1)}, f32[1,768]{1,0:T(1,128)S(1)}, u32[]{:S(2)}, u32[]{:S(2)}) collective-permute-start(f32[1,768]{1,0:T(1,128)S(1)} %get-tuple-element.44.rest_2_), channel_id=1, source_target_pairs={{0,1},{1,2},{2,3},{3,0},{4,5},{5,6},{6,7},{7,4},{8,9},{9,10},{10,1... | collective-permute-start | bytes 9224 | tf_op jit(solution)/shard_map/ppermute | solution.py:804
  136.0 5.2 %collective-permute-start.28 = (f32[1,768]{1,0:T(1,128)S(1)}, f32[1,768]{1,0:T(1,128)S(1)}, u32[]{:S(2)}, u32[]{:S(2)}) collective-permute-start(f32[1,768]{1,0:T(1,128)S(1)} %get-tuple-element.44.rest_2_), channel_id=1, source_target_pairs={{0,2},{1,3},{2,0},{3,1},{4,6},{5,7},{6,4},{7,5},{8,10},{9,11},{10,... | collective-permute-start | bytes 9224 | tf_op jit(solution)/shard_map/ppermute | solution.py:804
  138.6 3.6 %collective-permute-start.29 = (f32[1,768]{1,0:T(1,128)S(1)}, f32[1,768]{1,0:T(1,128)S(1)}, u32[]{:S(2)}, u32[]{:S(2)}) collective-permute-start(f32[1,768]{1,0:T(1,128)S(1)} %get-tuple-element.44.rest_2_), channel_id=1, source_target_pairs={{0,3},{1,0},{2,1},{3,2},{4,7},{5,4},{6,5},{7,6},{8,11},{9,8},{10,9... | collective-permute-start | bytes 9224 | tf_op jit(solution)/shard_map/ppermute | solution.py:804
  (13 other events, 67.4 us)

commit v15 on v13

--- a/solution.py
+++ b/solution.py
@@ -16,7 +16,7 @@
 rope_base = 10000.0
 NEG = -1e30
 Q_TILE = 128
-K_TILE = 256
+K_TILE = 384
 CHUNKS = 2
 LANES = 128
 TAIL = 16
@@ -214,44 +214,91 @@
     return copies
 
 
-def far_sum(src_ref, x_ref, weight):
+def far_sum(src_ref, first, x_ref, weight):
     count, _, cols = x_ref.shape
     total = None
     for k in range(count):
-        row = pl.multiple_of(src_ref[k] * cols, TAIL)
+        row = pl.multiple_of(src_ref[first + k] * cols, TAIL)
         term = jnp.dot(x_ref[k], weight[pl.ds(row, cols), :], preferred_element_type=F32)
         total = term if total is None else total + term
     return total
 
 
-def far_kv_kernel(place_ref, src_ref, gain_ref, own_ref, got_ref, *rest, order, cuts):
+def prepare(x_refs, gain, x_out, k):
+    column, row = [], 0
+    for x_ref in x_refs:
+        x = x_ref[...].astype(F32)
+        column.append(jnp.sum(x * x, axis=1, keepdims=True))
+        x_out[k, row : row + x.shape[0]] = (x * gain).astype(BF16)
+        row += x.shape[0]
+    return jnp.concatenate(column, axis=0)
+
+
+def far_own_kernel(
+    place_ref, src_ref, gain_ref, own_ref, got_ref, x_ref, x_out, sq_ref, out_ref, weight, sems,
+    *, order
+):
+    copies = place_weights(place_ref, own_ref, got_ref, weight, sems, order)
+    gain = gain_ref[place_ref[1] + src_ref[0]]
+    sq_ref[...] = to_row(prepare([x_ref], gain, x_out, 0))
+    for copy in copies:
+        copy.wait()
+    out_ref[...] = far_sum(src_ref, 0, x_out, weight)
+
+
+def far_kv_kernel(
+    place_ref, src_ref, gain_ref, part_ref, own_sq_ref, own_ref, got_ref, *rest, order, cuts
+):
     x_refs, (out_ref, x_out, sq_ref, weight, sems) = rest[: sum(cuts)], rest[-5:]
     copies = place_weights(place_ref, own_ref, got_ref, weight, sems, order)
     rows = x_out.shape[1]
     columns, at = [], 0
     for k, pieces in enumerate(cuts):
-        gain = gain_ref[place_ref[1] + src_ref[k]]
-        column, row = [], 0
-        for x_ref in x_refs[at : at + pieces]:
-            x = x_ref[...].astype(F32)
-            column.append(jnp.sum(x * x, axis=1, keepdims=True))
-            x_out[k, row : row + x.shape[0]] = (x * gain).astype(BF16)
-            row += x.shape[0]
-        columns.append(jnp.concatenate(column, axis=0))
+        gain = gain_ref[place_ref[1] + src_ref[1 + k]]
+        columns.append(prepare(x_refs[at : at + pieces], gain, x_out, k))
         at += pieces
-    sq = to_row(sum(columns[1:], columns[0]))
+    sq = to_row(sum(columns[1:], columns[0])) + own_sq_ref[...]
     sq_ref[...] = sq
     for copy in copies:
         copy.wait()
-    out_ref[:rows, :] = far_sum(src_ref, x_out, weight).astype(BF16)
+    total = part_ref[...] + far_sum(src_ref, 1, x_out, weight)
+    out_ref[:rows, :] = total.astype(BF16)
     high = sq.astype(BF16).astype(F32)
     out_ref[rows:, :] = lines_of((high, sq - high), out_ref.shape[1])
 
 
-def far_kv_product(place, sources, gains, blocks, gathered, after):
+def far_kv_scratch(gathered):
+    order, own, _ = gathered
+    return [
+        pltpu.VMEM((len(order) * own.shape[1], own.shape[2]), BF16),
+        pltpu.SemaphoreType.DMA((len(order),)),
+    ]
+
+
+def far_own_product(place, sources, gains, tokens, gathered):
     order, own, got = gathered
-    _, share, width = own.shape
-    rows, cols = blocks[0][0].shape
+    rows, cols = tokens.shape
+    dims = [(1, rows, cols), (1, rows), (rows, own.shape[2])]
+    whole = lambda d: pl.BlockSpec(d, lambda i, p, s: (0,) * len(d))
+    return pl.pallas_call(
+        partial(far_own_kernel, order=order),
+        out_shape=tuple(shape(d, t) for d, t in zip(dims, (BF16, F32, F32))),
+        grid_spec=pltpu.PrefetchScalarGridSpec(
+            num_scalar_prefetch=2,
+            grid=(1,),
+            in_specs=[whole(gains.shape), ANY, ANY, whole(tokens.shape)],
+            out_specs=[whole(d) for d in dims],
+            scratch_shapes=far_kv_scratch(gathered),
+        ),
+        compiler_params=PARAMS,
+        name="far_own",
+    )(place, sources, gains, own, got, tokens)
+
+
+def far_kv_product(place, sources, gains, part, own_sq, blocks, gathered, after):
+    order, own, got = gathered
+    rows, width = part.shape
+    cols = blocks[0][0].shape[1]
     pieces = [piece for block in blocks for piece in block]
     dims = [(rows + TAIL, width), (len(blocks), rows, cols), (1, rows)]
     whole = lambda d: pl.BlockSpec(d, lambda i, p, s: (0,) * len(d))
@@ -261,25 +308,23 @@
         grid_spec=pltpu.PrefetchScalarGridSpec(
             num_scalar_prefetch=2,
             grid=(1,),
-            in_specs=[whole(gains.shape), ANY, ANY]
+            in_specs=[whole(gains.shape), whole(part.shape), whole(own_sq.shape), ANY, ANY]
             + [whole(piece.shape) for piece in pieces]
             + [ANY for _ in after],
             out_specs=[whole(d) for d in dims],
-            scratch_shapes=[
-                pltpu.VMEM((len(order) * share, width), BF16),
-                pltpu.SemaphoreType.DMA((len(order),)),
-            ],
+            scratch_shapes=far_kv_scratch(gathered),
         ),
         compiler_params=PARAMS,
         name="far_kv",
-    )(place, sources, gains, own, got, *pieces, *after)
-
-
-def far_kernel(place_ref, src_ref, x_ref, own_ref, got_ref, *rest, order):
+    )(place, sources, gains, part, own_sq, own, got, *pieces, *after)
+
+
+def far_kernel(place_ref, src_ref, own_x_ref, x_ref, own_ref, got_ref, *rest, order):
     out_ref, weight, sems = rest[-3:]
     for copy in place_weights(place_ref, own_ref, got_ref, weight, sems, order):
         copy.wait()
-    out_ref[...] = far_sum(src_ref, x_ref, weight).astype(BF16)
+    total = far_sum(src_ref, 0, own_x_ref, weight) + far_sum(src_ref, 1, x_ref, weight)
+    out_ref[...] = total.astype(BF16)
 
 
 def lines_of(rows, width):
@@ -304,61 +349,69 @@
     return rows
 
 
-def far_product(place, sources, x, gathered, after):
+def far_product(place, sources, own_x, x, gathered, after):
     order, own, got = gathered
-    _, share, width = own.shape
-    rows = x.shape[1]
+    rows, width = x.shape[1], own.shape[2]
     return pl.pallas_call(
         partial(far_kernel, order=order),
         out_shape=shape((rows, width), BF16),
         grid_spec=pltpu.PrefetchScalarGridSpec(
             num_scalar_prefetch=2,
             grid=(1,),
-            in_specs=[pl.BlockSpec(x.shape, lambda i, p, s: (0, 0, 0)), ANY, ANY]
+            in_specs=[
+                pl.BlockSpec(own_x.shape, lambda i, p, s: (0, 0, 0)),
+                pl.BlockSpec(x.shape, lambda i, p, s: (0, 0, 0)),
+                ANY,
+                ANY,
+            ]
             + [ANY for _ in after],
             out_specs=pl.BlockSpec((rows, width), lambda i, p, s: (0, 0)),
-            scratch_shapes=[
-                pltpu.VMEM((len(order) * share, width), BF16),
-                pltpu.SemaphoreType.DMA((len(order),)),
-            ],
+            scratch_shapes=far_kv_scratch(gathered),
         ),
         compiler_params=PARAMS,
         name="far",
-    )(place, sources, x, own, got, *after)
-
-
-def near_kernel(src_ref, x_ref, k_ref, v_ref, q_ref, *rest):
+    )(place, sources, own_x, x, own, got, *after)
+
+
+def near_kernel(src_ref, own_x_ref, x_ref, k_ref, v_ref, q_ref, *rest):
     out_ref = rest[-1]
-    x = x_ref[0]
-
-    @pl.when(pl.program_id(0) == 0)
-    def _():
-        out_ref[...] = jnp.zeros_like(out_ref)
-
+    step = pl.program_id(0)
+    dot = partial(jnp.dot, preferred_element_type=F32)
     column = 0
     for ref in (k_ref, v_ref, q_ref):
         at = slice(column, column + ref.shape[1])
-        out_ref[:, at] += jnp.dot(x, ref[...], preferred_element_type=F32)
+
+        @pl.when(step == 0)
+        def _():
+            out_ref[:, at] = dot(own_x_ref[0], ref[...])
+
+        @pl.when(step > 0)
+        def _():
+            out_ref[:, at] += dot(x_ref[0], ref[...])
+
         column += ref.shape[1]
 
 
-def near_product(sources, x, weights, after):
-    count, chunk, cols = x.shape
+def near_product(sources, own_x, x, weights, after):
+    count, rows, cols = x.shape
     widths = [w.shape[1] for w in weights]
     return pl.pallas_call(
         near_kernel,
-        out_shape=shape((chunk, sum(widths)), F32),
+        out_shape=shape((rows, sum(widths)), F32),
         grid_spec=pltpu.PrefetchScalarGridSpec(
             num_scalar_prefetch=1,
-            grid=(count,),
-            in_specs=[pl.BlockSpec((1, chunk, cols), lambda i, s: (i, 0, 0))]
+            grid=(count + 1,),
+            in_specs=[
+                pl.BlockSpec((1, rows, cols), lambda i, s: (0, 0, 0)),
+                pl.BlockSpec((1, rows, cols), lambda i, s: (jnp.maximum(i - 1, 0), 0, 0)),
+            ]
             + [pl.BlockSpec((cols, w), lambda i, s: (s[i], 0)) for w in widths]
             + [ANY for _ in after],
-            out_specs=pl.BlockSpec((chunk, sum(widths)), lambda i, s: (0, 0)),
+            out_specs=pl.BlockSpec((rows, sum(widths)), lambda i, s: (0, 0)),
         ),
         compiler_params=PARAMS,
         name="near",
-    )(sources, x, *weights, *after)
+    )(sources, own_x, x, *weights, *after)
 
 
 def keys_kernel(near_ref, far_ref, sq_ref, id_ref, cos_ref, sin_ref, *rest, model):
@@ -733,13 +786,15 @@
         return own, lax.ppermute(own, PLANE, [(i, i ^ masks_kv[step]) for i in range(plane)])
 
     sources = (within + half - jnp.arange(half, dtype=jnp.int32)) % half
-    blocks = [[tokens], received]
-    for _ in range(half - 2):
-        blocks.append([lax.ppermute(part, "tensor", ring) for part in blocks[-1]])
     gains = in_gain.reshape(nz, 1, cols)
     place = jnp.stack([in_plane, side * half])
+    own_x, own_sq, part = far_own_product(place, sources, gains, tokens, far_kv)
+    received[-1] = gate(received[-1], own_sq)
+    blocks = [received]
+    for _ in range(half - 2):
+        blocks.append([lax.ppermute(block, "tensor", ring) for block in blocks[-1]])
     sent_kv, x, sq = far_kv_product(
-        place, sources, gains, blocks, far_kv, [far_q[2]]
+        place, sources, gains, part, own_sq, blocks, far_kv, [far_q[2]]
     )
     got_kv = lax.ppermute(sent_kv, "tensor", swap)
     pair_o = double(own_o, 0, [])
@@ -747,9 +802,9 @@
         pair_o = double(pair_o, step, [])
     weights = (k_weight, value_weight, q_weight)
 
-    near = near_product(side * half + sources, x, weights, [sent_kv])
-
-    sent_q = far_product(place, sources, x, far_q, [near])
+    near = near_product(side * half + sources, own_x, x, weights, [sent_kv])
+
+    sent_q = far_product(place, sources, own_x, x, far_q, [near])
     got_q = lax.ppermute(gate(sent_q, got_kv), "tensor", swap)
     pair_o = double(pair_o, last - 1, [sent_q])
     cosine, sine = rotation_table(seq * rows + jnp.arange(rows, dtype=jnp.int32))

time: 147 us -> 148 us (level); the launches traced: 147 us -> 146 us
  waiting for transfers between devices: 49.2 us -> 54.5 us
  Pallas kernels: 55.3 us -> 52.7 us
  local copies, waits for them, and re-layouts: 3.9 us -> 1.77 us
  starting transfers between devices: 36 us -> 34.1 us
    ppermute x2, waiting for transfers between devices: 7.07 us -> 1.57 us  [per_device(): received.append(lax.ppermute(outs[-1], 'tensor', ring))]
    pallas_call x2, Pallas kernels: 11.5 us -> 7.01 us  [attend(): pl.pallas_call(partial(attention_kernel, back=back, offset=c * rows), out...]
    pallas_call x1 -> x2, Pallas kernels: 5.72 us -> 9.19 us  [the longest x1 6.14 us: near_product(): pl.pallas_call(near_kernel, out_shape=shape((rows, sum(widths)), F32), gr...]
    ppermute x1, waiting for transfers between devices: 10.6 us -> 13.6 us  [per_device(): got_q = lax.ppermute(gate(sent_q, got_kv), 'tensor', swap)]
    ppermute x2, waiting for transfers between devices: 0.01 us -> 2.64 us  [per_device(): across = lax.ppermute(opposite, 'tensor', pairs)]
    pallas_call x1, Pallas kernels: 6.03 us -> 3.69 us  [far_kv_product(): pl.pallas_call(partial(far_kv_kernel, order=order, cuts=[len(block) for b...]
    unnamed x30 -> x34, local copies, waits for them, and re-layouts: 3.87 us -> 1.74 us
    ppermute x2, waiting for transfers between devices: 0.01 us -> 1.93 us  [per_device(): beside = lax.ppermute(context, 'tensor', pairs)]
  transfers between devices with their start and end apart: 30 -> 30, of which waited for: 12 -> 18; matrix products, arithmetic and copies ran while one was open for 1% -> 1% of each run, Pallas kernels for 28% -> 28%
where the time goes in v15:
time: 148 us; the launch traced here: 146 us
  waiting for transfers between devices  54.5 us (37%)
  Pallas kernels  52.7 us (36%)
  starting transfers between devices  34.1 us (23%)
  other arithmetic  2.08 us (1%)
  local copies, waits for them, and re-layouts  1.77 us (1%)
    ppermute x1, waiting for transfers between devices, per_device(): got_q = lax.ppermute(gate(sent_q, got_kv), 'tensor', swap)  13.6 us
    ppermute x3, waiting for transfers between devices, per_device(): lax.ppermute(p, 'tensor', turn(k + 1))  8.87 us
    ppermute x1, waiting for transfers between devices, per_device(): own_kv = lax.ppermute(packed_kv, 'tensor', swap)[None]  8.01 us
    pallas_call x5, Pallas kernels, stage(): pl.pallas_call(partial(stage_kernel, pairs=len(joined), first=first, coun...  7.53 us
    pallas_call x2, Pallas kernels, attend(): pl.pallas_call(partial(attention_kernel, back=back, offset=c * rows), out...  7.01 us
    pallas_call x2, Pallas kernels, first_output(): pl.pallas_call(first_output_kernel, out_shape=shape((chunk, cols), F32),...  6.48 us
    pallas_call x1, Pallas kernels, near_product(): pl.pallas_call(near_kernel, out_shape=shape((rows, sum(widths)), F32), gr...  6.14 us
    pallas_call x2, Pallas kernels, last_output(): pl.pallas_call(last_output_kernel, out_shape=(shape((chunk, cols), F32),...  5.06 us
  transfers between devices with their start and end apart: 30, of which 18 were waited for; matrix products, arithmetic and copies ran while one was open for 1% of the time, Pallas kernels for 28%

profile of v15, /device:TPU:2, one launch (start us, length us, event | category | flops | bytes accessed | tf_op | source)
XLA Modules:
  0.0 145.6 jit_solution(4648633059732307832)
XLA Ops:
  0.0 2.1 %pack.1 = (bf16[288,256]{1,0:T(8,128)(2,1)}, bf16[288,256]{1,0:T(8,128)(2,1)}, bf16[128,1152]{1,0:T(8,128)(2,1)}) custom-call(s32[1]{0:T(128)} %bitcast.9.at_ref, bf16[4608,256]{1,0:T(8,128)(2,1)} %q_ref.3, bf16[4608,128]{1,0:T(8,128)(2,1)} %k_ref.3, bf16[4608,128]{1,0:T(8,128)(2,1)} %v_ref.3, bf16[768,1152]{1,0:T(8,128)(2,1)} %token_ref.1), custom_call_target="tpu_custom_call" | custom-call | tf_op jit(solution)/shard_map/pack/pallas_call | solution.py:75
  3.7 2.6 %collective-permute-start = (bf16[288,256]{1,0:T(8,128)(2,1)}, bf16[288,256]{1,0:T(8,128)(2,1)S(1)}, u32[]{:S(2)}, u32[]{:S(2)}) collective-permute-start(bf16[288,256]{1,0:T(8,128)(2,1)} %get-tuple-element.28), channel_id=1, source_target_pairs={{0,2},{1,3},{2,0},{3,1},{4,6},{5,7},{6,4},{7,5},{8,10},{9,11},{10,... | collective-permute-start | bytes 442376 | tf_op jit(solution)/shard_map/ppermute | solution.py:750
  6.7 8.0 %collective-permute-done = bf16[288,256]{1,0:T(8,128)(2,1)S(1)} collective-permute-done((bf16[288,256]{1,0:T(8,128)(2,1)}, bf16[288,256]{1,0:T(8,128)(2,1)S(1)}, u32[]{:S(2)}, u32[]{:S(2)}) %collective-permute-start) | collective-permute-done | bytes 147488 | tf_op jit(solution)/shard_map/ppermute | solution.py:750
  14.7 5.0 %collective-permute-done.6 = bf16[288,256]{1,0:T(8,128)(2,1)S(1)} collective-permute-done((bf16[288,256]{1,0:T(8,128)(2,1)}, bf16[288,256]{1,0:T(8,128)(2,1)S(1)}, u32[]{:S(2)}, u32[]{:S(2)}) %collective-permute-start.6) | collective-permute-done | bytes 147488 | tf_op jit(solution)/shard_map/ppermute | solution.py:751
  23.2 3.1 %collective-permute-done.5.refs_1_ = bf16[1,288,256]{2,1,0:T(8,128)(2,1)S(1)} collective-permute-done((bf16[1,288,256]{2,1,0:T(8,128)(2,1)S(1)}, bf16[1,288,256]{2,1,0:T(8,128)(2,1)S(1)}, u32[]{:S(2)}, u32[]{:S(2)}) %collective-permute-start.5) | collective-permute-done | bytes 147488 | tf_op jit(solution)/shard_map/ppermute | solution.py:775
  26.9 2.0 %stage.5 = (bf16[2,288,256]{2,1,0:T(8,128)(2,1)}, bf16[2,288,256]{2,1,0:T(8,128)(2,1)}, bf16[288,1152]{1,0:T(8,128)(2,1)}) custom-call(bf16[1,288,256]{2,1,0:T(8,128)(2,1)S(1)} %bitcast.20, bf16[1,288,256]{2,1,0:T(8,128)(2,1)S(1)} %collective-permute-done.5.refs_1_, bf16[1,288,256]{2,1,0:T(8,128)(2,1)S(1)} %bitcast.24, ...), custom_call_target="tpu_custom_call" | custom-call | tf_op jit(solution)/shard_map/stage/pallas_call | solution.py:130
  32.1 1.7 %copy-done.5 = bf16[256,4608]{1,0:T(8,128)(2,1)S(1)} copy-done((bf16[256,4608]{1,0:T(8,128)(2,1)S(1)}, bf16[256,4608]{1,0:T(8,128)(2,1)}, u32[]{:S(2)}) %copy-start.5) | copy-done | bytes 2359320
  37.2 5.7 %collective-permute-done.1.refs_6_ = bf16[32,1152]{1,0:T(8,128)(2,1)S(1)} collective-permute-done((bf16[32,1152]{1,0:T(8,128)(2,1)S(1)}, bf16[32,1152]{1,0:T(8,128)(2,1)S(1)}, u32[]{:S(2)}, u32[]{:S(2)}) %collective-permute-start.1) | collective-permute-done | bytes 73760 | tf_op jit(solution)/shard_map/ppermute | solution.py:756
  42.9 2.0 %collective-permute-start.13 = (bf16[288,1152]{1,0:T(8,128)(2,1)}, bf16[288,1152]{1,0:T(8,128)(2,1)S(1)}, u32[]{:S(2)}, u32[]{:S(2)}) collective-permute-start(bf16[288,1152]{1,0:T(8,128)(2,1)} %get-tuple-element.40), channel_id=1, source_target_pairs={{0,1},{1,0},{2,3},{3,2},{4,5},{5,4},{6,7},{7,6},{8,9},{9,8},{10,11... | collective-permute-start | bytes 1990664 | tf_op jit(solution)/shard_map/ppermute | solution.py:773
  45.0 3.2 %collective-permute-done.3.refs_8_ = bf16[32,1152]{1,0:T(8,128)(2,1)S(1)} collective-permute-done((bf16[32,1152]{1,0:T(8,128)(2,1)S(1)}, bf16[32,1152]{1,0:T(8,128)(2,1)S(1)}, u32[]{:S(2)}, u32[]{:S(2)}) %collective-permute-start.3) | collective-permute-done | bytes 73760 | tf_op jit(solution)/shard_map/ppermute | solution.py:756
  48.2 2.6 %stage.7 = (bf16[4,288,256]{2,1,0:T(8,128)(2,1)}, bf16[4,288,256]{2,1,0:T(8,128)(2,1)}) custom-call(bf16[2,288,256]{2,1,0:T(8,128)(2,1)} %get-tuple-element.33.refs_0_, bf16[2,288,256]{2,1,0:T(8,128)(2,1)} %collective-permute-done.8.refs_1_, bf16[2,288,256]{2,1,0:T(8,128)(2,1)} %get-tuple-element.34.refs_2_, ...), custom_call_target="tpu_custom_call" | custom-call | flops 49999998976 | bytes 100000000 | tf_op jit(solution)/shard_map/stage/pallas_call | solution.py:130
  51.5 1.7 %collective-permute-done.12.got_ref = bf16[4,288,256]{2,1,0:T(8,128)(2,1)} collective-permute-done((bf16[4,288,256]{2,1,0:T(8,128)(2,1)}, bf16[4,288,256]{2,1,0:T(8,128)(2,1)}, u32[]{:S(2)}, u32[]{:S(2)}) %collective-permute-start.12) | collective-permute-done | bytes 589856 | tf_op jit(solution)/shard_map/ppermute | solution.py:775
  53.3 3.0 %far_own.1 = (bf16[1,768,1152]{2,1,0:T(8,128)(2,1)S(1)}, f32[1,768]{1,0:T(1,128)S(1)}, f32[768,256]{1,0:T(8,128)S(1)}) custom-call(s32[2]{0:T(128)S(1)} %get-tuple-element.55.place_ref, s32[2]{0:T(128)S(1)} %get-tuple-element.54.src_ref, f32[4,1,1152]{2,1,0:T(1,128)S(1)} %reshape.21.gain_ref, bf16[4,288,256]{2,1,0:T(8,128)(2,1)} %get-tuple-element.36.own_ref, ...), custom_call_target="tpu_custom_call" | custom-call | tf_op jit(solution)/shard_map/far_own/pallas_call | solution.py:283
  57.9 3.7 %far_kv.1 = (bf16[784,256]{1,0:T(8,128)(2,1)S(1)}, bf16[1,768,1152]{2,1,0:T(8,128)(2,1)}, f32[1,768]{1,0:T(1,128)S(1)}) custom-call(s32[2]{0:T(128)S(1)} %get-tuple-element.55.place_ref, s32[2]{0:T(128)S(1)} %get-tuple-element.54.src_ref, f32[4,1,1152]{2,1,0:T(1,128)S(1)} %reshape.21.gain_ref, f32[768,256]{1,0:T(8,128)S(1)} %get-tuple-element.38.part_ref, ...), custom_call_target="tpu_custom_call" | custom-call | tf_op jit(solution)/shard_map/far_kv/pallas_call | solution.py:305
  61.6 2.0 %collective-permute-start.16 = (bf16[784,256]{1,0:T(8,128)(2,1)S(1)}, bf16[784,256]{1,0:T(8,128)(2,1)S(1)}, u32[]{:S(2)}, u32[]{:S(2)}) collective-permute-start(bf16[784,256]{1,0:T(8,128)(2,1)S(1)} %get-tuple-element.43.rest_0_), channel_id=1, source_target_pairs={{0,2},{1,3},{2,0},{3,1},{4,6},{5,7},{6,4},{7,5},{8,10},{9,11},{10,... | collective-permute-start | bytes 1204232 | tf_op jit(solution)/shard_map/ppermute | solution.py:799
  65.8 6.1 %near.1.rest_0_.near_ref = f32[768,512]{1,0:T(8,128)S(1)} custom-call(s32[2]{0:T(128)S(1)} %broadcast_add_fusion.src_ref, bf16[1,768,1152]{2,1,0:T(8,128)(2,1)S(1)} %get-tuple-element.37.own_x_ref, bf16[1,768,1152]{2,1,0:T(8,128)(2,1)} %get-tuple-element.42.x_ref, bf16[4608,128]{1,0:T(8,128)(2,1)S(1)} %copy-done.3, bf16[4608,128]{1,0:T(8,128)(2,1)S(1)} %copy-done.4, ...), custom_call_target="tpu_custom_call" | custom-call | tf_op jit(solution)/shard_map/near/pallas_call | solution.py:398
  71.9 4.4 %far.1.refs_3_.rest_0_.x_ref = bf16[768,256]{1,0:T(8,128)(2,1)S(1)} custom-call(s32[2]{0:T(128)S(1)} %get-tuple-element.55.place_ref, s32[2]{0:T(128)S(1)} %get-tuple-element.54.src_ref, bf16[1,768,1152]{2,1,0:T(8,128)(2,1)S(1)} %get-tuple-element.37.own_x_ref, bf16[1,768,1152]{2,1,0:T(8,128)(2,1)} %get-tuple-element.42.x_ref, ...), custom_call_target="tpu_custom_call" | custom-call | tf_op jit(solution)/shard_map/far/pallas_call | solution.py:355
  82.4 2.1 %collective-permute-start.20 = (bf16[784,256]{1,0:T(8,128)(2,1)S(1)}, bf16[784,256]{1,0:T(8,128)(2,1)S(1)}, u32[]{:S(2)}, u32[]{:S(2)}) collective-permute-start(bf16[784,256]{1,0:T(8,128)(2,1)S(1)} %get-tuple-element.45.refs_3_.after_ref.rest_2_), channel_id=1, source_target_pairs={{0,4},{4,8},{8,12},{1,5},{5,9},{9,13},{2,6},{6,10},{10,14},{3,7},{... | collective-permute-start | bytes 1204232 | tf_op jit(solution)/shard_map/ppermute | solution.py:822
  86.9 13.6 %collective-permute-done.18.far_ref = bf16[768,256]{1,0:T(8,128)(2,1)} collective-permute-done((bf16[768,256]{1,0:T(8,128)(2,1)S(1)}, bf16[768,256]{1,0:T(8,128)(2,1)}, u32[]{:S(2)}, u32[]{:S(2)}) %collective-permute-start.18) | collective-permute-done | bytes 393248 | tf_op jit(solution)/shard_map/ppermute | solution.py:808
  102.1 3.0 %attend.2.rest_0_ = bf16[384,256]{1,0:T(8,128)(2,1)S(1)} custom-call(s32[1]{0:T(128)} %bitcast.16.seq_ref, bf16[768,256]{1,0:T(8,128)(2,1)S(1)} %queries.1.q_ref, s32[1,768]{1,0:T(1,128)S(1)} %broadcast_in_dim.21.id_ref, bf16[784,256]{1,0:T(8,128)(2,1)S(1)} %get-tuple-element.45.refs_3_.after_ref.rest_2_, ...), custom_call_target="tpu_custom_call" | custom-call | flops 905969664 | bytes 2359296 | tf_op jit(solution)/shard_map/attend/pallas_call | solution.py:564
  105.1 2.5 %collective-permute-start.21 = (bf16[384,256]{1,0:T(8,128)(2,1)S(1)}, bf16[384,256]{1,0:T(8,128)(2,1)S(1)}, u32[]{:S(2)}, u32[]{:S(2)}) collective-permute-start(bf16[384,256]{1,0:T(8,128)(2,1)S(1)} %attend.2.rest_0_), channel_id=1, source_target_pairs={{0,1},{1,0},{2,3},{3,2},{4,5},{5,4},{6,7},{7,6},{8,9},{9,8},{10,11... | collective-permute-start | bytes 589832 | tf_op jit(solution)/shard_map/ppermute | solution.py:835
  109.1 4.0 %attend.3.rest_2_.after_ref.rest_0_ = bf16[384,256]{1,0:T(8,128)(2,1)S(1)} custom-call(s32[1]{0:T(128)} %bitcast.16.seq_ref, bf16[768,256]{1,0:T(8,128)(2,1)S(1)} %queries.1.q_ref, s32[1,768]{1,0:T(1,128)S(1)} %broadcast_in_dim.21.id_ref, bf16[3,256,1152]{2,1,0:T(8,128)(2,1)S(1)} %lay.1.after_ref.o_ref, ...), custom_call_target="tpu_custom_call" | custom-call | flops 905969664 | bytes 2359296 | tf_op jit(solution)/shard_map/attend/pallas_call | solution.py:564
  113.3 2.4 %collective-permute-start.25 = (bf16[384,256]{1,0:T(8,128)(2,1)S(1)}, bf16[384,256]{1,0:T(8,128)(2,1)S(1)}, u32[]{:S(2)}, u32[]{:S(2)}) collective-permute-start(bf16[384,256]{1,0:T(8,128)(2,1)S(1)} %attend.3.rest_2_.after_ref.rest_0_), channel_id=1, source_target_pairs={{0,2},{1,3},{2,0},{3,1},{4,6},{5,7},{6,4},{7,5},{8,10},{9,11},{10,... | collective-permute-start | bytes 589832 | tf_op jit(solution)/shard_map/ppermute | solution.py:834
  117.1 3.2 %first_output.2.part_ref = f32[384,1152]{1,0:T(8,128)S(1)} custom-call(s32[2]{0:T(128)S(1)} %pad_add_fusion.1.at_ref, bf16[256,4608]{1,0:T(8,128)(2,1)} %own_o_ref.3, bf16[3,256,1152]{2,1,0:T(8,128)(2,1)S(1)} %lay.1.after_ref.o_ref, bf16[384,256]{1,0:T(8,128)(2,1)S(1)} %attend.2.rest_0_, bf16[384,256]{1,0:T(8,128)(2,1)S(1)} %collective-permute-done.21.rest_1_, ...), custom_call_target="tpu_custom_call" | custom-call | flops 49999998976 | bytes 100000000 | tf_op jit(solution)/shard_map/first_output/pallas_call | solution.py:639
  121.7 1.7 %collective-permute-start.26 = (bf16[384,256]{1,0:T(8,128)(2,1)S(1)}, bf16[384,256]{1,0:T(8,128)(2,1)S(1)}, u32[]{:S(2)}, u32[]{:S(2)}) collective-permute-start(bf16[384,256]{1,0:T(8,128)(2,1)S(1)} %collective-permute-done.25.rest_0_), channel_id=1, source_target_pairs={{0,1},{1,0},{2,3},{3,2},{4,5},{5,4},{6,7},{7,6},{8,9},{9,8},{10,11... | collective-permute-start | bytes 589832 | tf_op jit(solution)/shard_map/ppermute | solution.py:838
  123.4 1.9 %collective-permute-done.24.rest_1_ = bf16[384,256]{1,0:T(8,128)(2,1)S(1)} collective-permute-done((bf16[384,256]{1,0:T(8,128)(2,1)S(1)}, bf16[384,256]{1,0:T(8,128)(2,1)S(1)}, u32[]{:S(2)}, u32[]{:S(2)}) %collective-permute-start.24) | collective-permute-done | bytes 196640 | tf_op jit(solution)/shard_map/ppermute | solution.py:835
  125.3 3.2 %first_output.3.part_ref = f32[384,1152]{1,0:T(8,128)S(1)} custom-call(s32[2]{0:T(128)S(1)} %pad_add_fusion.1.at_ref, bf16[256,4608]{1,0:T(8,128)(2,1)} %own_o_ref.3, bf16[3,256,1152]{2,1,0:T(8,128)(2,1)S(1)} %lay.1.after_ref.o_ref, bf16[384,256]{1,0:T(8,128)(2,1)S(1)} %attend.3.rest_2_.after_ref.rest_0_, ...), custom_call_target="tpu_custom_call" | custom-call | flops 49999998976 | bytes 100000000 | tf_op jit(solution)/shard_map/first_output/pallas_call | solution.py:639
  129.5 2.5 %last_output.2 = (f32[384,1152]{1,0:T(8,128)S(1)}, f32[1,384]{1,0:T(1,128)S(1)}) custom-call(s32[2]{0:T(128)S(1)} %pad_add_fusion.at_ref, f32[384,1152]{1,0:T(8,128)S(1)} %first_output.2.part_ref, bf16[3,256,1152]{2,1,0:T(8,128)(2,1)S(1)} %lay.1.after_ref.o_ref, bf16[384,256]{1,0:T(8,128)(2,1)S(1)} %gate.5.rest_0_, ...), custom_call_target="tpu_custom_call" | custom-call | tf_op jit(solution)/shard_map/last_output/pallas_call | solution.py:663
  132.1 1.7 %collective-permute-done.26.rest_1_ = bf16[384,256]{1,0:T(8,128)(2,1)S(1)} collective-permute-done((bf16[384,256]{1,0:T(8,128)(2,1)S(1)}, bf16[384,256]{1,0:T(8,128)(2,1)S(1)}, u32[]{:S(2)}, u32[]{:S(2)}) %collective-permute-start.26) | collective-permute-done | bytes 196640 | tf_op jit(solution)/shard_map/ppermute | solution.py:838
  133.8 2.5 %last_output.3 = (f32[384,1152]{1,0:T(8,128)S(1)}, f32[1,768]{1,0:T(1,128)S(1)}) custom-call(s32[2]{0:T(128)S(1)} %pad_add_fusion.at_ref, f32[384,1152]{1,0:T(8,128)S(1)} %first_output.3.part_ref, bf16[3,256,1152]{2,1,0:T(8,128)(2,1)S(1)} %lay.1.after_ref.o_ref, bf16[384,256]{1,0:T(8,128)(2,1)S(1)} %collective-permute-done.25.rest_0_, ...), custom_call_target="tpu_custom_call" | custom-call | tf_op jit(solution)/shard_map/last_output/pallas_call | solution.py:663
  136.4 2.4 %collective-permute-start.28 = (f32[1,768]{1,0:T(1,128)S(1)}, f32[1,768]{1,0:T(1,128)S(1)}, u32[]{:S(2)}, u32[]{:S(2)}) collective-permute-start(f32[1,768]{1,0:T(1,128)S(1)} %get-tuple-element.50.rest_2_), channel_id=1, source_target_pairs={{0,2},{1,3},{2,0},{3,1},{4,6},{5,7},{6,4},{7,5},{8,10},{9,11},{10,... | collective-permute-start | bytes 9224 | tf_op jit(solution)/shard_map/ppermute | solution.py:853
  142.4 3.2 %finish.1 = bf16[768,1152]{1,0:T(8,128)(2,1)} custom-call(bf16[768,1152]{1,0:T(8,128)(2,1)S(1)} %copy-done, f32[1,1152]{1,0:T(1,128)S(1)} %broadcast_in_dim.17.gain_ref, f32[384,1152]{1,0:T(8,128)S(1)} %get-tuple-element.47.rest_0_, f32[384,1152]{1,0:T(8,128)S(1)} %get-tuple-element.49.rest_1_, f32[1,768]{1,0:T(1,128)S(1)} %get-tuple-element.50.rest_2_, ...), custom_call_target="tpu_custom_call" | custom-call | tf_op jit(solution)/shard_map/finish/pallas_call | solution.py:704
  (99 shorter events, 36.0 us)
Async XLA Ops:
  0.0 19.7 %copy-start = (bf16[768,1152]{1,0:T(8,128)(2,1)S(1)}, bf16[768,1152]{1,0:T(8,128)(2,1)}, u32[]{:S(2)}) copy-start(bf16[768,1152]{1,0:T(8,128)(2,1)} %token_ref.1) | copy-start | bytes 5308420
  2.1 17.6 %collective-permute-start.10 = (bf16[128,1152]{1,0:T(8,128)(2,1)}, bf16[128,1152]{1,0:T(8,128)(2,1)S(1)}, u32[]{:S(2)}, u32[]{:S(2)}) collective-permute-start(bf16[128,1152]{1,0:T(8,128)(2,1)} %get-tuple-element.35), channel_id=1, source_target_pairs={{0,1},{1,0},{2,3},{3,2},{4,5},{5,4},{6,7},{7,6},{8,9},{9,8},{10,11... | collective-permute-start | bytes 884744 | tf_op jit(solution)/shard_map/ppermute | solution.py:752
  3.7 10.9 %collective-permute-start = (bf16[288,256]{1,0:T(8,128)(2,1)}, bf16[288,256]{1,0:T(8,128)(2,1)S(1)}, u32[]{:S(2)}, u32[]{:S(2)}) collective-permute-start(bf16[288,256]{1,0:T(8,128)(2,1)} %get-tuple-element.28), channel_id=1, source_target_pairs={{0,2},{1,3},{2,0},{3,1},{4,6},{5,7},{6,4},{7,5},{8,10},{9,11},{10,... | collective-permute-start | bytes 442376 | tf_op jit(solution)/shard_map/ppermute | solution.py:750
  6.3 13.4 %collective-permute-start.6 = (bf16[288,256]{1,0:T(8,128)(2,1)}, bf16[288,256]{1,0:T(8,128)(2,1)S(1)}, u32[]{:S(2)}, u32[]{:S(2)}) collective-permute-start(bf16[288,256]{1,0:T(8,128)(2,1)} %get-tuple-element.32), channel_id=1, source_target_pairs={{0,2},{1,3},{2,0},{3,1},{4,6},{5,7},{6,4},{7,5},{8,10},{9,11},{10,... | collective-permute-start | bytes 442376 | tf_op jit(solution)/shard_map/ppermute | solution.py:751
  20.7 27.5 %collective-permute-start.11 = (bf16[352,1152]{1,0:T(8,128)(2,1)}, bf16[352,1152]{1,0:T(8,128)(2,1)S(1)}, u32[]{:S(2)}, u32[]{:S(2)}) collective-permute-start(bf16[352,1152]{1,0:T(8,128)(2,1)} %stage.6), channel_id=1, source_target_pairs={{0,1},{1,0},{2,3},{3,2},{4,5},{5,4},{6,7},{7,6},{8,9},{9,8},{10,11... | collective-permute-start | bytes 2433032 | tf_op jit(solution)/shard_map/ppermute | solution.py:773
  21.2 5.1 %collective-permute-start.5 = (bf16[1,288,256]{2,1,0:T(8,128)(2,1)S(1)}, bf16[1,288,256]{2,1,0:T(8,128)(2,1)S(1)}, u32[]{:S(2)}, u32[]{:S(2)}) collective-permute-start(bf16[1,288,256]{2,1,0:T(8,128)(2,1)S(1)} %bitcast.19), channel_id=1, source_target_pairs={{0,8},{4,12},{8,0},{12,4},{16,24},{20,28},{24,16},{28,20},{1,9},{5... | collective-permute-start | bytes 442376 | tf_op jit(solution)/shard_map/ppermute | solution.py:775
  21.7 5.1 %collective-permute-start.7 = (bf16[1,288,256]{2,1,0:T(8,128)(2,1)S(1)}, bf16[1,288,256]{2,1,0:T(8,128)(2,1)S(1)}, u32[]{:S(2)}, u32[]{:S(2)}) collective-permute-start(bf16[1,288,256]{2,1,0:T(8,128)(2,1)S(1)} %bitcast.23), channel_id=1, source_target_pairs={{0,16},{4,20},{8,24},{12,28},{16,0},{20,4},{24,8},{28,12},{1,17},{... | collective-permute-start | bytes 442376 | tf_op jit(solution)/shard_map/ppermute | solution.py:776
  28.9 19.2 %collective-permute-start.8 = (bf16[2,288,256]{2,1,0:T(8,128)(2,1)}, bf16[2,288,256]{2,1,0:T(8,128)(2,1)}, u32[]{:S(2)}, u32[]{:S(2)}) collective-permute-start(bf16[2,288,256]{2,1,0:T(8,128)(2,1)} %get-tuple-element.33.refs_0_), channel_id=1, source_target_pairs={{0,16},{4,20},{8,24},{12,28},{16,0},{20,4},{24,8},{28,12},{1,17},{... | collective-permute-start | bytes 884744 | tf_op jit(solution)/shard_map/ppermute | solution.py:775
  30.5 17.6 %collective-permute-start.9 = (bf16[2,288,256]{2,1,0:T(8,128)(2,1)}, bf16[2,288,256]{2,1,0:T(8,128)(2,1)}, u32[]{:S(2)}, u32[]{:S(2)}) collective-permute-start(bf16[2,288,256]{2,1,0:T(8,128)(2,1)} %get-tuple-element.34.refs_2_), channel_id=1, source_target_pairs={{0,8},{4,12},{8,0},{12,4},{16,24},{20,28},{24,16},{28,20},{1,9},{5... | collective-permute-start | bytes 884744 | tf_op jit(solution)/shard_map/ppermute | solution.py:776
  34.4 8.5 %collective-permute-start.1 = (bf16[32,1152]{1,0:T(8,128)(2,1)S(1)}, bf16[32,1152]{1,0:T(8,128)(2,1)S(1)}, u32[]{:S(2)}, u32[]{:S(2)}) collective-permute-start(bf16[32,1152]{1,0:T(8,128)(2,1)S(1)} %get-tuple-element.29), channel_id=1, source_target_pairs={{0,1},{1,2},{2,3},{3,0},{4,5},{5,6},{6,7},{7,4},{8,9},{9,10},{10,1... | collective-permute-start | bytes 221192 | tf_op jit(solution)/shard_map/ppermute | solution.py:756
  36.0 6.9 %collective-permute-start.2 = (bf16[32,1152]{1,0:T(8,128)(2,1)S(1)}, bf16[32,1152]{1,0:T(8,128)(2,1)S(1)}, u32[]{:S(2)}, u32[]{:S(2)}) collective-permute-start(bf16[32,1152]{1,0:T(8,128)(2,1)S(1)} %get-tuple-element.30), channel_id=1, source_target_pairs={{0,2},{1,3},{2,0},{3,1},{4,6},{5,7},{6,4},{7,5},{8,10},{9,11},{10,... | collective-permute-start | bytes 221192 | tf_op jit(solution)/shard_map/ppermute | solution.py:756
  42.9 5.2 %collective-permute-start.3 = (bf16[32,1152]{1,0:T(8,128)(2,1)S(1)}, bf16[32,1152]{1,0:T(8,128)(2,1)S(1)}, u32[]{:S(2)}, u32[]{:S(2)}) collective-permute-start(bf16[32,1152]{1,0:T(8,128)(2,1)S(1)} %get-tuple-element.31), channel_id=1, source_target_pairs={{0,3},{1,0},{2,1},{3,2},{4,7},{5,4},{6,5},{7,6},{8,11},{9,8},{10,9... | collective-permute-start | bytes 221192 | tf_op jit(solution)/shard_map/ppermute | solution.py:756
  42.9 14.9 %collective-permute-start.13 = (bf16[288,1152]{1,0:T(8,128)(2,1)}, bf16[288,1152]{1,0:T(8,128)(2,1)S(1)}, u32[]{:S(2)}, u32[]{:S(2)}) collective-permute-start(bf16[288,1152]{1,0:T(8,128)(2,1)} %get-tuple-element.40), channel_id=1, source_target_pairs={{0,1},{1,0},{2,3},{3,2},{4,5},{5,4},{6,7},{7,6},{8,9},{9,8},{10,11... | collective-permute-start | bytes 1990664 | tf_op jit(solution)/shard_map/ppermute | solution.py:773
  50.8 2.5 %collective-permute-start.12 = (bf16[4,288,256]{2,1,0:T(8,128)(2,1)}, bf16[4,288,256]{2,1,0:T(8,128)(2,1)}, u32[]{:S(2)}, u32[]{:S(2)}) collective-permute-start(bf16[4,288,256]{2,1,0:T(8,128)(2,1)} %get-tuple-element.36.own_ref), channel_id=1, source_target_pairs={{0,4},{4,0},{8,12},{12,8},{16,20},{20,16},{24,28},{28,24},{1,5},{5... | collective-permute-start | bytes 1769480 | tf_op jit(solution)/shard_map/ppermute | solution.py:775
  50.9 7.0 %collective-permute-start.14 = (bf16[4,288,256]{2,1,0:T(8,128)(2,1)}, bf16[4,288,256]{2,1,0:T(8,128)(2,1)S(1)}, u32[]{:S(2)}, u32[]{:S(2)}) collective-permute-start(bf16[4,288,256]{2,1,0:T(8,128)(2,1)} %get-tuple-element.41.own_ref), channel_id=1, source_target_pairs={{0,4},{4,0},{8,12},{12,8},{16,20},{20,16},{24,28},{28,24},{1,5},{5... | collective-permute-start | bytes 1769480 | tf_op jit(solution)/shard_map/ppermute | solution.py:776
  61.6 18.7 %collective-permute-start.16 = (bf16[784,256]{1,0:T(8,128)(2,1)S(1)}, bf16[784,256]{1,0:T(8,128)(2,1)S(1)}, u32[]{:S(2)}, u32[]{:S(2)}) collective-permute-start(bf16[784,256]{1,0:T(8,128)(2,1)S(1)} %get-tuple-element.43.rest_0_), channel_id=1, source_target_pairs={{0,2},{1,3},{2,0},{3,1},{4,6},{5,7},{6,4},{7,5},{8,10},{9,11},{10,... | collective-permute-start | bytes 1204232 | tf_op jit(solution)/shard_map/ppermute | solution.py:799
  63.7 12.6 %collective-permute-start.4 = (bf16[1,3,32,1152]{3,2,1,0:T(8,128)(2,1)S(1)}, bf16[1,3,32,1152]{3,2,1,0:T(8,128)(2,1)S(1)}, u32[]{:S(2)}, u32[]{:S(2)}) collective-permute-start(bf16[1,3,32,1152]{3,2,1,0:T(8,128)(2,1)S(1)} %maximum_bitcast_fusion.refs_0_), channel_id=1, source_target_pairs={{0,8},{4,12},{8,0},{12,4},{16,24},{20,28},{24,16},{28,20},{1,9},{5... | collective-permute-start | bytes 663560 | tf_op jit(solution)/shard_map/ppermute | solution.py:786
  77.0 8.6 %collective-permute-start.15 = (bf16[2,3,32,1152]{3,2,1,0:T(8,128)(2,1)S(1)}, bf16[2,3,32,1152]{3,2,1,0:T(8,128)(2,1)}, u32[]{:S(2)}, u32[]{:S(2)}) collective-permute-start(bf16[2,3,32,1152]{3,2,1,0:T(8,128)(2,1)S(1)} %stage.8.rest_1_.refs_0_), channel_id=1, source_target_pairs={{0,16},{4,20},{8,24},{12,28},{16,0},{20,4},{24,8},{28,12},{1,17},{... | collective-permute-start | bytes 1327112 | tf_op jit(solution)/shard_map/ppermute | solution.py:786
  80.8 19.7 %collective-permute-start.18 = (bf16[768,256]{1,0:T(8,128)(2,1)S(1)}, bf16[768,256]{1,0:T(8,128)(2,1)}, u32[]{:S(2)}, u32[]{:S(2)}) collective-permute-start(bf16[768,256]{1,0:T(8,128)(2,1)S(1)} %gate.4), channel_id=1, source_target_pairs={{0,2},{1,3},{2,0},{3,1},{4,6},{5,7},{6,4},{7,5},{8,10},{9,11},{10,... | collective-permute-start | bytes 1179656 | tf_op jit(solution)/shard_map/ppermute | solution.py:808
  81.0 19.6 %copy-start.9 = (f32[768,128]{1,0:T(8,128)S(1)}, f32[768,128]{1,0:T(8,128)}, u32[]{:S(2)}) copy-start(f32[768,128]{1,0:T(8,128)} %copy-done.8) | copy-start | bytes 1179652
  81.0 21.1 %collective-permute-start.19 = (bf16[784,256]{1,0:T(8,128)(2,1)S(1)}, bf16[784,256]{1,0:T(8,128)(2,1)S(1)}, u32[]{:S(2)}, u32[]{:S(2)}) collective-permute-start(bf16[784,256]{1,0:T(8,128)(2,1)S(1)} %get-tuple-element.45.refs_3_.after_ref.rest_2_), channel_id=1, source_target_pairs={{0,8},{4,12},{1,9},{5,13},{2,10},{6,14},{3,11},{7,15},{16,24},{20,... | collective-permute-start | bytes 1204232 | tf_op jit(solution)/shard_map/ppermute | solution.py:822
  82.4 19.7 %collective-permute-start.20 = (bf16[784,256]{1,0:T(8,128)(2,1)S(1)}, bf16[784,256]{1,0:T(8,128)(2,1)S(1)}, u32[]{:S(2)}, u32[]{:S(2)}) collective-permute-start(bf16[784,256]{1,0:T(8,128)(2,1)S(1)} %get-tuple-element.45.refs_3_.after_ref.rest_2_), channel_id=1, source_target_pairs={{0,4},{4,8},{8,12},{1,5},{5,9},{9,13},{2,6},{6,10},{10,14},{3,7},{... | collective-permute-start | bytes 1204232 | tf_op jit(solution)/shard_map/ppermute | solution.py:822
  86.8 20.9 %collective-permute-start.17 = (bf16[4,3,32,1152]{3,2,1,0:T(8,128)(2,1)S(1)}, bf16[4,3,32,1152]{3,2,1,0:T(8,128)(2,1)S(1)}, u32[]{:S(2)}, u32[]{:S(2)}) collective-permute-start(bf16[4,3,32,1152]{3,2,1,0:T(8,128)(2,1)S(1)} %stage.9.own_ref), channel_id=1, source_target_pairs={{0,4},{4,0},{8,12},{12,8},{16,20},{20,16},{24,28},{28,24},{1,5},{5... | collective-permute-start | bytes 2654216 | tf_op jit(solution)/shard_map/ppermute | solution.py:786
  105.0 12.0 %collective-permute-start.22 = (bf16[384,256]{1,0:T(8,128)(2,1)S(1)}, bf16[384,256]{1,0:T(8,128)(2,1)S(1)}, u32[]{:S(2)}, u32[]{:S(2)}) collective-permute-start(bf16[384,256]{1,0:T(8,128)(2,1)S(1)} %attend.2.rest_0_), channel_id=1, source_target_pairs={{0,2},{1,3},{2,0},{3,1},{4,6},{5,7},{6,4},{7,5},{8,10},{9,11},{10,... | collective-permute-start | bytes 589832 | tf_op jit(solution)/shard_map/ppermute | solution.py:834
  105.1 12.0 %collective-permute-start.21 = (bf16[384,256]{1,0:T(8,128)(2,1)S(1)}, bf16[384,256]{1,0:T(8,128)(2,1)S(1)}, u32[]{:S(2)}, u32[]{:S(2)}) collective-permute-start(bf16[384,256]{1,0:T(8,128)(2,1)S(1)} %attend.2.rest_0_), channel_id=1, source_target_pairs={{0,1},{1,0},{2,3},{3,2},{4,5},{5,4},{6,7},{7,6},{8,9},{9,8},{10,11... | collective-permute-start | bytes 589832 | tf_op jit(solution)/shard_map/ppermute | solution.py:835
  113.2 12.1 %collective-permute-start.24 = (bf16[384,256]{1,0:T(8,128)(2,1)S(1)}, bf16[384,256]{1,0:T(8,128)(2,1)S(1)}, u32[]{:S(2)}, u32[]{:S(2)}) collective-permute-start(bf16[384,256]{1,0:T(8,128)(2,1)S(1)} %attend.3.rest_2_.after_ref.rest_0_), channel_id=1, source_target_pairs={{0,1},{1,0},{2,3},{3,2},{4,5},{5,4},{6,7},{7,6},{8,9},{9,8},{10,11... | collective-permute-start | bytes 589832 | tf_op jit(solution)/shard_map/ppermute | solution.py:835
  113.3 8.5 %collective-permute-start.25 = (bf16[384,256]{1,0:T(8,128)(2,1)S(1)}, bf16[384,256]{1,0:T(8,128)(2,1)S(1)}, u32[]{:S(2)}, u32[]{:S(2)}) collective-permute-start(bf16[384,256]{1,0:T(8,128)(2,1)S(1)} %attend.3.rest_2_.after_ref.rest_0_), channel_id=1, source_target_pairs={{0,2},{1,3},{2,0},{3,1},{4,6},{5,7},{6,4},{7,5},{8,10},{9,11},{10,... | collective-permute-start | bytes 589832 | tf_op jit(solution)/shard_map/ppermute | solution.py:834
  117.1 12.5 %collective-permute-start.23 = (bf16[384,256]{1,0:T(8,128)(2,1)S(1)}, bf16[384,256]{1,0:T(8,128)(2,1)S(1)}, u32[]{:S(2)}, u32[]{:S(2)}) collective-permute-start(bf16[384,256]{1,0:T(8,128)(2,1)S(1)} %gate.5.rest_0_), channel_id=1, source_target_pairs={{0,1},{1,0},{2,3},{3,2},{4,5},{5,4},{6,7},{7,6},{8,9},{9,8},{10,11... | collective-permute-start | bytes 589832 | tf_op jit(solution)/shard_map/ppermute | solution.py:838
  121.7 12.0 %collective-permute-start.26 = (bf16[384,256]{1,0:T(8,128)(2,1)S(1)}, bf16[384,256]{1,0:T(8,128)(2,1)S(1)}, u32[]{:S(2)}, u32[]{:S(2)}) collective-permute-start(bf16[384,256]{1,0:T(8,128)(2,1)S(1)} %collective-permute-done.25.rest_0_), channel_id=1, source_target_pairs={{0,1},{1,0},{2,3},{3,2},{4,5},{5,4},{6,7},{7,6},{8,9},{9,8},{10,11... | collective-permute-start | bytes 589832 | tf_op jit(solution)/shard_map/ppermute | solution.py:838
  136.3 5.4 %collective-permute-start.27 = (f32[1,768]{1,0:T(1,128)S(1)}, f32[1,768]{1,0:T(1,128)S(1)}, u32[]{:S(2)}, u32[]{:S(2)}) collective-permute-start(f32[1,768]{1,0:T(1,128)S(1)} %get-tuple-element.50.rest_2_), channel_id=1, source_target_pairs={{0,1},{1,2},{2,3},{3,0},{4,5},{5,6},{6,7},{7,4},{8,9},{9,10},{10,1... | collective-permute-start | bytes 9224 | tf_op jit(solution)/shard_map/ppermute | solution.py:853
  136.4 5.4 %collective-permute-start.28 = (f32[1,768]{1,0:T(1,128)S(1)}, f32[1,768]{1,0:T(1,128)S(1)}, u32[]{:S(2)}, u32[]{:S(2)}) collective-permute-start(f32[1,768]{1,0:T(1,128)S(1)} %get-tuple-element.50.rest_2_), channel_id=1, source_target_pairs={{0,2},{1,3},{2,0},{3,1},{4,6},{5,7},{6,4},{7,5},{8,10},{9,11},{10,... | collective-permute-start | bytes 9224 | tf_op jit(solution)/shard_map/ppermute | solution.py:853
  138.8 3.6 %collective-permute-start.29 = (f32[1,768]{1,0:T(1,128)S(1)}, f32[1,768]{1,0:T(1,128)S(1)}, u32[]{:S(2)}, u32[]{:S(2)}) collective-permute-start(f32[1,768]{1,0:T(1,128)S(1)} %get-tuple-element.50.rest_2_), channel_id=1, source_target_pairs={{0,3},{1,0},{2,1},{3,2},{4,7},{5,4},{6,5},{7,6},{8,11},{9,8},{10,9... | collective-permute-start | bytes 9224 | tf_op jit(solution)/shard_map/ppermute | solution.py:853
  (15 other events, 103.6 us)

commit v16 on v15

--- a/solution.py
+++ b/solution.py
@@ -759,7 +759,7 @@
     for step, (mask_kv, mask_q) in enumerate(zip(masks_kv, masks_q)):
         after, count = [], 0
         if step == 0:
-            pairs, after = [], [own_kv, own_q, received[0]]
+            pairs, after = [], [own_kv, received[0]]
         else:
             pairs = [(own_kv, far_kv), (own_q, far_q)]
         if step < 2:

time: 148 us -> 163 us (1.10); the launches traced: 146 us -> 163 us
  waiting for transfers between devices: 54.5 us -> 61.2 us
  Pallas kernels: 52.7 us -> 59.3 us
  starting transfers between devices: 34.1 us -> 37.8 us
    ppermute x1, waiting for transfers between devices: 5.01 us -> 17.7 us  [per_device(): own_q = lax.ppermute(packed_q, 'tensor', swap)[None]]
    pallas_call x2, Pallas kernels: 7.01 us -> 13.6 us  [attend(): pl.pallas_call(partial(attention_kernel, back=back, offset=c * rows), out...]
    ppermute x3, waiting for transfers between devices: 4.82 us -> 1.74 us  [per_device(): lax.ppermute(own_kv, PLANE, [(i, i ^ mask_kv) for i in range(plane)])]
    ppermute x3, waiting for transfers between devices: 0.54 us -> 3.63 us  [per_device(): far_q = lax.ppermute(own_q, PLANE, [(i, i ^ mask_q) for i in range(plane)])]
    ppermute x2, waiting for transfers between devices: 2.64 us -> 0.01 us  [per_device(): across = lax.ppermute(opposite, 'tensor', pairs)]
    ppermute x3, waiting for transfers between devices: 8.87 us -> 6.37 us  [per_device(): lax.ppermute(p, 'tensor', turn(k + 1))]
    ppermute x2, starting transfers between devices: 2.53 us -> 4.93 us  [per_device(): received.append(lax.ppermute(outs[-1], 'tensor', ring))]
    ppermute x2, waiting for transfers between devices: 1.93 us -> 0.01 us  [per_device(): beside = lax.ppermute(context, 'tensor', pairs)]
  transfers between devices with their start and end apart: 30 -> 30, of which waited for: 18 -> 15; matrix products, arithmetic and copies ran while one was open for 1% -> 1% of each run, Pallas kernels for 28% -> 29%
where the time goes in v16:
time: 163 us
  waiting for transfers between devices  61.2 us (38%)
  Pallas kernels  59.3 us (36%)
  starting transfers between devices  37.8 us (23%)
  other arithmetic  2.08 us (1%)
  local copies, waits for them, and re-layouts  1.77 us (1%)
    ppermute x1, waiting for transfers between devices, per_device(): own_q = lax.ppermute(packed_q, 'tensor', swap)[None]  17.7 us
    pallas_call x2, Pallas kernels, attend(): pl.pallas_call(partial(attention_kernel, back=back, offset=c * rows), out...  13.6 us
    ppermute x1, waiting for transfers between devices, per_device(): got_q = lax.ppermute(gate(sent_q, got_kv), 'tensor', swap)  12.6 us
    pallas_call x5, Pallas kernels, stage(): pl.pallas_call(partial(stage_kernel, pairs=len(joined), first=first, coun...  7.53 us
    ppermute x1, waiting for transfers between devices, per_device(): own_kv = lax.ppermute(packed_kv, 'tensor', swap)[None]  7.15 us
    pallas_call x2, Pallas kernels, first_output(): pl.pallas_call(first_output_kernel, out_shape=shape((chunk, cols), F32),...  6.48 us
    ppermute x3, waiting for transfers between devices, per_device(): lax.ppermute(p, 'tensor', turn(k + 1))  6.37 us
    pallas_call x1, Pallas kernels, near_product(): pl.pallas_call(near_kernel, out_shape=shape((rows, sum(widths)), F32), gr...  6.14 us
  transfers between devices with their start and end apart: 30, of which 15 were waited for; matrix products, arithmetic and copies ran while one was open for 1% of the time, Pallas kernels for 29%

profile of v16, /device:TPU:2, one launch (start us, length us, event | category | flops | bytes accessed | tf_op | source)
XLA Modules:
  0.0 162.6 jit_solution(17143191025430857812)
XLA Ops:
  0.0 2.1 %pack.1 = (bf16[288,256]{1,0:T(8,128)(2,1)}, bf16[288,256]{1,0:T(8,128)(2,1)}, bf16[128,1152]{1,0:T(8,128)(2,1)}) custom-call(s32[1]{0:T(128)} %bitcast.9.at_ref, bf16[4608,256]{1,0:T(8,128)(2,1)} %q_ref.3, bf16[4608,128]{1,0:T(8,128)(2,1)} %k_ref.3, bf16[4608,128]{1,0:T(8,128)(2,1)} %v_ref.3, bf16[768,1152]{1,0:T(8,128)(2,1)} %token_ref.1), custom_call_target="tpu_custom_call" | custom-call | tf_op jit(solution)/shard_map/pack/pallas_call | solution.py:75
  3.7 2.6 %collective-permute-start = (bf16[288,256]{1,0:T(8,128)(2,1)}, bf16[288,256]{1,0:T(8,128)(2,1)S(1)}, u32[]{:S(2)}, u32[]{:S(2)}) collective-permute-start(bf16[288,256]{1,0:T(8,128)(2,1)} %get-tuple-element.28), channel_id=1, source_target_pairs={{0,2},{1,3},{2,0},{3,1},{4,6},{5,7},{6,4},{7,5},{8,10},{9,11},{10,... | collective-permute-start | bytes 442376 | tf_op jit(solution)/shard_map/ppermute | solution.py:750
  6.3 7.2 %collective-permute-done = bf16[288,256]{1,0:T(8,128)(2,1)S(1)} collective-permute-done((bf16[288,256]{1,0:T(8,128)(2,1)}, bf16[288,256]{1,0:T(8,128)(2,1)S(1)}, u32[]{:S(2)}, u32[]{:S(2)}) %collective-permute-start) | collective-permute-done | bytes 147488 | tf_op jit(solution)/shard_map/ppermute | solution.py:750
  15.3 2.7 %collective-permute-start.11 = (bf16[352,1152]{1,0:T(8,128)(2,1)}, bf16[352,1152]{1,0:T(8,128)(2,1)S(1)}, u32[]{:S(2)}, u32[]{:S(2)}) collective-permute-start(bf16[352,1152]{1,0:T(8,128)(2,1)} %stage.6), channel_id=1, source_target_pairs={{0,1},{1,0},{2,3},{3,2},{4,5},{5,4},{6,7},{7,6},{8,9},{9,8},{10,11... | collective-permute-start | bytes 2433032 | tf_op jit(solution)/shard_map/ppermute | solution.py:773
  20.1 17.7 %collective-permute-done.6 = bf16[288,256]{1,0:T(8,128)(2,1)S(1)} collective-permute-done((bf16[288,256]{1,0:T(8,128)(2,1)S(1)}, bf16[288,256]{1,0:T(8,128)(2,1)S(1)}, u32[]{:S(2)}, u32[]{:S(2)}) %collective-permute-start.6) | collective-permute-done | bytes 147488 | tf_op jit(solution)/shard_map/ppermute | solution.py:751
  39.3 3.6 %collective-permute-done.7.refs_3_ = bf16[1,288,256]{2,1,0:T(8,128)(2,1)S(1)} collective-permute-done((bf16[1,288,256]{2,1,0:T(8,128)(2,1)S(1)}, bf16[1,288,256]{2,1,0:T(8,128)(2,1)S(1)}, u32[]{:S(2)}, u32[]{:S(2)}) %collective-permute-start.7) | collective-permute-done | bytes 147488 | tf_op jit(solution)/shard_map/ppermute | solution.py:776
  42.9 2.0 %stage.5 = (bf16[2,288,256]{2,1,0:T(8,128)(2,1)}, bf16[2,288,256]{2,1,0:T(8,128)(2,1)}, bf16[288,1152]{1,0:T(8,128)(2,1)}) custom-call(bf16[1,288,256]{2,1,0:T(8,128)(2,1)S(1)} %bitcast.20, bf16[1,288,256]{2,1,0:T(8,128)(2,1)S(1)} %collective-permute-done.5.refs_1_, bf16[1,288,256]{2,1,0:T(8,128)(2,1)S(1)} %bitcast.23, ...), custom_call_target="tpu_custom_call" | custom-call | tf_op jit(solution)/shard_map/stage/pallas_call | solution.py:130
  49.5 2.4 %collective-permute-start.1 = (bf16[32,1152]{1,0:T(8,128)(2,1)S(1)}, bf16[32,1152]{1,0:T(8,128)(2,1)S(1)}, u32[]{:S(2)}, u32[]{:S(2)}) collective-permute-start(bf16[32,1152]{1,0:T(8,128)(2,1)S(1)} %get-tuple-element.29), channel_id=1, source_target_pairs={{0,1},{1,2},{2,3},{3,0},{4,5},{5,6},{6,7},{7,4},{8,9},{9,10},{10,1... | collective-permute-start | bytes 221192 | tf_op jit(solution)/shard_map/ppermute | solution.py:756
  53.0 3.6 %collective-permute-done.1.refs_6_ = bf16[32,1152]{1,0:T(8,128)(2,1)S(1)} collective-permute-done((bf16[32,1152]{1,0:T(8,128)(2,1)S(1)}, bf16[32,1152]{1,0:T(8,128)(2,1)S(1)}, u32[]{:S(2)}, u32[]{:S(2)}) %collective-permute-start.1) | collective-permute-done | bytes 73760 | tf_op jit(solution)/shard_map/ppermute | solution.py:756
  57.3 2.3 %collective-permute-start.13 = (bf16[288,1152]{1,0:T(8,128)(2,1)}, bf16[288,1152]{1,0:T(8,128)(2,1)S(1)}, u32[]{:S(2)}, u32[]{:S(2)}) collective-permute-start(bf16[288,1152]{1,0:T(8,128)(2,1)} %get-tuple-element.40), channel_id=1, source_target_pairs={{0,1},{1,0},{2,3},{3,2},{4,5},{5,4},{6,7},{7,6},{8,9},{9,8},{10,11... | collective-permute-start | bytes 1990664 | tf_op jit(solution)/shard_map/ppermute | solution.py:773
  59.6 2.2 %collective-permute-done.3.refs_8_ = bf16[32,1152]{1,0:T(8,128)(2,1)S(1)} collective-permute-done((bf16[32,1152]{1,0:T(8,128)(2,1)S(1)}, bf16[32,1152]{1,0:T(8,128)(2,1)S(1)}, u32[]{:S(2)}, u32[]{:S(2)}) %collective-permute-start.3) | collective-permute-done | bytes 73760 | tf_op jit(solution)/shard_map/ppermute | solution.py:756
  61.8 2.6 %stage.7 = (bf16[4,288,256]{2,1,0:T(8,128)(2,1)}, bf16[4,288,256]{2,1,0:T(8,128)(2,1)}) custom-call(bf16[2,288,256]{2,1,0:T(8,128)(2,1)} %get-tuple-element.33.refs_0_, bf16[2,288,256]{2,1,0:T(8,128)(2,1)} %collective-permute-done.8.refs_1_, bf16[2,288,256]{2,1,0:T(8,128)(2,1)} %get-tuple-element.34.refs_2_, ...), custom_call_target="tpu_custom_call" | custom-call | flops 49999998976 | bytes 100000000 | tf_op jit(solution)/shard_map/stage/pallas_call | solution.py:130
  66.9 3.0 %far_own.1 = (bf16[1,768,1152]{2,1,0:T(8,128)(2,1)S(1)}, f32[1,768]{1,0:T(1,128)S(1)}, f32[768,256]{1,0:T(8,128)S(1)}) custom-call(s32[2]{0:T(128)S(1)} %get-tuple-element.55.place_ref, s32[2]{0:T(128)S(1)} %get-tuple-element.54.src_ref, f32[4,1,1152]{2,1,0:T(1,128)S(1)} %reshape.21.gain_ref, bf16[4,288,256]{2,1,0:T(8,128)(2,1)} %get-tuple-element.36.own_ref, ...), custom_call_target="tpu_custom_call" | custom-call | tf_op jit(solution)/shard_map/far_own/pallas_call | solution.py:283
  71.4 3.7 %far_kv.1 = (bf16[784,256]{1,0:T(8,128)(2,1)S(1)}, bf16[1,768,1152]{2,1,0:T(8,128)(2,1)}, f32[1,768]{1,0:T(1,128)S(1)}) custom-call(s32[2]{0:T(128)S(1)} %get-tuple-element.55.place_ref, s32[2]{0:T(128)S(1)} %get-tuple-element.54.src_ref, f32[4,1,1152]{2,1,0:T(1,128)S(1)} %reshape.21.gain_ref, f32[768,256]{1,0:T(8,128)S(1)} %get-tuple-element.38.part_ref, ...), custom_call_target="tpu_custom_call" | custom-call | tf_op jit(solution)/shard_map/far_kv/pallas_call | solution.py:305
  79.4 6.1 %near.1.rest_0_.near_ref = f32[768,512]{1,0:T(8,128)S(1)} custom-call(s32[2]{0:T(128)S(1)} %broadcast_add_fusion.src_ref, bf16[1,768,1152]{2,1,0:T(8,128)(2,1)S(1)} %get-tuple-element.37.own_x_ref, bf16[1,768,1152]{2,1,0:T(8,128)(2,1)} %get-tuple-element.42.x_ref, bf16[4608,128]{1,0:T(8,128)(2,1)S(1)} %copy-done.3, bf16[4608,128]{1,0:T(8,128)(2,1)S(1)} %copy-done.4, ...), custom_call_target="tpu_custom_call" | custom-call | tf_op jit(solution)/shard_map/near/pallas_call | solution.py:398
  85.6 4.4 %far.1.refs_3_.rest_0_.x_ref = bf16[768,256]{1,0:T(8,128)(2,1)S(1)} custom-call(s32[2]{0:T(128)S(1)} %get-tuple-element.55.place_ref, s32[2]{0:T(128)S(1)} %get-tuple-element.54.src_ref, bf16[1,768,1152]{2,1,0:T(8,128)(2,1)S(1)} %get-tuple-element.37.own_x_ref, bf16[1,768,1152]{2,1,0:T(8,128)(2,1)} %get-tuple-element.42.x_ref, ...), custom_call_target="tpu_custom_call" | custom-call | tf_op jit(solution)/shard_map/far/pallas_call | solution.py:355
  91.5 2.5 %collective-permute-done.16.far_ref.after_ref = bf16[784,256]{1,0:T(8,128)(2,1)S(1)} collective-permute-done((bf16[784,256]{1,0:T(8,128)(2,1)S(1)}, bf16[784,256]{1,0:T(8,128)(2,1)S(1)}, u32[]{:S(2)}, u32[]{:S(2)}) %collective-permute-start.16) | collective-permute-done | bytes 401440 | tf_op jit(solution)/shard_map/ppermute | solution.py:799
  96.0 2.1 %collective-permute-start.20 = (bf16[784,256]{1,0:T(8,128)(2,1)S(1)}, bf16[784,256]{1,0:T(8,128)(2,1)S(1)}, u32[]{:S(2)}, u32[]{:S(2)}) collective-permute-start(bf16[784,256]{1,0:T(8,128)(2,1)S(1)} %get-tuple-element.45.refs_3_.after_ref.rest_2_), channel_id=1, source_target_pairs={{0,4},{4,8},{8,12},{1,5},{5,9},{9,13},{2,6},{6,10},{10,14},{3,7},{... | collective-permute-start | bytes 1204232 | tf_op jit(solution)/shard_map/ppermute | solution.py:822
  98.1 2.6 %collective-permute-done.15.refs_1_ = bf16[2,3,32,1152]{3,2,1,0:T(8,128)(2,1)} collective-permute-done((bf16[2,3,32,1152]{3,2,1,0:T(8,128)(2,1)S(1)}, bf16[2,3,32,1152]{3,2,1,0:T(8,128)(2,1)}, u32[]{:S(2)}, u32[]{:S(2)}) %collective-permute-start.15) | collective-permute-done | bytes 442400 | tf_op jit(solution)/shard_map/ppermute | solution.py:786
  102.1 12.6 %collective-permute-done.18.far_ref = bf16[768,256]{1,0:T(8,128)(2,1)} collective-permute-done((bf16[768,256]{1,0:T(8,128)(2,1)S(1)}, bf16[768,256]{1,0:T(8,128)(2,1)}, u32[]{:S(2)}, u32[]{:S(2)}) %collective-permute-start.18) | collective-permute-done | bytes 393248 | tf_op jit(solution)/shard_map/ppermute | solution.py:808
  116.3 6.3 %attend.2.rest_0_ = bf16[384,256]{1,0:T(8,128)(2,1)S(1)} custom-call(s32[1]{0:T(128)} %bitcast.16.seq_ref, bf16[768,256]{1,0:T(8,128)(2,1)S(1)} %queries.1.q_ref, s32[1,768]{1,0:T(1,128)S(1)} %broadcast_in_dim.21.id_ref, bf16[784,256]{1,0:T(8,128)(2,1)S(1)} %get-tuple-element.45.refs_3_.after_ref.rest_2_, ...), custom_call_target="tpu_custom_call" | custom-call | flops 905969664 | bytes 2359296 | tf_op jit(solution)/shard_map/attend/pallas_call | solution.py:564
  122.6 1.9 %collective-permute-start.21 = (bf16[384,256]{1,0:T(8,128)(2,1)S(1)}, bf16[384,256]{1,0:T(8,128)(2,1)S(1)}, u32[]{:S(2)}, u32[]{:S(2)}) collective-permute-start(bf16[384,256]{1,0:T(8,128)(2,1)S(1)} %attend.2.rest_0_), channel_id=1, source_target_pairs={{0,1},{1,0},{2,3},{3,2},{4,5},{5,4},{6,7},{7,6},{8,9},{9,8},{10,11... | collective-permute-start | bytes 589832 | tf_op jit(solution)/shard_map/ppermute | solution.py:835
  126.0 7.3 %attend.3.rest_2_.after_ref.rest_0_ = bf16[384,256]{1,0:T(8,128)(2,1)S(1)} custom-call(s32[1]{0:T(128)} %bitcast.16.seq_ref, bf16[768,256]{1,0:T(8,128)(2,1)S(1)} %queries.1.q_ref, s32[1,768]{1,0:T(1,128)S(1)} %broadcast_in_dim.21.id_ref, bf16[3,256,1152]{2,1,0:T(8,128)(2,1)S(1)} %lay.1.after_ref.o_ref, ...), custom_call_target="tpu_custom_call" | custom-call | flops 905969664 | bytes 2359296 | tf_op jit(solution)/shard_map/attend/pallas_call | solution.py:564
  133.6 2.9 %collective-permute-start.25 = (bf16[384,256]{1,0:T(8,128)(2,1)S(1)}, bf16[384,256]{1,0:T(8,128)(2,1)S(1)}, u32[]{:S(2)}, u32[]{:S(2)}) collective-permute-start(bf16[384,256]{1,0:T(8,128)(2,1)S(1)} %attend.3.rest_2_.after_ref.rest_0_), channel_id=1, source_target_pairs={{0,2},{1,3},{2,0},{3,1},{4,6},{5,7},{6,4},{7,5},{8,10},{9,11},{10,... | collective-permute-start | bytes 589832 | tf_op jit(solution)/shard_map/ppermute | solution.py:834
  136.6 3.2 %first_output.2.part_ref = f32[384,1152]{1,0:T(8,128)S(1)} custom-call(s32[2]{0:T(128)S(1)} %pad_add_fusion.1.at_ref, bf16[256,4608]{1,0:T(8,128)(2,1)} %own_o_ref.3, bf16[3,256,1152]{2,1,0:T(8,128)(2,1)S(1)} %lay.1.after_ref.o_ref, bf16[384,256]{1,0:T(8,128)(2,1)S(1)} %attend.2.rest_0_, bf16[384,256]{1,0:T(8,128)(2,1)S(1)} %collective-permute-done.21.rest_1_, ...), custom_call_target="tpu_custom_call" | custom-call | flops 49999998976 | bytes 100000000 | tf_op jit(solution)/shard_map/first_output/pallas_call | solution.py:639
  139.8 2.1 %collective-permute-done.25.rest_0_ = bf16[384,256]{1,0:T(8,128)(2,1)S(1)} collective-permute-done((bf16[384,256]{1,0:T(8,128)(2,1)S(1)}, bf16[384,256]{1,0:T(8,128)(2,1)S(1)}, u32[]{:S(2)}, u32[]{:S(2)}) %collective-permute-start.25) | collective-permute-done | bytes 196640 | tf_op jit(solution)/shard_map/ppermute | solution.py:834
  142.0 2.7 %collective-permute-start.26 = (bf16[384,256]{1,0:T(8,128)(2,1)S(1)}, bf16[384,256]{1,0:T(8,128)(2,1)S(1)}, u32[]{:S(2)}, u32[]{:S(2)}) collective-permute-start(bf16[384,256]{1,0:T(8,128)(2,1)S(1)} %collective-permute-done.25.rest_0_), channel_id=1, source_target_pairs={{0,1},{1,0},{2,3},{3,2},{4,5},{5,4},{6,7},{7,6},{8,9},{9,8},{10,11... | collective-permute-start | bytes 589832 | tf_op jit(solution)/shard_map/ppermute | solution.py:838
  144.7 3.2 %first_output.3.part_ref = f32[384,1152]{1,0:T(8,128)S(1)} custom-call(s32[2]{0:T(128)S(1)} %pad_add_fusion.1.at_ref, bf16[256,4608]{1,0:T(8,128)(2,1)} %own_o_ref.3, bf16[3,256,1152]{2,1,0:T(8,128)(2,1)S(1)} %lay.1.after_ref.o_ref, bf16[384,256]{1,0:T(8,128)(2,1)S(1)} %attend.3.rest_2_.after_ref.rest_0_, ...), custom_call_target="tpu_custom_call" | custom-call | flops 49999998976 | bytes 100000000 | tf_op jit(solution)/shard_map/first_output/pallas_call | solution.py:639
  147.9 2.5 %last_output.2 = (f32[384,1152]{1,0:T(8,128)S(1)}, f32[1,384]{1,0:T(1,128)S(1)}) custom-call(s32[2]{0:T(128)S(1)} %pad_add_fusion.at_ref, f32[384,1152]{1,0:T(8,128)S(1)} %first_output.2.part_ref, bf16[3,256,1152]{2,1,0:T(8,128)(2,1)S(1)} %lay.1.after_ref.o_ref, bf16[384,256]{1,0:T(8,128)(2,1)S(1)} %gate.5.rest_0_, ...), custom_call_target="tpu_custom_call" | custom-call | tf_op jit(solution)/shard_map/last_output/pallas_call | solution.py:663
  150.5 2.5 %last_output.3 = (f32[384,1152]{1,0:T(8,128)S(1)}, f32[1,768]{1,0:T(1,128)S(1)}) custom-call(s32[2]{0:T(128)S(1)} %pad_add_fusion.at_ref, f32[384,1152]{1,0:T(8,128)S(1)} %first_output.3.part_ref, bf16[3,256,1152]{2,1,0:T(8,128)(2,1)S(1)} %lay.1.after_ref.o_ref, bf16[384,256]{1,0:T(8,128)(2,1)S(1)} %collective-permute-done.25.rest_0_, ...), custom_call_target="tpu_custom_call" | custom-call | tf_op jit(solution)/shard_map/last_output/pallas_call | solution.py:663
  153.1 2.7 %collective-permute-start.28 = (f32[1,768]{1,0:T(1,128)S(1)}, f32[1,768]{1,0:T(1,128)S(1)}, u32[]{:S(2)}, u32[]{:S(2)}) collective-permute-start(f32[1,768]{1,0:T(1,128)S(1)} %get-tuple-element.50.rest_2_), channel_id=1, source_target_pairs={{0,2},{1,3},{2,0},{3,1},{4,6},{5,7},{6,4},{7,5},{8,10},{9,11},{10,... | collective-permute-start | bytes 9224 | tf_op jit(solution)/shard_map/ppermute | solution.py:853
  159.4 3.2 %finish.1 = bf16[768,1152]{1,0:T(8,128)(2,1)} custom-call(bf16[768,1152]{1,0:T(8,128)(2,1)S(1)} %copy-done, f32[1,1152]{1,0:T(1,128)S(1)} %broadcast_in_dim.17.gain_ref, f32[384,1152]{1,0:T(8,128)S(1)} %get-tuple-element.47.rest_0_, f32[384,1152]{1,0:T(8,128)S(1)} %get-tuple-element.49.rest_1_, f32[1,768]{1,0:T(1,128)S(1)} %get-tuple-element.50.rest_2_, ...), custom_call_target="tpu_custom_call" | custom-call | tf_op jit(solution)/shard_map/finish/pallas_call | solution.py:704
  (101 shorter events, 33.4 us)
Async XLA Ops:
  2.1 12.2 %collective-permute-start.10 = (bf16[128,1152]{1,0:T(8,128)(2,1)}, bf16[128,1152]{1,0:T(8,128)(2,1)S(1)}, u32[]{:S(2)}, u32[]{:S(2)}) collective-permute-start(bf16[128,1152]{1,0:T(8,128)(2,1)} %get-tuple-element.35), channel_id=1, source_target_pairs={{0,1},{1,0},{2,3},{3,2},{4,5},{5,4},{6,7},{7,6},{8,9},{9,8},{10,11... | collective-permute-start | bytes 884744 | tf_op jit(solution)/shard_map/ppermute | solution.py:752
  3.7 9.7 %collective-permute-start = (bf16[288,256]{1,0:T(8,128)(2,1)}, bf16[288,256]{1,0:T(8,128)(2,1)S(1)}, u32[]{:S(2)}, u32[]{:S(2)}) collective-permute-start(bf16[288,256]{1,0:T(8,128)(2,1)} %get-tuple-element.28), channel_id=1, source_target_pairs={{0,2},{1,3},{2,0},{3,1},{4,6},{5,7},{6,4},{7,5},{8,10},{9,11},{10,... | collective-permute-start | bytes 442376 | tf_op jit(solution)/shard_map/ppermute | solution.py:750
  14.3 30.7 %copy-start.10 = (bf16[128,1152]{1,0:T(8,128)(2,1)}, bf16[128,1152]{1,0:T(8,128)(2,1)S(1)}, u32[]{:S(2)}) copy-start(bf16[128,1152]{1,0:T(8,128)(2,1)S(1)} %collective-permute-done.10.refs_2_.rest_0_) | copy-start | bytes 884740
  15.3 46.5 %collective-permute-start.11 = (bf16[352,1152]{1,0:T(8,128)(2,1)}, bf16[352,1152]{1,0:T(8,128)(2,1)S(1)}, u32[]{:S(2)}, u32[]{:S(2)}) collective-permute-start(bf16[352,1152]{1,0:T(8,128)(2,1)} %stage.6), channel_id=1, source_target_pairs={{0,1},{1,0},{2,3},{3,2},{4,5},{5,4},{6,7},{7,6},{8,9},{9,8},{10,11... | collective-permute-start | bytes 2433032 | tf_op jit(solution)/shard_map/ppermute | solution.py:773
  17.9 19.8 %collective-permute-start.6 = (bf16[288,256]{1,0:T(8,128)(2,1)S(1)}, bf16[288,256]{1,0:T(8,128)(2,1)S(1)}, u32[]{:S(2)}, u32[]{:S(2)}) collective-permute-start(bf16[288,256]{1,0:T(8,128)(2,1)S(1)} %copy-done.17), channel_id=1, source_target_pairs={{0,2},{1,3},{2,0},{3,1},{4,6},{5,7},{6,4},{7,5},{8,10},{9,11},{10,... | collective-permute-start | bytes 442376 | tf_op jit(solution)/shard_map/ppermute | solution.py:751
  19.5 19.8 %collective-permute-start.5 = (bf16[1,288,256]{2,1,0:T(8,128)(2,1)S(1)}, bf16[1,288,256]{2,1,0:T(8,128)(2,1)S(1)}, u32[]{:S(2)}, u32[]{:S(2)}) collective-permute-start(bf16[1,288,256]{2,1,0:T(8,128)(2,1)S(1)} %bitcast.19), channel_id=1, source_target_pairs={{0,8},{4,12},{8,0},{12,4},{16,24},{20,28},{24,16},{28,20},{1,9},{5... | collective-permute-start | bytes 442376 | tf_op jit(solution)/shard_map/ppermute | solution.py:775
  37.8 5.1 %collective-permute-start.7 = (bf16[1,288,256]{2,1,0:T(8,128)(2,1)S(1)}, bf16[1,288,256]{2,1,0:T(8,128)(2,1)S(1)}, u32[]{:S(2)}, u32[]{:S(2)}) collective-permute-start(bf16[1,288,256]{2,1,0:T(8,128)(2,1)S(1)} %bitcast.22), channel_id=1, source_target_pairs={{0,16},{4,20},{8,24},{12,28},{16,0},{20,4},{24,8},{28,12},{1,17},{... | collective-permute-start | bytes 442376 | tf_op jit(solution)/shard_map/ppermute | solution.py:776
  45.0 16.8 %collective-permute-start.8 = (bf16[2,288,256]{2,1,0:T(8,128)(2,1)}, bf16[2,288,256]{2,1,0:T(8,128)(2,1)}, u32[]{:S(2)}, u32[]{:S(2)}) collective-permute-start(bf16[2,288,256]{2,1,0:T(8,128)(2,1)} %get-tuple-element.33.refs_0_), channel_id=1, source_target_pairs={{0,16},{4,20},{8,24},{12,28},{16,0},{20,4},{24,8},{28,12},{1,17},{... | collective-permute-start | bytes 884744 | tf_op jit(solution)/shard_map/ppermute | solution.py:775
  46.6 15.2 %collective-permute-start.9 = (bf16[2,288,256]{2,1,0:T(8,128)(2,1)}, bf16[2,288,256]{2,1,0:T(8,128)(2,1)}, u32[]{:S(2)}, u32[]{:S(2)}) collective-permute-start(bf16[2,288,256]{2,1,0:T(8,128)(2,1)} %get-tuple-element.34.refs_2_), channel_id=1, source_target_pairs={{0,8},{4,12},{8,0},{12,4},{16,24},{20,28},{24,16},{28,20},{1,9},{5... | collective-permute-start | bytes 884744 | tf_op jit(solution)/shard_map/ppermute | solution.py:776
  49.5 7.1 %collective-permute-start.1 = (bf16[32,1152]{1,0:T(8,128)(2,1)S(1)}, bf16[32,1152]{1,0:T(8,128)(2,1)S(1)}, u32[]{:S(2)}, u32[]{:S(2)}) collective-permute-start(bf16[32,1152]{1,0:T(8,128)(2,1)S(1)} %get-tuple-element.29), channel_id=1, source_target_pairs={{0,1},{1,2},{2,3},{3,0},{4,5},{5,6},{6,7},{7,4},{8,9},{9,10},{10,1... | collective-permute-start | bytes 221192 | tf_op jit(solution)/shard_map/ppermute | solution.py:756
  51.9 5.4 %collective-permute-start.2 = (bf16[32,1152]{1,0:T(8,128)(2,1)S(1)}, bf16[32,1152]{1,0:T(8,128)(2,1)S(1)}, u32[]{:S(2)}, u32[]{:S(2)}) collective-permute-start(bf16[32,1152]{1,0:T(8,128)(2,1)S(1)} %get-tuple-element.30), channel_id=1, source_target_pairs={{0,2},{1,3},{2,0},{3,1},{4,6},{5,7},{6,4},{7,5},{8,10},{9,11},{10,... | collective-permute-start | bytes 221192 | tf_op jit(solution)/shard_map/ppermute | solution.py:756
  56.6 5.2 %collective-permute-start.3 = (bf16[32,1152]{1,0:T(8,128)(2,1)S(1)}, bf16[32,1152]{1,0:T(8,128)(2,1)S(1)}, u32[]{:S(2)}, u32[]{:S(2)}) collective-permute-start(bf16[32,1152]{1,0:T(8,128)(2,1)S(1)} %get-tuple-element.31), channel_id=1, source_target_pairs={{0,3},{1,0},{2,1},{3,2},{4,7},{5,4},{6,5},{7,6},{8,11},{9,8},{10,9... | collective-permute-start | bytes 221192 | tf_op jit(solution)/shard_map/ppermute | solution.py:756
  57.3 14.1 %collective-permute-start.13 = (bf16[288,1152]{1,0:T(8,128)(2,1)}, bf16[288,1152]{1,0:T(8,128)(2,1)S(1)}, u32[]{:S(2)}, u32[]{:S(2)}) collective-permute-start(bf16[288,1152]{1,0:T(8,128)(2,1)} %get-tuple-element.40), channel_id=1, source_target_pairs={{0,1},{1,0},{2,3},{3,2},{4,5},{5,4},{6,7},{7,6},{8,9},{9,8},{10,11... | collective-permute-start | bytes 1990664 | tf_op jit(solution)/shard_map/ppermute | solution.py:773
  64.4 2.5 %collective-permute-start.12 = (bf16[4,288,256]{2,1,0:T(8,128)(2,1)}, bf16[4,288,256]{2,1,0:T(8,128)(2,1)}, u32[]{:S(2)}, u32[]{:S(2)}) collective-permute-start(bf16[4,288,256]{2,1,0:T(8,128)(2,1)} %get-tuple-element.36.own_ref), channel_id=1, source_target_pairs={{0,4},{4,0},{8,12},{12,8},{16,20},{20,16},{24,28},{28,24},{1,5},{5... | collective-permute-start | bytes 1769480 | tf_op jit(solution)/shard_map/ppermute | solution.py:775
  64.5 6.9 %collective-permute-start.14 = (bf16[4,288,256]{2,1,0:T(8,128)(2,1)}, bf16[4,288,256]{2,1,0:T(8,128)(2,1)S(1)}, u32[]{:S(2)}, u32[]{:S(2)}) collective-permute-start(bf16[4,288,256]{2,1,0:T(8,128)(2,1)} %get-tuple-element.41.own_ref), channel_id=1, source_target_pairs={{0,4},{4,0},{8,12},{12,8},{16,20},{20,16},{24,28},{28,24},{1,5},{5... | collective-permute-start | bytes 1769480 | tf_op jit(solution)/shard_map/ppermute | solution.py:776
  75.1 18.8 %collective-permute-start.16 = (bf16[784,256]{1,0:T(8,128)(2,1)S(1)}, bf16[784,256]{1,0:T(8,128)(2,1)S(1)}, u32[]{:S(2)}, u32[]{:S(2)}) collective-permute-start(bf16[784,256]{1,0:T(8,128)(2,1)S(1)} %get-tuple-element.43.rest_0_), channel_id=1, source_target_pairs={{0,2},{1,3},{2,0},{3,1},{4,6},{5,7},{6,4},{7,5},{8,10},{9,11},{10,... | collective-permute-start | bytes 1204232 | tf_op jit(solution)/shard_map/ppermute | solution.py:799
  76.4 13.6 %collective-permute-start.4 = (bf16[1,3,32,1152]{3,2,1,0:T(8,128)(2,1)S(1)}, bf16[1,3,32,1152]{3,2,1,0:T(8,128)(2,1)S(1)}, u32[]{:S(2)}, u32[]{:S(2)}) collective-permute-start(bf16[1,3,32,1152]{3,2,1,0:T(8,128)(2,1)S(1)} %maximum_bitcast_fusion.refs_0_), channel_id=1, source_target_pairs={{0,8},{4,12},{8,0},{12,4},{16,24},{20,28},{24,16},{28,20},{1,9},{5... | collective-permute-start | bytes 663560 | tf_op jit(solution)/shard_map/ppermute | solution.py:786
  90.6 10.1 %collective-permute-start.15 = (bf16[2,3,32,1152]{3,2,1,0:T(8,128)(2,1)S(1)}, bf16[2,3,32,1152]{3,2,1,0:T(8,128)(2,1)}, u32[]{:S(2)}, u32[]{:S(2)}) collective-permute-start(bf16[2,3,32,1152]{3,2,1,0:T(8,128)(2,1)S(1)} %stage.8.rest_1_.refs_0_), channel_id=1, source_target_pairs={{0,16},{4,20},{8,24},{12,28},{16,0},{20,4},{24,8},{28,12},{1,17},{... | collective-permute-start | bytes 1327112 | tf_op jit(solution)/shard_map/ppermute | solution.py:786
  94.4 20.3 %collective-permute-start.18 = (bf16[768,256]{1,0:T(8,128)(2,1)S(1)}, bf16[768,256]{1,0:T(8,128)(2,1)}, u32[]{:S(2)}, u32[]{:S(2)}) collective-permute-start(bf16[768,256]{1,0:T(8,128)(2,1)S(1)} %gate.4), channel_id=1, source_target_pairs={{0,2},{1,3},{2,0},{3,1},{4,6},{5,7},{6,4},{7,5},{8,10},{9,11},{10,... | collective-permute-start | bytes 1179656 | tf_op jit(solution)/shard_map/ppermute | solution.py:808
  94.6 20.2 %copy-start.9 = (f32[768,128]{1,0:T(8,128)S(1)}, f32[768,128]{1,0:T(8,128)}, u32[]{:S(2)}) copy-start(f32[768,128]{1,0:T(8,128)} %copy-done.8) | copy-start | bytes 1179652
  94.6 21.7 %collective-permute-start.19 = (bf16[784,256]{1,0:T(8,128)(2,1)S(1)}, bf16[784,256]{1,0:T(8,128)(2,1)S(1)}, u32[]{:S(2)}, u32[]{:S(2)}) collective-permute-start(bf16[784,256]{1,0:T(8,128)(2,1)S(1)} %get-tuple-element.45.refs_3_.after_ref.rest_2_), channel_id=1, source_target_pairs={{0,8},{4,12},{1,9},{5,13},{2,10},{6,14},{3,11},{7,15},{16,24},{20,... | collective-permute-start | bytes 1204232 | tf_op jit(solution)/shard_map/ppermute | solution.py:822
  96.0 20.3 %collective-permute-start.20 = (bf16[784,256]{1,0:T(8,128)(2,1)S(1)}, bf16[784,256]{1,0:T(8,128)(2,1)S(1)}, u32[]{:S(2)}, u32[]{:S(2)}) collective-permute-start(bf16[784,256]{1,0:T(8,128)(2,1)S(1)} %get-tuple-element.45.refs_3_.after_ref.rest_2_), channel_id=1, source_target_pairs={{0,4},{4,8},{8,12},{1,5},{5,9},{9,13},{2,6},{6,10},{10,14},{3,7},{... | collective-permute-start | bytes 1204232 | tf_op jit(solution)/shard_map/ppermute | solution.py:822
  102.0 22.6 %collective-permute-start.17 = (bf16[4,3,32,1152]{3,2,1,0:T(8,128)(2,1)S(1)}, bf16[4,3,32,1152]{3,2,1,0:T(8,128)(2,1)S(1)}, u32[]{:S(2)}, u32[]{:S(2)}) collective-permute-start(bf16[4,3,32,1152]{3,2,1,0:T(8,128)(2,1)S(1)} %stage.9.own_ref), channel_id=1, source_target_pairs={{0,4},{4,0},{8,12},{12,8},{16,20},{20,16},{24,28},{28,24},{1,5},{5... | collective-permute-start | bytes 2654216 | tf_op jit(solution)/shard_map/ppermute | solution.py:786
  122.6 13.9 %collective-permute-start.22 = (bf16[384,256]{1,0:T(8,128)(2,1)S(1)}, bf16[384,256]{1,0:T(8,128)(2,1)S(1)}, u32[]{:S(2)}, u32[]{:S(2)}) collective-permute-start(bf16[384,256]{1,0:T(8,128)(2,1)S(1)} %attend.2.rest_0_), channel_id=1, source_target_pairs={{0,2},{1,3},{2,0},{3,1},{4,6},{5,7},{6,4},{7,5},{8,10},{9,11},{10,... | collective-permute-start | bytes 589832 | tf_op jit(solution)/shard_map/ppermute | solution.py:834
  122.6 13.9 %collective-permute-start.21 = (bf16[384,256]{1,0:T(8,128)(2,1)S(1)}, bf16[384,256]{1,0:T(8,128)(2,1)S(1)}, u32[]{:S(2)}, u32[]{:S(2)}) collective-permute-start(bf16[384,256]{1,0:T(8,128)(2,1)S(1)} %attend.2.rest_0_), channel_id=1, source_target_pairs={{0,1},{1,0},{2,3},{3,2},{4,5},{5,4},{6,7},{7,6},{8,9},{9,8},{10,11... | collective-permute-start | bytes 589832 | tf_op jit(solution)/shard_map/ppermute | solution.py:835
  133.4 11.3 %collective-permute-start.24 = (bf16[384,256]{1,0:T(8,128)(2,1)S(1)}, bf16[384,256]{1,0:T(8,128)(2,1)S(1)}, u32[]{:S(2)}, u32[]{:S(2)}) collective-permute-start(bf16[384,256]{1,0:T(8,128)(2,1)S(1)} %attend.3.rest_2_.after_ref.rest_0_), channel_id=1, source_target_pairs={{0,1},{1,0},{2,3},{3,2},{4,5},{5,4},{6,7},{7,6},{8,9},{9,8},{10,11... | collective-permute-start | bytes 589832 | tf_op jit(solution)/shard_map/ppermute | solution.py:835
  133.6 8.3 %collective-permute-start.25 = (bf16[384,256]{1,0:T(8,128)(2,1)S(1)}, bf16[384,256]{1,0:T(8,128)(2,1)S(1)}, u32[]{:S(2)}, u32[]{:S(2)}) collective-permute-start(bf16[384,256]{1,0:T(8,128)(2,1)S(1)} %attend.3.rest_2_.after_ref.rest_0_), channel_id=1, source_target_pairs={{0,2},{1,3},{2,0},{3,1},{4,6},{5,7},{6,4},{7,5},{8,10},{9,11},{10,... | collective-permute-start | bytes 589832 | tf_op jit(solution)/shard_map/ppermute | solution.py:834
  136.5 11.4 %collective-permute-start.23 = (bf16[384,256]{1,0:T(8,128)(2,1)S(1)}, bf16[384,256]{1,0:T(8,128)(2,1)S(1)}, u32[]{:S(2)}, u32[]{:S(2)}) collective-permute-start(bf16[384,256]{1,0:T(8,128)(2,1)S(1)} %gate.5.rest_0_), channel_id=1, source_target_pairs={{0,1},{1,0},{2,3},{3,2},{4,5},{5,4},{6,7},{7,6},{8,9},{9,8},{10,11... | collective-permute-start | bytes 589832 | tf_op jit(solution)/shard_map/ppermute | solution.py:838
  142.0 8.5 %collective-permute-start.26 = (bf16[384,256]{1,0:T(8,128)(2,1)S(1)}, bf16[384,256]{1,0:T(8,128)(2,1)S(1)}, u32[]{:S(2)}, u32[]{:S(2)}) collective-permute-start(bf16[384,256]{1,0:T(8,128)(2,1)S(1)} %collective-permute-done.25.rest_0_), channel_id=1, source_target_pairs={{0,1},{1,0},{2,3},{3,2},{4,5},{5,4},{6,7},{7,6},{8,9},{9,8},{10,11... | collective-permute-start | bytes 589832 | tf_op jit(solution)/shard_map/ppermute | solution.py:838
  153.0 5.4 %collective-permute-start.27 = (f32[1,768]{1,0:T(1,128)S(1)}, f32[1,768]{1,0:T(1,128)S(1)}, u32[]{:S(2)}, u32[]{:S(2)}) collective-permute-start(f32[1,768]{1,0:T(1,128)S(1)} %get-tuple-element.50.rest_2_), channel_id=1, source_target_pairs={{0,1},{1,2},{2,3},{3,0},{4,5},{5,6},{6,7},{7,4},{8,9},{9,10},{10,1... | collective-permute-start | bytes 9224 | tf_op jit(solution)/shard_map/ppermute | solution.py:853
  153.1 5.4 %collective-permute-start.28 = (f32[1,768]{1,0:T(1,128)S(1)}, f32[1,768]{1,0:T(1,128)S(1)}, u32[]{:S(2)}, u32[]{:S(2)}) collective-permute-start(f32[1,768]{1,0:T(1,128)S(1)} %get-tuple-element.50.rest_2_), channel_id=1, source_target_pairs={{0,2},{1,3},{2,0},{3,1},{4,6},{5,7},{6,4},{7,5},{8,10},{9,11},{10,... | collective-permute-start | bytes 9224 | tf_op jit(solution)/shard_map/ppermute | solution.py:853
  155.8 3.6 %collective-permute-start.29 = (f32[1,768]{1,0:T(1,128)S(1)}, f32[1,768]{1,0:T(1,128)S(1)}, u32[]{:S(2)}, u32[]{:S(2)}) collective-permute-start(f32[1,768]{1,0:T(1,128)S(1)} %get-tuple-element.50.rest_2_), channel_id=1, source_target_pairs={{0,3},{1,0},{2,1},{3,2},{4,7},{5,4},{6,5},{7,6},{8,11},{9,8},{10,9... | collective-permute-start | bytes 9224 | tf_op jit(solution)/shard_map/ppermute | solution.py:853
  (16 other events, 125.9 us)

commit v17 on v15

--- a/solution.py
+++ b/solution.py
@@ -826,7 +826,7 @@
     contexts, after = [], own_kv
     for c in range(CHUNKS):
         contexts.append(attend(seq_at, queries, ids, after, kv_blocks, c))
-        after = gathered_o
+        after = contexts[-1]
     early, late = [], []
     for c, context in enumerate(contexts):
         if nz == 4:

time: 148 us -> 152 us (1.027)
  Pallas kernels: 52.7 us -> 57 us
    pallas_call x2, Pallas kernels: 7.01 us -> 11.4 us  [attend(): pl.pallas_call(partial(attention_kernel, back=back, offset=c * rows), out...]
    ppermute x2, waiting for transfers between devices: 2.83 us -> 6.99 us  [per_device(): opposite = lax.ppermute(context, 'tensor', swap)]
    ppermute x2, waiting for transfers between devices: 2.64 us -> 0.01 us  [per_device(): across = lax.ppermute(opposite, 'tensor', pairs)]
    ppermute x2, waiting for transfers between devices: 1.93 us -> 0.01 us  [per_device(): beside = lax.ppermute(context, 'tensor', pairs)]
    ppermute x2, starting transfers between devices: 2.46 us -> 0.55 us  [per_device(): opposite = lax.ppermute(context, 'tensor', swap)]
    ppermute x2, starting transfers between devices: 2.61 us -> 4.5 us  [per_device(): beside = lax.ppermute(context, 'tensor', pairs)]
  transfers between devices with their start and end apart: 30 -> 30, of which waited for: 18 -> 15; matrix products, arithmetic and copies ran while one was open for 1% -> 1% of each run, Pallas kernels for 28% -> 29%
where the time goes in v17:
time: 152 us; the launch traced here: 151 us
  Pallas kernels  57 us (38%)
  waiting for transfers between devices  54.3 us (36%)
  starting transfers between devices  35.3 us (23%)
  other arithmetic  2.09 us (1%)
  local copies, waits for them, and re-layouts  1.77 us (1%)
    ppermute x1, waiting for transfers between devices, per_device(): got_q = lax.ppermute(gate(sent_q, got_kv), 'tensor', swap)  13.6 us
    pallas_call x2, Pallas kernels, attend(): pl.pallas_call(partial(attention_kernel, back=back, offset=c * rows), out...  11.4 us
    ppermute x3, waiting for transfers between devices, per_device(): lax.ppermute(p, 'tensor', turn(k + 1))  8.88 us
    ppermute x1, waiting for transfers between devices, per_device(): own_kv = lax.ppermute(packed_kv, 'tensor', swap)[None]  8.01 us
    pallas_call x5, Pallas kernels, stage(): pl.pallas_call(partial(stage_kernel, pairs=len(joined), first=first, coun...  7.52 us
    ppermute x2, waiting for transfers between devices, per_device(): opposite = lax.ppermute(context, 'tensor', swap)  6.99 us
    pallas_call x2, Pallas kernels, first_output(): pl.pallas_call(first_output_kernel, out_shape=shape((chunk, cols), F32),...  6.48 us
    pallas_call x1, Pallas kernels, near_product(): pl.pallas_call(near_kernel, out_shape=shape((rows, sum(widths)), F32), gr...  6.14 us
  transfers between devices with their start and end apart: 30, of which 15 were waited for; matrix products, arithmetic and copies ran while one was open for 1% of the time, Pallas kernels for 29%

profile of v17, /device:TPU:2, one launch (start us, length us, event | category | flops | bytes accessed | tf_op | source)
XLA Modules:
  0.0 150.9 jit_solution(14375436955301369098)
XLA Ops:
  0.0 2.1 %pack.1 = (bf16[288,256]{1,0:T(8,128)(2,1)}, bf16[288,256]{1,0:T(8,128)(2,1)}, bf16[128,1152]{1,0:T(8,128)(2,1)}) custom-call(s32[1]{0:T(128)} %bitcast.9.at_ref, bf16[4608,256]{1,0:T(8,128)(2,1)} %q_ref.3, bf16[4608,128]{1,0:T(8,128)(2,1)} %k_ref.3, bf16[4608,128]{1,0:T(8,128)(2,1)} %v_ref.3, bf16[768,1152]{1,0:T(8,128)(2,1)} %token_ref.1), custom_call_target="tpu_custom_call" | custom-call | tf_op jit(solution)/shard_map/pack/pallas_call | solution.py:75
  2.1 1.6 %collective-permute-start.10 = (bf16[128,1152]{1,0:T(8,128)(2,1)}, bf16[128,1152]{1,0:T(8,128)(2,1)S(1)}, u32[]{:S(2)}, u32[]{:S(2)}) collective-permute-start(bf16[128,1152]{1,0:T(8,128)(2,1)} %get-tuple-element.35), channel_id=1, source_target_pairs={{0,1},{1,0},{2,3},{3,2},{4,5},{5,4},{6,7},{7,6},{8,9},{9,8},{10,11... | collective-permute-start | bytes 884744 | tf_op jit(solution)/shard_map/ppermute | solution.py:752
  3.7 2.6 %collective-permute-start = (bf16[288,256]{1,0:T(8,128)(2,1)}, bf16[288,256]{1,0:T(8,128)(2,1)S(1)}, u32[]{:S(2)}, u32[]{:S(2)}) collective-permute-start(bf16[288,256]{1,0:T(8,128)(2,1)} %get-tuple-element.28), channel_id=1, source_target_pairs={{0,2},{1,3},{2,0},{3,1},{4,6},{5,7},{6,4},{7,5},{8,10},{9,11},{10,... | collective-permute-start | bytes 442376 | tf_op jit(solution)/shard_map/ppermute | solution.py:750
  6.7 8.0 %collective-permute-done = bf16[288,256]{1,0:T(8,128)(2,1)S(1)} collective-permute-done((bf16[288,256]{1,0:T(8,128)(2,1)}, bf16[288,256]{1,0:T(8,128)(2,1)S(1)}, u32[]{:S(2)}, u32[]{:S(2)}) %collective-permute-start) | collective-permute-done | bytes 147488 | tf_op jit(solution)/shard_map/ppermute | solution.py:750
  14.7 5.0 %collective-permute-done.6 = bf16[288,256]{1,0:T(8,128)(2,1)S(1)} collective-permute-done((bf16[288,256]{1,0:T(8,128)(2,1)}, bf16[288,256]{1,0:T(8,128)(2,1)S(1)}, u32[]{:S(2)}, u32[]{:S(2)}) %collective-permute-start.6) | collective-permute-done | bytes 147488 | tf_op jit(solution)/shard_map/ppermute | solution.py:751
  23.2 3.1 %collective-permute-done.5.refs_1_ = bf16[1,288,256]{2,1,0:T(8,128)(2,1)S(1)} collective-permute-done((bf16[1,288,256]{2,1,0:T(8,128)(2,1)S(1)}, bf16[1,288,256]{2,1,0:T(8,128)(2,1)S(1)}, u32[]{:S(2)}, u32[]{:S(2)}) %collective-permute-start.5) | collective-permute-done | bytes 147488 | tf_op jit(solution)/shard_map/ppermute | solution.py:775
  26.9 2.1 %stage.5 = (bf16[2,288,256]{2,1,0:T(8,128)(2,1)}, bf16[2,288,256]{2,1,0:T(8,128)(2,1)}, bf16[288,1152]{1,0:T(8,128)(2,1)}) custom-call(bf16[1,288,256]{2,1,0:T(8,128)(2,1)S(1)} %bitcast.20, bf16[1,288,256]{2,1,0:T(8,128)(2,1)S(1)} %collective-permute-done.5.refs_1_, bf16[1,288,256]{2,1,0:T(8,128)(2,1)S(1)} %bitcast.24, ...), custom_call_target="tpu_custom_call" | custom-call | tf_op jit(solution)/shard_map/stage/pallas_call | solution.py:130
  32.1 1.7 %copy-done.5 = bf16[256,4608]{1,0:T(8,128)(2,1)S(1)} copy-done((bf16[256,4608]{1,0:T(8,128)(2,1)S(1)}, bf16[256,4608]{1,0:T(8,128)(2,1)}, u32[]{:S(2)}) %copy-start.5) | copy-done | bytes 2359320
  37.2 5.7 %collective-permute-done.1.refs_6_ = bf16[32,1152]{1,0:T(8,128)(2,1)S(1)} collective-permute-done((bf16[32,1152]{1,0:T(8,128)(2,1)S(1)}, bf16[32,1152]{1,0:T(8,128)(2,1)S(1)}, u32[]{:S(2)}, u32[]{:S(2)}) %collective-permute-start.1) | collective-permute-done | bytes 73760 | tf_op jit(solution)/shard_map/ppermute | solution.py:756
  42.9 2.0 %collective-permute-start.13 = (bf16[288,1152]{1,0:T(8,128)(2,1)}, bf16[288,1152]{1,0:T(8,128)(2,1)S(1)}, u32[]{:S(2)}, u32[]{:S(2)}) collective-permute-start(bf16[288,1152]{1,0:T(8,128)(2,1)} %get-tuple-element.40), channel_id=1, source_target_pairs={{0,1},{1,0},{2,3},{3,2},{4,5},{5,4},{6,7},{7,6},{8,9},{9,8},{10,11... | collective-permute-start | bytes 1990664 | tf_op jit(solution)/shard_map/ppermute | solution.py:773
  45.0 3.2 %collective-permute-done.3.refs_8_ = bf16[32,1152]{1,0:T(8,128)(2,1)S(1)} collective-permute-done((bf16[32,1152]{1,0:T(8,128)(2,1)S(1)}, bf16[32,1152]{1,0:T(8,128)(2,1)S(1)}, u32[]{:S(2)}, u32[]{:S(2)}) %collective-permute-start.3) | collective-permute-done | bytes 73760 | tf_op jit(solution)/shard_map/ppermute | solution.py:756
  48.2 2.6 %stage.7 = (bf16[4,288,256]{2,1,0:T(8,128)(2,1)}, bf16[4,288,256]{2,1,0:T(8,128)(2,1)}) custom-call(bf16[2,288,256]{2,1,0:T(8,128)(2,1)} %get-tuple-element.33.refs_0_, bf16[2,288,256]{2,1,0:T(8,128)(2,1)} %collective-permute-done.8.refs_1_, bf16[2,288,256]{2,1,0:T(8,128)(2,1)} %get-tuple-element.34.refs_2_, ...), custom_call_target="tpu_custom_call" | custom-call | flops 49999998976 | bytes 100000000 | tf_op jit(solution)/shard_map/stage/pallas_call | solution.py:130
  51.5 1.7 %collective-permute-done.12.got_ref = bf16[4,288,256]{2,1,0:T(8,128)(2,1)} collective-permute-done((bf16[4,288,256]{2,1,0:T(8,128)(2,1)}, bf16[4,288,256]{2,1,0:T(8,128)(2,1)}, u32[]{:S(2)}, u32[]{:S(2)}) %collective-permute-start.12) | collective-permute-done | bytes 589856 | tf_op jit(solution)/shard_map/ppermute | solution.py:775
  53.2 3.0 %far_own.1 = (bf16[1,768,1152]{2,1,0:T(8,128)(2,1)S(1)}, f32[1,768]{1,0:T(1,128)S(1)}, f32[768,256]{1,0:T(8,128)S(1)}) custom-call(s32[2]{0:T(128)S(1)} %get-tuple-element.55.place_ref, s32[2]{0:T(128)S(1)} %get-tuple-element.54.src_ref, f32[4,1,1152]{2,1,0:T(1,128)S(1)} %reshape.21.gain_ref, bf16[4,288,256]{2,1,0:T(8,128)(2,1)} %get-tuple-element.36.own_ref, ...), custom_call_target="tpu_custom_call" | custom-call | tf_op jit(solution)/shard_map/far_own/pallas_call | solution.py:283
  57.9 3.7 %far_kv.1 = (bf16[784,256]{1,0:T(8,128)(2,1)S(1)}, bf16[1,768,1152]{2,1,0:T(8,128)(2,1)}, f32[1,768]{1,0:T(1,128)S(1)}) custom-call(s32[2]{0:T(128)S(1)} %get-tuple-element.55.place_ref, s32[2]{0:T(128)S(1)} %get-tuple-element.54.src_ref, f32[4,1,1152]{2,1,0:T(1,128)S(1)} %reshape.21.gain_ref, f32[768,256]{1,0:T(8,128)S(1)} %get-tuple-element.38.part_ref, ...), custom_call_target="tpu_custom_call" | custom-call | tf_op jit(solution)/shard_map/far_kv/pallas_call | solution.py:305
  61.6 2.0 %collective-permute-start.16 = (bf16[784,256]{1,0:T(8,128)(2,1)S(1)}, bf16[784,256]{1,0:T(8,128)(2,1)S(1)}, u32[]{:S(2)}, u32[]{:S(2)}) collective-permute-start(bf16[784,256]{1,0:T(8,128)(2,1)S(1)} %get-tuple-element.43.rest_0_), channel_id=1, source_target_pairs={{0,2},{1,3},{2,0},{3,1},{4,6},{5,7},{6,4},{7,5},{8,10},{9,11},{10,... | collective-permute-start | bytes 1204232 | tf_op jit(solution)/shard_map/ppermute | solution.py:799
  65.8 6.1 %near.1.rest_0_.near_ref = f32[768,512]{1,0:T(8,128)S(1)} custom-call(s32[2]{0:T(128)S(1)} %broadcast_add_fusion.src_ref, bf16[1,768,1152]{2,1,0:T(8,128)(2,1)S(1)} %get-tuple-element.37.own_x_ref, bf16[1,768,1152]{2,1,0:T(8,128)(2,1)} %get-tuple-element.42.x_ref, bf16[4608,128]{1,0:T(8,128)(2,1)S(1)} %copy-done.3, bf16[4608,128]{1,0:T(8,128)(2,1)S(1)} %copy-done.4, ...), custom_call_target="tpu_custom_call" | custom-call | tf_op jit(solution)/shard_map/near/pallas_call | solution.py:398
  71.9 4.4 %far.1.refs_3_.rest_0_.x_ref = bf16[768,256]{1,0:T(8,128)(2,1)S(1)} custom-call(s32[2]{0:T(128)S(1)} %get-tuple-element.55.place_ref, s32[2]{0:T(128)S(1)} %get-tuple-element.54.src_ref, bf16[1,768,1152]{2,1,0:T(8,128)(2,1)S(1)} %get-tuple-element.37.own_x_ref, bf16[1,768,1152]{2,1,0:T(8,128)(2,1)} %get-tuple-element.42.x_ref, ...), custom_call_target="tpu_custom_call" | custom-call | tf_op jit(solution)/shard_map/far/pallas_call | solution.py:355
  82.3 2.1 %collective-permute-start.20 = (bf16[784,256]{1,0:T(8,128)(2,1)S(1)}, bf16[784,256]{1,0:T(8,128)(2,1)S(1)}, u32[]{:S(2)}, u32[]{:S(2)}) collective-permute-start(bf16[784,256]{1,0:T(8,128)(2,1)S(1)} %get-tuple-element.45.refs_3_.after_ref.rest_2_), channel_id=1, source_target_pairs={{0,4},{4,8},{8,12},{1,5},{5,9},{9,13},{2,6},{6,10},{10,14},{3,7},{... | collective-permute-start | bytes 1204232 | tf_op jit(solution)/shard_map/ppermute | solution.py:822
  86.9 13.6 %collective-permute-done.18.far_ref = bf16[768,256]{1,0:T(8,128)(2,1)} collective-permute-done((bf16[768,256]{1,0:T(8,128)(2,1)S(1)}, bf16[768,256]{1,0:T(8,128)(2,1)}, u32[]{:S(2)}, u32[]{:S(2)}) %collective-permute-start.18) | collective-permute-done | bytes 393248 | tf_op jit(solution)/shard_map/ppermute | solution.py:808
  102.0 5.1 %attend.2.after_ref.rest_0_ = bf16[384,256]{1,0:T(8,128)(2,1)S(1)} custom-call(s32[1]{0:T(128)} %bitcast.16.seq_ref, bf16[768,256]{1,0:T(8,128)(2,1)S(1)} %queries.1.q_ref, s32[1,768]{1,0:T(1,128)S(1)} %broadcast_in_dim.21.id_ref, bf16[784,256]{1,0:T(8,128)(2,1)S(1)} %get-tuple-element.45.refs_3_.after_ref.rest_2_, ...), custom_call_target="tpu_custom_call" | custom-call | flops 905969664 | bytes 2359296 | tf_op jit(solution)/shard_map/attend/pallas_call | solution.py:564
  107.2 6.2 %attend.3.rest_2_.after_ref.rest_0_ = bf16[384,256]{1,0:T(8,128)(2,1)S(1)} custom-call(s32[1]{0:T(128)} %bitcast.16.seq_ref, bf16[768,256]{1,0:T(8,128)(2,1)S(1)} %queries.1.q_ref, s32[1,768]{1,0:T(1,128)S(1)} %broadcast_in_dim.21.id_ref, bf16[384,256]{1,0:T(8,128)(2,1)S(1)} %attend.2.after_ref.rest_0_, ...), custom_call_target="tpu_custom_call" | custom-call | flops 905969664 | bytes 2359296 | tf_op jit(solution)/shard_map/attend/pallas_call | solution.py:564
  113.5 2.6 %collective-permute-start.24 = (bf16[384,256]{1,0:T(8,128)(2,1)S(1)}, bf16[384,256]{1,0:T(8,128)(2,1)S(1)}, u32[]{:S(2)}, u32[]{:S(2)}) collective-permute-start(bf16[384,256]{1,0:T(8,128)(2,1)S(1)} %attend.3.rest_2_.after_ref.rest_0_), channel_id=1, source_target_pairs={{0,1},{1,0},{2,3},{3,2},{4,5},{5,4},{6,7},{7,6},{8,9},{9,8},{10,11... | collective-permute-start | bytes 589832 | tf_op jit(solution)/shard_map/ppermute | solution.py:835
  116.6 1.9 %collective-permute-start.21 = (bf16[384,256]{1,0:T(8,128)(2,1)S(1)}, bf16[384,256]{1,0:T(8,128)(2,1)S(1)}, u32[]{:S(2)}, u32[]{:S(2)}) collective-permute-start(bf16[384,256]{1,0:T(8,128)(2,1)S(1)} %attend.2.after_ref.rest_0_), channel_id=1, source_target_pairs={{0,1},{1,0},{2,3},{3,2},{4,5},{5,4},{6,7},{7,6},{8,9},{9,8},{10,11... | collective-permute-start | bytes 589832 | tf_op jit(solution)/shard_map/ppermute | solution.py:835
  120.1 5.5 %collective-permute-done.25.rest_0_ = bf16[384,256]{1,0:T(8,128)(2,1)S(1)} collective-permute-done((bf16[384,256]{1,0:T(8,128)(2,1)S(1)}, bf16[384,256]{1,0:T(8,128)(2,1)S(1)}, u32[]{:S(2)}, u32[]{:S(2)}) %collective-permute-start.25) | collective-permute-done | bytes 196640 | tf_op jit(solution)/shard_map/ppermute | solution.py:834
  125.6 2.9 %collective-permute-start.26 = (bf16[384,256]{1,0:T(8,128)(2,1)S(1)}, bf16[384,256]{1,0:T(8,128)(2,1)S(1)}, u32[]{:S(2)}, u32[]{:S(2)}) collective-permute-start(bf16[384,256]{1,0:T(8,128)(2,1)S(1)} %collective-permute-done.25.rest_0_), channel_id=1, source_target_pairs={{0,1},{1,0},{2,3},{3,2},{4,5},{5,4},{6,7},{7,6},{8,9},{9,8},{10,11... | collective-permute-start | bytes 589832 | tf_op jit(solution)/shard_map/ppermute | solution.py:838
  129.9 3.2 %first_output.3.part_ref = f32[384,1152]{1,0:T(8,128)S(1)} custom-call(s32[2]{0:T(128)S(1)} %pad_add_fusion.1.at_ref, bf16[256,4608]{1,0:T(8,128)(2,1)} %own_o_ref.3, bf16[3,256,1152]{2,1,0:T(8,128)(2,1)S(1)} %lay.1.o_ref, bf16[384,256]{1,0:T(8,128)(2,1)S(1)} %attend.3.rest_2_.after_ref.rest_0_, bf16[384,256]{1,0:T(8,128)(2,1)S(1)} %collective-permute-done.24.rest_1_, ...), custom_call_target="tpu_custom_call" | custom-call | flops 49999998976 | bytes 100000000 | tf_op jit(solution)/shard_map/first_output/pallas_call | solution.py:639
  133.1 3.2 %first_output.2.part_ref = f32[384,1152]{1,0:T(8,128)S(1)} custom-call(s32[2]{0:T(128)S(1)} %pad_add_fusion.1.at_ref, bf16[256,4608]{1,0:T(8,128)(2,1)} %own_o_ref.3, bf16[3,256,1152]{2,1,0:T(8,128)(2,1)S(1)} %lay.1.o_ref, bf16[384,256]{1,0:T(8,128)(2,1)S(1)} %attend.2.after_ref.rest_0_, bf16[384,256]{1,0:T(8,128)(2,1)S(1)} %collective-permute-done.21.rest_1_, ...), custom_call_target="tpu_custom_call" | custom-call | flops 49999998976 | bytes 100000000 | tf_op jit(solution)/shard_map/first_output/pallas_call | solution.py:639
  136.4 2.5 %last_output.2 = (f32[384,1152]{1,0:T(8,128)S(1)}, f32[1,384]{1,0:T(1,128)S(1)}) custom-call(s32[2]{0:T(128)S(1)} %pad_add_fusion.at_ref, f32[384,1152]{1,0:T(8,128)S(1)} %first_output.2.part_ref, bf16[3,256,1152]{2,1,0:T(8,128)(2,1)S(1)} %lay.1.o_ref, bf16[384,256]{1,0:T(8,128)(2,1)S(1)} %gate.5.rest_0_, ...), custom_call_target="tpu_custom_call" | custom-call | tf_op jit(solution)/shard_map/last_output/pallas_call | solution.py:663
  139.0 2.5 %last_output.3 = (f32[384,1152]{1,0:T(8,128)S(1)}, f32[1,768]{1,0:T(1,128)S(1)}) custom-call(s32[2]{0:T(128)S(1)} %pad_add_fusion.at_ref, f32[384,1152]{1,0:T(8,128)S(1)} %first_output.3.part_ref, bf16[3,256,1152]{2,1,0:T(8,128)(2,1)S(1)} %lay.1.o_ref, bf16[384,256]{1,0:T(8,128)(2,1)S(1)} %collective-permute-done.25.rest_0_, ...), custom_call_target="tpu_custom_call" | custom-call | tf_op jit(solution)/shard_map/last_output/pallas_call | solution.py:663
  141.6 2.5 %collective-permute-start.28 = (f32[1,768]{1,0:T(1,128)S(1)}, f32[1,768]{1,0:T(1,128)S(1)}, u32[]{:S(2)}, u32[]{:S(2)}) collective-permute-start(f32[1,768]{1,0:T(1,128)S(1)} %get-tuple-element.50.rest_2_), channel_id=1, source_target_pairs={{0,2},{1,3},{2,0},{3,1},{4,6},{5,7},{6,4},{7,5},{8,10},{9,11},{10,... | collective-permute-start | bytes 9224 | tf_op jit(solution)/shard_map/ppermute | solution.py:853
  147.7 3.2 %finish.1 = bf16[768,1152]{1,0:T(8,128)(2,1)} custom-call(bf16[768,1152]{1,0:T(8,128)(2,1)S(1)} %copy-done, f32[1,1152]{1,0:T(1,128)S(1)} %broadcast_in_dim.17.gain_ref, f32[384,1152]{1,0:T(8,128)S(1)} %get-tuple-element.47.rest_0_, f32[384,1152]{1,0:T(8,128)S(1)} %get-tuple-element.49.rest_1_, f32[1,768]{1,0:T(1,128)S(1)} %get-tuple-element.50.rest_2_, ...), custom_call_target="tpu_custom_call" | custom-call | tf_op jit(solution)/shard_map/finish/pallas_call | solution.py:704
  (95 shorter events, 32.5 us)
Async XLA Ops:
  0.0 19.7 %copy-start = (bf16[768,1152]{1,0:T(8,128)(2,1)S(1)}, bf16[768,1152]{1,0:T(8,128)(2,1)}, u32[]{:S(2)}) copy-start(bf16[768,1152]{1,0:T(8,128)(2,1)} %token_ref.1) | copy-start | bytes 5308420
  2.1 17.6 %collective-permute-start.10 = (bf16[128,1152]{1,0:T(8,128)(2,1)}, bf16[128,1152]{1,0:T(8,128)(2,1)S(1)}, u32[]{:S(2)}, u32[]{:S(2)}) collective-permute-start(bf16[128,1152]{1,0:T(8,128)(2,1)} %get-tuple-element.35), channel_id=1, source_target_pairs={{0,1},{1,0},{2,3},{3,2},{4,5},{5,4},{6,7},{7,6},{8,9},{9,8},{10,11... | collective-permute-start | bytes 884744 | tf_op jit(solution)/shard_map/ppermute | solution.py:752
  3.7 10.9 %collective-permute-start = (bf16[288,256]{1,0:T(8,128)(2,1)}, bf16[288,256]{1,0:T(8,128)(2,1)S(1)}, u32[]{:S(2)}, u32[]{:S(2)}) collective-permute-start(bf16[288,256]{1,0:T(8,128)(2,1)} %get-tuple-element.28), channel_id=1, source_target_pairs={{0,2},{1,3},{2,0},{3,1},{4,6},{5,7},{6,4},{7,5},{8,10},{9,11},{10,... | collective-permute-start | bytes 442376 | tf_op jit(solution)/shard_map/ppermute | solution.py:750
  6.3 13.4 %collective-permute-start.6 = (bf16[288,256]{1,0:T(8,128)(2,1)}, bf16[288,256]{1,0:T(8,128)(2,1)S(1)}, u32[]{:S(2)}, u32[]{:S(2)}) collective-permute-start(bf16[288,256]{1,0:T(8,128)(2,1)} %get-tuple-element.32), channel_id=1, source_target_pairs={{0,2},{1,3},{2,0},{3,1},{4,6},{5,7},{6,4},{7,5},{8,10},{9,11},{10,... | collective-permute-start | bytes 442376 | tf_op jit(solution)/shard_map/ppermute | solution.py:751
  20.7 27.5 %collective-permute-start.11 = (bf16[352,1152]{1,0:T(8,128)(2,1)}, bf16[352,1152]{1,0:T(8,128)(2,1)S(1)}, u32[]{:S(2)}, u32[]{:S(2)}) collective-permute-start(bf16[352,1152]{1,0:T(8,128)(2,1)} %stage.6), channel_id=1, source_target_pairs={{0,1},{1,0},{2,3},{3,2},{4,5},{5,4},{6,7},{7,6},{8,9},{9,8},{10,11... | collective-permute-start | bytes 2433032 | tf_op jit(solution)/shard_map/ppermute | solution.py:773
  21.2 5.1 %collective-permute-start.5 = (bf16[1,288,256]{2,1,0:T(8,128)(2,1)S(1)}, bf16[1,288,256]{2,1,0:T(8,128)(2,1)S(1)}, u32[]{:S(2)}, u32[]{:S(2)}) collective-permute-start(bf16[1,288,256]{2,1,0:T(8,128)(2,1)S(1)} %bitcast.19), channel_id=1, source_target_pairs={{0,8},{4,12},{8,0},{12,4},{16,24},{20,28},{24,16},{28,20},{1,9},{5... | collective-permute-start | bytes 442376 | tf_op jit(solution)/shard_map/ppermute | solution.py:775
  21.7 5.1 %collective-permute-start.7 = (bf16[1,288,256]{2,1,0:T(8,128)(2,1)S(1)}, bf16[1,288,256]{2,1,0:T(8,128)(2,1)S(1)}, u32[]{:S(2)}, u32[]{:S(2)}) collective-permute-start(bf16[1,288,256]{2,1,0:T(8,128)(2,1)S(1)} %bitcast.23), channel_id=1, source_target_pairs={{0,16},{4,20},{8,24},{12,28},{16,0},{20,4},{24,8},{28,12},{1,17},{... | collective-permute-start | bytes 442376 | tf_op jit(solution)/shard_map/ppermute | solution.py:776
  28.9 19.2 %collective-permute-start.8 = (bf16[2,288,256]{2,1,0:T(8,128)(2,1)}, bf16[2,288,256]{2,1,0:T(8,128)(2,1)}, u32[]{:S(2)}, u32[]{:S(2)}) collective-permute-start(bf16[2,288,256]{2,1,0:T(8,128)(2,1)} %get-tuple-element.33.refs_0_), channel_id=1, source_target_pairs={{0,16},{4,20},{8,24},{12,28},{16,0},{20,4},{24,8},{28,12},{1,17},{... | collective-permute-start | bytes 884744 | tf_op jit(solution)/shard_map/ppermute | solution.py:775
  30.5 17.6 %collective-permute-start.9 = (bf16[2,288,256]{2,1,0:T(8,128)(2,1)}, bf16[2,288,256]{2,1,0:T(8,128)(2,1)}, u32[]{:S(2)}, u32[]{:S(2)}) collective-permute-start(bf16[2,288,256]{2,1,0:T(8,128)(2,1)} %get-tuple-element.34.refs_2_), channel_id=1, source_target_pairs={{0,8},{4,12},{8,0},{12,4},{16,24},{20,28},{24,16},{28,20},{1,9},{5... | collective-permute-start | bytes 884744 | tf_op jit(solution)/shard_map/ppermute | solution.py:776
  34.4 8.5 %collective-permute-start.1 = (bf16[32,1152]{1,0:T(8,128)(2,1)S(1)}, bf16[32,1152]{1,0:T(8,128)(2,1)S(1)}, u32[]{:S(2)}, u32[]{:S(2)}) collective-permute-start(bf16[32,1152]{1,0:T(8,128)(2,1)S(1)} %get-tuple-element.29), channel_id=1, source_target_pairs={{0,1},{1,2},{2,3},{3,0},{4,5},{5,6},{6,7},{7,4},{8,9},{9,10},{10,1... | collective-permute-start | bytes 221192 | tf_op jit(solution)/shard_map/ppermute | solution.py:756
  36.0 6.9 %collective-permute-start.2 = (bf16[32,1152]{1,0:T(8,128)(2,1)S(1)}, bf16[32,1152]{1,0:T(8,128)(2,1)S(1)}, u32[]{:S(2)}, u32[]{:S(2)}) collective-permute-start(bf16[32,1152]{1,0:T(8,128)(2,1)S(1)} %get-tuple-element.30), channel_id=1, source_target_pairs={{0,2},{1,3},{2,0},{3,1},{4,6},{5,7},{6,4},{7,5},{8,10},{9,11},{10,... | collective-permute-start | bytes 221192 | tf_op jit(solution)/shard_map/ppermute | solution.py:756
  42.9 5.2 %collective-permute-start.3 = (bf16[32,1152]{1,0:T(8,128)(2,1)S(1)}, bf16[32,1152]{1,0:T(8,128)(2,1)S(1)}, u32[]{:S(2)}, u32[]{:S(2)}) collective-permute-start(bf16[32,1152]{1,0:T(8,128)(2,1)S(1)} %get-tuple-element.31), channel_id=1, source_target_pairs={{0,3},{1,0},{2,1},{3,2},{4,7},{5,4},{6,5},{7,6},{8,11},{9,8},{10,9... | collective-permute-start | bytes 221192 | tf_op jit(solution)/shard_map/ppermute | solution.py:756
  42.9 14.9 %collective-permute-start.13 = (bf16[288,1152]{1,0:T(8,128)(2,1)}, bf16[288,1152]{1,0:T(8,128)(2,1)S(1)}, u32[]{:S(2)}, u32[]{:S(2)}) collective-permute-start(bf16[288,1152]{1,0:T(8,128)(2,1)} %get-tuple-element.40), channel_id=1, source_target_pairs={{0,1},{1,0},{2,3},{3,2},{4,5},{5,4},{6,7},{7,6},{8,9},{9,8},{10,11... | collective-permute-start | bytes 1990664 | tf_op jit(solution)/shard_map/ppermute | solution.py:773
  50.8 2.5 %collective-permute-start.12 = (bf16[4,288,256]{2,1,0:T(8,128)(2,1)}, bf16[4,288,256]{2,1,0:T(8,128)(2,1)}, u32[]{:S(2)}, u32[]{:S(2)}) collective-permute-start(bf16[4,288,256]{2,1,0:T(8,128)(2,1)} %get-tuple-element.36.own_ref), channel_id=1, source_target_pairs={{0,4},{4,0},{8,12},{12,8},{16,20},{20,16},{24,28},{28,24},{1,5},{5... | collective-permute-start | bytes 1769480 | tf_op jit(solution)/shard_map/ppermute | solution.py:775
  50.9 7.0 %collective-permute-start.14 = (bf16[4,288,256]{2,1,0:T(8,128)(2,1)}, bf16[4,288,256]{2,1,0:T(8,128)(2,1)S(1)}, u32[]{:S(2)}, u32[]{:S(2)}) collective-permute-start(bf16[4,288,256]{2,1,0:T(8,128)(2,1)} %get-tuple-element.41.own_ref), channel_id=1, source_target_pairs={{0,4},{4,0},{8,12},{12,8},{16,20},{20,16},{24,28},{28,24},{1,5},{5... | collective-permute-start | bytes 1769480 | tf_op jit(solution)/shard_map/ppermute | solution.py:776
  61.6 18.7 %collective-permute-start.16 = (bf16[784,256]{1,0:T(8,128)(2,1)S(1)}, bf16[784,256]{1,0:T(8,128)(2,1)S(1)}, u32[]{:S(2)}, u32[]{:S(2)}) collective-permute-start(bf16[784,256]{1,0:T(8,128)(2,1)S(1)} %get-tuple-element.43.rest_0_), channel_id=1, source_target_pairs={{0,2},{1,3},{2,0},{3,1},{4,6},{5,7},{6,4},{7,5},{8,10},{9,11},{10,... | collective-permute-start | bytes 1204232 | tf_op jit(solution)/shard_map/ppermute | solution.py:799
  63.7 12.7 %collective-permute-start.4 = (bf16[1,3,32,1152]{3,2,1,0:T(8,128)(2,1)S(1)}, bf16[1,3,32,1152]{3,2,1,0:T(8,128)(2,1)S(1)}, u32[]{:S(2)}, u32[]{:S(2)}) collective-permute-start(bf16[1,3,32,1152]{3,2,1,0:T(8,128)(2,1)S(1)} %maximum_bitcast_fusion.refs_0_), channel_id=1, source_target_pairs={{0,8},{4,12},{8,0},{12,4},{16,24},{20,28},{24,16},{28,20},{1,9},{5... | collective-permute-start | bytes 663560 | tf_op jit(solution)/shard_map/ppermute | solution.py:786
  77.0 8.6 %collective-permute-start.15 = (bf16[2,3,32,1152]{3,2,1,0:T(8,128)(2,1)S(1)}, bf16[2,3,32,1152]{3,2,1,0:T(8,128)(2,1)}, u32[]{:S(2)}, u32[]{:S(2)}) collective-permute-start(bf16[2,3,32,1152]{3,2,1,0:T(8,128)(2,1)S(1)} %stage.8.rest_1_.refs_0_), channel_id=1, source_target_pairs={{0,16},{4,20},{8,24},{12,28},{16,0},{20,4},{24,8},{28,12},{1,17},{... | collective-permute-start | bytes 1327112 | tf_op jit(solution)/shard_map/ppermute | solution.py:786
  80.7 19.8 %collective-permute-start.18 = (bf16[768,256]{1,0:T(8,128)(2,1)S(1)}, bf16[768,256]{1,0:T(8,128)(2,1)}, u32[]{:S(2)}, u32[]{:S(2)}) collective-permute-start(bf16[768,256]{1,0:T(8,128)(2,1)S(1)} %gate.4), channel_id=1, source_target_pairs={{0,2},{1,3},{2,0},{3,1},{4,6},{5,7},{6,4},{7,5},{8,10},{9,11},{10,... | collective-permute-start | bytes 1179656 | tf_op jit(solution)/shard_map/ppermute | solution.py:808
  80.8 19.7 %copy-start.2 = (f32[768,512]{1,0:T(8,128)S(1)}, f32[768,512]{1,0:T(8,128)}, u32[]{:S(2)}) copy-start(f32[768,512]{1,0:T(8,128)} %copy-done.1) | copy-start | bytes 4718596
  80.9 21.1 %collective-permute-start.19 = (bf16[784,256]{1,0:T(8,128)(2,1)S(1)}, bf16[784,256]{1,0:T(8,128)(2,1)S(1)}, u32[]{:S(2)}, u32[]{:S(2)}) collective-permute-start(bf16[784,256]{1,0:T(8,128)(2,1)S(1)} %get-tuple-element.45.refs_3_.after_ref.rest_2_), channel_id=1, source_target_pairs={{0,8},{4,12},{1,9},{5,13},{2,10},{6,14},{3,11},{7,15},{16,24},{20,... | collective-permute-start | bytes 1204232 | tf_op jit(solution)/shard_map/ppermute | solution.py:822
  82.3 19.7 %collective-permute-start.20 = (bf16[784,256]{1,0:T(8,128)(2,1)S(1)}, bf16[784,256]{1,0:T(8,128)(2,1)S(1)}, u32[]{:S(2)}, u32[]{:S(2)}) collective-permute-start(bf16[784,256]{1,0:T(8,128)(2,1)S(1)} %get-tuple-element.45.refs_3_.after_ref.rest_2_), channel_id=1, source_target_pairs={{0,4},{4,8},{8,12},{1,5},{5,9},{9,13},{2,6},{6,10},{10,14},{3,7},{... | collective-permute-start | bytes 1204232 | tf_op jit(solution)/shard_map/ppermute | solution.py:822
  86.8 41.6 %collective-permute-start.17 = (bf16[4,3,32,1152]{3,2,1,0:T(8,128)(2,1)S(1)}, bf16[4,3,32,1152]{3,2,1,0:T(8,128)(2,1)S(1)}, u32[]{:S(2)}, u32[]{:S(2)}) collective-permute-start(bf16[4,3,32,1152]{3,2,1,0:T(8,128)(2,1)S(1)} %stage.9.own_ref), channel_id=1, source_target_pairs={{0,4},{4,0},{8,12},{12,8},{16,20},{20,16},{24,28},{28,24},{1,5},{5... | collective-permute-start | bytes 2654216 | tf_op jit(solution)/shard_map/ppermute | solution.py:786
  107.1 12.9 %collective-permute-start.22 = (bf16[384,256]{1,0:T(8,128)(2,1)S(1)}, bf16[384,256]{1,0:T(8,128)(2,1)S(1)}, u32[]{:S(2)}, u32[]{:S(2)}) collective-permute-start(bf16[384,256]{1,0:T(8,128)(2,1)S(1)} %attend.2.after_ref.rest_0_), channel_id=1, source_target_pairs={{0,2},{1,3},{2,0},{3,1},{4,6},{5,7},{6,4},{7,5},{8,10},{9,11},{10,... | collective-permute-start | bytes 589832 | tf_op jit(solution)/shard_map/ppermute | solution.py:834
  113.5 16.4 %collective-permute-start.24 = (bf16[384,256]{1,0:T(8,128)(2,1)S(1)}, bf16[384,256]{1,0:T(8,128)(2,1)S(1)}, u32[]{:S(2)}, u32[]{:S(2)}) collective-permute-start(bf16[384,256]{1,0:T(8,128)(2,1)S(1)} %attend.3.rest_2_.after_ref.rest_0_), channel_id=1, source_target_pairs={{0,1},{1,0},{2,3},{3,2},{4,5},{5,4},{6,7},{7,6},{8,9},{9,8},{10,11... | collective-permute-start | bytes 589832 | tf_op jit(solution)/shard_map/ppermute | solution.py:835
  116.0 9.6 %collective-permute-start.25 = (bf16[384,256]{1,0:T(8,128)(2,1)S(1)}, bf16[384,256]{1,0:T(8,128)(2,1)S(1)}, u32[]{:S(2)}, u32[]{:S(2)}) collective-permute-start(bf16[384,256]{1,0:T(8,128)(2,1)S(1)} %attend.3.rest_2_.after_ref.rest_0_), channel_id=1, source_target_pairs={{0,2},{1,3},{2,0},{3,1},{4,6},{5,7},{6,4},{7,5},{8,10},{9,11},{10,... | collective-permute-start | bytes 589832 | tf_op jit(solution)/shard_map/ppermute | solution.py:834
  116.6 16.5 %collective-permute-start.21 = (bf16[384,256]{1,0:T(8,128)(2,1)S(1)}, bf16[384,256]{1,0:T(8,128)(2,1)S(1)}, u32[]{:S(2)}, u32[]{:S(2)}) collective-permute-start(bf16[384,256]{1,0:T(8,128)(2,1)S(1)} %attend.2.after_ref.rest_0_), channel_id=1, source_target_pairs={{0,1},{1,0},{2,3},{3,2},{4,5},{5,4},{6,7},{7,6},{8,9},{9,8},{10,11... | collective-permute-start | bytes 589832 | tf_op jit(solution)/shard_map/ppermute | solution.py:835
  120.1 16.3 %collective-permute-start.23 = (bf16[384,256]{1,0:T(8,128)(2,1)S(1)}, bf16[384,256]{1,0:T(8,128)(2,1)S(1)}, u32[]{:S(2)}, u32[]{:S(2)}) collective-permute-start(bf16[384,256]{1,0:T(8,128)(2,1)S(1)} %gate.5.rest_0_), channel_id=1, source_target_pairs={{0,1},{1,0},{2,3},{3,2},{4,5},{5,4},{6,7},{7,6},{8,9},{9,8},{10,11... | collective-permute-start | bytes 589832 | tf_op jit(solution)/shard_map/ppermute | solution.py:838
  125.6 13.4 %collective-permute-start.26 = (bf16[384,256]{1,0:T(8,128)(2,1)S(1)}, bf16[384,256]{1,0:T(8,128)(2,1)S(1)}, u32[]{:S(2)}, u32[]{:S(2)}) collective-permute-start(bf16[384,256]{1,0:T(8,128)(2,1)S(1)} %collective-permute-done.25.rest_0_), channel_id=1, source_target_pairs={{0,1},{1,0},{2,3},{3,2},{4,5},{5,4},{6,7},{7,6},{8,9},{9,8},{10,11... | collective-permute-start | bytes 589832 | tf_op jit(solution)/shard_map/ppermute | solution.py:838
  141.5 5.4 %collective-permute-start.27 = (f32[1,768]{1,0:T(1,128)S(1)}, f32[1,768]{1,0:T(1,128)S(1)}, u32[]{:S(2)}, u32[]{:S(2)}) collective-permute-start(f32[1,768]{1,0:T(1,128)S(1)} %get-tuple-element.50.rest_2_), channel_id=1, source_target_pairs={{0,1},{1,2},{2,3},{3,0},{4,5},{5,6},{6,7},{7,4},{8,9},{9,10},{10,1... | collective-permute-start | bytes 9224 | tf_op jit(solution)/shard_map/ppermute | solution.py:853
  141.6 5.4 %collective-permute-start.28 = (f32[1,768]{1,0:T(1,128)S(1)}, f32[1,768]{1,0:T(1,128)S(1)}, u32[]{:S(2)}, u32[]{:S(2)}) collective-permute-start(f32[1,768]{1,0:T(1,128)S(1)} %get-tuple-element.50.rest_2_), channel_id=1, source_target_pairs={{0,2},{1,3},{2,0},{3,1},{4,6},{5,7},{6,4},{7,5},{8,10},{9,11},{10,... | collective-permute-start | bytes 9224 | tf_op jit(solution)/shard_map/ppermute | solution.py:853
  144.1 3.6 %collective-permute-start.29 = (f32[1,768]{1,0:T(1,128)S(1)}, f32[1,768]{1,0:T(1,128)S(1)}, u32[]{:S(2)}, u32[]{:S(2)}) collective-permute-start(f32[1,768]{1,0:T(1,128)S(1)} %get-tuple-element.50.rest_2_), channel_id=1, source_target_pairs={{0,3},{1,0},{2,1},{3,2},{4,7},{5,4},{6,5},{7,6},{8,11},{9,8},{10,9... | collective-permute-start | bytes 9224 | tf_op jit(solution)/shard_map/ppermute | solution.py:853
  (13 other events, 82.1 us)

commit v18 on v15

--- a/solution.py
+++ b/solution.py
@@ -247,7 +247,7 @@
 
 
 def far_kv_kernel(
-    place_ref, src_ref, gain_ref, part_ref, own_sq_ref, own_ref, got_ref, *rest, order, cuts
+    place_ref, src_ref, gain_ref, part_ref, own_sq_ref, own_ref, got_ref, *rest, order, cuts, first
 ):
     x_refs, (out_ref, x_out, sq_ref, weight, sems) = rest[: sum(cuts)], rest[-5:]
     copies = place_weights(place_ref, own_ref, got_ref, weight, sems, order)
@@ -257,11 +257,12 @@
         gain = gain_ref[place_ref[1] + src_ref[1 + k]]
         columns.append(prepare(x_refs[at : at + pieces], gain, x_out, k))
         at += pieces
-    sq = to_row(sum(columns[1:], columns[0])) + own_sq_ref[...]
+    mine = slice(first, first + rows)
+    sq = to_row(sum(columns[1:], columns[0])) + own_sq_ref[:, mine]
     sq_ref[...] = sq
     for copy in copies:
         copy.wait()
-    total = part_ref[...] + far_sum(src_ref, 1, x_out, weight)
+    total = part_ref[mine, :] + far_sum(src_ref, 1, x_out, weight)
     out_ref[:rows, :] = total.astype(BF16)
     high = sq.astype(BF16).astype(F32)
     out_ref[rows:, :] = lines_of((high, sq - high), out_ref.shape[1])
@@ -295,15 +296,17 @@
     )(place, sources, gains, own, got, tokens)
 
 
-def far_kv_product(place, sources, gains, part, own_sq, blocks, gathered, after):
+def far_kv_product(place, sources, gains, part, own_sq, first, blocks, gathered, after):
     order, own, got = gathered
-    rows, width = part.shape
+    rows, width = sum(piece.shape[0] for piece in blocks[0]), part.shape[1]
     cols = blocks[0][0].shape[1]
     pieces = [piece for block in blocks for piece in block]
     dims = [(rows + TAIL, width), (len(blocks), rows, cols), (1, rows)]
     whole = lambda d: pl.BlockSpec(d, lambda i, p, s: (0,) * len(d))
     return pl.pallas_call(
-        partial(far_kv_kernel, order=order, cuts=[len(block) for block in blocks]),
+        partial(
+            far_kv_kernel, order=order, cuts=[len(block) for block in blocks], first=first
+        ),
         out_shape=tuple(shape(d, t) for d, t in zip(dims, (BF16, BF16, F32))),
         grid_spec=pltpu.PrefetchScalarGridSpec(
             num_scalar_prefetch=2,
@@ -319,12 +322,17 @@
     )(place, sources, gains, part, own_sq, own, got, *pieces, *after)
 
 
-def far_kernel(place_ref, src_ref, own_x_ref, x_ref, own_ref, got_ref, *rest, order):
-    out_ref, weight, sems = rest[-3:]
+def far_kernel(place_ref, src_ref, own_x_ref, own_ref, got_ref, *rest, order, groups):
+    x_refs, (out_ref, weight, sems) = rest[:groups], rest[-3:]
     for copy in place_weights(place_ref, own_ref, got_ref, weight, sems, order):
         copy.wait()
-    total = far_sum(src_ref, 0, own_x_ref, weight) + far_sum(src_ref, 1, x_ref, weight)
-    out_ref[...] = total.astype(BF16)
+    total = far_sum(src_ref, 0, own_x_ref, weight)
+    first = 0
+    for x_ref in x_refs:
+        mine = slice(first, first + x_ref.shape[1])
+        part = total[mine, :] + far_sum(src_ref, 1, x_ref, weight)
+        out_ref[mine, :] = part.astype(BF16)
+        first += x_ref.shape[1]
 
 
 def lines_of(rows, width):
@@ -349,32 +357,29 @@
     return rows
 
 
-def far_product(place, sources, own_x, x, gathered, after):
+def far_product(place, sources, own_x, xs, gathered, after):
     order, own, got = gathered
-    rows, width = x.shape[1], own.shape[2]
-    return pl.pallas_call(
-        partial(far_kernel, order=order),
+    rows, width = own_x.shape[1], own.shape[2]
+    whole = lambda d: pl.BlockSpec(d, lambda i, p, s: (0,) * len(d))
+    return pl.pallas_call(
+        partial(far_kernel, order=order, groups=len(xs)),
         out_shape=shape((rows, width), BF16),
         grid_spec=pltpu.PrefetchScalarGridSpec(
             num_scalar_prefetch=2,
             grid=(1,),
-            in_specs=[
-                pl.BlockSpec(own_x.shape, lambda i, p, s: (0, 0, 0)),
-                pl.BlockSpec(x.shape, lambda i, p, s: (0, 0, 0)),
-                ANY,
-                ANY,
-            ]
+            in_specs=[whole(own_x.shape), ANY, ANY]
+            + [whole(x.shape) for x in xs]
             + [ANY for _ in after],
-            out_specs=pl.BlockSpec((rows, width), lambda i, p, s: (0, 0)),
+            out_specs=whole((rows, width)),
             scratch_shapes=far_kv_scratch(gathered),
         ),
         compiler_params=PARAMS,
         name="far",
-    )(place, sources, own_x, x, own, got, *after)
-
-
-def near_kernel(src_ref, own_x_ref, x_ref, k_ref, v_ref, q_ref, *rest):
-    out_ref = rest[-1]
+    )(place, sources, own_x, own, got, *xs, *after)
+
+
+def near_kernel(src_ref, own_x_ref, k_ref, v_ref, q_ref, *rest, groups):
+    x_refs, out_ref = rest[:groups], rest[-1]
     step = pl.program_id(0)
     dot = partial(jnp.dot, preferred_element_type=F32)
     column = 0
@@ -387,67 +392,81 @@
 
         @pl.when(step > 0)
         def _():
-            out_ref[:, at] += dot(x_ref[0], ref[...])
+            first = 0
+            for x_ref in x_refs:
+                mine = slice(first, first + x_ref.shape[1])
+                out_ref[mine, at] += dot(x_ref[0], ref[...])
+                first += x_ref.shape[1]
 
         column += ref.shape[1]
 
 
-def near_product(sources, own_x, x, weights, after):
-    count, rows, cols = x.shape
+def near_product(sources, own_x, xs, weights, after):
+    count, rows, cols = own_x.shape[0] + xs[0].shape[0], own_x.shape[1], own_x.shape[2]
     widths = [w.shape[1] for w in weights]
     return pl.pallas_call(
-        near_kernel,
+        partial(near_kernel, groups=len(xs)),
         out_shape=shape((rows, sum(widths)), F32),
         grid_spec=pltpu.PrefetchScalarGridSpec(
             num_scalar_prefetch=1,
-            grid=(count + 1,),
-            in_specs=[
-                pl.BlockSpec((1, rows, cols), lambda i, s: (0, 0, 0)),
-                pl.BlockSpec((1, rows, cols), lambda i, s: (jnp.maximum(i - 1, 0), 0, 0)),
+            grid=(count,),
+            in_specs=[pl.BlockSpec((1, rows, cols), lambda i, s: (0, 0, 0))]
+            + [pl.BlockSpec((cols, w), lambda i, s: (s[i], 0)) for w in widths]
+            + [
+                pl.BlockSpec((1,) + x.shape[1:], lambda i, s: (jnp.maximum(i - 1, 0), 0, 0))
+                for x in xs
             ]
-            + [pl.BlockSpec((cols, w), lambda i, s: (s[i], 0)) for w in widths]
             + [ANY for _ in after],
             out_specs=pl.BlockSpec((rows, sum(widths)), lambda i, s: (0, 0)),
         ),
         compiler_params=PARAMS,
         name="near",
-    )(sources, own_x, x, *weights, *after)
-
-
-def keys_kernel(near_ref, far_ref, sq_ref, id_ref, cos_ref, sin_ref, *rest, model):
+    )(sources, own_x, *weights, *xs, *after)
+
+
+def keys_kernel(near_ref, id_ref, cos_ref, sin_ref, *rest, model, groups):
+    far_refs, sq_refs = rest[:groups], rest[groups : 2 * groups]
     out_ref, sum_ref = rest[-2:]
-    rows, width = near_ref.shape[0], far_ref.shape[1]
-    tail = far_ref[rows:, :].astype(F32)
-    total = sum(rows_of(tail, 2, rows), sq_ref[...])
-    factor = to_column(lax.rsqrt(total / model + epsilon))
-    sum_ref[...] = total
+    rows, width = near_ref.shape[0], out_ref.shape[1]
     keys, values = slice(0, HEAD_SIZE), slice(HEAD_SIZE, 2 * HEAD_SIZE)
-    part = (near_ref[:, keys] + far_ref[:rows, keys].astype(F32)) * factor
-    part = rotate(part, cos_ref[...], sin_ref[...]).astype(BF16)
+    key_parts, value_parts, first = [], [], 0
+    for far_ref, sq_ref in zip(far_refs, sq_refs):
+        count = sq_ref.shape[1]
+        at = slice(first, first + count)
+        tail = far_ref[count:, :].astype(F32)
+        total = sum(rows_of(tail, 2, count), sq_ref[...])
+        factor = to_column(lax.rsqrt(total / model + epsilon))
+        sum_ref[:, at] = total
+        part = (near_ref[at, keys] + far_ref[:count, keys].astype(F32)) * factor
+        key_parts.append(rotate(part, cos_ref[at, :], sin_ref[at, :]).astype(BF16))
+        part = (near_ref[at, values] + far_ref[:count, values].astype(F32)) * factor
+        value_parts.append(part.T.astype(BF16))
+        first += count
+    part = jnp.concatenate(key_parts, axis=0)
     out_ref[: rows // 2, keys] = part[: rows // 2]
     out_ref[: rows // 2, values] = part[rows // 2 :]
-    part = (near_ref[:, values] + far_ref[:rows, values].astype(F32)) * factor
-    part = part.T.astype(BF16)
+    part = jnp.concatenate(value_parts, axis=1)
     for i, at in enumerate(range(0, rows, width)):
         row = rows // 2 + i * HEAD_SIZE
         out_ref[row : row + HEAD_SIZE, :] = part[:, at : at + width]
     out_ref[rows:, :] = lines_of((id_ref[...].astype(F32),), width)
 
 
-def keys_values(near, far, sq, ids, cosine, sine, after, model):
-    rows, width = near.shape[0], far.shape[1]
+def keys_values(near, fars, sqs, ids, cosine, sine, after, model):
+    rows, width = near.shape[0], fars[0].shape[1]
     whole = lambda i: (0, 0)
-    return pl.pallas_call(
-        partial(keys_kernel, model=model),
-        out_shape=(shape(far.shape, BF16), shape(sq.shape, F32)),
+    dims = [(rows + TAIL, width), (1, rows)]
+    return pl.pallas_call(
+        partial(keys_kernel, model=model, groups=len(fars)),
+        out_shape=tuple(shape(d, t) for d, t in zip(dims, (BF16, F32))),
         grid=(1,),
         in_specs=[pl.BlockSpec((rows, width), whole)]
-        + [pl.BlockSpec(a.shape, whole) for a in (far, sq, ids, cosine, sine)]
+        + [pl.BlockSpec(a.shape, whole) for a in (ids, cosine, sine, *fars, *sqs)]
         + [ANY for _ in after],
-        out_specs=[pl.BlockSpec(far.shape, whole), pl.BlockSpec(sq.shape, whole)],
+        out_specs=[pl.BlockSpec(d, whole) for d in dims],
         compiler_params=PARAMS,
         name="keys",
-    )(near, far, sq, ids, cosine, sine, *after)
+    )(near, ids, cosine, sine, *fars, *sqs, *after)
 
 
 def queries_kernel(near_ref, far_ref, sum_ref, cos_ref, sin_ref, out_ref, *, model):
@@ -743,7 +762,7 @@
     masks_kv, masks_q = inner + [1], inner[::-1] + [1]
     last = len(masks_kv) - 1
     eighth = rows // 48 * 8
-    counts = [eighth, rows // 2 - 2 * TAIL, rows // 2 + 2 * TAIL - eighth]
+    counts = [eighth, rows // 2 - eighth, rows // 2]
     packed_kv, packed_q, cut = pack(
         at, q_weight, k_weight, value_weight, share, tokens, counts[0]
     )
@@ -765,7 +784,7 @@
         if step < 2:
             count = counts[1 + step]
         if step == last:
-            after = [received[1]] + moved
+            after = [received[1]]
         outs = stage(pairs, tokens, first, count, after, HIDE if step == last else 0)
         if pairs:
             own_kv, own_q = outs[:2]
@@ -790,27 +809,31 @@
     place = jnp.stack([in_plane, side * half])
     own_x, own_sq, part = far_own_product(place, sources, gains, tokens, far_kv)
     received[-1] = gate(received[-1], own_sq)
-    blocks = [received]
-    for _ in range(half - 2):
-        blocks.append([lax.ppermute(block, "tensor", ring) for block in blocks[-1]])
-    sent_kv, x, sq = far_kv_product(
-        place, sources, gains, part, own_sq, blocks, far_kv, [far_q[2]]
-    )
-    got_kv = lax.ppermute(sent_kv, "tensor", swap)
+    weights = (k_weight, value_weight, q_weight)
     pair_o = double(own_o, 0, [])
     for step in range(1, last - 1):
         pair_o = double(pair_o, step, [])
-    weights = (k_weight, value_weight, q_weight)
-
-    near = near_product(side * half + sources, own_x, x, weights, [sent_kv])
-
-    sent_q = far_product(place, sources, own_x, x, far_q, [near])
-    got_q = lax.ppermute(gate(sent_q, got_kv), "tensor", swap)
+    xs, sqs, got_kv, first, after = [], [], [], 0, [far_q[2]] + moved
+    for pieces in (received[:2], received[2:]):
+        blocks = [pieces]
+        for _ in range(half - 2):
+            blocks.append([lax.ppermute(block, "tensor", ring) for block in blocks[-1]])
+        sent_kv, x, sq = far_kv_product(
+            place, sources, gains, part, own_sq, first, blocks, far_kv, after
+        )
+        xs.append(x)
+        sqs.append(sq)
+        got_kv.append(lax.ppermute(sent_kv, "tensor", swap))
+        first, after = first + x.shape[1], [sent_kv]
+
+    sent_q = far_product(place, sources, own_x, xs, far_q, [sent_kv, got_kv[0]])
+    got_q = lax.ppermute(gate(sent_q, got_kv[1]), "tensor", swap)
+    near = near_product(side * half + sources, own_x, xs, weights, [sent_q])
     pair_o = double(pair_o, last - 1, [sent_q])
     cosine, sine = rotation_table(seq * rows + jnp.arange(rows, dtype=jnp.int32))
     ids = seg_ids[None, :]
     own_kv, sums = keys_values(
-        near, got_kv, sq, ids, cosine, sine, [sent_q, pair_o[0]], model
+        near, got_kv, sqs, ids, cosine, sine, [sent_q, pair_o[0]], model
     )
     pair_o = double(pair_o, last, [own_kv])
     gathered_o = lay_pieces(place, order_kv, *pair_o)

time: 148 us -> 154 us (1.041)
  the two profiles are of different devices: /device:TPU:2 before, /device:TPU:0 now
where the time goes in v18:
time: 154 us; the launch traced here: 153 us
  Pallas kernels  52.8 us (34%)
  waiting for transfers between devices  50.5 us (33%)
  starting transfers between devices  44.3 us (29%)
  local copies, waits for them, and re-layouts  3.35 us (2%)
  other arithmetic  2.07 us (1%)
    ppermute x3, waiting for transfers between devices, per_device(): lax.ppermute(p, 'tensor', turn(k + 1))  11.6 us
    ppermute x1, waiting for transfers between devices, per_device(): own_kv = lax.ppermute(packed_kv, 'tensor', swap)[None]  8.01 us
    ppermute x1, waiting for transfers between devices, per_device(): got_q = lax.ppermute(gate(sent_q, got_kv[1]), 'tensor', swap)  7.26 us
    pallas_call x2, Pallas kernels, far_kv_product(): pl.pallas_call(partial(far_kv_kernel, order=order, cuts=[len(block) for b...  7.2 us
    pallas_call x2, Pallas kernels, attend(): pl.pallas_call(partial(attention_kernel, back=back, offset=c * rows), out...  6.99 us
    pallas_call x2, Pallas kernels, first_output(): pl.pallas_call(first_output_kernel, out_shape=shape((chunk, cols), F32),...  6.48 us
    pallas_call x1, Pallas kernels, near_product(): pl.pallas_call(partial(near_kernel, groups=len(xs)), out_shape=shape((row...  6.15 us
    pallas_call x5, Pallas kernels, stage(): pl.pallas_call(partial(stage_kernel, pairs=len(joined), first=first, coun...  5.93 us
  transfers between devices with their start and end apart: 31, of which 17 were waited for; matrix products, arithmetic and copies ran while one was open for 1% of the time, Pallas kernels for 29%

profile of v18, /device:TPU:0, one launch (start us, length us, event | category | flops | bytes accessed | tf_op | source)
XLA Modules:
  0.0 153.4 jit_solution(15746809428017837483)
XLA Ops:
  0.0 2.1 %pack.1 = (bf16[288,256]{1,0:T(8,128)(2,1)}, bf16[288,256]{1,0:T(8,128)(2,1)}, bf16[128,1152]{1,0:T(8,128)(2,1)}) custom-call(s32[1]{0:T(128)} %bitcast.9.at_ref, bf16[4608,256]{1,0:T(8,128)(2,1)} %q_ref.3, bf16[4608,128]{1,0:T(8,128)(2,1)} %k_ref.3, bf16[4608,128]{1,0:T(8,128)(2,1)} %v_ref.3, bf16[768,1152]{1,0:T(8,128)(2,1)} %token_ref.1), custom_call_target="tpu_custom_call" | custom-call | tf_op jit(solution)/shard_map/pack/pallas_call | solution.py:75
  2.1 3.1 %collective-permute-start.10 = (bf16[128,1152]{1,0:T(8,128)(2,1)}, bf16[128,1152]{1,0:T(8,128)(2,1)S(1)}, u32[]{:S(2)}, u32[]{:S(2)}) collective-permute-start(bf16[128,1152]{1,0:T(8,128)(2,1)} %get-tuple-element.38), channel_id=1, source_target_pairs={{0,1},{1,0},{2,3},{3,2},{4,5},{5,4},{6,7},{7,6},{8,9},{9,8},{10,11... | collective-permute-start | bytes 884744 | tf_op jit(solution)/shard_map/ppermute | solution.py:771
  5.2 2.6 %collective-permute-start = (bf16[288,256]{1,0:T(8,128)(2,1)}, bf16[288,256]{1,0:T(8,128)(2,1)S(1)}, u32[]{:S(2)}, u32[]{:S(2)}) collective-permute-start(bf16[288,256]{1,0:T(8,128)(2,1)} %get-tuple-element.31), channel_id=1, source_target_pairs={{0,2},{1,3},{2,0},{3,1},{4,6},{5,7},{6,4},{7,5},{8,10},{9,11},{10,... | collective-permute-start | bytes 442376 | tf_op jit(solution)/shard_map/ppermute | solution.py:769
  8.1 8.0 %collective-permute-done = bf16[288,256]{1,0:T(8,128)(2,1)S(1)} collective-permute-done((bf16[288,256]{1,0:T(8,128)(2,1)}, bf16[288,256]{1,0:T(8,128)(2,1)S(1)}, u32[]{:S(2)}, u32[]{:S(2)}) %collective-permute-start) | collective-permute-done | bytes 147488 | tf_op jit(solution)/shard_map/ppermute | solution.py:769
  16.1 5.0 %collective-permute-done.6 = bf16[288,256]{1,0:T(8,128)(2,1)S(1)} collective-permute-done((bf16[288,256]{1,0:T(8,128)(2,1)}, bf16[288,256]{1,0:T(8,128)(2,1)S(1)}, u32[]{:S(2)}, u32[]{:S(2)}) %collective-permute-start.6) | collective-permute-done | bytes 147488 | tf_op jit(solution)/shard_map/ppermute | solution.py:770
  24.8 2.1 %collective-permute-done.5.refs_1_ = bf16[1,288,256]{2,1,0:T(8,128)(2,1)S(1)} collective-permute-done((bf16[1,288,256]{2,1,0:T(8,128)(2,1)S(1)}, bf16[1,288,256]{2,1,0:T(8,128)(2,1)S(1)}, u32[]{:S(2)}, u32[]{:S(2)}) %collective-permute-start.5) | collective-permute-done | bytes 147488 | tf_op jit(solution)/shard_map/ppermute | solution.py:794
  34.7 3.2 %collective-permute-done.8.refs_1_ = bf16[2,288,256]{2,1,0:T(8,128)(2,1)} collective-permute-done((bf16[2,288,256]{2,1,0:T(8,128)(2,1)S(1)}, bf16[2,288,256]{2,1,0:T(8,128)(2,1)}, u32[]{:S(2)}, u32[]{:S(2)}) %collective-permute-start.8) | collective-permute-done | bytes 294944 | tf_op jit(solution)/shard_map/ppermute | solution.py:794
  37.9 1.7 %collective-permute-done.9.refs_3_ = bf16[2,288,256]{2,1,0:T(8,128)(2,1)} collective-permute-done((bf16[2,288,256]{2,1,0:T(8,128)(2,1)}, bf16[2,288,256]{2,1,0:T(8,128)(2,1)}, u32[]{:S(2)}, u32[]{:S(2)}) %collective-permute-start.9) | collective-permute-done | bytes 294944 | tf_op jit(solution)/shard_map/ppermute | solution.py:795
  39.6 2.2 %stage.7 = (bf16[4,288,256]{2,1,0:T(8,128)(2,1)S(1)}, bf16[4,288,256]{2,1,0:T(8,128)(2,1)}) custom-call(bf16[2,288,256]{2,1,0:T(8,128)(2,1)S(1)} %get-tuple-element.36.refs_0_, bf16[2,288,256]{2,1,0:T(8,128)(2,1)} %collective-permute-done.8.refs_1_, bf16[2,288,256]{2,1,0:T(8,128)(2,1)} %get-tuple-element.37.refs_2_, ...), custom_call_target="tpu_custom_call" | custom-call | flops 49999998976 | bytes 100000000 | tf_op jit(solution)/shard_map/stage/pallas_call | solution.py:130
  47.8 8.9 %collective-permute-done.1.rest_3_ = bf16[32,1152]{1,0:T(8,128)(2,1)S(1)} collective-permute-done((bf16[32,1152]{1,0:T(8,128)(2,1)S(1)}, bf16[32,1152]{1,0:T(8,128)(2,1)S(1)}, u32[]{:S(2)}, u32[]{:S(2)}) %collective-permute-start.1) | collective-permute-done | bytes 73760 | tf_op jit(solution)/shard_map/ppermute | solution.py:775
  58.4 2.7 %collective-permute-done.3.rest_5_ = bf16[32,1152]{1,0:T(8,128)(2,1)S(1)} collective-permute-done((bf16[32,1152]{1,0:T(8,128)(2,1)S(1)}, bf16[32,1152]{1,0:T(8,128)(2,1)S(1)}, u32[]{:S(2)}, u32[]{:S(2)}) %collective-permute-start.3) | collective-permute-done | bytes 73760 | tf_op jit(solution)/shard_map/ppermute | solution.py:775
  62.6 3.5 %far_own.1 = (bf16[1,768,1152]{2,1,0:T(8,128)(2,1)S(1)}, f32[1,768]{1,0:T(1,128)S(1)}, f32[768,256]{1,0:T(8,128)S(1)}) custom-call(s32[2]{0:T(128)S(1)} %get-tuple-element.61.place_ref, s32[2]{0:T(128)S(1)} %get-tuple-element.60.src_ref, f32[4,1,1152]{2,1,0:T(1,128)S(1)} %reshape.21.gain_ref, bf16[4,288,256]{2,1,0:T(8,128)(2,1)S(1)} %get-tuple-element.39.own_ref, ...), custom_call_target="tpu_custom_call" | custom-call | tf_op jit(solution)/shard_map/far_own/pallas_call | solution.py:284
  66.2 3.1 %far_kv.2 = (bf16[400,256]{1,0:T(8,128)(2,1)S(1)}, bf16[1,384,1152]{2,1,0:T(8,128)(2,1)S(1)}, f32[1,384]{1,0:T(1,128)S(1)}) custom-call(s32[2]{0:T(128)S(1)} %get-tuple-element.61.place_ref, s32[2]{0:T(128)S(1)} %get-tuple-element.60.src_ref, f32[4,1,1152]{2,1,0:T(1,128)S(1)} %reshape.21.gain_ref, f32[768,256]{1,0:T(8,128)S(1)} %get-tuple-element.42.part_ref, ...), custom_call_target="tpu_custom_call" | custom-call | tf_op jit(solution)/shard_map/far_kv/pallas_call | solution.py:306
  71.1 4.1 %far_kv.3 = (bf16[400,256]{1,0:T(8,128)(2,1)S(1)}, bf16[1,384,1152]{2,1,0:T(8,128)(2,1)S(1)}, f32[1,384]{1,0:T(1,128)S(1)}) custom-call(s32[2]{0:T(128)S(1)} %get-tuple-element.61.place_ref, s32[2]{0:T(128)S(1)} %get-tuple-element.60.src_ref, f32[4,1,1152]{2,1,0:T(1,128)S(1)} %reshape.21.gain_ref, f32[768,256]{1,0:T(8,128)S(1)} %get-tuple-element.42.part_ref, ...), custom_call_target="tpu_custom_call" | custom-call | tf_op jit(solution)/shard_map/far_kv/pallas_call | solution.py:306
  75.2 2.8 %collective-permute-start.17 = (bf16[400,256]{1,0:T(8,128)(2,1)S(1)}, bf16[400,256]{1,0:T(8,128)(2,1)S(1)}, u32[]{:S(2)}, u32[]{:S(2)}) collective-permute-start(bf16[400,256]{1,0:T(8,128)(2,1)S(1)} %get-tuple-element.48.rest_2_), channel_id=1, source_target_pairs={{0,2},{1,3},{2,0},{3,1},{4,6},{5,7},{6,4},{7,5},{8,10},{9,11},{10,... | collective-permute-start | bytes 614408 | tf_op jit(solution)/shard_map/ppermute | solution.py:826
  78.3 3.6 %collective-permute-done.15.rest_3_.rest_0_ = bf16[400,256]{1,0:T(8,128)(2,1)S(1)} collective-permute-done((bf16[400,256]{1,0:T(8,128)(2,1)S(1)}, bf16[400,256]{1,0:T(8,128)(2,1)S(1)}, u32[]{:S(2)}, u32[]{:S(2)}) %collective-permute-start.15) | collective-permute-done | bytes 204832 | tf_op jit(solution)/shard_map/ppermute | solution.py:826
  81.9 3.1 %far.1.refs_3_.rest_2_.rest_4_.x_ref = bf16[768,256]{1,0:T(8,128)(2,1)S(1)} custom-call(s32[2]{0:T(128)S(1)} %get-tuple-element.61.place_ref, s32[2]{0:T(128)S(1)} %get-tuple-element.60.src_ref, bf16[1,768,1152]{2,1,0:T(8,128)(2,1)S(1)} %get-tuple-element.40.own_x_ref, bf16[4,288,256]{2,1,0:T(8,128)(2,1)} %get-tuple-element.41.own_ref, ...), custom_call_target="tpu_custom_call" | custom-call | tf_op jit(solution)/shard_map/far/pallas_call | solution.py:364
  85.7 2.1 %collective-permute-start.16 = (bf16[2,3,32,1152]{3,2,1,0:T(8,128)(2,1)S(1)}, bf16[2,3,32,1152]{3,2,1,0:T(8,128)(2,1)}, u32[]{:S(2)}, u32[]{:S(2)}) collective-permute-start(bf16[2,3,32,1152]{3,2,1,0:T(8,128)(2,1)S(1)} %stage.8.rest_5_.refs_0_), channel_id=1, source_target_pairs={{0,16},{4,20},{8,24},{12,28},{16,0},{20,4},{24,8},{28,12},{1,17},{... | collective-permute-start | bytes 1327112 | tf_op jit(solution)/shard_map/ppermute | solution.py:805
  87.9 6.2 %near.1.near_ref = f32[768,512]{1,0:T(8,128)S(1)} custom-call(s32[2]{0:T(128)S(1)} %broadcast_add_fusion.src_ref, bf16[1,768,1152]{2,1,0:T(8,128)(2,1)} %copy-done.1, bf16[4608,128]{1,0:T(8,128)(2,1)S(1)} %copy-done.4, bf16[4608,128]{1,0:T(8,128)(2,1)S(1)} %copy-done.5, bf16[4608,256]{1,0:T(8,128)(2,1)} %q_ref.3, ...), custom_call_target="tpu_custom_call" | custom-call | tf_op jit(solution)/shard_map/near/pallas_call | solution.py:407
  95.3 2.6 %collective-permute-start.20 = (bf16[784,256]{1,0:T(8,128)(2,1)S(1)}, bf16[784,256]{1,0:T(8,128)(2,1)S(1)}, u32[]{:S(2)}, u32[]{:S(2)}) collective-permute-start(bf16[784,256]{1,0:T(8,128)(2,1)S(1)} %get-tuple-element.51.refs_3_.after_ref.rest_2_), channel_id=1, source_target_pairs={{0,8},{4,12},{1,9},{5,13},{2,10},{6,14},{3,11},{7,15},{16,24},{20,... | collective-permute-start | bytes 1204232 | tf_op jit(solution)/shard_map/ppermute | solution.py:845
  100.8 7.3 %collective-permute-done.19.far_ref = bf16[768,256]{1,0:T(8,128)(2,1)S(1)} collective-permute-done((bf16[768,256]{1,0:T(8,128)(2,1)S(1)}, bf16[768,256]{1,0:T(8,128)(2,1)S(1)}, u32[]{:S(2)}, u32[]{:S(2)}) %collective-permute-start.19) | collective-permute-done | bytes 393248 | tf_op jit(solution)/shard_map/ppermute | solution.py:830
  108.6 2.9 %attend.2.rest_0_ = bf16[384,256]{1,0:T(8,128)(2,1)S(1)} custom-call(s32[1]{0:T(128)} %bitcast.16.seq_ref, bf16[768,256]{1,0:T(8,128)(2,1)S(1)} %queries.1.q_ref, s32[1,768]{1,0:T(1,128)S(1)} %broadcast_in_dim.21.id_ref, bf16[784,256]{1,0:T(8,128)(2,1)S(1)} %get-tuple-element.51.refs_3_.after_ref.rest_2_, ...), custom_call_target="tpu_custom_call" | custom-call | flops 905969664 | bytes 2359296 | tf_op jit(solution)/shard_map/attend/pallas_call | solution.py:583
  115.5 4.0 %attend.3.rest_2_.after_ref.rest_0_ = bf16[384,256]{1,0:T(8,128)(2,1)S(1)} custom-call(s32[1]{0:T(128)} %bitcast.16.seq_ref, bf16[768,256]{1,0:T(8,128)(2,1)S(1)} %queries.1.q_ref, s32[1,768]{1,0:T(1,128)S(1)} %broadcast_in_dim.21.id_ref, bf16[3,256,1152]{2,1,0:T(8,128)(2,1)S(1)} %lay.1.after_ref.o_ref, ...), custom_call_target="tpu_custom_call" | custom-call | flops 905969664 | bytes 2359296 | tf_op jit(solution)/shard_map/attend/pallas_call | solution.py:583
  120.4 2.1 %collective-permute-start.26 = (bf16[384,256]{1,0:T(8,128)(2,1)S(1)}, bf16[384,256]{1,0:T(8,128)(2,1)S(1)}, u32[]{:S(2)}, u32[]{:S(2)}) collective-permute-start(bf16[384,256]{1,0:T(8,128)(2,1)S(1)} %attend.3.rest_2_.after_ref.rest_0_), channel_id=1, source_target_pairs={{0,2},{1,3},{2,0},{3,1},{4,6},{5,7},{6,4},{7,5},{8,10},{9,11},{10,... | collective-permute-start | bytes 589832 | tf_op jit(solution)/shard_map/ppermute | solution.py:857
  124.5 3.2 %first_output.2.part_ref = f32[384,1152]{1,0:T(8,128)S(1)} custom-call(s32[2]{0:T(128)S(1)} %pad_add_fusion.1.at_ref, bf16[256,4608]{1,0:T(8,128)(2,1)} %own_o_ref.3, bf16[3,256,1152]{2,1,0:T(8,128)(2,1)S(1)} %lay.1.after_ref.o_ref, bf16[384,256]{1,0:T(8,128)(2,1)S(1)} %attend.2.rest_0_, bf16[384,256]{1,0:T(8,128)(2,1)S(1)} %collective-permute-done.22.rest_1_, ...), custom_call_target="tpu_custom_call" | custom-call | flops 49999998976 | bytes 100000000 | tf_op jit(solution)/shard_map/first_output/pallas_call | solution.py:658
  127.8 4.5 %collective-permute-start.27 = (bf16[384,256]{1,0:T(8,128)(2,1)S(1)}, bf16[384,256]{1,0:T(8,128)(2,1)S(1)}, u32[]{:S(2)}, u32[]{:S(2)}) collective-permute-start(bf16[384,256]{1,0:T(8,128)(2,1)S(1)} %collective-permute-done.26.rest_0_), channel_id=1, source_target_pairs={{0,1},{1,0},{2,3},{3,2},{4,5},{5,4},{6,7},{7,6},{8,9},{9,8},{10,11... | collective-permute-start | bytes 589832 | tf_op jit(solution)/shard_map/ppermute | solution.py:861
  132.4 3.2 %first_output.3.part_ref = f32[384,1152]{1,0:T(8,128)S(1)} custom-call(s32[2]{0:T(128)S(1)} %pad_add_fusion.1.at_ref, bf16[256,4608]{1,0:T(8,128)(2,1)} %own_o_ref.3, bf16[3,256,1152]{2,1,0:T(8,128)(2,1)S(1)} %lay.1.after_ref.o_ref, bf16[384,256]{1,0:T(8,128)(2,1)S(1)} %attend.3.rest_2_.after_ref.rest_0_, ...), custom_call_target="tpu_custom_call" | custom-call | flops 49999998976 | bytes 100000000 | tf_op jit(solution)/shard_map/first_output/pallas_call | solution.py:658
  136.6 2.5 %last_output.2 = (f32[384,1152]{1,0:T(8,128)S(1)}, f32[1,384]{1,0:T(1,128)S(1)}) custom-call(s32[2]{0:T(128)S(1)} %pad_add_fusion.at_ref, f32[384,1152]{1,0:T(8,128)S(1)} %first_output.2.part_ref, bf16[3,256,1152]{2,1,0:T(8,128)(2,1)S(1)} %lay.1.after_ref.o_ref, bf16[384,256]{1,0:T(8,128)(2,1)S(1)} %gate.5.rest_0_, ...), custom_call_target="tpu_custom_call" | custom-call | tf_op jit(solution)/shard_map/last_output/pallas_call | solution.py:682
  139.7 2.5 %last_output.3 = (f32[384,1152]{1,0:T(8,128)S(1)}, f32[1,768]{1,0:T(1,128)S(1)}) custom-call(s32[2]{0:T(128)S(1)} %pad_add_fusion.at_ref, f32[384,1152]{1,0:T(8,128)S(1)} %first_output.3.part_ref, bf16[3,256,1152]{2,1,0:T(8,128)(2,1)S(1)} %lay.1.after_ref.o_ref, bf16[384,256]{1,0:T(8,128)(2,1)S(1)} %collective-permute-done.26.rest_0_, ...), custom_call_target="tpu_custom_call" | custom-call | tf_op jit(solution)/shard_map/last_output/pallas_call | solution.py:682
  142.3 4.3 %collective-permute-start.29 = (f32[1,768]{1,0:T(1,128)S(1)}, f32[1,768]{1,0:T(1,128)S(1)}, u32[]{:S(2)}, u32[]{:S(2)}) collective-permute-start(f32[1,768]{1,0:T(1,128)S(1)} %get-tuple-element.56.rest_2_), channel_id=1, source_target_pairs={{0,2},{1,3},{2,0},{3,1},{4,6},{5,7},{6,4},{7,5},{8,10},{9,11},{10,... | collective-permute-start | bytes 9224 | tf_op jit(solution)/shard_map/ppermute | solution.py:876
  148.2 2.0 %collective-permute-done.30.rest_5_ = f32[1,768]{1,0:T(1,128)S(1)} collective-permute-done((f32[1,768]{1,0:T(1,128)S(1)}, f32[1,768]{1,0:T(1,128)S(1)}, u32[]{:S(2)}, u32[]{:S(2)}) %collective-permute-start.30) | collective-permute-done | bytes 3104 | tf_op jit(solution)/shard_map/ppermute | solution.py:876
  150.2 3.2 %finish.1 = bf16[768,1152]{1,0:T(8,128)(2,1)} custom-call(bf16[768,1152]{1,0:T(8,128)(2,1)S(1)} %copy-done, f32[1,1152]{1,0:T(1,128)S(1)} %broadcast_in_dim.17.gain_ref, f32[384,1152]{1,0:T(8,128)S(1)} %get-tuple-element.53.rest_0_, f32[384,1152]{1,0:T(8,128)S(1)} %get-tuple-element.55.rest_1_, f32[1,768]{1,0:T(1,128)S(1)} %get-tuple-element.56.rest_2_, ...), custom_call_target="tpu_custom_call" | custom-call | tf_op jit(solution)/shard_map/finish/pallas_call | solution.py:723
  (106 shorter events, 38.1 us)
Async XLA Ops:
  2.1 19.0 %collective-permute-start.10 = (bf16[128,1152]{1,0:T(8,128)(2,1)}, bf16[128,1152]{1,0:T(8,128)(2,1)S(1)}, u32[]{:S(2)}, u32[]{:S(2)}) collective-permute-start(bf16[128,1152]{1,0:T(8,128)(2,1)} %get-tuple-element.38), channel_id=1, source_target_pairs={{0,1},{1,0},{2,3},{3,2},{4,5},{5,4},{6,7},{7,6},{8,9},{9,8},{10,11... | collective-permute-start | bytes 884744 | tf_op jit(solution)/shard_map/ppermute | solution.py:771
  5.2 10.9 %collective-permute-start = (bf16[288,256]{1,0:T(8,128)(2,1)}, bf16[288,256]{1,0:T(8,128)(2,1)S(1)}, u32[]{:S(2)}, u32[]{:S(2)}) collective-permute-start(bf16[288,256]{1,0:T(8,128)(2,1)} %get-tuple-element.31), channel_id=1, source_target_pairs={{0,2},{1,3},{2,0},{3,1},{4,6},{5,7},{6,4},{7,5},{8,10},{9,11},{10,... | collective-permute-start | bytes 442376 | tf_op jit(solution)/shard_map/ppermute | solution.py:769
  7.8 13.4 %collective-permute-start.6 = (bf16[288,256]{1,0:T(8,128)(2,1)}, bf16[288,256]{1,0:T(8,128)(2,1)S(1)}, u32[]{:S(2)}, u32[]{:S(2)}) collective-permute-start(bf16[288,256]{1,0:T(8,128)(2,1)} %get-tuple-element.35), channel_id=1, source_target_pairs={{0,2},{1,3},{2,0},{3,1},{4,6},{5,7},{6,4},{7,5},{8,10},{9,11},{10,... | collective-permute-start | bytes 442376 | tf_op jit(solution)/shard_map/ppermute | solution.py:770
  21.3 18.4 %collective-permute-start.11 = (bf16[256,1152]{1,0:T(8,128)(2,1)S(1)}, bf16[256,1152]{1,0:T(8,128)(2,1)S(1)}, u32[]{:S(2)}, u32[]{:S(2)}) collective-permute-start(bf16[256,1152]{1,0:T(8,128)(2,1)S(1)} %stage.6), channel_id=1, source_target_pairs={{0,1},{1,0},{2,3},{3,2},{4,5},{5,4},{6,7},{7,6},{8,9},{9,8},{10,11... | collective-permute-start | bytes 1769480 | tf_op jit(solution)/shard_map/ppermute | solution.py:792
  21.8 5.1 %collective-permute-start.5 = (bf16[1,288,256]{2,1,0:T(8,128)(2,1)S(1)}, bf16[1,288,256]{2,1,0:T(8,128)(2,1)S(1)}, u32[]{:S(2)}, u32[]{:S(2)}) collective-permute-start(bf16[1,288,256]{2,1,0:T(8,128)(2,1)S(1)} %bitcast.19), channel_id=1, source_target_pairs={{0,8},{4,12},{8,0},{12,4},{16,24},{20,28},{24,16},{28,20},{1,9},{5... | collective-permute-start | bytes 442376 | tf_op jit(solution)/shard_map/ppermute | solution.py:794
  23.3 5.1 %collective-permute-start.7 = (bf16[1,288,256]{2,1,0:T(8,128)(2,1)S(1)}, bf16[1,288,256]{2,1,0:T(8,128)(2,1)S(1)}, u32[]{:S(2)}, u32[]{:S(2)}) collective-permute-start(bf16[1,288,256]{2,1,0:T(8,128)(2,1)S(1)} %bitcast.23), channel_id=1, source_target_pairs={{0,16},{4,20},{8,24},{12,28},{16,0},{20,4},{24,8},{28,12},{1,17},{... | collective-permute-start | bytes 442376 | tf_op jit(solution)/shard_map/ppermute | solution.py:795
  31.1 6.8 %collective-permute-start.8 = (bf16[2,288,256]{2,1,0:T(8,128)(2,1)S(1)}, bf16[2,288,256]{2,1,0:T(8,128)(2,1)}, u32[]{:S(2)}, u32[]{:S(2)}) collective-permute-start(bf16[2,288,256]{2,1,0:T(8,128)(2,1)S(1)} %get-tuple-element.36.refs_0_), channel_id=1, source_target_pairs={{0,16},{4,20},{8,24},{12,28},{16,0},{20,4},{24,8},{28,12},{1,17},{... | collective-permute-start | bytes 884744 | tf_op jit(solution)/shard_map/ppermute | solution.py:794
  32.6 7.0 %collective-permute-start.9 = (bf16[2,288,256]{2,1,0:T(8,128)(2,1)}, bf16[2,288,256]{2,1,0:T(8,128)(2,1)}, u32[]{:S(2)}, u32[]{:S(2)}) collective-permute-start(bf16[2,288,256]{2,1,0:T(8,128)(2,1)} %get-tuple-element.37.refs_2_), channel_id=1, source_target_pairs={{0,8},{4,12},{8,0},{12,4},{16,24},{20,28},{24,16},{28,20},{1,9},{5... | collective-permute-start | bytes 884744 | tf_op jit(solution)/shard_map/ppermute | solution.py:795
  33.1 37.9 %collective-permute-start.14 = (bf16[384,1152]{1,0:T(8,128)(2,1)}, bf16[384,1152]{1,0:T(8,128)(2,1)}, u32[]{:S(2)}, u32[]{:S(2)}) collective-permute-start(bf16[384,1152]{1,0:T(8,128)(2,1)} %copy-done.15), channel_id=1, source_target_pairs={{0,1},{1,0},{2,3},{3,2},{4,5},{5,4},{6,7},{7,6},{8,9},{9,8},{10,11... | collective-permute-start | bytes 2654216 | tf_op jit(solution)/shard_map/ppermute | solution.py:792
  41.9 20.8 %collective-permute-start.12 = (bf16[4,288,256]{2,1,0:T(8,128)(2,1)S(1)}, bf16[4,288,256]{2,1,0:T(8,128)(2,1)S(1)}, u32[]{:S(2)}, u32[]{:S(2)}) collective-permute-start(bf16[4,288,256]{2,1,0:T(8,128)(2,1)S(1)} %get-tuple-element.39.own_ref), channel_id=1, source_target_pairs={{0,4},{4,0},{8,12},{12,8},{16,20},{20,16},{24,28},{28,24},{1,5},{5... | collective-permute-start | bytes 1769480 | tf_op jit(solution)/shard_map/ppermute | solution.py:794
  42.0 24.2 %collective-permute-start.13 = (bf16[4,288,256]{2,1,0:T(8,128)(2,1)}, bf16[4,288,256]{2,1,0:T(8,128)(2,1)}, u32[]{:S(2)}, u32[]{:S(2)}) collective-permute-start(bf16[4,288,256]{2,1,0:T(8,128)(2,1)} %get-tuple-element.41.own_ref), channel_id=1, source_target_pairs={{0,4},{4,0},{8,12},{12,8},{16,20},{20,16},{24,28},{28,24},{1,5},{5... | collective-permute-start | bytes 1769480 | tf_op jit(solution)/shard_map/ppermute | solution.py:795
  44.9 21.3 %copy-start.12 = (bf16[128,1152]{1,0:T(8,128)(2,1)S(1)}, bf16[128,1152]{1,0:T(8,128)(2,1)}, u32[]{:S(2)}) copy-start(bf16[128,1152]{1,0:T(8,128)(2,1)} %copy-done.11) | copy-start | bytes 884740
  44.9 11.8 %collective-permute-start.1 = (bf16[32,1152]{1,0:T(8,128)(2,1)S(1)}, bf16[32,1152]{1,0:T(8,128)(2,1)S(1)}, u32[]{:S(2)}, u32[]{:S(2)}) collective-permute-start(bf16[32,1152]{1,0:T(8,128)(2,1)S(1)} %get-tuple-element.32), channel_id=1, source_target_pairs={{0,1},{1,2},{2,3},{3,0},{4,5},{5,6},{6,7},{7,4},{8,9},{9,10},{10,1... | collective-permute-start | bytes 221192 | tf_op jit(solution)/shard_map/ppermute | solution.py:775
  46.6 11.7 %collective-permute-start.2 = (bf16[32,1152]{1,0:T(8,128)(2,1)S(1)}, bf16[32,1152]{1,0:T(8,128)(2,1)S(1)}, u32[]{:S(2)}, u32[]{:S(2)}) collective-permute-start(bf16[32,1152]{1,0:T(8,128)(2,1)S(1)} %get-tuple-element.33), channel_id=1, source_target_pairs={{0,2},{1,3},{2,0},{3,1},{4,6},{5,7},{6,4},{7,5},{8,10},{9,11},{10,... | collective-permute-start | bytes 221192 | tf_op jit(solution)/shard_map/ppermute | solution.py:775
  56.7 4.4 %collective-permute-start.3 = (bf16[32,1152]{1,0:T(8,128)(2,1)S(1)}, bf16[32,1152]{1,0:T(8,128)(2,1)S(1)}, u32[]{:S(2)}, u32[]{:S(2)}) collective-permute-start(bf16[32,1152]{1,0:T(8,128)(2,1)S(1)} %get-tuple-element.34), channel_id=1, source_target_pairs={{0,3},{1,0},{2,1},{3,2},{4,7},{5,4},{6,5},{7,6},{8,11},{9,8},{10,9... | collective-permute-start | bytes 221192 | tf_op jit(solution)/shard_map/ppermute | solution.py:775
  61.1 24.0 %collective-permute-start.4 = (bf16[1,3,32,1152]{3,2,1,0:T(8,128)(2,1)S(1)}, bf16[1,3,32,1152]{3,2,1,0:T(8,128)(2,1)S(1)}, u32[]{:S(2)}, u32[]{:S(2)}) collective-permute-start(bf16[1,3,32,1152]{3,2,1,0:T(8,128)(2,1)S(1)} %maximum_bitcast_fusion.refs_0_), channel_id=1, source_target_pairs={{0,8},{4,12},{8,0},{12,4},{16,24},{20,28},{24,16},{28,20},{1,9},{5... | collective-permute-start | bytes 663560 | tf_op jit(solution)/shard_map/ppermute | solution.py:805
  69.3 12.6 %collective-permute-start.15 = (bf16[400,256]{1,0:T(8,128)(2,1)S(1)}, bf16[400,256]{1,0:T(8,128)(2,1)S(1)}, u32[]{:S(2)}, u32[]{:S(2)}) collective-permute-start(bf16[400,256]{1,0:T(8,128)(2,1)S(1)} %get-tuple-element.46.rest_1_), channel_id=1, source_target_pairs={{0,2},{1,3},{2,0},{3,1},{4,6},{5,7},{6,4},{7,5},{8,10},{9,11},{10,... | collective-permute-start | bytes 614408 | tf_op jit(solution)/shard_map/ppermute | solution.py:826
  75.2 18.9 %collective-permute-start.17 = (bf16[400,256]{1,0:T(8,128)(2,1)S(1)}, bf16[400,256]{1,0:T(8,128)(2,1)S(1)}, u32[]{:S(2)}, u32[]{:S(2)}) collective-permute-start(bf16[400,256]{1,0:T(8,128)(2,1)S(1)} %get-tuple-element.48.rest_2_), channel_id=1, source_target_pairs={{0,2},{1,3},{2,0},{3,1},{4,6},{5,7},{6,4},{7,5},{8,10},{9,11},{10,... | collective-permute-start | bytes 614408 | tf_op jit(solution)/shard_map/ppermute | solution.py:826
  85.7 13.7 %collective-permute-start.16 = (bf16[2,3,32,1152]{3,2,1,0:T(8,128)(2,1)S(1)}, bf16[2,3,32,1152]{3,2,1,0:T(8,128)(2,1)}, u32[]{:S(2)}, u32[]{:S(2)}) collective-permute-start(bf16[2,3,32,1152]{3,2,1,0:T(8,128)(2,1)S(1)} %stage.8.rest_5_.refs_0_), channel_id=1, source_target_pairs={{0,16},{4,20},{8,24},{12,28},{16,0},{20,4},{24,8},{28,12},{1,17},{... | collective-permute-start | bytes 1327112 | tf_op jit(solution)/shard_map/ppermute | solution.py:805
  95.2 12.9 %collective-permute-start.19 = (bf16[768,256]{1,0:T(8,128)(2,1)S(1)}, bf16[768,256]{1,0:T(8,128)(2,1)S(1)}, u32[]{:S(2)}, u32[]{:S(2)}) collective-permute-start(bf16[768,256]{1,0:T(8,128)(2,1)S(1)} %gate.4), channel_id=1, source_target_pairs={{0,2},{1,3},{2,0},{3,1},{4,6},{5,7},{6,4},{7,5},{8,10},{9,11},{10,... | collective-permute-start | bytes 1179656 | tf_op jit(solution)/shard_map/ppermute | solution.py:830
  95.3 13.3 %collective-permute-start.20 = (bf16[784,256]{1,0:T(8,128)(2,1)S(1)}, bf16[784,256]{1,0:T(8,128)(2,1)S(1)}, u32[]{:S(2)}, u32[]{:S(2)}) collective-permute-start(bf16[784,256]{1,0:T(8,128)(2,1)S(1)} %get-tuple-element.51.refs_3_.after_ref.rest_2_), channel_id=1, source_target_pairs={{0,8},{4,12},{1,9},{5,13},{2,10},{6,14},{3,11},{7,15},{16,24},{20,... | collective-permute-start | bytes 1204232 | tf_op jit(solution)/shard_map/ppermute | solution.py:845
  97.9 10.7 %collective-permute-start.21 = (bf16[784,256]{1,0:T(8,128)(2,1)S(1)}, bf16[784,256]{1,0:T(8,128)(2,1)S(1)}, u32[]{:S(2)}, u32[]{:S(2)}) collective-permute-start(bf16[784,256]{1,0:T(8,128)(2,1)S(1)} %get-tuple-element.51.refs_3_.after_ref.rest_2_), channel_id=1, source_target_pairs={{0,4},{4,8},{8,12},{1,5},{5,9},{9,13},{2,6},{6,10},{10,14},{3,7},{... | collective-permute-start | bytes 1204232 | tf_op jit(solution)/shard_map/ppermute | solution.py:845
  100.7 13.4 %collective-permute-start.18 = (bf16[4,3,32,1152]{3,2,1,0:T(8,128)(2,1)S(1)}, bf16[4,3,32,1152]{3,2,1,0:T(8,128)(2,1)S(1)}, u32[]{:S(2)}, u32[]{:S(2)}) collective-permute-start(bf16[4,3,32,1152]{3,2,1,0:T(8,128)(2,1)S(1)} %stage.9.own_ref), channel_id=1, source_target_pairs={{0,4},{4,0},{8,12},{12,8},{16,20},{20,16},{24,28},{28,24},{1,5},{5... | collective-permute-start | bytes 2654216 | tf_op jit(solution)/shard_map/ppermute | solution.py:805
  111.6 12.5 %collective-permute-start.23 = (bf16[384,256]{1,0:T(8,128)(2,1)S(1)}, bf16[384,256]{1,0:T(8,128)(2,1)S(1)}, u32[]{:S(2)}, u32[]{:S(2)}) collective-permute-start(bf16[384,256]{1,0:T(8,128)(2,1)S(1)} %attend.2.rest_0_), channel_id=1, source_target_pairs={{0,2},{1,3},{2,0},{3,1},{4,6},{5,7},{6,4},{7,5},{8,10},{9,11},{10,... | collective-permute-start | bytes 589832 | tf_op jit(solution)/shard_map/ppermute | solution.py:857
  112.8 11.7 %collective-permute-start.22 = (bf16[384,256]{1,0:T(8,128)(2,1)S(1)}, bf16[384,256]{1,0:T(8,128)(2,1)S(1)}, u32[]{:S(2)}, u32[]{:S(2)}) collective-permute-start(bf16[384,256]{1,0:T(8,128)(2,1)S(1)} %attend.2.rest_0_), channel_id=1, source_target_pairs={{0,1},{1,0},{2,3},{3,2},{4,5},{5,4},{6,7},{7,6},{8,9},{9,8},{10,11... | collective-permute-start | bytes 589832 | tf_op jit(solution)/shard_map/ppermute | solution.py:858
  119.5 12.9 %collective-permute-start.25 = (bf16[384,256]{1,0:T(8,128)(2,1)S(1)}, bf16[384,256]{1,0:T(8,128)(2,1)S(1)}, u32[]{:S(2)}, u32[]{:S(2)}) collective-permute-start(bf16[384,256]{1,0:T(8,128)(2,1)S(1)} %attend.3.rest_2_.after_ref.rest_0_), channel_id=1, source_target_pairs={{0,1},{1,0},{2,3},{3,2},{4,5},{5,4},{6,7},{7,6},{8,9},{9,8},{10,11... | collective-permute-start | bytes 589832 | tf_op jit(solution)/shard_map/ppermute | solution.py:858
  120.4 7.5 %collective-permute-start.26 = (bf16[384,256]{1,0:T(8,128)(2,1)S(1)}, bf16[384,256]{1,0:T(8,128)(2,1)S(1)}, u32[]{:S(2)}, u32[]{:S(2)}) collective-permute-start(bf16[384,256]{1,0:T(8,128)(2,1)S(1)} %attend.3.rest_2_.after_ref.rest_0_), channel_id=1, source_target_pairs={{0,2},{1,3},{2,0},{3,1},{4,6},{5,7},{6,4},{7,5},{8,10},{9,11},{10,... | collective-permute-start | bytes 589832 | tf_op jit(solution)/shard_map/ppermute | solution.py:857
  124.1 12.6 %collective-permute-start.24 = (bf16[384,256]{1,0:T(8,128)(2,1)S(1)}, bf16[384,256]{1,0:T(8,128)(2,1)S(1)}, u32[]{:S(2)}, u32[]{:S(2)}) collective-permute-start(bf16[384,256]{1,0:T(8,128)(2,1)S(1)} %gate.5.rest_0_), channel_id=1, source_target_pairs={{0,1},{1,0},{2,3},{3,2},{4,5},{5,4},{6,7},{7,6},{8,9},{9,8},{10,11... | collective-permute-start | bytes 589832 | tf_op jit(solution)/shard_map/ppermute | solution.py:861
  127.8 11.8 %collective-permute-start.27 = (bf16[384,256]{1,0:T(8,128)(2,1)S(1)}, bf16[384,256]{1,0:T(8,128)(2,1)S(1)}, u32[]{:S(2)}, u32[]{:S(2)}) collective-permute-start(bf16[384,256]{1,0:T(8,128)(2,1)S(1)} %collective-permute-done.26.rest_0_), channel_id=1, source_target_pairs={{0,1},{1,0},{2,3},{3,2},{4,5},{5,4},{6,7},{7,6},{8,9},{9,8},{10,11... | collective-permute-start | bytes 589832 | tf_op jit(solution)/shard_map/ppermute | solution.py:861
  142.2 5.4 %collective-permute-start.28 = (f32[1,768]{1,0:T(1,128)S(1)}, f32[1,768]{1,0:T(1,128)S(1)}, u32[]{:S(2)}, u32[]{:S(2)}) collective-permute-start(f32[1,768]{1,0:T(1,128)S(1)} %get-tuple-element.56.rest_2_), channel_id=1, source_target_pairs={{0,1},{1,2},{2,3},{3,0},{4,5},{5,6},{6,7},{7,4},{8,9},{9,10},{10,1... | collective-permute-start | bytes 9224 | tf_op jit(solution)/shard_map/ppermute | solution.py:876
  142.3 5.9 %collective-permute-start.29 = (f32[1,768]{1,0:T(1,128)S(1)}, f32[1,768]{1,0:T(1,128)S(1)}, u32[]{:S(2)}, u32[]{:S(2)}) collective-permute-start(f32[1,768]{1,0:T(1,128)S(1)} %get-tuple-element.56.rest_2_), channel_id=1, source_target_pairs={{0,2},{1,3},{2,0},{3,1},{4,6},{5,7},{6,4},{7,5},{8,10},{9,11},{10,... | collective-permute-start | bytes 9224 | tf_op jit(solution)/shard_map/ppermute | solution.py:876
  146.6 3.6 %collective-permute-start.30 = (f32[1,768]{1,0:T(1,128)S(1)}, f32[1,768]{1,0:T(1,128)S(1)}, u32[]{:S(2)}, u32[]{:S(2)}) collective-permute-start(f32[1,768]{1,0:T(1,128)S(1)} %get-tuple-element.56.rest_2_), channel_id=1, source_target_pairs={{0,3},{1,0},{2,1},{3,2},{4,7},{5,4},{6,5},{7,6},{8,11},{9,8},{10,9... | collective-permute-start | bytes 9224 | tf_op jit(solution)/shard_map/ppermute | solution.py:876
  (18 other events, 168.5 us)

commit v19 on v18

--- a/solution.py
+++ b/solution.py
@@ -813,7 +813,7 @@
     pair_o = double(own_o, 0, [])
     for step in range(1, last - 1):
         pair_o = double(pair_o, step, [])
-    xs, sqs, got_kv, first, after = [], [], [], 0, [far_q[2]] + moved
+    xs, sqs, got_kv, first, after = [], [], [], 0, [far_q[2]]
     for pieces in (received[:2], received[2:]):
         blocks = [pieces]
         for _ in range(half - 2):

time: 154 us -> 155 us (level)
  the two profiles are of different devices: /device:TPU:0 before, /device:TPU:2 now
where the time goes in v19:
time: 155 us; the launch traced here: 152 us
  Pallas kernels  52.8 us (34%)
  waiting for transfers between devices  49.9 us (32%)
  starting transfers between devices  43.7 us (28%)
  local copies, waits for them, and re-layouts  3.36 us (2%)
  other arithmetic  2.07 us (1%)
    ppermute x3, waiting for transfers between devices, per_device(): lax.ppermute(p, 'tensor', turn(k + 1))  12.5 us
    ppermute x1, waiting for transfers between devices, per_device(): own_kv = lax.ppermute(packed_kv, 'tensor', swap)[None]  8.01 us
    ppermute x1, waiting for transfers between devices, per_device(): got_q = lax.ppermute(gate(sent_q, got_kv[1]), 'tensor', swap)  7.89 us
    pallas_call x2, Pallas kernels, far_kv_product(): pl.pallas_call(partial(far_kv_kernel, order=order, cuts=[len(block) for b...  7.2 us
    pallas_call x2, Pallas kernels, attend(): pl.pallas_call(partial(attention_kernel, back=back, offset=c * rows), out...  6.97 us
    ppermute x2, starting transfers between devices, per_device(): across = lax.ppermute(opposite, 'tensor', pairs)  6.58 us
    pallas_call x2, Pallas kernels, first_output(): pl.pallas_call(first_output_kernel, out_shape=shape((chunk, cols), F32),...  6.48 us
    pallas_call x1, Pallas kernels, near_product(): pl.pallas_call(partial(near_kernel, groups=len(xs)), out_shape=shape((row...  6.16 us
  transfers between devices with their start and end apart: 31, of which 15 were waited for; matrix products, arithmetic and copies ran while one was open for 1% of the time, Pallas kernels for 29%

profile of v19, /device:TPU:2, one launch (start us, length us, event | category | flops | bytes accessed | tf_op | source)
XLA Modules:
  0.0 152.3 jit_solution(17531817376778413654)
XLA Ops:
  0.0 2.1 %pack.1 = (bf16[288,256]{1,0:T(8,128)(2,1)}, bf16[288,256]{1,0:T(8,128)(2,1)}, bf16[128,1152]{1,0:T(8,128)(2,1)}) custom-call(s32[1]{0:T(128)} %bitcast.9.at_ref, bf16[4608,256]{1,0:T(8,128)(2,1)} %q_ref.3, bf16[4608,128]{1,0:T(8,128)(2,1)} %k_ref.3, bf16[4608,128]{1,0:T(8,128)(2,1)} %v_ref.3, bf16[768,1152]{1,0:T(8,128)(2,1)} %token_ref.1), custom_call_target="tpu_custom_call" | custom-call | tf_op jit(solution)/shard_map/pack/pallas_call | solution.py:75
  3.7 2.6 %collective-permute-start = (bf16[288,256]{1,0:T(8,128)(2,1)}, bf16[288,256]{1,0:T(8,128)(2,1)S(1)}, u32[]{:S(2)}, u32[]{:S(2)}) collective-permute-start(bf16[288,256]{1,0:T(8,128)(2,1)} %get-tuple-element.31), channel_id=1, source_target_pairs={{0,2},{1,3},{2,0},{3,1},{4,6},{5,7},{6,4},{7,5},{8,10},{9,11},{10,... | collective-permute-start | bytes 442376 | tf_op jit(solution)/shard_map/ppermute | solution.py:769
  6.7 8.0 %collective-permute-done = bf16[288,256]{1,0:T(8,128)(2,1)S(1)} collective-permute-done((bf16[288,256]{1,0:T(8,128)(2,1)}, bf16[288,256]{1,0:T(8,128)(2,1)S(1)}, u32[]{:S(2)}, u32[]{:S(2)}) %collective-permute-start) | collective-permute-done | bytes 147488 | tf_op jit(solution)/shard_map/ppermute | solution.py:769
  14.7 5.0 %collective-permute-done.6 = bf16[288,256]{1,0:T(8,128)(2,1)S(1)} collective-permute-done((bf16[288,256]{1,0:T(8,128)(2,1)}, bf16[288,256]{1,0:T(8,128)(2,1)S(1)}, u32[]{:S(2)}, u32[]{:S(2)}) %collective-permute-start.6) | collective-permute-done | bytes 147488 | tf_op jit(solution)/shard_map/ppermute | solution.py:770
  22.4 3.1 %collective-permute-done.5.refs_1_ = bf16[1,288,256]{2,1,0:T(8,128)(2,1)S(1)} collective-permute-done((bf16[1,288,256]{2,1,0:T(8,128)(2,1)S(1)}, bf16[1,288,256]{2,1,0:T(8,128)(2,1)S(1)}, u32[]{:S(2)}, u32[]{:S(2)}) %collective-permute-start.5) | collective-permute-done | bytes 147488 | tf_op jit(solution)/shard_map/ppermute | solution.py:794
  33.3 2.2 %collective-permute-done.8.refs_1_ = bf16[2,288,256]{2,1,0:T(8,128)(2,1)} collective-permute-done((bf16[2,288,256]{2,1,0:T(8,128)(2,1)S(1)}, bf16[2,288,256]{2,1,0:T(8,128)(2,1)}, u32[]{:S(2)}, u32[]{:S(2)}) %collective-permute-start.8) | collective-permute-done | bytes 294944 | tf_op jit(solution)/shard_map/ppermute | solution.py:794
  37.2 2.2 %stage.7 = (bf16[4,288,256]{2,1,0:T(8,128)(2,1)S(1)}, bf16[4,288,256]{2,1,0:T(8,128)(2,1)}) custom-call(bf16[2,288,256]{2,1,0:T(8,128)(2,1)S(1)} %get-tuple-element.36.refs_0_, bf16[2,288,256]{2,1,0:T(8,128)(2,1)} %collective-permute-done.8.refs_1_, bf16[2,288,256]{2,1,0:T(8,128)(2,1)} %get-tuple-element.37.refs_2_, ...), custom_call_target="tpu_custom_call" | custom-call | flops 49999998976 | bytes 100000000 | tf_op jit(solution)/shard_map/stage/pallas_call | solution.py:130
  45.4 9.9 %collective-permute-done.1 = bf16[32,1152]{1,0:T(8,128)(2,1)S(1)} collective-permute-done((bf16[32,1152]{1,0:T(8,128)(2,1)S(1)}, bf16[32,1152]{1,0:T(8,128)(2,1)S(1)}, u32[]{:S(2)}, u32[]{:S(2)}) %collective-permute-start.1) | collective-permute-done | bytes 73760 | tf_op jit(solution)/shard_map/ppermute | solution.py:775
  56.9 2.7 %collective-permute-done.3 = bf16[32,1152]{1,0:T(8,128)(2,1)S(1)} collective-permute-done((bf16[32,1152]{1,0:T(8,128)(2,1)S(1)}, bf16[32,1152]{1,0:T(8,128)(2,1)S(1)}, u32[]{:S(2)}, u32[]{:S(2)}) %collective-permute-start.3) | collective-permute-done | bytes 73760 | tf_op jit(solution)/shard_map/ppermute | solution.py:775
  60.2 3.5 %far_own.1 = (bf16[1,768,1152]{2,1,0:T(8,128)(2,1)S(1)}, f32[1,768]{1,0:T(1,128)S(1)}, f32[768,256]{1,0:T(8,128)S(1)}) custom-call(s32[2]{0:T(128)S(1)} %get-tuple-element.61.place_ref, s32[2]{0:T(128)S(1)} %get-tuple-element.60.src_ref, f32[4,1,1152]{2,1,0:T(1,128)S(1)} %reshape.21.gain_ref, bf16[4,288,256]{2,1,0:T(8,128)(2,1)S(1)} %get-tuple-element.39.own_ref, ...), custom_call_target="tpu_custom_call" | custom-call | tf_op jit(solution)/shard_map/far_own/pallas_call | solution.py:284
  63.8 3.1 %far_kv.2 = (bf16[400,256]{1,0:T(8,128)(2,1)S(1)}, bf16[1,384,1152]{2,1,0:T(8,128)(2,1)S(1)}, f32[1,384]{1,0:T(1,128)S(1)}) custom-call(s32[2]{0:T(128)S(1)} %get-tuple-element.61.place_ref, s32[2]{0:T(128)S(1)} %get-tuple-element.60.src_ref, f32[4,1,1152]{2,1,0:T(1,128)S(1)} %reshape.21.gain_ref, f32[768,256]{1,0:T(8,128)S(1)} %get-tuple-element.42.part_ref, ...), custom_call_target="tpu_custom_call" | custom-call | tf_op jit(solution)/shard_map/far_kv/pallas_call | solution.py:306
  68.7 4.1 %far_kv.3 = (bf16[400,256]{1,0:T(8,128)(2,1)S(1)}, bf16[1,384,1152]{2,1,0:T(8,128)(2,1)S(1)}, f32[1,384]{1,0:T(1,128)S(1)}) custom-call(s32[2]{0:T(128)S(1)} %get-tuple-element.61.place_ref, s32[2]{0:T(128)S(1)} %get-tuple-element.60.src_ref, f32[4,1,1152]{2,1,0:T(1,128)S(1)} %reshape.21.gain_ref, f32[768,256]{1,0:T(8,128)S(1)} %get-tuple-element.42.part_ref, ...), custom_call_target="tpu_custom_call" | custom-call | tf_op jit(solution)/shard_map/far_kv/pallas_call | solution.py:306
  72.8 2.8 %collective-permute-start.17 = (bf16[400,256]{1,0:T(8,128)(2,1)S(1)}, bf16[400,256]{1,0:T(8,128)(2,1)S(1)}, u32[]{:S(2)}, u32[]{:S(2)}) collective-permute-start(bf16[400,256]{1,0:T(8,128)(2,1)S(1)} %get-tuple-element.48.rest_2_), channel_id=1, source_target_pairs={{0,2},{1,3},{2,0},{3,1},{4,6},{5,7},{6,4},{7,5},{8,10},{9,11},{10,... | collective-permute-start | bytes 614408 | tf_op jit(solution)/shard_map/ppermute | solution.py:826
  75.9 3.7 %collective-permute-done.15.rest_3_.rest_0_ = bf16[400,256]{1,0:T(8,128)(2,1)S(1)} collective-permute-done((bf16[400,256]{1,0:T(8,128)(2,1)S(1)}, bf16[400,256]{1,0:T(8,128)(2,1)S(1)}, u32[]{:S(2)}, u32[]{:S(2)}) %collective-permute-start.15) | collective-permute-done | bytes 204832 | tf_op jit(solution)/shard_map/ppermute | solution.py:826
  79.5 3.1 %far.1.refs_3_.rest_2_.rest_4_.x_ref = bf16[768,256]{1,0:T(8,128)(2,1)S(1)} custom-call(s32[2]{0:T(128)S(1)} %get-tuple-element.61.place_ref, s32[2]{0:T(128)S(1)} %get-tuple-element.60.src_ref, bf16[1,768,1152]{2,1,0:T(8,128)(2,1)S(1)} %get-tuple-element.40.own_x_ref, bf16[4,288,256]{2,1,0:T(8,128)(2,1)} %get-tuple-element.41.own_ref, ...), custom_call_target="tpu_custom_call" | custom-call | tf_op jit(solution)/shard_map/far/pallas_call | solution.py:364
  83.3 2.1 %collective-permute-start.16 = (bf16[2,3,32,1152]{3,2,1,0:T(8,128)(2,1)S(1)}, bf16[2,3,32,1152]{3,2,1,0:T(8,128)(2,1)}, u32[]{:S(2)}, u32[]{:S(2)}) collective-permute-start(bf16[2,3,32,1152]{3,2,1,0:T(8,128)(2,1)S(1)} %stage.8.rest_5_.refs_0_), channel_id=1, source_target_pairs={{0,16},{4,20},{8,24},{12,28},{16,0},{20,4},{24,8},{28,12},{1,17},{... | collective-permute-start | bytes 1327112 | tf_op jit(solution)/shard_map/ppermute | solution.py:805
  85.5 6.2 %near.1.near_ref = f32[768,512]{1,0:T(8,128)S(1)} custom-call(s32[2]{0:T(128)S(1)} %broadcast_add_fusion.src_ref, bf16[1,768,1152]{2,1,0:T(8,128)(2,1)} %copy-done.1, bf16[4608,128]{1,0:T(8,128)(2,1)S(1)} %copy-done.4, bf16[4608,128]{1,0:T(8,128)(2,1)S(1)} %copy-done.5, bf16[4608,256]{1,0:T(8,128)(2,1)} %q_ref.3, ...), custom_call_target="tpu_custom_call" | custom-call | tf_op jit(solution)/shard_map/near/pallas_call | solution.py:407
  94.3 2.1 %collective-permute-start.21 = (bf16[784,256]{1,0:T(8,128)(2,1)S(1)}, bf16[784,256]{1,0:T(8,128)(2,1)S(1)}, u32[]{:S(2)}, u32[]{:S(2)}) collective-permute-start(bf16[784,256]{1,0:T(8,128)(2,1)S(1)} %get-tuple-element.51.refs_3_.after_ref.rest_2_), channel_id=1, source_target_pairs={{0,4},{4,8},{8,12},{1,5},{5,9},{9,13},{2,6},{6,10},{10,14},{3,7},{... | collective-permute-start | bytes 1204232 | tf_op jit(solution)/shard_map/ppermute | solution.py:845
  97.8 7.9 %collective-permute-done.19.far_ref = bf16[768,256]{1,0:T(8,128)(2,1)S(1)} collective-permute-done((bf16[768,256]{1,0:T(8,128)(2,1)S(1)}, bf16[768,256]{1,0:T(8,128)(2,1)S(1)}, u32[]{:S(2)}, u32[]{:S(2)}) %collective-permute-start.19) | collective-permute-done | bytes 393248 | tf_op jit(solution)/shard_map/ppermute | solution.py:830
  107.1 2.9 %attend.2.rest_0_ = bf16[384,256]{1,0:T(8,128)(2,1)S(1)} custom-call(s32[1]{0:T(128)} %bitcast.16.seq_ref, bf16[768,256]{1,0:T(8,128)(2,1)S(1)} %queries.1.q_ref, s32[1,768]{1,0:T(1,128)S(1)} %broadcast_in_dim.21.id_ref, bf16[784,256]{1,0:T(8,128)(2,1)S(1)} %get-tuple-element.51.refs_3_.after_ref.rest_2_, ...), custom_call_target="tpu_custom_call" | custom-call | flops 905969664 | bytes 2359296 | tf_op jit(solution)/shard_map/attend/pallas_call | solution.py:583
  110.0 3.0 %collective-permute-start.23 = (bf16[384,256]{1,0:T(8,128)(2,1)S(1)}, bf16[384,256]{1,0:T(8,128)(2,1)S(1)}, u32[]{:S(2)}, u32[]{:S(2)}) collective-permute-start(bf16[384,256]{1,0:T(8,128)(2,1)S(1)} %attend.2.rest_0_), channel_id=1, source_target_pairs={{0,2},{1,3},{2,0},{3,1},{4,6},{5,7},{6,4},{7,5},{8,10},{9,11},{10,... | collective-permute-start | bytes 589832 | tf_op jit(solution)/shard_map/ppermute | solution.py:857
  115.7 4.0 %attend.3.rest_2_.after_ref.rest_0_ = bf16[384,256]{1,0:T(8,128)(2,1)S(1)} custom-call(s32[1]{0:T(128)} %bitcast.16.seq_ref, bf16[768,256]{1,0:T(8,128)(2,1)S(1)} %queries.1.q_ref, s32[1,768]{1,0:T(1,128)S(1)} %broadcast_in_dim.21.id_ref, bf16[3,256,1152]{2,1,0:T(8,128)(2,1)S(1)} %lay.1.after_ref.o_ref, ...), custom_call_target="tpu_custom_call" | custom-call | flops 905969664 | bytes 2359296 | tf_op jit(solution)/shard_map/attend/pallas_call | solution.py:583
  120.6 2.1 %collective-permute-start.26 = (bf16[384,256]{1,0:T(8,128)(2,1)S(1)}, bf16[384,256]{1,0:T(8,128)(2,1)S(1)}, u32[]{:S(2)}, u32[]{:S(2)}) collective-permute-start(bf16[384,256]{1,0:T(8,128)(2,1)S(1)} %attend.3.rest_2_.after_ref.rest_0_), channel_id=1, source_target_pairs={{0,2},{1,3},{2,0},{3,1},{4,6},{5,7},{6,4},{7,5},{8,10},{9,11},{10,... | collective-permute-start | bytes 589832 | tf_op jit(solution)/shard_map/ppermute | solution.py:857
  122.7 1.9 %collective-permute-start.24 = (bf16[384,256]{1,0:T(8,128)(2,1)S(1)}, bf16[384,256]{1,0:T(8,128)(2,1)S(1)}, u32[]{:S(2)}, u32[]{:S(2)}) collective-permute-start(bf16[384,256]{1,0:T(8,128)(2,1)S(1)} %gate.5.rest_0_), channel_id=1, source_target_pairs={{0,1},{1,0},{2,3},{3,2},{4,5},{5,4},{6,7},{7,6},{8,9},{9,8},{10,11... | collective-permute-start | bytes 589832 | tf_op jit(solution)/shard_map/ppermute | solution.py:861
  124.7 3.2 %first_output.2.part_ref = f32[384,1152]{1,0:T(8,128)S(1)} custom-call(s32[2]{0:T(128)S(1)} %pad_add_fusion.1.at_ref, bf16[256,4608]{1,0:T(8,128)(2,1)} %own_o_ref.3, bf16[3,256,1152]{2,1,0:T(8,128)(2,1)S(1)} %lay.1.after_ref.o_ref, bf16[384,256]{1,0:T(8,128)(2,1)S(1)} %attend.2.rest_0_, bf16[384,256]{1,0:T(8,128)(2,1)S(1)} %collective-permute-done.22.rest_1_, ...), custom_call_target="tpu_custom_call" | custom-call | flops 49999998976 | bytes 100000000 | tf_op jit(solution)/shard_map/first_output/pallas_call | solution.py:658
  127.9 2.1 %collective-permute-done.26.rest_0_ = bf16[384,256]{1,0:T(8,128)(2,1)S(1)} collective-permute-done((bf16[384,256]{1,0:T(8,128)(2,1)S(1)}, bf16[384,256]{1,0:T(8,128)(2,1)S(1)}, u32[]{:S(2)}, u32[]{:S(2)}) %collective-permute-start.26) | collective-permute-done | bytes 196640 | tf_op jit(solution)/shard_map/ppermute | solution.py:857
  130.1 4.6 %collective-permute-start.27 = (bf16[384,256]{1,0:T(8,128)(2,1)S(1)}, bf16[384,256]{1,0:T(8,128)(2,1)S(1)}, u32[]{:S(2)}, u32[]{:S(2)}) collective-permute-start(bf16[384,256]{1,0:T(8,128)(2,1)S(1)} %collective-permute-done.26.rest_0_), channel_id=1, source_target_pairs={{0,1},{1,0},{2,3},{3,2},{4,5},{5,4},{6,7},{7,6},{8,9},{9,8},{10,11... | collective-permute-start | bytes 589832 | tf_op jit(solution)/shard_map/ppermute | solution.py:861
  134.7 3.2 %first_output.3.part_ref = f32[384,1152]{1,0:T(8,128)S(1)} custom-call(s32[2]{0:T(128)S(1)} %pad_add_fusion.1.at_ref, bf16[256,4608]{1,0:T(8,128)(2,1)} %own_o_ref.3, bf16[3,256,1152]{2,1,0:T(8,128)(2,1)S(1)} %lay.1.after_ref.o_ref, bf16[384,256]{1,0:T(8,128)(2,1)S(1)} %attend.3.rest_2_.after_ref.rest_0_, ...), custom_call_target="tpu_custom_call" | custom-call | flops 49999998976 | bytes 100000000 | tf_op jit(solution)/shard_map/first_output/pallas_call | solution.py:658
  138.0 2.5 %last_output.2 = (f32[384,1152]{1,0:T(8,128)S(1)}, f32[1,384]{1,0:T(1,128)S(1)}) custom-call(s32[2]{0:T(128)S(1)} %pad_add_fusion.at_ref, f32[384,1152]{1,0:T(8,128)S(1)} %first_output.2.part_ref, bf16[3,256,1152]{2,1,0:T(8,128)(2,1)S(1)} %lay.1.after_ref.o_ref, bf16[384,256]{1,0:T(8,128)(2,1)S(1)} %gate.5.rest_0_, ...), custom_call_target="tpu_custom_call" | custom-call | tf_op jit(solution)/shard_map/last_output/pallas_call | solution.py:682
  140.5 2.5 %last_output.3 = (f32[384,1152]{1,0:T(8,128)S(1)}, f32[1,768]{1,0:T(1,128)S(1)}) custom-call(s32[2]{0:T(128)S(1)} %pad_add_fusion.at_ref, f32[384,1152]{1,0:T(8,128)S(1)} %first_output.3.part_ref, bf16[3,256,1152]{2,1,0:T(8,128)(2,1)S(1)} %lay.1.after_ref.o_ref, bf16[384,256]{1,0:T(8,128)(2,1)S(1)} %collective-permute-done.26.rest_0_, ...), custom_call_target="tpu_custom_call" | custom-call | tf_op jit(solution)/shard_map/last_output/pallas_call | solution.py:682
  143.9 3.1 %collective-permute-start.30 = (f32[1,768]{1,0:T(1,128)S(1)}, f32[1,768]{1,0:T(1,128)S(1)}, u32[]{:S(2)}, u32[]{:S(2)}) collective-permute-start(f32[1,768]{1,0:T(1,128)S(1)} %get-tuple-element.56.rest_2_), channel_id=1, source_target_pairs={{0,3},{1,0},{2,1},{3,2},{4,7},{5,4},{6,5},{7,6},{8,11},{9,8},{10,9... | collective-permute-start | bytes 9224 | tf_op jit(solution)/shard_map/ppermute | solution.py:876
  149.1 3.2 %finish.1 = bf16[768,1152]{1,0:T(8,128)(2,1)} custom-call(bf16[768,1152]{1,0:T(8,128)(2,1)S(1)} %copy-done, f32[1,1152]{1,0:T(1,128)S(1)} %broadcast_in_dim.17.gain_ref, f32[384,1152]{1,0:T(8,128)S(1)} %get-tuple-element.53.rest_0_, f32[384,1152]{1,0:T(8,128)S(1)} %get-tuple-element.55.rest_1_, f32[1,768]{1,0:T(1,128)S(1)} %get-tuple-element.56.rest_2_, ...), custom_call_target="tpu_custom_call" | custom-call | tf_op jit(solution)/shard_map/finish/pallas_call | solution.py:723
  (106 shorter events, 36.8 us)
Async XLA Ops:
  2.1 17.6 %collective-permute-start.10 = (bf16[128,1152]{1,0:T(8,128)(2,1)}, bf16[128,1152]{1,0:T(8,128)(2,1)S(1)}, u32[]{:S(2)}, u32[]{:S(2)}) collective-permute-start(bf16[128,1152]{1,0:T(8,128)(2,1)} %get-tuple-element.38), channel_id=1, source_target_pairs={{0,1},{1,0},{2,3},{3,2},{4,5},{5,4},{6,7},{7,6},{8,9},{9,8},{10,11... | collective-permute-start | bytes 884744 | tf_op jit(solution)/shard_map/ppermute | solution.py:771
  3.7 10.9 %collective-permute-start = (bf16[288,256]{1,0:T(8,128)(2,1)}, bf16[288,256]{1,0:T(8,128)(2,1)S(1)}, u32[]{:S(2)}, u32[]{:S(2)}) collective-permute-start(bf16[288,256]{1,0:T(8,128)(2,1)} %get-tuple-element.31), channel_id=1, source_target_pairs={{0,2},{1,3},{2,0},{3,1},{4,6},{5,7},{6,4},{7,5},{8,10},{9,11},{10,... | collective-permute-start | bytes 442376 | tf_op jit(solution)/shard_map/ppermute | solution.py:769
  6.3 13.4 %collective-permute-start.6 = (bf16[288,256]{1,0:T(8,128)(2,1)}, bf16[288,256]{1,0:T(8,128)(2,1)S(1)}, u32[]{:S(2)}, u32[]{:S(2)}) collective-permute-start(bf16[288,256]{1,0:T(8,128)(2,1)} %get-tuple-element.35), channel_id=1, source_target_pairs={{0,2},{1,3},{2,0},{3,1},{4,6},{5,7},{6,4},{7,5},{8,10},{9,11},{10,... | collective-permute-start | bytes 442376 | tf_op jit(solution)/shard_map/ppermute | solution.py:770
  19.8 17.4 %collective-permute-start.11 = (bf16[256,1152]{1,0:T(8,128)(2,1)S(1)}, bf16[256,1152]{1,0:T(8,128)(2,1)S(1)}, u32[]{:S(2)}, u32[]{:S(2)}) collective-permute-start(bf16[256,1152]{1,0:T(8,128)(2,1)S(1)} %stage.6), channel_id=1, source_target_pairs={{0,1},{1,0},{2,3},{3,2},{4,5},{5,4},{6,7},{7,6},{8,9},{9,8},{10,11... | collective-permute-start | bytes 1769480 | tf_op jit(solution)/shard_map/ppermute | solution.py:792
  20.3 5.1 %collective-permute-start.5 = (bf16[1,288,256]{2,1,0:T(8,128)(2,1)S(1)}, bf16[1,288,256]{2,1,0:T(8,128)(2,1)S(1)}, u32[]{:S(2)}, u32[]{:S(2)}) collective-permute-start(bf16[1,288,256]{2,1,0:T(8,128)(2,1)S(1)} %bitcast.19), channel_id=1, source_target_pairs={{0,8},{4,12},{8,0},{12,4},{16,24},{20,28},{24,16},{28,20},{1,9},{5... | collective-permute-start | bytes 442376 | tf_op jit(solution)/shard_map/ppermute | solution.py:794
  20.9 5.1 %collective-permute-start.7 = (bf16[1,288,256]{2,1,0:T(8,128)(2,1)S(1)}, bf16[1,288,256]{2,1,0:T(8,128)(2,1)S(1)}, u32[]{:S(2)}, u32[]{:S(2)}) collective-permute-start(bf16[1,288,256]{2,1,0:T(8,128)(2,1)S(1)} %bitcast.23), channel_id=1, source_target_pairs={{0,16},{4,20},{8,24},{12,28},{16,0},{20,4},{24,8},{28,12},{1,17},{... | collective-permute-start | bytes 442376 | tf_op jit(solution)/shard_map/ppermute | solution.py:795
  28.7 6.8 %collective-permute-start.8 = (bf16[2,288,256]{2,1,0:T(8,128)(2,1)S(1)}, bf16[2,288,256]{2,1,0:T(8,128)(2,1)}, u32[]{:S(2)}, u32[]{:S(2)}) collective-permute-start(bf16[2,288,256]{2,1,0:T(8,128)(2,1)S(1)} %get-tuple-element.36.refs_0_), channel_id=1, source_target_pairs={{0,16},{4,20},{8,24},{12,28},{16,0},{20,4},{24,8},{28,12},{1,17},{... | collective-permute-start | bytes 884744 | tf_op jit(solution)/shard_map/ppermute | solution.py:794
  30.2 7.0 %collective-permute-start.9 = (bf16[2,288,256]{2,1,0:T(8,128)(2,1)}, bf16[2,288,256]{2,1,0:T(8,128)(2,1)}, u32[]{:S(2)}, u32[]{:S(2)}) collective-permute-start(bf16[2,288,256]{2,1,0:T(8,128)(2,1)} %get-tuple-element.37.refs_2_), channel_id=1, source_target_pairs={{0,8},{4,12},{8,0},{12,4},{16,24},{20,28},{24,16},{28,20},{1,9},{5... | collective-permute-start | bytes 884744 | tf_op jit(solution)/shard_map/ppermute | solution.py:795
  31.7 37.0 %collective-permute-start.14 = (bf16[384,1152]{1,0:T(8,128)(2,1)}, bf16[384,1152]{1,0:T(8,128)(2,1)}, u32[]{:S(2)}, u32[]{:S(2)}) collective-permute-start(bf16[384,1152]{1,0:T(8,128)(2,1)} %copy-done.15), channel_id=1, source_target_pairs={{0,1},{1,0},{2,3},{3,2},{4,5},{5,4},{6,7},{7,6},{8,9},{9,8},{10,11... | collective-permute-start | bytes 2654216 | tf_op jit(solution)/shard_map/ppermute | solution.py:792
  39.5 20.8 %collective-permute-start.12 = (bf16[4,288,256]{2,1,0:T(8,128)(2,1)S(1)}, bf16[4,288,256]{2,1,0:T(8,128)(2,1)S(1)}, u32[]{:S(2)}, u32[]{:S(2)}) collective-permute-start(bf16[4,288,256]{2,1,0:T(8,128)(2,1)S(1)} %get-tuple-element.39.own_ref), channel_id=1, source_target_pairs={{0,4},{4,0},{8,12},{12,8},{16,20},{20,16},{24,28},{28,24},{1,5},{5... | collective-permute-start | bytes 1769480 | tf_op jit(solution)/shard_map/ppermute | solution.py:794
  39.6 24.2 %collective-permute-start.13 = (bf16[4,288,256]{2,1,0:T(8,128)(2,1)}, bf16[4,288,256]{2,1,0:T(8,128)(2,1)}, u32[]{:S(2)}, u32[]{:S(2)}) collective-permute-start(bf16[4,288,256]{2,1,0:T(8,128)(2,1)} %get-tuple-element.41.own_ref), channel_id=1, source_target_pairs={{0,4},{4,0},{8,12},{12,8},{16,20},{20,16},{24,28},{28,24},{1,5},{5... | collective-permute-start | bytes 1769480 | tf_op jit(solution)/shard_map/ppermute | solution.py:795
  42.5 21.3 %copy-start.12 = (bf16[128,1152]{1,0:T(8,128)(2,1)S(1)}, bf16[128,1152]{1,0:T(8,128)(2,1)}, u32[]{:S(2)}) copy-start(bf16[128,1152]{1,0:T(8,128)(2,1)} %copy-done.11) | copy-start | bytes 884740
  42.5 12.7 %collective-permute-start.1 = (bf16[32,1152]{1,0:T(8,128)(2,1)S(1)}, bf16[32,1152]{1,0:T(8,128)(2,1)S(1)}, u32[]{:S(2)}, u32[]{:S(2)}) collective-permute-start(bf16[32,1152]{1,0:T(8,128)(2,1)S(1)} %get-tuple-element.32), channel_id=1, source_target_pairs={{0,1},{1,2},{2,3},{3,0},{4,5},{5,6},{6,7},{7,4},{8,9},{9,10},{10,1... | collective-permute-start | bytes 221192 | tf_op jit(solution)/shard_map/ppermute | solution.py:775
  44.2 12.7 %collective-permute-start.2 = (bf16[32,1152]{1,0:T(8,128)(2,1)S(1)}, bf16[32,1152]{1,0:T(8,128)(2,1)S(1)}, u32[]{:S(2)}, u32[]{:S(2)}) collective-permute-start(bf16[32,1152]{1,0:T(8,128)(2,1)S(1)} %get-tuple-element.33), channel_id=1, source_target_pairs={{0,2},{1,3},{2,0},{3,1},{4,6},{5,7},{6,4},{7,5},{8,10},{9,11},{10,... | collective-permute-start | bytes 221192 | tf_op jit(solution)/shard_map/ppermute | solution.py:775
  55.2 4.4 %collective-permute-start.3 = (bf16[32,1152]{1,0:T(8,128)(2,1)S(1)}, bf16[32,1152]{1,0:T(8,128)(2,1)S(1)}, u32[]{:S(2)}, u32[]{:S(2)}) collective-permute-start(bf16[32,1152]{1,0:T(8,128)(2,1)S(1)} %get-tuple-element.34), channel_id=1, source_target_pairs={{0,3},{1,0},{2,1},{3,2},{4,7},{5,4},{6,5},{7,6},{8,11},{9,8},{10,9... | collective-permute-start | bytes 221192 | tf_op jit(solution)/shard_map/ppermute | solution.py:775
  59.6 23.1 %collective-permute-start.4 = (bf16[1,3,32,1152]{3,2,1,0:T(8,128)(2,1)S(1)}, bf16[1,3,32,1152]{3,2,1,0:T(8,128)(2,1)S(1)}, u32[]{:S(2)}, u32[]{:S(2)}) collective-permute-start(bf16[1,3,32,1152]{3,2,1,0:T(8,128)(2,1)S(1)} %maximum_bitcast_fusion.refs_0_), channel_id=1, source_target_pairs={{0,8},{4,12},{8,0},{12,4},{16,24},{20,28},{24,16},{28,20},{1,9},{5... | collective-permute-start | bytes 663560 | tf_op jit(solution)/shard_map/ppermute | solution.py:805
  66.9 12.6 %collective-permute-start.15 = (bf16[400,256]{1,0:T(8,128)(2,1)S(1)}, bf16[400,256]{1,0:T(8,128)(2,1)S(1)}, u32[]{:S(2)}, u32[]{:S(2)}) collective-permute-start(bf16[400,256]{1,0:T(8,128)(2,1)S(1)} %get-tuple-element.46.rest_1_), channel_id=1, source_target_pairs={{0,2},{1,3},{2,0},{3,1},{4,6},{5,7},{6,4},{7,5},{8,10},{9,11},{10,... | collective-permute-start | bytes 614408 | tf_op jit(solution)/shard_map/ppermute | solution.py:826
  72.8 18.9 %collective-permute-start.17 = (bf16[400,256]{1,0:T(8,128)(2,1)S(1)}, bf16[400,256]{1,0:T(8,128)(2,1)S(1)}, u32[]{:S(2)}, u32[]{:S(2)}) collective-permute-start(bf16[400,256]{1,0:T(8,128)(2,1)S(1)} %get-tuple-element.48.rest_2_), channel_id=1, source_target_pairs={{0,2},{1,3},{2,0},{3,1},{4,6},{5,7},{6,4},{7,5},{8,10},{9,11},{10,... | collective-permute-start | bytes 614408 | tf_op jit(solution)/shard_map/ppermute | solution.py:826
  83.3 13.1 %collective-permute-start.16 = (bf16[2,3,32,1152]{3,2,1,0:T(8,128)(2,1)S(1)}, bf16[2,3,32,1152]{3,2,1,0:T(8,128)(2,1)}, u32[]{:S(2)}, u32[]{:S(2)}) collective-permute-start(bf16[2,3,32,1152]{3,2,1,0:T(8,128)(2,1)S(1)} %stage.8.rest_5_.refs_0_), channel_id=1, source_target_pairs={{0,16},{4,20},{8,24},{12,28},{16,0},{20,4},{24,8},{28,12},{1,17},{... | collective-permute-start | bytes 1327112 | tf_op jit(solution)/shard_map/ppermute | solution.py:805
  92.8 12.9 %collective-permute-start.19 = (bf16[768,256]{1,0:T(8,128)(2,1)S(1)}, bf16[768,256]{1,0:T(8,128)(2,1)S(1)}, u32[]{:S(2)}, u32[]{:S(2)}) collective-permute-start(bf16[768,256]{1,0:T(8,128)(2,1)S(1)} %gate.4), channel_id=1, source_target_pairs={{0,2},{1,3},{2,0},{3,1},{4,6},{5,7},{6,4},{7,5},{8,10},{9,11},{10,... | collective-permute-start | bytes 1179656 | tf_op jit(solution)/shard_map/ppermute | solution.py:830
  92.9 13.5 %collective-permute-start.20 = (bf16[784,256]{1,0:T(8,128)(2,1)S(1)}, bf16[784,256]{1,0:T(8,128)(2,1)S(1)}, u32[]{:S(2)}, u32[]{:S(2)}) collective-permute-start(bf16[784,256]{1,0:T(8,128)(2,1)S(1)} %get-tuple-element.51.refs_3_.after_ref.rest_2_), channel_id=1, source_target_pairs={{0,8},{4,12},{1,9},{5,13},{2,10},{6,14},{3,11},{7,15},{16,24},{20,... | collective-permute-start | bytes 1204232 | tf_op jit(solution)/shard_map/ppermute | solution.py:845
  94.3 12.8 %collective-permute-start.21 = (bf16[784,256]{1,0:T(8,128)(2,1)S(1)}, bf16[784,256]{1,0:T(8,128)(2,1)S(1)}, u32[]{:S(2)}, u32[]{:S(2)}) collective-permute-start(bf16[784,256]{1,0:T(8,128)(2,1)S(1)} %get-tuple-element.51.refs_3_.after_ref.rest_2_), channel_id=1, source_target_pairs={{0,4},{4,8},{8,12},{1,5},{5,9},{9,13},{2,6},{6,10},{10,14},{3,7},{... | collective-permute-start | bytes 1204232 | tf_op jit(solution)/shard_map/ppermute | solution.py:845
  97.7 16.5 %collective-permute-start.18 = (bf16[4,3,32,1152]{3,2,1,0:T(8,128)(2,1)S(1)}, bf16[4,3,32,1152]{3,2,1,0:T(8,128)(2,1)S(1)}, u32[]{:S(2)}, u32[]{:S(2)}) collective-permute-start(bf16[4,3,32,1152]{3,2,1,0:T(8,128)(2,1)S(1)} %stage.9.own_ref), channel_id=1, source_target_pairs={{0,4},{4,0},{8,12},{12,8},{16,20},{20,16},{24,28},{28,24},{1,5},{5... | collective-permute-start | bytes 2654216 | tf_op jit(solution)/shard_map/ppermute | solution.py:805
  110.0 12.7 %collective-permute-start.23 = (bf16[384,256]{1,0:T(8,128)(2,1)S(1)}, bf16[384,256]{1,0:T(8,128)(2,1)S(1)}, u32[]{:S(2)}, u32[]{:S(2)}) collective-permute-start(bf16[384,256]{1,0:T(8,128)(2,1)S(1)} %attend.2.rest_0_), channel_id=1, source_target_pairs={{0,2},{1,3},{2,0},{3,1},{4,6},{5,7},{6,4},{7,5},{8,10},{9,11},{10,... | collective-permute-start | bytes 589832 | tf_op jit(solution)/shard_map/ppermute | solution.py:857
  113.0 11.7 %collective-permute-start.22 = (bf16[384,256]{1,0:T(8,128)(2,1)S(1)}, bf16[384,256]{1,0:T(8,128)(2,1)S(1)}, u32[]{:S(2)}, u32[]{:S(2)}) collective-permute-start(bf16[384,256]{1,0:T(8,128)(2,1)S(1)} %attend.2.rest_0_), channel_id=1, source_target_pairs={{0,1},{1,0},{2,3},{3,2},{4,5},{5,4},{6,7},{7,6},{8,9},{9,8},{10,11... | collective-permute-start | bytes 589832 | tf_op jit(solution)/shard_map/ppermute | solution.py:858
  119.7 15.0 %collective-permute-start.25 = (bf16[384,256]{1,0:T(8,128)(2,1)S(1)}, bf16[384,256]{1,0:T(8,128)(2,1)S(1)}, u32[]{:S(2)}, u32[]{:S(2)}) collective-permute-start(bf16[384,256]{1,0:T(8,128)(2,1)S(1)} %attend.3.rest_2_.after_ref.rest_0_), channel_id=1, source_target_pairs={{0,1},{1,0},{2,3},{3,2},{4,5},{5,4},{6,7},{7,6},{8,9},{9,8},{10,11... | collective-permute-start | bytes 589832 | tf_op jit(solution)/shard_map/ppermute | solution.py:858
  120.6 9.5 %collective-permute-start.26 = (bf16[384,256]{1,0:T(8,128)(2,1)S(1)}, bf16[384,256]{1,0:T(8,128)(2,1)S(1)}, u32[]{:S(2)}, u32[]{:S(2)}) collective-permute-start(bf16[384,256]{1,0:T(8,128)(2,1)S(1)} %attend.3.rest_2_.after_ref.rest_0_), channel_id=1, source_target_pairs={{0,2},{1,3},{2,0},{3,1},{4,6},{5,7},{6,4},{7,5},{8,10},{9,11},{10,... | collective-permute-start | bytes 589832 | tf_op jit(solution)/shard_map/ppermute | solution.py:857
  122.7 15.2 %collective-permute-start.24 = (bf16[384,256]{1,0:T(8,128)(2,1)S(1)}, bf16[384,256]{1,0:T(8,128)(2,1)S(1)}, u32[]{:S(2)}, u32[]{:S(2)}) collective-permute-start(bf16[384,256]{1,0:T(8,128)(2,1)S(1)} %gate.5.rest_0_), channel_id=1, source_target_pairs={{0,1},{1,0},{2,3},{3,2},{4,5},{5,4},{6,7},{7,6},{8,9},{9,8},{10,11... | collective-permute-start | bytes 589832 | tf_op jit(solution)/shard_map/ppermute | solution.py:861
  130.1 10.4 %collective-permute-start.27 = (bf16[384,256]{1,0:T(8,128)(2,1)S(1)}, bf16[384,256]{1,0:T(8,128)(2,1)S(1)}, u32[]{:S(2)}, u32[]{:S(2)}) collective-permute-start(bf16[384,256]{1,0:T(8,128)(2,1)S(1)} %collective-permute-done.26.rest_0_), channel_id=1, source_target_pairs={{0,1},{1,0},{2,3},{3,2},{4,5},{5,4},{6,7},{7,6},{8,9},{9,8},{10,11... | collective-permute-start | bytes 589832 | tf_op jit(solution)/shard_map/ppermute | solution.py:861
  143.1 5.4 %collective-permute-start.28 = (f32[1,768]{1,0:T(1,128)S(1)}, f32[1,768]{1,0:T(1,128)S(1)}, u32[]{:S(2)}, u32[]{:S(2)}) collective-permute-start(f32[1,768]{1,0:T(1,128)S(1)} %get-tuple-element.56.rest_2_), channel_id=1, source_target_pairs={{0,1},{1,2},{2,3},{3,0},{4,5},{5,6},{6,7},{7,4},{8,9},{9,10},{10,1... | collective-permute-start | bytes 9224 | tf_op jit(solution)/shard_map/ppermute | solution.py:876
  143.1 5.4 %collective-permute-start.29 = (f32[1,768]{1,0:T(1,128)S(1)}, f32[1,768]{1,0:T(1,128)S(1)}, u32[]{:S(2)}, u32[]{:S(2)}) collective-permute-start(f32[1,768]{1,0:T(1,128)S(1)} %get-tuple-element.56.rest_2_), channel_id=1, source_target_pairs={{0,2},{1,3},{2,0},{3,1},{4,6},{5,7},{6,4},{7,5},{8,10},{9,11},{10,... | collective-permute-start | bytes 9224 | tf_op jit(solution)/shard_map/ppermute | solution.py:876
  143.9 5.2 %collective-permute-start.30 = (f32[1,768]{1,0:T(1,128)S(1)}, f32[1,768]{1,0:T(1,128)S(1)}, u32[]{:S(2)}, u32[]{:S(2)}) collective-permute-start(f32[1,768]{1,0:T(1,128)S(1)} %get-tuple-element.56.rest_2_), channel_id=1, source_target_pairs={{0,3},{1,0},{2,1},{3,2},{4,7},{5,4},{6,5},{7,6},{8,11},{9,8},{10,9... | collective-permute-start | bytes 9224 | tf_op jit(solution)/shard_map/ppermute | solution.py:876
  (18 other events, 164.2 us)

commit v20 on v15

--- a/solution.py
+++ b/solution.py
@@ -16,7 +16,7 @@
 rope_base = 10000.0
 NEG = -1e30
 Q_TILE = 128
-K_TILE = 384
+K_TILE = 256
 CHUNKS = 2
 LANES = 128
 TAIL = 16

time: 148 us -> 149 us (level)
  Pallas kernels: 52.7 us -> 55.7 us
    pallas_call x2, Pallas kernels: 7.01 us -> 10.1 us  [attend(): pl.pallas_call(partial(attention_kernel, back=back, offset=c * rows), out...]
    ppermute x2, waiting for transfers between devices: 1.93 us -> 0.01 us  [per_device(): beside = lax.ppermute(context, 'tensor', pairs)]
    ppermute x2, waiting for transfers between devices: 2.83 us -> 4.71 us  [per_device(): opposite = lax.ppermute(context, 'tensor', swap)]
  transfers between devices with their start and end apart: 30 -> 30, of which waited for: 18 -> 15; matrix products, arithmetic and copies ran while one was open for 1% -> 1% of each run, Pallas kernels for 28% -> 29%
where the time goes in v20:
time: 149 us; the launch traced here: 148 us
  Pallas kernels  55.7 us (37%)
  waiting for transfers between devices  53.2 us (36%)
  starting transfers between devices  34.6 us (23%)
  other arithmetic  2.08 us (1%)
  local copies, waits for them, and re-layouts  1.77 us (1%)
    ppermute x1, waiting for transfers between devices, per_device(): got_q = lax.ppermute(gate(sent_q, got_kv), 'tensor', swap)  13.6 us
    pallas_call x2, Pallas kernels, attend(): pl.pallas_call(partial(attention_kernel, back=back, offset=c * rows), out...  10.1 us
    ppermute x3, waiting for transfers between devices, per_device(): lax.ppermute(p, 'tensor', turn(k + 1))  8.87 us
    ppermute x1, waiting for transfers between devices, per_device(): own_kv = lax.ppermute(packed_kv, 'tensor', swap)[None]  8.01 us
    pallas_call x5, Pallas kernels, stage(): pl.pallas_call(partial(stage_kernel, pairs=len(joined), first=first, coun...  7.53 us
    pallas_call x2, Pallas kernels, first_output(): pl.pallas_call(first_output_kernel, out_shape=shape((chunk, cols), F32),...  6.48 us
    pallas_call x1, Pallas kernels, near_product(): pl.pallas_call(near_kernel, out_shape=shape((rows, sum(widths)), F32), gr...  6.14 us
    pallas_call x2, Pallas kernels, last_output(): pl.pallas_call(last_output_kernel, out_shape=(shape((chunk, cols), F32),...  5.07 us
  transfers between devices with their start and end apart: 30, of which 15 were waited for; matrix products, arithmetic and copies ran while one was open for 1% of the time, Pallas kernels for 29%

profile of v20, /device:TPU:2, one launch (start us, length us, event | category | flops | bytes accessed | tf_op | source)
XLA Modules:
  0.0 147.8 jit_solution(6461124108436090833)
XLA Ops:
  0.0 2.1 %pack.1 = (bf16[288,256]{1,0:T(8,128)(2,1)}, bf16[288,256]{1,0:T(8,128)(2,1)}, bf16[128,1152]{1,0:T(8,128)(2,1)}) custom-call(s32[1]{0:T(128)} %bitcast.9.at_ref, bf16[4608,256]{1,0:T(8,128)(2,1)} %q_ref.3, bf16[4608,128]{1,0:T(8,128)(2,1)} %k_ref.3, bf16[4608,128]{1,0:T(8,128)(2,1)} %v_ref.3, bf16[768,1152]{1,0:T(8,128)(2,1)} %token_ref.1), custom_call_target="tpu_custom_call" | custom-call | tf_op jit(solution)/shard_map/pack/pallas_call | solution.py:75
  2.1 1.6 %collective-permute-start.10 = (bf16[128,1152]{1,0:T(8,128)(2,1)}, bf16[128,1152]{1,0:T(8,128)(2,1)S(1)}, u32[]{:S(2)}, u32[]{:S(2)}) collective-permute-start(bf16[128,1152]{1,0:T(8,128)(2,1)} %get-tuple-element.35), channel_id=1, source_target_pairs={{0,1},{1,0},{2,3},{3,2},{4,5},{5,4},{6,7},{7,6},{8,9},{9,8},{10,11... | collective-permute-start | bytes 884744 | tf_op jit(solution)/shard_map/ppermute | solution.py:752
  3.7 2.6 %collective-permute-start = (bf16[288,256]{1,0:T(8,128)(2,1)}, bf16[288,256]{1,0:T(8,128)(2,1)S(1)}, u32[]{:S(2)}, u32[]{:S(2)}) collective-permute-start(bf16[288,256]{1,0:T(8,128)(2,1)} %get-tuple-element.28), channel_id=1, source_target_pairs={{0,2},{1,3},{2,0},{3,1},{4,6},{5,7},{6,4},{7,5},{8,10},{9,11},{10,... | collective-permute-start | bytes 442376 | tf_op jit(solution)/shard_map/ppermute | solution.py:750
  6.7 8.0 %collective-permute-done = bf16[288,256]{1,0:T(8,128)(2,1)S(1)} collective-permute-done((bf16[288,256]{1,0:T(8,128)(2,1)}, bf16[288,256]{1,0:T(8,128)(2,1)S(1)}, u32[]{:S(2)}, u32[]{:S(2)}) %collective-permute-start) | collective-permute-done | bytes 147488 | tf_op jit(solution)/shard_map/ppermute | solution.py:750
  14.7 5.0 %collective-permute-done.6 = bf16[288,256]{1,0:T(8,128)(2,1)S(1)} collective-permute-done((bf16[288,256]{1,0:T(8,128)(2,1)}, bf16[288,256]{1,0:T(8,128)(2,1)S(1)}, u32[]{:S(2)}, u32[]{:S(2)}) %collective-permute-start.6) | collective-permute-done | bytes 147488 | tf_op jit(solution)/shard_map/ppermute | solution.py:751
  23.2 3.1 %collective-permute-done.5.refs_1_ = bf16[1,288,256]{2,1,0:T(8,128)(2,1)S(1)} collective-permute-done((bf16[1,288,256]{2,1,0:T(8,128)(2,1)S(1)}, bf16[1,288,256]{2,1,0:T(8,128)(2,1)S(1)}, u32[]{:S(2)}, u32[]{:S(2)}) %collective-permute-start.5) | collective-permute-done | bytes 147488 | tf_op jit(solution)/shard_map/ppermute | solution.py:775
  26.9 2.0 %stage.5 = (bf16[2,288,256]{2,1,0:T(8,128)(2,1)}, bf16[2,288,256]{2,1,0:T(8,128)(2,1)}, bf16[288,1152]{1,0:T(8,128)(2,1)}) custom-call(bf16[1,288,256]{2,1,0:T(8,128)(2,1)S(1)} %bitcast.20, bf16[1,288,256]{2,1,0:T(8,128)(2,1)S(1)} %collective-permute-done.5.refs_1_, bf16[1,288,256]{2,1,0:T(8,128)(2,1)S(1)} %bitcast.24, ...), custom_call_target="tpu_custom_call" | custom-call | tf_op jit(solution)/shard_map/stage/pallas_call | solution.py:130
  32.1 1.7 %copy-done.5 = bf16[256,4608]{1,0:T(8,128)(2,1)S(1)} copy-done((bf16[256,4608]{1,0:T(8,128)(2,1)S(1)}, bf16[256,4608]{1,0:T(8,128)(2,1)}, u32[]{:S(2)}) %copy-start.5) | copy-done | bytes 2359320
  37.2 5.7 %collective-permute-done.1.refs_6_ = bf16[32,1152]{1,0:T(8,128)(2,1)S(1)} collective-permute-done((bf16[32,1152]{1,0:T(8,128)(2,1)S(1)}, bf16[32,1152]{1,0:T(8,128)(2,1)S(1)}, u32[]{:S(2)}, u32[]{:S(2)}) %collective-permute-start.1) | collective-permute-done | bytes 73760 | tf_op jit(solution)/shard_map/ppermute | solution.py:756
  42.9 2.0 %collective-permute-start.13 = (bf16[288,1152]{1,0:T(8,128)(2,1)}, bf16[288,1152]{1,0:T(8,128)(2,1)S(1)}, u32[]{:S(2)}, u32[]{:S(2)}) collective-permute-start(bf16[288,1152]{1,0:T(8,128)(2,1)} %get-tuple-element.40), channel_id=1, source_target_pairs={{0,1},{1,0},{2,3},{3,2},{4,5},{5,4},{6,7},{7,6},{8,9},{9,8},{10,11... | collective-permute-start | bytes 1990664 | tf_op jit(solution)/shard_map/ppermute | solution.py:773
  45.0 3.2 %collective-permute-done.3.refs_8_ = bf16[32,1152]{1,0:T(8,128)(2,1)S(1)} collective-permute-done((bf16[32,1152]{1,0:T(8,128)(2,1)S(1)}, bf16[32,1152]{1,0:T(8,128)(2,1)S(1)}, u32[]{:S(2)}, u32[]{:S(2)}) %collective-permute-start.3) | collective-permute-done | bytes 73760 | tf_op jit(solution)/shard_map/ppermute | solution.py:756
  48.2 2.6 %stage.7 = (bf16[4,288,256]{2,1,0:T(8,128)(2,1)}, bf16[4,288,256]{2,1,0:T(8,128)(2,1)}) custom-call(bf16[2,288,256]{2,1,0:T(8,128)(2,1)} %get-tuple-element.33.refs_0_, bf16[2,288,256]{2,1,0:T(8,128)(2,1)} %collective-permute-done.8.refs_1_, bf16[2,288,256]{2,1,0:T(8,128)(2,1)} %get-tuple-element.34.refs_2_, ...), custom_call_target="tpu_custom_call" | custom-call | flops 49999998976 | bytes 100000000 | tf_op jit(solution)/shard_map/stage/pallas_call | solution.py:130
  51.5 1.7 %collective-permute-done.12.got_ref = bf16[4,288,256]{2,1,0:T(8,128)(2,1)} collective-permute-done((bf16[4,288,256]{2,1,0:T(8,128)(2,1)}, bf16[4,288,256]{2,1,0:T(8,128)(2,1)}, u32[]{:S(2)}, u32[]{:S(2)}) %collective-permute-start.12) | collective-permute-done | bytes 589856 | tf_op jit(solution)/shard_map/ppermute | solution.py:775
  53.3 3.0 %far_own.1 = (bf16[1,768,1152]{2,1,0:T(8,128)(2,1)S(1)}, f32[1,768]{1,0:T(1,128)S(1)}, f32[768,256]{1,0:T(8,128)S(1)}) custom-call(s32[2]{0:T(128)S(1)} %get-tuple-element.55.place_ref, s32[2]{0:T(128)S(1)} %get-tuple-element.54.src_ref, f32[4,1,1152]{2,1,0:T(1,128)S(1)} %reshape.21.gain_ref, bf16[4,288,256]{2,1,0:T(8,128)(2,1)} %get-tuple-element.36.own_ref, ...), custom_call_target="tpu_custom_call" | custom-call | tf_op jit(solution)/shard_map/far_own/pallas_call | solution.py:283
  57.9 3.7 %far_kv.1 = (bf16[784,256]{1,0:T(8,128)(2,1)S(1)}, bf16[1,768,1152]{2,1,0:T(8,128)(2,1)}, f32[1,768]{1,0:T(1,128)S(1)}) custom-call(s32[2]{0:T(128)S(1)} %get-tuple-element.55.place_ref, s32[2]{0:T(128)S(1)} %get-tuple-element.54.src_ref, f32[4,1,1152]{2,1,0:T(1,128)S(1)} %reshape.21.gain_ref, f32[768,256]{1,0:T(8,128)S(1)} %get-tuple-element.38.part_ref, ...), custom_call_target="tpu_custom_call" | custom-call | tf_op jit(solution)/shard_map/far_kv/pallas_call | solution.py:305
  61.6 2.0 %collective-permute-start.16 = (bf16[784,256]{1,0:T(8,128)(2,1)S(1)}, bf16[784,256]{1,0:T(8,128)(2,1)S(1)}, u32[]{:S(2)}, u32[]{:S(2)}) collective-permute-start(bf16[784,256]{1,0:T(8,128)(2,1)S(1)} %get-tuple-element.43.rest_0_), channel_id=1, source_target_pairs={{0,2},{1,3},{2,0},{3,1},{4,6},{5,7},{6,4},{7,5},{8,10},{9,11},{10,... | collective-permute-start | bytes 1204232 | tf_op jit(solution)/shard_map/ppermute | solution.py:799
  65.8 6.1 %near.1.rest_0_.near_ref = f32[768,512]{1,0:T(8,128)S(1)} custom-call(s32[2]{0:T(128)S(1)} %broadcast_add_fusion.src_ref, bf16[1,768,1152]{2,1,0:T(8,128)(2,1)S(1)} %get-tuple-element.37.own_x_ref, bf16[1,768,1152]{2,1,0:T(8,128)(2,1)} %get-tuple-element.42.x_ref, bf16[4608,128]{1,0:T(8,128)(2,1)S(1)} %copy-done.3, bf16[4608,128]{1,0:T(8,128)(2,1)S(1)} %copy-done.4, ...), custom_call_target="tpu_custom_call" | custom-call | tf_op jit(solution)/shard_map/near/pallas_call | solution.py:398
  71.9 4.4 %far.1.refs_3_.rest_0_.x_ref = bf16[768,256]{1,0:T(8,128)(2,1)S(1)} custom-call(s32[2]{0:T(128)S(1)} %get-tuple-element.55.place_ref, s32[2]{0:T(128)S(1)} %get-tuple-element.54.src_ref, bf16[1,768,1152]{2,1,0:T(8,128)(2,1)S(1)} %get-tuple-element.37.own_x_ref, bf16[1,768,1152]{2,1,0:T(8,128)(2,1)} %get-tuple-element.42.x_ref, ...), custom_call_target="tpu_custom_call" | custom-call | tf_op jit(solution)/shard_map/far/pallas_call | solution.py:355
  82.4 2.1 %collective-permute-start.20 = (bf16[784,256]{1,0:T(8,128)(2,1)S(1)}, bf16[784,256]{1,0:T(8,128)(2,1)S(1)}, u32[]{:S(2)}, u32[]{:S(2)}) collective-permute-start(bf16[784,256]{1,0:T(8,128)(2,1)S(1)} %get-tuple-element.45.refs_3_.after_ref.rest_2_), channel_id=1, source_target_pairs={{0,4},{4,8},{8,12},{1,5},{5,9},{9,13},{2,6},{6,10},{10,14},{3,7},{... | collective-permute-start | bytes 1204232 | tf_op jit(solution)/shard_map/ppermute | solution.py:822
  86.9 13.6 %collective-permute-done.18.far_ref = bf16[768,256]{1,0:T(8,128)(2,1)} collective-permute-done((bf16[768,256]{1,0:T(8,128)(2,1)S(1)}, bf16[768,256]{1,0:T(8,128)(2,1)}, u32[]{:S(2)}, u32[]{:S(2)}) %collective-permute-start.18) | collective-permute-done | bytes 393248 | tf_op jit(solution)/shard_map/ppermute | solution.py:808
  102.1 4.5 %attend.2.rest_0_ = bf16[384,256]{1,0:T(8,128)(2,1)S(1)} custom-call(s32[1]{0:T(128)} %bitcast.16.seq_ref, bf16[768,256]{1,0:T(8,128)(2,1)S(1)} %queries.1.q_ref, s32[1,768]{1,0:T(1,128)S(1)} %broadcast_in_dim.21.id_ref, bf16[784,256]{1,0:T(8,128)(2,1)S(1)} %get-tuple-element.45.refs_3_.after_ref.rest_2_, ...), custom_call_target="tpu_custom_call" | custom-call | flops 905969664 | bytes 2359296 | tf_op jit(solution)/shard_map/attend/pallas_call | solution.py:564
  106.7 2.5 %collective-permute-start.21 = (bf16[384,256]{1,0:T(8,128)(2,1)S(1)}, bf16[384,256]{1,0:T(8,128)(2,1)S(1)}, u32[]{:S(2)}, u32[]{:S(2)}) collective-permute-start(bf16[384,256]{1,0:T(8,128)(2,1)S(1)} %attend.2.rest_0_), channel_id=1, source_target_pairs={{0,1},{1,0},{2,3},{3,2},{4,5},{5,4},{6,7},{7,6},{8,9},{9,8},{10,11... | collective-permute-start | bytes 589832 | tf_op jit(solution)/shard_map/ppermute | solution.py:835
  110.7 5.6 %attend.3.rest_2_.after_ref.rest_0_ = bf16[384,256]{1,0:T(8,128)(2,1)S(1)} custom-call(s32[1]{0:T(128)} %bitcast.16.seq_ref, bf16[768,256]{1,0:T(8,128)(2,1)S(1)} %queries.1.q_ref, s32[1,768]{1,0:T(1,128)S(1)} %broadcast_in_dim.21.id_ref, bf16[3,256,1152]{2,1,0:T(8,128)(2,1)S(1)} %lay.1.after_ref.o_ref, ...), custom_call_target="tpu_custom_call" | custom-call | flops 905969664 | bytes 2359296 | tf_op jit(solution)/shard_map/attend/pallas_call | solution.py:564
  116.4 2.4 %collective-permute-start.25 = (bf16[384,256]{1,0:T(8,128)(2,1)S(1)}, bf16[384,256]{1,0:T(8,128)(2,1)S(1)}, u32[]{:S(2)}, u32[]{:S(2)}) collective-permute-start(bf16[384,256]{1,0:T(8,128)(2,1)S(1)} %attend.3.rest_2_.after_ref.rest_0_), channel_id=1, source_target_pairs={{0,2},{1,3},{2,0},{3,1},{4,6},{5,7},{6,4},{7,5},{8,10},{9,11},{10,... | collective-permute-start | bytes 589832 | tf_op jit(solution)/shard_map/ppermute | solution.py:834
  118.8 3.2 %first_output.2.part_ref = f32[384,1152]{1,0:T(8,128)S(1)} custom-call(s32[2]{0:T(128)S(1)} %pad_add_fusion.1.at_ref, bf16[256,4608]{1,0:T(8,128)(2,1)} %own_o_ref.3, bf16[3,256,1152]{2,1,0:T(8,128)(2,1)S(1)} %lay.1.after_ref.o_ref, bf16[384,256]{1,0:T(8,128)(2,1)S(1)} %attend.2.rest_0_, bf16[384,256]{1,0:T(8,128)(2,1)S(1)} %collective-permute-done.21.rest_1_, ...), custom_call_target="tpu_custom_call" | custom-call | flops 49999998976 | bytes 100000000 | tf_op jit(solution)/shard_map/first_output/pallas_call | solution.py:639
  122.1 4.7 %collective-permute-done.25.rest_0_ = bf16[384,256]{1,0:T(8,128)(2,1)S(1)} collective-permute-done((bf16[384,256]{1,0:T(8,128)(2,1)S(1)}, bf16[384,256]{1,0:T(8,128)(2,1)S(1)}, u32[]{:S(2)}, u32[]{:S(2)}) %collective-permute-start.25) | collective-permute-done | bytes 196640 | tf_op jit(solution)/shard_map/ppermute | solution.py:834
  126.8 2.0 %collective-permute-start.26 = (bf16[384,256]{1,0:T(8,128)(2,1)S(1)}, bf16[384,256]{1,0:T(8,128)(2,1)S(1)}, u32[]{:S(2)}, u32[]{:S(2)}) collective-permute-start(bf16[384,256]{1,0:T(8,128)(2,1)S(1)} %collective-permute-done.25.rest_0_), channel_id=1, source_target_pairs={{0,1},{1,0},{2,3},{3,2},{4,5},{5,4},{6,7},{7,6},{8,9},{9,8},{10,11... | collective-permute-start | bytes 589832 | tf_op jit(solution)/shard_map/ppermute | solution.py:838
  128.8 3.2 %first_output.3.part_ref = f32[384,1152]{1,0:T(8,128)S(1)} custom-call(s32[2]{0:T(128)S(1)} %pad_add_fusion.1.at_ref, bf16[256,4608]{1,0:T(8,128)(2,1)} %own_o_ref.3, bf16[3,256,1152]{2,1,0:T(8,128)(2,1)S(1)} %lay.1.after_ref.o_ref, bf16[384,256]{1,0:T(8,128)(2,1)S(1)} %attend.3.rest_2_.after_ref.rest_0_, ...), custom_call_target="tpu_custom_call" | custom-call | flops 49999998976 | bytes 100000000 | tf_op jit(solution)/shard_map/first_output/pallas_call | solution.py:639
  132.1 2.5 %last_output.2 = (f32[384,1152]{1,0:T(8,128)S(1)}, f32[1,384]{1,0:T(1,128)S(1)}) custom-call(s32[2]{0:T(128)S(1)} %pad_add_fusion.at_ref, f32[384,1152]{1,0:T(8,128)S(1)} %first_output.2.part_ref, bf16[3,256,1152]{2,1,0:T(8,128)(2,1)S(1)} %lay.1.after_ref.o_ref, bf16[384,256]{1,0:T(8,128)(2,1)S(1)} %gate.5.rest_0_, ...), custom_call_target="tpu_custom_call" | custom-call | tf_op jit(solution)/shard_map/last_output/pallas_call | solution.py:663
  136.0 2.5 %last_output.3 = (f32[384,1152]{1,0:T(8,128)S(1)}, f32[1,768]{1,0:T(1,128)S(1)}) custom-call(s32[2]{0:T(128)S(1)} %pad_add_fusion.at_ref, f32[384,1152]{1,0:T(8,128)S(1)} %first_output.3.part_ref, bf16[3,256,1152]{2,1,0:T(8,128)(2,1)S(1)} %lay.1.after_ref.o_ref, bf16[384,256]{1,0:T(8,128)(2,1)S(1)} %collective-permute-done.25.rest_0_, ...), custom_call_target="tpu_custom_call" | custom-call | tf_op jit(solution)/shard_map/last_output/pallas_call | solution.py:663
  138.6 2.4 %collective-permute-start.28 = (f32[1,768]{1,0:T(1,128)S(1)}, f32[1,768]{1,0:T(1,128)S(1)}, u32[]{:S(2)}, u32[]{:S(2)}) collective-permute-start(f32[1,768]{1,0:T(1,128)S(1)} %get-tuple-element.50.rest_2_), channel_id=1, source_target_pairs={{0,2},{1,3},{2,0},{3,1},{4,6},{5,7},{6,4},{7,5},{8,10},{9,11},{10,... | collective-permute-start | bytes 9224 | tf_op jit(solution)/shard_map/ppermute | solution.py:853
  144.6 3.2 %finish.1 = bf16[768,1152]{1,0:T(8,128)(2,1)} custom-call(bf16[768,1152]{1,0:T(8,128)(2,1)S(1)} %copy-done, f32[1,1152]{1,0:T(1,128)S(1)} %broadcast_in_dim.17.gain_ref, f32[384,1152]{1,0:T(8,128)S(1)} %get-tuple-element.47.rest_0_, f32[384,1152]{1,0:T(8,128)S(1)} %get-tuple-element.49.rest_1_, f32[1,768]{1,0:T(1,128)S(1)} %get-tuple-element.50.rest_2_, ...), custom_call_target="tpu_custom_call" | custom-call | tf_op jit(solution)/shard_map/finish/pallas_call | solution.py:704
  (99 shorter events, 32.0 us)
Async XLA Ops:
  0.0 19.7 %copy-start = (bf16[768,1152]{1,0:T(8,128)(2,1)S(1)}, bf16[768,1152]{1,0:T(8,128)(2,1)}, u32[]{:S(2)}) copy-start(bf16[768,1152]{1,0:T(8,128)(2,1)} %token_ref.1) | copy-start | bytes 5308420
  2.1 17.6 %collective-permute-start.10 = (bf16[128,1152]{1,0:T(8,128)(2,1)}, bf16[128,1152]{1,0:T(8,128)(2,1)S(1)}, u32[]{:S(2)}, u32[]{:S(2)}) collective-permute-start(bf16[128,1152]{1,0:T(8,128)(2,1)} %get-tuple-element.35), channel_id=1, source_target_pairs={{0,1},{1,0},{2,3},{3,2},{4,5},{5,4},{6,7},{7,6},{8,9},{9,8},{10,11... | collective-permute-start | bytes 884744 | tf_op jit(solution)/shard_map/ppermute | solution.py:752
  3.7 10.9 %collective-permute-start = (bf16[288,256]{1,0:T(8,128)(2,1)}, bf16[288,256]{1,0:T(8,128)(2,1)S(1)}, u32[]{:S(2)}, u32[]{:S(2)}) collective-permute-start(bf16[288,256]{1,0:T(8,128)(2,1)} %get-tuple-element.28), channel_id=1, source_target_pairs={{0,2},{1,3},{2,0},{3,1},{4,6},{5,7},{6,4},{7,5},{8,10},{9,11},{10,... | collective-permute-start | bytes 442376 | tf_op jit(solution)/shard_map/ppermute | solution.py:750
  6.3 13.4 %collective-permute-start.6 = (bf16[288,256]{1,0:T(8,128)(2,1)}, bf16[288,256]{1,0:T(8,128)(2,1)S(1)}, u32[]{:S(2)}, u32[]{:S(2)}) collective-permute-start(bf16[288,256]{1,0:T(8,128)(2,1)} %get-tuple-element.32), channel_id=1, source_target_pairs={{0,2},{1,3},{2,0},{3,1},{4,6},{5,7},{6,4},{7,5},{8,10},{9,11},{10,... | collective-permute-start | bytes 442376 | tf_op jit(solution)/shard_map/ppermute | solution.py:751
  20.7 27.5 %collective-permute-start.11 = (bf16[352,1152]{1,0:T(8,128)(2,1)}, bf16[352,1152]{1,0:T(8,128)(2,1)S(1)}, u32[]{:S(2)}, u32[]{:S(2)}) collective-permute-start(bf16[352,1152]{1,0:T(8,128)(2,1)} %stage.6), channel_id=1, source_target_pairs={{0,1},{1,0},{2,3},{3,2},{4,5},{5,4},{6,7},{7,6},{8,9},{9,8},{10,11... | collective-permute-start | bytes 2433032 | tf_op jit(solution)/shard_map/ppermute | solution.py:773
  21.2 5.1 %collective-permute-start.5 = (bf16[1,288,256]{2,1,0:T(8,128)(2,1)S(1)}, bf16[1,288,256]{2,1,0:T(8,128)(2,1)S(1)}, u32[]{:S(2)}, u32[]{:S(2)}) collective-permute-start(bf16[1,288,256]{2,1,0:T(8,128)(2,1)S(1)} %bitcast.19), channel_id=1, source_target_pairs={{0,8},{4,12},{8,0},{12,4},{16,24},{20,28},{24,16},{28,20},{1,9},{5... | collective-permute-start | bytes 442376 | tf_op jit(solution)/shard_map/ppermute | solution.py:775
  21.7 5.1 %collective-permute-start.7 = (bf16[1,288,256]{2,1,0:T(8,128)(2,1)S(1)}, bf16[1,288,256]{2,1,0:T(8,128)(2,1)S(1)}, u32[]{:S(2)}, u32[]{:S(2)}) collective-permute-start(bf16[1,288,256]{2,1,0:T(8,128)(2,1)S(1)} %bitcast.23), channel_id=1, source_target_pairs={{0,16},{4,20},{8,24},{12,28},{16,0},{20,4},{24,8},{28,12},{1,17},{... | collective-permute-start | bytes 442376 | tf_op jit(solution)/shard_map/ppermute | solution.py:776
  28.9 19.2 %collective-permute-start.8 = (bf16[2,288,256]{2,1,0:T(8,128)(2,1)}, bf16[2,288,256]{2,1,0:T(8,128)(2,1)}, u32[]{:S(2)}, u32[]{:S(2)}) collective-permute-start(bf16[2,288,256]{2,1,0:T(8,128)(2,1)} %get-tuple-element.33.refs_0_), channel_id=1, source_target_pairs={{0,16},{4,20},{8,24},{12,28},{16,0},{20,4},{24,8},{28,12},{1,17},{... | collective-permute-start | bytes 884744 | tf_op jit(solution)/shard_map/ppermute | solution.py:775
  30.5 17.6 %collective-permute-start.9 = (bf16[2,288,256]{2,1,0:T(8,128)(2,1)}, bf16[2,288,256]{2,1,0:T(8,128)(2,1)}, u32[]{:S(2)}, u32[]{:S(2)}) collective-permute-start(bf16[2,288,256]{2,1,0:T(8,128)(2,1)} %get-tuple-element.34.refs_2_), channel_id=1, source_target_pairs={{0,8},{4,12},{8,0},{12,4},{16,24},{20,28},{24,16},{28,20},{1,9},{5... | collective-permute-start | bytes 884744 | tf_op jit(solution)/shard_map/ppermute | solution.py:776
  34.4 8.5 %collective-permute-start.1 = (bf16[32,1152]{1,0:T(8,128)(2,1)S(1)}, bf16[32,1152]{1,0:T(8,128)(2,1)S(1)}, u32[]{:S(2)}, u32[]{:S(2)}) collective-permute-start(bf16[32,1152]{1,0:T(8,128)(2,1)S(1)} %get-tuple-element.29), channel_id=1, source_target_pairs={{0,1},{1,2},{2,3},{3,0},{4,5},{5,6},{6,7},{7,4},{8,9},{9,10},{10,1... | collective-permute-start | bytes 221192 | tf_op jit(solution)/shard_map/ppermute | solution.py:756
  36.0 6.9 %collective-permute-start.2 = (bf16[32,1152]{1,0:T(8,128)(2,1)S(1)}, bf16[32,1152]{1,0:T(8,128)(2,1)S(1)}, u32[]{:S(2)}, u32[]{:S(2)}) collective-permute-start(bf16[32,1152]{1,0:T(8,128)(2,1)S(1)} %get-tuple-element.30), channel_id=1, source_target_pairs={{0,2},{1,3},{2,0},{3,1},{4,6},{5,7},{6,4},{7,5},{8,10},{9,11},{10,... | collective-permute-start | bytes 221192 | tf_op jit(solution)/shard_map/ppermute | solution.py:756
  42.9 5.2 %collective-permute-start.3 = (bf16[32,1152]{1,0:T(8,128)(2,1)S(1)}, bf16[32,1152]{1,0:T(8,128)(2,1)S(1)}, u32[]{:S(2)}, u32[]{:S(2)}) collective-permute-start(bf16[32,1152]{1,0:T(8,128)(2,1)S(1)} %get-tuple-element.31), channel_id=1, source_target_pairs={{0,3},{1,0},{2,1},{3,2},{4,7},{5,4},{6,5},{7,6},{8,11},{9,8},{10,9... | collective-permute-start | bytes 221192 | tf_op jit(solution)/shard_map/ppermute | solution.py:756
  42.9 14.9 %collective-permute-start.13 = (bf16[288,1152]{1,0:T(8,128)(2,1)}, bf16[288,1152]{1,0:T(8,128)(2,1)S(1)}, u32[]{:S(2)}, u32[]{:S(2)}) collective-permute-start(bf16[288,1152]{1,0:T(8,128)(2,1)} %get-tuple-element.40), channel_id=1, source_target_pairs={{0,1},{1,0},{2,3},{3,2},{4,5},{5,4},{6,7},{7,6},{8,9},{9,8},{10,11... | collective-permute-start | bytes 1990664 | tf_op jit(solution)/shard_map/ppermute | solution.py:773
  50.8 2.5 %collective-permute-start.12 = (bf16[4,288,256]{2,1,0:T(8,128)(2,1)}, bf16[4,288,256]{2,1,0:T(8,128)(2,1)}, u32[]{:S(2)}, u32[]{:S(2)}) collective-permute-start(bf16[4,288,256]{2,1,0:T(8,128)(2,1)} %get-tuple-element.36.own_ref), channel_id=1, source_target_pairs={{0,4},{4,0},{8,12},{12,8},{16,20},{20,16},{24,28},{28,24},{1,5},{5... | collective-permute-start | bytes 1769480 | tf_op jit(solution)/shard_map/ppermute | solution.py:775
  50.9 7.0 %collective-permute-start.14 = (bf16[4,288,256]{2,1,0:T(8,128)(2,1)}, bf16[4,288,256]{2,1,0:T(8,128)(2,1)S(1)}, u32[]{:S(2)}, u32[]{:S(2)}) collective-permute-start(bf16[4,288,256]{2,1,0:T(8,128)(2,1)} %get-tuple-element.41.own_ref), channel_id=1, source_target_pairs={{0,4},{4,0},{8,12},{12,8},{16,20},{20,16},{24,28},{28,24},{1,5},{5... | collective-permute-start | bytes 1769480 | tf_op jit(solution)/shard_map/ppermute | solution.py:776
  61.6 18.7 %collective-permute-start.16 = (bf16[784,256]{1,0:T(8,128)(2,1)S(1)}, bf16[784,256]{1,0:T(8,128)(2,1)S(1)}, u32[]{:S(2)}, u32[]{:S(2)}) collective-permute-start(bf16[784,256]{1,0:T(8,128)(2,1)S(1)} %get-tuple-element.43.rest_0_), channel_id=1, source_target_pairs={{0,2},{1,3},{2,0},{3,1},{4,6},{5,7},{6,4},{7,5},{8,10},{9,11},{10,... | collective-permute-start | bytes 1204232 | tf_op jit(solution)/shard_map/ppermute | solution.py:799
  63.7 12.6 %collective-permute-start.4 = (bf16[1,3,32,1152]{3,2,1,0:T(8,128)(2,1)S(1)}, bf16[1,3,32,1152]{3,2,1,0:T(8,128)(2,1)S(1)}, u32[]{:S(2)}, u32[]{:S(2)}) collective-permute-start(bf16[1,3,32,1152]{3,2,1,0:T(8,128)(2,1)S(1)} %maximum_bitcast_fusion.refs_0_), channel_id=1, source_target_pairs={{0,8},{4,12},{8,0},{12,4},{16,24},{20,28},{24,16},{28,20},{1,9},{5... | collective-permute-start | bytes 663560 | tf_op jit(solution)/shard_map/ppermute | solution.py:786
  77.0 8.6 %collective-permute-start.15 = (bf16[2,3,32,1152]{3,2,1,0:T(8,128)(2,1)S(1)}, bf16[2,3,32,1152]{3,2,1,0:T(8,128)(2,1)}, u32[]{:S(2)}, u32[]{:S(2)}) collective-permute-start(bf16[2,3,32,1152]{3,2,1,0:T(8,128)(2,1)S(1)} %stage.8.rest_1_.refs_0_), channel_id=1, source_target_pairs={{0,16},{4,20},{8,24},{12,28},{16,0},{20,4},{24,8},{28,12},{1,17},{... | collective-permute-start | bytes 1327112 | tf_op jit(solution)/shard_map/ppermute | solution.py:786
  80.8 19.7 %collective-permute-start.18 = (bf16[768,256]{1,0:T(8,128)(2,1)S(1)}, bf16[768,256]{1,0:T(8,128)(2,1)}, u32[]{:S(2)}, u32[]{:S(2)}) collective-permute-start(bf16[768,256]{1,0:T(8,128)(2,1)S(1)} %gate.4), channel_id=1, source_target_pairs={{0,2},{1,3},{2,0},{3,1},{4,6},{5,7},{6,4},{7,5},{8,10},{9,11},{10,... | collective-permute-start | bytes 1179656 | tf_op jit(solution)/shard_map/ppermute | solution.py:808
  81.0 19.6 %copy-start.9 = (f32[768,128]{1,0:T(8,128)S(1)}, f32[768,128]{1,0:T(8,128)}, u32[]{:S(2)}) copy-start(f32[768,128]{1,0:T(8,128)} %copy-done.8) | copy-start | bytes 1179652
  81.0 21.1 %collective-permute-start.19 = (bf16[784,256]{1,0:T(8,128)(2,1)S(1)}, bf16[784,256]{1,0:T(8,128)(2,1)S(1)}, u32[]{:S(2)}, u32[]{:S(2)}) collective-permute-start(bf16[784,256]{1,0:T(8,128)(2,1)S(1)} %get-tuple-element.45.refs_3_.after_ref.rest_2_), channel_id=1, source_target_pairs={{0,8},{4,12},{1,9},{5,13},{2,10},{6,14},{3,11},{7,15},{16,24},{20,... | collective-permute-start | bytes 1204232 | tf_op jit(solution)/shard_map/ppermute | solution.py:822
  82.4 19.7 %collective-permute-start.20 = (bf16[784,256]{1,0:T(8,128)(2,1)S(1)}, bf16[784,256]{1,0:T(8,128)(2,1)S(1)}, u32[]{:S(2)}, u32[]{:S(2)}) collective-permute-start(bf16[784,256]{1,0:T(8,128)(2,1)S(1)} %get-tuple-element.45.refs_3_.after_ref.rest_2_), channel_id=1, source_target_pairs={{0,4},{4,8},{8,12},{1,5},{5,9},{9,13},{2,6},{6,10},{10,14},{3,7},{... | collective-permute-start | bytes 1204232 | tf_op jit(solution)/shard_map/ppermute | solution.py:822
  86.8 22.4 %collective-permute-start.17 = (bf16[4,3,32,1152]{3,2,1,0:T(8,128)(2,1)S(1)}, bf16[4,3,32,1152]{3,2,1,0:T(8,128)(2,1)S(1)}, u32[]{:S(2)}, u32[]{:S(2)}) collective-permute-start(bf16[4,3,32,1152]{3,2,1,0:T(8,128)(2,1)S(1)} %stage.9.own_ref), channel_id=1, source_target_pairs={{0,4},{4,0},{8,12},{12,8},{16,20},{20,16},{24,28},{28,24},{1,5},{5... | collective-permute-start | bytes 2654216 | tf_op jit(solution)/shard_map/ppermute | solution.py:786
  106.6 12.2 %collective-permute-start.22 = (bf16[384,256]{1,0:T(8,128)(2,1)S(1)}, bf16[384,256]{1,0:T(8,128)(2,1)S(1)}, u32[]{:S(2)}, u32[]{:S(2)}) collective-permute-start(bf16[384,256]{1,0:T(8,128)(2,1)S(1)} %attend.2.rest_0_), channel_id=1, source_target_pairs={{0,2},{1,3},{2,0},{3,1},{4,6},{5,7},{6,4},{7,5},{8,10},{9,11},{10,... | collective-permute-start | bytes 589832 | tf_op jit(solution)/shard_map/ppermute | solution.py:834
  106.7 12.2 %collective-permute-start.21 = (bf16[384,256]{1,0:T(8,128)(2,1)S(1)}, bf16[384,256]{1,0:T(8,128)(2,1)S(1)}, u32[]{:S(2)}, u32[]{:S(2)}) collective-permute-start(bf16[384,256]{1,0:T(8,128)(2,1)S(1)} %attend.2.rest_0_), channel_id=1, source_target_pairs={{0,1},{1,0},{2,3},{3,2},{4,5},{5,4},{6,7},{7,6},{8,9},{9,8},{10,11... | collective-permute-start | bytes 589832 | tf_op jit(solution)/shard_map/ppermute | solution.py:835
  116.3 12.5 %collective-permute-start.24 = (bf16[384,256]{1,0:T(8,128)(2,1)S(1)}, bf16[384,256]{1,0:T(8,128)(2,1)S(1)}, u32[]{:S(2)}, u32[]{:S(2)}) collective-permute-start(bf16[384,256]{1,0:T(8,128)(2,1)S(1)} %attend.3.rest_2_.after_ref.rest_0_), channel_id=1, source_target_pairs={{0,1},{1,0},{2,3},{3,2},{4,5},{5,4},{6,7},{7,6},{8,9},{9,8},{10,11... | collective-permute-start | bytes 589832 | tf_op jit(solution)/shard_map/ppermute | solution.py:835
  116.4 10.4 %collective-permute-start.25 = (bf16[384,256]{1,0:T(8,128)(2,1)S(1)}, bf16[384,256]{1,0:T(8,128)(2,1)S(1)}, u32[]{:S(2)}, u32[]{:S(2)}) collective-permute-start(bf16[384,256]{1,0:T(8,128)(2,1)S(1)} %attend.3.rest_2_.after_ref.rest_0_), channel_id=1, source_target_pairs={{0,2},{1,3},{2,0},{3,1},{4,6},{5,7},{6,4},{7,5},{8,10},{9,11},{10,... | collective-permute-start | bytes 589832 | tf_op jit(solution)/shard_map/ppermute | solution.py:834
  118.8 13.3 %collective-permute-start.23 = (bf16[384,256]{1,0:T(8,128)(2,1)S(1)}, bf16[384,256]{1,0:T(8,128)(2,1)S(1)}, u32[]{:S(2)}, u32[]{:S(2)}) collective-permute-start(bf16[384,256]{1,0:T(8,128)(2,1)S(1)} %gate.5.rest_0_), channel_id=1, source_target_pairs={{0,1},{1,0},{2,3},{3,2},{4,5},{5,4},{6,7},{7,6},{8,9},{9,8},{10,11... | collective-permute-start | bytes 589832 | tf_op jit(solution)/shard_map/ppermute | solution.py:838
  126.8 9.2 %collective-permute-start.26 = (bf16[384,256]{1,0:T(8,128)(2,1)S(1)}, bf16[384,256]{1,0:T(8,128)(2,1)S(1)}, u32[]{:S(2)}, u32[]{:S(2)}) collective-permute-start(bf16[384,256]{1,0:T(8,128)(2,1)S(1)} %collective-permute-done.25.rest_0_), channel_id=1, source_target_pairs={{0,1},{1,0},{2,3},{3,2},{4,5},{5,4},{6,7},{7,6},{8,9},{9,8},{10,11... | collective-permute-start | bytes 589832 | tf_op jit(solution)/shard_map/ppermute | solution.py:838
  138.6 5.4 %collective-permute-start.27 = (f32[1,768]{1,0:T(1,128)S(1)}, f32[1,768]{1,0:T(1,128)S(1)}, u32[]{:S(2)}, u32[]{:S(2)}) collective-permute-start(f32[1,768]{1,0:T(1,128)S(1)} %get-tuple-element.50.rest_2_), channel_id=1, source_target_pairs={{0,1},{1,2},{2,3},{3,0},{4,5},{5,6},{6,7},{7,4},{8,9},{9,10},{10,1... | collective-permute-start | bytes 9224 | tf_op jit(solution)/shard_map/ppermute | solution.py:853
  138.6 5.4 %collective-permute-start.28 = (f32[1,768]{1,0:T(1,128)S(1)}, f32[1,768]{1,0:T(1,128)S(1)}, u32[]{:S(2)}, u32[]{:S(2)}) collective-permute-start(f32[1,768]{1,0:T(1,128)S(1)} %get-tuple-element.50.rest_2_), channel_id=1, source_target_pairs={{0,2},{1,3},{2,0},{3,1},{4,6},{5,7},{6,4},{7,5},{8,10},{9,11},{10,... | collective-permute-start | bytes 9224 | tf_op jit(solution)/shard_map/ppermute | solution.py:853
  141.0 3.6 %collective-permute-start.29 = (f32[1,768]{1,0:T(1,128)S(1)}, f32[1,768]{1,0:T(1,128)S(1)}, u32[]{:S(2)}, u32[]{:S(2)}) collective-permute-start(f32[1,768]{1,0:T(1,128)S(1)} %get-tuple-element.50.rest_2_), channel_id=1, source_target_pairs={{0,3},{1,0},{2,1},{3,2},{4,7},{5,4},{6,5},{7,6},{8,11},{9,8},{10,9... | collective-permute-start | bytes 9224 | tf_op jit(solution)/shard_map/ppermute | solution.py:853
  (15 other events, 103.6 us)
